TPU v7x, 32 devices: a whole 2x2x4 slice. The times are simulated.
32 devices in a mesh: ctx: 8 (over z, y), fsdp: 4 (over x, core).
Axes of the slice: x: 2, y: 2, z: 4, core: 2. Of those that a mesh axis runs over, the one named last changes fastest.
Arguments:
- hidden_in: bfloat16 [4, 1024, 2048], P('fsdp', 'ctx'), may hold values from -7 to 7
- out_grad: bfloat16 [4, 1024, 2048], P('fsdp', 'ctx'), may hold values from -6 to 6
- norm_gains: float32 [4608], replicated, may hold values from 0.5 to 1.5
- w_query: bfloat16 [2048, 3072], P(('ctx', 'fsdp')), may hold values from -3 to 3
- w_latent: bfloat16 [2048, 576], P(('ctx', 'fsdp')), may hold values from -3 to 3
- w_expand: bfloat16 [512, 4096], P(None, ('ctx', 'fsdp')), may hold values from -0.25 to 0.25
- w_output: bfloat16 [2048, 2048], P(None, ('ctx', 'fsdp')), may hold values from -1 to 1
- shared_gate_up: bfloat16 [2048, 5632], P(('ctx', 'fsdp')), may hold values from -0.125 to 0.125
- shared_down: bfloat16 [2816, 2048], P(None, ('ctx', 'fsdp')), may hold values from -0.109375 to 0.109375
- expert_gate_up: bfloat16 [16, 2048, 2816], P('ctx', 'fsdp'), may hold values from -0.125 to 0.125
- expert_down: bfloat16 [16, 1408, 2048], P('ctx', None, 'fsdp'), may hold values from -0.15625 to 0.15625
- expert_ids: int32 [4, 1024, 6], P('fsdp', 'ctx'), may hold values from 0 to 15, all different within a row; in each aligned block of 128 rows (0 to 127, 128 to 255, ..., all dimensions but the last counted through in order) at most 54 rows name the same one
- expert_gates: float32 [4, 1024, 6], P('fsdp', 'ctx'), may hold values from 0.1 to 0.6
Outputs:
- hidden_out: bfloat16 [4, 1024, 2048], P('fsdp', 'ctx')
- hidden_in_grad: bfloat16 [4, 1024, 2048], P('fsdp', 'ctx')
- gains_grad: float32 [4608], P(('ctx', 'fsdp'))
- w_query_grad: float32 [2048, 3072], P(('ctx', 'fsdp'))
- w_latent_grad: float32 [2048, 576], P(('ctx', 'fsdp'))
- w_expand_grad: float32 [512, 4096], P(None, ('ctx', 'fsdp'))
- w_output_grad: float32 [2048, 2048], P(None, ('ctx', 'fsdp'))
- shared_gate_up_grad: float32 [2048, 5632], P(('ctx', 'fsdp'))
- shared_down_grad: float32 [2816, 2048], P(None, ('ctx', 'fsdp'))
- expert_gate_up_grad: float32 [16, 2048, 2816], P('ctx', 'fsdp')
- expert_down_grad: float32 [16, 1408, 2048], P('ctx', None, 'fsdp')
Inputs may be any that keep to these rules, and one draw needn't show every extreme that they name: `expert_ids`: each token names 6 different experts. In the rows of one device (aligned blocks of 128 rows) no expert is named more than 54 times, a bound that some block reaches.
All inputs are finite; a program needn't handle non-finite values.
Results may differ from a plain program's by a relative error of at most 0.02.
Values may be sent and summed in bfloat16 or wider, within the bound.
No kernel may reach another device: no remote copies, remote signals or barrier semaphores. Data moves between devices by JAX's collectives and lax.ppermute only.
A program may use at most 512 MiB of HBM per device.

v0:
```python
import math

import jax
import jax.numpy as jnp
from jax import lax
from jax.sharding import PartitionSpec as P

D = 2048
H = 16
DN = 128
DR = 64
DV = 128
KVL = 512
FF = 1408
TOP = 6
SFF = 2816


EPS = 1e-06


def positions(row_count, tok_dev, n_ctx):
    row_ids = jnp.arange(row_count, dtype=jnp.int32)
    device = row_ids // tok_dev
    within = row_ids % tok_dev
    half_rows = tok_dev // 2
    early_pos = device * half_rows + within
    late_pos = (2 * n_ctx - 1 - device) * half_rows + within - half_rows
    return jnp.where(within < half_rows, early_pos, late_pos)


def rope_tables(where_at, feat_width):
    frequency = 10000.0 ** (-2.0 * jnp.arange(feat_width // 2, dtype=jnp.float32) / feat_width)
    angles = where_at.astype(jnp.float32)[:, None] * frequency[None, :]
    return (jnp.cos(angles), jnp.sin(angles))


def rope_apply(values, cos_table, sin_table):
    half_width = values.shape[-1] // 2
    first_half = values[..., :half_width]
    second_half = values[..., half_width:]
    return jnp.concatenate(
        [
            first_half * cos_table - second_half * sin_table,
            second_half * cos_table + first_half * sin_table,
        ],
        -1,
    )


def rope_back(cotangent, cos_table, sin_table):
    half_width = cotangent.shape[-1] // 2
    first_half = cotangent[..., :half_width]
    second_half = cotangent[..., half_width:]
    return jnp.concatenate(
        [
            first_half * cos_table + second_half * sin_table,
            second_half * cos_table - first_half * sin_table,
        ],
        -1,
    )


def norm_forward(values, gain_vec):
    inverse = lax.rsqrt(jnp.mean(values * values, -1, keepdims=True) + EPS)
    return (values * inverse * gain_vec, inverse)


def norm_backward(values, inverse, gain_vec, cotangent):
    gain_grad = jnp.sum(cotangent * values * inverse, 0)
    scaled = cotangent * gain_vec
    inner_mean = jnp.mean(scaled * values, -1, keepdims=True)
    return (inverse * scaled - values * inverse * inverse * inverse * inner_mean, gain_grad)


def swiglu_forward(inputs, gate_up, down_proj, hidden):
    gate_and_up = jnp.dot(inputs, gate_up, preferred_element_type=jnp.float32)
    gate_part = gate_and_up[:, :hidden]
    up_part = gate_and_up[:, hidden:]
    active = (gate_part * jax.nn.sigmoid(gate_part) * up_part).astype(jnp.bfloat16)
    return (jnp.dot(active, down_proj, preferred_element_type=jnp.float32), gate_and_up)


def swiglu_backward(inputs, gate_up, down_proj, hidden, gate_and_up, cotangent):
    gate_part = gate_and_up[:, :hidden]
    up_part = gate_and_up[:, hidden:]
    sigmoid = jax.nn.sigmoid(gate_part)
    silu_val = gate_part * sigmoid
    active = (silu_val * up_part).astype(jnp.bfloat16)
    active_grad = jnp.dot(cotangent, down_proj.T, preferred_element_type=jnp.float32)
    down_grad = jnp.dot(active.T, cotangent, preferred_element_type=jnp.float32)
    gate_grad = active_grad * up_part * sigmoid * (1.0 + gate_part * (1.0 - sigmoid))
    up_grad = active_grad * silu_val
    both_grad = jnp.concatenate([gate_grad, up_grad], -1).astype(jnp.bfloat16)
    input_grad = jnp.dot(both_grad, gate_up.T, preferred_element_type=jnp.float32)
    gate_up_grad = jnp.dot(inputs.T, both_grad, preferred_element_type=jnp.float32)
    return (input_grad, gate_up_grad, down_grad)


def expert_forward(received, gate_up, down_proj):
    gate_and_up = jnp.einsum(
        "secd,edf->secf", received, gate_up, preferred_element_type=jnp.float32
    )
    gate_part = gate_and_up[..., :FF]
    up_part = gate_and_up[..., FF:]
    active = (gate_part * jax.nn.sigmoid(gate_part) * up_part).astype(jnp.bfloat16)
    expert_out = jnp.einsum("secf,efd->secd", active, down_proj, preferred_element_type=jnp.float32)
    return (expert_out.astype(jnp.bfloat16), gate_and_up)


def expert_backward(received, gate_up, down_proj, gate_and_up, slot_grad):
    gate_part = gate_and_up[..., :FF]
    up_part = gate_and_up[..., FF:]
    sigmoid = jax.nn.sigmoid(gate_part)
    silu_val = gate_part * sigmoid
    active = (silu_val * up_part).astype(jnp.bfloat16)
    active_grad = jnp.einsum(
        "secd,efd->secf", slot_grad, down_proj, preferred_element_type=jnp.float32
    )
    down_grad = jnp.einsum("secf,secd->efd", active, slot_grad, preferred_element_type=jnp.float32)
    gate_grad = active_grad * up_part * sigmoid * (1.0 + gate_part * (1.0 - sigmoid))
    up_grad = active_grad * silu_val
    both_grad = jnp.concatenate([gate_grad, up_grad], -1).astype(jnp.bfloat16)
    input_grad = jnp.einsum(
        "secf,edf->secd", both_grad, gate_up, preferred_element_type=jnp.float32
    )
    gate_up_grad = jnp.einsum(
        "secd,secf->edf", received, both_grad, preferred_element_type=jnp.float32
    )
    return (input_grad.astype(jnp.bfloat16), gate_up_grad, down_grad)


def slot_index(routes_flat, n_exp, capacity):
    onehot = (routes_flat[:, None] == jnp.arange(n_exp, dtype=jnp.int32)[None, :]).astype(jnp.int32)
    rank_table = jnp.cumsum(onehot, 0) - 1
    slot_rank = jnp.sum(rank_table * onehot, 1)
    return routes_flat * capacity + slot_rank


def sort_keys(values, n_ctx, half_rows):
    split_rows = values.reshape(n_ctx, 2, half_rows, values.shape[-1])
    early_part = split_rows[:, 0].reshape(n_ctx * half_rows, values.shape[-1])
    late_part = split_rows[::-1, 1].reshape(n_ctx * half_rows, values.shape[-1])
    return jnp.concatenate([early_part, late_part], 0)


def unsort_keys(values, n_ctx, half_rows):
    early_part = values[: n_ctx * half_rows].reshape(n_ctx, 1, half_rows, values.shape[-1])
    late_part = values[n_ctx * half_rows :].reshape(n_ctx, 1, half_rows, values.shape[-1])[::-1]
    return jnp.concatenate([early_part, late_part], 1).reshape(
        2 * n_ctx * half_rows, values.shape[-1]
    )


def block_scores(
    query_lat, query_rot, query_where, sorted_lat, sorted_rot, key_start, key_rows, score_scale
):
    lat_piece = lax.dynamic_slice_in_dim(sorted_lat, key_start, key_rows, 0)
    rot_piece = lax.dynamic_slice_in_dim(sorted_rot, key_start, key_rows, 0)
    scores = (
        jnp.einsum("thc,jc->thj", query_lat, lat_piece, preferred_element_type=jnp.float32)
        + jnp.einsum("thr,jr->thj", query_rot, rot_piece, preferred_element_type=jnp.float32)
    ) * score_scale
    key_where = key_start + jnp.arange(key_rows, dtype=jnp.int32)
    allowed = key_where[None, None, :] <= query_where[:, None, None]
    return (jnp.where(allowed, scores, -jnp.inf), lat_piece, rot_piece)


def half_forward(query_lat, query_rot, query_where, sorted_lat, sorted_rot, key_rows, score_scale):
    block_count = jnp.max(query_where) // key_rows + 1
    query_rows = query_lat.shape[0]
    head_count = query_lat.shape[1]

    def stat_step(block_idx, carried):
        top_score, exp_total = carried
        scores = block_scores(
            query_lat,
            query_rot,
            query_where,
            sorted_lat,
            sorted_rot,
            block_idx * key_rows,
            key_rows,
            score_scale,
        )[0]
        new_top = jnp.maximum(top_score, jnp.max(scores, -1))
        exp_total = exp_total * jnp.exp(top_score - new_top) + jnp.sum(
            jnp.exp(scores - new_top[..., None]), -1
        )
        return (new_top, exp_total)

    start_state = (
        jnp.full((query_rows, head_count), -jnp.inf, jnp.float32),
        jnp.zeros((query_rows, head_count), jnp.float32),
    )
    top_score, exp_total = lax.fori_loop(0, block_count, stat_step, start_state)
    log_total = top_score + jnp.log(exp_total)

    def mix_step(block_idx, mixed_lat):
        scores, lat_piece, rot_piece = block_scores(
            query_lat,
            query_rot,
            query_where,
            sorted_lat,
            sorted_rot,
            block_idx * key_rows,
            key_rows,
            score_scale,
        )
        prob_bf = jnp.exp(scores - log_total[..., None]).astype(jnp.bfloat16)
        return mixed_lat + jnp.einsum(
            "thj,jc->thc", prob_bf, lat_piece, preferred_element_type=jnp.float32
        )

    mixed_lat = lax.fori_loop(
        0,
        block_count,
        mix_step,
        jnp.zeros((query_rows, head_count, sorted_lat.shape[1]), jnp.float32),
    )
    return (mixed_lat, log_total)


def half_backward(
    query_lat,
    query_rot,
    query_where,
    sorted_lat,
    sorted_rot,
    key_rows,
    score_scale,
    log_total,
    mix_grad,
    row_delta,
    lat_buffer,
    rot_buffer,
):
    block_count = jnp.max(query_where) // key_rows + 1
    query_rows = query_lat.shape[0]
    head_count = query_lat.shape[1]

    def back_step(block_idx, carried):
        lat_q_grad, rot_q_grad, lat_store, rot_store = carried
        key_start = block_idx * key_rows
        scores, lat_piece, rot_piece = block_scores(
            query_lat,
            query_rot,
            query_where,
            sorted_lat,
            sorted_rot,
            key_start,
            key_rows,
            score_scale,
        )
        prob_f = jnp.exp(scores - log_total[..., None])
        prob_grad = jnp.einsum(
            "thc,jc->thj", mix_grad, lat_piece, preferred_element_type=jnp.float32
        )
        score_grad = (prob_f * (prob_grad - row_delta[..., None]) * score_scale).astype(
            jnp.bfloat16
        )
        lat_q_grad = lat_q_grad + jnp.einsum(
            "thj,jc->thc", score_grad, lat_piece, preferred_element_type=jnp.float32
        )
        rot_q_grad = rot_q_grad + jnp.einsum(
            "thj,jr->thr", score_grad, rot_piece, preferred_element_type=jnp.float32
        )
        lat_term = jnp.einsum(
            "thj,thc->jc", score_grad, query_lat, preferred_element_type=jnp.float32
        ) + jnp.einsum(
            "thj,thc->jc", prob_f.astype(jnp.bfloat16), mix_grad, preferred_element_type=jnp.float32
        )
        rot_term = jnp.einsum(
            "thj,thr->jr", score_grad, query_rot, preferred_element_type=jnp.float32
        )
        lat_store = lax.dynamic_update_slice_in_dim(
            lat_store,
            lax.dynamic_slice_in_dim(lat_store, key_start, key_rows, 0) + lat_term,
            key_start,
            0,
        )
        rot_store = lax.dynamic_update_slice_in_dim(
            rot_store,
            lax.dynamic_slice_in_dim(rot_store, key_start, key_rows, 0) + rot_term,
            key_start,
            0,
        )
        return (lat_q_grad, rot_q_grad, lat_store, rot_store)

    start_state = (
        jnp.zeros((query_rows, head_count, sorted_lat.shape[1]), jnp.float32),
        jnp.zeros((query_rows, head_count, sorted_rot.shape[1]), jnp.float32),
        lat_buffer,
        rot_buffer,
    )
    return lax.fori_loop(0, block_count, back_step, start_state)


def unpack_dense(dense_full):
    query_full, latent_full, expand_full, output_full, shared_gu_full, shared_down_full = dense_full
    expand_heads = expand_full.reshape(KVL, H, DN + DV)
    return (
        query_full,
        latent_full,
        expand_heads[:, :, :DN],
        expand_heads[:, :, DN:],
        output_full,
        shared_gu_full,
        shared_down_full,
    )


def on_device(
    hidden_in,
    out_grad,
    norm_gains,
    w_query,
    w_latent,
    w_expand,
    w_output,
    shared_gate_up,
    shared_down,
    expert_gate_up,
    expert_down,
    expert_ids,
    expert_gates,
):
    n_ctx = lax.axis_size("ctx")
    ctx_rank = lax.axis_index("ctx")
    tok_dev = hidden_in.shape[1]
    half_rows = tok_dev // 2
    length = tok_dev * n_ctx
    key_rows = min(256, length)
    score_scale = 1.0 / math.sqrt(DN + DR)
    halves = ((0, half_rows), (half_rows, tok_dev))
    gain_in = norm_gains[:D]
    gain_mid = norm_gains[D : 2 * D]
    gain_lat = norm_gains[2 * D :]
    where_all = positions(length, tok_dev, n_ctx)
    query_where = lax.dynamic_slice_in_dim(where_all, ctx_rank * tok_dev, tok_dev, 0)
    cos_table, sin_table = rope_tables(query_where, DR)
    dense_full = (
        lax.all_gather(w_query, ("ctx", "fsdp"), axis=0, tiled=True),
        lax.all_gather(w_latent, ("ctx", "fsdp"), axis=0, tiled=True),
        lax.all_gather(w_expand, ("ctx", "fsdp"), axis=1, tiled=True),
        lax.all_gather(w_output, ("ctx", "fsdp"), axis=1, tiled=True),
        lax.all_gather(shared_gate_up, ("ctx", "fsdp"), axis=0, tiled=True),
        lax.all_gather(shared_down, ("ctx", "fsdp"), axis=1, tiled=True),
    )
    expert_full = (
        lax.all_gather(expert_gate_up, "fsdp", axis=1, tiled=True),
        lax.all_gather(expert_down, "fsdp", axis=2, tiled=True),
    )
    query_full, latent_full, key_up, value_up, output_full, shared_gu_full, shared_down_full = (
        unpack_dense(dense_full)
    )
    expert_gu_full, expert_down_full = expert_full
    tokens = hidden_in[0].astype(jnp.float32)
    normed_in, inv_in = norm_forward(tokens, gain_in)
    normed_bf = normed_in.astype(jnp.bfloat16)
    query_all = jnp.dot(normed_bf, query_full, preferred_element_type=jnp.float32).reshape(
        tok_dev, H, DN + DR
    )
    query_nope = query_all[:, :, :DN].astype(jnp.bfloat16)
    query_rot = rope_apply(
        query_all[:, :, DN:], cos_table[:, None, :], sin_table[:, None, :]
    ).astype(jnp.bfloat16)
    query_lat = jnp.einsum(
        "thn,chn->thc", query_nope, key_up, preferred_element_type=jnp.float32
    ).astype(jnp.bfloat16)
    compressed = jnp.dot(normed_bf, latent_full, preferred_element_type=jnp.float32)
    lat_raw = compressed[:, :KVL]
    lat_normed, inv_lat = norm_forward(lat_raw, gain_lat)
    latent = lat_normed.astype(jnp.bfloat16)
    key_rot = rope_apply(compressed[:, KVL:], cos_table, sin_table).astype(jnp.bfloat16)
    latent_all, key_rot_all = (
        lax.all_gather(latent, "ctx", axis=0, tiled=True),
        lax.all_gather(key_rot, "ctx", axis=0, tiled=True),
    )
    sorted_lat = sort_keys(latent_all, n_ctx, half_rows)
    sorted_rot = sort_keys(key_rot_all, n_ctx, half_rows)
    mix_parts = []
    log_parts = []
    for row_lo, row_hi in halves:
        part_mix, part_log = half_forward(
            query_lat[row_lo:row_hi],
            query_rot[row_lo:row_hi],
            query_where[row_lo:row_hi],
            sorted_lat,
            sorted_rot,
            key_rows,
            score_scale,
        )
        mix_parts.append(part_mix)
        log_parts.append(part_log)
    mixed_lat = jnp.concatenate(mix_parts, 0)
    log_total = jnp.concatenate(log_parts, 0)
    mixed_bf = mixed_lat.astype(jnp.bfloat16)
    heads_out = (
        jnp.einsum("thc,chv->thv", mixed_bf, value_up, preferred_element_type=jnp.float32)
        .reshape(tok_dev, H * DV)
        .astype(jnp.bfloat16)
    )
    resid_mid = tokens + jnp.dot(heads_out, output_full, preferred_element_type=jnp.float32)
    normed_mid, inv_mid = norm_forward(resid_mid, gain_mid)
    mid_bf = normed_mid.astype(jnp.bfloat16)
    shared_out, shared_both = swiglu_forward(mid_bf, shared_gu_full, shared_down_full, SFF)
    exp_local = expert_gate_up.shape[0]
    n_exp = exp_local * n_ctx
    capacity = max(2, 9 * tok_dev * TOP // (8 * n_exp))
    routes_flat = expert_ids[0].reshape(-1)
    gates_rows = expert_gates[0]
    gates_flat = gates_rows.reshape(-1)
    slot_flat = slot_index(routes_flat, n_exp, capacity)
    entry_count = tok_dev * TOP
    entry_token = jnp.arange(entry_count, dtype=jnp.int32) // TOP
    token_of = jnp.full((n_exp * capacity,), tok_dev, jnp.int32).at[slot_flat].set(entry_token)
    entry_of = (
        jnp.full((n_exp * capacity,), entry_count, jnp.int32)
        .at[slot_flat]
        .set(jnp.arange(entry_count, dtype=jnp.int32))
    )
    mid_pad = jnp.concatenate([mid_bf, jnp.zeros((1, D), jnp.bfloat16)], 0)
    outgoing = mid_pad[token_of].reshape(n_ctx, exp_local, capacity, D)
    received = lax.all_to_all(outgoing, "ctx", split_axis=0, concat_axis=0, tiled=True)
    expert_out, expert_both = expert_forward(received, expert_gu_full, expert_down_full)
    returned = lax.all_to_all(expert_out, "ctx", split_axis=0, concat_axis=0, tiled=True).reshape(
        n_exp * capacity, D
    )
    picked = returned[slot_flat].reshape(tok_dev, TOP, D)
    routed_out = jnp.einsum("tk,tkd->td", gates_rows, picked.astype(jnp.float32))
    hidden_out = (resid_mid + shared_out + routed_out).astype(jnp.bfloat16)
    dense_full = (
        lax.all_gather(w_query, ("ctx", "fsdp"), axis=0, tiled=True),
        lax.all_gather(w_latent, ("ctx", "fsdp"), axis=0, tiled=True),
        lax.all_gather(w_expand, ("ctx", "fsdp"), axis=1, tiled=True),
        lax.all_gather(w_output, ("ctx", "fsdp"), axis=1, tiled=True),
        lax.all_gather(shared_gate_up, ("ctx", "fsdp"), axis=0, tiled=True),
        lax.all_gather(shared_down, ("ctx", "fsdp"), axis=1, tiled=True),
    )
    expert_full = (
        lax.all_gather(expert_gate_up, "fsdp", axis=1, tiled=True),
        lax.all_gather(expert_down, "fsdp", axis=2, tiled=True),
    )
    query_full, latent_full, key_up, value_up, output_full, shared_gu_full, shared_down_full = (
        unpack_dense(dense_full)
    )
    expert_gu_full, expert_down_full = expert_full
    grad_rows = out_grad[0].astype(jnp.float32)
    entry_grad = (gates_flat[:, None] * grad_rows[entry_token]).astype(jnp.bfloat16)
    entry_pad = jnp.concatenate([entry_grad, jnp.zeros((1, D), jnp.bfloat16)], 0)
    outgoing_grad = entry_pad[entry_of].reshape(n_ctx, exp_local, capacity, D)
    incoming_grad = lax.all_to_all(outgoing_grad, "ctx", split_axis=0, concat_axis=0, tiled=True)
    slot_in_grad, expert_gu_grad, expert_dn_grad = expert_backward(
        received, expert_gu_full, expert_down_full, expert_both, incoming_grad
    )
    returned_grad = lax.all_to_all(
        slot_in_grad, "ctx", split_axis=0, concat_axis=0, tiled=True
    ).reshape(n_exp * capacity, D)
    routed_grad = jnp.sum(returned_grad[slot_flat].reshape(tok_dev, TOP, D).astype(jnp.float32), 1)
    shared_in_grad, shared_gu_grad, shared_dn_grad = swiglu_backward(
        mid_bf, shared_gu_full, shared_down_full, SFF, shared_both, out_grad[0]
    )
    mid_grad = shared_in_grad + routed_grad
    resid_norm_grad, gain_mid_grad = norm_backward(resid_mid, inv_mid, gain_mid, mid_grad)
    resid_grad = grad_rows + resid_norm_grad
    resid_bf = resid_grad.astype(jnp.bfloat16)
    output_w_grad = jnp.dot(heads_out.T, resid_bf, preferred_element_type=jnp.float32)
    heads_grad = (
        jnp.dot(resid_bf, output_full.T, preferred_element_type=jnp.float32)
        .astype(jnp.bfloat16)
        .reshape(tok_dev, H, DV)
    )
    value_grad = jnp.einsum(
        "thc,thv->chv", mixed_bf, heads_grad, preferred_element_type=jnp.float32
    )
    mix_grad = jnp.einsum(
        "thv,chv->thc", heads_grad, value_up, preferred_element_type=jnp.float32
    ).astype(jnp.bfloat16)
    row_delta = jnp.sum(mix_grad.astype(jnp.float32) * mixed_lat, -1)
    lat_buffer = jnp.zeros((length, KVL), jnp.float32)
    rot_buffer = jnp.zeros((length, DR), jnp.float32)
    lat_q_parts = []
    rot_q_parts = []
    for row_lo, row_hi in halves:
        lat_q, rot_q, lat_buffer, rot_buffer = half_backward(
            query_lat[row_lo:row_hi],
            query_rot[row_lo:row_hi],
            query_where[row_lo:row_hi],
            sorted_lat,
            sorted_rot,
            key_rows,
            score_scale,
            log_total[row_lo:row_hi],
            mix_grad[row_lo:row_hi],
            row_delta[row_lo:row_hi],
            lat_buffer,
            rot_buffer,
        )
        lat_q_parts.append(lat_q)
        rot_q_parts.append(rot_q)
    latent_terms = unsort_keys(lat_buffer, n_ctx, half_rows)
    rot_terms = unsort_keys(rot_buffer, n_ctx, half_rows)
    latent_grad, key_rot_grad = (
        lax.psum_scatter(
            latent_terms.astype(jnp.bfloat16), "ctx", scatter_dimension=0, tiled=True
        ).astype(jnp.float32),
        lax.psum_scatter(
            rot_terms.astype(jnp.bfloat16), "ctx", scatter_dimension=0, tiled=True
        ).astype(jnp.float32),
    )
    query_lat_grad = jnp.concatenate(lat_q_parts, 0).astype(jnp.bfloat16)
    rot_q_grad = jnp.concatenate(rot_q_parts, 0)
    key_grad = jnp.einsum(
        "thc,thn->chn", query_lat_grad, query_nope, preferred_element_type=jnp.float32
    )
    nope_grad = jnp.einsum(
        "thc,chn->thn", query_lat_grad, key_up, preferred_element_type=jnp.float32
    )
    query_grad = (
        jnp.concatenate(
            [nope_grad, rope_back(rot_q_grad, cos_table[:, None, :], sin_table[:, None, :])], -1
        )
        .reshape(tok_dev, H * (DN + DR))
        .astype(jnp.bfloat16)
    )
    query_w_grad = jnp.dot(normed_bf.T, query_grad, preferred_element_type=jnp.float32)
    in_grad = jnp.dot(query_grad, query_full.T, preferred_element_type=jnp.float32)
    lat_in_grad, gain_lat_grad = norm_backward(lat_raw, inv_lat, gain_lat, latent_grad)
    compressed_grad = jnp.concatenate(
        [lat_in_grad, rope_back(key_rot_grad, cos_table, sin_table)], -1
    ).astype(jnp.bfloat16)
    latent_w_grad = jnp.dot(normed_bf.T, compressed_grad, preferred_element_type=jnp.float32)
    in_grad = in_grad + jnp.dot(compressed_grad, latent_full.T, preferred_element_type=jnp.float32)
    token_grad, gain_in_grad = norm_backward(tokens, inv_in, gain_in, in_grad)
    hidden_in_grad = (resid_grad + token_grad).astype(jnp.bfloat16)
    expand_grad = jnp.concatenate([key_grad, value_grad], -1).reshape(KVL, H * (DN + DV))
    gains_all_grad = jnp.concatenate([gain_in_grad, gain_mid_grad, gain_lat_grad], 0)
    dense_grads = (
        lax.psum_scatter(query_w_grad, ("ctx", "fsdp"), scatter_dimension=0, tiled=True),
        lax.psum_scatter(latent_w_grad, ("ctx", "fsdp"), scatter_dimension=0, tiled=True),
        lax.psum_scatter(expand_grad, ("ctx", "fsdp"), scatter_dimension=1, tiled=True),
        lax.psum_scatter(output_w_grad, ("ctx", "fsdp"), scatter_dimension=1, tiled=True),
        lax.psum_scatter(shared_gu_grad, ("ctx", "fsdp"), scatter_dimension=0, tiled=True),
        lax.psum_scatter(shared_dn_grad, ("ctx", "fsdp"), scatter_dimension=1, tiled=True),
        lax.psum_scatter(gains_all_grad, ("ctx", "fsdp"), scatter_dimension=0, tiled=True),
    )
    expert_grads = (
        lax.psum_scatter(
            expert_gu_grad.astype(jnp.bfloat16), "fsdp", scatter_dimension=1, tiled=True
        ).astype(jnp.float32),
        lax.psum_scatter(
            expert_dn_grad.astype(jnp.bfloat16), "fsdp", scatter_dimension=2, tiled=True
        ).astype(jnp.float32),
    )
    return (
        hidden_out[None],
        hidden_in_grad[None],
        dense_grads[6],
        dense_grads[0],
        dense_grads[1],
        dense_grads[2],
        dense_grads[3],
        dense_grads[4],
        dense_grads[5],
        expert_grads[0],
        expert_grads[1],
    )


def solution(mesh):
    placed = (
        P("fsdp", "ctx", None),
        P("fsdp", "ctx", None),
        P(),
        P(("ctx", "fsdp"), None),
        P(("ctx", "fsdp"), None),
        P(None, ("ctx", "fsdp")),
        P(None, ("ctx", "fsdp")),
        P(("ctx", "fsdp"), None),
        P(None, ("ctx", "fsdp")),
        P("ctx", "fsdp", None),
        P("ctx", None, "fsdp"),
        P("fsdp", "ctx", None),
        P("fsdp", "ctx", None),
    )
    return jax.shard_map(
        on_device,
        mesh=mesh,
        in_specs=placed,
        out_specs=(
            P("fsdp", "ctx", None),
            P("fsdp", "ctx", None),
            P(("ctx", "fsdp")),
            P(("ctx", "fsdp"), None),
            P(("ctx", "fsdp"), None),
            P(None, ("ctx", "fsdp")),
            P(None, ("ctx", "fsdp")),
            P(("ctx", "fsdp"), None),
            P(None, ("ctx", "fsdp")),
            P("ctx", "fsdp", None),
            P("ctx", None, "fsdp"),
        ),
        check_vma=False,
    )
```

profile of v0, /device:TPU:0, one launch (start us, length us, event | category | flops | bytes accessed | tf_op | source)
XLA Modules:
  0.0 2851.9 jit_solution(7681805977661642833)
XLA Ops:
  11.2 60.3 %all-gather.10.cloned.1.call-done = bf16[2048,576]{1,0:T(8,128)(2,1)} async-done(((bf16[64,576]{1,0:T(8,128)(2,1)}), bf16[2048,576]{1,0:T(8,128)(2,1)}) %all-gather.10.cloned.1.call-update) | async-done | bytes 2359312 | tf_op jit(solution)/shard_map/all_gather | solution.py:344
  93.4 26.6 all_gather.42
  123.3 89.8 %all-gather.14.cloned.1.call-done = bf16[2048,3072]{1,0:T(8,128)(2,1)} async-done(((bf16[64,3072]{1,0:T(8,128)(2,1)}), bf16[2048,3072]{1,0:T(8,128)(2,1)}) %all-gather.14.cloned.1.call-update) | async-done | bytes 12582928 | tf_op jit(solution)/shard_map/all_gather | solution.py:343
  213.1 16.8 copy.112
  229.9 6.6 fusion.200
  240.0 36.8 %all-gather.16.cloned.1.call-done = bf16[512,4096]{0,1:T(8,128)(2,1)} async-done(((bf16[512,128]{0,1:T(8,128)(2,1)}), bf16[512,4096]{0,1:T(8,128)(2,1)}) %all-gather.16.cloned.1.call-update) | async-done | bytes 4194320 | tf_op jit(solution)/shard_map/all_gather | solution.py:345
  280.9 18.7 while.78
  321.2 19.7 while.79
  348.6 6.9 all-gather.18.cloned.1.call-done
  355.5 6.4 multiply_reduce_fusion.3
  374.1 8.0 copy.132
  409.5 7.4 copy.137
  417.0 49.7 %all-to-all-done = bf16[8,2,54,2048]{3,1,2,0:T(2,128)(2,1)} async-done(((bf16[8,2,54,2048]{3,1,2,0:T(2,128)(2,1)}), bf16[8,2,54,2048]{3,1,2,0:T(2,128)(2,1)}, u32[]{:S(2)}, u32[]{:S(2)}) %all-to-all-start) | async-done | bytes 3538976 | tf_op jit(solution)/shard_map/all_to_all | solution.py:425
  470.7 26.7 all-gather.24.cloned.1.call-done
  497.4 22.9 fusion.142
  520.2 29.8 %all-to-all-done.2 = bf16[8,2,54,2048]{3,1,2,0:T(2,128)(2,1)S(1)} async-done(((bf16[8,2,54,2048]{3,1,2,0:T(2,128)(2,1)}), bf16[8,2,54,2048]{3,1,2,0:T(2,128)(2,1)S(1)}, u32[]{:S(2)}, u32[]{:S(2)}) %all-to-all-start.2) | async-done | bytes 3538976 | tf_op jit(solution)/shard_map/all_to_all | solution.py:453
  550.0 25.1 all-gather.26.cloned.1.call-done
  575.1 16.7 fusion.147
  591.9 15.7 convert_bitcast_fusion
  618.7 149.0 %all-to-all-done.3 = bf16[8,2,54,2048]{3,1,2,0:T(2,128)(2,1)S(1)} async-done(((bf16[8,2,54,2048]{3,1,2,0:T(2,128)(2,1)}), bf16[8,2,54,2048]{3,1,2,0:T(2,128)(2,1)S(1)}, u32[]{:S(2)}, u32[]{:S(2)}) %all-to-all-start.3) | async-done | bytes 3538976 | tf_op jit(solution)/shard_map/all_to_all | solution.py:457
  778.8 6.7 reshape.516
  791.6 12.7 fusion.282
  804.4 74.7 %all-gather.22.cloned.1.call-done = bf16[2816,2048]{0,1:T(8,128)(2,1)} async-done(((bf16[2816,64]{0,1:T(8,128)(2,1)}), bf16[2816,2048]{0,1:T(8,128)(2,1)}) %all-gather.22.cloned.1.call-update) | async-done | bytes 11534352 | tf_op jit(solution)/shard_map/all_gather | solution.py:348
  879.1 8.4 multiply_convert_fusion.3
  887.5 14.1 multiply_reduce_fusion.1
  920.0 12.2 while.80
  934.7 41.7 %while.81 = (s32[]{:T(128)}, f32[64,16,512]{2,1,0:T(8,128)}, f32[64,16,64]{2,1,0:T(8,128)}, f32[1024,512]{1,0:T(8,128)}, f32[1024,64]{0,1:T(8,128)}, /*index=5*/...) while((s32[]{:T(128)}, f32[64,16,512]{2,1,0:T(8,128)}, ...), condition=%wide.region_28.29_spmd, body=%wide.region_27.28_spmd.sunk | while | flops 1446084864 | bytes 26873472 | solution.py:296
  989.1 11.5 bitcast_convert_fusion.1
  1002.3 17.6 bitcast_convert_fusion
  1020.1 23.5 reduce-scatter.33.cloned.1.call-done
  1044.7 65.4 %reduce-scatter.31.cloned.1.call-done = bf16[128,512]{1,0:T(8,128)(2,1)} async-done(((bf16[1024,512]{1,0:T(8,128)(2,1)}), bf16[128,512]{1,0:T(8,128)(2,1)}) %reduce-scatter.31.cloned.1.call-update) | async-done | bytes 131088
  1132.3 9.3 copy.152
  1143.0 8.3 fusion.212
  1157.8 10.6 fusion.202
  1169.7 9.6 fusion.196
  1180.8 18.3 fusion.194
  1200.8 10.5 convert_bitcast_fusion.1
  1221.1 77.6 %all-to-all-done.1 = bf16[8,2,54,2048]{3,1,2,0:T(2,128)(2,1)S(1)} async-done(((bf16[8,2,54,2048]{3,1,2,0:T(2,128)(2,1)}), bf16[8,2,54,2048]{3,1,2,0:T(2,128)(2,1)S(1)}, u32[]{:S(2)}, u32[]{:S(2)}) %all-to-all-start.1) | async-done | bytes 3538976 | tf_op jit(solution)/shard_map/all_to_all | solution.py:427
  1319.8 9.2 fusion.284
  1329.1 9.2 fusion.160
  1339.5 38.9 %all-reduce.2 = f32[4608]{0:T(1024)S(1)} all-reduce(f32[4608]{0:T(1024)S(1)} %pad_maximum_fusion.18), channel_id=4, replica_groups=mesh['ctx'=8,'fsdp'=4] {'ctx','fsdp'}, use_global_device_ids=true, to_apply=%region_36.37.clone | all-reduce | flops 4608 | bytes 36864
  1385.4 7.9 convert_element_type.209
  1393.4 127.1 %reduce-scatter.17.cloned.1.call-done = f32[64,576]{1,0:T(8,128)} async-done(((f32[2048,576]{1,0:T(8,128)}), f32[64,576]{1,0:T(8,128)}) %reduce-scatter.17.cloned.1.call-update) | async-done | bytes 147472 | tf_op jit(solution)/shard_map/reduce_scatter | solution.py:541
  1520.5 147.4 %reduce-scatter.19.cloned.1.call-done = f32[512,128]{1,0:T(8,128)} async-done(((f32[512,4096]{1,0:T(8,128)}), f32[512,128]{1,0:T(8,128)}) %reduce-scatter.19.cloned.1.call-update) | async-done | bytes 262160 | tf_op jit(solution)/shard_map/reduce_scatter | solution.py:542
  1667.9 181.3 %reduce-scatter.21.cloned.1.call-done = f32[2048,64]{0,1:T(8,128)} async-done(((f32[2048,2048]{0,1:T(8,128)}), f32[2048,64]{0,1:T(8,128)}) %reduce-scatter.21.cloned.1.call-update) | async-done | bytes 524304 | tf_op jit(solution)/shard_map/reduce_scatter | solution.py:543
  1849.2 254.1 %reduce-scatter.15.cloned.1.call-done = f32[64,3072]{1,0:T(8,128)} async-done(((f32[2048,3072]{1,0:T(8,128)}), f32[64,3072]{1,0:T(8,128)}) %reduce-scatter.15.cloned.1.call-update) | async-done | bytes 786448 | tf_op jit(solution)/shard_map/reduce_scatter | solution.py:540
  2103.3 248.7 %reduce-scatter.25.cloned.1.call-done = f32[2816,64]{0,1:T(8,128)} async-done(((f32[2816,2048]{0,1:T(8,128)}), f32[2816,64]{0,1:T(8,128)}) %reduce-scatter.25.cloned.1.call-update) | async-done | bytes 720912 | tf_op jit(solution)/shard_map/reduce_scatter | solution.py:545
  2352.0 493.2 %reduce-scatter.23.cloned.1.call-done = f32[64,5632]{1,0:T(8,128)} async-done(((f32[2048,5632]{1,0:T(8,128)}), f32[64,5632]{1,0:T(8,128)}) %reduce-scatter.23.cloned.1.call-update) | async-done | bytes 1441808 | tf_op jit(solution)/shard_map/reduce_scatter | solution.py:544
  (558 shorter events, 330.4 us)
Async XLA Ops:
  7.2 69.1 %copy-start.81 = (bf16[512,128]{1,0:T(8,128)(2,1)S(1)}, bf16[512,128]{1,0:T(8,128)(2,1)}, u32[]{:S(2)}) copy-start(bf16[512,128]{1,0:T(8,128)(2,1)} %param.30) | copy-start | bytes 393220
  7.2 64.3 %all-gather.10.cloned.1.call-start = ((), (), s32[]{:S(2)}) async-start(), calls=%async_computation.14 | async-start | bytes 2703360 | tf_op jit(solution)/shard_map/all_gather | solution.py:344
  7.9 113.7 %all-gather.12.cloned.1.call-start = ((), (), s32[]{:S(2)}) async-start(), calls=%async_computation.15 | async-start | bytes 1179648 | tf_op jit(solution)/shard_map/all_gather | solution.py:377
  8.7 69.6 %copy-start.88 = (f32[512]{0:T(512)}, f32[512]{0:T(512)S(1)}, u32[]{:S(2)}) copy-start(f32[512]{0:T(512)S(1)} %slice.141) | copy-start | bytes 6148
  9.9 220.0 %copy-start.85 = (f32[128]{0:T(128)}, f32[128]{0:T(128)S(1)}, u32[]{:S(2)}) copy-start(f32[128]{0:T(128)S(1)} %add_rsqrt_fusion.2) | copy-start | bytes 1540
  11.2 218.7 %copy-start.59 = (f32[2048]{0:T(1024)}, f32[2048]{0:T(1024)S(1)}, u32[]{:S(2)}) copy-start(f32[2048]{0:T(1024)S(1)} %get-tuple-element.648) | copy-start | bytes 24580
  75.5 137.6 %all-gather.14.cloned.1.call-start = ((), (), s32[]{:S(2)}) async-start(), calls=%async_computation.16 | async-start | bytes 12976128 | tf_op jit(solution)/shard_map/all_gather | solution.py:343
  76.2 200.5 %all-gather.16.cloned.1.call-start = ((), (), s32[]{:S(2)}) async-start(), calls=%async_computation.17 | async-start | bytes 4325376 | tf_op jit(solution)/shard_map/all_gather | solution.py:345
  77.1 278.4 %all-gather.18.cloned.1.call-start = ((), (), s32[]{:S(2)}) async-start(), calls=%async_computation.18 | async-start | bytes 8650752 | tf_op jit(solution)/shard_map/all_gather | solution.py:346
  77.7 419.7 %all-gather.24.cloned.1.call-start = ((), (), s32[]{:S(2)}) async-start(), calls=%async_computation.21 | async-start | bytes 28835840 | tf_op jit(solution)/shard_map/all_gather | solution.py:351
  78.3 496.9 %all-gather.26.cloned.1.call-start = ((), (), s32[]{:S(2)}) async-start(), calls=%async_computation.22 | async-start | bytes 14417920 | tf_op jit(solution)/shard_map/all_gather | solution.py:352
  79.0 712.5 %all-gather.20.cloned.1.call-start = ((), (), s32[]{:S(2)}) async-start(), calls=%async_computation.19 | async-start | bytes 23789568 | tf_op jit(solution)/shard_map/all_gather | solution.py:347
  79.9 41.7 %copy-start.98 = (f32[128]{0:T(128)}, f32[128]{0:T(128)S(1)}, u32[]{:S(2)}) copy-start(f32[128]{0:T(128)S(1)} %get-tuple-element.617) | copy-start | bytes 1540
  93.4 143.1 %copy-start.72 = (f32[128,32]{0,1:T(8,128)}, f32[128,32]{0,1:T(8,128)S(1)}, u32[]{:S(2)}) copy-start(f32[128,32]{0,1:T(8,128)S(1)} %get-tuple-element.651) | copy-start | bytes 49156
  93.4 143.1 %copy-start.74 = (f32[128,32]{0,1:T(8,128)}, f32[128,32]{0,1:T(8,128)S(1)}, u32[]{:S(2)}) copy-start(f32[128,32]{0,1:T(8,128)S(1)} %get-tuple-element.652) | copy-start | bytes 49156
  236.5 40.2 %copy-start.29 = (f32[128,16,192]{0,2,1:T(8,128)}, f32[128,16,192]{0,2,1:T(8,128)S(1)}, u32[]{:S(2)}) copy-start(f32[128,16,192]{0,2,1:T(8,128)S(1)} %fusion.200) | copy-start | bytes 4718596
  236.8 40.0 %copy-start.7 = (bf16[64,16,64]{0,2,1:T(8,128)(2,1)}, bf16[64,16,64]{0,2,1:T(8,128)(2,1)S(1)}, u32[]{:S(2)}) copy-start(bf16[64,16,64]{0,2,1:T(8,128)(2,1)S(1)} %get-tuple-element.1289) | copy-start | bytes 393220
  236.8 40.0 %copy-start.9 = (bf16[64,16,64]{0,2,1:T(8,128)(2,1)}, bf16[64,16,64]{0,2,1:T(8,128)(2,1)S(1)}, u32[]{:S(2)}) copy-start(bf16[64,16,64]{0,2,1:T(8,128)(2,1)S(1)} %get-tuple-element.1235) | copy-start | bytes 393220
  382.1 84.5 %all-to-all-start = ((bf16[8,2,54,2048]{3,1,2,0:T(2,128)(2,1)}), bf16[8,2,54,2048]{3,1,2,0:T(2,128)(2,1)}, u32[]{:S(2)}, u32[]{:S(2)}) async-start(bf16[8,2,54,2048]{3,1,2,0:T(2,128)(2,1)} %copy.132), calls=%async_computation | async-start | bytes 7077888 | tf_op jit(solution)/shard_map/all_to_all | solution.py:425
  386.8 492.3 %all-gather.22.cloned.1.call-start = ((), (), s32[]{:S(2)}) async-start(), calls=%async_computation.20 | async-start | bytes 11894784 | tf_op jit(solution)/shard_map/all_gather | solution.py:348
  466.7 83.3 %all-to-all-start.2 = ((bf16[8,2,54,2048]{3,1,2,0:T(2,128)(2,1)}), bf16[8,2,54,2048]{3,1,2,0:T(2,128)(2,1)S(1)}, u32[]{:S(2)}, u32[]{:S(2)}) async-start(bf16[8,2,54,2048]{3,1,2,0:T(2,128)(2,1)} %copy.137), calls=%async_computation.2 | async-start | bytes 7077888 | tf_op jit(solution)/shard_map/all_to_all | solution.py:453
  550.0 41.9 %copy-start.52 = (bf16[8,2,54,2048]{3,1,2,0:T(2,128)(2,1)}, bf16[8,2,54,2048]{3,1,2,0:T(2,128)(2,1)S(1)}, u32[]{:S(2)}) copy-start(bf16[8,2,54,2048]{3,1,2,0:T(2,128)(2,1)S(1)} %all-to-all-done.2) | copy-start | bytes 10616836
  613.1 154.6 %all-to-all-start.3 = ((bf16[8,2,54,2048]{3,1,2,0:T(2,128)(2,1)}), bf16[8,2,54,2048]{3,1,2,0:T(2,128)(2,1)S(1)}, u32[]{:S(2)}, u32[]{:S(2)}) async-start(bf16[8,2,54,2048]{3,1,2,0:T(2,128)(2,1)} %copy.139), calls=%async_computation.3 | async-start | bytes 7077888 | tf_op jit(solution)/shard_map/all_to_all | solution.py:457
  618.6 425.1 %reduce-scatter.33.cloned.1.call-start = ((), (), s32[]{:S(2)}) async-start(), calls=%async_computation.32 | async-start | bytes 294912
  618.6 155.9 %copy-start.84 = (s32[1024]{0:T(1024)}, s32[1024]{0:T(1024)S(1)}, u32[]{:S(2)}) copy-start(s32[1024]{0:T(1024)S(1)} %pad_clamp_fusion.2) | copy-start | bytes 12292
  791.6 87.5 %copy-start.43 = (bf16[1,128,2048]{2,1,0:T(8,128)(2,1)S(1)}, bf16[1,128,2048]{2,1,0:T(8,128)(2,1)}, u32[]{:S(2)}) copy-start(bf16[1,128,2048]{2,1,0:T(8,128)(2,1)} %param.26) | copy-start | bytes 1572868
  804.3 83.1 %copy-start.19 = (f32[128,2048]{1,0:T(8,128)S(1)}, f32[128,2048]{1,0:T(8,128)}, u32[]{:S(2)}) copy-start(f32[128,2048]{1,0:T(8,128)} %copy-done.18) | copy-start | bytes 3145732
  804.3 83.1 %copy-start.97 = (f32[128]{0:T(128)S(1)}, f32[128]{0:T(128)}, u32[]{:S(2)}) copy-start(f32[128]{0:T(128)} %copy-done.96) | copy-start | bytes 1540
  982.2 127.9 %reduce-scatter.31.cloned.1.call-start = ((), (), s32[]{:S(2)}) async-start(), calls=%async_computation.31 | async-start | bytes 1179648
  989.1 391.2 %reduce-scatter.29.cloned.1.call-start = ((), (), s32[]{:S(2)}) async-start(), calls=%async_computation.30 | async-start | bytes 14417920 | tf_op jit(solution)/shard_map/reduce_scatter | solution.py:552
  1000.6 384.8 %reduce-scatter.27.cloned.1.call-start = ((), (), s32[]{:S(2)}) async-start(), calls=%async_computation.29 | async-start | bytes 28835840 | tf_op jit(solution)/shard_map/reduce_scatter | solution.py:549
  1020.0 24.5 copy-start.99
  1020.0 24.5 copy-start.104
  1020.0 91.1 %copy-start.41 = (f32[128,576]{0,1:T(8,128)S(1)}, f32[128,576]{0,1:T(8,128)}, u32[]{:S(2)}) copy-start(f32[128,576]{0,1:T(8,128)} %copy-done.40) | copy-start | bytes 884740
  1020.0 91.1 %copy-start.89 = (f32[512]{0:T(512)S(1)}, f32[512]{0:T(512)}, u32[]{:S(2)}) copy-start(f32[512]{0:T(512)} %copy-done.88) | copy-start | bytes 6148
  1020.0 91.1 %copy-start.101 = (f32[128]{0:T(128)S(1)}, f32[128]{0:T(128)}, u32[]{:S(2)}) copy-start(f32[128]{0:T(128)} %copy-done.100) | copy-start | bytes 1540
  1020.0 92.7 %copy-start.13 = (bf16[1,128,2048]{2,1,0:T(8,128)(2,1)S(1)}, bf16[1,128,2048]{2,1,0:T(8,128)(2,1)}, u32[]{:S(2)}) copy-start(bf16[1,128,2048]{2,1,0:T(8,128)(2,1)} %param.25) | copy-start | bytes 1572868
  1020.0 92.7 %copy-start.60 = (f32[2048]{0:T(1024)S(1)}, f32[2048]{0:T(1024)}, u32[]{:S(2)}) copy-start(f32[2048]{0:T(1024)} %copy-done.59) | copy-start | bytes 24580
  1020.0 92.7 %copy-start.86 = (f32[128]{0:T(128)S(1)}, f32[128]{0:T(128)}, u32[]{:S(2)}) copy-start(f32[128]{0:T(128)} %copy-done.85) | copy-start | bytes 1540
  1020.1 500.4 %reduce-scatter.17.cloned.1.call-start = ((), (), s32[]{:S(2)}) async-start(), calls=%async_computation.24 | async-start | bytes 5406720 | tf_op jit(solution)/shard_map/reduce_scatter | solution.py:541
  1044.7 71.3 %copy-start.82 = (bf16[128,32]{0,1:T(8,128)(2,1)}, bf16[128,32]{0,1:T(8,128)(2,1)S(1)}, u32[]{:S(2)}) copy-start(bf16[128,32]{0,1:T(8,128)(2,1)S(1)} %get-tuple-element.646) | copy-start | bytes 24580
  1116.0 551.8 %reduce-scatter.19.cloned.1.call-start = ((), (), s32[]{:S(2)}) async-start(), calls=%async_computation.25 | async-start | bytes 8650752 | tf_op jit(solution)/shard_map/reduce_scatter | solution.py:542
  1141.7 707.5 %reduce-scatter.21.cloned.1.call-start = ((), (), s32[]{:S(2)}) async-start(), calls=%async_computation.26 | async-start | bytes 17301504 | tf_op jit(solution)/shard_map/reduce_scatter | solution.py:543
  1151.3 952.0 %reduce-scatter.15.cloned.1.call-start = ((), (), s32[]{:S(2)}) async-start(), calls=%async_computation.23 | async-start | bytes 25952256 | tf_op jit(solution)/shard_map/reduce_scatter | solution.py:540
  1168.4 1183.5 %reduce-scatter.25.cloned.1.call-start = ((), (), s32[]{:S(2)}) async-start(), calls=%async_computation.28 | async-start | bytes 23789568 | tf_op jit(solution)/shard_map/reduce_scatter | solution.py:545
  1179.4 1665.8 %reduce-scatter.23.cloned.1.call-start = ((), (), s32[]{:S(2)}) async-start(), calls=%async_computation.27 | async-start | bytes 47579136 | tf_op jit(solution)/shard_map/reduce_scatter | solution.py:544
  1217.2 81.5 %all-to-all-start.1 = ((bf16[8,2,54,2048]{3,1,2,0:T(2,128)(2,1)}), bf16[8,2,54,2048]{3,1,2,0:T(2,128)(2,1)S(1)}, u32[]{:S(2)}, u32[]{:S(2)}) async-start(bf16[8,2,54,2048]{3,1,2,0:T(2,128)(2,1)} %copy.134), calls=%async_computation.1 | async-start | bytes 7077888 | tf_op jit(solution)/shard_map/all_to_all | solution.py:427
  1338.3 40.8 %copy-start.26 = (f32[128,2048]{1,0:T(8,128)S(1)}, f32[128,2048]{1,0:T(8,128)}, u32[]{:S(2)}) copy-start(f32[128,2048]{1,0:T(8,128)} %copy-done.24) | copy-start | bytes 3145732
  (103 other events, 424.4 us)
Sparse Core Ops, SparseCore 0:
  10.9 60.6 all-gather.9
  75.6 39.1 all-gather.11
  117.6 95.4 all-gather.13
  216.4 60.2 all-gather.15
  279.4 75.9 all-gather.17
  356.9 140.4 all-gather.23
  499.0 76.1 all-gather.25
  578.0 208.0 all-gather.19
  789.0 90.0 all-gather.21
  982.3 61.2 reduce-scatter.32
  1047.7 62.3 reduce-scatter.30
  1113.3 91.1 reduce-scatter.28
  1207.3 167.6 reduce-scatter.26
  1377.6 142.7 reduce-scatter.16
  1523.2 144.6 reduce-scatter.18
  1670.6 178.5 reduce-scatter.20
  1856.0 247.1 reduce-scatter.14
  2106.1 245.8 reduce-scatter.24
  2354.9 490.1 reduce-scatter.22
where the time goes:
time: 2870 us; the launch traced here: 2850 us
  waiting for transfers between devices  2170 us (76%)
  matrix products  315 us (11%)
  local copies, waits for them, and re-layouts  197 us (7%)
  blocking collectives  65.5 us (2%)
  other arithmetic  49.8 us (2%)
    reduce_scatter x1, waiting for transfers between devices, on_device(): lax.psum_scatter(shared_gu_grad, ('ctx', 'fsdp'), scatter_dimension=0, ti...  493 us
    reduce_scatter x1, waiting for transfers between devices, on_device(): lax.psum_scatter(query_w_grad, ('ctx', 'fsdp'), scatter_dimension=0, tile...  254 us
    reduce_scatter x1, waiting for transfers between devices, on_device(): lax.psum_scatter(shared_dn_grad, ('ctx', 'fsdp'), scatter_dimension=1, ti...  249 us
    reduce_scatter x1, waiting for transfers between devices, on_device(): lax.psum_scatter(output_w_grad, ('ctx', 'fsdp'), scatter_dimension=1, til...  181 us
    all_to_all x1, waiting for transfers between devices, on_device(): lax.all_to_all(slot_in_grad, 'ctx', split_axis=0, concat_axis=0, tiled=True)  149 us
    reduce_scatter x1, waiting for transfers between devices, on_device(): lax.psum_scatter(expand_grad, ('ctx', 'fsdp'), scatter_dimension=1, tiled...  147 us
    reduce_scatter x1, waiting for transfers between devices, on_device(): lax.psum_scatter(latent_w_grad, ('ctx', 'fsdp'), scatter_dimension=0, til...  127 us
    unnamed x21, waiting for transfers between devices  93.6 us
  transfers between devices with their start and end apart: 23, of which 19 were waited for; matrix products, arithmetic and copies ran while one was open for 15% of the time, Pallas kernels for 0%

commit v1 on v0

v1 whole, which is shorter than its diff:
```python
import math

import jax
import jax.numpy as jnp
from jax import lax
from jax.sharding import PartitionSpec as P

D = 2048
H = 16
DN = 128
DR = 64
DV = 128
KVL = 512
FF = 1408
TOP = 6
SFF = 2816


EPS = 1e-06


def positions(row_count, tok_dev, n_ctx):
    row_ids = jnp.arange(row_count, dtype=jnp.int32)
    device = row_ids // tok_dev
    within = row_ids % tok_dev
    half_rows = tok_dev // 2
    early_pos = device * half_rows + within
    late_pos = (2 * n_ctx - 1 - device) * half_rows + within - half_rows
    return jnp.where(within < half_rows, early_pos, late_pos)


def rope_tables(where_at, feat_width):
    frequency = 10000.0 ** (-2.0 * jnp.arange(feat_width // 2, dtype=jnp.float32) / feat_width)
    angles = where_at.astype(jnp.float32)[:, None] * frequency[None, :]
    return (jnp.cos(angles), jnp.sin(angles))


def rope_apply(values, cos_table, sin_table):
    half_width = values.shape[-1] // 2
    first_half = values[..., :half_width]
    second_half = values[..., half_width:]
    return jnp.concatenate(
        [
            first_half * cos_table - second_half * sin_table,
            second_half * cos_table + first_half * sin_table,
        ],
        -1,
    )


def rope_back(cotangent, cos_table, sin_table):
    half_width = cotangent.shape[-1] // 2
    first_half = cotangent[..., :half_width]
    second_half = cotangent[..., half_width:]
    return jnp.concatenate(
        [
            first_half * cos_table + second_half * sin_table,
            second_half * cos_table - first_half * sin_table,
        ],
        -1,
    )


def norm_forward(values, gain_vec):
    inverse = lax.rsqrt(jnp.mean(values * values, -1, keepdims=True) + EPS)
    return (values * inverse * gain_vec, inverse)


def norm_backward(values, inverse, gain_vec, cotangent):
    gain_grad = jnp.sum(cotangent * values * inverse, 0)
    scaled = cotangent * gain_vec
    inner_mean = jnp.mean(scaled * values, -1, keepdims=True)
    return (inverse * scaled - values * inverse * inverse * inverse * inner_mean, gain_grad)


def sort_keys(values, n_ctx, half_rows):
    split_rows = values.reshape(n_ctx, 2, half_rows, values.shape[-1])
    early_part = split_rows[:, 0].reshape(n_ctx * half_rows, values.shape[-1])
    late_part = split_rows[::-1, 1].reshape(n_ctx * half_rows, values.shape[-1])
    return jnp.concatenate([early_part, late_part], 0)


def unsort_keys(values, n_ctx, half_rows):
    early_part = values[: n_ctx * half_rows].reshape(n_ctx, 1, half_rows, values.shape[-1])
    late_part = values[n_ctx * half_rows :].reshape(n_ctx, 1, half_rows, values.shape[-1])[::-1]
    return jnp.concatenate([early_part, late_part], 1).reshape(
        2 * n_ctx * half_rows, values.shape[-1]
    )


def block_scores(
    query_lat, query_rot, query_where, sorted_lat, sorted_rot, key_start, key_rows, score_scale
):
    lat_piece = lax.dynamic_slice_in_dim(sorted_lat, key_start, key_rows, 0)
    rot_piece = lax.dynamic_slice_in_dim(sorted_rot, key_start, key_rows, 0)
    scores = (
        jnp.einsum("thc,jc->thj", query_lat, lat_piece, preferred_element_type=jnp.float32)
        + jnp.einsum("thr,jr->thj", query_rot, rot_piece, preferred_element_type=jnp.float32)
    ) * score_scale
    key_where = key_start + jnp.arange(key_rows, dtype=jnp.int32)
    allowed = key_where[None, None, :] <= query_where[:, None, None]
    return (jnp.where(allowed, scores, -jnp.inf), lat_piece, rot_piece)


def half_forward(query_lat, query_rot, query_where, sorted_lat, sorted_rot, key_rows, score_scale):
    block_count = jnp.max(query_where) // key_rows + 1
    query_rows = query_lat.shape[0]
    head_count = query_lat.shape[1]

    def stat_step(block_idx, carried):
        top_score, exp_total = carried
        scores = block_scores(
            query_lat,
            query_rot,
            query_where,
            sorted_lat,
            sorted_rot,
            block_idx * key_rows,
            key_rows,
            score_scale,
        )[0]
        new_top = jnp.maximum(top_score, jnp.max(scores, -1))
        exp_total = exp_total * jnp.exp(top_score - new_top) + jnp.sum(
            jnp.exp(scores - new_top[..., None]), -1
        )
        return (new_top, exp_total)

    start_state = (
        jnp.full((query_rows, head_count), -jnp.inf, jnp.float32),
        jnp.zeros((query_rows, head_count), jnp.float32),
    )
    top_score, exp_total = lax.fori_loop(0, block_count, stat_step, start_state)
    log_total = top_score + jnp.log(exp_total)

    def mix_step(block_idx, mixed_lat):
        scores, lat_piece, rot_piece = block_scores(
            query_lat,
            query_rot,
            query_where,
            sorted_lat,
            sorted_rot,
            block_idx * key_rows,
            key_rows,
            score_scale,
        )
        prob_bf = jnp.exp(scores - log_total[..., None]).astype(jnp.bfloat16)
        return mixed_lat + jnp.einsum(
            "thj,jc->thc", prob_bf, lat_piece, preferred_element_type=jnp.float32
        )

    mixed_lat = lax.fori_loop(
        0,
        block_count,
        mix_step,
        jnp.zeros((query_rows, head_count, sorted_lat.shape[1]), jnp.float32),
    )
    return (mixed_lat, log_total)


def half_backward(
    query_lat,
    query_rot,
    query_where,
    sorted_lat,
    sorted_rot,
    key_rows,
    score_scale,
    log_total,
    mix_grad,
    row_delta,
    lat_buffer,
    rot_buffer,
):
    block_count = jnp.max(query_where) // key_rows + 1
    query_rows = query_lat.shape[0]
    head_count = query_lat.shape[1]

    def back_step(block_idx, carried):
        lat_q_grad, rot_q_grad, lat_store, rot_store = carried
        key_start = block_idx * key_rows
        scores, lat_piece, rot_piece = block_scores(
            query_lat,
            query_rot,
            query_where,
            sorted_lat,
            sorted_rot,
            key_start,
            key_rows,
            score_scale,
        )
        prob_f = jnp.exp(scores - log_total[..., None])
        prob_grad = jnp.einsum(
            "thc,jc->thj", mix_grad, lat_piece, preferred_element_type=jnp.float32
        )
        score_grad = (prob_f * (prob_grad - row_delta[..., None]) * score_scale).astype(
            jnp.bfloat16
        )
        lat_q_grad = lat_q_grad + jnp.einsum(
            "thj,jc->thc", score_grad, lat_piece, preferred_element_type=jnp.float32
        )
        rot_q_grad = rot_q_grad + jnp.einsum(
            "thj,jr->thr", score_grad, rot_piece, preferred_element_type=jnp.float32
        )
        lat_term = jnp.einsum(
            "thj,thc->jc", score_grad, query_lat, preferred_element_type=jnp.float32
        ) + jnp.einsum(
            "thj,thc->jc", prob_f.astype(jnp.bfloat16), mix_grad, preferred_element_type=jnp.float32
        )
        rot_term = jnp.einsum(
            "thj,thr->jr", score_grad, query_rot, preferred_element_type=jnp.float32
        )
        lat_store = lax.dynamic_update_slice_in_dim(
            lat_store,
            lax.dynamic_slice_in_dim(lat_store, key_start, key_rows, 0) + lat_term,
            key_start,
            0,
        )
        rot_store = lax.dynamic_update_slice_in_dim(
            rot_store,
            lax.dynamic_slice_in_dim(rot_store, key_start, key_rows, 0) + rot_term,
            key_start,
            0,
        )
        return (lat_q_grad, rot_q_grad, lat_store, rot_store)

    start_state = (
        jnp.zeros((query_rows, head_count, sorted_lat.shape[1]), jnp.float32),
        jnp.zeros((query_rows, head_count, sorted_rot.shape[1]), jnp.float32),
        lat_buffer,
        rot_buffer,
    )
    return lax.fori_loop(0, block_count, back_step, start_state)


def fsdp_swap(values, distance):
    count = lax.axis_size("fsdp")
    return lax.ppermute(values, "fsdp", [(at, at ^ distance) for at in range(count)])


def fsdp_pieces(own):
    near = fsdp_swap(own, 1)
    far = fsdp_swap(own, 2)
    return [own, near, far, fsdp_swap(far, 1)]


def swap_chunks(values, rank, axis):
    width = values.shape[axis] // 4
    return jnp.concatenate(
        [lax.dynamic_slice_in_dim(values, (rank ^ k) * width, width, axis) for k in range(4)], axis
    )


def fsdp_reduce(blocks, rank):
    rel = [lax.dynamic_index_in_dim(blocks, rank ^ k, 0, False) for k in range(4)]
    mine = rel[0].astype(jnp.float32) + fsdp_swap(rel[1], 1).astype(jnp.float32)
    other = rel[2].astype(jnp.float32) + fsdp_swap(rel[3], 1).astype(jnp.float32)
    return mine + fsdp_swap(other.astype(jnp.bfloat16), 2).astype(jnp.float32)


def ctx_gather(values):
    return lax.all_gather(values, "ctx", axis=0, tiled=True)


def ctx_scatter(values):
    return lax.psum_scatter(values, "ctx", scatter_dimension=0, tiled=True)


def ctx_exchange(values):
    return lax.all_to_all(values, "ctx", split_axis=0, concat_axis=0, tiled=True)


def dot_f32(left, right, dims=((1,), (0,))):
    return lax.dot_general(left, right, (dims, ((), ())), preferred_element_type=jnp.float32)


def pad_last(values, width):
    return jnp.pad(values, [(0, 0)] * (values.ndim - 1) + [(0, width - values.shape[-1])])


def columns_by_dest(values, count):
    rows = values.shape[0]
    return values.reshape(rows, count, -1).transpose(1, 0, 2)


def rows_by_dest(values, count):
    cols = values.shape[1]
    return values.reshape(count, -1, cols).transpose(0, 2, 1)


def whole_rows(pieces, rank):
    stacked = swap_chunks(jnp.concatenate([p[None] for p in pieces], 0), rank, 0)
    return stacked.transpose(1, 0, 2, 3).reshape(-1, stacked.shape[-1])


def shard_rows(grads, n_ctx, rank):
    width = grads.shape[-1]
    blocks = grads.astype(jnp.bfloat16).reshape(n_ctx, 4, -1, width).transpose(1, 0, 2, 3)
    return fsdp_reduce(blocks, rank)


def attention_heads(rows_q, rows_rot, lat_all, rot_all, allowed, score_scale):
    query = jnp.concatenate([rows_q, rows_rot], -1)
    key = jnp.concatenate([lat_all, rot_all], -1)
    scores = dot_f32(query, key, ((1,), (1,))) * score_scale
    scores = jnp.where(allowed, scores, -jnp.inf)
    top_score = jnp.max(scores, -1, keepdims=True)
    log_total = top_score + jnp.log(jnp.sum(jnp.exp(scores - top_score), -1, keepdims=True))
    probs = jnp.exp(scores - log_total)
    mixed = dot_f32(probs.astype(jnp.bfloat16), lat_all)
    return mixed, log_total


def attention_heads_back(
    rows_q, rows_rot, lat_all, rot_all, allowed, score_scale, log_total, mix_grad, delta
):
    query = jnp.concatenate([rows_q, rows_rot], -1)
    key = jnp.concatenate([lat_all, rot_all], -1)
    scores = dot_f32(query, key, ((1,), (1,))) * score_scale
    probs = jnp.where(allowed, jnp.exp(scores - log_total), 0.0)
    prob_grad = dot_f32(mix_grad, lat_all, ((1,), (1,)))
    score_grad = (probs * (prob_grad - delta) * score_scale).astype(jnp.bfloat16)
    query_g = dot_f32(score_grad, key)
    key_g = dot_f32(score_grad, query, ((0,), (0,)))
    lat_g = dot_f32(probs.astype(jnp.bfloat16), mix_grad, ((0,), (0,)))
    return query_g, key_g[:, :KVL] + lat_g, key_g[:, KVL:]


def on_device(
    hidden_in,
    out_grad,
    norm_gains,
    w_query,
    w_latent,
    w_expand,
    w_output,
    shared_gate_up,
    shared_down,
    expert_gate_up,
    expert_down,
    expert_ids,
    expert_gates,
):
    n_ctx = lax.axis_size("ctx")
    ctx_rank = lax.axis_index("ctx")
    rank = lax.axis_index("fsdp")
    split_heads = H % n_ctx == 0
    tok_dev = hidden_in.shape[1]
    half_rows = tok_dev // 2
    length = tok_dev * n_ctx
    score_scale = 1.0 / math.sqrt(DN + DR)
    gain_in = norm_gains[:D]
    gain_mid = norm_gains[D : 2 * D]
    gain_lat = norm_gains[2 * D :]
    where_all = positions(length, tok_dev, n_ctx)
    query_where = lax.dynamic_slice_in_dim(where_all, ctx_rank * tok_dev, tok_dev, 0)
    tokens = hidden_in[0].astype(jnp.float32)
    first_row = ctx_rank * tok_dev

    def own_rows(values):
        return lax.dynamic_slice_in_dim(values, first_row, tok_dev, 0)

    sff_dev = SFF // n_ctx
    sff_pad = -(-sff_dev // 128) * 128
    gate_send = pad_last(columns_by_dest(shared_gate_up[:, :SFF], n_ctx), sff_pad)
    up_send = pad_last(columns_by_dest(shared_gate_up[:, SFF:], n_ctx), sff_pad)
    down_send = pad_last(rows_by_dest(shared_down, n_ctx), sff_pad)
    shared_send = jnp.concatenate([gate_send, up_send, down_send], -1)
    attn = attention_split if split_heads else attention_whole
    attn_state = attn(
        hidden_in[0], tokens, norm_gains, w_query, w_latent, w_expand, w_output, where_all, score_scale
    )
    resid_mid, attn_backward = attn_state
    shared_got = ctx_exchange(shared_send)
    shared_full = whole_rows(fsdp_pieces(shared_got), rank)
    shared_rel = swap_chunks(shared_full, rank, 0)
    shared_gu = shared_rel[:, : 2 * sff_pad]
    shared_dn = shared_rel[:, 2 * sff_pad :]

    gu_rel = jnp.concatenate(fsdp_pieces(expert_gate_up), 1)
    dn_rel = jnp.concatenate(fsdp_pieces(expert_down), 2)

    exp_local = expert_gate_up.shape[0]
    n_exp = exp_local * n_ctx
    capacity = max(2, 9 * tok_dev * TOP // (8 * n_exp))
    slots = capacity * n_ctx
    gates = expert_gates[0]
    gate_hi = gates.astype(jnp.bfloat16)
    gate_rest = gates - gate_hi.astype(jnp.float32)
    gate_md = gate_rest.astype(jnp.bfloat16)
    gate_lo = (gate_rest - gate_md.astype(jnp.float32)).astype(jnp.bfloat16)
    routes = pad_last(
        jnp.concatenate([expert_ids[0].astype(jnp.bfloat16), gate_hi, gate_md, gate_lo], -1), 128
    )
    grads_all = ctx_gather(
        jnp.concatenate([swap_chunks(out_grad[0], rank, 1), routes], -1)
    )
    routes_all = grads_all[:, D:]
    grads_all = grads_all[:, :D]
    ids_all = routes_all[:, :TOP].astype(jnp.float32)
    gates_all = (
        routes_all[:, TOP : 2 * TOP].astype(jnp.float32)
        + routes_all[:, 2 * TOP : 3 * TOP].astype(jnp.float32)
        + routes_all[:, 3 * TOP : 4 * TOP].astype(jnp.float32)
    )
    local_ids = (ctx_rank * exp_local + jnp.arange(exp_local)).astype(jnp.float32)
    chosen = ids_all.T[None] == local_ids[:, None, None]
    named = jnp.any(chosen, 1)
    gate_of = jnp.sum(jnp.where(chosen, gates_all.T[None], 0.0), 1)
    place = jnp.cumsum(named.astype(jnp.int32), 1) - 1
    slot_ids = jnp.arange(slots, dtype=jnp.int32)
    taken = (place[:, None, :] == slot_ids[None, :, None]) & named[:, None, :]
    pick = taken.astype(jnp.bfloat16).reshape(exp_local * slots, length)
    slot_gate = jnp.sum(jnp.where(taken, gate_of[:, None, :], 0.0), -1).reshape(-1, 1)

    normed_mid, inv_mid = norm_forward(resid_mid, gain_mid)
    mid_all = ctx_gather(swap_chunks(normed_mid.astype(jnp.bfloat16), rank, 1))

    s_both = dot_f32(mid_all, shared_gu)
    s_gate = s_both[:, :sff_pad]
    s_up = s_both[:, sff_pad:]
    s_sig = jax.nn.sigmoid(s_gate)
    s_silu = s_gate * s_sig
    s_act = (s_silu * s_up).astype(jnp.bfloat16)
    s_act_grad = dot_f32(grads_all, shared_dn)
    s_both_grad = jnp.concatenate(
        [s_act_grad * s_up * s_sig * (1.0 + s_gate * (1.0 - s_sig)), s_act_grad * s_silu], -1
    ).astype(jnp.bfloat16)

    x_slots = dot_f32(pick, mid_all).astype(jnp.bfloat16)
    y_slots = (dot_f32(pick, grads_all) * slot_gate).astype(jnp.bfloat16)
    x_exp = x_slots.reshape(exp_local, slots, D)
    y_exp = y_slots.reshape(exp_local, slots, D)
    e_both = jnp.einsum("esd,edf->esf", x_exp, gu_rel, preferred_element_type=jnp.float32)
    e_gate = e_both[..., :FF]
    e_up = e_both[..., FF:]
    e_sig = jax.nn.sigmoid(e_gate)
    e_silu = e_gate * e_sig
    e_act = (e_silu * e_up).astype(jnp.bfloat16)
    e_act_grad = jnp.einsum("esd,efd->esf", y_exp, dn_rel, preferred_element_type=jnp.float32)
    e_both_grad = jnp.concatenate(
        [e_act_grad * e_up * e_sig * (1.0 + e_gate * (1.0 - e_sig)), e_act_grad * e_silu], -1
    ).astype(jnp.bfloat16)
    in_slots = jnp.einsum("esf,edf->esd", e_both_grad, gu_rel, preferred_element_type=jnp.float32)
    in_slots = in_slots.astype(jnp.bfloat16).reshape(-1, D)
    mid_grad_part = dot_f32(s_both_grad, shared_gu, ((1,), (1,))) + dot_f32(
        pick, in_slots, ((0,), (0,))
    )
    mid_grad = swap_chunks(
        ctx_scatter(mid_grad_part.astype(jnp.bfloat16)).astype(jnp.float32), rank, 1
    )

    out_slots = jnp.einsum("esf,efd->esd", e_act, dn_rel, preferred_element_type=jnp.float32)
    out_slots = out_slots.astype(jnp.bfloat16).astype(jnp.float32).reshape(-1, D) * slot_gate
    out_part = dot_f32(s_act, shared_dn, ((1,), (1,))) + dot_f32(
        pick, out_slots.astype(jnp.bfloat16), ((0,), (0,))
    )
    ffn_out = swap_chunks(ctx_scatter(out_part.astype(jnp.bfloat16)), rank, 1)
    hidden_out = (resid_mid + ffn_out.astype(jnp.float32)).astype(jnp.bfloat16)

    x_abs = swap_chunks(x_exp, rank, 2)
    y_abs = swap_chunks(y_exp, rank, 2)
    gu_grad = jnp.einsum("esd,esf->edf", x_abs, e_both_grad, preferred_element_type=jnp.float32)
    dn_grad = jnp.einsum("esf,esd->efd", e_act, y_abs, preferred_element_type=jnp.float32)
    gu_grad = lax.psum_scatter(
        gu_grad.astype(jnp.bfloat16), "fsdp", scatter_dimension=1, tiled=True
    ).astype(jnp.float32)
    dn_grad = lax.psum_scatter(
        dn_grad.astype(jnp.bfloat16), "fsdp", scatter_dimension=2, tiled=True
    ).astype(jnp.float32)

    shared_grad = jnp.concatenate(
        [
            dot_f32(mid_all, s_both_grad, ((0,), (0,))),
            dot_f32(grads_all, s_act, ((0,), (0,))),
        ],
        -1,
    )
    shared_grad = shard_rows(swap_chunks(shared_grad, rank, 0), n_ctx, rank).astype(jnp.bfloat16)
    shared_grad = ctx_exchange(shared_grad).astype(jnp.float32)
    gate_grad = shared_grad[:, :, :sff_dev].transpose(1, 0, 2).reshape(-1, SFF)
    up_grad = shared_grad[:, :, sff_pad : sff_pad + sff_dev].transpose(1, 0, 2).reshape(-1, SFF)
    shared_gu_grad = jnp.concatenate([gate_grad, up_grad], -1)
    down_grad = shared_grad[:, :, 2 * sff_pad : 2 * sff_pad + sff_dev]
    shared_dn_grad = down_grad.transpose(0, 2, 1).reshape(SFF, -1)

    resid_norm_grad, gain_mid_grad = norm_backward(resid_mid, inv_mid, gain_mid, mid_grad)
    resid_grad = out_grad[0].astype(jnp.float32) + resid_norm_grad
    token_grad, gain_in_grad, gain_lat_grad, query_w, latent_w, expand_w, output_w = attn_backward(
        resid_grad.astype(jnp.bfloat16)
    )
    hidden_in_grad = (resid_grad + token_grad).astype(jnp.bfloat16)
    gains_grad = lax.psum_scatter(
        jnp.concatenate([gain_in_grad, gain_mid_grad, gain_lat_grad], 0),
        ("ctx", "fsdp"),
        scatter_dimension=0,
        tiled=True,
    )
    return (
        hidden_out[None],
        hidden_in_grad[None],
        gains_grad,
        query_w,
        latent_w,
        expand_w,
        output_w,
        shared_gu_grad,
        shared_dn_grad,
        gu_grad,
        dn_grad,
    )


def attention_split(
    hidden_bf, tokens, norm_gains, w_query, w_latent, w_expand, w_output, where_all, score_scale
):
    n_ctx = lax.axis_size("ctx")
    ctx_rank = lax.axis_index("ctx")
    rank = lax.axis_index("fsdp")
    tok_dev = hidden_bf.shape[0]
    length = tok_dev * n_ctx
    heads = H // n_ctx
    gain_in = norm_gains[:D]
    gain_lat = norm_gains[2 * D :]
    first_row = ctx_rank * tok_dev

    def own_rows(values):
        return lax.dynamic_slice_in_dim(values, first_row, tok_dev, 0)

    rows = w_query.shape[0]
    by_head = w_query.reshape(rows, n_ctx, heads, DN + DR)
    query_send = jnp.concatenate(
        [
            by_head[..., :DN].reshape(rows, n_ctx, heads * DN),
            by_head[..., DN:].reshape(rows, n_ctx, heads * DR),
        ],
        -1,
    ).transpose(1, 0, 2)
    output_send = rows_by_dest(w_output, n_ctx)
    latent_send = jnp.broadcast_to(w_latent[None], (n_ctx,) + w_latent.shape)
    got = ctx_exchange(jnp.concatenate([query_send, output_send, latent_send], -1))
    expand_own = w_expand.reshape(n_ctx, rows, -1)
    pieces = fsdp_pieces(jnp.concatenate([got, expand_own], -1))
    n_wide, r_wide, o_wide = heads * DN, heads * DR, heads * DV
    marks = [0, n_wide + r_wide, n_wide + r_wide + o_wide, n_wide + r_wide + o_wide + KVL + DR]
    full = whole_rows(pieces, rank)
    query_full = full[:, : marks[1]]
    output_full = full[:, marks[1] : marks[2]]
    latent_full = full[:, marks[2] : marks[3]]
    expand_full = (
        full[:, marks[3] :].reshape(n_ctx, 4, rows, -1).transpose(0, 2, 1, 3).reshape(KVL, -1)
    )
    expand_heads = expand_full.reshape(KVL, heads, DN + DV)
    key_up = [expand_heads[:, j, :DN] for j in range(heads)]
    value_up = [expand_heads[:, j, DN:] for j in range(heads)]

    hidden_all = ctx_gather(hidden_bf).astype(jnp.float32)
    cos_table, sin_table = rope_tables(where_all, DR)
    normed_all, inv_all = norm_forward(hidden_all, gain_in)
    normed_bf = normed_all.astype(jnp.bfloat16)
    query_all = dot_f32(normed_bf, query_full)
    compressed = dot_f32(normed_bf, latent_full)
    lat_raw = compressed[:, :KVL]
    lat_normed, inv_lat = norm_forward(lat_raw, gain_lat)
    latent = lat_normed.astype(jnp.bfloat16)
    key_rot = rope_apply(compressed[:, KVL:], cos_table, sin_table).astype(jnp.bfloat16)
    allowed = where_all[None, :] <= where_all[:, None]
    saved = []
    out_part = []
    for j in range(heads):
        nope = query_all[:, j * DN : (j + 1) * DN].astype(jnp.bfloat16)
        rot = rope_apply(
            query_all[:, n_wide + j * DR : n_wide + (j + 1) * DR], cos_table, sin_table
        ).astype(jnp.bfloat16)
        lat_q = dot_f32(nope, key_up[j], ((1,), (1,))).astype(jnp.bfloat16)
        mixed, log_total = attention_heads(lat_q, rot, latent, key_rot, allowed, score_scale)
        mixed_bf = mixed.astype(jnp.bfloat16)
        out_part.append(dot_f32(mixed_bf, value_up[j]).astype(jnp.bfloat16))
        saved.append((nope, rot, lat_q, mixed, mixed_bf, log_total))
    heads_out = jnp.concatenate(out_part, -1)
    attn_part = dot_f32(heads_out, output_full, ((1,), (1,))).astype(jnp.bfloat16)
    resid_mid = tokens + ctx_scatter(attn_part).astype(jnp.float32)

    def backward(resid_bf):
        resid_all = ctx_gather(resid_bf)
        output_g = dot_f32(resid_all, heads_out, ((0,), (0,)))
        heads_grad = dot_f32(resid_all, output_full).astype(jnp.bfloat16)
        lat_total = jnp.zeros((length, KVL), jnp.float32)
        rot_total = jnp.zeros((length, DR), jnp.float32)
        expand_parts = []
        nope_parts = []
        rope_parts = []
        for j in range(heads):
            nope, rot, lat_q, mixed, mixed_bf, log_total = saved[j]
            head_g = heads_grad[:, j * DV : (j + 1) * DV]
            value_g = dot_f32(mixed_bf, head_g, ((0,), (0,)))
            mix_grad = dot_f32(head_g, value_up[j], ((1,), (1,))).astype(jnp.bfloat16)
            delta = jnp.sum(mix_grad.astype(jnp.float32) * mixed, -1, keepdims=True)
            query_g, lat_g, rot_g = attention_heads_back(
                lat_q, rot, latent, key_rot, allowed, score_scale, log_total, mix_grad, delta
            )
            lat_total = lat_total + lat_g
            rot_total = rot_total + rot_g
            lat_q_grad = query_g[:, :KVL].astype(jnp.bfloat16)
            key_g = dot_f32(lat_q_grad, nope, ((0,), (0,)))
            nope_parts.append(dot_f32(lat_q_grad, key_up[j]))
            rope_parts.append(rope_back(query_g[:, KVL:], cos_table, sin_table))
            expand_parts += [key_g, value_g]
        key_terms = ctx_scatter(
            jnp.concatenate([lat_total, rot_total], -1).astype(jnp.bfloat16)
        ).astype(jnp.float32)
        query_grad = jnp.concatenate(nope_parts + rope_parts, -1).astype(jnp.bfloat16)
        query_g_w = dot_f32(normed_bf, query_grad, ((0,), (0,)))
        in_part = dot_f32(query_grad, query_full, ((1,), (1,))).astype(jnp.bfloat16)
        in_grad = ctx_scatter(in_part).astype(jnp.float32)
        own_cos, own_sin = own_rows(cos_table), own_rows(sin_table)
        lat_in_grad, gain_lat_grad = norm_backward(
            own_rows(lat_raw), own_rows(inv_lat), gain_lat, key_terms[:, :KVL]
        )
        compressed_grad = jnp.concatenate(
            [lat_in_grad, rope_back(key_terms[:, KVL:], own_cos, own_sin)], -1
        ).astype(jnp.bfloat16)
        latent_g = dot_f32(own_rows(normed_bf), compressed_grad, ((0,), (0,)))
        in_grad = in_grad + dot_f32(compressed_grad, latent_full, ((1,), (1,)))
        token_grad, gain_in_grad = norm_backward(tokens, own_rows(inv_all), gain_in, in_grad)
        expand_g = jnp.concatenate(expand_parts, -1)
        expand_cols = (
            expand_g.reshape(n_ctx, rows, 4, -1).transpose(0, 2, 1, 3).reshape(D, -1)
        )
        terms = shard_rows(
            jnp.concatenate([query_g_w, output_g, latent_g, expand_cols], -1), n_ctx, rank
        )
        expand_w = terms[:, :, marks[3] :].reshape(KVL, -1)
        sent = ctx_exchange(terms[:, :, : marks[3]].astype(jnp.bfloat16)).astype(jnp.float32)
        nope_w = sent[:, :, :n_wide].reshape(n_ctx, rows, heads, DN)
        rot_w = sent[:, :, n_wide : marks[1]].reshape(n_ctx, rows, heads, DR)
        query_w = (
            jnp.concatenate([nope_w, rot_w], -1).transpose(1, 0, 2, 3).reshape(rows, -1)
        )
        output_w = sent[:, :, marks[1] : marks[2]].transpose(0, 2, 1).reshape(H * DV, -1)
        latent_w = jnp.sum(sent[:, :, marks[2] :], 0)
        return token_grad, gain_in_grad, gain_lat_grad, query_w, latent_w, expand_w, output_w

    return resid_mid, backward


def attention_whole(
    hidden_bf, tokens, norm_gains, w_query, w_latent, w_expand, w_output, where_all, score_scale
):
    n_ctx = lax.axis_size("ctx")
    ctx_rank = lax.axis_index("ctx")
    tok_dev = hidden_bf.shape[0]
    half_rows = tok_dev // 2
    length = tok_dev * n_ctx
    key_rows = min(256, length)
    halves = ((0, half_rows), (half_rows, tok_dev))
    gain_in = norm_gains[:D]
    gain_lat = norm_gains[2 * D :]
    query_where = lax.dynamic_slice_in_dim(where_all, ctx_rank * tok_dev, tok_dev, 0)
    cos_table, sin_table = rope_tables(query_where, DR)
    both = ("ctx", "fsdp")
    query_full = lax.all_gather(w_query, both, axis=0, tiled=True)
    latent_full = lax.all_gather(w_latent, both, axis=0, tiled=True)
    expand_heads = lax.all_gather(w_expand, both, axis=1, tiled=True).reshape(KVL, H, DN + DV)
    output_full = lax.all_gather(w_output, both, axis=1, tiled=True)
    key_up = expand_heads[:, :, :DN]
    value_up = expand_heads[:, :, DN:]
    normed_in, inv_in = norm_forward(tokens, gain_in)
    normed_bf = normed_in.astype(jnp.bfloat16)
    query_all = dot_f32(normed_bf, query_full).reshape(tok_dev, H, DN + DR)
    query_nope = query_all[:, :, :DN].astype(jnp.bfloat16)
    query_rot = rope_apply(
        query_all[:, :, DN:], cos_table[:, None, :], sin_table[:, None, :]
    ).astype(jnp.bfloat16)
    query_lat = jnp.einsum(
        "thn,chn->thc", query_nope, key_up, preferred_element_type=jnp.float32
    ).astype(jnp.bfloat16)
    compressed = dot_f32(normed_bf, latent_full)
    lat_raw = compressed[:, :KVL]
    lat_normed, inv_lat = norm_forward(lat_raw, gain_lat)
    key_rot = rope_apply(compressed[:, KVL:], cos_table, sin_table).astype(jnp.bfloat16)
    sorted_lat = sort_keys(ctx_gather(lat_normed.astype(jnp.bfloat16)), n_ctx, half_rows)
    sorted_rot = sort_keys(ctx_gather(key_rot), n_ctx, half_rows)
    parts = [
        half_forward(
            query_lat[lo:hi], query_rot[lo:hi], query_where[lo:hi],
            sorted_lat, sorted_rot, key_rows, score_scale,
        )
        for lo, hi in halves
    ]
    mixed_lat = jnp.concatenate([p[0] for p in parts], 0)
    log_total = jnp.concatenate([p[1] for p in parts], 0)
    mixed_bf = mixed_lat.astype(jnp.bfloat16)
    heads_out = (
        jnp.einsum("thc,chv->thv", mixed_bf, value_up, preferred_element_type=jnp.float32)
        .reshape(tok_dev, H * DV)
        .astype(jnp.bfloat16)
    )
    resid_mid = tokens + dot_f32(heads_out, output_full)

    def backward(resid_bf):
        output_g = dot_f32(heads_out, resid_bf, ((0,), (0,)))
        heads_grad = (
            dot_f32(resid_bf, output_full, ((1,), (1,)))
            .astype(jnp.bfloat16)
            .reshape(tok_dev, H, DV)
        )
        value_grad = jnp.einsum(
            "thc,thv->chv", mixed_bf, heads_grad, preferred_element_type=jnp.float32
        )
        mix_grad = jnp.einsum(
            "thv,chv->thc", heads_grad, value_up, preferred_element_type=jnp.float32
        ).astype(jnp.bfloat16)
        row_delta = jnp.sum(mix_grad.astype(jnp.float32) * mixed_lat, -1)
        lat_buffer = jnp.zeros((length, KVL), jnp.float32)
        rot_buffer = jnp.zeros((length, DR), jnp.float32)
        lat_q_parts = []
        rot_q_parts = []
        for lo, hi in halves:
            lat_q, rot_q, lat_buffer, rot_buffer = half_backward(
                query_lat[lo:hi], query_rot[lo:hi], query_where[lo:hi],
                sorted_lat, sorted_rot, key_rows, score_scale,
                log_total[lo:hi], mix_grad[lo:hi], row_delta[lo:hi],
                lat_buffer, rot_buffer,
            )
            lat_q_parts.append(lat_q)
            rot_q_parts.append(rot_q)
        latent_terms = unsort_keys(lat_buffer, n_ctx, half_rows)
        rot_terms = unsort_keys(rot_buffer, n_ctx, half_rows)
        latent_grad = ctx_scatter(latent_terms.astype(jnp.bfloat16)).astype(jnp.float32)
        key_rot_grad = ctx_scatter(rot_terms.astype(jnp.bfloat16)).astype(jnp.float32)
        query_lat_grad = jnp.concatenate(lat_q_parts, 0).astype(jnp.bfloat16)
        rot_q_grad = jnp.concatenate(rot_q_parts, 0)
        key_grad = jnp.einsum(
            "thc,thn->chn", query_lat_grad, query_nope, preferred_element_type=jnp.float32
        )
        nope_grad = jnp.einsum(
            "thc,chn->thn", query_lat_grad, key_up, preferred_element_type=jnp.float32
        )
        query_grad = (
            jnp.concatenate(
                [nope_grad, rope_back(rot_q_grad, cos_table[:, None, :], sin_table[:, None, :])],
                -1,
            )
            .reshape(tok_dev, H * (DN + DR))
            .astype(jnp.bfloat16)
        )
        query_g = dot_f32(normed_bf, query_grad, ((0,), (0,)))
        in_grad = dot_f32(query_grad, query_full, ((1,), (1,)))
        lat_in_grad, gain_lat_grad = norm_backward(lat_raw, inv_lat, gain_lat, latent_grad)
        compressed_grad = jnp.concatenate(
            [lat_in_grad, rope_back(key_rot_grad, cos_table, sin_table)], -1
        ).astype(jnp.bfloat16)
        latent_g = dot_f32(normed_bf, compressed_grad, ((0,), (0,)))
        in_grad = in_grad + dot_f32(compressed_grad, latent_full, ((1,), (1,)))
        token_grad, gain_in_grad = norm_backward(tokens, inv_in, gain_in, in_grad)
        expand_g = jnp.concatenate([key_grad, value_grad], -1).reshape(KVL, H * (DN + DV))
        scattered = [
            lax.psum_scatter(g.astype(jnp.bfloat16), both, scatter_dimension=at, tiled=True).astype(
                jnp.float32
            )
            for g, at in ((query_g, 0), (latent_g, 0), (expand_g, 1), (output_g, 1))
        ]
        return (token_grad, gain_in_grad, gain_lat_grad, *scattered)

    return resid_mid, backward


def solution(mesh):
    placed = (
        P("fsdp", "ctx", None),
        P("fsdp", "ctx", None),
        P(),
        P(("ctx", "fsdp"), None),
        P(("ctx", "fsdp"), None),
        P(None, ("ctx", "fsdp")),
        P(None, ("ctx", "fsdp")),
        P(("ctx", "fsdp"), None),
        P(None, ("ctx", "fsdp")),
        P("ctx", "fsdp", None),
        P("ctx", None, "fsdp"),
        P("fsdp", "ctx", None),
        P("fsdp", "ctx", None),
    )
    return jax.shard_map(
        on_device,
        mesh=mesh,
        in_specs=placed,
        out_specs=(
            P("fsdp", "ctx", None),
            P("fsdp", "ctx", None),
            P(("ctx", "fsdp")),
            P(("ctx", "fsdp"), None),
            P(("ctx", "fsdp"), None),
            P(None, ("ctx", "fsdp")),
            P(None, ("ctx", "fsdp")),
            P(("ctx", "fsdp"), None),
            P(None, ("ctx", "fsdp")),
            P("ctx", "fsdp", None),
            P("ctx", None, "fsdp"),
        ),
        check_vma=False,
    )
```

time: 2870 us -> 1300 us (0.45)
  waiting for transfers between devices: 2170 us -> 792 us
  matrix products: 315 us -> 207 us
  local copies, waits for them, and re-layouts: 197 us -> 121 us
    reduce_scatter x8 -> x6, waiting for transfers between devices: 1450 us -> 321 us  [the longest x4 197 us: ctx_scatter(): return lax.psum_scatter(values, 'ctx', scatter_dimension=0, tiled=True)]
    ppermute x0 -> x18, waiting for transfers between devices: none -> 229 us  [fsdp_swap(): lax.ppermute(values, 'fsdp', [(at, at ^ distance) for at in range(count)])]
    all_gather x9 -> x4, waiting for transfers between devices: 320 us -> 101 us  [ctx_gather(): return lax.all_gather(values, 'ctx', axis=0, tiled=True)]
    all_to_all x4, waiting for transfers between devices: 306 us -> 141 us  [ctx_exchange(): lax.all_to_all(values, 'ctx', split_axis=0, concat_axis=0, tiled=True)]
    dot_general x88 -> x48, matrix products: 315 us -> 207 us  [the longest x43 131 us: dot_f32(): lax.dot_general(left, right, (dims, ((), ())), preferred_element_type=jnp...]
    unnamed x21 -> x12, waiting for transfers between devices: 93.6 us -> 0.85 us
    reshape x12 -> x19, local copies, waits for them, and re-layouts: 48.6 us -> 15.6 us  [the longest x1 2.37 us: on_device(): shared_grad[:, :, sff_pad:sff_pad + sff_dev].transpose(1, 0, 2)]
  transfers between devices with their start and end apart: 23 -> 33, of which waited for: 19 -> 15; matrix products, arithmetic and copies ran while one was open for 15% -> 19% of each run, Pallas kernels for 0% -> 0%
where the time goes in v1:
time: 1300 us; the launch traced here: 1290 us
  waiting for transfers between devices  792 us (61%)
  matrix products  207 us (16%)
  local copies, waits for them, and re-layouts  121 us (9%)
  other arithmetic  77.8 us (6%)
  blocking collectives  40.5 us (3%)
  starting transfers between devices  36 us (3%)
  between operations  16.5 us (1%)
    ppermute x18, waiting for transfers between devices, fsdp_swap(): lax.ppermute(values, 'fsdp', [(at, at ^ distance) for at in range(count)])  229 us
    reduce_scatter x4, waiting for transfers between devices, ctx_scatter(): return lax.psum_scatter(values, 'ctx', scatter_dimension=0, tiled=True)  197 us
    all_to_all x4, waiting for transfers between devices, ctx_exchange(): lax.all_to_all(values, 'ctx', split_axis=0, concat_axis=0, tiled=True)  141 us
    dot_general x43, matrix products, dot_f32(): lax.dot_general(left, right, (dims, ((), ())), preferred_element_type=jnp...  131 us
    reduce_scatter x1, waiting for transfers between devices, on_device(): lax.psum_scatter(gu_grad.astype(jnp.bfloat16), 'fsdp', scatter_dimension=...  124 us
    all_gather x4, waiting for transfers between devices, ctx_gather(): return lax.all_gather(values, 'ctx', axis=0, tiled=True)  101 us
    unnamed x245, local copies, waits for them, and re-layouts  48.8 us
    unnamed x1, blocking collectives  40.5 us
  transfers between devices with their start and end apart: 33, of which 15 were waited for; matrix products, arithmetic and copies ran while one was open for 19% of the time, Pallas kernels for 0%

profile of v1, /device:TPU:0, one launch (start us, length us, event | category | flops | bytes accessed | tf_op | source)
XLA Modules:
  0.0 1291.4 jit_solution(4079077475852326437)
XLA Ops:
  11.0 7.3 all-to-all-start
  19.1 46.3 %all-to-all-done = bf16[8,64,1216]{2,1,0:T(8,128)(2,1)S(1)} async-done(((bf16[8,64,1216]{2,1,0:T(8,128)(2,1)}), bf16[8,64,1216]{2,1,0:T(8,128)(2,1)S(1)}, u32[]{:S(2)}, u32[]{:S(2)}) %all-to-all-start) | async-done | bytes 1245216 | tf_op jit(solution)/shard_map/all_to_all | solution.py:269
  68.4 28.1 %collective-permute-done.1 = bf16[8,64,1344]{2,1,0:T(8,128)(2,1)S(1)} collective-permute-done((bf16[8,64,1344]{2,1,0:T(8,128)(2,1)}, bf16[8,64,1344]{2,1,0:T(8,128)(2,1)S(1)}, u32[]{:S(2)}, u32[]{:S(2)}) %collective-permute-start.1) | collective-permute-done | bytes 1376288 | tf_op jit(solution)/shard_map/ppermute | solution.py:237
  99.9 3.8 pad_maximum_fusion
  149.6 8.8 all-to-all-start.1
  159.9 54.9 %all-to-all-done.1 = bf16[8,64,1152]{2,1,0:T(8,128)(2,1)S(1)} async-done(((bf16[8,64,1152]{2,1,0:T(8,128)(2,1)}), bf16[8,64,1152]{2,1,0:T(8,128)(2,1)S(1)}, u32[]{:S(2)}, u32[]{:S(2)}) %all-to-all-start.1) | async-done | bytes 1179680 | tf_op jit(solution)/shard_map/all_to_all | solution.py:269
  215.0 5.8 constant_dynamic-update-slice_fusion.8
  222.6 111.4 %collective-permute-done.10 = bf16[2,1408,512]{2,1,0:T(8,128)(2,1)} collective-permute-done((bf16[2,1408,512]{2,1,0:T(8,128)(2,1)}, bf16[2,1408,512]{2,1,0:T(8,128)(2,1)}, u32[]{:S(2)}, u32[]{:S(2)}) %collective-permute-start.10) | collective-permute-done | bytes 2883616 | tf_op jit(solution)/shard_map/ppermute | solution.py:237
  338.0 20.3 %collective-permute-done.4 = bf16[8,64,1152]{2,1,0:T(8,128)(2,1)S(1)} collective-permute-done((bf16[8,64,1152]{2,1,0:T(8,128)(2,1)S(1)}, bf16[8,64,1152]{2,1,0:T(8,128)(2,1)S(1)}, u32[]{:S(2)}, u32[]{:S(2)}) %collective-permute-start.4) | collective-permute-done | bytes 1179680 | tf_op jit(solution)/shard_map/ppermute | solution.py:237
  361.9 3.6 constant_dynamic-update-slice_fusion.10
  372.4 3.8 constant_dynamic-update-slice_fusion.9
  376.2 5.5 constant_dynamic-update-slice_fusion.7
  381.7 5.6 constant_dynamic-update-slice_fusion.6
  398.3 8.4 multiply_convert_fusion
  406.8 5.4 constant_dynamic-update-slice_fusion.5
  412.2 27.6 %all-gather.6.cloned.1.call-done = bf16[1024,2048]{1,0:T(8,128)(2,1)} async-done(((bf16[128,2048]{1,0:T(8,128)(2,1)}), bf16[1024,2048]{1,0:T(8,128)(2,1)}) %all-gather.6.cloned.1.call-update) | async-done | bytes 4194320 | tf_op jit(solution)/shard_map/all_gather | solution.py:261
  439.8 6.3 convolution_convert_fusion.4
  446.1 18.1 %fusion.255 = f32[2,432,2816]{2,1,0:T(8,128)} fusion(bf16[2,432,2048]{2,1,0:T(8,128)(2,1)S(1)} %bitcast.244, bf16[2,2048,2816]{2,1,0:T(8,128)(2,1)} %constant_dynamic-update-slice_fusion.5), kind=kOutput, calls=%fused_computation.453 | convolution fusion | flops 9965666304 | bytes 36339712 | tf_op jit(solution)/shard_map/esd,edf->esf/dot_general | solution.py:433
  464.2 16.4 %multiply_convert_fusion.3 = (bf16[2,432,1408]{2,1,0:T(8,128)(2,1)}, bf16[2,432,1408]{2,1,0:T(8,128)(2,1)}, bf16[2,432,1408]{2,1,0:T(8,128)(2,1)}) fusion(f32[2,432,2816]{2,1,0:T(8,128)} %fusion.255, bf16[2,432,2048]{2,1,0:T(8,128)(2,1)} %bitcast.246, bf16[2,1408,2048]{2,1,0:T(8,128)(2,1)} %constant_dynamic-update-slice_fusion.9), kind=kOutput, calls=%fused_computation.29 | convolution fusion | flops 5001080832 | bytes 32104448 | tf_op jit(solution)/shard_map/esd,efd->esf/dot_general | solution.py:439
  480.6 16.7 %fusion.32 = bf16[2,432,2048]{2,1,0:T(8,128)(2,1)} fusion(bf16[2,2048,2816]{2,1,0:T(8,128)(2,1)} %constant_dynamic-update-slice_fusion.5, bf16[2,432,1408]{2,1,0:T(8,128)(2,1)} %get-tuple-element.22, bf16[2,432,1408]{2,1,0:T(8,128)(2,1)} %get-tuple-element.21), kind=kOutput, calls=%fused_computation.75 | convolution fusion | flops 9975398400 | bytes 31473664 | tf_op jit(solution)/shard_map/esf,edf->esd/dot_general | solution.py:443
  497.3 6.5 fusion.39
  503.8 5.6 multiply_convert_fusion.10
  513.0 6.5 fusion.3
  519.5 6.9 fusion.248
  526.4 16.4 %fusion.4 = bf16[1024,2048]{1,0:T(8,128)(2,1)} fusion(f32[1024,2048]{1,0:T(8,128)} %fusion.248, f32[2,432]{1,0:T(2,128)S(1)} %select_reduce_fusion, s32[2,1024]{1,0:T(2,128)S(1)} %bitcast.266, pred[2,1024]{1,0:T(4,128)(4,1)S(1)} %compare_reduce_fusion, bf16[2,432,1408]{2,1,0:T(8,128)(2,1)} %get-tuple-element.23, ...), kind=kOutput, calls=%fused_computation.18 | convolution fusion | flops 8619753472 | bytes 26563968 | tf_op jit(solution)/shard_map/dot_general | solution.py:273
  542.9 62.9 %reduce-scatter.14.cloned.1.call-done = bf16[128,2048]{1,0:T(8,128)(2,1)} async-done(((bf16[1024,2048]{1,0:T(8,128)(2,1)}), bf16[128,2048]{1,0:T(8,128)(2,1)}) %reduce-scatter.14.cloned.1.call-update) | async-done | bytes 524304 | tf_op jit(solution)/shard_map/reduce_scatter | solution.py:265
  607.4 89.7 %reduce-scatter.12.cloned.1.call-done = bf16[128,2048]{1,0:T(8,128)(2,1)} async-done(((bf16[1024,2048]{1,0:T(8,128)(2,1)}), bf16[128,2048]{1,0:T(8,128)(2,1)}) %reduce-scatter.12.cloned.1.call-update) | async-done | bytes 524304 | tf_op jit(solution)/shard_map/reduce_scatter | solution.py:265
  700.2 73.2 %all-gather.10.cloned.1.call-done = bf16[1024,2048]{1,0:T(8,128)(2,1)} async-done(((bf16[128,2048]{1,0:T(8,128)(2,1)}), bf16[1024,2048]{1,0:T(8,128)(2,1)}) %all-gather.10.cloned.1.call-update) | async-done | bytes 4194320 | tf_op jit(solution)/shard_map/all_gather | solution.py:261
  773.4 3.8 convolution_convert_fusion.12
  799.6 9.0 convolution_convert_fusion.1
  818.4 5.7 convolution_convert_fusion.2
  828.0 15.7 %convolution_convert_fusion = bf16[2,2048,2816]{2,1,0:T(8,128)(2,1)} fusion(bf16[2,432,512]{2,1,0:T(8,128)(2,1)S(1)} %get-tuple-element.51, bf16[2,432,512]{2,1,0:T(8,128)(2,1)S(1)} %get-tuple-element.52, bf16[2,432,512]{2,1,0:T(8,128)(2,1)S(1)} %get-tuple-element.53, bf16[2,432,512]{2,1,0:T(8,128)(2,1)S(1)} %get-tuple-element.50, ...), kind=kOutput, calls=%fused_computation.4 | convolution fusion | flops 10001088512 | bytes 31473664 | tf_op jit(solution)/shard_map/esd,esf->edf/dot_general | solution.py:462
  843.8 4.4 fusion.27
  848.2 4.3 fusion.112
  855.7 7.0 copy.166
  878.9 5.6 convolution_convert_fusion.7
  884.5 3.7 convolution_convert_fusion.6
  899.3 8.8 concatenate.161
  908.0 3.7 dynamic-slice_bitcast_fusion.1
  915.2 3.6 all-to-all-start.3
  922.8 63.8 %collective-permute-done.14 = bf16[8,64,1344]{2,1,0:T(8,128)(2,1)S(1)} collective-permute-done((bf16[8,64,1344]{2,1,0:T(8,128)(2,1)S(1)}, bf16[8,64,1344]{2,1,0:T(8,128)(2,1)S(1)}, u32[]{:S(2)}, u32[]{:S(2)}) %collective-permute-start.14) | collective-permute-done | bytes 1376288 | tf_op jit(solution)/shard_map/ppermute | solution.py:237
  991.3 6.0 all-to-all-start.2
  1012.3 39.7 %all-to-all-done.2 = bf16[8,64,1216]{2,1,0:T(8,128)(2,1)S(1)} async-done(((bf16[8,64,1216]{2,1,0:T(8,128)(2,1)}), bf16[8,64,1216]{2,1,0:T(8,128)(2,1)S(1)}, u32[]{:S(2)}, u32[]{:S(2)}) %all-to-all-start.2) | async-done | bytes 1245216 | tf_op jit(solution)/shard_map/all_to_all | solution.py:269
  1057.6 5.2 convert_element_type.404
  1062.8 44.4 %reduce-scatter.16.cloned.1.call-done = bf16[128,2048]{1,0:T(8,128)(2,1)} async-done(((bf16[1024,2048]{1,0:T(8,128)(2,1)}), bf16[128,2048]{1,0:T(8,128)(2,1)}) %reduce-scatter.16.cloned.1.call-update) | async-done | bytes 524304 | tf_op jit(solution)/shard_map/reduce_scatter | solution.py:265
  1110.3 40.5 %all-reduce.4 = f32[4608]{0:T(1024)S(1)} all-reduce(f32[4608]{0:T(1024)S(1)} %pad_maximum_fusion.33), channel_id=8, replica_groups=mesh['ctx'=8,'fsdp'=4] {'ctx','fsdp'}, use_global_device_ids=true, to_apply=%region_25.26.clone | all-reduce | flops 4608 | bytes 36864
  1152.7 123.7 %reduce-scatter.18.cloned.1.call-done = bf16[2,512,2816]{2,1,0:T(8,128)(2,1)} async-done(((bf16[2,2048,2816]{2,1,0:T(8,128)(2,1)}), bf16[2,512,2816]{2,1,0:T(8,128)(2,1)}) %reduce-scatter.18.cloned.1.call-update) | async-done | bytes 5767184 | tf_op jit(solution)/shard_map/reduce_scatter | solution.py:464
  1276.4 7.9 convert_element_type.402
  (460 shorter events, 196.5 us)
Async XLA Ops:
  9.8 55.6 %copy-start.56 = (bf16[512,128]{1,0:T(8,128)(2,1)S(1)}, bf16[512,128]{1,0:T(8,128)(2,1)}, u32[]{:S(2)}) copy-start(bf16[512,128]{1,0:T(8,128)(2,1)} %param.18) | copy-start | bytes 393220
  11.0 54.4 %all-to-all-start = ((bf16[8,64,1216]{2,1,0:T(8,128)(2,1)}), bf16[8,64,1216]{2,1,0:T(8,128)(2,1)S(1)}, u32[]{:S(2)}, u32[]{:S(2)}) async-start(bf16[8,64,1216]{2,1,0:T(8,128)(2,1)} %pad_maximum_fusion.13), calls=%async_computation | async-start | bytes 2621440 | tf_op jit(solution)/shard_map/all_to_all | solution.py:269
  18.3 78.3 %copy-start.80 = (f32[4608]{0:T(1024)S(1)}, f32[4608]{0:T(1024)}, u32[]{:S(2)}) copy-start(f32[4608]{0:T(1024)} %param.15) | copy-start | bytes 55300
  18.3 92.7 %all-gather.12.cloned.1.call-start = ((), (), s32[]{:S(2)}) async-start(), calls=%async_computation.20 | async-start | bytes 4718592 | tf_op jit(solution)/shard_map/all_gather | solution.py:261
  19.0 339.3 %reduce-scatter.10.cloned.1.call-start = ((), (), s32[]{:S(2)}) async-start(), calls=%async_computation.11 | async-start | bytes 4718592 | tf_op jit(solution)/shard_map/reduce_scatter | solution.py:265
  66.9 29.6 %collective-permute-start.1 = (bf16[8,64,1344]{2,1,0:T(8,128)(2,1)}, bf16[8,64,1344]{2,1,0:T(8,128)(2,1)S(1)}, u32[]{:S(2)}, u32[]{:S(2)}) collective-permute-start(bf16[8,64,1344]{2,1,0:T(8,128)(2,1)} %get-tuple-element.67), channel_id=1, source_target_pairs={{0,2},{1,3},{2,0},{3,1},{4,6},{5,7},{6,4},{7,5},{8,10},{9,11},{10,... | collective-permute-start | bytes 4128776 | tf_op jit(solution)/shard_map/ppermute | solution.py:237
  68.4 28.3 %collective-permute-start = (bf16[8,64,1344]{2,1,0:T(8,128)(2,1)}, bf16[8,64,1344]{2,1,0:T(8,128)(2,1)}, u32[]{:S(2)}, u32[]{:S(2)}) collective-permute-start(bf16[8,64,1344]{2,1,0:T(8,128)(2,1)} %get-tuple-element.67), channel_id=1, source_target_pairs={{0,1},{1,0},{2,3},{3,2},{4,5},{5,4},{6,7},{7,6},{8,9},{9,8},{10,11... | collective-permute-start | bytes 4128776 | tf_op jit(solution)/shard_map/ppermute | solution.py:237
  96.5 3.4 collective-permute-start.2
  96.6 263.0 %copy-start.54 = (f32[2048]{0:T(1024)}, f32[2048]{0:T(1024)S(1)}, u32[]{:S(2)}) copy-start(f32[2048]{0:T(1024)S(1)} %get-tuple-element.93) | copy-start | bytes 24580
  142.1 245.2 %all-gather.8.cloned.1.call-start = ((), (), s32[]{:S(2)}) async-start(), calls=%async_computation.13 | async-start | bytes 5013504 | tf_op jit(solution)/shard_map/all_gather | solution.py:261
  144.7 222.8 %collective-permute-start.7 = (bf16[2,512,2816]{2,1,0:T(8,128)(2,1)}, bf16[2,512,2816]{2,1,0:T(8,128)(2,1)}, u32[]{:S(2)}, u32[]{:S(2)}) collective-permute-start(bf16[2,512,2816]{2,1,0:T(8,128)(2,1)} %param.22), channel_id=1, source_target_pairs={{0,2},{1,3},{2,0},{3,1},{4,6},{5,7},{6,4},{7,5},{8,10},{9,11},{10,... | collective-permute-start | bytes 17301512 | tf_op jit(solution)/shard_map/ppermute | solution.py:237
  149.6 65.2 %all-to-all-start.1 = ((bf16[8,64,1152]{2,1,0:T(8,128)(2,1)}), bf16[8,64,1152]{2,1,0:T(8,128)(2,1)S(1)}, u32[]{:S(2)}, u32[]{:S(2)}) async-start(bf16[8,64,1152]{2,1,0:T(8,128)(2,1)} %copy.150), calls=%async_computation.2 | async-start | bytes 2359296 | tf_op jit(solution)/shard_map/all_to_all | solution.py:269
  158.5 281.3 %all-gather.6.cloned.1.call-start = ((), (), s32[]{:S(2)}) async-start(), calls=%async_computation.12 | async-start | bytes 4718592 | tf_op jit(solution)/shard_map/all_gather | solution.py:261
  158.7 175.2 %collective-permute-start.10 = (bf16[2,1408,512]{2,1,0:T(8,128)(2,1)}, bf16[2,1408,512]{2,1,0:T(8,128)(2,1)}, u32[]{:S(2)}, u32[]{:S(2)}) collective-permute-start(bf16[2,1408,512]{2,1,0:T(8,128)(2,1)} %param.23), channel_id=1, source_target_pairs={{0,2},{1,3},{2,0},{3,1},{4,6},{5,7},{6,4},{7,5},{8,10},{9,11},{10,... | collective-permute-start | bytes 8650760 | tf_op jit(solution)/shard_map/ppermute | solution.py:237
  159.3 174.7 %collective-permute-start.9 = (bf16[2,1408,512]{2,1,0:T(8,128)(2,1)}, bf16[2,1408,512]{2,1,0:T(8,128)(2,1)}, u32[]{:S(2)}, u32[]{:S(2)}) collective-permute-start(bf16[2,1408,512]{2,1,0:T(8,128)(2,1)} %param.23), channel_id=1, source_target_pairs={{0,1},{1,0},{2,3},{3,2},{4,5},{5,4},{6,7},{7,6},{8,9},{9,8},{10,11... | collective-permute-start | bytes 8650760 | tf_op jit(solution)/shard_map/ppermute | solution.py:237
  159.3 216.9 %collective-permute-start.6 = (bf16[2,512,2816]{2,1,0:T(8,128)(2,1)}, bf16[2,512,2816]{2,1,0:T(8,128)(2,1)}, u32[]{:S(2)}, u32[]{:S(2)}) collective-permute-start(bf16[2,512,2816]{2,1,0:T(8,128)(2,1)} %param.22), channel_id=1, source_target_pairs={{0,1},{1,0},{2,3},{3,2},{4,5},{5,4},{6,7},{7,6},{8,9},{9,8},{10,11... | collective-permute-start | bytes 17301512 | tf_op jit(solution)/shard_map/ppermute | solution.py:237
  214.8 143.5 %collective-permute-start.4 = (bf16[8,64,1152]{2,1,0:T(8,128)(2,1)S(1)}, bf16[8,64,1152]{2,1,0:T(8,128)(2,1)S(1)}, u32[]{:S(2)}, u32[]{:S(2)}) collective-permute-start(bf16[8,64,1152]{2,1,0:T(8,128)(2,1)S(1)} %all-to-all-done.1), channel_id=1, source_target_pairs={{0,2},{1,3},{2,0},{3,1},{4,6},{5,7},{6,4},{7,5},{8,10},{9,11},{10,... | collective-permute-start | bytes 3538952 | tf_op jit(solution)/shard_map/ppermute | solution.py:237
  220.8 167.2 %copy-start.94 = (f32[2]{0:T(128)}, f32[2]{0:T(128)S(1)}, u32[]{:S(2)}) copy-start(f32[2]{0:T(128)S(1)} %add_convert_fusion.2) | copy-start | bytes 28
  222.6 135.8 %copy-start.5 = (bf16[1,128,2048]{2,1,0:T(8,128)(2,1)S(1)}, bf16[1,128,2048]{2,1,0:T(8,128)(2,1)}, u32[]{:S(2)}) copy-start(bf16[1,128,2048]{2,1,0:T(8,128)(2,1)} %param.13) | copy-start | bytes 1572868
  334.0 31.5 %collective-permute-start.3 = (bf16[8,64,1152]{2,1,0:T(8,128)(2,1)S(1)}, bf16[8,64,1152]{2,1,0:T(8,128)(2,1)}, u32[]{:S(2)}, u32[]{:S(2)}) collective-permute-start(bf16[8,64,1152]{2,1,0:T(8,128)(2,1)S(1)} %all-to-all-done.1), channel_id=1, source_target_pairs={{0,1},{1,0},{2,3},{3,2},{4,5},{5,4},{6,7},{7,6},{8,9},{9,8},{10,11... | collective-permute-start | bytes 3538952 | tf_op jit(solution)/shard_map/ppermute | solution.py:237
  334.0 38.5 %collective-permute-start.11 = (bf16[2,1408,512]{2,1,0:T(8,128)(2,1)}, bf16[2,1408,512]{2,1,0:T(8,128)(2,1)}, u32[]{:S(2)}, u32[]{:S(2)}) collective-permute-start(bf16[2,1408,512]{2,1,0:T(8,128)(2,1)} %collective-permute-done.10), channel_id=1, source_target_pairs={{0,1},{1,0},{2,3},{3,2},{4,5},{5,4},{6,7},{7,6},{8,9},{9,8},{10,11... | collective-permute-start | bytes 8650760 | tf_op jit(solution)/shard_map/ppermute | solution.py:237
  358.3 7.2 collective-permute-start.5
  361.9 243.9 %reduce-scatter.14.cloned.1.call-start = ((), (), s32[]{:S(2)}) async-start(), calls=%async_computation.15 | async-start | bytes 4718592 | tf_op jit(solution)/shard_map/reduce_scatter | solution.py:265
  367.5 39.3 %collective-permute-start.8 = (bf16[2,512,2816]{2,1,0:T(8,128)(2,1)}, bf16[2,512,2816]{2,1,0:T(8,128)(2,1)}, u32[]{:S(2)}, u32[]{:S(2)}) collective-permute-start(bf16[2,512,2816]{2,1,0:T(8,128)(2,1)} %collective-permute-done.7), channel_id=1, source_target_pairs={{0,1},{1,0},{2,3},{3,2},{4,5},{5,4},{6,7},{7,6},{8,9},{9,8},{10,11... | collective-permute-start | bytes 17301512 | tf_op jit(solution)/shard_map/ppermute | solution.py:237
  519.5 177.6 %reduce-scatter.12.cloned.1.call-start = ((), (), s32[]{:S(2)}) async-start(), calls=%async_computation.14 | async-start | bytes 4718592 | tf_op jit(solution)/shard_map/reduce_scatter | solution.py:265
  542.8 64.3 %copy-start.6 = (bf16[1,128,2048]{2,1,0:T(8,128)(2,1)S(1)}, bf16[1,128,2048]{2,1,0:T(8,128)(2,1)}, u32[]{:S(2)}) copy-start(bf16[1,128,2048]{2,1,0:T(8,128)(2,1)} %param.13) | copy-start | bytes 1572868
  542.8 64.3 %copy-start.15 = (bf16[128,2048]{1,0:T(8,128)(2,1)S(1)}, bf16[128,2048]{1,0:T(8,128)(2,1)}, u32[]{:S(2)}) copy-start(bf16[128,2048]{1,0:T(8,128)(2,1)} %reduce-scatter.10.cloned.1.call-done) | copy-start | bytes 1572868
  542.8 64.3 %copy-start.55 = (f32[2048]{0:T(1024)S(1)}, f32[2048]{0:T(1024)}, u32[]{:S(2)}) copy-start(f32[2048]{0:T(1024)} %copy-done.54) | copy-start | bytes 24580
  542.8 64.3 %copy-start.88 = (f32[128]{0:T(128)S(1)}, f32[128]{0:T(128)}, u32[]{:S(2)}) copy-start(f32[128]{0:T(128)} %copy-done.87) | copy-start | bytes 1540
  542.8 230.6 %all-gather.10.cloned.1.call-start = ((), (), s32[]{:S(2)}) async-start(), calls=%async_computation.16 | async-start | bytes 4718592 | tf_op jit(solution)/shard_map/all_gather | solution.py:261
  606.9 91.3 %copy-start.25 = (bf16[1,128,2048]{2,1,0:T(8,128)(2,1)S(1)}, bf16[1,128,2048]{2,1,0:T(8,128)(2,1)}, u32[]{:S(2)}) copy-start(bf16[1,128,2048]{2,1,0:T(8,128)(2,1)} %param.14) | copy-start | bytes 1572868
  700.1 77.1 %copy-start.1 = (f32[1024,512]{0,1:T(8,128)S(1)}, f32[1024,512]{0,1:T(8,128)}, u32[]{:S(2)}) copy-start(f32[1024,512]{0,1:T(8,128)} %copy-done) | copy-start | bytes 6291460
  700.1 77.1 %copy-start.42 = (bf16[512,1,128]{2,1,0:T(2,128)(2,1)S(1)}, bf16[512,1,128]{2,1,0:T(2,128)(2,1)}, u32[]{:S(2)}) copy-start(bf16[512,1,128]{2,1,0:T(2,128)(2,1)} %copy-done.41) | copy-start | bytes 393220
  700.1 188.0 %reduce-scatter.22.cloned.1.call-start = ((), (), s32[]{:S(2)}) async-start(), calls=%async_computation.21 | async-start | bytes 1474560
  796.8 260.8 %reduce-scatter.20.cloned.1.call-start = ((), (), s32[]{:S(2)}) async-start(), calls=%async_computation.19 | async-start | bytes 14417920 | tf_op jit(solution)/shard_map/reduce_scatter | solution.py:467
  808.7 298.6 %reduce-scatter.16.cloned.1.call-start = ((), (), s32[]{:S(2)}) async-start(), calls=%async_computation.17 | async-start | bytes 4718592 | tf_op jit(solution)/shard_map/reduce_scatter | solution.py:265
  824.2 452.2 %reduce-scatter.18.cloned.1.call-start = ((), (), s32[]{:S(2)}) async-start(), calls=%async_computation.18 | async-start | bytes 28835840 | tf_op jit(solution)/shard_map/reduce_scatter | solution.py:464
  866.0 3.2 collective-permute-start.16
  866.9 44.8 %collective-permute-start.15 = (bf16[8,64,1152]{2,1,0:T(8,128)(2,1)}, bf16[8,64,1152]{2,1,0:T(8,128)(2,1)}, u32[]{:S(2)}, u32[]{:S(2)}) collective-permute-start(bf16[8,64,1152]{2,1,0:T(8,128)(2,1)} %get-tuple-element.30), channel_id=1, source_target_pairs={{0,1},{1,0},{2,3},{3,2},{4,5},{5,4},{6,7},{7,6},{8,9},{9,8},{10,11... | collective-permute-start | bytes 3538952 | tf_op jit(solution)/shard_map/ppermute | solution.py:237
  872.1 39.6 %collective-permute-start.17 = (bf16[8,64,1152]{2,1,0:T(8,128)(2,1)}, bf16[8,64,1152]{2,1,0:T(8,128)(2,1)}, u32[]{:S(2)}, u32[]{:S(2)}) collective-permute-start(bf16[8,64,1152]{2,1,0:T(8,128)(2,1)} %fusion.51), channel_id=1, source_target_pairs={{0,2},{1,3},{2,0},{3,1},{4,6},{5,7},{6,4},{7,5},{8,10},{9,11},{10,... | collective-permute-start | bytes 3538952 | tf_op jit(solution)/shard_map/ppermute | solution.py:237
  911.7 7.7 collective-permute-start.13
  915.2 76.1 %all-to-all-start.3 = ((bf16[8,64,1152]{2,1,0:T(8,128)(2,1)}), bf16[8,64,1152]{2,1,0:T(8,128)(2,1)S(1)}, u32[]{:S(2)}, u32[]{:S(2)}) async-start(bf16[8,64,1152]{2,1,0:T(8,128)(2,1)} %fusion.53), calls=%async_computation.7 | async-start | bytes 2359296 | tf_op jit(solution)/shard_map/all_to_all | solution.py:269
  918.9 3.9 collective-permute-start.12
  921.5 65.1 %collective-permute-start.14 = (bf16[8,64,1344]{2,1,0:T(8,128)(2,1)S(1)}, bf16[8,64,1344]{2,1,0:T(8,128)(2,1)S(1)}, u32[]{:S(2)}, u32[]{:S(2)}) collective-permute-start(bf16[8,64,1344]{2,1,0:T(8,128)(2,1)S(1)} %fusion.35), channel_id=1, source_target_pairs={{0,2},{1,3},{2,0},{3,1},{4,6},{5,7},{6,4},{7,5},{8,10},{9,11},{10,... | collective-permute-start | bytes 4128776 | tf_op jit(solution)/shard_map/ppermute | solution.py:237
  991.3 60.7 %all-to-all-start.2 = ((bf16[8,64,1216]{2,1,0:T(8,128)(2,1)}), bf16[8,64,1216]{2,1,0:T(8,128)(2,1)S(1)}, u32[]{:S(2)}, u32[]{:S(2)}) async-start(bf16[8,64,1216]{2,1,0:T(8,128)(2,1)} %slice.457), calls=%async_computation.6 | async-start | bytes 2621440 | tf_op jit(solution)/shard_map/all_to_all | solution.py:269
  1057.6 49.7 %copy-start.77 = (bf16[128,32]{0,1:T(8,128)(2,1)S(1)}, bf16[128,32]{0,1:T(8,128)(2,1)}, u32[]{:S(2)}) copy-start(bf16[128,32]{0,1:T(8,128)(2,1)} %copy-done.76) | copy-start | bytes 24580
  1057.6 49.7 %copy-start.95 = (f32[128]{0:T(128)S(1)}, f32[128]{0:T(128)}, u32[]{:S(2)}) copy-start(f32[128]{0:T(128)} %dynamic-slice.34) | copy-start | bytes 1540
  1062.8 88.6 %copy-start.21 = (f32[128,2048]{1,0:T(8,128)S(1)}, f32[128,2048]{1,0:T(8,128)}, u32[]{:S(2)}) copy-start(f32[128,2048]{1,0:T(8,128)} %get-tuple-element.20) | copy-start | bytes 3145732
  (99 other events, 607.7 us)
Sparse Core Ops, SparseCore 0:
  21.2 88.6 all-gather.11
  142.2 118.3 reduce-scatter.9
  263.4 77.7 all-gather.7
  362.0 77.7 all-gather.5
  519.6 86.1 reduce-scatter.13
  609.3 87.7 reduce-scatter.11
  700.2 73.1 all-gather.9
  796.9 62.5 reduce-scatter.21
  862.9 131.7 reduce-scatter.19
  998.6 108.6 reduce-scatter.15
  1109.8 166.5 reduce-scatter.17

commit v2 on v1

--- a/solution.py
+++ b/solution.py
@@ -237,6 +237,10 @@
     return lax.ppermute(values, "fsdp", [(at, at ^ distance) for at in range(count)])
 
 
+def after(values, *first):
+    return lax.optimization_barrier((values, *first))[0]
+
+
 def fsdp_pieces(own):
     near = fsdp_swap(own, 1)
     far = fsdp_swap(own, 2)
@@ -251,10 +255,11 @@
 
 
 def fsdp_reduce(blocks, rank):
+    kind = blocks.dtype
     rel = [lax.dynamic_index_in_dim(blocks, rank ^ k, 0, False) for k in range(4)]
     mine = rel[0].astype(jnp.float32) + fsdp_swap(rel[1], 1).astype(jnp.float32)
     other = rel[2].astype(jnp.float32) + fsdp_swap(rel[3], 1).astype(jnp.float32)
-    return mine + fsdp_swap(other.astype(jnp.bfloat16), 2).astype(jnp.float32)
+    return mine + fsdp_swap(other.astype(kind), 2).astype(jnp.float32)
 
 
 def ctx_gather(values):
@@ -359,27 +364,49 @@
     def own_rows(values):
         return lax.dynamic_slice_in_dim(values, first_row, tok_dev, 0)
 
+    exp_local = expert_gate_up.shape[0]
+    gu_far = []
+    for e in range(exp_local):
+        own = expert_gate_up[e]
+        gu_far.append(fsdp_swap(after(own, gu_far[-1]) if gu_far else own, 2))
     sff_dev = SFF // n_ctx
     sff_pad = -(-sff_dev // 128) * 128
+    attn = attention_split if H % n_ctx == 0 else attention_whole
+    attn_first, attn_mid, attn_backward = attn(
+        hidden_in[0], tokens, norm_gains, w_query, w_latent, w_expand, w_output, where_all, score_scale
+    )
+    first_done = attn_first(gu_far[0])
+
     gate_send = pad_last(columns_by_dest(shared_gate_up[:, :SFF], n_ctx), sff_pad)
     up_send = pad_last(columns_by_dest(shared_gate_up[:, SFF:], n_ctx), sff_pad)
     down_send = pad_last(rows_by_dest(shared_down, n_ctx), sff_pad)
     shared_send = jnp.concatenate([gate_send, up_send, down_send], -1)
-    attn = attention_split if split_heads else attention_whole
-    attn_state = attn(
-        hidden_in[0], tokens, norm_gains, w_query, w_latent, w_expand, w_output, where_all, score_scale
-    )
-    resid_mid, attn_backward = attn_state
-    shared_got = ctx_exchange(shared_send)
-    shared_full = whole_rows(fsdp_pieces(shared_got), rank)
+    shared_got = ctx_exchange(after(shared_send, first_done))
+    shared_near = fsdp_swap(shared_got, 1)
+    shared_far = fsdp_swap(after(shared_got, gu_far[-1]), 2)
+    shared_full = whole_rows(
+        [shared_got, shared_near, shared_far, fsdp_swap(shared_far, 1)], rank
+    )
     shared_rel = swap_chunks(shared_full, rank, 0)
     shared_gu = shared_rel[:, : 2 * sff_pad]
     shared_dn = shared_rel[:, 2 * sff_pad :]
-
-    gu_rel = jnp.concatenate(fsdp_pieces(expert_gate_up), 1)
-    dn_rel = jnp.concatenate(fsdp_pieces(expert_down), 2)
-
-    exp_local = expert_gate_up.shape[0]
+    dn_far = fsdp_swap(after(expert_down, shared_far), 2)
+    gu_rel = [
+        jnp.concatenate(
+            [expert_gate_up[e], fsdp_swap(expert_gate_up[e], 1), gu_far[e], fsdp_swap(gu_far[e], 1)],
+            0,
+        )
+        for e in range(exp_local)
+    ]
+    dn_rel = jnp.concatenate(
+        [expert_down, fsdp_swap(expert_down, 1), dn_far, fsdp_swap(dn_far, 1)], 2
+    )
+    dn_rel = [dn_rel[e] for e in range(exp_local)]
+
+    resid_mid = attn_mid(gu_far[-1])
+    normed_mid, inv_mid = norm_forward(resid_mid, gain_mid)
+    mid_all = ctx_gather(swap_chunks(normed_mid.astype(jnp.bfloat16), rank, 1))
+
     n_exp = exp_local * n_ctx
     capacity = max(2, 9 * tok_dev * TOP // (8 * n_exp))
     slots = capacity * n_ctx
@@ -388,14 +415,11 @@
     gate_rest = gates - gate_hi.astype(jnp.float32)
     gate_md = gate_rest.astype(jnp.bfloat16)
     gate_lo = (gate_rest - gate_md.astype(jnp.float32)).astype(jnp.bfloat16)
-    routes = pad_last(
-        jnp.concatenate([expert_ids[0].astype(jnp.bfloat16), gate_hi, gate_md, gate_lo], -1), 128
-    )
-    grads_all = ctx_gather(
-        jnp.concatenate([swap_chunks(out_grad[0], rank, 1), routes], -1)
-    )
-    routes_all = grads_all[:, D:]
-    grads_all = grads_all[:, :D]
+    routes = jnp.concatenate([expert_ids[0].astype(jnp.bfloat16), gate_hi, gate_md, gate_lo], -1)
+    routes_all = ctx_exchange(
+        after(jnp.broadcast_to(routes[None], (n_ctx, tok_dev, 4 * TOP)), shared_got)
+    ).reshape(length, 4 * TOP)
+    grads_all = ctx_gather(after(swap_chunks(out_grad[0], rank, 1), mid_all))
     ids_all = routes_all[:, :TOP].astype(jnp.float32)
     gates_all = (
         routes_all[:, TOP : 2 * TOP].astype(jnp.float32)
@@ -412,61 +436,89 @@
     pick = taken.astype(jnp.bfloat16).reshape(exp_local * slots, length)
     slot_gate = jnp.sum(jnp.where(taken, gate_of[:, None, :], 0.0), -1).reshape(-1, 1)
 
-    normed_mid, inv_mid = norm_forward(resid_mid, gain_mid)
-    mid_all = ctx_gather(swap_chunks(normed_mid.astype(jnp.bfloat16), rank, 1))
-
     s_both = dot_f32(mid_all, shared_gu)
     s_gate = s_both[:, :sff_pad]
     s_up = s_both[:, sff_pad:]
     s_sig = jax.nn.sigmoid(s_gate)
     s_silu = s_gate * s_sig
     s_act = (s_silu * s_up).astype(jnp.bfloat16)
+    x_slots = dot_f32(pick, mid_all).astype(jnp.bfloat16)
+    x_exp = [x_slots[e * slots : (e + 1) * slots] for e in range(exp_local)]
+    e_both = [dot_f32(x_exp[e], gu_rel[e]) for e in range(exp_local)]
+    e_gate = [v[:, :FF] for v in e_both]
+    e_up = [v[:, FF:] for v in e_both]
+    e_sig = [jax.nn.sigmoid(v) for v in e_gate]
+    e_silu = [g * v for g, v in zip(e_gate, e_sig)]
+    e_act = [(g * u).astype(jnp.bfloat16) for g, u in zip(e_silu, e_up)]
+    out_slots = [
+        dot_f32(e_act[e], dn_rel[e]).astype(jnp.bfloat16).astype(jnp.float32)
+        for e in range(exp_local)
+    ]
+    out_slots = (jnp.concatenate(out_slots, 0) * slot_gate).astype(jnp.bfloat16)
+    out_part = dot_f32(s_act, shared_dn, ((1,), (1,))) + dot_f32(pick, out_slots, ((0,), (0,)))
+    out_part = out_part.astype(jnp.bfloat16)
+
     s_act_grad = dot_f32(grads_all, shared_dn)
     s_both_grad = jnp.concatenate(
         [s_act_grad * s_up * s_sig * (1.0 + s_gate * (1.0 - s_sig)), s_act_grad * s_silu], -1
     ).astype(jnp.bfloat16)
-
-    x_slots = dot_f32(pick, mid_all).astype(jnp.bfloat16)
     y_slots = (dot_f32(pick, grads_all) * slot_gate).astype(jnp.bfloat16)
-    x_exp = x_slots.reshape(exp_local, slots, D)
-    y_exp = y_slots.reshape(exp_local, slots, D)
-    e_both = jnp.einsum("esd,edf->esf", x_exp, gu_rel, preferred_element_type=jnp.float32)
-    e_gate = e_both[..., :FF]
-    e_up = e_both[..., FF:]
-    e_sig = jax.nn.sigmoid(e_gate)
-    e_silu = e_gate * e_sig
-    e_act = (e_silu * e_up).astype(jnp.bfloat16)
-    e_act_grad = jnp.einsum("esd,efd->esf", y_exp, dn_rel, preferred_element_type=jnp.float32)
-    e_both_grad = jnp.concatenate(
-        [e_act_grad * e_up * e_sig * (1.0 + e_gate * (1.0 - e_sig)), e_act_grad * e_silu], -1
-    ).astype(jnp.bfloat16)
-    in_slots = jnp.einsum("esf,edf->esd", e_both_grad, gu_rel, preferred_element_type=jnp.float32)
-    in_slots = in_slots.astype(jnp.bfloat16).reshape(-1, D)
-    mid_grad_part = dot_f32(s_both_grad, shared_gu, ((1,), (1,))) + dot_f32(
+    y_exp = [y_slots[e * slots : (e + 1) * slots] for e in range(exp_local)]
+    both_grad = []
+    for e in range(exp_local):
+        act_grad = dot_f32(y_exp[e], dn_rel[e], ((1,), (1,)))
+        gate_part = act_grad * e_up[e] * e_sig[e] * (1.0 + e_gate[e] * (1.0 - e_sig[e]))
+        both_grad.append(
+            jnp.concatenate([gate_part, act_grad * e_silu[e]], -1).astype(jnp.bfloat16)
+        )
+    in_slots = jnp.concatenate(
+        [
+            dot_f32(both_grad[e], gu_rel[e], ((1,), (1,))).astype(jnp.bfloat16)
+            for e in range(exp_local)
+        ],
+        0,
+    )
+    mid_part = dot_f32(s_both_grad, shared_gu, ((1,), (1,))) + dot_f32(
         pick, in_slots, ((0,), (0,))
     )
-    mid_grad = swap_chunks(
-        ctx_scatter(mid_grad_part.astype(jnp.bfloat16)).astype(jnp.float32), rank, 1
-    )
-
-    out_slots = jnp.einsum("esf,efd->esd", e_act, dn_rel, preferred_element_type=jnp.float32)
-    out_slots = out_slots.astype(jnp.bfloat16).astype(jnp.float32).reshape(-1, D) * slot_gate
-    out_part = dot_f32(s_act, shared_dn, ((1,), (1,))) + dot_f32(
-        pick, out_slots.astype(jnp.bfloat16), ((0,), (0,))
-    )
-    ffn_out = swap_chunks(ctx_scatter(out_part.astype(jnp.bfloat16)), rank, 1)
+    mid_part = mid_part.astype(jnp.bfloat16)
+    mid_grad = ctx_scatter(mid_part)
+    ffn_out = swap_chunks(ctx_scatter(after(out_part, mid_grad)), rank, 1)
+    mid_grad = swap_chunks(mid_grad.astype(jnp.float32), rank, 1)
     hidden_out = (resid_mid + ffn_out.astype(jnp.float32)).astype(jnp.bfloat16)
 
-    x_abs = swap_chunks(x_exp, rank, 2)
-    y_abs = swap_chunks(y_exp, rank, 2)
-    gu_grad = jnp.einsum("esd,esf->edf", x_abs, e_both_grad, preferred_element_type=jnp.float32)
-    dn_grad = jnp.einsum("esf,esd->efd", e_act, y_abs, preferred_element_type=jnp.float32)
-    gu_grad = lax.psum_scatter(
-        gu_grad.astype(jnp.bfloat16), "fsdp", scatter_dimension=1, tiled=True
-    ).astype(jnp.float32)
-    dn_grad = lax.psum_scatter(
-        dn_grad.astype(jnp.bfloat16), "fsdp", scatter_dimension=2, tiled=True
-    ).astype(jnp.float32)
+    quarter = D // 4
+
+    def chunk(values, k):
+        return values[:, k * quarter : (k + 1) * quarter]
+
+    grad_far = []
+
+    def reduce_expert(term, depends):
+        out1 = fsdp_swap(term(1).astype(jnp.bfloat16), 1)
+        out3 = fsdp_swap(term(3).astype(jnp.bfloat16), 1)
+        other = (term(2) + out3.astype(jnp.float32)).astype(jnp.bfloat16)
+        if depends:
+            other = after(other, depends[-1])
+        far = fsdp_swap(other, 2)
+        depends.append(far)
+        return other, lambda: term(0) + out1.astype(jnp.float32) + far.astype(jnp.float32)
+
+    finish = []
+    ready = []
+    for e in range(exp_local):
+        x_e = after(x_exp[e], mid_part)
+
+        def dn_term(k, e=e):
+            return dot_f32(e_act[e], chunk(y_exp[e], k), ((0,), (0,)))
+
+        def gu_term(k, e=e, x_e=x_e):
+            return dot_f32(chunk(x_e, k), both_grad[e], ((0,), (0,)))
+
+        for term in (dn_term, gu_term):
+            other, last = reduce_expert(term, grad_far)
+            ready.append(other)
+            finish.append(last)
 
     shared_grad = jnp.concatenate(
         [
@@ -486,15 +538,15 @@
     resid_norm_grad, gain_mid_grad = norm_backward(resid_mid, inv_mid, gain_mid, mid_grad)
     resid_grad = out_grad[0].astype(jnp.float32) + resid_norm_grad
     token_grad, gain_in_grad, gain_lat_grad, query_w, latent_w, expand_w, output_w = attn_backward(
-        resid_grad.astype(jnp.bfloat16)
+        after(resid_grad.astype(jnp.bfloat16), *ready[:1]), grad_far
     )
     hidden_in_grad = (resid_grad + token_grad).astype(jnp.bfloat16)
-    gains_grad = lax.psum_scatter(
-        jnp.concatenate([gain_in_grad, gain_mid_grad, gain_lat_grad], 0),
-        ("ctx", "fsdp"),
-        scatter_dimension=0,
-        tiled=True,
-    )
+    gains = jnp.concatenate([gain_in_grad, gain_mid_grad, gain_lat_grad], 0)
+    gains = fsdp_reduce(gains.reshape(n_ctx, 4, -1).transpose(1, 0, 2), rank)
+    gains_grad = jnp.sum(ctx_exchange(gains), 0)
+    finals = [last() for last in finish]
+    dn_grad = jnp.stack(finals[0::2], 0)
+    gu_grad = jnp.stack(finals[1::2], 0)
     return (
         hidden_out[None],
         hidden_in_grad[None],
@@ -527,72 +579,92 @@
         return lax.dynamic_slice_in_dim(values, first_row, tok_dev, 0)
 
     rows = w_query.shape[0]
-    by_head = w_query.reshape(rows, n_ctx, heads, DN + DR)
-    query_send = jnp.concatenate(
-        [
-            by_head[..., :DN].reshape(rows, n_ctx, heads * DN),
-            by_head[..., DN:].reshape(rows, n_ctx, heads * DR),
-        ],
-        -1,
-    ).transpose(1, 0, 2)
-    output_send = rows_by_dest(w_output, n_ctx)
-    latent_send = jnp.broadcast_to(w_latent[None], (n_ctx,) + w_latent.shape)
-    got = ctx_exchange(jnp.concatenate([query_send, output_send, latent_send], -1))
-    expand_own = w_expand.reshape(n_ctx, rows, -1)
-    pieces = fsdp_pieces(jnp.concatenate([got, expand_own], -1))
-    n_wide, r_wide, o_wide = heads * DN, heads * DR, heads * DV
-    marks = [0, n_wide + r_wide, n_wide + r_wide + o_wide, n_wide + r_wide + o_wide + KVL + DR]
-    full = whole_rows(pieces, rank)
-    query_full = full[:, : marks[1]]
-    output_full = full[:, marks[1] : marks[2]]
-    latent_full = full[:, marks[2] : marks[3]]
-    expand_full = (
-        full[:, marks[3] :].reshape(n_ctx, 4, rows, -1).transpose(0, 2, 1, 3).reshape(KVL, -1)
-    )
-    expand_heads = expand_full.reshape(KVL, heads, DN + DV)
-    key_up = [expand_heads[:, j, :DN] for j in range(heads)]
-    value_up = [expand_heads[:, j, DN:] for j in range(heads)]
-
-    hidden_all = ctx_gather(hidden_bf).astype(jnp.float32)
-    cos_table, sin_table = rope_tables(where_all, DR)
-    normed_all, inv_all = norm_forward(hidden_all, gain_in)
-    normed_bf = normed_all.astype(jnp.bfloat16)
-    query_all = dot_f32(normed_bf, query_full)
-    compressed = dot_f32(normed_bf, latent_full)
-    lat_raw = compressed[:, :KVL]
-    lat_normed, inv_lat = norm_forward(lat_raw, gain_lat)
-    latent = lat_normed.astype(jnp.bfloat16)
-    key_rot = rope_apply(compressed[:, KVL:], cos_table, sin_table).astype(jnp.bfloat16)
-    allowed = where_all[None, :] <= where_all[:, None]
-    saved = []
-    out_part = []
-    for j in range(heads):
-        nope = query_all[:, j * DN : (j + 1) * DN].astype(jnp.bfloat16)
-        rot = rope_apply(
-            query_all[:, n_wide + j * DR : n_wide + (j + 1) * DR], cos_table, sin_table
-        ).astype(jnp.bfloat16)
-        lat_q = dot_f32(nope, key_up[j], ((1,), (1,))).astype(jnp.bfloat16)
-        mixed, log_total = attention_heads(lat_q, rot, latent, key_rot, allowed, score_scale)
-        mixed_bf = mixed.astype(jnp.bfloat16)
-        out_part.append(dot_f32(mixed_bf, value_up[j]).astype(jnp.bfloat16))
-        saved.append((nope, rot, lat_q, mixed, mixed_bf, log_total))
-    heads_out = jnp.concatenate(out_part, -1)
-    attn_part = dot_f32(heads_out, output_full, ((1,), (1,))).astype(jnp.bfloat16)
-    resid_mid = tokens + ctx_scatter(attn_part).astype(jnp.float32)
-
-    def backward(resid_bf):
-        resid_all = ctx_gather(resid_bf)
-        output_g = dot_f32(resid_all, heads_out, ((0,), (0,)))
-        heads_grad = dot_f32(resid_all, output_full).astype(jnp.bfloat16)
+    n_wide, r_wide = heads * DN, heads * DR
+    q_wide = n_wide + r_wide
+    saved = {}
+
+    def first(early):
+        by_head = w_query.reshape(rows, n_ctx, heads, DN + DR)
+        query_send = jnp.concatenate(
+            [
+                by_head[..., :DN].reshape(rows, n_ctx, n_wide),
+                by_head[..., DN:].reshape(rows, n_ctx, r_wide),
+            ],
+            -1,
+        ).transpose(1, 0, 2)
+        latent_send = jnp.broadcast_to(w_latent[None], (n_ctx,) + w_latent.shape)
+        got = ctx_exchange(jnp.concatenate([query_send, latent_send], -1))
+        pieces = fsdp_pieces(jnp.concatenate([got, w_expand.reshape(n_ctx, rows, -1)], -1))
+        full = whole_rows(pieces, rank)
+        query_full = full[:, :q_wide]
+        latent_full = full[:, q_wide : q_wide + KVL + DR]
+        expand_full = (
+            full[:, q_wide + KVL + DR :]
+            .reshape(n_ctx, 4, rows, -1)
+            .transpose(0, 2, 1, 3)
+            .reshape(KVL, -1)
+        )
+        expand_heads = expand_full.reshape(KVL, heads, DN + DV)
+        key_up = [expand_heads[:, j, :DN] for j in range(heads)]
+        value_up = [expand_heads[:, j, DN:] for j in range(heads)]
+
+        hidden_all = after(ctx_gather(hidden_bf), early)
+        output_full = lax.all_gather(
+            after(w_output, hidden_all), ("ctx", "fsdp"), axis=1, tiled=True
+        )
+        hidden_f = hidden_all.astype(jnp.float32)
+        cos_table, sin_table = rope_tables(where_all, DR)
+        normed_all, inv_all = norm_forward(hidden_f, gain_in)
+        normed_bf = normed_all.astype(jnp.bfloat16)
+        query_all = dot_f32(normed_bf, query_full)
+        compressed = dot_f32(normed_bf, latent_full)
+        lat_raw = compressed[:, :KVL]
+        lat_normed, inv_lat = norm_forward(lat_raw, gain_lat)
+        latent = lat_normed.astype(jnp.bfloat16)
+        key_rot = rope_apply(compressed[:, KVL:], cos_table, sin_table).astype(jnp.bfloat16)
+        allowed = where_all[None, :] <= where_all[:, None]
+        per_head = []
+        out_part = []
+        for j in range(heads):
+            nope = query_all[:, j * DN : (j + 1) * DN].astype(jnp.bfloat16)
+            rot = rope_apply(
+                query_all[:, n_wide + j * DR : n_wide + (j + 1) * DR], cos_table, sin_table
+            ).astype(jnp.bfloat16)
+            lat_q = dot_f32(nope, key_up[j], ((1,), (1,))).astype(jnp.bfloat16)
+            mixed, log_total = attention_heads(lat_q, rot, latent, key_rot, allowed, score_scale)
+            mixed_bf = mixed.astype(jnp.bfloat16)
+            out_part.append(dot_f32(mixed_bf, value_up[j]).astype(jnp.bfloat16))
+            per_head.append((nope, rot, lat_q, mixed, mixed_bf, log_total))
+        saved.update(locals())
+        return hidden_all
+
+    def middle(early):
+        heads_out = jnp.concatenate(saved["out_part"], -1).reshape(n_ctx, tok_dev, heads * DV)
+        own_heads = ctx_exchange(heads_out).transpose(1, 0, 2).reshape(tok_dev, H * DV)
+        saved["own_heads"] = own_heads
+        return tokens + dot_f32(after(own_heads, early), saved["output_full"])
+
+    def backward(resid_bf, stages):
+        query_full, latent_full = saved["query_full"], saved["latent_full"]
+        key_up, value_up = saved["key_up"], saved["value_up"]
+        latent, key_rot, allowed = saved["latent"], saved["key_rot"], saved["allowed"]
+        cos_table, sin_table = saved["cos_table"], saved["sin_table"]
+        normed_bf, own_heads = saved["normed_bf"], saved["own_heads"]
+        heads_grad = dot_f32(resid_bf, saved["output_full"], ((1,), (1,))).astype(jnp.bfloat16)
+        heads_grad = ctx_exchange(columns_by_dest(heads_grad, n_ctx)).reshape(length, heads * DV)
+        heads_grad = after(heads_grad, stages[0])
+        output_g = dot_f32(after(resid_bf, heads_grad), own_heads, ((0,), (0,)))
+        output_w = ctx_exchange(shard_rows(output_g, n_ctx, rank).astype(jnp.bfloat16))
+        output_w = jnp.sum(output_w.astype(jnp.float32), 0).T
         lat_total = jnp.zeros((length, KVL), jnp.float32)
         rot_total = jnp.zeros((length, DR), jnp.float32)
         expand_parts = []
         nope_parts = []
         rope_parts = []
+        query_parts = []
         for j in range(heads):
-            nope, rot, lat_q, mixed, mixed_bf, log_total = saved[j]
+            nope, rot, lat_q, mixed, mixed_bf, log_total = saved["per_head"][j]
             head_g = heads_grad[:, j * DV : (j + 1) * DV]
-            value_g = dot_f32(mixed_bf, head_g, ((0,), (0,)))
             mix_grad = dot_f32(head_g, value_up[j], ((1,), (1,))).astype(jnp.bfloat16)
             delta = jnp.sum(mix_grad.astype(jnp.float32) * mixed, -1, keepdims=True)
             query_g, lat_g, rot_g = attention_heads_back(
@@ -600,47 +672,55 @@
             )
             lat_total = lat_total + lat_g
             rot_total = rot_total + rot_g
-            lat_q_grad = query_g[:, :KVL].astype(jnp.bfloat16)
-            key_g = dot_f32(lat_q_grad, nope, ((0,), (0,)))
+            query_parts.append(query_g)
+        key_terms = jnp.concatenate([lat_total, rot_total], -1).astype(jnp.bfloat16)
+        key_got = ctx_exchange(
+            after(key_terms, stages[1]).reshape(n_ctx, tok_dev, KVL + DR)
+        )
+        for j in range(heads):
+            nope, rot, lat_q, mixed, mixed_bf, log_total = saved["per_head"][j]
+            head_g = heads_grad[:, j * DV : (j + 1) * DV]
+            lat_q_grad = query_parts[j][:, :KVL].astype(jnp.bfloat16)
             nope_parts.append(dot_f32(lat_q_grad, key_up[j]))
-            rope_parts.append(rope_back(query_g[:, KVL:], cos_table, sin_table))
-            expand_parts += [key_g, value_g]
-        key_terms = ctx_scatter(
-            jnp.concatenate([lat_total, rot_total], -1).astype(jnp.bfloat16)
-        ).astype(jnp.float32)
+            rope_parts.append(rope_back(query_parts[j][:, KVL:], cos_table, sin_table))
+            lat_q_grad = after(lat_q_grad, key_terms)
+            expand_parts.append(dot_f32(lat_q_grad, nope, ((0,), (0,))))
+            expand_parts.append(dot_f32(mixed_bf, head_g, ((0,), (0,))))
         query_grad = jnp.concatenate(nope_parts + rope_parts, -1).astype(jnp.bfloat16)
-        query_g_w = dot_f32(normed_bf, query_grad, ((0,), (0,)))
         in_part = dot_f32(query_grad, query_full, ((1,), (1,))).astype(jnp.bfloat16)
         in_grad = ctx_scatter(in_part).astype(jnp.float32)
+        gain_in_grad = jnp.sum(
+            in_part.astype(jnp.float32) * (saved["hidden_f"] * saved["inv_all"]), 0
+        )
+        query_g_w = dot_f32(normed_bf, query_grad, ((0,), (0,)))
+        key_sum = jnp.sum(key_got.astype(jnp.float32), 0)
         own_cos, own_sin = own_rows(cos_table), own_rows(sin_table)
         lat_in_grad, gain_lat_grad = norm_backward(
-            own_rows(lat_raw), own_rows(inv_lat), gain_lat, key_terms[:, :KVL]
+            own_rows(saved["lat_raw"]), own_rows(saved["inv_lat"]), gain_lat, key_sum[:, :KVL]
         )
         compressed_grad = jnp.concatenate(
-            [lat_in_grad, rope_back(key_terms[:, KVL:], own_cos, own_sin)], -1
+            [lat_in_grad, rope_back(key_sum[:, KVL:], own_cos, own_sin)], -1
         ).astype(jnp.bfloat16)
         latent_g = dot_f32(own_rows(normed_bf), compressed_grad, ((0,), (0,)))
-        in_grad = in_grad + dot_f32(compressed_grad, latent_full, ((1,), (1,)))
-        token_grad, gain_in_grad = norm_backward(tokens, own_rows(inv_all), gain_in, in_grad)
+        inv_in = own_rows(saved["inv_all"])
+        in_own = dot_f32(compressed_grad, latent_full, ((1,), (1,)))
+        gain_in_grad = gain_in_grad + jnp.sum(in_own * (tokens * inv_in), 0)
+        token_grad = norm_backward(tokens, inv_in, gain_in, in_grad + in_own)[0]
         expand_g = jnp.concatenate(expand_parts, -1)
-        expand_cols = (
-            expand_g.reshape(n_ctx, rows, 4, -1).transpose(0, 2, 1, 3).reshape(D, -1)
-        )
+        expand_cols = expand_g.reshape(n_ctx, rows, 4, -1).transpose(0, 2, 1, 3).reshape(D, -1)
         terms = shard_rows(
-            jnp.concatenate([query_g_w, output_g, latent_g, expand_cols], -1), n_ctx, rank
-        )
-        expand_w = terms[:, :, marks[3] :].reshape(KVL, -1)
-        sent = ctx_exchange(terms[:, :, : marks[3]].astype(jnp.bfloat16)).astype(jnp.float32)
+            jnp.concatenate([query_g_w, latent_g, expand_cols], -1), n_ctx, rank
+        )
+        expand_w = terms[:, :, q_wide + KVL + DR :].reshape(KVL, -1)
+        sent = ctx_exchange(terms[:, :, : q_wide + KVL + DR].astype(jnp.bfloat16))
+        sent = sent.astype(jnp.float32)
         nope_w = sent[:, :, :n_wide].reshape(n_ctx, rows, heads, DN)
-        rot_w = sent[:, :, n_wide : marks[1]].reshape(n_ctx, rows, heads, DR)
-        query_w = (
-            jnp.concatenate([nope_w, rot_w], -1).transpose(1, 0, 2, 3).reshape(rows, -1)
-        )
-        output_w = sent[:, :, marks[1] : marks[2]].transpose(0, 2, 1).reshape(H * DV, -1)
-        latent_w = jnp.sum(sent[:, :, marks[2] :], 0)
+        rot_w = sent[:, :, n_wide:q_wide].reshape(n_ctx, rows, heads, DR)
+        query_w = jnp.concatenate([nope_w, rot_w], -1).transpose(1, 0, 2, 3).reshape(rows, -1)
+        latent_w = jnp.sum(sent[:, :, q_wide:], 0)
         return token_grad, gain_in_grad, gain_lat_grad, query_w, latent_w, expand_w, output_w
 
-    return resid_mid, backward
+    return first, middle, backward
 
 
 def attention_whole(
@@ -697,7 +777,7 @@
     )
     resid_mid = tokens + dot_f32(heads_out, output_full)
 
-    def backward(resid_bf):
+    def backward(resid_bf, stages):
         output_g = dot_f32(heads_out, resid_bf, ((0,), (0,)))
         heads_grad = (
             dot_f32(resid_bf, output_full, ((1,), (1,)))
@@ -762,7 +842,7 @@
         ]
         return (token_grad, gain_in_grad, gain_lat_grad, *scattered)
 
-    return resid_mid, backward
+    return (lambda early: latent_full), (lambda early: resid_mid), backward
 
 
 def solution(mesh):

time: 1300 us -> 1080 us (0.83)
  waiting for transfers between devices: 792 us -> 496 us
  matrix products: 207 us -> 268 us
  starting transfers between devices: 36 us -> 66.6 us
    dot_general x43 -> x67, matrix products: 131 us -> 268 us  [dot_f32(): lax.dot_general(left, right, (dims, ((), ())), preferred_element_type=jnp...]
    reduce_scatter x2 -> x0, waiting for transfers between devices: 124 us -> none  [the longest x1 124 us: on_device(): lax.psum_scatter(gu_grad.astype(jnp.bfloat16), 'fsdp', scatter_dimension=...]
    reduce_scatter x4 -> x3, waiting for transfers between devices: 197 us -> 96.4 us  [ctx_scatter(): return lax.psum_scatter(values, 'ctx', scatter_dimension=0, tiled=True)]
    dot_general x5 -> x0, matrix products: 75.9 us -> none  [the longest x1 18.1 us: on_device(): jnp.einsum('esd,edf->esf', x_exp, gu_rel, preferred_element_type=jnp.floa...]
    all_to_all x4 -> x9, waiting for transfers between devices: 141 us -> 71.5 us  [ctx_exchange(): lax.all_to_all(values, 'ctx', split_axis=0, concat_axis=0, tiled=True)]
    all_gather x4 -> x3, waiting for transfers between devices: 101 us -> 44.8 us  [ctx_gather(): return lax.all_gather(values, 'ctx', axis=0, tiled=True)]
    ppermute x18 -> x39, waiting for transfers between devices: 229 us -> 282 us  [fsdp_swap(): lax.ppermute(values, 'fsdp', [(at, at ^ distance) for at in range(count)])]
    unnamed x1 -> x0, blocking collectives: 40.5 us -> none
  transfers between devices with their start and end apart: 33 -> 55, of which waited for: 15 -> 21; matrix products, arithmetic and copies ran while one was open for 19% -> 34% of each run, Pallas kernels for 0% -> 0%
where the time goes in v2:
time: 1080 us
  waiting for transfers between devices  496 us (46%)
  matrix products  268 us (25%)
  local copies, waits for them, and re-layouts  112 us (10%)
  other arithmetic  83.8 us (8%)
  starting transfers between devices  66.6 us (6%)
  blocking collectives  34.2 us (3%)
  between operations  16.8 us (2%)
    ppermute x39, waiting for transfers between devices, fsdp_swap(): lax.ppermute(values, 'fsdp', [(at, at ^ distance) for at in range(count)])  282 us
    dot_general x67, matrix products, dot_f32(): lax.dot_general(left, right, (dims, ((), ())), preferred_element_type=jnp...  268 us
    reduce_scatter x3, waiting for transfers between devices, ctx_scatter(): return lax.psum_scatter(values, 'ctx', scatter_dimension=0, tiled=True)  96.4 us
    all_to_all x9, waiting for transfers between devices, ctx_exchange(): lax.all_to_all(values, 'ctx', split_axis=0, concat_axis=0, tiled=True)  71.5 us
    all_gather x3, waiting for transfers between devices, ctx_gather(): return lax.all_gather(values, 'ctx', axis=0, tiled=True)  44.8 us
    all_to_all x9, starting transfers between devices, ctx_exchange(): lax.all_to_all(values, 'ctx', split_axis=0, concat_axis=0, tiled=True)  44 us
    all_to_all x1, blocking collectives, ctx_exchange(): lax.all_to_all(values, 'ctx', split_axis=0, concat_axis=0, tiled=True)  34.2 us
    unnamed x270, local copies, waits for them, and re-layouts  30.5 us
  transfers between devices with their start and end apart: 55, of which 21 were waited for; matrix products, arithmetic and copies ran while one was open for 34% of the time, Pallas kernels for 0%

profile of v2, /device:TPU:0, one launch (start us, length us, event | category | flops | bytes accessed | tf_op | source)
XLA Modules:
  0.0 1077.1 jit_solution(13768927171359834122)
XLA Ops:
  17.3 62.6 %collective-permute-done = bf16[512,2816]{1,0:T(8,128)(2,1)} collective-permute-done((bf16[512,2816]{1,0:T(8,128)(2,1)S(1)}, bf16[512,2816]{1,0:T(8,128)(2,1)}, u32[]{:S(2)}, u32[]{:S(2)}) %collective-permute-start) | collective-permute-done | bytes 2883616 | tf_op jit(solution)/shard_map/ppermute | solution.py:237
  79.9 6.4 all-gather.12.cloned.1.call-done
  88.1 34.2 %all_to_all.54 = bf16[8,64,960]{2,1,0:T(8,128)(2,1)S(1)} all-to-all(bf16[8,64,960]{2,1,0:T(8,128)(2,1)S(1)} %pad_maximum_fusion.24), channel_id=1, replica_groups=mesh['ctx'=8,'fsdp'=4] {'ctx'}, dimensions={0} | all-to-all | bytes 1966080 | tf_op jit(solution)/shard_map/all_to_all | solution.py:274
  125.1 36.4 %collective-permute-done.2 = bf16[8,64,1088]{2,1,0:T(8,128)(2,1)S(1)} collective-permute-done((bf16[8,64,1088]{2,1,0:T(8,128)(2,1)}, bf16[8,64,1088]{2,1,0:T(8,128)(2,1)S(1)}, u32[]{:S(2)}, u32[]{:S(2)}) %collective-permute-start.2) | collective-permute-done | bytes 1114144 | tf_op jit(solution)/shard_map/ppermute | solution.py:237
  200.2 5.6 all-to-all-start.1
  209.3 11.4 %all-to-all-done.1 = bf16[8,128,256]{1,2,0:T(8,128)(2,1)S(1)} async-done(((bf16[8,128,256]{1,2,0:T(8,128)(2,1)}), bf16[8,128,256]{1,2,0:T(8,128)(2,1)S(1)}, u32[]{:S(2)}, u32[]{:S(2)}) %all-to-all-start.1) | async-done | bytes 524320 | tf_op jit(solution)/shard_map/all_to_all | solution.py:274
  224.4 6.5 collective-permute-done.4
  230.9 6.4 multiply_reduce_fusion.5
  239.5 19.7 %all-to-all-done.2 = bf16[8,64,1152]{2,1,0:T(8,128)(2,1)S(1)} async-done(((bf16[8,64,1152]{2,1,0:T(8,128)(2,1)}), bf16[8,64,1152]{2,1,0:T(8,128)(2,1)S(1)}, u32[]{:S(2)}, u32[]{:S(2)}) %all-to-all-start.2) | async-done | bytes 1179680 | tf_op jit(solution)/shard_map/all_to_all | solution.py:274
  261.1 24.0 %collective-permute-done.6 = bf16[8,64,1152]{2,1,0:T(8,128)(2,1)S(1)} collective-permute-done((bf16[8,64,1152]{2,1,0:T(8,128)(2,1)S(1)}, bf16[8,64,1152]{2,1,0:T(8,128)(2,1)S(1)}, u32[]{:S(2)}, u32[]{:S(2)}) %collective-permute-start.6) | collective-permute-done | bytes 1179680 | tf_op jit(solution)/shard_map/ppermute | solution.py:237
  307.3 34.5 %collective-permute-done.11 = bf16[2,1408,512]{2,1,0:T(8,128)(2,1)} collective-permute-done((bf16[2,1408,512]{2,1,0:T(8,128)(2,1)}, bf16[2,1408,512]{2,1,0:T(8,128)(2,1)}, u32[]{:S(2)}, u32[]{:S(2)}) %collective-permute-start.11) | collective-permute-done | bytes 2883616 | tf_op jit(solution)/shard_map/ppermute | solution.py:237
  348.7 5.3 constant_dynamic-update-slice_fusion.1
  361.9 5.2 fusion.28
  367.2 9.8 fusion.84
  377.0 9.9 fusion.83
  386.9 38.4 %all-gather.10.cloned.1.call-done = bf16[1024,2048]{1,0:T(8,128)(2,1)} async-done(((bf16[128,2048]{1,0:T(8,128)(2,1)}), bf16[1024,2048]{1,0:T(8,128)(2,1)}) %all-gather.10.cloned.1.call-update) | async-done | bytes 4194320 | tf_op jit(solution)/shard_map/all_gather | solution.py:266
  425.3 8.2 multiply_convert_fusion
  433.5 10.2 multiply_convert_fusion.8
  443.7 7.9 multiply_convert_fusion.6
  451.6 5.5 multiply_convert_fusion.13
  457.2 5.9 fusion.26
  463.0 13.8 %convolution_convert_fusion.13 = bf16[432,2048]{1,0:T(8,128)(2,1)} fusion(bf16[512,2816]{1,0:T(8,128)(2,1)} %collective-permute-done.9, bf16[512,2816]{1,0:T(8,128)(2,1)} %collective-permute-done, bf16[512,2816]{1,0:T(8,128)(2,1)} %collective-permute-done.8, bf16[512,2816]{1,0:T(8,128)(2,1)} %copy-done.31, bf16[432,1408]{1,0:T(8,128)(2,1)} %get-tuple-element.66, ...), kind=kOutput, calls=%fused_computation.93 | convolution fusion | flops 5034721280 | bytes 15736832 | tf_op jit(solution)/shard_map/dot_general | solution.py:278
  476.8 13.7 %convolution_convert_fusion.12 = bf16[432,2048]{1,0:T(8,128)(2,1)} fusion(bf16[512,2816]{1,0:T(8,128)(2,1)} %collective-permute-done.14, bf16[512,2816]{1,0:T(8,128)(2,1)} %collective-permute-done.4, bf16[512,2816]{1,0:T(8,128)(2,1)} %collective-permute-done.13, bf16[512,2816]{1,0:T(8,128)(2,1)} %get-tuple-element.33, ...), kind=kOutput, calls=%fused_computation.92 | convolution fusion | flops 5034721280 | bytes 15736832 | tf_op jit(solution)/shard_map/dot_general | solution.py:278
  490.6 11.3 %add_convert_fusion = bf16[1024,2048]{1,0:T(8,128)(2,1)} fusion(f32[1024,2048]{1,0:T(8,128)} %fusion.26, pred[864,1024]{1,0:T(32,128)(4,1)} %fusion.21, bf16[432,2048]{1,0:T(8,128)(2,1)} %convolution_convert_fusion.12, bf16[432,2048]{1,0:T(8,128)(2,1)} %convolution_convert_fusion.13), kind=kOutput, calls=%fused_computation.18 | convolution fusion | flops 3635150848 | bytes 17006592 | tf_op jit(solution)/shard_map/dot_general | solution.py:278
  502.3 6.0 fusion.25
  508.4 5.6 fusion.24
  514.0 4.8 fusion.12
  523.2 65.2 %reduce-scatter.4.cloned.1.call-done = bf16[128,2048]{1,0:T(8,128)(2,1)} async-done(((bf16[1024,2048]{1,0:T(8,128)(2,1)}), bf16[128,2048]{1,0:T(8,128)(2,1)}) %reduce-scatter.4.cloned.1.call-update) | async-done | bytes 524304 | tf_op jit(solution)/shard_map/reduce_scatter | solution.py:270
  605.8 6.8 copy.168
  649.3 31.2 %reduce-scatter.6.cloned.1.call-done = bf16[128,2048]{1,0:T(8,128)(2,1)} async-done(((bf16[1024,2048]{1,0:T(8,128)(2,1)}), bf16[128,2048]{1,0:T(8,128)(2,1)}) %reduce-scatter.6.cloned.1.call-update) | async-done | bytes 524304 | tf_op jit(solution)/shard_map/reduce_scatter | solution.py:270
  698.2 5.6 add_convert_fusion.3
  741.5 44.9 %collective-permute-done.18 = bf16[512,2816]{1,0:T(8,128)(2,1)} collective-permute-done((bf16[512,2816]{1,0:T(8,128)(2,1)}, bf16[512,2816]{1,0:T(8,128)(2,1)}, u32[]{:S(2)}, u32[]{:S(2)}) %collective-permute-start.18) | collective-permute-done | bytes 2883616 | tf_op jit(solution)/shard_map/ppermute | solution.py:237
  787.6 5.7 all-to-all-start.5
  806.8 5.8 convolution_convert_fusion.14
  812.6 8.3 all-to-all-done.5
  830.5 7.3 concatenate.173
  841.1 6.7 fusion.3
  873.9 14.0 %collective-permute-done.24 = bf16[8,64,1088]{2,1,0:T(8,128)(2,1)S(1)} collective-permute-done((bf16[8,64,1088]{2,1,0:T(8,128)(2,1)S(1)}, bf16[8,64,1088]{2,1,0:T(8,128)(2,1)S(1)}, u32[]{:S(2)}, u32[]{:S(2)}) %collective-permute-start.24) | collective-permute-done | bytes 1114144 | tf_op jit(solution)/shard_map/ppermute | solution.py:237
  893.7 19.3 %all-to-all-done.9 = bf16[8,64,1152]{2,1,0:T(8,128)(2,1)} async-done(((bf16[8,64,1152]{2,1,0:T(8,128)(2,1)}), bf16[8,64,1152]{2,1,0:T(8,128)(2,1)}, u32[]{:S(2)}, u32[]{:S(2)}) %all-to-all-start.9) | async-done | bytes 1179680 | tf_op jit(solution)/shard_map/all_to_all | solution.py:274
  917.3 6.0 add_convert_fusion.2
  941.9 21.9 %collective-permute-done.27 = bf16[8,64,2048]{2,1,0:T(8,128)(2,1)} collective-permute-done((bf16[8,64,2048]{2,1,0:T(8,128)(2,1)}, bf16[8,64,2048]{2,1,0:T(8,128)(2,1)}, u32[]{:S(2)}, u32[]{:S(2)}) %collective-permute-start.27) | collective-permute-done | bytes 2097184 | tf_op jit(solution)/shard_map/ppermute | solution.py:237
  963.9 5.6 fusion.11
  969.5 5.9 all-to-all-start.8
  975.4 8.0 add_bitcast_fusion.1
  989.7 35.1 %collective-permute-done.36 = bf16[512,2816]{1,0:T(8,128)(2,1)} collective-permute-done((bf16[512,2816]{1,0:T(8,128)(2,1)}, bf16[512,2816]{1,0:T(8,128)(2,1)}, u32[]{:S(2)}, u32[]{:S(2)}) %collective-permute-start.36) | collective-permute-done | bytes 2883616 | tf_op jit(solution)/shard_map/ppermute | solution.py:237
  1028.5 7.8 pad_maximum_fusion.2
  1056.9 5.9 all-to-all-start.6
  1064.0 5.3 all-to-all-done.6
  (558 shorter events, 329.0 us)
Async XLA Ops:
  7.2 79.1 %all-gather.12.cloned.1.call-start = ((), (), s32[]{:S(2)}) async-start(), calls=%async_computation.19 | async-start | bytes 4718592 | tf_op jit(solution)/shard_map/all_gather | solution.py:266
  7.9 223.0 %all-gather.6.cloned.1.call-start = ((), (), s32[]{:S(2)}) async-start(), calls=%async_computation.13 | async-start | bytes 8650752 | tf_op jit(solution)/shard_map/all_gather | solution.py:612
  14.3 65.5 %collective-permute-start = (bf16[512,2816]{1,0:T(8,128)(2,1)S(1)}, bf16[512,2816]{1,0:T(8,128)(2,1)}, u32[]{:S(2)}, u32[]{:S(2)}) collective-permute-start(bf16[512,2816]{1,0:T(8,128)(2,1)S(1)} %get-tuple-element.70), channel_id=1, source_target_pairs={{0,2},{1,3},{2,0},{3,1},{4,6},{5,7},{6,4},{7,5},{8,10},{9,11},{10,... | collective-permute-start | bytes 8650760 | tf_op jit(solution)/shard_map/ppermute | solution.py:237
  123.7 37.9 %collective-permute-start.2 = (bf16[8,64,1088]{2,1,0:T(8,128)(2,1)}, bf16[8,64,1088]{2,1,0:T(8,128)(2,1)S(1)}, u32[]{:S(2)}, u32[]{:S(2)}) collective-permute-start(bf16[8,64,1088]{2,1,0:T(8,128)(2,1)} %get-tuple-element.110), channel_id=1, source_target_pairs={{0,2},{1,3},{2,0},{3,1},{4,6},{5,7},{6,4},{7,5},{8,10},{9,11},{10,... | collective-permute-start | bytes 3342344 | tf_op jit(solution)/shard_map/ppermute | solution.py:237
  125.1 39.9 %collective-permute-start.1 = (bf16[8,64,1088]{2,1,0:T(8,128)(2,1)}, bf16[8,64,1088]{2,1,0:T(8,128)(2,1)S(1)}, u32[]{:S(2)}, u32[]{:S(2)}) collective-permute-start(bf16[8,64,1088]{2,1,0:T(8,128)(2,1)} %get-tuple-element.110), channel_id=1, source_target_pairs={{0,1},{1,0},{2,3},{3,2},{4,5},{5,4},{6,7},{7,6},{8,9},{9,8},{10,11... | collective-permute-start | bytes 3342344 | tf_op jit(solution)/shard_map/ppermute | solution.py:237
  164.7 66.2 %collective-permute-start.4 = (bf16[512,2816]{1,0:T(8,128)(2,1)}, bf16[512,2816]{1,0:T(8,128)(2,1)}, u32[]{:S(2)}, u32[]{:S(2)}) collective-permute-start(bf16[512,2816]{1,0:T(8,128)(2,1)} %get-tuple-element.33), channel_id=1, source_target_pairs={{0,2},{1,3},{2,0},{3,1},{4,6},{5,7},{6,4},{7,5},{8,10},{9,11},{10,... | collective-permute-start | bytes 8650760 | tf_op jit(solution)/shard_map/ppermute | solution.py:237
  200.2 20.5 %all-to-all-start.1 = ((bf16[8,128,256]{1,2,0:T(8,128)(2,1)}), bf16[8,128,256]{1,2,0:T(8,128)(2,1)S(1)}, u32[]{:S(2)}, u32[]{:S(2)}) async-start(bf16[8,128,256]{1,2,0:T(8,128)(2,1)} %copy_bitcast_fusion.1), calls=%async_computation.1 | async-start | bytes 1048576 | tf_op jit(solution)/shard_map/all_to_all | solution.py:274
  220.7 38.4 %all-to-all-start.2 = ((bf16[8,64,1152]{2,1,0:T(8,128)(2,1)}), bf16[8,64,1152]{2,1,0:T(8,128)(2,1)S(1)}, u32[]{:S(2)}, u32[]{:S(2)}) async-start(bf16[8,64,1152]{2,1,0:T(8,128)(2,1)} %copy.153), calls=%async_computation.2 | async-start | bytes 2359296 | tf_op jit(solution)/shard_map/all_to_all | solution.py:274
  224.3 120.9 %all-gather.8.cloned.1.call-start = ((), (), s32[]{:S(2)}) async-start(), calls=%async_computation.14 | async-start | bytes 4718592 | tf_op jit(solution)/shard_map/all_gather | solution.py:266
  239.4 56.3 %collective-permute-start.10 = (bf16[2,1408,512]{2,1,0:T(8,128)(2,1)}, bf16[2,1408,512]{2,1,0:T(8,128)(2,1)}, u32[]{:S(2)}, u32[]{:S(2)}) collective-permute-start(bf16[2,1408,512]{2,1,0:T(8,128)(2,1)} %param.23), channel_id=1, source_target_pairs={{0,1},{1,0},{2,3},{3,2},{4,5},{5,4},{6,7},{7,6},{8,9},{9,8},{10,11... | collective-permute-start | bytes 8650760 | tf_op jit(solution)/shard_map/ppermute | solution.py:237
  259.2 25.9 %collective-permute-start.6 = (bf16[8,64,1152]{2,1,0:T(8,128)(2,1)S(1)}, bf16[8,64,1152]{2,1,0:T(8,128)(2,1)S(1)}, u32[]{:S(2)}, u32[]{:S(2)}) collective-permute-start(bf16[8,64,1152]{2,1,0:T(8,128)(2,1)S(1)} %all-to-all-done.2), channel_id=1, source_target_pairs={{0,2},{1,3},{2,0},{3,1},{4,6},{5,7},{6,4},{7,5},{8,10},{9,11},{10,... | collective-permute-start | bytes 3538952 | tf_op jit(solution)/shard_map/ppermute | solution.py:237
  260.5 106.7 %collective-permute-start.8 = (bf16[512,2816]{1,0:T(8,128)(2,1)}, bf16[512,2816]{1,0:T(8,128)(2,1)}, u32[]{:S(2)}, u32[]{:S(2)}) collective-permute-start(bf16[512,2816]{1,0:T(8,128)(2,1)} %copy-done.31), channel_id=1, source_target_pairs={{0,1},{1,0},{2,3},{3,2},{4,5},{5,4},{6,7},{7,6},{8,9},{9,8},{10,11... | collective-permute-start | bytes 8650760 | tf_op jit(solution)/shard_map/ppermute | solution.py:237
  260.5 116.5 %collective-permute-start.13 = (bf16[512,2816]{1,0:T(8,128)(2,1)}, bf16[512,2816]{1,0:T(8,128)(2,1)}, u32[]{:S(2)}, u32[]{:S(2)}) collective-permute-start(bf16[512,2816]{1,0:T(8,128)(2,1)} %get-tuple-element.33), channel_id=1, source_target_pairs={{0,1},{1,0},{2,3},{3,2},{4,5},{5,4},{6,7},{7,6},{8,9},{9,8},{10,11... | collective-permute-start | bytes 8650760 | tf_op jit(solution)/shard_map/ppermute | solution.py:237
  285.1 56.7 %collective-permute-start.11 = (bf16[2,1408,512]{2,1,0:T(8,128)(2,1)}, bf16[2,1408,512]{2,1,0:T(8,128)(2,1)}, u32[]{:S(2)}, u32[]{:S(2)}) collective-permute-start(bf16[2,1408,512]{2,1,0:T(8,128)(2,1)} %param.23), channel_id=1, source_target_pairs={{0,2},{1,3},{2,0},{3,1},{4,6},{5,7},{6,4},{7,5},{8,10},{9,11},{10,... | collective-permute-start | bytes 8650760 | tf_op jit(solution)/shard_map/ppermute | solution.py:237
  295.7 129.6 %all-gather.10.cloned.1.call-start = ((), (), s32[]{:S(2)}) async-start(), calls=%async_computation.15 | async-start | bytes 4718592 | tf_op jit(solution)/shard_map/all_gather | solution.py:266
  306.7 60.4 %collective-permute-start.9 = (bf16[512,2816]{1,0:T(8,128)(2,1)}, bf16[512,2816]{1,0:T(8,128)(2,1)}, u32[]{:S(2)}, u32[]{:S(2)}) collective-permute-start(bf16[512,2816]{1,0:T(8,128)(2,1)} %collective-permute-done), channel_id=1, source_target_pairs={{0,1},{1,0},{2,3},{3,2},{4,5},{5,4},{6,7},{7,6},{8,9},{9,8},{10,11... | collective-permute-start | bytes 8650760 | tf_op jit(solution)/shard_map/ppermute | solution.py:237
  307.2 69.7 %collective-permute-start.14 = (bf16[512,2816]{1,0:T(8,128)(2,1)}, bf16[512,2816]{1,0:T(8,128)(2,1)}, u32[]{:S(2)}, u32[]{:S(2)}) collective-permute-start(bf16[512,2816]{1,0:T(8,128)(2,1)} %collective-permute-done.4), channel_id=1, source_target_pairs={{0,1},{1,0},{2,3},{3,2},{4,5},{5,4},{6,7},{7,6},{8,9},{9,8},{10,11... | collective-permute-start | bytes 8650760 | tf_op jit(solution)/shard_map/ppermute | solution.py:237
  341.8 12.2 %collective-permute-start.12 = (bf16[2,1408,512]{2,1,0:T(8,128)(2,1)}, bf16[2,1408,512]{2,1,0:T(8,128)(2,1)}, u32[]{:S(2)}, u32[]{:S(2)}) collective-permute-start(bf16[2,1408,512]{2,1,0:T(8,128)(2,1)} %collective-permute-done.11), channel_id=1, source_target_pairs={{0,1},{1,0},{2,3},{3,2},{4,5},{5,4},{6,7},{7,6},{8,9},{9,8},{10,11... | collective-permute-start | bytes 8650760 | tf_op jit(solution)/shard_map/ppermute | solution.py:237
  345.3 243.1 %reduce-scatter.4.cloned.1.call-start = ((), (), s32[]{:S(2)}) async-start(), calls=%async_computation.16 | async-start | bytes 4718592 | tf_op jit(solution)/shard_map/reduce_scatter | solution.py:270
  501.9 178.7 %reduce-scatter.6.cloned.1.call-start = ((), (), s32[]{:S(2)}) async-start(), calls=%async_computation.17 | async-start | bytes 4718592 | tf_op jit(solution)/shard_map/reduce_scatter | solution.py:270
  595.7 48.4 %collective-permute-start.15 = (bf16[1408,512]{1,0:T(8,128)(2,1)}, bf16[1408,512]{1,0:T(8,128)(2,1)S(1)}, u32[]{:S(2)}, u32[]{:S(2)}) collective-permute-start(bf16[1408,512]{1,0:T(8,128)(2,1)} %convolution_convert_fusion.11), channel_id=1, source_target_pairs={{0,1},{1,0},{2,3},{3,2},{4,5},{5,4},{6,7},{7,6},{8,9},{9,8},{10,11... | collective-permute-start | bytes 4325384 | tf_op jit(solution)/shard_map/ppermute | solution.py:237
  629.2 229.8 %collective-permute-start.34 = (bf16[1408,512]{1,0:T(8,128)(2,1)}, bf16[1408,512]{1,0:T(8,128)(2,1)}, u32[]{:S(2)}, u32[]{:S(2)}) collective-permute-start(bf16[1408,512]{1,0:T(8,128)(2,1)} %convolution_convert_fusion.10), channel_id=1, source_target_pairs={{0,1},{1,0},{2,3},{3,2},{4,5},{5,4},{6,7},{7,6},{8,9},{9,8},{10,11... | collective-permute-start | bytes 4325384 | tf_op jit(solution)/shard_map/ppermute | solution.py:237
  629.7 68.4 %collective-permute-start.17 = (bf16[512,2816]{1,0:T(8,128)(2,1)}, bf16[512,2816]{1,0:T(8,128)(2,1)}, u32[]{:S(2)}, u32[]{:S(2)}) collective-permute-start(bf16[512,2816]{1,0:T(8,128)(2,1)} %convolution_convert_fusion.4), channel_id=1, source_target_pairs={{0,1},{1,0},{2,3},{3,2},{4,5},{5,4},{6,7},{7,6},{8,9},{9,8},{10,11... | collective-permute-start | bytes 8650760 | tf_op jit(solution)/shard_map/ppermute | solution.py:237
  629.7 64.0 %collective-permute-start.29 = (bf16[8,64,1152]{2,1,0:T(8,128)(2,1)}, bf16[8,64,1152]{2,1,0:T(8,128)(2,1)}, u32[]{:S(2)}, u32[]{:S(2)}) collective-permute-start(bf16[8,64,1152]{2,1,0:T(8,128)(2,1)} %get-tuple-element.74), channel_id=1, source_target_pairs={{0,1},{1,0},{2,3},{3,2},{4,5},{5,4},{6,7},{7,6},{8,9},{9,8},{10,11... | collective-permute-start | bytes 3538952 | tf_op jit(solution)/shard_map/ppermute | solution.py:237
  630.2 217.6 %collective-permute-start.28 = (bf16[8,64,1152]{2,1,0:T(8,128)(2,1)}, bf16[8,64,1152]{2,1,0:T(8,128)(2,1)}, u32[]{:S(2)}, u32[]{:S(2)}) collective-permute-start(bf16[8,64,1152]{2,1,0:T(8,128)(2,1)} %get-tuple-element.73), channel_id=1, source_target_pairs={{0,1},{1,0},{2,3},{3,2},{4,5},{5,4},{6,7},{7,6},{8,9},{9,8},{10,11... | collective-permute-start | bytes 3538952 | tf_op jit(solution)/shard_map/ppermute | solution.py:237
  647.3 56.5 %collective-permute-start.16 = (bf16[1408,512]{1,0:T(8,128)(2,1)}, bf16[1408,512]{1,0:T(8,128)(2,1)}, u32[]{:S(2)}, u32[]{:S(2)}) collective-permute-start(bf16[1408,512]{1,0:T(8,128)(2,1)} %add_convert_fusion.5), channel_id=1, source_target_pairs={{0,2},{1,3},{2,0},{3,1},{4,6},{5,7},{6,4},{7,5},{8,10},{9,11},{10,... | collective-permute-start | bytes 4325384 | tf_op jit(solution)/shard_map/ppermute | solution.py:237
  689.2 19.2 %all-to-all-start.4 = ((bf16[8,128,256]{2,1,0:T(8,128)(2,1)}), bf16[8,128,256]{2,1,0:T(8,128)(2,1)S(1)}, u32[]{:S(2)}, u32[]{:S(2)}) async-start(bf16[8,128,256]{2,1,0:T(8,128)(2,1)} %bitcast.281), calls=%async_computation.6 | async-start | bytes 1048576 | tf_op jit(solution)/shard_map/all_to_all | solution.py:274
  696.7 151.8 %collective-permute-start.30 = (bf16[8,64,1152]{2,1,0:T(8,128)(2,1)}, bf16[8,64,1152]{2,1,0:T(8,128)(2,1)}, u32[]{:S(2)}, u32[]{:S(2)}) collective-permute-start(bf16[8,64,1152]{2,1,0:T(8,128)(2,1)} %fusion.42), channel_id=1, source_target_pairs={{0,2},{1,3},{2,0},{3,1},{4,6},{5,7},{6,4},{7,5},{8,10},{9,11},{10,... | collective-permute-start | bytes 3538952 | tf_op jit(solution)/shard_map/ppermute | solution.py:237
  703.8 82.6 %collective-permute-start.18 = (bf16[512,2816]{1,0:T(8,128)(2,1)}, bf16[512,2816]{1,0:T(8,128)(2,1)}, u32[]{:S(2)}, u32[]{:S(2)}) collective-permute-start(bf16[512,2816]{1,0:T(8,128)(2,1)} %add_convert_fusion.3), channel_id=1, source_target_pairs={{0,2},{1,3},{2,0},{3,1},{4,6},{5,7},{6,4},{7,5},{8,10},{9,11},{10,... | collective-permute-start | bytes 8650760 | tf_op jit(solution)/shard_map/ppermute | solution.py:237
  726.7 141.6 %collective-permute-start.26 = (bf16[8,64,2048]{2,1,0:T(8,128)(2,1)}, bf16[8,64,2048]{2,1,0:T(8,128)(2,1)}, u32[]{:S(2)}, u32[]{:S(2)}) collective-permute-start(bf16[8,64,2048]{2,1,0:T(8,128)(2,1)} %get-tuple-element.64), channel_id=1, source_target_pairs={{0,1},{1,0},{2,3},{3,2},{4,5},{5,4},{6,7},{7,6},{8,9},{9,8},{10,11... | collective-permute-start | bytes 6291464 | tf_op jit(solution)/shard_map/ppermute | solution.py:237
  787.6 33.2 %all-to-all-start.5 = ((bf16[8,128,576]{1,2,0:T(8,128)(2,1)}), bf16[8,128,576]{1,2,0:T(8,128)(2,1)S(1)}, u32[]{:S(2)}, u32[]{:S(2)}) async-start(bf16[8,128,576]{1,2,0:T(8,128)(2,1)} %copy_bitcast_fusion), calls=%async_computation.8 | async-start | bytes 2359296 | tf_op jit(solution)/shard_map/all_to_all | solution.py:274
  793.4 252.7 %reduce-scatter.8.cloned.1.call-start = ((), (), s32[]{:S(2)}) async-start(), calls=%async_computation.18 | async-start | bytes 4718592 | tf_op jit(solution)/shard_map/reduce_scatter | solution.py:270
  841.1 15.5 %collective-permute-start.23 = (bf16[8,64,1088]{2,1,0:T(8,128)(2,1)}, bf16[8,64,1088]{2,1,0:T(8,128)(2,1)}, u32[]{:S(2)}, u32[]{:S(2)}) collective-permute-start(bf16[8,64,1088]{2,1,0:T(8,128)(2,1)} %get-tuple-element.80), channel_id=1, source_target_pairs={{0,1},{1,0},{2,3},{3,2},{4,5},{5,4},{6,7},{7,6},{8,9},{9,8},{10,11... | collective-permute-start | bytes 3342344 | tf_op jit(solution)/shard_map/ppermute | solution.py:237
  847.9 16.3 %collective-permute-start.37 = (bf16[1408,512]{1,0:T(8,128)(2,1)}, bf16[1408,512]{1,0:T(8,128)(2,1)S(1)}, u32[]{:S(2)}, u32[]{:S(2)}) collective-permute-start(bf16[1408,512]{1,0:T(8,128)(2,1)} %convolution_convert_fusion.9), channel_id=1, source_target_pairs={{0,1},{1,0},{2,3},{3,2},{4,5},{5,4},{6,7},{7,6},{8,9},{9,8},{10,11... | collective-permute-start | bytes 4325384 | tf_op jit(solution)/shard_map/ppermute | solution.py:237
  848.5 45.3 %collective-permute-start.33 = (bf16[512,2816]{1,0:T(8,128)(2,1)}, bf16[512,2816]{1,0:T(8,128)(2,1)}, u32[]{:S(2)}, u32[]{:S(2)}) collective-permute-start(bf16[512,2816]{1,0:T(8,128)(2,1)} %convolution_convert_fusion.1), channel_id=1, source_target_pairs={{0,1},{1,0},{2,3},{3,2},{4,5},{5,4},{6,7},{7,6},{8,9},{9,8},{10,11... | collective-permute-start | bytes 8650760 | tf_op jit(solution)/shard_map/ppermute | solution.py:237
  852.0 61.0 %all-to-all-start.9 = ((bf16[8,64,1152]{2,1,0:T(8,128)(2,1)}), bf16[8,64,1152]{2,1,0:T(8,128)(2,1)}, u32[]{:S(2)}, u32[]{:S(2)}) async-start(bf16[8,64,1152]{2,1,0:T(8,128)(2,1)} %fusion.44), calls=%async_computation.12 | async-start | bytes 2359296 | tf_op jit(solution)/shard_map/all_to_all | solution.py:274
  856.6 12.3 %collective-permute-start.22 = (bf16[8,64,1088]{2,1,0:T(8,128)(2,1)}, bf16[8,64,1088]{2,1,0:T(8,128)(2,1)S(1)}, u32[]{:S(2)}, u32[]{:S(2)}) collective-permute-start(bf16[8,64,1088]{2,1,0:T(8,128)(2,1)} %get-tuple-element.79), channel_id=1, source_target_pairs={{0,1},{1,0},{2,3},{3,2},{4,5},{5,4},{6,7},{7,6},{8,9},{9,8},{10,11... | collective-permute-start | bytes 3342344 | tf_op jit(solution)/shard_map/ppermute | solution.py:237
  859.0 28.9 %collective-permute-start.24 = (bf16[8,64,1088]{2,1,0:T(8,128)(2,1)S(1)}, bf16[8,64,1088]{2,1,0:T(8,128)(2,1)S(1)}, u32[]{:S(2)}, u32[]{:S(2)}) collective-permute-start(bf16[8,64,1088]{2,1,0:T(8,128)(2,1)S(1)} %fusion.45), channel_id=1, source_target_pairs={{0,2},{1,3},{2,0},{3,1},{4,6},{5,7},{6,4},{7,5},{8,10},{9,11},{10,... | collective-permute-start | bytes 3342344 | tf_op jit(solution)/shard_map/ppermute | solution.py:237
  865.3 70.5 %collective-permute-start.25 = (bf16[8,64,2048]{2,1,0:T(8,128)(2,1)}, bf16[8,64,2048]{2,1,0:T(8,128)(2,1)}, u32[]{:S(2)}, u32[]{:S(2)}) collective-permute-start(bf16[8,64,2048]{2,1,0:T(8,128)(2,1)} %get-tuple-element.63), channel_id=1, source_target_pairs={{0,1},{1,0},{2,3},{3,2},{4,5},{5,4},{6,7},{7,6},{8,9},{9,8},{10,11... | collective-permute-start | bytes 6291464 | tf_op jit(solution)/shard_map/ppermute | solution.py:237
  868.4 107.0 %collective-permute-start.31 = (bf16[512,2816]{1,0:T(8,128)(2,1)}, bf16[512,2816]{1,0:T(8,128)(2,1)}, u32[]{:S(2)}, u32[]{:S(2)}) collective-permute-start(bf16[512,2816]{1,0:T(8,128)(2,1)} %convolution_convert_fusion.3), channel_id=1, source_target_pairs={{0,1},{1,0},{2,3},{3,2},{4,5},{5,4},{6,7},{7,6},{8,9},{9,8},{10,11... | collective-permute-start | bytes 8650760 | tf_op jit(solution)/shard_map/ppermute | solution.py:237
  868.9 55.9 %collective-permute-start.35 = (bf16[1408,512]{1,0:T(8,128)(2,1)}, bf16[1408,512]{1,0:T(8,128)(2,1)}, u32[]{:S(2)}, u32[]{:S(2)}) collective-permute-start(bf16[1408,512]{1,0:T(8,128)(2,1)} %add_convert_fusion.4), channel_id=1, source_target_pairs={{0,2},{1,3},{2,0},{3,1},{4,6},{5,7},{6,4},{7,5},{8,10},{9,11},{10,... | collective-permute-start | bytes 4325384 | tf_op jit(solution)/shard_map/ppermute | solution.py:237
  887.9 75.9 %collective-permute-start.27 = (bf16[8,64,2048]{2,1,0:T(8,128)(2,1)}, bf16[8,64,2048]{2,1,0:T(8,128)(2,1)}, u32[]{:S(2)}, u32[]{:S(2)}) collective-permute-start(bf16[8,64,2048]{2,1,0:T(8,128)(2,1)} %fusion.9), channel_id=1, source_target_pairs={{0,2},{1,3},{2,0},{3,1},{4,6},{5,7},{6,4},{7,5},{8,10},{9,11},{10,... | collective-permute-start | bytes 6291464 | tf_op jit(solution)/shard_map/ppermute | solution.py:237
  893.7 96.0 %collective-permute-start.32 = (bf16[512,2816]{1,0:T(8,128)(2,1)}, bf16[512,2816]{1,0:T(8,128)(2,1)}, u32[]{:S(2)}, u32[]{:S(2)}) collective-permute-start(bf16[512,2816]{1,0:T(8,128)(2,1)} %convolution_convert_fusion.2), channel_id=1, source_target_pairs={{0,1},{1,0},{2,3},{3,2},{4,5},{5,4},{6,7},{7,6},{8,9},{9,8},{10,11... | collective-permute-start | bytes 8650760 | tf_op jit(solution)/shard_map/ppermute | solution.py:237
  913.0 56.5 %all-to-all-start.7 = ((bf16[8,64,960]{2,1,0:T(8,128)(2,1)}), bf16[8,64,960]{2,1,0:T(8,128)(2,1)}, u32[]{:S(2)}, u32[]{:S(2)}) async-start(bf16[8,64,960]{2,1,0:T(8,128)(2,1)} %slice.628), calls=%async_computation.10 | async-start | bytes 2097152 | tf_op jit(solution)/shard_map/all_to_all | solution.py:274
  924.8 100.1 %collective-permute-start.36 = (bf16[512,2816]{1,0:T(8,128)(2,1)}, bf16[512,2816]{1,0:T(8,128)(2,1)}, u32[]{:S(2)}, u32[]{:S(2)}) collective-permute-start(bf16[512,2816]{1,0:T(8,128)(2,1)} %add_convert_fusion.2), channel_id=1, source_target_pairs={{0,2},{1,3},{2,0},{3,1},{4,6},{5,7},{6,4},{7,5},{8,10},{9,11},{10,... | collective-permute-start | bytes 8650760 | tf_op jit(solution)/shard_map/ppermute | solution.py:237
  935.8 47.6 %collective-permute-start.38 = (bf16[1408,512]{1,0:T(8,128)(2,1)}, bf16[1408,512]{1,0:T(8,128)(2,1)}, u32[]{:S(2)}, u32[]{:S(2)}) collective-permute-start(bf16[1408,512]{1,0:T(8,128)(2,1)} %convolution_convert_fusion.8), channel_id=1, source_target_pairs={{0,1},{1,0},{2,3},{3,2},{4,5},{5,4},{6,7},{7,6},{8,9},{9,8},{10,11... | collective-permute-start | bytes 4325384 | tf_op jit(solution)/shard_map/ppermute | solution.py:237
  969.5 79.8 %all-to-all-start.8 = ((bf16[8,64,2048]{2,1,0:T(8,128)(2,1)}), bf16[8,64,2048]{2,1,0:T(8,128)(2,1)}, u32[]{:S(2)}, u32[]{:S(2)}) async-start(bf16[8,64,2048]{2,1,0:T(8,128)(2,1)} %fusion.11), calls=%async_computation.11 | async-start | bytes 4194304 | tf_op jit(solution)/shard_map/all_to_all | solution.py:274
  1056.9 12.4 %all-to-all-start.6 = ((f32[8,1,144]{2,1,0:T(1,128)}), f32[8,1,144]{2,1,0:T(1,128)S(1)}, u32[]{:S(2)}, u32[]{:S(2)}) async-start(f32[8,1,144]{2,1,0:T(1,128)} %all_to_all.39), calls=%async_computation.9 | async-start | bytes 16384 | tf_op jit(solution)/shard_map/all_to_all | solution.py:274
  (138 other events, 1392.7 us)
Sparse Core Ops, SparseCore 0:
  10.1 76.0 all-gather.11
  89.1 93.8 all-gather.5
  239.5 74.9 all-gather.7
  345.4 79.8 all-gather.9
  502.0 86.3 reduce-scatter.3
  592.9 87.6 reduce-scatter.5
  848.0 120.5 reduce-scatter.7

commit v3 on v2

--- a/solution.py
+++ b/solution.py
@@ -1,8 +1,11 @@
+import functools
 import math
 
 import jax
 import jax.numpy as jnp
 from jax import lax
+from jax.experimental import pallas as pl
+from jax.experimental.pallas import tpu as pltpu
 from jax.sharding import PartitionSpec as P
 
 D = 2048
@@ -17,6 +20,8 @@
 
 
 EPS = 1e-06
+VMEM_BYTES = 50 * 2**20
+VMEM_EXPERTS = 58 * 2**20
 
 
 def positions(row_count, tok_dev, n_ctx):
@@ -238,7 +243,7 @@
 
 
 def after(values, *first):
-    return lax.optimization_barrier((values, *first))[0]
+    return lax.optimization_barrier((values, first))[0]
 
 
 def fsdp_pieces(own):
@@ -254,12 +259,25 @@
     )
 
 
-def fsdp_reduce(blocks, rank):
-    kind = blocks.dtype
+def fsdp_reduce(blocks, rank, *gate):
     rel = [lax.dynamic_index_in_dim(blocks, rank ^ k, 0, False) for k in range(4)]
-    mine = rel[0].astype(jnp.float32) + fsdp_swap(rel[1], 1).astype(jnp.float32)
-    other = rel[2].astype(jnp.float32) + fsdp_swap(rel[3], 1).astype(jnp.float32)
-    return mine + fsdp_swap(other.astype(kind), 2).astype(jnp.float32)
+    return fsdp_reduce_terms(lambda k: rel[k].astype(jnp.float32), blocks.dtype, *gate)
+
+
+def fsdp_reduce_terms(term, kind, *gate):
+    near = [fsdp_swap(term(k).astype(kind), 1).astype(jnp.float32) for k in (1, 3)]
+    far = fsdp_swap((term(2) + near[1]).astype(kind), 2)
+    if gate:
+        far = after(far, *gate)
+    return term(0) + near[0] + far.astype(jnp.float32)
+
+
+def columns_by_distance(values, n_ctx, rank):
+    rows = values.shape[0]
+    split = values.reshape(rows, n_ctx, 4, -1)
+    return [
+        lax.dynamic_index_in_dim(split, rank ^ k, 2, False).reshape(rows, -1) for k in range(4)
+    ]
 
 
 def ctx_gather(values):
@@ -276,6 +294,10 @@
 
 def dot_f32(left, right, dims=((1,), (0,))):
     return lax.dot_general(left, right, (dims, ((), ())), preferred_element_type=jnp.float32)
+
+
+def experts_dot(spec, left, right):
+    return jnp.einsum(spec, left, right, preferred_element_type=jnp.float32)
 
 
 def pad_last(values, width):
@@ -297,37 +319,205 @@
     return stacked.transpose(1, 0, 2, 3).reshape(-1, stacked.shape[-1])
 
 
-def shard_rows(grads, n_ctx, rank):
+def shard_rows(grads, n_ctx, rank, *gate):
     width = grads.shape[-1]
     blocks = grads.astype(jnp.bfloat16).reshape(n_ctx, 4, -1, width).transpose(1, 0, 2, 3)
-    return fsdp_reduce(blocks, rank)
-
-
-def attention_heads(rows_q, rows_rot, lat_all, rot_all, allowed, score_scale):
-    query = jnp.concatenate([rows_q, rows_rot], -1)
-    key = jnp.concatenate([lat_all, rot_all], -1)
-    scores = dot_f32(query, key, ((1,), (1,))) * score_scale
-    scores = jnp.where(allowed, scores, -jnp.inf)
+    return fsdp_reduce(blocks, rank, *gate)
+
+
+def attention_forward_body(
+    nope_ref, rot_ref, lat_ref, key_rot_ref, key_up_ref, value_up_ref, row_pos_ref, key_pos_ref,
+    heads_ref, mixed_ref, total_ref, *, score_scale
+):
+    lat = lat_ref[...]
+    query = dot_f32(nope_ref[...], key_up_ref[0], ((1,), (1,))).astype(jnp.bfloat16)
+    scores = dot_f32(query, lat, ((1,), (1,))) + dot_f32(rot_ref[0], key_rot_ref[...], ((1,), (1,)))
+    scores = jnp.where(key_pos_ref[...] <= row_pos_ref[...], scores * score_scale, -jnp.inf)
     top_score = jnp.max(scores, -1, keepdims=True)
     log_total = top_score + jnp.log(jnp.sum(jnp.exp(scores - top_score), -1, keepdims=True))
-    probs = jnp.exp(scores - log_total)
-    mixed = dot_f32(probs.astype(jnp.bfloat16), lat_all)
-    return mixed, log_total
-
-
-def attention_heads_back(
-    rows_q, rows_rot, lat_all, rot_all, allowed, score_scale, log_total, mix_grad, delta
+    probs = jnp.exp(scores - log_total).astype(jnp.bfloat16)
+    mixed = dot_f32(probs, lat)
+    mixed_ref[0] = mixed
+    total_ref[0] = log_total
+    heads_ref[...] = dot_f32(mixed.astype(jnp.bfloat16), value_up_ref[0]).astype(jnp.bfloat16)
+
+
+def attention_backward_body(
+    grad_ref, nope_ref, rot_ref, mixed_ref, total_ref, lat_ref, key_rot_ref, key_up_ref,
+    value_up_ref, row_pos_ref, key_pos_ref, nope_grad_ref, rot_grad_ref, expand_ref, lat_sum_ref,
+    rot_sum_ref, *, score_scale
 ):
-    query = jnp.concatenate([rows_q, rows_rot], -1)
-    key = jnp.concatenate([lat_all, rot_all], -1)
-    scores = dot_f32(query, key, ((1,), (1,))) * score_scale
-    probs = jnp.where(allowed, jnp.exp(scores - log_total), 0.0)
-    prob_grad = dot_f32(mix_grad, lat_all, ((1,), (1,)))
+    head, block = pl.program_id(0), pl.program_id(1)
+    lat, key_rot = lat_ref[...], key_rot_ref[...]
+    nope, rot = nope_ref[...], rot_ref[0]
+    key_up, value_up = key_up_ref[0], value_up_ref[0]
+    head_grad = grad_ref[...]
+    mixed = mixed_ref[0]
+    query = dot_f32(nope, key_up, ((1,), (1,))).astype(jnp.bfloat16)
+    mix_grad = dot_f32(head_grad, value_up, ((1,), (1,))).astype(jnp.bfloat16)
+    delta = jnp.sum(mix_grad.astype(jnp.float32) * mixed, -1, keepdims=True)
+    scores = dot_f32(query, lat, ((1,), (1,))) + dot_f32(rot, key_rot, ((1,), (1,)))
+    probs = jnp.where(
+        key_pos_ref[...] <= row_pos_ref[...], jnp.exp(scores * score_scale - total_ref[0]), 0.0
+    )
+    prob_grad = dot_f32(mix_grad, lat, ((1,), (1,)))
     score_grad = (probs * (prob_grad - delta) * score_scale).astype(jnp.bfloat16)
-    query_g = dot_f32(score_grad, key)
-    key_g = dot_f32(score_grad, query, ((0,), (0,)))
-    lat_g = dot_f32(probs.astype(jnp.bfloat16), mix_grad, ((0,), (0,)))
-    return query_g, key_g[:, :KVL] + lat_g, key_g[:, KVL:]
+    lat_q_grad = dot_f32(score_grad, lat).astype(jnp.bfloat16)
+    rot_grad_ref[0] = dot_f32(score_grad, key_rot)
+    nope_grad_ref[...] = dot_f32(lat_q_grad, key_up).astype(jnp.bfloat16)
+    lat_terms = dot_f32(score_grad, query, ((0,), (0,))) + dot_f32(
+        probs.astype(jnp.bfloat16), mix_grad, ((0,), (0,))
+    )
+    rot_terms = dot_f32(score_grad, rot, ((0,), (0,)))
+    key_grad = dot_f32(lat_q_grad, nope, ((0,), (0,)))
+    value_grad = dot_f32(mixed.astype(jnp.bfloat16), head_grad, ((0,), (0,)))
+
+    @pl.when((head == 0) & (block == 0))
+    def _():
+        lat_sum_ref[...] = jnp.zeros_like(lat_sum_ref)
+        rot_sum_ref[...] = jnp.zeros_like(rot_sum_ref)
+
+    @pl.when(block == 0)
+    def _():
+        expand_ref[...] = jnp.zeros_like(expand_ref)
+
+    lat_sum_ref[...] += lat_terms
+    rot_sum_ref[...] += rot_terms
+    expand_ref[0, :, :DN] += key_grad
+    expand_ref[0, :, DN:] += value_grad
+
+
+def attention_forward_call(nope, rot, lat, key_rot, key_up, value_up, where_all, score_scale):
+    length, heads = nope.shape[0], rot.shape[0]
+    rows = min(256, length)
+    at_head = lambda h, i: (h, 0, 0)
+    whole = lambda h, i: (0, 0)
+    return pl.pallas_call(
+        functools.partial(attention_forward_body, score_scale=score_scale),
+        grid=(heads, length // rows),
+        in_specs=[
+            pl.BlockSpec((rows, DN), lambda h, i: (i, h)),
+            pl.BlockSpec((1, rows, DR), lambda h, i: (h, i, 0)),
+            pl.BlockSpec((length, KVL), whole),
+            pl.BlockSpec((length, DR), whole),
+            pl.BlockSpec((1, KVL, DN), at_head),
+            pl.BlockSpec((1, KVL, DV), at_head),
+            pl.BlockSpec((rows, 1), lambda h, i: (i, 0)),
+            pl.BlockSpec((1, length), whole),
+        ],
+        out_specs=[
+            pl.BlockSpec((rows, DV), lambda h, i: (i, h)),
+            pl.BlockSpec((1, rows, KVL), lambda h, i: (h, i, 0)),
+            pl.BlockSpec((1, rows, 1), lambda h, i: (h, i, 0)),
+        ],
+        out_shape=[
+            jax.ShapeDtypeStruct((length, heads * DV), jnp.bfloat16),
+            jax.ShapeDtypeStruct((heads, length, KVL), jnp.float32),
+            jax.ShapeDtypeStruct((heads, length, 1), jnp.float32),
+        ],
+        compiler_params=pltpu.CompilerParams(vmem_limit_bytes=VMEM_BYTES),
+    )(nope, rot, lat, key_rot, key_up, value_up, where_all[:, None], where_all[None, :])
+
+
+def attention_backward_call(
+    head_grad, nope, rot, mixed, total, lat, key_rot, key_up, value_up, where_all, score_scale
+):
+    length, heads = nope.shape[0], rot.shape[0]
+    rows = min(256, length)
+    at_head = lambda h, i: (h, 0, 0)
+    at_rows = lambda h, i: (h, i, 0)
+    whole = lambda h, i: (0, 0)
+    return pl.pallas_call(
+        functools.partial(attention_backward_body, score_scale=score_scale),
+        grid=(heads, length // rows),
+        in_specs=[
+            pl.BlockSpec((rows, DV), lambda h, i: (i, h)),
+            pl.BlockSpec((rows, DN), lambda h, i: (i, h)),
+            pl.BlockSpec((1, rows, DR), at_rows),
+            pl.BlockSpec((1, rows, KVL), at_rows),
+            pl.BlockSpec((1, rows, 1), at_rows),
+            pl.BlockSpec((length, KVL), whole),
+            pl.BlockSpec((length, DR), whole),
+            pl.BlockSpec((1, KVL, DN), at_head),
+            pl.BlockSpec((1, KVL, DV), at_head),
+            pl.BlockSpec((rows, 1), lambda h, i: (i, 0)),
+            pl.BlockSpec((1, length), whole),
+        ],
+        out_specs=[
+            pl.BlockSpec((rows, DN), lambda h, i: (i, h)),
+            pl.BlockSpec((1, rows, DR), at_rows),
+            pl.BlockSpec((1, KVL, DN + DV), at_head),
+            pl.BlockSpec((length, KVL), whole),
+            pl.BlockSpec((length, DR), whole),
+        ],
+        out_shape=[
+            jax.ShapeDtypeStruct((length, heads * DN), jnp.bfloat16),
+            jax.ShapeDtypeStruct((heads, length, DR), jnp.float32),
+            jax.ShapeDtypeStruct((heads, KVL, DN + DV), jnp.float32),
+            jax.ShapeDtypeStruct((length, KVL), jnp.float32),
+            jax.ShapeDtypeStruct((length, DR), jnp.float32),
+        ],
+        compiler_params=pltpu.CompilerParams(vmem_limit_bytes=VMEM_BYTES),
+    )(
+        head_grad, nope, rot, mixed, total, lat, key_rot, key_up, value_up,
+        where_all[:, None], where_all[None, :],
+    )
+
+
+def experts_body(x_ref, y_ref, gate_ref, gu_ref, dn_ref, act_ref, both_ref, out_ref, in_ref):
+    x, y = x_ref[0], y_ref[0]
+
+    def hidden_step(at, width):
+        cols, ups = pl.ds(at, width), pl.ds(FF + at, width)
+        gate = dot_f32(x, gu_ref[0, :, cols])
+        up = dot_f32(x, gu_ref[0, :, ups])
+        act_grad = dot_f32(y, dn_ref[0, cols, :], ((1,), (1,)))
+        sig = jax.nn.sigmoid(gate)
+        silu = gate * sig
+        act_ref[0, :, cols] = (silu * up).astype(jnp.bfloat16)
+        both_ref[0, :, cols] = (act_grad * up * sig * (1.0 + gate * (1.0 - sig))).astype(
+            jnp.bfloat16
+        )
+        both_ref[0, :, ups] = (act_grad * silu).astype(jnp.bfloat16)
+
+    tile = 256
+    whole = FF // tile
+
+    @pl.loop(0, whole, unroll=True)
+    def _(i):
+        hidden_step(pl.multiple_of(i * tile, 128), tile)
+
+    if FF % tile:
+        hidden_step(whole * tile, FF % tile)
+
+    @pl.loop(0, D // tile, unroll=2)
+    def _(i):
+        cols = pl.ds(pl.multiple_of(i * tile, tile), tile)
+        in_ref[0, :, cols] = dot_f32(both_ref[0], gu_ref[0, cols, :], ((1,), (1,))).astype(
+            jnp.bfloat16
+        )
+        out = dot_f32(act_ref[0], dn_ref[0, :, cols]).astype(jnp.bfloat16)
+        out_ref[0, :, cols] = (out.astype(jnp.float32) * gate_ref[0]).astype(jnp.bfloat16)
+
+
+def experts_call(x_exp, y_exp, slot_gate, gu_rel, dn_rel):
+    count, slots = x_exp.shape[:2]
+    at = lambda e: (e, 0, 0)
+    shape = lambda width: jax.ShapeDtypeStruct((count, slots, width), jnp.bfloat16)
+    return pl.pallas_call(
+        experts_body,
+        grid=(count,),
+        in_specs=[
+            pl.BlockSpec((1, slots, D), at, pipeline_mode=pl.Buffered(1)),
+            pl.BlockSpec((1, slots, D), at, pipeline_mode=pl.Buffered(1)),
+            pl.BlockSpec((1, slots, 1), at, pipeline_mode=pl.Buffered(1)),
+            pl.BlockSpec((1, D, 2 * FF), at),
+            pl.BlockSpec((1, FF, D), at),
+        ],
+        out_specs=[pl.BlockSpec((1, slots, w), at) for w in (FF, 2 * FF, D, D)],
+        out_shape=[shape(w) for w in (FF, 2 * FF, D, D)],
+        compiler_params=pltpu.CompilerParams(vmem_limit_bytes=VMEM_EXPERTS),
+    )(x_exp, y_exp, slot_gate, gu_rel, dn_rel)
 
 
 def on_device(
@@ -365,48 +555,45 @@
         return lax.dynamic_slice_in_dim(values, first_row, tok_dev, 0)
 
     exp_local = expert_gate_up.shape[0]
-    gu_far = []
-    for e in range(exp_local):
-        own = expert_gate_up[e]
-        gu_far.append(fsdp_swap(after(own, gu_far[-1]) if gu_far else own, 2))
+    steps = 4
+    step_rows = D // 4 // steps
+    gu_far = [
+        fsdp_swap(expert_gate_up[:, i * step_rows : (i + 1) * step_rows], 2) for i in range(steps)
+    ]
     sff_dev = SFF // n_ctx
     sff_pad = -(-sff_dev // 128) * 128
     attn = attention_split if H % n_ctx == 0 else attention_whole
     attn_first, attn_mid, attn_backward = attn(
         hidden_in[0], tokens, norm_gains, w_query, w_latent, w_expand, w_output, where_all, score_scale
     )
-    first_done = attn_first(gu_far[0])
+    first_done, grads_all = attn_first(gu_far, swap_chunks(out_grad[0], rank, 1))
 
     gate_send = pad_last(columns_by_dest(shared_gate_up[:, :SFF], n_ctx), sff_pad)
     up_send = pad_last(columns_by_dest(shared_gate_up[:, SFF:], n_ctx), sff_pad)
     down_send = pad_last(rows_by_dest(shared_down, n_ctx), sff_pad)
     shared_send = jnp.concatenate([gate_send, up_send, down_send], -1)
     shared_got = ctx_exchange(after(shared_send, first_done))
-    shared_near = fsdp_swap(shared_got, 1)
-    shared_far = fsdp_swap(after(shared_got, gu_far[-1]), 2)
+    shared_far = fsdp_swap(shared_got, 2)
+
+    resid_mid = attn_mid(gu_far)
+    normed_mid, inv_mid = norm_forward(resid_mid, gain_mid)
+    mid_send = swap_chunks(normed_mid.astype(jnp.bfloat16), rank, 1)
+    mid_all = ctx_gather(mid_send)
     shared_full = whole_rows(
-        [shared_got, shared_near, shared_far, fsdp_swap(shared_far, 1)], rank
+        [shared_got, fsdp_swap(shared_got, 1), shared_far, fsdp_swap(after(shared_far, resid_mid), 1)], rank
     )
     shared_rel = swap_chunks(shared_full, rank, 0)
     shared_gu = shared_rel[:, : 2 * sff_pad]
     shared_dn = shared_rel[:, 2 * sff_pad :]
-    dn_far = fsdp_swap(after(expert_down, shared_far), 2)
-    gu_rel = [
-        jnp.concatenate(
-            [expert_gate_up[e], fsdp_swap(expert_gate_up[e], 1), gu_far[e], fsdp_swap(gu_far[e], 1)],
-            0,
-        )
-        for e in range(exp_local)
-    ]
+    gu_rel = jnp.concatenate(
+        [expert_gate_up, fsdp_swap(expert_gate_up, 1), *gu_far]
+        + [fsdp_swap(after(v, resid_mid), 1) for v in gu_far],
+        1,
+    )
+    dn_far = fsdp_swap(after(expert_down, first_done), 2)
     dn_rel = jnp.concatenate(
-        [expert_down, fsdp_swap(expert_down, 1), dn_far, fsdp_swap(dn_far, 1)], 2
-    )
-    dn_rel = [dn_rel[e] for e in range(exp_local)]
-
-    resid_mid = attn_mid(gu_far[-1])
-    normed_mid, inv_mid = norm_forward(resid_mid, gain_mid)
-    mid_all = ctx_gather(swap_chunks(normed_mid.astype(jnp.bfloat16), rank, 1))
-
+        [expert_down, fsdp_swap(expert_down, 1), dn_far, fsdp_swap(after(dn_far, mid_send), 1)], 2
+    )
     n_exp = exp_local * n_ctx
     capacity = max(2, 9 * tok_dev * TOP // (8 * n_exp))
     slots = capacity * n_ctx
@@ -419,7 +606,6 @@
     routes_all = ctx_exchange(
         after(jnp.broadcast_to(routes[None], (n_ctx, tok_dev, 4 * TOP)), shared_got)
     ).reshape(length, 4 * TOP)
-    grads_all = ctx_gather(after(swap_chunks(out_grad[0], rank, 1), mid_all))
     ids_all = routes_all[:, :TOP].astype(jnp.float32)
     gates_all = (
         routes_all[:, TOP : 2 * TOP].astype(jnp.float32)
@@ -436,117 +622,84 @@
     pick = taken.astype(jnp.bfloat16).reshape(exp_local * slots, length)
     slot_gate = jnp.sum(jnp.where(taken, gate_of[:, None, :], 0.0), -1).reshape(-1, 1)
 
+    quarter = D // 4
+    y_exp = (dot_f32(pick, grads_all) * slot_gate).astype(jnp.bfloat16)
+    y_exp = y_exp.reshape(exp_local, slots, D)
+    s_act_grad = dot_f32(grads_all, shared_dn)
+    x_exp = dot_f32(pick, mid_all).astype(jnp.bfloat16).reshape(exp_local, slots, D)
+    e_act, both_grad, out_slots, in_slots = experts_call(
+        x_exp, y_exp, slot_gate.reshape(exp_local, slots, 1), gu_rel, dn_rel
+    )
     s_both = dot_f32(mid_all, shared_gu)
     s_gate = s_both[:, :sff_pad]
     s_up = s_both[:, sff_pad:]
     s_sig = jax.nn.sigmoid(s_gate)
     s_silu = s_gate * s_sig
     s_act = (s_silu * s_up).astype(jnp.bfloat16)
-    x_slots = dot_f32(pick, mid_all).astype(jnp.bfloat16)
-    x_exp = [x_slots[e * slots : (e + 1) * slots] for e in range(exp_local)]
-    e_both = [dot_f32(x_exp[e], gu_rel[e]) for e in range(exp_local)]
-    e_gate = [v[:, :FF] for v in e_both]
-    e_up = [v[:, FF:] for v in e_both]
-    e_sig = [jax.nn.sigmoid(v) for v in e_gate]
-    e_silu = [g * v for g, v in zip(e_gate, e_sig)]
-    e_act = [(g * u).astype(jnp.bfloat16) for g, u in zip(e_silu, e_up)]
-    out_slots = [
-        dot_f32(e_act[e], dn_rel[e]).astype(jnp.bfloat16).astype(jnp.float32)
-        for e in range(exp_local)
-    ]
-    out_slots = (jnp.concatenate(out_slots, 0) * slot_gate).astype(jnp.bfloat16)
-    out_part = dot_f32(s_act, shared_dn, ((1,), (1,))) + dot_f32(pick, out_slots, ((0,), (0,)))
-    out_part = out_part.astype(jnp.bfloat16)
-
-    s_act_grad = dot_f32(grads_all, shared_dn)
     s_both_grad = jnp.concatenate(
         [s_act_grad * s_up * s_sig * (1.0 + s_gate * (1.0 - s_sig)), s_act_grad * s_silu], -1
     ).astype(jnp.bfloat16)
-    y_slots = (dot_f32(pick, grads_all) * slot_gate).astype(jnp.bfloat16)
-    y_exp = [y_slots[e * slots : (e + 1) * slots] for e in range(exp_local)]
-    both_grad = []
-    for e in range(exp_local):
-        act_grad = dot_f32(y_exp[e], dn_rel[e], ((1,), (1,)))
-        gate_part = act_grad * e_up[e] * e_sig[e] * (1.0 + e_gate[e] * (1.0 - e_sig[e]))
-        both_grad.append(
-            jnp.concatenate([gate_part, act_grad * e_silu[e]], -1).astype(jnp.bfloat16)
-        )
-    in_slots = jnp.concatenate(
-        [
-            dot_f32(both_grad[e], gu_rel[e], ((1,), (1,))).astype(jnp.bfloat16)
-            for e in range(exp_local)
-        ],
-        0,
-    )
     mid_part = dot_f32(s_both_grad, shared_gu, ((1,), (1,))) + dot_f32(
-        pick, in_slots, ((0,), (0,))
+        pick, in_slots.reshape(-1, D), ((0,), (0,))
     )
     mid_part = mid_part.astype(jnp.bfloat16)
-    mid_grad = ctx_scatter(mid_part)
-    ffn_out = swap_chunks(ctx_scatter(after(out_part, mid_grad)), rank, 1)
-    mid_grad = swap_chunks(mid_grad.astype(jnp.float32), rank, 1)
-    hidden_out = (resid_mid + ffn_out.astype(jnp.float32)).astype(jnp.bfloat16)
-
-    quarter = D // 4
-
-    def chunk(values, k):
-        return values[:, k * quarter : (k + 1) * quarter]
-
-    grad_far = []
-
-    def reduce_expert(term, depends):
-        out1 = fsdp_swap(term(1).astype(jnp.bfloat16), 1)
-        out3 = fsdp_swap(term(3).astype(jnp.bfloat16), 1)
-        other = (term(2) + out3.astype(jnp.float32)).astype(jnp.bfloat16)
-        if depends:
-            other = after(other, depends[-1])
-        far = fsdp_swap(other, 2)
-        depends.append(far)
-        return other, lambda: term(0) + out1.astype(jnp.float32) + far.astype(jnp.float32)
-
-    finish = []
-    ready = []
-    for e in range(exp_local):
-        x_e = after(x_exp[e], mid_part)
-
-        def dn_term(k, e=e):
-            return dot_f32(e_act[e], chunk(y_exp[e], k), ((0,), (0,)))
-
-        def gu_term(k, e=e, x_e=x_e):
-            return dot_f32(chunk(x_e, k), both_grad[e], ((0,), (0,)))
-
-        for term in (dn_term, gu_term):
-            other, last = reduce_expert(term, grad_far)
-            ready.append(other)
-            finish.append(last)
-
+
+    x_late, y_late, act_late = after((x_exp, y_exp, e_act), mid_part)
+
+    def dn_term(k):
+        return experts_dot("esf,esd->efd", act_late, y_late[..., k * quarter : (k + 1) * quarter])
+
+    dn_send = [dn_term(k).astype(jnp.bfloat16) for k in (1, 3)]
+    dn_got = [fsdp_swap(v, 1).astype(jnp.float32) for v in dn_send]
+    dn_other = (dn_term(2) + dn_got[1]).astype(jnp.bfloat16)
+    dn_back = [fsdp_swap(dn_other[e], 2) for e in range(exp_local)]
+
+    def gu_term(k):
+        return experts_dot("esd,esf->edf", x_late[..., k * quarter : (k + 1) * quarter], both_grad)
+
+    gu_send = [gu_term(k).astype(jnp.bfloat16) for k in (1, 3)]
+    gu_got = [fsdp_swap(v, 1).astype(jnp.float32) for v in gu_send]
+    gu_other = (gu_term(2) + gu_got[1]).astype(jnp.bfloat16)
+    gu_back = [fsdp_swap(gu_other[e], 2) for e in range(exp_local)]
     shared_grad = jnp.concatenate(
         [
-            dot_f32(mid_all, s_both_grad, ((0,), (0,))),
-            dot_f32(grads_all, s_act, ((0,), (0,))),
+            dot_f32(after(mid_all, mid_part), s_both_grad, ((0,), (0,))),
+            dot_f32(after(grads_all, mid_part), s_act, ((0,), (0,))),
         ],
         -1,
     )
-    shared_grad = shard_rows(swap_chunks(shared_grad, rank, 0), n_ctx, rank).astype(jnp.bfloat16)
-    shared_grad = ctx_exchange(shared_grad).astype(jnp.float32)
+    shared_grad = swap_chunks(shared_grad, rank, 0).astype(jnp.bfloat16)
+    out_late = after(out_slots, mid_part).reshape(-1, D)
+    out_part = dot_f32(s_act, shared_dn, ((1,), (1,))) + dot_f32(pick, out_late, ((0,), (0,)))
+    out_part = out_part.astype(jnp.bfloat16)
+    mid_grad = after(ctx_scatter(mid_part), dn_back[0], gu_other, shared_grad, out_part)
+    ffn_out = ctx_exchange(after(out_part, mid_grad).reshape(n_ctx, tok_dev, D))
+    mid_grad = swap_chunks(mid_grad.astype(jnp.float32), rank, 1)
+    resid_norm_grad, gain_mid_grad = norm_backward(resid_mid, inv_mid, gain_mid, mid_grad)
+    resid_grad = out_grad[0].astype(jnp.float32) + resid_norm_grad
+
+    def reduce_gains(gain_in_grad, gain_lat_grad):
+        gains = jnp.concatenate([gain_in_grad, gain_mid_grad, gain_lat_grad], 0)
+        gains = fsdp_reduce(gains.reshape(n_ctx, 4, -1).transpose(1, 0, 2), rank)
+        return jnp.sum(ctx_exchange(gains), 0)
+
+    token_grad, stage, gains_grad, query_w, latent_w, expand_w, output_w = attn_backward(
+        resid_grad.astype(jnp.bfloat16), (dn_back[1:] + gu_back[:1], gu_back[1:], ffn_out), reduce_gains
+    )
+    heads_there, keys_there = stage
+    shared_term = shard_rows(shared_grad, n_ctx, rank, heads_there).astype(jnp.bfloat16)
+    shared_grad = after(ctx_exchange(shared_term), keys_there).astype(jnp.float32)
     gate_grad = shared_grad[:, :, :sff_dev].transpose(1, 0, 2).reshape(-1, SFF)
     up_grad = shared_grad[:, :, sff_pad : sff_pad + sff_dev].transpose(1, 0, 2).reshape(-1, SFF)
     shared_gu_grad = jnp.concatenate([gate_grad, up_grad], -1)
     down_grad = shared_grad[:, :, 2 * sff_pad : 2 * sff_pad + sff_dev]
     shared_dn_grad = down_grad.transpose(0, 2, 1).reshape(SFF, -1)
 
-    resid_norm_grad, gain_mid_grad = norm_backward(resid_mid, inv_mid, gain_mid, mid_grad)
-    resid_grad = out_grad[0].astype(jnp.float32) + resid_norm_grad
-    token_grad, gain_in_grad, gain_lat_grad, query_w, latent_w, expand_w, output_w = attn_backward(
-        after(resid_grad.astype(jnp.bfloat16), *ready[:1]), grad_far
-    )
     hidden_in_grad = (resid_grad + token_grad).astype(jnp.bfloat16)
-    gains = jnp.concatenate([gain_in_grad, gain_mid_grad, gain_lat_grad], 0)
-    gains = fsdp_reduce(gains.reshape(n_ctx, 4, -1).transpose(1, 0, 2), rank)
-    gains_grad = jnp.sum(ctx_exchange(gains), 0)
-    finals = [last() for last in finish]
-    dn_grad = jnp.stack(finals[0::2], 0)
-    gu_grad = jnp.stack(finals[1::2], 0)
+    ffn_out = jnp.sum(after(ffn_out, keys_there, gains_grad).astype(jnp.float32), 0)
+    hidden_out = (resid_mid + swap_chunks(ffn_out, rank, 1)).astype(jnp.bfloat16)
+    dn_grad = dn_term(0) + dn_got[0] + after(jnp.stack(dn_back), keys_there).astype(jnp.float32)
+    gu_grad = gu_term(0) + gu_got[0] + after(jnp.stack(gu_back), keys_there).astype(jnp.float32)
     return (
         hidden_out[None],
         hidden_in_grad[None],
@@ -583,7 +736,7 @@
     q_wide = n_wide + r_wide
     saved = {}
 
-    def first(early):
+    def first(early, extra):
         by_head = w_query.reshape(rows, n_ctx, heads, DN + DR)
         query_send = jnp.concatenate(
             [
@@ -594,6 +747,7 @@
         ).transpose(1, 0, 2)
         latent_send = jnp.broadcast_to(w_latent[None], (n_ctx,) + w_latent.shape)
         got = ctx_exchange(jnp.concatenate([query_send, latent_send], -1))
+        got = after(got, early[0])
         pieces = fsdp_pieces(jnp.concatenate([got, w_expand.reshape(n_ctx, rows, -1)], -1))
         full = whole_rows(pieces, rank)
         query_full = full[:, :q_wide]
@@ -605,10 +759,12 @@
             .reshape(KVL, -1)
         )
         expand_heads = expand_full.reshape(KVL, heads, DN + DV)
-        key_up = [expand_heads[:, j, :DN] for j in range(heads)]
-        value_up = [expand_heads[:, j, DN:] for j in range(heads)]
-
-        hidden_all = after(ctx_gather(hidden_bf), early)
+        key_up = expand_heads[:, :, :DN].transpose(1, 0, 2)
+        value_up = expand_heads[:, :, DN:].transpose(1, 0, 2)
+
+        both_all = lax.all_gather(jnp.stack([hidden_bf, extra]), "ctx", axis=1, tiled=True)
+        both_all = after(both_all, early[1:3], full)
+        hidden_all = both_all[0]
         output_full = lax.all_gather(
             after(w_output, hidden_all), ("ctx", "fsdp"), axis=1, tiled=True
         )
@@ -622,77 +778,65 @@
         lat_normed, inv_lat = norm_forward(lat_raw, gain_lat)
         latent = lat_normed.astype(jnp.bfloat16)
         key_rot = rope_apply(compressed[:, KVL:], cos_table, sin_table).astype(jnp.bfloat16)
-        allowed = where_all[None, :] <= where_all[:, None]
-        per_head = []
-        out_part = []
-        for j in range(heads):
-            nope = query_all[:, j * DN : (j + 1) * DN].astype(jnp.bfloat16)
-            rot = rope_apply(
-                query_all[:, n_wide + j * DR : n_wide + (j + 1) * DR], cos_table, sin_table
-            ).astype(jnp.bfloat16)
-            lat_q = dot_f32(nope, key_up[j], ((1,), (1,))).astype(jnp.bfloat16)
-            mixed, log_total = attention_heads(lat_q, rot, latent, key_rot, allowed, score_scale)
-            mixed_bf = mixed.astype(jnp.bfloat16)
-            out_part.append(dot_f32(mixed_bf, value_up[j]).astype(jnp.bfloat16))
-            per_head.append((nope, rot, lat_q, mixed, mixed_bf, log_total))
+        nope = query_all[:, :n_wide].astype(jnp.bfloat16)
+        rot = jnp.stack(
+            [
+                rope_apply(
+                    query_all[:, n_wide + j * DR : n_wide + (j + 1) * DR], cos_table, sin_table
+                )
+                for j in range(heads)
+            ]
+        ).astype(jnp.bfloat16)
+        heads_out, mixed, log_total = attention_forward_call(
+            nope, rot, latent, key_rot, key_up, value_up, where_all, score_scale
+        )
         saved.update(locals())
-        return hidden_all
+        return hidden_all, both_all[1]
 
     def middle(early):
-        heads_out = jnp.concatenate(saved["out_part"], -1).reshape(n_ctx, tok_dev, heads * DV)
+        heads_out = saved["heads_out"].reshape(n_ctx, tok_dev, heads * DV)
         own_heads = ctx_exchange(heads_out).transpose(1, 0, 2).reshape(tok_dev, H * DV)
-        saved["own_heads"] = own_heads
         return tokens + dot_f32(after(own_heads, early), saved["output_full"])
 
-    def backward(resid_bf, stages):
+    def backward(resid_bf, stages, reduce_gains):
         query_full, latent_full = saved["query_full"], saved["latent_full"]
-        key_up, value_up = saved["key_up"], saved["value_up"]
-        latent, key_rot, allowed = saved["latent"], saved["key_rot"], saved["allowed"]
         cos_table, sin_table = saved["cos_table"], saved["sin_table"]
-        normed_bf, own_heads = saved["normed_bf"], saved["own_heads"]
+        normed_bf = saved["normed_bf"]
         heads_grad = dot_f32(resid_bf, saved["output_full"], ((1,), (1,))).astype(jnp.bfloat16)
         heads_grad = ctx_exchange(columns_by_dest(heads_grad, n_ctx)).reshape(length, heads * DV)
         heads_grad = after(heads_grad, stages[0])
-        output_g = dot_f32(after(resid_bf, heads_grad), own_heads, ((0,), (0,)))
-        output_w = ctx_exchange(shard_rows(output_g, n_ctx, rank).astype(jnp.bfloat16))
-        output_w = jnp.sum(output_w.astype(jnp.float32), 0).T
-        lat_total = jnp.zeros((length, KVL), jnp.float32)
-        rot_total = jnp.zeros((length, DR), jnp.float32)
-        expand_parts = []
-        nope_parts = []
-        rope_parts = []
-        query_parts = []
-        for j in range(heads):
-            nope, rot, lat_q, mixed, mixed_bf, log_total = saved["per_head"][j]
-            head_g = heads_grad[:, j * DV : (j + 1) * DV]
-            mix_grad = dot_f32(head_g, value_up[j], ((1,), (1,))).astype(jnp.bfloat16)
-            delta = jnp.sum(mix_grad.astype(jnp.float32) * mixed, -1, keepdims=True)
-            query_g, lat_g, rot_g = attention_heads_back(
-                lat_q, rot, latent, key_rot, allowed, score_scale, log_total, mix_grad, delta
-            )
-            lat_total = lat_total + lat_g
-            rot_total = rot_total + rot_g
-            query_parts.append(query_g)
+        resid_all = ctx_gather(after(resid_bf, heads_grad))
+        nope_grad, rot_grad, expand_g, lat_total, rot_total = attention_backward_call(
+            heads_grad, saved["nope"], saved["rot"], saved["mixed"], saved["log_total"],
+            saved["latent"], saved["key_rot"], saved["key_up"], saved["value_up"], where_all,
+            score_scale,
+        )
         key_terms = jnp.concatenate([lat_total, rot_total], -1).astype(jnp.bfloat16)
+        key_terms = after(key_terms, stages[1])
         key_got = ctx_exchange(
-            after(key_terms, stages[1]).reshape(n_ctx, tok_dev, KVL + DR)
-        )
-        for j in range(heads):
-            nope, rot, lat_q, mixed, mixed_bf, log_total = saved["per_head"][j]
-            head_g = heads_grad[:, j * DV : (j + 1) * DV]
-            lat_q_grad = query_parts[j][:, :KVL].astype(jnp.bfloat16)
-            nope_parts.append(dot_f32(lat_q_grad, key_up[j]))
-            rope_parts.append(rope_back(query_parts[j][:, KVL:], cos_table, sin_table))
-            lat_q_grad = after(lat_q_grad, key_terms)
-            expand_parts.append(dot_f32(lat_q_grad, nope, ((0,), (0,))))
-            expand_parts.append(dot_f32(mixed_bf, head_g, ((0,), (0,))))
-        query_grad = jnp.concatenate(nope_parts + rope_parts, -1).astype(jnp.bfloat16)
+            key_terms.reshape(n_ctx, tok_dev, KVL + DR)
+        )
+        rot_grads = [
+            rope_back(rot_grad[j], cos_table, sin_table).astype(jnp.bfloat16) for j in range(heads)
+        ]
+        query_grad = jnp.concatenate([nope_grad, *rot_grads], -1)
+        key_got = after(key_got, resid_all)
         in_part = dot_f32(query_grad, query_full, ((1,), (1,))).astype(jnp.bfloat16)
-        in_grad = ctx_scatter(in_part).astype(jnp.float32)
+        in_grad = ctx_scatter(after(in_part, resid_all))
         gain_in_grad = jnp.sum(
             in_part.astype(jnp.float32) * (saved["hidden_f"] * saved["inv_all"]), 0
         )
-        query_g_w = dot_f32(normed_bf, query_grad, ((0,), (0,)))
+        normed_cols = columns_by_distance(normed_bf, n_ctx, rank)
+        query_terms = fsdp_reduce_terms(
+            lambda k: dot_f32(after(normed_cols[k], in_part), query_grad, ((0,), (0,))),
+            jnp.bfloat16,
+        )
+        query_terms = ctx_exchange(query_terms.astype(jnp.bfloat16).reshape(n_ctx, rows, q_wide))
+        query_terms = query_terms.astype(jnp.float32)
+        resid_cols = columns_by_distance(after(resid_all, in_part), n_ctx, rank)
+        output_w = fsdp_reduce_terms(
+            lambda k: dot_f32(resid_cols[k], saved["heads_out"], ((0,), (0,))), jnp.bfloat16
+        )
         key_sum = jnp.sum(key_got.astype(jnp.float32), 0)
         own_cos, own_sin = own_rows(cos_table), own_rows(sin_table)
         lat_in_grad, gain_lat_grad = norm_backward(
@@ -701,24 +845,28 @@
         compressed_grad = jnp.concatenate(
             [lat_in_grad, rope_back(key_sum[:, KVL:], own_cos, own_sin)], -1
         ).astype(jnp.bfloat16)
-        latent_g = dot_f32(own_rows(normed_bf), compressed_grad, ((0,), (0,)))
+        own_cols = columns_by_distance(own_rows(normed_bf), n_ctx, rank)
+        latent_w = fsdp_reduce_terms(
+            lambda k: dot_f32(own_cols[k], compressed_grad, ((0,), (0,))), jnp.bfloat16
+        )
+        latent_w = after(latent_w.astype(jnp.bfloat16), stages[2])
+        latent_w = ctx_exchange(latent_w.reshape(n_ctx, rows, KVL + DR))
+        latent_w = jnp.sum(after(latent_w, in_grad).astype(jnp.float32), 0)
+        output_w = ctx_exchange(output_w.astype(jnp.bfloat16).reshape(n_ctx, rows, heads * DV))
+        output_w = output_w.astype(jnp.float32).transpose(0, 2, 1).reshape(H * DV, rows)
         inv_in = own_rows(saved["inv_all"])
         in_own = dot_f32(compressed_grad, latent_full, ((1,), (1,)))
         gain_in_grad = gain_in_grad + jnp.sum(in_own * (tokens * inv_in), 0)
-        token_grad = norm_backward(tokens, inv_in, gain_in, in_grad + in_own)[0]
-        expand_g = jnp.concatenate(expand_parts, -1)
-        expand_cols = expand_g.reshape(n_ctx, rows, 4, -1).transpose(0, 2, 1, 3).reshape(D, -1)
-        terms = shard_rows(
-            jnp.concatenate([query_g_w, latent_g, expand_cols], -1), n_ctx, rank
-        )
-        expand_w = terms[:, :, q_wide + KVL + DR :].reshape(KVL, -1)
-        sent = ctx_exchange(terms[:, :, : q_wide + KVL + DR].astype(jnp.bfloat16))
-        sent = sent.astype(jnp.float32)
-        nope_w = sent[:, :, :n_wide].reshape(n_ctx, rows, heads, DN)
-        rot_w = sent[:, :, n_wide:q_wide].reshape(n_ctx, rows, heads, DR)
+        gains_grad = reduce_gains(gain_in_grad, gain_lat_grad)
+        expand_g = expand_g.transpose(1, 0, 2)
+        expand_blocks = expand_g.reshape(KVL, 4, -1).transpose(1, 0, 2).astype(jnp.bfloat16)
+        expand_w = fsdp_reduce(expand_blocks, rank)
+        nope_w = query_terms[:, :, :n_wide].reshape(n_ctx, rows, heads, DN)
+        rot_w = query_terms[:, :, n_wide:].reshape(n_ctx, rows, heads, DR)
         query_w = jnp.concatenate([nope_w, rot_w], -1).transpose(1, 0, 2, 3).reshape(rows, -1)
-        latent_w = jnp.sum(sent[:, :, q_wide:], 0)
-        return token_grad, gain_in_grad, gain_lat_grad, query_w, latent_w, expand_w, output_w
+        in_grad = after(in_grad, gains_grad).astype(jnp.float32) + in_own
+        token_grad = norm_backward(tokens, inv_in, gain_in, in_grad)[0]
+        return token_grad, (heads_grad, key_got), gains_grad, query_w, latent_w, expand_w, output_w
 
     return first, middle, backward
 
@@ -777,7 +925,7 @@
     )
     resid_mid = tokens + dot_f32(heads_out, output_full)
 
-    def backward(resid_bf, stages):
+    def backward(resid_bf, stages, reduce_gains):
         output_g = dot_f32(heads_out, resid_bf, ((0,), (0,)))
         heads_grad = (
             dot_f32(resid_bf, output_full, ((1,), (1,)))
@@ -840,9 +988,10 @@
             )
             for g, at in ((query_g, 0), (latent_g, 0), (expand_g, 1), (output_g, 1))
         ]
-        return (token_grad, gain_in_grad, gain_lat_grad, *scattered)
-
-    return (lambda early: latent_full), (lambda early: resid_mid), backward
+        gains_grad = reduce_gains(gain_in_grad, gain_lat_grad)
+        return (token_grad, (heads_grad, latent_grad), gains_grad, *scattered)
+
+    return (lambda early, extra: (latent_full, ctx_gather(extra))), (lambda early: resid_mid), backward
 
 
 def solution(mesh):

time: 1080 us -> 1020 us (0.944)
  matrix products: 268 us -> 162 us
  Pallas kernels: 0 us -> 87.8 us
  waiting for transfers between devices: 496 us -> 413 us
  other arithmetic: 83.8 us -> 124 us
  blocking collectives: 34.2 us -> 0 us
  starting transfers between devices: 66.6 us -> 87.4 us
    dot_general x67 -> x28, matrix products: 268 us -> 113 us  [dot_f32(): lax.dot_general(left, right, (dims, ((), ())), preferred_element_type=jnp...]
    reduce_scatter x3 -> x2, waiting for transfers between devices: 96.4 us -> 6.52 us  [ctx_scatter(): return lax.psum_scatter(values, 'ctx', scatter_dimension=0, tiled=True)]
    pallas_call x0 -> x3, Pallas kernels: none -> 87.8 us  [the longest x1 48.7 us: experts_call(): pl.pallas_call(experts_body, grid=(count,), in_specs=[pl.BlockSpec((1, sl...]
    all_to_all x9 -> x12, waiting for transfers between devices: 71.5 us -> 131 us  [ctx_exchange(): lax.all_to_all(values, 'ctx', split_axis=0, concat_axis=0, tiled=True)]
    dot_general x0 -> x8, matrix products: none -> 49.4 us  [experts_dot(): return jnp.einsum(spec, left, right, preferred_element_type=jnp.float32)]
    all_gather x3 -> x2, waiting for transfers between devices: 44.8 us -> 0.01 us  [ctx_gather(): return lax.all_gather(values, 'ctx', axis=0, tiled=True)]
    all_to_all x1 -> x0, blocking collectives: 34.2 us -> none  [ctx_exchange(): lax.all_to_all(values, 'ctx', split_axis=0, concat_axis=0, tiled=True)]
    all_to_all x9 -> x12, starting transfers between devices: 44 us -> 63 us  [ctx_exchange(): lax.all_to_all(values, 'ctx', split_axis=0, concat_axis=0, tiled=True)]
  transfers between devices with their start and end apart: 55 -> 62, of which waited for: 21 -> 22; matrix products, arithmetic and copies ran while one was open for 34% -> 35% of each run, Pallas kernels for 0% -> 4%
where the time goes in v3:
time: 1020 us; the launch traced here: 1010 us
  waiting for transfers between devices  413 us (40%)
  matrix products  162 us (16%)
  other arithmetic  124 us (12%)
  local copies, waits for them, and re-layouts  118 us (12%)
  Pallas kernels  87.8 us (9%)
  starting transfers between devices  87.4 us (9%)
  between operations  16 us (2%)
    ppermute x44, waiting for transfers between devices, fsdp_swap(): lax.ppermute(values, 'fsdp', [(at, at ^ distance) for at in range(count)])  275 us
    all_to_all x12, waiting for transfers between devices, ctx_exchange(): lax.all_to_all(values, 'ctx', split_axis=0, concat_axis=0, tiled=True)  131 us
    dot_general x28, matrix products, dot_f32(): lax.dot_general(left, right, (dims, ((), ())), preferred_element_type=jnp...  113 us
    all_to_all x12, starting transfers between devices, ctx_exchange(): lax.all_to_all(values, 'ctx', split_axis=0, concat_axis=0, tiled=True)  63 us
    dot_general x8, matrix products, experts_dot(): return jnp.einsum(spec, left, right, preferred_element_type=jnp.float32)  49.4 us
    pallas_call x1, Pallas kernels, experts_call(): pl.pallas_call(experts_body, grid=(count,), in_specs=[pl.BlockSpec((1, sl...  48.7 us
    unnamed x206, local copies, waits for them, and re-layouts  29.2 us
    pallas_call x1, Pallas kernels, attention_backward_call(): pl.pallas_call(functools.partial(attention_backward_body, score_scale=sco...  25.3 us
  transfers between devices with their start and end apart: 62, of which 22 were waited for; matrix products, arithmetic and copies ran while one was open for 35% of the time, Pallas kernels for 4%

profile of v3, /device:TPU:0, one launch (start us, length us, event | category | flops | bytes accessed | tf_op | source)
XLA Modules:
  0.0 1008.1 jit_solution(10467074228039324181)
XLA Ops:
  13.4 7.3 all-to-all-start
  27.6 31.7 %collective-permute-done.2 = bf16[2,128,2816]{2,1,0:T(8,128)(2,1)} collective-permute-done((bf16[2,128,2816]{2,1,0:T(8,128)(2,1)S(1)}, bf16[2,128,2816]{2,1,0:T(8,128)(2,1)}, u32[]{:S(2)}, u32[]{:S(2)}) %collective-permute-start.2) | collective-permute-done | bytes 1441824 | tf_op jit(solution)/shard_map/ppermute | solution.py:242
  59.3 12.9 %all-to-all-done = bf16[8,64,960]{2,1,0:T(8,128)(2,1)S(1)} async-done(((bf16[8,64,960]{2,1,0:T(8,128)(2,1)}), bf16[8,64,960]{2,1,0:T(8,128)(2,1)S(1)}, u32[]{:S(2)}, u32[]{:S(2)}) %all-to-all-start) | async-done | bytes 983072 | tf_op jit(solution)/shard_map/all_to_all | solution.py:292
  75.2 18.3 %collective-permute-done.4 = bf16[8,64,1088]{2,1,0:T(8,128)(2,1)} collective-permute-done((bf16[8,64,1088]{2,1,0:T(8,128)(2,1)}, bf16[8,64,1088]{2,1,0:T(8,128)(2,1)}, u32[]{:S(2)}, u32[]{:S(2)}) %collective-permute-start.4) | collective-permute-done | bytes 1114144 | tf_op jit(solution)/shard_map/ppermute | solution.py:242
  102.1 26.1 %collective-permute-done = bf16[2,128,2816]{2,1,0:T(8,128)(2,1)} collective-permute-done((bf16[2,128,2816]{2,1,0:T(8,128)(2,1)}, bf16[2,128,2816]{2,1,0:T(8,128)(2,1)}, u32[]{:S(2)}, u32[]{:S(2)}) %collective-permute-start) | collective-permute-done | bytes 1441824 | tf_op jit(solution)/shard_map/ppermute | solution.py:242
  128.2 30.4 %collective-permute-done.1 = bf16[2,128,2816]{2,1,0:T(8,128)(2,1)S(1)} collective-permute-done((bf16[2,128,2816]{2,1,0:T(8,128)(2,1)}, bf16[2,128,2816]{2,1,0:T(8,128)(2,1)S(1)}, u32[]{:S(2)}, u32[]{:S(2)}) %collective-permute-start.1) | collective-permute-done | bytes 1441824 | tf_op jit(solution)/shard_map/ppermute | solution.py:242
  158.6 8.1 slice_bitcast_fusion
  171.3 5.5 constant_dynamic-update-slice_fusion.9
  186.1 13.2 %all-to-all-start.2 = ((bf16[8,64,1152]{2,1,0:T(8,128)(2,1)}), bf16[8,64,1152]{2,1,0:T(8,128)(2,1)}, u32[]{:S(2)}, u32[]{:S(2)}) async-start(bf16[8,64,1152]{2,1,0:T(8,128)(2,1)} %copy.298), calls=%async_computation.2 | async-start | bytes 2359296 | tf_op jit(solution)/shard_map/all_to_all | solution.py:292
  217.5 13.8 %shard_map.212 = (bf16[1024,256]{1,0:T(8,128)(2,1)S(1)}, f32[2,1024,512]{2,1,0:T(8,128)}, f32[2,1024,1]{2,1,0:T(8,128)S(1)}) custom-call(bf16[1024,256]{1,0:T(8,128)(2,1)S(1)} %slice.392.nope_ref, bf16[2,1024,64]{2,1,0:T(8,128)(2,1)S(1)} %pad_maximum_fusion.20.rot_ref, bf16[1024,512]{1,0:T(8,128)(2,1)} %multiply_convert_fusion.2.lat_ref, ...), custom_call_target="tpu_custom_call" | custom-call | tf_op jit(solution)/shard_map/pallas_call | solution.py:395
  233.3 6.4 all-to-all-done.2
  250.4 22.6 %all-to-all-done.1 = bf16[8,128,256]{1,2,0:T(8,128)(2,1)S(1)} async-done(((bf16[8,128,256]{1,2,0:T(8,128)(2,1)}), bf16[8,128,256]{1,2,0:T(8,128)(2,1)S(1)}, u32[]{:S(2)}, u32[]{:S(2)}) %all-to-all-start.1) | async-done | bytes 524320 | tf_op jit(solution)/shard_map/all_to_all | solution.py:292
  284.4 6.5 multiply_reduce_fusion.3
  292.1 76.1 %collective-permute-done.8 = bf16[8,64,1152]{2,1,0:T(8,128)(2,1)} collective-permute-done((bf16[8,64,1152]{2,1,0:T(8,128)(2,1)}, bf16[8,64,1152]{2,1,0:T(8,128)(2,1)}, u32[]{:S(2)}, u32[]{:S(2)}) %collective-permute-start.8) | collective-permute-done | bytes 1179680 | tf_op jit(solution)/shard_map/ppermute | solution.py:242
  371.3 7.8 multiply_convert_fusion.1
  394.2 8.9 pad_maximum_fusion.dn_ref
  403.2 6.4 fusion.11
  409.6 5.6 multiply_convert_fusion.4
  415.3 5.8 fusion.9
  421.1 5.5 convolution_convert_fusion.5
  426.6 48.7 %shard_map.213 = (bf16[2,432,1408]{2,1,0:T(8,128)(2,1)}, bf16[2,432,2816]{2,1,0:T(8,128)(2,1)}, bf16[2,432,2048]{2,1,0:T(8,128)(2,1)}, bf16[2,432,2048]{2,1,0:T(8,128)(2,1)}) custom-call(bf16[2,432,2048]{2,1,0:T(8,128)(2,1)} %bitcast.305, bf16[2,432,2048]{2,1,0:T(8,128)(2,1)} %bitcast.310, f32[2,432,1]{2,1,0:T(8,128)} %copy.303.gate_ref, ...), custom_call_target="tpu_custom_call" | custom-call | tf_op jit(solution)/shard_map/pallas_call | solution.py:507
  475.4 9.8 fusion.6
  485.2 8.5 convolution_convert_fusion.1
  500.1 9.3 copy.309
  511.5 5.6 multiply_convert_fusion
  520.7 6.5 fusion.5
  534.5 6.0 add_convert_fusion
  543.8 23.1 %collective-permute-done.19 = bf16[1408,512]{1,0:T(8,128)(2,1)} collective-permute-done((bf16[1408,512]{1,0:T(8,128)(2,1)S(1)}, bf16[1408,512]{1,0:T(8,128)(2,1)}, u32[]{:S(2)}, u32[]{:S(2)}) %collective-permute-start.19) | collective-permute-done | bytes 1441824 | tf_op jit(solution)/shard_map/ppermute | solution.py:242
  567.0 6.5 reduce-scatter.3.cloned.1.call-done
  588.2 5.5 fusion.158
  593.7 5.7 fusion.52
  599.4 59.7 %collective-permute-done.22 = bf16[512,2816]{1,0:T(8,128)(2,1)} collective-permute-done((bf16[512,2816]{1,0:T(8,128)(2,1)}, bf16[512,2816]{1,0:T(8,128)(2,1)}, u32[]{:S(2)}, u32[]{:S(2)}) %collective-permute-start.22) | collective-permute-done | bytes 2883616 | tf_op jit(solution)/shard_map/ppermute | solution.py:242
  664.8 6.7 copy.317
  680.5 6.7 convolution_convert_fusion
  691.9 25.3 %shard_map.214 = (bf16[1024,256]{1,0:T(8,128)(2,1)S(1)}, f32[2,1024,64]{2,1,0:T(8,128)}, f32[2,512,256]{2,1,0:T(8,128)}, f32[1024,512]{1,0:T(8,128)}, f32[1024,64]{1,0:T(8,128)S(1)}) custom-call(bf16[1024,256]{1,0:T(8,128)(2,1)S(1)} %bitcast.288, bf16[1024,256]{1,0:T(8,128)(2,1)S(1)} %copy-done.3, bf16[2,1024,64]{2,1,0:T(8,128)(2,1)S(1)} %copy-done.1, ...), custom_call_target="tpu_custom_call" | custom-call | tf_op jit(solution)/shard_map/pallas_call | solution.py:430
  720.1 7.4 collective-permute-done.23
  729.9 6.0 all-to-all-start.6
  735.9 6.2 fusion.54
  745.7 5.8 pad_maximum_fusion.1
  775.9 6.6 fusion.3
  784.3 6.4 copy.315
  790.8 6.6 constant_dynamic-slice_fusion.2
  797.4 6.0 all-to-all-start.4
  833.2 7.7 convert_add_fusion.1
  841.1 9.2 convert_add_fusion
  870.0 58.4 %all-to-all-done.4 = bf16[8,128,2048]{2,1,0:T(8,128)(2,1)} async-done(((bf16[8,128,2048]{2,1,0:T(8,128)(2,1)}), bf16[8,128,2048]{2,1,0:T(8,128)(2,1)}, u32[]{:S(2)}, u32[]{:S(2)}) %all-to-all-start.4) | async-done | bytes 4194336 | tf_op jit(solution)/shard_map/all_to_all | solution.py:292
  964.8 11.3 %all-to-all-done.8 = bf16[8,64,384]{2,1,0:T(8,128)(2,1)S(1)} async-done(((bf16[8,64,384]{2,1,0:T(8,128)(2,1)}), bf16[8,64,384]{2,1,0:T(8,128)(2,1)S(1)}, u32[]{:S(2)}, u32[]{:S(2)}) %all-to-all-start.8) | async-done | bytes 393248 | tf_op jit(solution)/shard_map/all_to_all | solution.py:292
  990.3 5.8 all-to-all-done.9
  (496 shorter events, 296.2 us)
Async XLA Ops:
  7.2 151.4 %all-gather.5.cloned.1.call-start = ((), (), s32[]{:S(2)}) async-start(), calls=%async_computation.14 | async-start | bytes 9437184 | tf_op jit(solution)/shard_map/all_gather | solution.py:765
  13.4 58.9 %all-to-all-start = ((bf16[8,64,960]{2,1,0:T(8,128)(2,1)}), bf16[8,64,960]{2,1,0:T(8,128)(2,1)S(1)}, u32[]{:S(2)}, u32[]{:S(2)}) async-start(bf16[8,64,960]{2,1,0:T(8,128)(2,1)} %pad_maximum_fusion.15), calls=%async_computation | async-start | bytes 2097152 | tf_op jit(solution)/shard_map/all_to_all | solution.py:292
  20.7 263.7 %all-gather.7.cloned.1.call-start = ((), (), s32[]{:S(2)}) async-start(), calls=%async_computation.15 | async-start | bytes 8650752 | tf_op jit(solution)/shard_map/all_gather | solution.py:768
  26.2 33.2 %collective-permute-start.2 = (bf16[2,128,2816]{2,1,0:T(8,128)(2,1)S(1)}, bf16[2,128,2816]{2,1,0:T(8,128)(2,1)}, u32[]{:S(2)}, u32[]{:S(2)}) collective-permute-start(bf16[2,128,2816]{2,1,0:T(8,128)(2,1)S(1)} %get-tuple-element.202), channel_id=1, source_target_pairs={{0,2},{1,3},{2,0},{3,1},{4,6},{5,7},{6,4},{7,5},{8,10},{9,11},{10,... | collective-permute-start | bytes 4325384 | tf_op jit(solution)/shard_map/ppermute | solution.py:242
  73.6 19.8 %collective-permute-start.4 = (bf16[8,64,1088]{2,1,0:T(8,128)(2,1)}, bf16[8,64,1088]{2,1,0:T(8,128)(2,1)}, u32[]{:S(2)}, u32[]{:S(2)}) collective-permute-start(bf16[8,64,1088]{2,1,0:T(8,128)(2,1)} %get-tuple-element.250), channel_id=1, source_target_pairs={{0,2},{1,3},{2,0},{3,1},{4,6},{5,7},{6,4},{7,5},{8,10},{9,11},{10,... | collective-permute-start | bytes 3342344 | tf_op jit(solution)/shard_map/ppermute | solution.py:242
  75.2 20.3 %collective-permute-start.3 = (bf16[8,64,1088]{2,1,0:T(8,128)(2,1)}, bf16[8,64,1088]{2,1,0:T(8,128)(2,1)}, u32[]{:S(2)}, u32[]{:S(2)}) collective-permute-start(bf16[8,64,1088]{2,1,0:T(8,128)(2,1)} %get-tuple-element.250), channel_id=1, source_target_pairs={{0,1},{1,0},{2,3},{3,2},{4,5},{5,4},{6,7},{7,6},{8,9},{9,8},{10,11... | collective-permute-start | bytes 3342344 | tf_op jit(solution)/shard_map/ppermute | solution.py:242
  93.5 34.7 %collective-permute-start = (bf16[2,128,2816]{2,1,0:T(8,128)(2,1)}, bf16[2,128,2816]{2,1,0:T(8,128)(2,1)}, u32[]{:S(2)}, u32[]{:S(2)}) collective-permute-start(bf16[2,128,2816]{2,1,0:T(8,128)(2,1)} %get-tuple-element.204), channel_id=1, source_target_pairs={{0,2},{1,3},{2,0},{3,1},{4,6},{5,7},{6,4},{7,5},{8,10},{9,11},{10,... | collective-permute-start | bytes 4325384 | tf_op jit(solution)/shard_map/ppermute | solution.py:242
  95.0 63.6 %collective-permute-start.1 = (bf16[2,128,2816]{2,1,0:T(8,128)(2,1)}, bf16[2,128,2816]{2,1,0:T(8,128)(2,1)S(1)}, u32[]{:S(2)}, u32[]{:S(2)}) collective-permute-start(bf16[2,128,2816]{2,1,0:T(8,128)(2,1)} %get-tuple-element.203), channel_id=1, source_target_pairs={{0,2},{1,3},{2,0},{3,1},{4,6},{5,7},{6,4},{7,5},{8,10},{9,11},{10,... | collective-permute-start | bytes 4325384 | tf_op jit(solution)/shard_map/ppermute | solution.py:242
  166.9 109.5 %collective-permute-start.6 = (bf16[2,128,2816]{2,1,0:T(8,128)(2,1)}, bf16[2,128,2816]{2,1,0:T(8,128)(2,1)}, u32[]{:S(2)}, u32[]{:S(2)}) collective-permute-start(bf16[2,128,2816]{2,1,0:T(8,128)(2,1)} %get-tuple-element.201), channel_id=1, source_target_pairs={{0,2},{1,3},{2,0},{3,1},{4,6},{5,7},{6,4},{7,5},{8,10},{9,11},{10,... | collective-permute-start | bytes 4325384 | tf_op jit(solution)/shard_map/ppermute | solution.py:242
  168.5 225.7 %collective-permute-start.15 = (bf16[2,1408,512]{2,1,0:T(8,128)(2,1)}, bf16[2,1408,512]{2,1,0:T(8,128)(2,1)}, u32[]{:S(2)}, u32[]{:S(2)}) collective-permute-start(bf16[2,1408,512]{2,1,0:T(8,128)(2,1)} %param.23), channel_id=1, source_target_pairs={{0,1},{1,0},{2,3},{3,2},{4,5},{5,4},{6,7},{7,6},{8,9},{9,8},{10,11... | collective-permute-start | bytes 8650760 | tf_op jit(solution)/shard_map/ppermute | solution.py:242
  186.1 53.5 %all-to-all-start.2 = ((bf16[8,64,1152]{2,1,0:T(8,128)(2,1)}), bf16[8,64,1152]{2,1,0:T(8,128)(2,1)}, u32[]{:S(2)}, u32[]{:S(2)}) async-start(bf16[8,64,1152]{2,1,0:T(8,128)(2,1)} %copy.298), calls=%async_computation.2 | async-start | bytes 2359296 | tf_op jit(solution)/shard_map/all_to_all | solution.py:292
  239.6 33.3 %all-to-all-start.1 = ((bf16[8,128,256]{1,2,0:T(8,128)(2,1)}), bf16[8,128,256]{1,2,0:T(8,128)(2,1)S(1)}, u32[]{:S(2)}, u32[]{:S(2)}) async-start(bf16[8,128,256]{1,2,0:T(8,128)(2,1)} %copy.297), calls=%async_computation.1 | async-start | bytes 1048576 | tf_op jit(solution)/shard_map/all_to_all | solution.py:292
  276.3 126.8 %all-gather.9.cloned.1.call-start = ((), (), s32[]{:S(2)}) async-start(), calls=%async_computation.16 | async-start | bytes 4718592 | tf_op jit(solution)/shard_map/all_gather | solution.py:284
  279.0 100.6 %collective-permute-start.16 = (bf16[2,1408,512]{2,1,0:T(8,128)(2,1)}, bf16[2,1408,512]{2,1,0:T(8,128)(2,1)}, u32[]{:S(2)}, u32[]{:S(2)}) collective-permute-start(bf16[2,1408,512]{2,1,0:T(8,128)(2,1)} %param.23), channel_id=1, source_target_pairs={{0,2},{1,3},{2,0},{3,1},{4,6},{5,7},{6,4},{7,5},{8,10},{9,11},{10,... | collective-permute-start | bytes 8650760 | tf_op jit(solution)/shard_map/ppermute | solution.py:242
  279.6 88.6 %collective-permute-start.8 = (bf16[8,64,1152]{2,1,0:T(8,128)(2,1)}, bf16[8,64,1152]{2,1,0:T(8,128)(2,1)}, u32[]{:S(2)}, u32[]{:S(2)}) collective-permute-start(bf16[8,64,1152]{2,1,0:T(8,128)(2,1)} %all-to-all-done.2), channel_id=1, source_target_pairs={{0,2},{1,3},{2,0},{3,1},{4,6},{5,7},{6,4},{7,5},{8,10},{9,11},{10,... | collective-permute-start | bytes 3538952 | tf_op jit(solution)/shard_map/ppermute | solution.py:242
  281.0 98.6 %collective-permute-start.7 = (bf16[8,64,1152]{2,1,0:T(8,128)(2,1)}, bf16[8,64,1152]{2,1,0:T(8,128)(2,1)}, u32[]{:S(2)}, u32[]{:S(2)}) collective-permute-start(bf16[8,64,1152]{2,1,0:T(8,128)(2,1)} %all-to-all-done.2), channel_id=1, source_target_pairs={{0,1},{1,0},{2,3},{3,2},{4,5},{5,4},{6,7},{7,6},{8,9},{9,8},{10,11... | collective-permute-start | bytes 3538952 | tf_op jit(solution)/shard_map/ppermute | solution.py:242
  292.1 281.4 %reduce-scatter.3.cloned.1.call-start = ((), (), s32[]{:S(2)}) async-start(), calls=%async_computation.17 | async-start | bytes 4718592 | tf_op jit(solution)/shard_map/reduce_scatter | solution.py:288
  380.1 14.1 %collective-permute-start.17 = (bf16[2,1408,512]{2,1,0:T(8,128)(2,1)}, bf16[2,1408,512]{2,1,0:T(8,128)(2,1)S(1)}, u32[]{:S(2)}, u32[]{:S(2)}) collective-permute-start(bf16[2,1408,512]{2,1,0:T(8,128)(2,1)} %collective-permute-done.16), channel_id=1, source_target_pairs={{0,1},{1,0},{2,3},{3,2},{4,5},{5,4},{6,7},{7,6},{8,9},{9,8},{10,11... | collective-permute-start | bytes 8650760 | tf_op jit(solution)/shard_map/ppermute | solution.py:242
  493.7 40.8 %collective-permute-start.20 = (bf16[2,512,2816]{2,1,0:T(8,128)(2,1)}, bf16[2,512,2816]{2,1,0:T(8,128)(2,1)}, u32[]{:S(2)}, u32[]{:S(2)}) collective-permute-start(bf16[2,512,2816]{2,1,0:T(8,128)(2,1)} %convolution_convert_fusion.1), channel_id=1, source_target_pairs={{0,1},{1,0},{2,3},{3,2},{4,5},{5,4},{6,7},{7,6},{8,9},{9,8},{10,11... | collective-permute-start | bytes 17301512 | tf_op jit(solution)/shard_map/ppermute | solution.py:242
  498.6 28.6 %collective-permute-start.18 = (bf16[2,1408,512]{2,1,0:T(8,128)(2,1)}, bf16[2,1408,512]{2,1,0:T(8,128)(2,1)}, u32[]{:S(2)}, u32[]{:S(2)}) collective-permute-start(bf16[2,1408,512]{2,1,0:T(8,128)(2,1)} %convolution_convert_fusion.4), channel_id=1, source_target_pairs={{0,1},{1,0},{2,3},{3,2},{4,5},{5,4},{6,7},{7,6},{8,9},{9,8},{10,11... | collective-permute-start | bytes 8650760 | tf_op jit(solution)/shard_map/ppermute | solution.py:242
  532.5 34.5 %collective-permute-start.19 = (bf16[1408,512]{1,0:T(8,128)(2,1)S(1)}, bf16[1408,512]{1,0:T(8,128)(2,1)}, u32[]{:S(2)}, u32[]{:S(2)}) collective-permute-start(bf16[1408,512]{1,0:T(8,128)(2,1)S(1)} %get-tuple-element.235), channel_id=1, source_target_pairs={{0,2},{1,3},{2,0},{3,1},{4,6},{5,7},{6,4},{7,5},{8,10},{9,11},{10,... | collective-permute-start | bytes 4325384 | tf_op jit(solution)/shard_map/ppermute | solution.py:242
  533.0 66.4 %collective-permute-start.21 = (bf16[1408,512]{1,0:T(8,128)(2,1)}, bf16[1408,512]{1,0:T(8,128)(2,1)}, u32[]{:S(2)}, u32[]{:S(2)}) collective-permute-start(bf16[1408,512]{1,0:T(8,128)(2,1)} %get-tuple-element.234), channel_id=1, source_target_pairs={{0,2},{1,3},{2,0},{3,1},{4,6},{5,7},{6,4},{7,5},{8,10},{9,11},{10,... | collective-permute-start | bytes 4325384 | tf_op jit(solution)/shard_map/ppermute | solution.py:242
  543.4 115.7 %collective-permute-start.22 = (bf16[512,2816]{1,0:T(8,128)(2,1)}, bf16[512,2816]{1,0:T(8,128)(2,1)}, u32[]{:S(2)}, u32[]{:S(2)}) collective-permute-start(bf16[512,2816]{1,0:T(8,128)(2,1)} %get-tuple-element.200), channel_id=1, source_target_pairs={{0,2},{1,3},{2,0},{3,1},{4,6},{5,7},{6,4},{7,5},{8,10},{9,11},{10,... | collective-permute-start | bytes 8650760 | tf_op jit(solution)/shard_map/ppermute | solution.py:242
  583.7 75.3 %all-to-all-start.5 = ((bf16[8,128,256]{2,1,0:T(8,128)(2,1)}), bf16[8,128,256]{2,1,0:T(8,128)(2,1)S(1)}, u32[]{:S(2)}, u32[]{:S(2)}) async-start(bf16[8,128,256]{2,1,0:T(8,128)(2,1)} %bitcast.274), calls=%async_computation.6 | async-start | bytes 1048576 | tf_op jit(solution)/shard_map/all_to_all | solution.py:292
  588.1 196.2 %all-gather.11.cloned.1.call-start = ((), (), s32[]{:S(2)}) async-start(), calls=%async_computation.18 | async-start | bytes 4718592 | tf_op jit(solution)/shard_map/all_gather | solution.py:284
  661.7 65.8 %collective-permute-start.23 = (bf16[512,2816]{1,0:T(8,128)(2,1)}, bf16[512,2816]{1,0:T(8,128)(2,1)}, u32[]{:S(2)}, u32[]{:S(2)}) collective-permute-start(bf16[512,2816]{1,0:T(8,128)(2,1)} %get-tuple-element.199), channel_id=1, source_target_pairs={{0,2},{1,3},{2,0},{3,1},{4,6},{5,7},{6,4},{7,5},{8,10},{9,11},{10,... | collective-permute-start | bytes 8650760 | tf_op jit(solution)/shard_map/ppermute | solution.py:242
  674.6 13.1 %collective-permute-start.40 = (bf16[8,64,1152]{2,1,0:T(8,128)(2,1)S(1)}, bf16[8,64,1152]{2,1,0:T(8,128)(2,1)S(1)}, u32[]{:S(2)}, u32[]{:S(2)}) collective-permute-start(bf16[8,64,1152]{2,1,0:T(8,128)(2,1)S(1)} %get-tuple-element.206), channel_id=1, source_target_pairs={{0,1},{1,0},{2,3},{3,2},{4,5},{5,4},{6,7},{7,6},{8,9},{9,8},{10,11... | collective-permute-start | bytes 3538952 | tf_op jit(solution)/shard_map/ppermute | solution.py:242
  680.0 152.6 %collective-permute-start.43 = (bf16[2,1408,512]{2,1,0:T(8,128)(2,1)}, bf16[2,1408,512]{2,1,0:T(8,128)(2,1)}, u32[]{:S(2)}, u32[]{:S(2)}) collective-permute-start(bf16[2,1408,512]{2,1,0:T(8,128)(2,1)} %convolution_convert_fusion.3), channel_id=1, source_target_pairs={{0,1},{1,0},{2,3},{3,2},{4,5},{5,4},{6,7},{7,6},{8,9},{9,8},{10,11... | collective-permute-start | bytes 8650760 | tf_op jit(solution)/shard_map/ppermute | solution.py:242
  687.2 153.8 %collective-permute-start.42 = (bf16[2,512,2816]{2,1,0:T(8,128)(2,1)}, bf16[2,512,2816]{2,1,0:T(8,128)(2,1)}, u32[]{:S(2)}, u32[]{:S(2)}) collective-permute-start(bf16[2,512,2816]{2,1,0:T(8,128)(2,1)} %convolution_convert_fusion), channel_id=1, source_target_pairs={{0,1},{1,0},{2,3},{3,2},{4,5},{5,4},{6,7},{7,6},{8,9},{9,8},{10,11... | collective-permute-start | bytes 17301512 | tf_op jit(solution)/shard_map/ppermute | solution.py:242
  687.2 66.0 %collective-permute-start.39 = (bf16[8,64,1152]{2,1,0:T(8,128)(2,1)}, bf16[8,64,1152]{2,1,0:T(8,128)(2,1)}, u32[]{:S(2)}, u32[]{:S(2)}) collective-permute-start(bf16[8,64,1152]{2,1,0:T(8,128)(2,1)} %get-tuple-element.205), channel_id=1, source_target_pairs={{0,1},{1,0},{2,3},{3,2},{4,5},{5,4},{6,7},{7,6},{8,9},{9,8},{10,11... | collective-permute-start | bytes 3538952 | tf_op jit(solution)/shard_map/ppermute | solution.py:242
  690.3 61.2 %collective-permute-start.41 = (bf16[8,64,1152]{2,1,0:T(8,128)(2,1)}, bf16[8,64,1152]{2,1,0:T(8,128)(2,1)}, u32[]{:S(2)}, u32[]{:S(2)}) collective-permute-start(bf16[8,64,1152]{2,1,0:T(8,128)(2,1)} %fusion.21), channel_id=1, source_target_pairs={{0,2},{1,3},{2,0},{3,1},{4,6},{5,7},{6,4},{7,5},{8,10},{9,11},{10,... | collective-permute-start | bytes 3538952 | tf_op jit(solution)/shard_map/ppermute | solution.py:242
  729.9 32.1 %all-to-all-start.6 = ((bf16[8,128,576]{1,2,0:T(8,128)(2,1)}), bf16[8,128,576]{1,2,0:T(8,128)(2,1)}, u32[]{:S(2)}, u32[]{:S(2)}) async-start(bf16[8,128,576]{1,2,0:T(8,128)(2,1)} %copy.305), calls=%async_computation.7 | async-start | bytes 2359296 | tf_op jit(solution)/shard_map/all_to_all | solution.py:292
  752.7 21.2 %collective-permute-start.34 = (bf16[512,128]{0,1:T(8,128)(2,1)}, bf16[512,128]{0,1:T(8,128)(2,1)S(1)}, u32[]{:S(2)}, u32[]{:S(2)}) collective-permute-start(bf16[512,128]{0,1:T(8,128)(2,1)} %get-tuple-element.268), channel_id=1, source_target_pairs={{0,1},{1,0},{2,3},{3,2},{4,5},{5,4},{6,7},{7,6},{8,9},{9,8},{10,11... | collective-permute-start | bytes 393224 | tf_op jit(solution)/shard_map/ppermute | solution.py:242
  752.7 29.8 %collective-permute-start.33 = (bf16[512,128]{0,1:T(8,128)(2,1)}, bf16[512,128]{0,1:T(8,128)(2,1)}, u32[]{:S(2)}, u32[]{:S(2)}) collective-permute-start(bf16[512,128]{0,1:T(8,128)(2,1)} %get-tuple-element.267), channel_id=1, source_target_pairs={{0,1},{1,0},{2,3},{3,2},{4,5},{5,4},{6,7},{7,6},{8,9},{9,8},{10,11... | collective-permute-start | bytes 393224 | tf_op jit(solution)/shard_map/ppermute | solution.py:242
  762.0 35.4 %all-to-all-start.11 = ((bf16[8,64,1152]{2,1,0:T(8,128)(2,1)}), bf16[8,64,1152]{2,1,0:T(8,128)(2,1)}, u32[]{:S(2)}, u32[]{:S(2)}) async-start(bf16[8,64,1152]{2,1,0:T(8,128)(2,1)} %fusion.23), calls=%async_computation.13 | async-start | bytes 2359296 | tf_op jit(solution)/shard_map/all_to_all | solution.py:292
  797.4 131.0 %all-to-all-start.4 = ((bf16[8,128,2048]{2,1,0:T(8,128)(2,1)}), bf16[8,128,2048]{2,1,0:T(8,128)(2,1)}, u32[]{:S(2)}, u32[]{:S(2)}) async-start(bf16[8,128,2048]{2,1,0:T(8,128)(2,1)} %bitcast.326), calls=%async_computation.5 | async-start | bytes 8388608 | tf_op jit(solution)/shard_map/all_to_all | solution.py:292
  803.4 192.7 %reduce-scatter.5.cloned.1.call-start = ((), (), s32[]{:S(2)}) async-start(), calls=%async_computation.19 | async-start | bytes 4718592 | tf_op jit(solution)/shard_map/reduce_scatter | solution.py:288
  809.0 123.1 %collective-permute-start.36 = (bf16[512,256]{1,0:T(8,128)(2,1)}, bf16[512,256]{1,0:T(8,128)(2,1)}, u32[]{:S(2)}, u32[]{:S(2)}) collective-permute-start(bf16[512,256]{1,0:T(8,128)(2,1)} %convolution_convert_fusion.12), channel_id=1, source_target_pairs={{0,1},{1,0},{2,3},{3,2},{4,5},{5,4},{6,7},{7,6},{8,9},{9,8},{10,11... | collective-permute-start | bytes 786440 | tf_op jit(solution)/shard_map/ppermute | solution.py:242
  810.1 53.2 %collective-permute-start.37 = (bf16[512,256]{1,0:T(8,128)(2,1)}, bf16[512,256]{1,0:T(8,128)(2,1)}, u32[]{:S(2)}, u32[]{:S(2)}) collective-permute-start(bf16[512,256]{1,0:T(8,128)(2,1)} %convolution_convert_fusion.11), channel_id=1, source_target_pairs={{0,1},{1,0},{2,3},{3,2},{4,5},{5,4},{6,7},{7,6},{8,9},{9,8},{10,11... | collective-permute-start | bytes 786440 | tf_op jit(solution)/shard_map/ppermute | solution.py:242
  819.4 142.5 %collective-permute-start.30 = (bf16[512,576]{0,1:T(8,128)(2,1)}, bf16[512,576]{0,1:T(8,128)(2,1)}, u32[]{:S(2)}, u32[]{:S(2)}) collective-permute-start(bf16[512,576]{0,1:T(8,128)(2,1)} %convolution_convert_fusion.8), channel_id=1, source_target_pairs={{0,1},{1,0},{2,3},{3,2},{4,5},{5,4},{6,7},{7,6},{8,9},{9,8},{10,11... | collective-permute-start | bytes 1769480 | tf_op jit(solution)/shard_map/ppermute | solution.py:242
  832.6 19.1 %collective-permute-start.25 = (f32[8,144]{1,0:T(8,128)S(1)}, f32[8,144]{1,0:T(8,128)S(1)}, u32[]{:S(2)}, u32[]{:S(2)}) collective-permute-start(f32[8,144]{1,0:T(8,128)S(1)} %bitcast.360), channel_id=1, source_target_pairs={{0,1},{1,0},{2,3},{3,2},{4,5},{5,4},{6,7},{7,6},{8,9},{9,8},{10,11... | collective-permute-start | bytes 13832 | tf_op jit(solution)/shard_map/ppermute | solution.py:242
  862.1 80.0 %collective-permute-start.31 = (bf16[512,576]{0,1:T(8,128)(2,1)}, bf16[512,576]{0,1:T(8,128)(2,1)}, u32[]{:S(2)}, u32[]{:S(2)}) collective-permute-start(bf16[512,576]{0,1:T(8,128)(2,1)} %convolution_convert_fusion.7), channel_id=1, source_target_pairs={{0,1},{1,0},{2,3},{3,2},{4,5},{5,4},{6,7},{7,6},{8,9},{9,8},{10,11... | collective-permute-start | bytes 1769480 | tf_op jit(solution)/shard_map/ppermute | solution.py:242
  863.3 82.2 %collective-permute-start.27 = (bf16[512,384]{1,0:T(8,128)(2,1)}, bf16[512,384]{1,0:T(8,128)(2,1)}, u32[]{:S(2)}, u32[]{:S(2)}) collective-permute-start(bf16[512,384]{1,0:T(8,128)(2,1)} %convolution_convert_fusion.10), channel_id=1, source_target_pairs={{0,1},{1,0},{2,3},{3,2},{4,5},{5,4},{6,7},{7,6},{8,9},{9,8},{10,11... | collective-permute-start | bytes 1179656 | tf_op jit(solution)/shard_map/ppermute | solution.py:242
  865.9 67.2 %collective-permute-start.38 = (bf16[512,256]{1,0:T(8,128)(2,1)}, bf16[512,256]{1,0:T(8,128)(2,1)S(1)}, u32[]{:S(2)}, u32[]{:S(2)}) collective-permute-start(bf16[512,256]{1,0:T(8,128)(2,1)} %add_convert_fusion.7), channel_id=1, source_target_pairs={{0,2},{1,3},{2,0},{3,1},{4,6},{5,7},{6,4},{7,5},{8,10},{9,11},{10,... | collective-permute-start | bytes 786440 | tf_op jit(solution)/shard_map/ppermute | solution.py:242
  932.0 13.4 %collective-permute-start.29 = (bf16[512,384]{1,0:T(8,128)(2,1)}, bf16[512,384]{1,0:T(8,128)(2,1)S(1)}, u32[]{:S(2)}, u32[]{:S(2)}) collective-permute-start(bf16[512,384]{1,0:T(8,128)(2,1)} %add_convert_fusion.5), channel_id=1, source_target_pairs={{0,2},{1,3},{2,0},{3,1},{4,6},{5,7},{6,4},{7,5},{8,10},{9,11},{10,... | collective-permute-start | bytes 1179656 | tf_op jit(solution)/shard_map/ppermute | solution.py:242
  944.5 17.4 %collective-permute-start.32 = (bf16[512,576]{0,1:T(8,128)(2,1)}, bf16[512,576]{0,1:T(8,128)(2,1)}, u32[]{:S(2)}, u32[]{:S(2)}) collective-permute-start(bf16[512,576]{0,1:T(8,128)(2,1)} %add_convert_fusion.3), channel_id=1, source_target_pairs={{0,2},{1,3},{2,0},{3,1},{4,6},{5,7},{6,4},{7,5},{8,10},{9,11},{10,... | collective-permute-start | bytes 1769480 | tf_op jit(solution)/shard_map/ppermute | solution.py:242
  950.3 25.8 %all-to-all-start.8 = ((bf16[8,64,384]{2,1,0:T(8,128)(2,1)}), bf16[8,64,384]{2,1,0:T(8,128)(2,1)S(1)}, u32[]{:S(2)}, u32[]{:S(2)}) async-start(bf16[8,64,384]{2,1,0:T(8,128)(2,1)} %bitcast.338), calls=%async_computation.10 | async-start | bytes 786432 | tf_op jit(solution)/shard_map/all_to_all | solution.py:292
  976.1 20.0 %all-to-all-start.9 = ((bf16[8,64,576]{2,1,0:T(8,128)(2,1)}), bf16[8,64,576]{2,1,0:T(8,128)(2,1)}, u32[]{:S(2)}, u32[]{:S(2)}) async-start(bf16[8,64,576]{2,1,0:T(8,128)(2,1)} %bitcast.77), calls=%async_computation.11 | async-start | bytes 1310720 | tf_op jit(solution)/shard_map/all_to_all | solution.py:292
  (107 other events, 1176.0 us)
Sparse Core Ops, SparseCore 0:
  10.8 147.8 all-gather.4
  166.9 110.4 all-gather.6
  292.2 71.8 all-gather.8
  485.3 88.1 reduce-scatter.2
  659.2 73.4 all-gather.10
  819.6 160.0 reduce-scatter.4

commit v4 on v3

--- a/solution.py
+++ b/solution.py
@@ -260,15 +260,15 @@
 
 
 def fsdp_reduce(blocks, rank, *gate):
-    rel = [lax.dynamic_index_in_dim(blocks, rank ^ k, 0, False) for k in range(4)]
-    return fsdp_reduce_terms(lambda k: rel[k].astype(jnp.float32), blocks.dtype, *gate)
-
-
-def fsdp_reduce_terms(term, kind, *gate):
+    rel = after([lax.dynamic_index_in_dim(blocks, rank ^ k, 0, False) for k in range(4)], *gate)
+    near = [fsdp_swap(rel[k], 1).astype(jnp.float32) for k in (1, 3)]
+    far = fsdp_swap((rel[2].astype(jnp.float32) + near[1]).astype(blocks.dtype), 2)
+    return rel[0].astype(jnp.float32) + near[0] + far.astype(jnp.float32)
+
+
+def fsdp_reduce_terms(term, kind):
     near = [fsdp_swap(term(k).astype(kind), 1).astype(jnp.float32) for k in (1, 3)]
     far = fsdp_swap((term(2) + near[1]).astype(kind), 2)
-    if gate:
-        far = after(far, *gate)
     return term(0) + near[0] + far.astype(jnp.float32)
 
 
@@ -520,6 +520,83 @@
     )(x_exp, y_exp, slot_gate, gu_rel, dn_rel)
 
 
+def expert_grad_body(*refs, each):
+    left_ref, right_ref, *more, out_ref = refs
+    total = dot_f32(left_ref[0], right_ref[0], ((0,), (0,)))
+    for ref in more[: len(more) - each]:
+        total = total + ref[0].astype(jnp.float32)
+    for e, ref in enumerate(more[len(more) - each :]):
+        here = pl.program_id(0) == e
+        total = total + jnp.where(here, ref[0].astype(jnp.float32), 0.0)
+    out_ref[0] = total.astype(out_ref.dtype)
+
+
+def expert_grad_call(left, right, left_at, right_at, kind, *more, each=(), only=None):
+    count, slots = left.shape[:2]
+    (rows, row_block), (cols, col_block) = left_at, right_at
+    first = 0
+    if only is not None:
+        count, first = 1, only
+    parts = 2 if cols % 256 == 0 and cols > rows else 1
+    step = cols // parts
+    block = pl.BlockSpec((1, rows, step), lambda e, i: (e, 0, i))
+    one = pl.BlockSpec((1, rows, step), lambda e, i: (0, 0, i))
+    return pl.pallas_call(
+        functools.partial(expert_grad_body, each=len(each)),
+        grid=(count, parts),
+        in_specs=[
+            pl.BlockSpec((1, slots, rows), lambda e, i: (e + first, 0, row_block)),
+            pl.BlockSpec((1, slots, step), lambda e, i: (e + first, 0, col_block * parts + i)),
+        ]
+        + [block] * len(more)
+        + [one] * len(each),
+        out_specs=block,
+        out_shape=jax.ShapeDtypeStruct((count, rows, cols), kind),
+        compiler_params=pltpu.CompilerParams(vmem_limit_bytes=VMEM_BYTES),
+    )(left, right, *more, *each)
+
+
+def combine_body(
+    pick_ref, both_ref, act_ref, in_ref, out_ref, gate_up_ref, down_ref, total_ref, *, blocks
+):
+    at = pl.program_id(0)
+
+    @pl.when(at < blocks)
+    def _():
+        total = dot_f32(both_ref[...], gate_up_ref[...], ((1,), (1,)))
+        total_ref[...] = (total + dot_f32(pick_ref[...], in_ref[...])).astype(jnp.bfloat16)
+
+    @pl.when(at >= blocks)
+    def _():
+        total = dot_f32(act_ref[...], down_ref[...], ((1,), (1,)))
+        total_ref[...] = (total + dot_f32(pick_ref[...], out_ref[...])).astype(jnp.bfloat16)
+
+
+def combine_call(pick_rows, s_both_grad, s_act, in_slots, out_slots, shared_gu, shared_dn):
+    length, entries = pick_rows.shape
+    width = 512
+    blocks = D // width
+    early = lambda j: jnp.minimum(j, blocks - 1)
+    late = lambda j: jnp.maximum(j - blocks, 0)
+    whole = lambda j: (0, 0)
+    return pl.pallas_call(
+        functools.partial(combine_body, blocks=blocks),
+        grid=(2 * blocks,),
+        in_specs=[
+            pl.BlockSpec((length, entries), whole),
+            pl.BlockSpec(s_both_grad.shape, whole),
+            pl.BlockSpec(s_act.shape, whole),
+            pl.BlockSpec((entries, width), lambda j: (0, early(j))),
+            pl.BlockSpec((entries, width), lambda j: (0, late(j))),
+            pl.BlockSpec((width, shared_gu.shape[1]), lambda j: (early(j), 0)),
+            pl.BlockSpec((width, shared_dn.shape[1]), lambda j: (late(j), 0)),
+        ],
+        out_specs=pl.BlockSpec((length, width), lambda j: (0, j)),
+        out_shape=jax.ShapeDtypeStruct((length, 2 * D), jnp.bfloat16),
+        compiler_params=pltpu.CompilerParams(vmem_limit_bytes=VMEM_BYTES),
+    )(pick_rows, s_both_grad, s_act, in_slots, out_slots, shared_gu, shared_dn)
+
+
 def on_device(
     hidden_in,
     out_grad,
@@ -566,7 +643,7 @@
     attn_first, attn_mid, attn_backward = attn(
         hidden_in[0], tokens, norm_gains, w_query, w_latent, w_expand, w_output, where_all, score_scale
     )
-    first_done, grads_all = attn_first(gu_far, swap_chunks(out_grad[0], rank, 1))
+    first_done = attn_first(gu_far)
 
     gate_send = pad_last(columns_by_dest(shared_gate_up[:, :SFF], n_ctx), sff_pad)
     up_send = pad_last(columns_by_dest(shared_gate_up[:, SFF:], n_ctx), sff_pad)
@@ -575,10 +652,11 @@
     shared_got = ctx_exchange(after(shared_send, first_done))
     shared_far = fsdp_swap(shared_got, 2)
 
-    resid_mid = attn_mid(gu_far)
+    resid_mid = attn_mid((gu_far[2], shared_got))
     normed_mid, inv_mid = norm_forward(resid_mid, gain_mid)
     mid_send = swap_chunks(normed_mid.astype(jnp.bfloat16), rank, 1)
     mid_all = ctx_gather(mid_send)
+    grads_all = ctx_gather(after(swap_chunks(out_grad[0], rank, 1), mid_all))
     shared_full = whole_rows(
         [shared_got, fsdp_swap(shared_got, 1), shared_far, fsdp_swap(after(shared_far, resid_mid), 1)], rank
     )
@@ -622,59 +700,59 @@
     pick = taken.astype(jnp.bfloat16).reshape(exp_local * slots, length)
     slot_gate = jnp.sum(jnp.where(taken, gate_of[:, None, :], 0.0), -1).reshape(-1, 1)
 
-    quarter = D // 4
-    y_exp = (dot_f32(pick, grads_all) * slot_gate).astype(jnp.bfloat16)
-    y_exp = y_exp.reshape(exp_local, slots, D)
-    s_act_grad = dot_f32(grads_all, shared_dn)
-    x_exp = dot_f32(pick, mid_all).astype(jnp.bfloat16).reshape(exp_local, slots, D)
-    e_act, both_grad, out_slots, in_slots = experts_call(
-        x_exp, y_exp, slot_gate.reshape(exp_local, slots, 1), gu_rel, dn_rel
-    )
+    pick_rows = pick.T
     s_both = dot_f32(mid_all, shared_gu)
     s_gate = s_both[:, :sff_pad]
     s_up = s_both[:, sff_pad:]
     s_sig = jax.nn.sigmoid(s_gate)
     s_silu = s_gate * s_sig
     s_act = (s_silu * s_up).astype(jnp.bfloat16)
+    x_exp = dot_f32(pick, mid_all).astype(jnp.bfloat16).reshape(exp_local, slots, D)
+    y_exp = (dot_f32(pick, grads_all) * slot_gate).astype(jnp.bfloat16)
+    y_exp = y_exp.reshape(exp_local, slots, D)
+    s_act_grad = dot_f32(grads_all, shared_dn)
     s_both_grad = jnp.concatenate(
         [s_act_grad * s_up * s_sig * (1.0 + s_gate * (1.0 - s_sig)), s_act_grad * s_silu], -1
     ).astype(jnp.bfloat16)
-    mid_part = dot_f32(s_both_grad, shared_gu, ((1,), (1,))) + dot_f32(
-        pick, in_slots.reshape(-1, D), ((0,), (0,))
-    )
-    mid_part = mid_part.astype(jnp.bfloat16)
-
-    x_late, y_late, act_late = after((x_exp, y_exp, e_act), mid_part)
-
-    def dn_term(k):
-        return experts_dot("esf,esd->efd", act_late, y_late[..., k * quarter : (k + 1) * quarter])
-
-    dn_send = [dn_term(k).astype(jnp.bfloat16) for k in (1, 3)]
-    dn_got = [fsdp_swap(v, 1).astype(jnp.float32) for v in dn_send]
-    dn_other = (dn_term(2) + dn_got[1]).astype(jnp.bfloat16)
-    dn_back = [fsdp_swap(dn_other[e], 2) for e in range(exp_local)]
-
-    def gu_term(k):
-        return experts_dot("esd,esf->edf", x_late[..., k * quarter : (k + 1) * quarter], both_grad)
-
-    gu_send = [gu_term(k).astype(jnp.bfloat16) for k in (1, 3)]
-    gu_got = [fsdp_swap(v, 1).astype(jnp.float32) for v in gu_send]
-    gu_other = (gu_term(2) + gu_got[1]).astype(jnp.bfloat16)
-    gu_back = [fsdp_swap(gu_other[e], 2) for e in range(exp_local)]
+    e_act, both_grad, out_slots, in_slots = experts_call(
+        x_exp, y_exp, slot_gate.reshape(exp_local, slots, 1), gu_rel, dn_rel
+    )
+    sums_part = combine_call(
+        pick_rows, s_both_grad, s_act, in_slots.reshape(-1, D), out_slots.reshape(-1, D),
+        shared_gu, shared_dn,
+    )
+
+    x_late, y_late, act_late = after((x_exp, y_exp, e_act), sums_part)
+    quarter = D // 4
+
+    def dn_term(k, kind, *more):
+        return expert_grad_call(act_late, y_late, (FF, 0), (quarter, k), kind, *more)
+
+    def gu_term(k, kind, *more, **which):
+        return expert_grad_call(x_late, both_grad, (quarter, k), (2 * FF, 0), kind, *more, **which)
+
+    dn_send = [dn_term(k, jnp.bfloat16) for k in (1, 3)]
+    dn_got = [fsdp_swap(v, 1) for v in dn_send]
+    x_late = after(x_late, dn_send)
+    gu_send = [gu_term(k, jnp.bfloat16) for k in (1, 3)]
+    gu_got = [fsdp_swap(v, 1) for v in gu_send]
+    dn_other = dn_term(2, jnp.bfloat16, dn_got[1])
+    dn_back = fsdp_swap(dn_other, 2)
+    gu_other = [gu_term(2, jnp.bfloat16, gu_got[1][e : e + 1], only=e) for e in range(exp_local)]
+    gu_back = [fsdp_swap(v, 2) for v in gu_other]
+    mid_late, grads_late = after((mid_all, grads_all), gu_send)
     shared_grad = jnp.concatenate(
         [
-            dot_f32(after(mid_all, mid_part), s_both_grad, ((0,), (0,))),
-            dot_f32(after(grads_all, mid_part), s_act, ((0,), (0,))),
+            dot_f32(mid_late, s_both_grad, ((0,), (0,))),
+            dot_f32(grads_late, s_act, ((0,), (0,))),
         ],
         -1,
     )
     shared_grad = swap_chunks(shared_grad, rank, 0).astype(jnp.bfloat16)
-    out_late = after(out_slots, mid_part).reshape(-1, D)
-    out_part = dot_f32(s_act, shared_dn, ((1,), (1,))) + dot_f32(pick, out_late, ((0,), (0,)))
-    out_part = out_part.astype(jnp.bfloat16)
-    mid_grad = after(ctx_scatter(mid_part), dn_back[0], gu_other, shared_grad, out_part)
-    ffn_out = ctx_exchange(after(out_part, mid_grad).reshape(n_ctx, tok_dev, D))
-    mid_grad = swap_chunks(mid_grad.astype(jnp.float32), rank, 1)
+    sums = after(ctx_scatter(sums_part), dn_back, gu_back[0], gu_other, shared_grad).astype(jnp.float32)
+    mid_grad = swap_chunks(sums[:, :D], rank, 1)
+    ffn_out = swap_chunks(sums[:, D:], rank, 1)
+
     resid_norm_grad, gain_mid_grad = norm_backward(resid_mid, inv_mid, gain_mid, mid_grad)
     resid_grad = out_grad[0].astype(jnp.float32) + resid_norm_grad
 
@@ -684,11 +762,11 @@
         return jnp.sum(ctx_exchange(gains), 0)
 
     token_grad, stage, gains_grad, query_w, latent_w, expand_w, output_w = attn_backward(
-        resid_grad.astype(jnp.bfloat16), (dn_back[1:] + gu_back[:1], gu_back[1:], ffn_out), reduce_gains
-    )
-    heads_there, keys_there = stage
-    shared_term = shard_rows(shared_grad, n_ctx, rank, heads_there).astype(jnp.bfloat16)
-    shared_grad = after(ctx_exchange(shared_term), keys_there).astype(jnp.float32)
+        resid_grad.astype(jnp.bfloat16), gu_back[1:], reduce_gains
+    )
+    keys_there, sums_there = stage
+    shared_term = shard_rows(shared_grad, n_ctx, rank, keys_there).astype(jnp.bfloat16)
+    shared_grad = ctx_exchange(shared_term).astype(jnp.float32)
     gate_grad = shared_grad[:, :, :sff_dev].transpose(1, 0, 2).reshape(-1, SFF)
     up_grad = shared_grad[:, :, sff_pad : sff_pad + sff_dev].transpose(1, 0, 2).reshape(-1, SFF)
     shared_gu_grad = jnp.concatenate([gate_grad, up_grad], -1)
@@ -696,10 +774,9 @@
     shared_dn_grad = down_grad.transpose(0, 2, 1).reshape(SFF, -1)
 
     hidden_in_grad = (resid_grad + token_grad).astype(jnp.bfloat16)
-    ffn_out = jnp.sum(after(ffn_out, keys_there, gains_grad).astype(jnp.float32), 0)
-    hidden_out = (resid_mid + swap_chunks(ffn_out, rank, 1)).astype(jnp.bfloat16)
-    dn_grad = dn_term(0) + dn_got[0] + after(jnp.stack(dn_back), keys_there).astype(jnp.float32)
-    gu_grad = gu_term(0) + gu_got[0] + after(jnp.stack(gu_back), keys_there).astype(jnp.float32)
+    hidden_out = (resid_mid + ffn_out).astype(jnp.bfloat16)
+    dn_grad = dn_term(0, jnp.float32, dn_got[0], after(dn_back, sums_there))
+    gu_grad = gu_term(0, jnp.float32, gu_got[0], each=after(gu_back, sums_there))
     return (
         hidden_out[None],
         hidden_in_grad[None],
@@ -736,7 +813,7 @@
     q_wide = n_wide + r_wide
     saved = {}
 
-    def first(early, extra):
+    def first(early):
         by_head = w_query.reshape(rows, n_ctx, heads, DN + DR)
         query_send = jnp.concatenate(
             [
@@ -747,7 +824,7 @@
         ).transpose(1, 0, 2)
         latent_send = jnp.broadcast_to(w_latent[None], (n_ctx,) + w_latent.shape)
         got = ctx_exchange(jnp.concatenate([query_send, latent_send], -1))
-        got = after(got, early[0])
+        got = after(got, early[:2])
         pieces = fsdp_pieces(jnp.concatenate([got, w_expand.reshape(n_ctx, rows, -1)], -1))
         full = whole_rows(pieces, rank)
         query_full = full[:, :q_wide]
@@ -762,9 +839,7 @@
         key_up = expand_heads[:, :, :DN].transpose(1, 0, 2)
         value_up = expand_heads[:, :, DN:].transpose(1, 0, 2)
 
-        both_all = lax.all_gather(jnp.stack([hidden_bf, extra]), "ctx", axis=1, tiled=True)
-        both_all = after(both_all, early[1:3], full)
-        hidden_all = both_all[0]
+        hidden_all = after(ctx_gather(hidden_bf), full)
         output_full = lax.all_gather(
             after(w_output, hidden_all), ("ctx", "fsdp"), axis=1, tiled=True
         )
@@ -791,7 +866,7 @@
             nope, rot, latent, key_rot, key_up, value_up, where_all, score_scale
         )
         saved.update(locals())
-        return hidden_all, both_all[1]
+        return hidden_all
 
     def middle(early):
         heads_out = saved["heads_out"].reshape(n_ctx, tok_dev, heads * DV)
@@ -804,23 +879,19 @@
         normed_bf = saved["normed_bf"]
         heads_grad = dot_f32(resid_bf, saved["output_full"], ((1,), (1,))).astype(jnp.bfloat16)
         heads_grad = ctx_exchange(columns_by_dest(heads_grad, n_ctx)).reshape(length, heads * DV)
-        heads_grad = after(heads_grad, stages[0])
-        resid_all = ctx_gather(after(resid_bf, heads_grad))
+        resid_all = ctx_gather(resid_bf)
         nope_grad, rot_grad, expand_g, lat_total, rot_total = attention_backward_call(
             heads_grad, saved["nope"], saved["rot"], saved["mixed"], saved["log_total"],
             saved["latent"], saved["key_rot"], saved["key_up"], saved["value_up"], where_all,
             score_scale,
         )
         key_terms = jnp.concatenate([lat_total, rot_total], -1).astype(jnp.bfloat16)
-        key_terms = after(key_terms, stages[1])
-        key_got = ctx_exchange(
-            key_terms.reshape(n_ctx, tok_dev, KVL + DR)
-        )
+        key_sent = ctx_exchange(key_terms.reshape(n_ctx, tok_dev, KVL + DR))
         rot_grads = [
             rope_back(rot_grad[j], cos_table, sin_table).astype(jnp.bfloat16) for j in range(heads)
         ]
         query_grad = jnp.concatenate([nope_grad, *rot_grads], -1)
-        key_got = after(key_got, resid_all)
+        key_got = after(key_sent, resid_all, stages)
         in_part = dot_f32(query_grad, query_full, ((1,), (1,))).astype(jnp.bfloat16)
         in_grad = ctx_scatter(after(in_part, resid_all))
         gain_in_grad = jnp.sum(
@@ -849,7 +920,7 @@
         latent_w = fsdp_reduce_terms(
             lambda k: dot_f32(own_cols[k], compressed_grad, ((0,), (0,))), jnp.bfloat16
         )
-        latent_w = after(latent_w.astype(jnp.bfloat16), stages[2])
+        latent_w = latent_w.astype(jnp.bfloat16)
         latent_w = ctx_exchange(latent_w.reshape(n_ctx, rows, KVL + DR))
         latent_w = jnp.sum(after(latent_w, in_grad).astype(jnp.float32), 0)
         output_w = ctx_exchange(output_w.astype(jnp.bfloat16).reshape(n_ctx, rows, heads * DV))
@@ -866,7 +937,7 @@
         query_w = jnp.concatenate([nope_w, rot_w], -1).transpose(1, 0, 2, 3).reshape(rows, -1)
         in_grad = after(in_grad, gains_grad).astype(jnp.float32) + in_own
         token_grad = norm_backward(tokens, inv_in, gain_in, in_grad)[0]
-        return token_grad, (heads_grad, key_got), gains_grad, query_w, latent_w, expand_w, output_w
+        return token_grad, (key_sent, in_part), gains_grad, query_w, latent_w, expand_w, output_w
 
     return first, middle, backward
 
@@ -989,9 +1060,9 @@
             for g, at in ((query_g, 0), (latent_g, 0), (expand_g, 1), (output_g, 1))
         ]
         gains_grad = reduce_gains(gain_in_grad, gain_lat_grad)
-        return (token_grad, (heads_grad, latent_grad), gains_grad, *scattered)
-
-    return (lambda early, extra: (latent_full, ctx_gather(extra))), (lambda early: resid_mid), backward
+        return (token_grad, (resid_bf, latent_grad), gains_grad, *scattered)
+
+    return (lambda early: latent_full), (lambda early: resid_mid), backward
 
 
 def solution(mesh):

time: 1020 us -> 1020 us (level)
  matrix products: 162 us -> 76.6 us
  Pallas kernels: 87.8 us -> 163 us
  waiting for transfers between devices: 413 us -> 465 us
  other arithmetic: 124 us -> 86 us
  local copies, waits for them, and re-layouts: 118 us -> 131 us
    ppermute x44 -> x43, waiting for transfers between devices: 275 us -> 353 us  [fsdp_swap(): lax.ppermute(values, 'fsdp', [(at, at ^ distance) for at in range(count)])]
    pallas_call x0 -> x10, Pallas kernels: none -> 74.4 us  [the longest x9 55.4 us: expert_grad_call(): pl.pallas_call(functools.partial(expert_grad_body, each=len(each)), grid=...]
    all_to_all x12 -> x11, waiting for transfers between devices: 131 us -> 78.7 us  [ctx_exchange(): lax.all_to_all(values, 'ctx', split_axis=0, concat_axis=0, tiled=True)]
    dot_general x8 -> x0, matrix products: 49.4 us -> none  [experts_dot(): return jnp.einsum(spec, left, right, preferred_element_type=jnp.float32)]
    dot_general x28 -> x24, matrix products: 113 us -> 76.6 us  [dot_f32(): lax.dot_general(left, right, (dims, ((), ())), preferred_element_type=jnp...]
    all_gather x2 -> x4, waiting for transfers between devices: 0.01 us -> 32.2 us  [ctx_gather(): return lax.all_gather(values, 'ctx', axis=0, tiled=True)]
    another operation x12 -> x9, other arithmetic: 21.6 us -> 11.4 us
    all_to_all x12 -> x11, starting transfers between devices: 63 us -> 53.2 us  [ctx_exchange(): lax.all_to_all(values, 'ctx', split_axis=0, concat_axis=0, tiled=True)]
  transfers between devices with their start and end apart: 62 -> 61, of which waited for: 22 -> 23; matrix products, arithmetic and copies ran while one was open for 35% -> 26% of each run, Pallas kernels for 4% -> 9%
where the time goes in v4:
time: 1020 us
  waiting for transfers between devices  465 us (46%)
  Pallas kernels  163 us (16%)
  local copies, waits for them, and re-layouts  131 us (13%)
  other arithmetic  86 us (8%)
  starting transfers between devices  79.2 us (8%)
  matrix products  76.6 us (8%)
  between operations  16.1 us (2%)
    ppermute x43, waiting for transfers between devices, fsdp_swap(): lax.ppermute(values, 'fsdp', [(at, at ^ distance) for at in range(count)])  353 us
    all_to_all x11, waiting for transfers between devices, ctx_exchange(): lax.all_to_all(values, 'ctx', split_axis=0, concat_axis=0, tiled=True)  78.7 us
    dot_general x24, matrix products, dot_f32(): lax.dot_general(left, right, (dims, ((), ())), preferred_element_type=jnp...  76.6 us
    pallas_call x9, Pallas kernels, expert_grad_call(): pl.pallas_call(functools.partial(expert_grad_body, each=len(each)), grid=...  55.4 us
    all_to_all x11, starting transfers between devices, ctx_exchange(): lax.all_to_all(values, 'ctx', split_axis=0, concat_axis=0, tiled=True)  53.2 us
    pallas_call x1, Pallas kernels, experts_call(): pl.pallas_call(experts_body, grid=(count,), in_specs=[pl.BlockSpec((1, sl...  49 us
    unnamed x189, local copies, waits for them, and re-layouts  36.9 us
    all_gather x4, waiting for transfers between devices, ctx_gather(): return lax.all_gather(values, 'ctx', axis=0, tiled=True)  32.2 us
  transfers between devices with their start and end apart: 61, of which 23 were waited for; matrix products, arithmetic and copies ran while one was open for 26% of the time, Pallas kernels for 9%

profile of v4, /device:TPU:0, one launch (start us, length us, event | category | flops | bytes accessed | tf_op | source)
XLA Modules:
  0.0 1017.0 jit_solution(6625512293206759391)
XLA Ops:
  11.6 7.3 all-to-all-start
  18.9 5.0 fusion.120
  25.9 32.6 %collective-permute-done = bf16[2,128,2816]{2,1,0:T(8,128)(2,1)} collective-permute-done((bf16[2,128,2816]{2,1,0:T(8,128)(2,1)S(1)}, bf16[2,128,2816]{2,1,0:T(8,128)(2,1)}, u32[]{:S(2)}, u32[]{:S(2)}) %collective-permute-start) | collective-permute-done | bytes 1441824 | tf_op jit(solution)/shard_map/ppermute | solution.py:242
  58.5 29.3 %collective-permute-done.1 = bf16[2,128,2816]{2,1,0:T(8,128)(2,1)} collective-permute-done((bf16[2,128,2816]{2,1,0:T(8,128)(2,1)S(1)}, bf16[2,128,2816]{2,1,0:T(8,128)(2,1)}, u32[]{:S(2)}, u32[]{:S(2)}) %collective-permute-start.1) | collective-permute-done | bytes 1441824 | tf_op jit(solution)/shard_map/ppermute | solution.py:242
  90.6 25.1 %collective-permute-done.3 = bf16[8,64,1088]{2,1,0:T(8,128)(2,1)S(1)} collective-permute-done((bf16[8,64,1088]{2,1,0:T(8,128)(2,1)}, bf16[8,64,1088]{2,1,0:T(8,128)(2,1)S(1)}, u32[]{:S(2)}, u32[]{:S(2)}) %collective-permute-start.3) | collective-permute-done | bytes 1114144 | tf_op jit(solution)/shard_map/ppermute | solution.py:242
  144.0 14.2 %shard_map.212 = (bf16[1024,256]{1,0:T(8,128)(2,1)S(1)}, f32[2,1024,512]{2,1,0:T(8,128)}, f32[2,1024,1]{2,1,0:T(8,128)S(1)}) custom-call(bf16[1024,256]{1,0:T(8,128)(2,1)S(1)} %slice.308.nope_ref, bf16[2,1024,64]{2,1,0:T(8,128)(2,1)S(1)} %pad_maximum_fusion.17.rot_ref, bf16[1024,512]{1,0:T(8,128)(2,1)} %multiply_convert_fusion.1.lat_ref, ...), custom_call_target="tpu_custom_call" | custom-call | tf_op jit(solution)/shard_map/pallas_call | solution.py:395
  160.2 5.4 all-to-all-start.1
  170.1 18.1 %all-to-all-done.1 = bf16[8,128,256]{1,2,0:T(8,128)(2,1)S(1)} async-done(((bf16[8,128,256]{1,2,0:T(8,128)(2,1)}), bf16[8,128,256]{1,2,0:T(8,128)(2,1)S(1)}, u32[]{:S(2)}, u32[]{:S(2)}) %all-to-all-start.1) | async-done | bytes 524320 | tf_op jit(solution)/shard_map/all_to_all | solution.py:292
  188.2 5.0 all-to-all-start.2
  194.8 31.9 %collective-permute-done.5 = bf16[2,128,2816]{2,1,0:T(8,128)(2,1)} collective-permute-done((bf16[2,128,2816]{2,1,0:T(8,128)(2,1)}, bf16[2,128,2816]{2,1,0:T(8,128)(2,1)}, u32[]{:S(2)}, u32[]{:S(2)}) %collective-permute-start.5) | collective-permute-done | bytes 1441824 | tf_op jit(solution)/shard_map/ppermute | solution.py:242
  228.4 6.4 multiply_reduce_fusion.3
  238.6 5.5 constant_dynamic-update-slice_fusion.9
  244.1 5.6 constant_dynamic-update-slice_fusion.8
  264.4 6.3 collective-permute-done.10
  274.5 82.3 %collective-permute-done.7 = bf16[8,64,1152]{2,1,0:T(8,128)(2,1)} collective-permute-done((bf16[8,64,1152]{2,1,0:T(8,128)(2,1)S(1)}, bf16[8,64,1152]{2,1,0:T(8,128)(2,1)}, u32[]{:S(2)}, u32[]{:S(2)}) %collective-permute-start.7) | collective-permute-done | bytes 1179680 | tf_op jit(solution)/shard_map/ppermute | solution.py:242
  378.9 5.8 pad_maximum_fusion.6.gate_up_ref
  393.5 10.1 pad_maximum_fusion.dn_ref
  403.7 5.5 convolution_convert_fusion.1
  409.1 5.1 fusion.127
  414.2 32.2 %all-gather.11.cloned.1.call-done = bf16[1024,2048]{1,0:T(8,128)(2,1)} async-done(((bf16[128,2048]{1,0:T(8,128)(2,1)}), bf16[1024,2048]{1,0:T(8,128)(2,1)}) %all-gather.11.cloned.1.call-update) | async-done | bytes 4194320 | tf_op jit(solution)/shard_map/all_gather | solution.py:284
  446.4 6.2 multiply_convert_fusion.4
  454.5 5.4 multiply_convert_fusion
  459.9 49.0 %shard_map.213 = (bf16[2,432,1408]{2,1,0:T(8,128)(2,1)}, bf16[2,432,2816]{2,1,0:T(8,128)(2,1)}, bf16[2,432,2048]{2,1,0:T(8,128)(2,1)}, bf16[2,432,2048]{2,1,0:T(8,128)(2,1)}) custom-call(bf16[2,432,2048]{2,1,0:T(8,128)(2,1)} %bitcast.237, bf16[2,432,2048]{2,1,0:T(8,128)(2,1)} %bitcast.248, f32[2,432,1]{2,1,0:T(8,128)} %copy.393.gate_ref, ...), custom_call_target="tpu_custom_call" | custom-call | tf_op jit(solution)/shard_map/pallas_call | solution.py:507
  508.9 19.0 %shard_map.214 = bf16[1024,4096]{1,0:T(8,128)(2,1)} custom-call(bf16[1024,864]{1,0:T(8,128)(2,1)} %get-tuple-element.131.pick_ref, bf16[1024,768]{1,0:T(8,128)(2,1)S(1)} %pad_maximum_fusion.10.both_ref, bf16[1024,384]{1,0:T(8,128)(2,1)S(1)} %get-tuple-element.169.act_ref, bf16[864,2048]{1,0:T(8,128)(2,1)} %bitcast.274, bf16[864,2048]{1,0:T(8,128)(2,1)} %bitcast.273, ...), custom_call_target="tpu_custom_call" | custom-call | tf_op jit(solution)/shard_map/pallas_call | solution.py:582
  538.5 7.4 shard_map.218
  546.4 13.0 %collective-permute-done.18.refs_2_ = bf16[2,1408,512]{2,1,0:T(8,128)(2,1)} collective-permute-done((bf16[2,1408,512]{2,1,0:T(8,128)(2,1)}, bf16[2,1408,512]{2,1,0:T(8,128)(2,1)}, u32[]{:S(2)}, u32[]{:S(2)}) %collective-permute-start.18) | collective-permute-done | bytes 2883616 | tf_op jit(solution)/shard_map/ppermute | solution.py:242
  573.1 5.2 shard_map.220
  578.2 51.4 %collective-permute-done.19.refs_3_ = bf16[2,1408,512]{2,1,0:T(8,128)(2,1)} collective-permute-done((bf16[2,1408,512]{2,1,0:T(8,128)(2,1)}, bf16[2,1408,512]{2,1,0:T(8,128)(2,1)}, u32[]{:S(2)}, u32[]{:S(2)}) %collective-permute-start.19) | collective-permute-done | bytes 2883616 | tf_op jit(solution)/shard_map/ppermute | solution.py:242
  629.6 61.1 %collective-permute-done.21.refs_3_ = bf16[1,512,2816]{2,1,0:T(8,128)(2,1)S(1)} collective-permute-done((bf16[1,512,2816]{2,1,0:T(8,128)(2,1)S(1)}, bf16[1,512,2816]{2,1,0:T(8,128)(2,1)S(1)}, u32[]{:S(2)}, u32[]{:S(2)}) %collective-permute-start.21) | collective-permute-done | bytes 2883616 | tf_op jit(solution)/shard_map/ppermute | solution.py:242
  706.9 7.6 shard_map.222
  720.4 14.4 %all-to-all-done.4 = bf16[8,128,256]{2,1,0:T(8,128)(2,1)} async-done(((bf16[8,128,256]{2,1,0:T(8,128)(2,1)}), bf16[8,128,256]{2,1,0:T(8,128)(2,1)}, u32[]{:S(2)}, u32[]{:S(2)}) %all-to-all-start.4) | async-done | bytes 524320 | tf_op jit(solution)/shard_map/all_to_all | solution.py:292
  734.8 25.0 %shard_map.221 = (bf16[1024,256]{1,0:T(8,128)(2,1)S(1)}, f32[2,1024,64]{2,1,0:T(8,128)}, f32[2,512,256]{2,1,0:T(8,128)}, f32[1024,512]{1,0:T(8,128)}, f32[1024,64]{1,0:T(8,128)S(1)}) custom-call(bf16[1024,256]{1,0:T(8,128)(2,1)} %bitcast.54.grad_ref, bf16[1024,256]{1,0:T(8,128)(2,1)S(1)} %copy-done.8, bf16[2,1024,64]{2,1,0:T(8,128)(2,1)S(1)} %copy-done.10, ...), custom_call_target="tpu_custom_call" | custom-call | tf_op jit(solution)/shard_map/pallas_call | solution.py:430
  778.3 6.8 copy.412
  789.3 15.4 %all-to-all-done.5 = bf16[8,128,576]{1,2,0:T(8,128)(2,1)S(1)} async-done(((bf16[8,128,576]{1,2,0:T(8,128)(2,1)}), bf16[8,128,576]{1,2,0:T(8,128)(2,1)S(1)}, u32[]{:S(2)}, u32[]{:S(2)}) %all-to-all-start.5) | async-done | bytes 1179680 | tf_op jit(solution)/shard_map/all_to_all | solution.py:292
  804.7 6.8 copy.400
  829.8 10.2 %collective-permute-done.22.refs_4_ = bf16[1,512,2816]{2,1,0:T(8,128)(2,1)} collective-permute-done((bf16[1,512,2816]{2,1,0:T(8,128)(2,1)}, bf16[1,512,2816]{2,1,0:T(8,128)(2,1)}, u32[]{:S(2)}, u32[]{:S(2)}) %collective-permute-start.22) | collective-permute-done | bytes 2883616 | tf_op jit(solution)/shard_map/ppermute | solution.py:242
  841.5 6.6 fusion.3
  848.1 5.7 shard_map.224
  853.8 11.9 %shard_map.223 = f32[2,512,2816]{2,1,0:T(8,128)} custom-call(bf16[2,432,2048]{2,1,0:T(8,128)(2,1)} %bitcast.240, bf16[2,432,2816]{2,1,0:T(8,128)(2,1)} %get-tuple-element.90.refs_1_, bf16[2,512,2816]{2,1,0:T(8,128)(2,1)} %collective-permute-done.41.refs_2_, bf16[1,512,2816]{2,1,0:T(8,128)(2,1)S(1)} %copy-done.12, ...), custom_call_target="tpu_custom_call" | custom-call | tf_op jit(solution)/shard_map/pallas_call | solution.py:544
  871.2 6.7 copy.410
  885.8 6.4 constant_dynamic-slice_fusion.2
  898.2 5.6 all-to-all-start.6
  905.0 5.6 all-to-all-done.6
  927.8 5.6 collective-permute-done.37
  935.2 6.4 all-to-all-done.10
  950.8 8.3 all-to-all-done.9
  983.4 6.2 all-to-all-start.8
  996.1 8.9 all-to-all-done.8
  (473 shorter events, 274.5 us)
Async XLA Ops:
  7.2 116.6 %all-gather.15.cloned.1.call-start = ((), (), s32[]{:S(2)}) async-start(), calls=%async_computation.19 | async-start | bytes 4718592 | tf_op jit(solution)/shard_map/all_gather | solution.py:284
  11.6 76.2 %all-to-all-start = ((bf16[8,64,960]{2,1,0:T(8,128)(2,1)}), bf16[8,64,960]{2,1,0:T(8,128)(2,1)S(1)}, u32[]{:S(2)}, u32[]{:S(2)}) async-start(bf16[8,64,960]{2,1,0:T(8,128)(2,1)} %pad_maximum_fusion.14), calls=%async_computation | async-start | bytes 2097152 | tf_op jit(solution)/shard_map/all_to_all | solution.py:292
  18.8 209.5 %all-gather.7.cloned.1.call-start = ((), (), s32[]{:S(2)}) async-start(), calls=%async_computation.13 | async-start | bytes 8650752 | tf_op jit(solution)/shard_map/all_gather | solution.py:843
  23.9 34.6 %collective-permute-start = (bf16[2,128,2816]{2,1,0:T(8,128)(2,1)S(1)}, bf16[2,128,2816]{2,1,0:T(8,128)(2,1)}, u32[]{:S(2)}, u32[]{:S(2)}) collective-permute-start(bf16[2,128,2816]{2,1,0:T(8,128)(2,1)S(1)} %get-tuple-element.138), channel_id=1, source_target_pairs={{0,2},{1,3},{2,0},{3,1},{4,6},{5,7},{6,4},{7,5},{8,10},{9,11},{10,... | collective-permute-start | bytes 4325384 | tf_op jit(solution)/shard_map/ppermute | solution.py:242
  25.3 62.4 %collective-permute-start.1 = (bf16[2,128,2816]{2,1,0:T(8,128)(2,1)S(1)}, bf16[2,128,2816]{2,1,0:T(8,128)(2,1)}, u32[]{:S(2)}, u32[]{:S(2)}) collective-permute-start(bf16[2,128,2816]{2,1,0:T(8,128)(2,1)S(1)} %get-tuple-element.137), channel_id=1, source_target_pairs={{0,2},{1,3},{2,0},{3,1},{4,6},{5,7},{6,4},{7,5},{8,10},{9,11},{10,... | collective-permute-start | bytes 4325384 | tf_op jit(solution)/shard_map/ppermute | solution.py:242
  89.1 26.5 %collective-permute-start.3 = (bf16[8,64,1088]{2,1,0:T(8,128)(2,1)}, bf16[8,64,1088]{2,1,0:T(8,128)(2,1)S(1)}, u32[]{:S(2)}, u32[]{:S(2)}) collective-permute-start(bf16[8,64,1088]{2,1,0:T(8,128)(2,1)} %get-tuple-element.184), channel_id=1, source_target_pairs={{0,2},{1,3},{2,0},{3,1},{4,6},{5,7},{6,4},{7,5},{8,10},{9,11},{10,... | collective-permute-start | bytes 3342344 | tf_op jit(solution)/shard_map/ppermute | solution.py:242
  90.6 25.1 %collective-permute-start.2 = (bf16[8,64,1088]{2,1,0:T(8,128)(2,1)}, bf16[8,64,1088]{2,1,0:T(8,128)(2,1)S(1)}, u32[]{:S(2)}, u32[]{:S(2)}) collective-permute-start(bf16[8,64,1088]{2,1,0:T(8,128)(2,1)} %get-tuple-element.184), channel_id=1, source_target_pairs={{0,1},{1,0},{2,3},{3,2},{4,5},{5,4},{6,7},{7,6},{8,9},{9,8},{10,11... | collective-permute-start | bytes 3342344 | tf_op jit(solution)/shard_map/ppermute | solution.py:242
  160.2 27.9 %all-to-all-start.1 = ((bf16[8,128,256]{1,2,0:T(8,128)(2,1)}), bf16[8,128,256]{1,2,0:T(8,128)(2,1)S(1)}, u32[]{:S(2)}, u32[]{:S(2)}) async-start(bf16[8,128,256]{1,2,0:T(8,128)(2,1)} %copy.377), calls=%async_computation.1 | async-start | bytes 1048576 | tf_op jit(solution)/shard_map/all_to_all | solution.py:292
  188.2 40.2 %all-to-all-start.2 = ((bf16[8,64,1152]{2,1,0:T(8,128)(2,1)}), bf16[8,64,1152]{2,1,0:T(8,128)(2,1)S(1)}, u32[]{:S(2)}, u32[]{:S(2)}) async-start(bf16[8,64,1152]{2,1,0:T(8,128)(2,1)} %fusion.29), calls=%async_computation.2 | async-start | bytes 2359296 | tf_op jit(solution)/shard_map/all_to_all | solution.py:292
  193.1 180.4 %all-gather.9.cloned.1.call-start = ((), (), s32[]{:S(2)}) async-start(), calls=%async_computation.14 | async-start | bytes 4718592 | tf_op jit(solution)/shard_map/all_gather | solution.py:284
  193.2 33.5 %collective-permute-start.5 = (bf16[2,128,2816]{2,1,0:T(8,128)(2,1)}, bf16[2,128,2816]{2,1,0:T(8,128)(2,1)}, u32[]{:S(2)}, u32[]{:S(2)}) collective-permute-start(bf16[2,128,2816]{2,1,0:T(8,128)(2,1)} %get-tuple-element.136), channel_id=1, source_target_pairs={{0,2},{1,3},{2,0},{3,1},{4,6},{5,7},{6,4},{7,5},{8,10},{9,11},{10,... | collective-permute-start | bytes 4325384 | tf_op jit(solution)/shard_map/ppermute | solution.py:242
  194.8 49.3 %collective-permute-start.9 = (bf16[2,512,2816]{2,1,0:T(8,128)(2,1)}, bf16[2,512,2816]{2,1,0:T(8,128)(2,1)}, u32[]{:S(2)}, u32[]{:S(2)}) collective-permute-start(bf16[2,512,2816]{2,1,0:T(8,128)(2,1)} %param.22), channel_id=1, source_target_pairs={{0,1},{1,0},{2,3},{3,2},{4,5},{5,4},{6,7},{7,6},{8,9},{9,8},{10,11... | collective-permute-start | bytes 17301512 | tf_op jit(solution)/shard_map/ppermute | solution.py:242
  235.9 34.8 %collective-permute-start.10 = (bf16[2,128,2816]{2,1,0:T(8,128)(2,1)}, bf16[2,128,2816]{2,1,0:T(8,128)(2,1)}, u32[]{:S(2)}, u32[]{:S(2)}) collective-permute-start(bf16[2,128,2816]{2,1,0:T(8,128)(2,1)} %get-tuple-element.135), channel_id=1, source_target_pairs={{0,2},{1,3},{2,0},{3,1},{4,6},{5,7},{6,4},{7,5},{8,10},{9,11},{10,... | collective-permute-start | bytes 4325384 | tf_op jit(solution)/shard_map/ppermute | solution.py:242
  237.5 156.0 %collective-permute-start.15 = (bf16[2,1408,512]{2,1,0:T(8,128)(2,1)}, bf16[2,1408,512]{2,1,0:T(8,128)(2,1)}, u32[]{:S(2)}, u32[]{:S(2)}) collective-permute-start(bf16[2,1408,512]{2,1,0:T(8,128)(2,1)} %param.23), channel_id=1, source_target_pairs={{0,1},{1,0},{2,3},{3,2},{4,5},{5,4},{6,7},{7,6},{8,9},{9,8},{10,11... | collective-permute-start | bytes 8650760 | tf_op jit(solution)/shard_map/ppermute | solution.py:242
  252.3 121.2 %collective-permute-start.16 = (bf16[2,1408,512]{2,1,0:T(8,128)(2,1)}, bf16[2,1408,512]{2,1,0:T(8,128)(2,1)}, u32[]{:S(2)}, u32[]{:S(2)}) collective-permute-start(bf16[2,1408,512]{2,1,0:T(8,128)(2,1)} %param.23), channel_id=1, source_target_pairs={{0,2},{1,3},{2,0},{3,1},{4,6},{5,7},{6,4},{7,5},{8,10},{9,11},{10,... | collective-permute-start | bytes 8650760 | tf_op jit(solution)/shard_map/ppermute | solution.py:242
  262.8 183.6 %all-gather.11.cloned.1.call-start = ((), (), s32[]{:S(2)}) async-start(), calls=%async_computation.15 | async-start | bytes 4718592 | tf_op jit(solution)/shard_map/all_gather | solution.py:284
  262.9 93.9 %collective-permute-start.7 = (bf16[8,64,1152]{2,1,0:T(8,128)(2,1)S(1)}, bf16[8,64,1152]{2,1,0:T(8,128)(2,1)}, u32[]{:S(2)}, u32[]{:S(2)}) collective-permute-start(bf16[8,64,1152]{2,1,0:T(8,128)(2,1)S(1)} %all-to-all-done.2), channel_id=1, source_target_pairs={{0,2},{1,3},{2,0},{3,1},{4,6},{5,7},{6,4},{7,5},{8,10},{9,11},{10,... | collective-permute-start | bytes 3538952 | tf_op jit(solution)/shard_map/ppermute | solution.py:242
  273.3 100.5 %collective-permute-start.6 = (bf16[8,64,1152]{2,1,0:T(8,128)(2,1)S(1)}, bf16[8,64,1152]{2,1,0:T(8,128)(2,1)}, u32[]{:S(2)}, u32[]{:S(2)}) collective-permute-start(bf16[8,64,1152]{2,1,0:T(8,128)(2,1)S(1)} %all-to-all-done.2), channel_id=1, source_target_pairs={{0,1},{1,0},{2,3},{3,2},{4,5},{5,4},{6,7},{7,6},{8,9},{9,8},{10,11... | collective-permute-start | bytes 3538952 | tf_op jit(solution)/shard_map/ppermute | solution.py:242
  356.8 17.6 %collective-permute-start.8 = (bf16[8,64,1152]{2,1,0:T(8,128)(2,1)}, bf16[8,64,1152]{2,1,0:T(8,128)(2,1)}, u32[]{:S(2)}, u32[]{:S(2)}) collective-permute-start(bf16[8,64,1152]{2,1,0:T(8,128)(2,1)} %collective-permute-done.7), channel_id=1, source_target_pairs={{0,1},{1,0},{2,3},{3,2},{4,5},{5,4},{6,7},{7,6},{8,9},{9,8},{10,11... | collective-permute-start | bytes 3538952 | tf_op jit(solution)/shard_map/ppermute | solution.py:242
  373.5 14.9 %collective-permute-start.12 = (bf16[2,128,2816]{2,1,0:T(8,128)(2,1)}, bf16[2,128,2816]{2,1,0:T(8,128)(2,1)}, u32[]{:S(2)}, u32[]{:S(2)}) collective-permute-start(bf16[2,128,2816]{2,1,0:T(8,128)(2,1)} %collective-permute-done.1), channel_id=1, source_target_pairs={{0,1},{1,0},{2,3},{3,2},{4,5},{5,4},{6,7},{7,6},{8,9},{9,8},{10,11... | collective-permute-start | bytes 4325384 | tf_op jit(solution)/shard_map/ppermute | solution.py:242
  373.6 318.7 %reduce-scatter.3.cloned.1.call-start = ((), (), s32[]{:S(2)}) async-start(), calls=%async_computation.16 | async-start | bytes 9437184 | tf_op jit(solution)/shard_map/reduce_scatter | solution.py:288
  373.8 17.1 %collective-permute-start.13 = (bf16[2,128,2816]{2,1,0:T(8,128)(2,1)}, bf16[2,128,2816]{2,1,0:T(8,128)(2,1)S(1)}, u32[]{:S(2)}, u32[]{:S(2)}) collective-permute-start(bf16[2,128,2816]{2,1,0:T(8,128)(2,1)} %collective-permute-done.5), channel_id=1, source_target_pairs={{0,1},{1,0},{2,3},{3,2},{4,5},{5,4},{6,7},{7,6},{8,9},{9,8},{10,11... | collective-permute-start | bytes 4325384 | tf_op jit(solution)/shard_map/ppermute | solution.py:242
  374.3 19.2 %collective-permute-start.17 = (bf16[2,1408,512]{2,1,0:T(8,128)(2,1)}, bf16[2,1408,512]{2,1,0:T(8,128)(2,1)S(1)}, u32[]{:S(2)}, u32[]{:S(2)}) collective-permute-start(bf16[2,1408,512]{2,1,0:T(8,128)(2,1)} %collective-permute-done.16), channel_id=1, source_target_pairs={{0,1},{1,0},{2,3},{3,2},{4,5},{5,4},{6,7},{7,6},{8,9},{9,8},{10,11... | collective-permute-start | bytes 8650760 | tf_op jit(solution)/shard_map/ppermute | solution.py:242
  528.0 340.1 %all-gather.13.cloned.1.call-start = ((), (), s32[]{:S(2)}) async-start(), calls=%async_computation.17 | async-start | bytes 4718592 | tf_op jit(solution)/shard_map/all_gather | solution.py:284
  545.9 19.6 %collective-permute-start.20 = (bf16[2,512,2816]{2,1,0:T(8,128)(2,1)}, bf16[2,512,2816]{2,1,0:T(8,128)(2,1)S(1)}, u32[]{:S(2)}, u32[]{:S(2)}) collective-permute-start(bf16[2,512,2816]{2,1,0:T(8,128)(2,1)} %shard_map.218), channel_id=1, source_target_pairs={{0,1},{1,0},{2,3},{3,2},{4,5},{5,4},{6,7},{7,6},{8,9},{9,8},{10,11... | collective-permute-start | bytes 17301512 | tf_op jit(solution)/shard_map/ppermute | solution.py:242
  564.0 65.6 %collective-permute-start.19 = (bf16[2,1408,512]{2,1,0:T(8,128)(2,1)}, bf16[2,1408,512]{2,1,0:T(8,128)(2,1)}, u32[]{:S(2)}, u32[]{:S(2)}) collective-permute-start(bf16[2,1408,512]{2,1,0:T(8,128)(2,1)} %shard_map.216), channel_id=1, source_target_pairs={{0,2},{1,3},{2,0},{3,1},{4,6},{5,7},{6,4},{7,5},{8,10},{9,11},{10,... | collective-permute-start | bytes 8650760 | tf_op jit(solution)/shard_map/ppermute | solution.py:242
  572.7 118.0 %collective-permute-start.21 = (bf16[1,512,2816]{2,1,0:T(8,128)(2,1)S(1)}, bf16[1,512,2816]{2,1,0:T(8,128)(2,1)S(1)}, u32[]{:S(2)}, u32[]{:S(2)}) collective-permute-start(bf16[1,512,2816]{2,1,0:T(8,128)(2,1)S(1)} %shard_map.219), channel_id=1, source_target_pairs={{0,2},{1,3},{2,0},{3,1},{4,6},{5,7},{6,4},{7,5},{8,10},{9,11},{10,... | collective-permute-start | bytes 8650760 | tf_op jit(solution)/shard_map/ppermute | solution.py:242
  702.5 32.3 %all-to-all-start.4 = ((bf16[8,128,256]{2,1,0:T(8,128)(2,1)}), bf16[8,128,256]{2,1,0:T(8,128)(2,1)}, u32[]{:S(2)}, u32[]{:S(2)}) async-start(bf16[8,128,256]{2,1,0:T(8,128)(2,1)} %bitcast.276), calls=%async_computation.5 | async-start | bytes 1048576 | tf_op jit(solution)/shard_map/all_to_all | solution.py:292
  706.8 122.9 %collective-permute-start.42 = (bf16[2,1408,512]{2,1,0:T(8,128)(2,1)}, bf16[2,1408,512]{2,1,0:T(8,128)(2,1)}, u32[]{:S(2)}, u32[]{:S(2)}) collective-permute-start(bf16[2,1408,512]{2,1,0:T(8,128)(2,1)} %shard_map.217), channel_id=1, source_target_pairs={{0,1},{1,0},{2,3},{3,2},{4,5},{5,4},{6,7},{7,6},{8,9},{9,8},{10,11... | collective-permute-start | bytes 8650760 | tf_op jit(solution)/shard_map/ppermute | solution.py:242
  714.5 139.3 %collective-permute-start.41 = (bf16[2,512,2816]{2,1,0:T(8,128)(2,1)}, bf16[2,512,2816]{2,1,0:T(8,128)(2,1)}, u32[]{:S(2)}, u32[]{:S(2)}) collective-permute-start(bf16[2,512,2816]{2,1,0:T(8,128)(2,1)} %shard_map.222), channel_id=1, source_target_pairs={{0,1},{1,0},{2,3},{3,2},{4,5},{5,4},{6,7},{7,6},{8,9},{9,8},{10,11... | collective-permute-start | bytes 17301512 | tf_op jit(solution)/shard_map/ppermute | solution.py:242
  765.5 39.2 %all-to-all-start.5 = ((bf16[8,128,576]{1,2,0:T(8,128)(2,1)}), bf16[8,128,576]{1,2,0:T(8,128)(2,1)S(1)}, u32[]{:S(2)}, u32[]{:S(2)}) async-start(bf16[8,128,576]{1,2,0:T(8,128)(2,1)} %pad_maximum_fusion.13), calls=%async_computation.7 | async-start | bytes 2359296 | tf_op jit(solution)/shard_map/all_to_all | solution.py:292
  769.1 235.9 %reduce-scatter.5.cloned.1.call-start = ((), (), s32[]{:S(2)}) async-start(), calls=%async_computation.18 | async-start | bytes 4718592 | tf_op jit(solution)/shard_map/reduce_scatter | solution.py:288
  774.2 65.8 %collective-permute-start.22 = (bf16[1,512,2816]{2,1,0:T(8,128)(2,1)}, bf16[1,512,2816]{2,1,0:T(8,128)(2,1)}, u32[]{:S(2)}, u32[]{:S(2)}) collective-permute-start(bf16[1,512,2816]{2,1,0:T(8,128)(2,1)} %shard_map.220), channel_id=1, source_target_pairs={{0,2},{1,3},{2,0},{3,1},{4,6},{5,7},{6,4},{7,5},{8,10},{9,11},{10,... | collective-permute-start | bytes 8650760 | tf_op jit(solution)/shard_map/ppermute | solution.py:242
  819.2 48.9 %collective-permute-start.38 = (bf16[8,64,1152]{2,1,0:T(8,128)(2,1)}, bf16[8,64,1152]{2,1,0:T(8,128)(2,1)}, u32[]{:S(2)}, u32[]{:S(2)}) collective-permute-start(bf16[8,64,1152]{2,1,0:T(8,128)(2,1)} %get-tuple-element.119), channel_id=1, source_target_pairs={{0,1},{1,0},{2,3},{3,2},{4,5},{5,4},{6,7},{7,6},{8,9},{9,8},{10,11... | collective-permute-start | bytes 3538952 | tf_op jit(solution)/shard_map/ppermute | solution.py:242
  822.3 45.8 %collective-permute-start.40 = (bf16[8,64,1152]{2,1,0:T(8,128)(2,1)}, bf16[8,64,1152]{2,1,0:T(8,128)(2,1)}, u32[]{:S(2)}, u32[]{:S(2)}) collective-permute-start(bf16[8,64,1152]{2,1,0:T(8,128)(2,1)} %add_convert_fusion.1), channel_id=1, source_target_pairs={{0,2},{1,3},{2,0},{3,1},{4,6},{5,7},{6,4},{7,5},{8,10},{9,11},{10,... | collective-permute-start | bytes 3538952 | tf_op jit(solution)/shard_map/ppermute | solution.py:242
  829.7 35.9 %collective-permute-start.32 = (bf16[512,128]{1,0:T(8,128)(2,1)}, bf16[512,128]{1,0:T(8,128)(2,1)}, u32[]{:S(2)}, u32[]{:S(2)}) collective-permute-start(bf16[512,128]{1,0:T(8,128)(2,1)} %bitcast.302), channel_id=1, source_target_pairs={{0,1},{1,0},{2,3},{3,2},{4,5},{5,4},{6,7},{7,6},{8,9},{9,8},{10,11... | collective-permute-start | bytes 393224 | tf_op jit(solution)/shard_map/ppermute | solution.py:242
  840.0 26.3 %collective-permute-start.34 = (bf16[512,128]{1,0:T(8,128)(2,1)S(1)}, bf16[512,128]{1,0:T(8,128)(2,1)}, u32[]{:S(2)}, u32[]{:S(2)}) collective-permute-start(bf16[512,128]{1,0:T(8,128)(2,1)S(1)} %add_convert_fusion.8), channel_id=1, source_target_pairs={{0,2},{1,3},{2,0},{3,1},{4,6},{5,7},{6,4},{7,5},{8,10},{9,11},{10,... | collective-permute-start | bytes 393224 | tf_op jit(solution)/shard_map/ppermute | solution.py:242
  893.4 33.9 %collective-permute-start.35 = (bf16[512,256]{1,0:T(8,128)(2,1)}, bf16[512,256]{1,0:T(8,128)(2,1)}, u32[]{:S(2)}, u32[]{:S(2)}) collective-permute-start(bf16[512,256]{1,0:T(8,128)(2,1)} %convolution_convert_fusion.8), channel_id=1, source_target_pairs={{0,1},{1,0},{2,3},{3,2},{4,5},{5,4},{6,7},{7,6},{8,9},{9,8},{10,11... | collective-permute-start | bytes 786440 | tf_op jit(solution)/shard_map/ppermute | solution.py:242
  896.5 26.1 %collective-permute-start.36 = (bf16[512,256]{1,0:T(8,128)(2,1)}, bf16[512,256]{1,0:T(8,128)(2,1)}, u32[]{:S(2)}, u32[]{:S(2)}) collective-permute-start(bf16[512,256]{1,0:T(8,128)(2,1)} %convolution_convert_fusion.7), channel_id=1, source_target_pairs={{0,1},{1,0},{2,3},{3,2},{4,5},{5,4},{6,7},{7,6},{8,9},{9,8},{10,11... | collective-permute-start | bytes 786440 | tf_op jit(solution)/shard_map/ppermute | solution.py:242
  905.0 73.8 %collective-permute-start.29 = (bf16[512,576]{0,1:T(8,128)(2,1)}, bf16[512,576]{0,1:T(8,128)(2,1)}, u32[]{:S(2)}, u32[]{:S(2)}) collective-permute-start(bf16[512,576]{0,1:T(8,128)(2,1)} %convolution_convert_fusion.4), channel_id=1, source_target_pairs={{0,1},{1,0},{2,3},{3,2},{4,5},{5,4},{6,7},{7,6},{8,9},{9,8},{10,11... | collective-permute-start | bytes 1769480 | tf_op jit(solution)/shard_map/ppermute | solution.py:242
  910.6 31.0 %all-to-all-start.10 = ((bf16[8,64,1152]{2,1,0:T(8,128)(2,1)}), bf16[8,64,1152]{2,1,0:T(8,128)(2,1)S(1)}, u32[]{:S(2)}, u32[]{:S(2)}) async-start(bf16[8,64,1152]{2,1,0:T(8,128)(2,1)} %add_convert_fusion), calls=%async_computation.12 | async-start | bytes 2359296 | tf_op jit(solution)/shard_map/all_to_all | solution.py:292
  916.4 28.6 %collective-permute-start.30 = (bf16[512,576]{0,1:T(8,128)(2,1)}, bf16[512,576]{0,1:T(8,128)(2,1)}, u32[]{:S(2)}, u32[]{:S(2)}) collective-permute-start(bf16[512,576]{0,1:T(8,128)(2,1)} %convolution_convert_fusion.3), channel_id=1, source_target_pairs={{0,1},{1,0},{2,3},{3,2},{4,5},{5,4},{6,7},{7,6},{8,9},{9,8},{10,11... | collective-permute-start | bytes 1769480 | tf_op jit(solution)/shard_map/ppermute | solution.py:242
  922.7 26.1 %collective-permute-start.26 = (bf16[512,384]{1,0:T(8,128)(2,1)}, bf16[512,384]{1,0:T(8,128)(2,1)}, u32[]{:S(2)}, u32[]{:S(2)}) collective-permute-start(bf16[512,384]{1,0:T(8,128)(2,1)} %convolution_convert_fusion.6), channel_id=1, source_target_pairs={{0,1},{1,0},{2,3},{3,2},{4,5},{5,4},{6,7},{7,6},{8,9},{9,8},{10,11... | collective-permute-start | bytes 1179656 | tf_op jit(solution)/shard_map/ppermute | solution.py:242
  927.2 21.5 %collective-permute-start.28 = (bf16[512,384]{1,0:T(8,128)(2,1)}, bf16[512,384]{1,0:T(8,128)(2,1)}, u32[]{:S(2)}, u32[]{:S(2)}) collective-permute-start(bf16[512,384]{1,0:T(8,128)(2,1)} %add_convert_fusion.5), channel_id=1, source_target_pairs={{0,2},{1,3},{2,0},{3,1},{4,6},{5,7},{6,4},{7,5},{8,10},{9,11},{10,... | collective-permute-start | bytes 1179656 | tf_op jit(solution)/shard_map/ppermute | solution.py:242
  941.5 17.6 %all-to-all-start.9 = ((bf16[8,64,256]{2,1,0:T(8,128)(2,1)}), bf16[8,64,256]{2,1,0:T(8,128)(2,1)S(1)}, u32[]{:S(2)}, u32[]{:S(2)}) async-start(bf16[8,64,256]{2,1,0:T(8,128)(2,1)} %bitcast.85), calls=%async_computation.11 | async-start | bytes 524288 | tf_op jit(solution)/shard_map/all_to_all | solution.py:292
  947.3 31.5 %collective-permute-start.31 = (bf16[512,576]{0,1:T(8,128)(2,1)}, bf16[512,576]{0,1:T(8,128)(2,1)}, u32[]{:S(2)}, u32[]{:S(2)}) collective-permute-start(bf16[512,576]{0,1:T(8,128)(2,1)} %add_convert_fusion.3), channel_id=1, source_target_pairs={{0,2},{1,3},{2,0},{3,1},{4,6},{5,7},{6,4},{7,5},{8,10},{9,11},{10,... | collective-permute-start | bytes 1769480 | tf_op jit(solution)/shard_map/ppermute | solution.py:242
  959.1 24.3 %all-to-all-start.7 = ((bf16[8,64,384]{2,1,0:T(8,128)(2,1)}), bf16[8,64,384]{2,1,0:T(8,128)(2,1)S(1)}, u32[]{:S(2)}, u32[]{:S(2)}) async-start(bf16[8,64,384]{2,1,0:T(8,128)(2,1)} %bitcast.66), calls=%async_computation.9 | async-start | bytes 786432 | tf_op jit(solution)/shard_map/all_to_all | solution.py:292
  983.4 21.6 %all-to-all-start.8 = ((bf16[8,64,576]{2,1,0:T(8,128)(2,1)}), bf16[8,64,576]{2,1,0:T(8,128)(2,1)}, u32[]{:S(2)}, u32[]{:S(2)}) async-start(bf16[8,64,576]{2,1,0:T(8,128)(2,1)} %bitcast.73), calls=%async_computation.10 | async-start | bytes 1310720 | tf_op jit(solution)/shard_map/all_to_all | solution.py:292
  (98 other events, 1142.7 us)
Sparse Core Ops, SparseCore 0:
  10.1 93.2 all-gather.14
  123.9 87.9 all-gather.6
  236.0 72.7 all-gather.8
  373.7 72.6 all-gather.10
  528.1 147.2 reduce-scatter.2
  696.8 89.9 all-gather.12
  868.2 110.2 reduce-scatter.4

commit v5 on v4

--- a/solution.py
+++ b/solution.py
@@ -319,10 +319,13 @@
     return stacked.transpose(1, 0, 2, 3).reshape(-1, stacked.shape[-1])
 
 
-def shard_rows(grads, n_ctx, rank, *gate):
+def shard_rows(grads, n_ctx, rank):
     width = grads.shape[-1]
-    blocks = grads.astype(jnp.bfloat16).reshape(n_ctx, 4, -1, width).transpose(1, 0, 2, 3)
-    return fsdp_reduce(blocks, rank, *gate)
+    blocks = grads.reshape(n_ctx, 4, -1, width).transpose(1, 0, 2, 3)
+    rel = [lax.dynamic_index_in_dim(blocks, rank ^ k, 0, False) for k in range(4)]
+    near = [fsdp_swap(rel[k], 1).astype(jnp.float32) for k in (1, 3)]
+    own = (rel[0].astype(jnp.float32) + near[0]).astype(jnp.bfloat16)
+    return own, (rel[2].astype(jnp.float32) + near[1]).astype(jnp.bfloat16)
 
 
 def attention_forward_body(
@@ -651,12 +654,14 @@
     shared_send = jnp.concatenate([gate_send, up_send, down_send], -1)
     shared_got = ctx_exchange(after(shared_send, first_done))
     shared_far = fsdp_swap(shared_got, 2)
-
-    resid_mid = attn_mid((gu_far[2], shared_got))
+    dn_far = fsdp_swap(after(expert_down, first_done), 2)
+
+    resid_mid = attn_mid((shared_got,))
     normed_mid, inv_mid = norm_forward(resid_mid, gain_mid)
     mid_send = swap_chunks(normed_mid.astype(jnp.bfloat16), rank, 1)
+    grads_all = ctx_gather(after(swap_chunks(out_grad[0], rank, 1), first_done))
+    mid_send = after(mid_send, grads_all, gu_far[2], dn_far, shared_far)
     mid_all = ctx_gather(mid_send)
-    grads_all = ctx_gather(after(swap_chunks(out_grad[0], rank, 1), mid_all))
     shared_full = whole_rows(
         [shared_got, fsdp_swap(shared_got, 1), shared_far, fsdp_swap(after(shared_far, resid_mid), 1)], rank
     )
@@ -668,7 +673,6 @@
         + [fsdp_swap(after(v, resid_mid), 1) for v in gu_far],
         1,
     )
-    dn_far = fsdp_swap(after(expert_down, first_done), 2)
     dn_rel = jnp.concatenate(
         [expert_down, fsdp_swap(expert_down, 1), dn_far, fsdp_swap(after(dn_far, mid_send), 1)], 2
     )
@@ -731,16 +735,17 @@
     def gu_term(k, kind, *more, **which):
         return expert_grad_call(x_late, both_grad, (quarter, k), (2 * FF, 0), kind, *more, **which)
 
-    dn_send = [dn_term(k, jnp.bfloat16) for k in (1, 3)]
-    dn_got = [fsdp_swap(v, 1) for v in dn_send]
+    dn_send = dn_term(3, jnp.bfloat16)
+    dn_got = fsdp_swap(dn_send, 1)
     x_late = after(x_late, dn_send)
-    gu_send = [gu_term(k, jnp.bfloat16) for k in (1, 3)]
-    gu_got = [fsdp_swap(v, 1) for v in gu_send]
-    dn_other = dn_term(2, jnp.bfloat16, dn_got[1])
+    gu_send = gu_term(3, jnp.bfloat16)
+    gu_got = fsdp_swap(gu_send, 1)
+    dn_other = dn_term(2, jnp.bfloat16, after(dn_got, gu_send))
     dn_back = fsdp_swap(dn_other, 2)
-    gu_other = [gu_term(2, jnp.bfloat16, gu_got[1][e : e + 1], only=e) for e in range(exp_local)]
+    gu_got = after(gu_got, dn_other)
+    gu_other = [gu_term(2, jnp.bfloat16, gu_got[e : e + 1], only=e) for e in range(exp_local)]
     gu_back = [fsdp_swap(v, 2) for v in gu_other]
-    mid_late, grads_late = after((mid_all, grads_all), gu_send)
+    mid_late, grads_late = after((mid_all, grads_all), gu_other, dn_back)
     shared_grad = jnp.concatenate(
         [
             dot_f32(mid_late, s_both_grad, ((0,), (0,))),
@@ -749,7 +754,10 @@
         -1,
     )
     shared_grad = swap_chunks(shared_grad, rank, 0).astype(jnp.bfloat16)
-    sums = after(ctx_scatter(sums_part), dn_back, gu_back[0], gu_other, shared_grad).astype(jnp.float32)
+    shared_own, shared_other = shard_rows(shared_grad, n_ctx, rank)
+    sums = after(
+        ctx_scatter(sums_part), gu_back[0], shared_own, shared_other
+    ).astype(jnp.float32)
     mid_grad = swap_chunks(sums[:, :D], rank, 1)
     ffn_out = swap_chunks(sums[:, D:], rank, 1)
 
@@ -764,9 +772,13 @@
     token_grad, stage, gains_grad, query_w, latent_w, expand_w, output_w = attn_backward(
         resid_grad.astype(jnp.bfloat16), gu_back[1:], reduce_gains
     )
-    keys_there, sums_there = stage
-    shared_term = shard_rows(shared_grad, n_ctx, rank, keys_there).astype(jnp.bfloat16)
-    shared_grad = ctx_exchange(shared_term).astype(jnp.float32)
+    scored, keys_there, sums_there = stage
+    x_late, y_late, act_late = after((x_late, y_late, act_late), scored)
+    dn_near = fsdp_swap(dn_term(1, jnp.bfloat16), 1)
+    gu_near = fsdp_swap(gu_term(1, jnp.bfloat16), 1)
+    shared_far = fsdp_swap(after(shared_other, keys_there), 2)
+    shared_term = shared_own.astype(jnp.float32) + shared_far.astype(jnp.float32)
+    shared_grad = ctx_exchange(shared_term.astype(jnp.bfloat16)).astype(jnp.float32)
     gate_grad = shared_grad[:, :, :sff_dev].transpose(1, 0, 2).reshape(-1, SFF)
     up_grad = shared_grad[:, :, sff_pad : sff_pad + sff_dev].transpose(1, 0, 2).reshape(-1, SFF)
     shared_gu_grad = jnp.concatenate([gate_grad, up_grad], -1)
@@ -775,8 +787,8 @@
 
     hidden_in_grad = (resid_grad + token_grad).astype(jnp.bfloat16)
     hidden_out = (resid_mid + ffn_out).astype(jnp.bfloat16)
-    dn_grad = dn_term(0, jnp.float32, dn_got[0], after(dn_back, sums_there))
-    gu_grad = gu_term(0, jnp.float32, gu_got[0], each=after(gu_back, sums_there))
+    dn_grad = dn_term(0, jnp.float32, dn_near, after(dn_back, sums_there))
+    gu_grad = gu_term(0, jnp.float32, gu_near, each=after(gu_back, sums_there))
     return (
         hidden_out[None],
         hidden_in_grad[None],
@@ -893,21 +905,26 @@
         query_grad = jnp.concatenate([nope_grad, *rot_grads], -1)
         key_got = after(key_sent, resid_all, stages)
         in_part = dot_f32(query_grad, query_full, ((1,), (1,))).astype(jnp.bfloat16)
-        in_grad = ctx_scatter(after(in_part, resid_all))
+        in_grad = ctx_scatter(in_part)
         gain_in_grad = jnp.sum(
-            in_part.astype(jnp.float32) * (saved["hidden_f"] * saved["inv_all"]), 0
+            in_part.astype(jnp.float32)
+            * (saved["hidden_all"].astype(jnp.float32) * saved["inv_all"]),
+            0,
         )
         normed_cols = columns_by_distance(normed_bf, n_ctx, rank)
-        query_terms = fsdp_reduce_terms(
-            lambda k: dot_f32(after(normed_cols[k], in_part), query_grad, ((0,), (0,))),
-            jnp.bfloat16,
-        )
-        query_terms = ctx_exchange(query_terms.astype(jnp.bfloat16).reshape(n_ctx, rows, q_wide))
-        query_terms = query_terms.astype(jnp.float32)
-        resid_cols = columns_by_distance(after(resid_all, in_part), n_ctx, rank)
-        output_w = fsdp_reduce_terms(
-            lambda k: dot_f32(resid_cols[k], saved["heads_out"], ((0,), (0,))), jnp.bfloat16
-        )
+        resid_cols = columns_by_distance(resid_all, n_ctx, rank)
+        query_late = after(query_grad, key_got)
+
+        def head_terms(k):
+            query_term = dot_f32(normed_cols[k], query_late, ((0,), (0,)))
+            output_term = dot_f32(resid_cols[k], saved["heads_out"], ((0,), (0,)))
+            return jnp.concatenate([query_term, output_term], -1)
+
+        head_sums = fsdp_reduce_terms(head_terms, jnp.bfloat16).astype(jnp.bfloat16)
+        head_sums = ctx_exchange(head_sums.reshape(n_ctx, rows, -1))
+        query_terms = head_sums[:, :, :q_wide].astype(jnp.float32)
+        output_w = head_sums[:, :, q_wide:].astype(jnp.float32)
+        output_w = output_w.transpose(0, 2, 1).reshape(H * DV, rows)
         key_sum = jnp.sum(key_got.astype(jnp.float32), 0)
         own_cos, own_sin = own_rows(cos_table), own_rows(sin_table)
         lat_in_grad, gain_lat_grad = norm_backward(
@@ -923,8 +940,6 @@
         latent_w = latent_w.astype(jnp.bfloat16)
         latent_w = ctx_exchange(latent_w.reshape(n_ctx, rows, KVL + DR))
         latent_w = jnp.sum(after(latent_w, in_grad).astype(jnp.float32), 0)
-        output_w = ctx_exchange(output_w.astype(jnp.bfloat16).reshape(n_ctx, rows, heads * DV))
-        output_w = output_w.astype(jnp.float32).transpose(0, 2, 1).reshape(H * DV, rows)
         inv_in = own_rows(saved["inv_all"])
         in_own = dot_f32(compressed_grad, latent_full, ((1,), (1,)))
         gain_in_grad = gain_in_grad + jnp.sum(in_own * (tokens * inv_in), 0)
@@ -937,7 +952,7 @@
         query_w = jnp.concatenate([nope_w, rot_w], -1).transpose(1, 0, 2, 3).reshape(rows, -1)
         in_grad = after(in_grad, gains_grad).astype(jnp.float32) + in_own
         token_grad = norm_backward(tokens, inv_in, gain_in, in_grad)[0]
-        return token_grad, (key_sent, in_part), gains_grad, query_w, latent_w, expand_w, output_w
+        return token_grad, (lat_total, key_sent, head_sums), gains_grad, query_w, latent_w, expand_w, output_w
 
     return first, middle, backward
 
@@ -1060,7 +1075,7 @@
             for g, at in ((query_g, 0), (latent_g, 0), (expand_g, 1), (output_g, 1))
         ]
         gains_grad = reduce_gains(gain_in_grad, gain_lat_grad)
-        return (token_grad, (resid_bf, latent_grad), gains_grad, *scattered)
+        return (token_grad, (resid_bf, lat_buffer, latent_grad), gains_grad, *scattered)
 
     return (lambda early: latent_full), (lambda early: resid_mid), backward
 

time: 1020 us -> 993 us (0.974)
  waiting for transfers between devices: 465 us -> 364 us
  blocking collectives: 0 us -> 74.1 us
  starting transfers between devices: 79.2 us -> 62 us
    all_to_all x0 -> x2, blocking collectives: none -> 74.1 us  [ctx_exchange(): lax.all_to_all(values, 'ctx', split_axis=0, concat_axis=0, tiled=True)]
    ppermute x43 -> x40, waiting for transfers between devices: 353 us -> 301 us  [fsdp_swap(): lax.ppermute(values, 'fsdp', [(at, at ^ distance) for at in range(count)])]
    all_to_all x11 -> x8, waiting for transfers between devices: 78.7 us -> 32.4 us  [ctx_exchange(): lax.all_to_all(values, 'ctx', split_axis=0, concat_axis=0, tiled=True)]
    all_to_all x11 -> x8, starting transfers between devices: 53.2 us -> 39.3 us  [ctx_exchange(): lax.all_to_all(values, 'ctx', split_axis=0, concat_axis=0, tiled=True)]
    ppermute x43 -> x40, starting transfers between devices: 25.6 us -> 21.7 us  [fsdp_swap(): lax.ppermute(values, 'fsdp', [(at, at ^ distance) for at in range(count)])]
    unnamed x189 -> x229, local copies, waits for them, and re-layouts: 36.9 us -> 35.3 us
  transfers between devices with their start and end apart: 61 -> 55, of which waited for: 23 -> 20; matrix products, arithmetic and copies ran while one was open for 26% -> 28% of each run, Pallas kernels for 9% -> 8%
where the time goes in v5:
time: 993 us; the launch traced here: 983 us
  waiting for transfers between devices  364 us (37%)
  Pallas kernels  163 us (16%)
  local copies, waits for them, and re-layouts  136 us (14%)
  other arithmetic  92.4 us (9%)
  matrix products  75 us (8%)
  blocking collectives  74.1 us (7%)
  starting transfers between devices  62 us (6%)
  between operations  16.3 us (2%)
    ppermute x40, waiting for transfers between devices, fsdp_swap(): lax.ppermute(values, 'fsdp', [(at, at ^ distance) for at in range(count)])  301 us
    dot_general x24, matrix products, dot_f32(): lax.dot_general(left, right, (dims, ((), ())), preferred_element_type=jnp...  75 us
    all_to_all x2, blocking collectives, ctx_exchange(): lax.all_to_all(values, 'ctx', split_axis=0, concat_axis=0, tiled=True)  74.1 us
    pallas_call x9, Pallas kernels, expert_grad_call(): pl.pallas_call(functools.partial(expert_grad_body, each=len(each)), grid=...  56.4 us
    pallas_call x1, Pallas kernels, experts_call(): pl.pallas_call(experts_body, grid=(count,), in_specs=[pl.BlockSpec((1, sl...  48.8 us
    all_to_all x8, starting transfers between devices, ctx_exchange(): lax.all_to_all(values, 'ctx', split_axis=0, concat_axis=0, tiled=True)  39.3 us
    unnamed x229, local copies, waits for them, and re-layouts  35.3 us
    all_to_all x8, waiting for transfers between devices, ctx_exchange(): lax.all_to_all(values, 'ctx', split_axis=0, concat_axis=0, tiled=True)  32.4 us
  transfers between devices with their start and end apart: 55, of which 20 were waited for; matrix products, arithmetic and copies ran while one was open for 28% of the time, Pallas kernels for 8%

profile of v5, /device:TPU:0, one launch (start us, length us, event | category | flops | bytes accessed | tf_op | source)
XLA Modules:
  0.0 983.2 jit_solution(14150888548735147920)
XLA Ops:
  11.6 7.3 all-to-all-start
  18.9 5.0 fusion.125
  25.9 32.5 %collective-permute-done = bf16[2,128,2816]{2,1,0:T(8,128)(2,1)S(1)} collective-permute-done((bf16[2,128,2816]{2,1,0:T(8,128)(2,1)S(1)}, bf16[2,128,2816]{2,1,0:T(8,128)(2,1)S(1)}, u32[]{:S(2)}, u32[]{:S(2)}) %collective-permute-start) | collective-permute-done | bytes 1441824 | tf_op jit(solution)/shard_map/ppermute | solution.py:242
  59.6 28.2 %collective-permute-done.1 = bf16[2,128,2816]{2,1,0:T(8,128)(2,1)} collective-permute-done((bf16[2,128,2816]{2,1,0:T(8,128)(2,1)S(1)}, bf16[2,128,2816]{2,1,0:T(8,128)(2,1)}, u32[]{:S(2)}, u32[]{:S(2)}) %collective-permute-start.1) | collective-permute-done | bytes 1441824 | tf_op jit(solution)/shard_map/ppermute | solution.py:242
  90.6 25.1 %collective-permute-done.3 = bf16[8,64,1088]{2,1,0:T(8,128)(2,1)S(1)} collective-permute-done((bf16[8,64,1088]{2,1,0:T(8,128)(2,1)}, bf16[8,64,1088]{2,1,0:T(8,128)(2,1)S(1)}, u32[]{:S(2)}, u32[]{:S(2)}) %collective-permute-start.3) | collective-permute-done | bytes 1114144 | tf_op jit(solution)/shard_map/ppermute | solution.py:242
  131.8 5.7 constant_dynamic-update-slice_fusion.9
  140.2 5.6 constant_dynamic-update-slice_fusion.8
  145.8 5.4 all-to-all-start.2
  158.2 6.1 fusion.22
  174.2 13.9 %shard_map.212 = (bf16[1024,256]{1,0:T(8,128)(2,1)S(1)}, f32[2,1024,512]{2,1,0:T(8,128)}, f32[2,1024,1]{2,1,0:T(8,128)S(1)}) custom-call(bf16[1024,256]{1,0:T(8,128)(2,1)S(1)} %slice.318.nope_ref, bf16[2,1024,64]{2,1,0:T(8,128)(2,1)S(1)} %pad_maximum_fusion.18.rot_ref, bf16[1024,512]{1,0:T(8,128)(2,1)} %multiply_convert_fusion.1.lat_ref, ...), custom_call_target="tpu_custom_call" | custom-call | tf_op jit(solution)/shard_map/pallas_call | solution.py:398
  203.1 22.4 %all-to-all-done.1 = bf16[8,128,256]{1,2,0:T(8,128)(2,1)S(1)} async-done(((bf16[8,128,256]{1,2,0:T(8,128)(2,1)}), bf16[8,128,256]{1,2,0:T(8,128)(2,1)S(1)}, u32[]{:S(2)}, u32[]{:S(2)}) %all-to-all-start.1) | async-done | bytes 524320 | tf_op jit(solution)/shard_map/all_to_all | solution.py:292
  238.3 7.0 multiply_reduce_fusion.3
  247.3 49.9 %collective-permute-done.9 = bf16[2,1408,512]{2,1,0:T(8,128)(2,1)S(1)} collective-permute-done((bf16[2,1408,512]{2,1,0:T(8,128)(2,1)}, bf16[2,1408,512]{2,1,0:T(8,128)(2,1)S(1)}, u32[]{:S(2)}, u32[]{:S(2)}) %collective-permute-start.9) | collective-permute-done | bytes 2883616 | tf_op jit(solution)/shard_map/ppermute | solution.py:242
  297.2 23.8 %collective-permute-done.6 = bf16[8,64,1152]{2,1,0:T(8,128)(2,1)} collective-permute-done((bf16[8,64,1152]{2,1,0:T(8,128)(2,1)}, bf16[8,64,1152]{2,1,0:T(8,128)(2,1)}, u32[]{:S(2)}, u32[]{:S(2)}) %collective-permute-start.6) | collective-permute-done | bytes 1179680 | tf_op jit(solution)/shard_map/ppermute | solution.py:242
  334.9 5.5 multiply_convert_fusion
  346.0 7.0 pad_maximum_fusion.6.gate_up_ref
  357.9 8.0 pad_maximum_fusion.dn_ref
  366.0 29.6 %all-gather.11.cloned.1.call-done = bf16[1024,2048]{1,0:T(8,128)(2,1)} async-done(((bf16[128,2048]{1,0:T(8,128)(2,1)}), bf16[1024,2048]{1,0:T(8,128)(2,1)}) %all-gather.11.cloned.1.call-update) | async-done | bytes 4194320 | tf_op jit(solution)/shard_map/all_gather | solution.py:284
  395.6 6.4 fusion.132
  406.3 5.5 convolution_convert_fusion.1
  411.7 48.8 %shard_map.213 = (bf16[2,432,1408]{2,1,0:T(8,128)(2,1)}, bf16[2,432,2816]{2,1,0:T(8,128)(2,1)}, bf16[2,432,2048]{2,1,0:T(8,128)(2,1)}, bf16[2,432,2048]{2,1,0:T(8,128)(2,1)}) custom-call(bf16[2,432,2048]{2,1,0:T(8,128)(2,1)} %bitcast.240, bf16[2,432,2048]{2,1,0:T(8,128)(2,1)} %bitcast.248, f32[2,432,1]{2,1,0:T(8,128)} %copy.402.gate_ref, ...), custom_call_target="tpu_custom_call" | custom-call | tf_op jit(solution)/shard_map/pallas_call | solution.py:510
  460.5 19.0 %shard_map.214 = bf16[1024,4096]{1,0:T(8,128)(2,1)} custom-call(bf16[1024,864]{1,0:T(8,128)(2,1)} %get-tuple-element.127.pick_ref, bf16[1024,768]{1,0:T(8,128)(2,1)S(1)} %pad_maximum_fusion.10.both_ref, bf16[1024,384]{1,0:T(8,128)(2,1)S(1)} %get-tuple-element.165.act_ref, bf16[864,2048]{1,0:T(8,128)(2,1)} %bitcast.276, bf16[864,2048]{1,0:T(8,128)(2,1)} %bitcast.275, ...), custom_call_target="tpu_custom_call" | custom-call | tf_op jit(solution)/shard_map/pallas_call | solution.py:585
  481.3 4.6 shard_map.215
  485.9 7.6 shard_map.216
  494.0 12.8 %collective-permute-done.19.refs_2_ = bf16[2,1408,512]{2,1,0:T(8,128)(2,1)} collective-permute-done((bf16[2,1408,512]{2,1,0:T(8,128)(2,1)S(1)}, bf16[2,1408,512]{2,1,0:T(8,128)(2,1)}, u32[]{:S(2)}, u32[]{:S(2)}) %collective-permute-start.19) | collective-permute-done | bytes 2883616 | tf_op jit(solution)/shard_map/ppermute | solution.py:242
  515.8 5.1 shard_map.219
  521.0 5.3 shard_map.218
  527.1 49.9 %collective-permute-done.21.refs_3_ = bf16[2,1408,512]{2,1,0:T(8,128)(2,1)} collective-permute-done((bf16[2,1408,512]{2,1,0:T(8,128)(2,1)}, bf16[2,1408,512]{2,1,0:T(8,128)(2,1)}, u32[]{:S(2)}, u32[]{:S(2)}) %collective-permute-start.21) | collective-permute-done | bytes 2883616 | tf_op jit(solution)/shard_map/ppermute | solution.py:242
  586.0 7.0 copy.403
  601.7 36.4 %collective-permute-done.20.refs_3_ = bf16[1,512,2816]{2,1,0:T(8,128)(2,1)S(1)} collective-permute-done((bf16[1,512,2816]{2,1,0:T(8,128)(2,1)}, bf16[1,512,2816]{2,1,0:T(8,128)(2,1)S(1)}, u32[]{:S(2)}, u32[]{:S(2)}) %collective-permute-start.20) | collective-permute-done | bytes 2883616 | tf_op jit(solution)/shard_map/ppermute | solution.py:242
  644.2 4.9 convolution_convert_fusion.2
  649.2 31.8 %all_to_all.54 = bf16[8,128,256]{2,1,0:T(8,128)(2,1)S(1)} all-to-all(bf16[8,128,256]{2,1,0:T(8,128)(2,1)S(1)} %bitcast.282), channel_id=1, replica_groups=mesh['ctx'=8,'fsdp'=4] {'ctx'}, dimensions={0} | all-to-all | bytes 1048576 | tf_op jit(solution)/shard_map/all_to_all | solution.py:292
  681.0 25.0 %shard_map.220 = (bf16[1024,256]{1,0:T(8,128)(2,1)S(1)}, f32[2,1024,64]{2,1,0:T(8,128)}, f32[2,512,256]{2,1,0:T(8,128)}, f32[1024,512]{1,0:T(8,128)}, f32[1024,64]{1,0:T(8,128)S(1)}) custom-call(bf16[1024,256]{1,0:T(8,128)(2,1)S(1)} %bitcast.247, bf16[1024,256]{1,0:T(8,128)(2,1)S(1)} %copy-done.12, bf16[2,1024,64]{2,1,0:T(8,128)(2,1)S(1)} %copy-done.10, ...), custom_call_target="tpu_custom_call" | custom-call | tf_op jit(solution)/shard_map/pallas_call | solution.py:433
  708.7 42.3 %all_to_all.55 = bf16[8,128,576]{1,2,0:T(8,128)(2,1)} all-to-all(bf16[8,128,576]{1,2,0:T(8,128)(2,1)S(1)} %pad_maximum_fusion.13), channel_id=1, replica_groups=mesh['ctx'=8,'fsdp'=4] {'ctx'}, dimensions={0} | all-to-all | bytes 2359296 | tf_op jit(solution)/shard_map/all_to_all | solution.py:292
  756.7 23.5 %collective-permute-done.37 = bf16[8,64,1152]{2,1,0:T(8,128)(2,1)} collective-permute-done((bf16[8,64,1152]{2,1,0:T(8,128)(2,1)}, bf16[8,64,1152]{2,1,0:T(8,128)(2,1)}, u32[]{:S(2)}, u32[]{:S(2)}) %collective-permute-start.37) | collective-permute-done | bytes 1179680 | tf_op jit(solution)/shard_map/ppermute | solution.py:242
  795.1 6.9 fusion.3
  803.9 6.4 copy.411
  813.0 4.6 constant_dynamic-slice_fusion.14
  823.3 7.6 shard_map.221
  835.1 7.1 collective-permute-done.36
  845.4 6.6 copy.412
  891.3 4.9 all-to-all-start.6
  900.6 5.2 collective-permute-done.33
  910.3 4.9 all-to-all-start.8
  931.3 4.7 all-to-all-start.7
  947.1 4.6 all-to-all-done.7
  958.4 5.7 shard_map.224
  964.0 11.9 %shard_map.222 = f32[2,512,2816]{2,1,0:T(8,128)} custom-call(bf16[2,432,2048]{2,1,0:T(8,128)(2,1)} %bitcast.243, bf16[2,432,2816]{2,1,0:T(8,128)(2,1)} %get-tuple-element.89.refs_1_, bf16[2,512,2816]{2,1,0:T(8,128)(2,1)} %collective-permute-done.38.refs_2_, bf16[1,512,2816]{2,1,0:T(8,128)(2,1)S(1)} %copy-done.14, ...), custom_call_target="tpu_custom_call" | custom-call | tf_op jit(solution)/shard_map/pallas_call | solution.py:547
  (507 shorter events, 261.9 us)
Async XLA Ops:
  7.2 116.4 %all-gather.15.cloned.1.call-start = ((), (), s32[]{:S(2)}) async-start(), calls=%async_computation.18 | async-start | bytes 4718592 | tf_op jit(solution)/shard_map/all_gather | solution.py:284
  11.6 76.2 %all-to-all-start = ((bf16[8,64,960]{2,1,0:T(8,128)(2,1)}), bf16[8,64,960]{2,1,0:T(8,128)(2,1)S(1)}, u32[]{:S(2)}, u32[]{:S(2)}) async-start(bf16[8,64,960]{2,1,0:T(8,128)(2,1)} %pad_maximum_fusion.14), calls=%async_computation | async-start | bytes 2097152 | tf_op jit(solution)/shard_map/all_to_all | solution.py:292
  18.8 219.5 %all-gather.7.cloned.1.call-start = ((), (), s32[]{:S(2)}) async-start(), calls=%async_computation.12 | async-start | bytes 8650752 | tf_op jit(solution)/shard_map/all_gather | solution.py:855
  23.9 34.5 %collective-permute-start = (bf16[2,128,2816]{2,1,0:T(8,128)(2,1)S(1)}, bf16[2,128,2816]{2,1,0:T(8,128)(2,1)S(1)}, u32[]{:S(2)}, u32[]{:S(2)}) collective-permute-start(bf16[2,128,2816]{2,1,0:T(8,128)(2,1)S(1)} %get-tuple-element.134), channel_id=1, source_target_pairs={{0,2},{1,3},{2,0},{3,1},{4,6},{5,7},{6,4},{7,5},{8,10},{9,11},{10,... | collective-permute-start | bytes 4325384 | tf_op jit(solution)/shard_map/ppermute | solution.py:242
  25.3 62.4 %collective-permute-start.1 = (bf16[2,128,2816]{2,1,0:T(8,128)(2,1)S(1)}, bf16[2,128,2816]{2,1,0:T(8,128)(2,1)}, u32[]{:S(2)}, u32[]{:S(2)}) collective-permute-start(bf16[2,128,2816]{2,1,0:T(8,128)(2,1)S(1)} %get-tuple-element.133), channel_id=1, source_target_pairs={{0,2},{1,3},{2,0},{3,1},{4,6},{5,7},{6,4},{7,5},{8,10},{9,11},{10,... | collective-permute-start | bytes 4325384 | tf_op jit(solution)/shard_map/ppermute | solution.py:242
  89.1 26.5 %collective-permute-start.3 = (bf16[8,64,1088]{2,1,0:T(8,128)(2,1)}, bf16[8,64,1088]{2,1,0:T(8,128)(2,1)S(1)}, u32[]{:S(2)}, u32[]{:S(2)}) collective-permute-start(bf16[8,64,1088]{2,1,0:T(8,128)(2,1)} %get-tuple-element.180), channel_id=1, source_target_pairs={{0,2},{1,3},{2,0},{3,1},{4,6},{5,7},{6,4},{7,5},{8,10},{9,11},{10,... | collective-permute-start | bytes 3342344 | tf_op jit(solution)/shard_map/ppermute | solution.py:242
  90.6 25.1 %collective-permute-start.2 = (bf16[8,64,1088]{2,1,0:T(8,128)(2,1)}, bf16[8,64,1088]{2,1,0:T(8,128)(2,1)S(1)}, u32[]{:S(2)}, u32[]{:S(2)}) collective-permute-start(bf16[8,64,1088]{2,1,0:T(8,128)(2,1)} %get-tuple-element.180), channel_id=1, source_target_pairs={{0,1},{1,0},{2,3},{3,2},{4,5},{5,4},{6,7},{7,6},{8,9},{9,8},{10,11... | collective-permute-start | bytes 3342344 | tf_op jit(solution)/shard_map/ppermute | solution.py:242
  123.6 16.5 %collective-permute-start.10 = (bf16[2,512,2816]{2,1,0:T(8,128)(2,1)}, bf16[2,512,2816]{2,1,0:T(8,128)(2,1)}, u32[]{:S(2)}, u32[]{:S(2)}) collective-permute-start(bf16[2,512,2816]{2,1,0:T(8,128)(2,1)} %param.22), channel_id=1, source_target_pairs={{0,1},{1,0},{2,3},{3,2},{4,5},{5,4},{6,7},{7,6},{8,9},{9,8},{10,11... | collective-permute-start | bytes 17301512 | tf_op jit(solution)/shard_map/ppermute | solution.py:242
  123.9 76.1 %collective-permute-start.8 = (bf16[2,128,2816]{2,1,0:T(8,128)(2,1)}, bf16[2,128,2816]{2,1,0:T(8,128)(2,1)}, u32[]{:S(2)}, u32[]{:S(2)}) collective-permute-start(bf16[2,128,2816]{2,1,0:T(8,128)(2,1)} %get-tuple-element.132), channel_id=1, source_target_pairs={{0,2},{1,3},{2,0},{3,1},{4,6},{5,7},{6,4},{7,5},{8,10},{9,11},{10,... | collective-permute-start | bytes 4325384 | tf_op jit(solution)/shard_map/ppermute | solution.py:242
  125.3 103.6 %collective-permute-start.11 = (bf16[2,128,2816]{2,1,0:T(8,128)(2,1)}, bf16[2,128,2816]{2,1,0:T(8,128)(2,1)}, u32[]{:S(2)}, u32[]{:S(2)}) collective-permute-start(bf16[2,128,2816]{2,1,0:T(8,128)(2,1)} %get-tuple-element.131), channel_id=1, source_target_pairs={{0,2},{1,3},{2,0},{3,1},{4,6},{5,7},{6,4},{7,5},{8,10},{9,11},{10,... | collective-permute-start | bytes 4325384 | tf_op jit(solution)/shard_map/ppermute | solution.py:242
  125.9 232.0 %collective-permute-start.16 = (bf16[2,1408,512]{2,1,0:T(8,128)(2,1)}, bf16[2,1408,512]{2,1,0:T(8,128)(2,1)}, u32[]{:S(2)}, u32[]{:S(2)}) collective-permute-start(bf16[2,1408,512]{2,1,0:T(8,128)(2,1)} %param.23), channel_id=1, source_target_pairs={{0,1},{1,0},{2,3},{3,2},{4,5},{5,4},{6,7},{7,6},{8,9},{9,8},{10,11... | collective-permute-start | bytes 8650760 | tf_op jit(solution)/shard_map/ppermute | solution.py:242
  145.8 45.9 %all-to-all-start.2 = ((bf16[8,64,1152]{2,1,0:T(8,128)(2,1)}), bf16[8,64,1152]{2,1,0:T(8,128)(2,1)}, u32[]{:S(2)}, u32[]{:S(2)}) async-start(bf16[8,64,1152]{2,1,0:T(8,128)(2,1)} %fusion.34), calls=%async_computation.2 | async-start | bytes 2359296 | tf_op jit(solution)/shard_map/all_to_all | solution.py:292
  151.2 169.8 %all-gather.9.cloned.1.call-start = ((), (), s32[]{:S(2)}) async-start(), calls=%async_computation.13 | async-start | bytes 4718592 | tf_op jit(solution)/shard_map/all_gather | solution.py:284
  191.8 33.8 %all-to-all-start.1 = ((bf16[8,128,256]{1,2,0:T(8,128)(2,1)}), bf16[8,128,256]{1,2,0:T(8,128)(2,1)S(1)}, u32[]{:S(2)}, u32[]{:S(2)}) async-start(bf16[8,128,256]{1,2,0:T(8,128)(2,1)} %copy.386), calls=%async_computation.1 | async-start | bytes 1048576 | tf_op jit(solution)/shard_map/all_to_all | solution.py:292
  225.5 10.1 %all-to-all-start.3 = ((bf16[8,128,24]{1,2,0:T(8,128)(2,1)}), bf16[8,128,24]{1,2,0:T(8,128)(2,1)S(1)}, u32[]{:S(2)}, u32[]{:S(2)}) async-start(bf16[8,128,24]{1,2,0:T(8,128)(2,1)} %broadcast_in_dim.53), calls=%async_computation.3 | async-start | bytes 98304 | tf_op jit(solution)/shard_map/all_to_all | solution.py:292
  228.9 166.7 %all-gather.11.cloned.1.call-start = ((), (), s32[]{:S(2)}) async-start(), calls=%async_computation.14 | async-start | bytes 4718592 | tf_op jit(solution)/shard_map/all_gather | solution.py:284
  231.5 65.6 %collective-permute-start.9 = (bf16[2,1408,512]{2,1,0:T(8,128)(2,1)}, bf16[2,1408,512]{2,1,0:T(8,128)(2,1)S(1)}, u32[]{:S(2)}, u32[]{:S(2)}) collective-permute-start(bf16[2,1408,512]{2,1,0:T(8,128)(2,1)} %param.23), channel_id=1, source_target_pairs={{0,2},{1,3},{2,0},{3,1},{4,6},{5,7},{6,4},{7,5},{8,10},{9,11},{10,... | collective-permute-start | bytes 8650760 | tf_op jit(solution)/shard_map/ppermute | solution.py:242
  233.0 88.0 %collective-permute-start.6 = (bf16[8,64,1152]{2,1,0:T(8,128)(2,1)}, bf16[8,64,1152]{2,1,0:T(8,128)(2,1)}, u32[]{:S(2)}, u32[]{:S(2)}) collective-permute-start(bf16[8,64,1152]{2,1,0:T(8,128)(2,1)} %all-to-all-done.2), channel_id=1, source_target_pairs={{0,2},{1,3},{2,0},{3,1},{4,6},{5,7},{6,4},{7,5},{8,10},{9,11},{10,... | collective-permute-start | bytes 3538952 | tf_op jit(solution)/shard_map/ppermute | solution.py:242
  233.6 107.4 %collective-permute-start.5 = (bf16[8,64,1152]{2,1,0:T(8,128)(2,1)}, bf16[8,64,1152]{2,1,0:T(8,128)(2,1)}, u32[]{:S(2)}, u32[]{:S(2)}) collective-permute-start(bf16[8,64,1152]{2,1,0:T(8,128)(2,1)} %all-to-all-done.2), channel_id=1, source_target_pairs={{0,1},{1,0},{2,3},{3,2},{4,5},{5,4},{6,7},{7,6},{8,9},{9,8},{10,11... | collective-permute-start | bytes 3538952 | tf_op jit(solution)/shard_map/ppermute | solution.py:242
  321.0 317.1 %reduce-scatter.3.cloned.1.call-start = ((), (), s32[]{:S(2)}) async-start(), calls=%async_computation.15 | async-start | bytes 9437184 | tf_op jit(solution)/shard_map/reduce_scatter | solution.py:288
  330.4 10.9 %collective-permute-start.7 = (bf16[8,64,1152]{2,1,0:T(8,128)(2,1)}, bf16[8,64,1152]{2,1,0:T(8,128)(2,1)S(1)}, u32[]{:S(2)}, u32[]{:S(2)}) collective-permute-start(bf16[8,64,1152]{2,1,0:T(8,128)(2,1)} %collective-permute-done.6), channel_id=1, source_target_pairs={{0,1},{1,0},{2,3},{3,2},{4,5},{5,4},{6,7},{7,6},{8,9},{9,8},{10,11... | collective-permute-start | bytes 3538952 | tf_op jit(solution)/shard_map/ppermute | solution.py:242
  340.8 13.4 %collective-permute-start.13 = (bf16[2,128,2816]{2,1,0:T(8,128)(2,1)}, bf16[2,128,2816]{2,1,0:T(8,128)(2,1)S(1)}, u32[]{:S(2)}, u32[]{:S(2)}) collective-permute-start(bf16[2,128,2816]{2,1,0:T(8,128)(2,1)} %collective-permute-done.1), channel_id=1, source_target_pairs={{0,1},{1,0},{2,3},{3,2},{4,5},{5,4},{6,7},{7,6},{8,9},{9,8},{10,11... | collective-permute-start | bytes 4325384 | tf_op jit(solution)/shard_map/ppermute | solution.py:242
  340.9 14.5 %collective-permute-start.14 = (bf16[2,128,2816]{2,1,0:T(8,128)(2,1)}, bf16[2,128,2816]{2,1,0:T(8,128)(2,1)S(1)}, u32[]{:S(2)}, u32[]{:S(2)}) collective-permute-start(bf16[2,128,2816]{2,1,0:T(8,128)(2,1)} %collective-permute-done.8), channel_id=1, source_target_pairs={{0,1},{1,0},{2,3},{3,2},{4,5},{5,4},{6,7},{7,6},{8,9},{9,8},{10,11... | collective-permute-start | bytes 4325384 | tf_op jit(solution)/shard_map/ppermute | solution.py:242
  341.3 16.6 %collective-permute-start.17 = (bf16[2,1408,512]{2,1,0:T(8,128)(2,1)S(1)}, bf16[2,1408,512]{2,1,0:T(8,128)(2,1)S(1)}, u32[]{:S(2)}, u32[]{:S(2)}) collective-permute-start(bf16[2,1408,512]{2,1,0:T(8,128)(2,1)S(1)} %copy-done.49), channel_id=1, source_target_pairs={{0,1},{1,0},{2,3},{3,2},{4,5},{5,4},{6,7},{7,6},{8,9},{9,8},{10,11... | collective-permute-start | bytes 8650760 | tf_op jit(solution)/shard_map/ppermute | solution.py:242
  345.4 11.3 %collective-permute-start.15 = (bf16[2,128,2816]{2,1,0:T(8,128)(2,1)}, bf16[2,128,2816]{2,1,0:T(8,128)(2,1)S(1)}, u32[]{:S(2)}, u32[]{:S(2)}) collective-permute-start(bf16[2,128,2816]{2,1,0:T(8,128)(2,1)} %collective-permute-done.11), channel_id=1, source_target_pairs={{0,1},{1,0},{2,3},{3,2},{4,5},{5,4},{6,7},{7,6},{8,9},{9,8},{10,11... | collective-permute-start | bytes 4325384 | tf_op jit(solution)/shard_map/ppermute | solution.py:242
  479.6 365.9 %all-gather.13.cloned.1.call-start = ((), (), s32[]{:S(2)}) async-start(), calls=%async_computation.17 | async-start | bytes 4718592 | tf_op jit(solution)/shard_map/all_gather | solution.py:284
  493.5 19.3 %collective-permute-start.18 = (bf16[2,512,2816]{2,1,0:T(8,128)(2,1)}, bf16[2,512,2816]{2,1,0:T(8,128)(2,1)S(1)}, u32[]{:S(2)}, u32[]{:S(2)}) collective-permute-start(bf16[2,512,2816]{2,1,0:T(8,128)(2,1)} %shard_map.216), channel_id=1, source_target_pairs={{0,1},{1,0},{2,3},{3,2},{4,5},{5,4},{6,7},{7,6},{8,9},{9,8},{10,11... | collective-permute-start | bytes 17301512 | tf_op jit(solution)/shard_map/ppermute | solution.py:242
  493.5 13.3 %collective-permute-start.19 = (bf16[2,1408,512]{2,1,0:T(8,128)(2,1)S(1)}, bf16[2,1408,512]{2,1,0:T(8,128)(2,1)}, u32[]{:S(2)}, u32[]{:S(2)}) collective-permute-start(bf16[2,1408,512]{2,1,0:T(8,128)(2,1)S(1)} %copy-done.46), channel_id=1, source_target_pairs={{0,1},{1,0},{2,3},{3,2},{4,5},{5,4},{6,7},{7,6},{8,9},{9,8},{10,11... | collective-permute-start | bytes 8650760 | tf_op jit(solution)/shard_map/ppermute | solution.py:242
  511.3 65.6 %collective-permute-start.21 = (bf16[2,1408,512]{2,1,0:T(8,128)(2,1)}, bf16[2,1408,512]{2,1,0:T(8,128)(2,1)}, u32[]{:S(2)}, u32[]{:S(2)}) collective-permute-start(bf16[2,1408,512]{2,1,0:T(8,128)(2,1)} %shard_map.217), channel_id=1, source_target_pairs={{0,2},{1,3},{2,0},{3,1},{4,6},{5,7},{6,4},{7,5},{8,10},{9,11},{10,... | collective-permute-start | bytes 8650760 | tf_op jit(solution)/shard_map/ppermute | solution.py:242
  526.2 111.9 %collective-permute-start.20 = (bf16[1,512,2816]{2,1,0:T(8,128)(2,1)}, bf16[1,512,2816]{2,1,0:T(8,128)(2,1)S(1)}, u32[]{:S(2)}, u32[]{:S(2)}) collective-permute-start(bf16[1,512,2816]{2,1,0:T(8,128)(2,1)} %shard_map.218), channel_id=1, source_target_pairs={{0,2},{1,3},{2,0},{3,1},{4,6},{5,7},{6,4},{7,5},{8,10},{9,11},{10,... | collective-permute-start | bytes 8650760 | tf_op jit(solution)/shard_map/ppermute | solution.py:242
  751.0 29.2 %collective-permute-start.37 = (bf16[8,64,1152]{2,1,0:T(8,128)(2,1)}, bf16[8,64,1152]{2,1,0:T(8,128)(2,1)}, u32[]{:S(2)}, u32[]{:S(2)}) collective-permute-start(bf16[8,64,1152]{2,1,0:T(8,128)(2,1)} %get-tuple-element.114), channel_id=1, source_target_pairs={{0,2},{1,3},{2,0},{3,1},{4,6},{5,7},{6,4},{7,5},{8,10},{9,11},{10,... | collective-permute-start | bytes 3538952 | tf_op jit(solution)/shard_map/ppermute | solution.py:242
  752.5 92.9 %collective-permute-start.24 = (bf16[1,512,2816]{2,1,0:T(8,128)(2,1)}, bf16[1,512,2816]{2,1,0:T(8,128)(2,1)}, u32[]{:S(2)}, u32[]{:S(2)}) collective-permute-start(bf16[1,512,2816]{2,1,0:T(8,128)(2,1)} %shard_map.219), channel_id=1, source_target_pairs={{0,2},{1,3},{2,0},{3,1},{4,6},{5,7},{6,4},{7,5},{8,10},{9,11},{10,... | collective-permute-start | bytes 8650760 | tf_op jit(solution)/shard_map/ppermute | solution.py:242
  782.8 61.1 %all-to-all-start.9 = ((bf16[8,64,1152]{2,1,0:T(8,128)(2,1)}), bf16[8,64,1152]{2,1,0:T(8,128)(2,1)}, u32[]{:S(2)}, u32[]{:S(2)}) async-start(bf16[8,64,1152]{2,1,0:T(8,128)(2,1)} %add_convert_fusion), calls=%async_computation.11 | async-start | bytes 2359296 | tf_op jit(solution)/shard_map/all_to_all | solution.py:292
  787.2 155.4 %reduce-scatter.5.cloned.1.call-start = ((), (), s32[]{:S(2)}) async-start(), calls=%async_computation.16 | async-start | bytes 4718592 | tf_op jit(solution)/shard_map/reduce_scatter | solution.py:288
  789.1 21.7 %collective-permute-start.35 = (bf16[512,128]{1,0:T(8,128)(2,1)S(1)}, bf16[512,128]{1,0:T(8,128)(2,1)S(1)}, u32[]{:S(2)}, u32[]{:S(2)}) collective-permute-start(bf16[512,128]{1,0:T(8,128)(2,1)S(1)} %bitcast.300), channel_id=1, source_target_pairs={{0,1},{1,0},{2,3},{3,2},{4,5},{5,4},{6,7},{7,6},{8,9},{9,8},{10,11... | collective-permute-start | bytes 393224 | tf_op jit(solution)/shard_map/ppermute | solution.py:242
  810.3 24.7 %collective-permute-start.34 = (bf16[512,128]{1,0:T(8,128)(2,1)}, bf16[512,128]{1,0:T(8,128)(2,1)}, u32[]{:S(2)}, u32[]{:S(2)}) collective-permute-start(bf16[512,128]{1,0:T(8,128)(2,1)} %bitcast.87), channel_id=1, source_target_pairs={{0,1},{1,0},{2,3},{3,2},{4,5},{5,4},{6,7},{7,6},{8,9},{9,8},{10,11... | collective-permute-start | bytes 393224 | tf_op jit(solution)/shard_map/ppermute | solution.py:242
  811.5 30.7 %collective-permute-start.36 = (bf16[512,128]{1,0:T(8,128)(2,1)}, bf16[512,128]{1,0:T(8,128)(2,1)}, u32[]{:S(2)}, u32[]{:S(2)}) collective-permute-start(bf16[512,128]{1,0:T(8,128)(2,1)} %add_convert_fusion.3), channel_id=1, source_target_pairs={{0,2},{1,3},{2,0},{3,1},{4,6},{5,7},{6,4},{7,5},{8,10},{9,11},{10,... | collective-permute-start | bytes 393224 | tf_op jit(solution)/shard_map/ppermute | solution.py:242
  830.9 133.1 %collective-permute-start.38 = (bf16[2,512,2816]{2,1,0:T(8,128)(2,1)}, bf16[2,512,2816]{2,1,0:T(8,128)(2,1)}, u32[]{:S(2)}, u32[]{:S(2)}) collective-permute-start(bf16[2,512,2816]{2,1,0:T(8,128)(2,1)} %shard_map.221), channel_id=1, source_target_pairs={{0,1},{1,0},{2,3},{3,2},{4,5},{5,4},{6,7},{7,6},{8,9},{9,8},{10,11... | collective-permute-start | bytes 17301512 | tf_op jit(solution)/shard_map/ppermute | solution.py:242
  858.4 37.9 %collective-permute-start.29 = (bf16[512,640]{0,1:T(8,128)(2,1)}, bf16[512,640]{0,1:T(8,128)(2,1)}, u32[]{:S(2)}, u32[]{:S(2)}) collective-permute-start(bf16[512,640]{0,1:T(8,128)(2,1)} %pad_maximum_fusion.17), channel_id=1, source_target_pairs={{0,1},{1,0},{2,3},{3,2},{4,5},{5,4},{6,7},{7,6},{8,9},{9,8},{10,11... | collective-permute-start | bytes 1966088 | tf_op jit(solution)/shard_map/ppermute | solution.py:242
  868.2 31.0 %collective-permute-start.31 = (bf16[512,576]{0,1:T(8,128)(2,1)}, bf16[512,576]{0,1:T(8,128)(2,1)}, u32[]{:S(2)}, u32[]{:S(2)}) collective-permute-start(bf16[512,576]{0,1:T(8,128)(2,1)} %convolution_convert_fusion.4), channel_id=1, source_target_pairs={{0,1},{1,0},{2,3},{3,2},{4,5},{5,4},{6,7},{7,6},{8,9},{9,8},{10,11... | collective-permute-start | bytes 1769480 | tf_op jit(solution)/shard_map/ppermute | solution.py:242
  870.8 14.7 %collective-permute-start.32 = (bf16[512,576]{0,1:T(8,128)(2,1)}, bf16[512,576]{0,1:T(8,128)(2,1)}, u32[]{:S(2)}, u32[]{:S(2)}) collective-permute-start(bf16[512,576]{0,1:T(8,128)(2,1)} %convolution_convert_fusion.3), channel_id=1, source_target_pairs={{0,1},{1,0},{2,3},{3,2},{4,5},{5,4},{6,7},{7,6},{8,9},{9,8},{10,11... | collective-permute-start | bytes 1769480 | tf_op jit(solution)/shard_map/ppermute | solution.py:242
  889.3 16.5 %collective-permute-start.33 = (bf16[512,576]{0,1:T(8,128)(2,1)}, bf16[512,576]{0,1:T(8,128)(2,1)}, u32[]{:S(2)}, u32[]{:S(2)}) collective-permute-start(bf16[512,576]{0,1:T(8,128)(2,1)} %add_convert_fusion.2), channel_id=1, source_target_pairs={{0,2},{1,3},{2,0},{3,1},{4,6},{5,7},{6,4},{7,5},{8,10},{9,11},{10,... | collective-permute-start | bytes 1769480 | tf_op jit(solution)/shard_map/ppermute | solution.py:242
  890.7 67.7 %collective-permute-start.39 = (bf16[2,1408,512]{2,1,0:T(8,128)(2,1)}, bf16[2,1408,512]{2,1,0:T(8,128)(2,1)}, u32[]{:S(2)}, u32[]{:S(2)}) collective-permute-start(bf16[2,1408,512]{2,1,0:T(8,128)(2,1)} %shard_map.223), channel_id=1, source_target_pairs={{0,1},{1,0},{2,3},{3,2},{4,5},{5,4},{6,7},{7,6},{8,9},{9,8},{10,11... | collective-permute-start | bytes 8650760 | tf_op jit(solution)/shard_map/ppermute | solution.py:242
  891.3 19.0 %all-to-all-start.6 = ((f32[8,1,144]{2,1,0:T(1,128)}), f32[8,1,144]{2,1,0:T(1,128)S(1)}, u32[]{:S(2)}, u32[]{:S(2)}) async-start(f32[8,1,144]{2,1,0:T(1,128)} %all_to_all.39), calls=%async_computation.8 | async-start | bytes 16384 | tf_op jit(solution)/shard_map/all_to_all | solution.py:292
  896.3 30.5 %collective-permute-start.28 = (bf16[512,640]{0,1:T(8,128)(2,1)}, bf16[512,640]{0,1:T(8,128)(2,1)}, u32[]{:S(2)}, u32[]{:S(2)}) collective-permute-start(bf16[512,640]{0,1:T(8,128)(2,1)} %pad_maximum_fusion.16), channel_id=1, source_target_pairs={{0,1},{1,0},{2,3},{3,2},{4,5},{5,4},{6,7},{7,6},{8,9},{9,8},{10,11... | collective-permute-start | bytes 1966088 | tf_op jit(solution)/shard_map/ppermute | solution.py:242
  899.2 27.6 %collective-permute-start.30 = (bf16[512,640]{0,1:T(8,128)(2,1)}, bf16[512,640]{0,1:T(8,128)(2,1)}, u32[]{:S(2)}, u32[]{:S(2)}) collective-permute-start(bf16[512,640]{0,1:T(8,128)(2,1)} %fusion.30), channel_id=1, source_target_pairs={{0,2},{1,3},{2,0},{3,1},{4,6},{5,7},{6,4},{7,5},{8,10},{9,11},{10,... | collective-permute-start | bytes 1966088 | tf_op jit(solution)/shard_map/ppermute | solution.py:242
  910.3 21.0 %all-to-all-start.8 = ((bf16[8,64,576]{2,1,0:T(8,128)(2,1)}), bf16[8,64,576]{2,1,0:T(8,128)(2,1)}, u32[]{:S(2)}, u32[]{:S(2)}) async-start(bf16[8,64,576]{2,1,0:T(8,128)(2,1)} %bitcast.277), calls=%async_computation.10 | async-start | bytes 1310720 | tf_op jit(solution)/shard_map/all_to_all | solution.py:292
  931.3 20.4 %all-to-all-start.7 = ((bf16[8,64,640]{2,1,0:T(8,128)(2,1)}), bf16[8,64,640]{2,1,0:T(8,128)(2,1)}, u32[]{:S(2)}, u32[]{:S(2)}) async-start(bf16[8,64,640]{2,1,0:T(8,128)(2,1)} %bitcast.76), calls=%async_computation.9 | async-start | bytes 1310720 | tf_op jit(solution)/shard_map/all_to_all | solution.py:292
  (112 other events, 1583.7 us)
Sparse Core Ops, SparseCore 0:
  10.1 93.2 all-gather.14
  123.8 106.1 all-gather.6
  232.7 72.3 all-gather.8
  321.2 74.3 all-gather.10
  479.7 147.2 reduce-scatter.2
  644.3 100.6 all-gather.12
  802.2 89.3 reduce-scatter.4

commit v6 on v5

--- a/solution.py
+++ b/solution.py
@@ -266,18 +266,26 @@
     return rel[0].astype(jnp.float32) + near[0] + far.astype(jnp.float32)
 
 
-def fsdp_reduce_terms(term, kind):
-    near = [fsdp_swap(term(k).astype(kind), 1).astype(jnp.float32) for k in (1, 3)]
-    far = fsdp_swap((term(2) + near[1]).astype(kind), 2)
-    return term(0) + near[0] + far.astype(jnp.float32)
+def fsdp_reduce_terms(term):
+    send = term(3)
+    near = fsdp_swap(send, 1)
+    far = fsdp_swap(term(2, near), 2)
+    return send, term(0, fsdp_swap(term(1), 1), far)
 
 
 def columns_by_distance(values, n_ctx, rank):
     rows = values.shape[0]
     split = values.reshape(rows, n_ctx, 4, -1)
-    return [
+    parts = [
         lax.dynamic_index_in_dim(split, rank ^ k, 2, False).reshape(rows, -1) for k in range(4)
     ]
+    return jnp.concatenate(parts, -1)
+
+
+def columns_in_order(values, n_ctx, rank):
+    rows = values.shape[0]
+    split = swap_chunks(values.reshape(rows, 4, n_ctx, -1), rank, 1)
+    return split.transpose(0, 2, 1, 3).reshape(rows, -1)
 
 
 def ctx_gather(values):
@@ -559,6 +567,42 @@
     )(left, right, *more, *each)
 
 
+def head_terms_body(*refs):
+    normed_ref, query_ref, resid_ref, heads_ref, *more, out_ref = refs
+    total = jnp.concatenate(
+        [
+            dot_f32(normed_ref[...], query_ref[...], ((0,), (0,))),
+            dot_f32(resid_ref[...], heads_ref[...], ((0,), (0,))),
+        ],
+        -1,
+    )
+    for ref in more:
+        total = total + ref[...].astype(jnp.float32)
+    out_ref[...] = total.astype(jnp.bfloat16)
+
+
+def head_terms_call(k, normed, query_grad, resid, heads_out, *more):
+    length, columns = normed.shape
+    width = query_grad.shape[1] + heads_out.shape[1]
+    columns = columns // 4
+    whole = lambda i: (0, 0)
+    block = pl.BlockSpec((columns, width), whole)
+    return pl.pallas_call(
+        head_terms_body,
+        grid=(1,),
+        in_specs=[
+            pl.BlockSpec((length, columns), lambda i: (0, k)),
+            pl.BlockSpec(query_grad.shape, whole),
+            pl.BlockSpec((length, columns), lambda i: (0, k)),
+            pl.BlockSpec(heads_out.shape, whole),
+        ]
+        + [block] * len(more),
+        out_specs=block,
+        out_shape=jax.ShapeDtypeStruct((columns, width), jnp.bfloat16),
+        compiler_params=pltpu.CompilerParams(vmem_limit_bytes=VMEM_BYTES),
+    )(normed, query_grad, resid, heads_out, *more)
+
+
 def combine_body(
     pick_ref, both_ref, act_ref, in_ref, out_ref, gate_up_ref, down_ref, total_ref, *, blocks
 ):
@@ -838,26 +882,23 @@
         got = ctx_exchange(jnp.concatenate([query_send, latent_send], -1))
         got = after(got, early[:2])
         pieces = fsdp_pieces(jnp.concatenate([got, w_expand.reshape(n_ctx, rows, -1)], -1))
-        full = whole_rows(pieces, rank)
+        full = jnp.concatenate([p.reshape(n_ctx * rows, -1) for p in pieces], 0)
         query_full = full[:, :q_wide]
         latent_full = full[:, q_wide : q_wide + KVL + DR]
-        expand_full = (
-            full[:, q_wide + KVL + DR :]
-            .reshape(n_ctx, 4, rows, -1)
-            .transpose(0, 2, 1, 3)
-            .reshape(KVL, -1)
-        )
+        expand_full = full[:, q_wide + KVL + DR :].reshape(4, KVL, -1)
+        expand_full = swap_chunks(expand_full, rank, 0).transpose(1, 0, 2).reshape(KVL, -1)
         expand_heads = expand_full.reshape(KVL, heads, DN + DV)
         key_up = expand_heads[:, :, :DN].transpose(1, 0, 2)
         value_up = expand_heads[:, :, DN:].transpose(1, 0, 2)
 
-        hidden_all = after(ctx_gather(hidden_bf), full)
+        hidden_all = after(ctx_gather(columns_by_distance(hidden_bf, n_ctx, rank)), full)
         output_full = lax.all_gather(
             after(w_output, hidden_all), ("ctx", "fsdp"), axis=1, tiled=True
         )
         hidden_f = hidden_all.astype(jnp.float32)
         cos_table, sin_table = rope_tables(where_all, DR)
-        normed_all, inv_all = norm_forward(hidden_f, gain_in)
+        gain_cols = columns_by_distance(gain_in[None], n_ctx, rank)[0]
+        normed_all, inv_all = norm_forward(hidden_f, gain_cols)
         normed_bf = normed_all.astype(jnp.bfloat16)
         query_all = dot_f32(normed_bf, query_full)
         compressed = dot_f32(normed_bf, latent_full)
@@ -891,36 +932,33 @@
         normed_bf = saved["normed_bf"]
         heads_grad = dot_f32(resid_bf, saved["output_full"], ((1,), (1,))).astype(jnp.bfloat16)
         heads_grad = ctx_exchange(columns_by_dest(heads_grad, n_ctx)).reshape(length, heads * DV)
-        resid_all = ctx_gather(resid_bf)
+        resid_all = ctx_gather(columns_by_distance(resid_bf, n_ctx, rank))
         nope_grad, rot_grad, expand_g, lat_total, rot_total = attention_backward_call(
             heads_grad, saved["nope"], saved["rot"], saved["mixed"], saved["log_total"],
             saved["latent"], saved["key_rot"], saved["key_up"], saved["value_up"], where_all,
             score_scale,
         )
-        key_terms = jnp.concatenate([lat_total, rot_total], -1).astype(jnp.bfloat16)
-        key_sent = ctx_exchange(key_terms.reshape(n_ctx, tok_dev, KVL + DR))
         rot_grads = [
             rope_back(rot_grad[j], cos_table, sin_table).astype(jnp.bfloat16) for j in range(heads)
         ]
         query_grad = jnp.concatenate([nope_grad, *rot_grads], -1)
-        key_got = after(key_sent, resid_all, stages)
         in_part = dot_f32(query_grad, query_full, ((1,), (1,))).astype(jnp.bfloat16)
         in_grad = ctx_scatter(in_part)
+        key_terms = jnp.concatenate([lat_total, rot_total], -1).astype(jnp.bfloat16)
+        key_terms = after(key_terms.reshape(n_ctx, tok_dev, KVL + DR), in_part, stages)
+        key_sent = ctx_exchange(key_terms)
+        key_got = after(key_sent, resid_all)
         gain_in_grad = jnp.sum(
             in_part.astype(jnp.float32)
             * (saved["hidden_all"].astype(jnp.float32) * saved["inv_all"]),
             0,
         )
-        normed_cols = columns_by_distance(normed_bf, n_ctx, rank)
-        resid_cols = columns_by_distance(resid_all, n_ctx, rank)
         query_late = after(query_grad, key_got)
 
-        def head_terms(k):
-            query_term = dot_f32(normed_cols[k], query_late, ((0,), (0,)))
-            output_term = dot_f32(resid_cols[k], saved["heads_out"], ((0,), (0,)))
-            return jnp.concatenate([query_term, output_term], -1)
-
-        head_sums = fsdp_reduce_terms(head_terms, jnp.bfloat16).astype(jnp.bfloat16)
+        def head_terms(k, *more):
+            return head_terms_call(k, normed_bf, query_late, resid_all, saved["heads_out"], *more)
+
+        head_sums = fsdp_reduce_terms(head_terms)[1]
         head_sums = ctx_exchange(head_sums.reshape(n_ctx, rows, -1))
         query_terms = head_sums[:, :, :q_wide].astype(jnp.float32)
         output_w = head_sums[:, :, q_wide:].astype(jnp.float32)
@@ -933,16 +971,21 @@
         compressed_grad = jnp.concatenate(
             [lat_in_grad, rope_back(key_sum[:, KVL:], own_cos, own_sin)], -1
         ).astype(jnp.bfloat16)
-        own_cols = columns_by_distance(own_rows(normed_bf), n_ctx, rank)
-        latent_w = fsdp_reduce_terms(
-            lambda k: dot_f32(own_cols[k], compressed_grad, ((0,), (0,))), jnp.bfloat16
-        )
-        latent_w = latent_w.astype(jnp.bfloat16)
+        own_normed = own_rows(normed_bf)[None]
+
+        def latent_terms(k, *more):
+            return expert_grad_call(
+                own_normed, compressed_grad[None], (D // 4, k), (KVL + DR, 0), jnp.bfloat16, *more
+            )
+
+        latent_sent, latent_w = fsdp_reduce_terms(latent_terms)
         latent_w = ctx_exchange(latent_w.reshape(n_ctx, rows, KVL + DR))
         latent_w = jnp.sum(after(latent_w, in_grad).astype(jnp.float32), 0)
         inv_in = own_rows(saved["inv_all"])
         in_own = dot_f32(compressed_grad, latent_full, ((1,), (1,)))
-        gain_in_grad = gain_in_grad + jnp.sum(in_own * (tokens * inv_in), 0)
+        token_cols = columns_by_distance(tokens, n_ctx, rank)
+        gain_in_grad = gain_in_grad + jnp.sum(in_own * (token_cols * inv_in), 0)
+        gain_in_grad = columns_in_order(gain_in_grad[None], n_ctx, rank)[0]
         gains_grad = reduce_gains(gain_in_grad, gain_lat_grad)
         expand_g = expand_g.transpose(1, 0, 2)
         expand_blocks = expand_g.reshape(KVL, 4, -1).transpose(1, 0, 2).astype(jnp.bfloat16)
@@ -951,8 +994,10 @@
         rot_w = query_terms[:, :, n_wide:].reshape(n_ctx, rows, heads, DR)
         query_w = jnp.concatenate([nope_w, rot_w], -1).transpose(1, 0, 2, 3).reshape(rows, -1)
         in_grad = after(in_grad, gains_grad).astype(jnp.float32) + in_own
-        token_grad = norm_backward(tokens, inv_in, gain_in, in_grad)[0]
-        return token_grad, (lat_total, key_sent, head_sums), gains_grad, query_w, latent_w, expand_w, output_w
+        token_grad = norm_backward(token_cols, inv_in, saved["gain_cols"], in_grad)[0]
+        token_grad = columns_in_order(token_grad, n_ctx, rank)
+        stage = (lat_total, key_sent, latent_sent)
+        return token_grad, stage, gains_grad, query_w, latent_w, expand_w, output_w
 
     return first, middle, backward
 

time: 993 us -> 988 us (level)
  blocking collectives: 74.1 us -> 31 us
  local copies, waits for them, and re-layouts: 136 us -> 153 us
  matrix products: 75 us -> 58.6 us
  waiting for transfers between devices: 364 us -> 380 us
  Pallas kernels: 163 us -> 176 us
    all_to_all x8 -> x9, waiting for transfers between devices: 32.4 us -> 86.8 us  [ctx_exchange(): lax.all_to_all(values, 'ctx', split_axis=0, concat_axis=0, tiled=True)]
    all_to_all x2 -> x1, blocking collectives: 74.1 us -> 31 us  [ctx_exchange(): lax.all_to_all(values, 'ctx', split_axis=0, concat_axis=0, tiled=True)]
    ppermute x40, waiting for transfers between devices: 301 us -> 264 us  [fsdp_swap(): lax.ppermute(values, 'fsdp', [(at, at ^ distance) for at in range(count)])]
    unnamed x229 -> x216, local copies, waits for them, and re-layouts: 35.3 us -> 54 us
    dot_general x24 -> x12, matrix products: 75 us -> 58.6 us  [dot_f32(): lax.dot_general(left, right, (dims, ((), ())), preferred_element_type=jnp...]
    pallas_call x0 -> x4, Pallas kernels: none -> 12.6 us  [head_terms_call(): pl.pallas_call(head_terms_body, grid=(1,), in_specs=[pl.BlockSpec((length...]
    all_to_all x8 -> x9, starting transfers between devices: 39.3 us -> 47.4 us  [ctx_exchange(): lax.all_to_all(values, 'ctx', split_axis=0, concat_axis=0, tiled=True)]
    pallas_call x9 -> x13, Pallas kernels: 56.4 us -> 56.8 us  [expert_grad_call(): pl.pallas_call(functools.partial(expert_grad_body, each=len(each)), grid=...]
  transfers between devices with their start and end apart: 55 -> 56, of which waited for: 20 -> 18; matrix products, arithmetic and copies ran while one was open for 28% -> 25% of each run, Pallas kernels for 8% -> 11%
where the time goes in v6:
time: 988 us; the launch traced here: 977 us
  waiting for transfers between devices  380 us (38%)
  Pallas kernels  176 us (18%)
  local copies, waits for them, and re-layouts  153 us (15%)
  other arithmetic  92.4 us (9%)
  starting transfers between devices  69.7 us (7%)
  matrix products  58.6 us (6%)
  blocking collectives  31 us (3%)
  between operations  16.4 us (2%)
    ppermute x40, waiting for transfers between devices, fsdp_swap(): lax.ppermute(values, 'fsdp', [(at, at ^ distance) for at in range(count)])  264 us
    all_to_all x9, waiting for transfers between devices, ctx_exchange(): lax.all_to_all(values, 'ctx', split_axis=0, concat_axis=0, tiled=True)  86.8 us
    dot_general x12, matrix products, dot_f32(): lax.dot_general(left, right, (dims, ((), ())), preferred_element_type=jnp...  58.6 us
    pallas_call x13, Pallas kernels, expert_grad_call(): pl.pallas_call(functools.partial(expert_grad_body, each=len(each)), grid=...  56.8 us
    unnamed x216, local copies, waits for them, and re-layouts  54 us
    pallas_call x1, Pallas kernels, experts_call(): pl.pallas_call(experts_body, grid=(count,), in_specs=[pl.BlockSpec((1, sl...  48.8 us
    all_to_all x9, starting transfers between devices, ctx_exchange(): lax.all_to_all(values, 'ctx', split_axis=0, concat_axis=0, tiled=True)  47.4 us
    all_to_all x1, blocking collectives, ctx_exchange(): lax.all_to_all(values, 'ctx', split_axis=0, concat_axis=0, tiled=True)  31 us
  transfers between devices with their start and end apart: 56, of which 18 were waited for; matrix products, arithmetic and copies ran while one was open for 25% of the time, Pallas kernels for 11%

profile of v6, /device:TPU:0, one launch (start us, length us, event | category | flops | bytes accessed | tf_op | source)
XLA Modules:
  0.0 977.0 jit_solution(1682328733309977386)
XLA Ops:
  12.8 7.3 all-to-all-start
  20.1 5.0 fusion.123
  27.2 32.5 %collective-permute-done = bf16[2,128,2816]{2,1,0:T(8,128)(2,1)S(1)} collective-permute-done((bf16[2,128,2816]{2,1,0:T(8,128)(2,1)S(1)}, bf16[2,128,2816]{2,1,0:T(8,128)(2,1)S(1)}, u32[]{:S(2)}, u32[]{:S(2)}) %collective-permute-start) | collective-permute-done | bytes 1441824 | tf_op jit(solution)/shard_map/ppermute | solution.py:242
  60.8 28.3 %collective-permute-done.1 = bf16[2,128,2816]{2,1,0:T(8,128)(2,1)} collective-permute-done((bf16[2,128,2816]{2,1,0:T(8,128)(2,1)S(1)}, bf16[2,128,2816]{2,1,0:T(8,128)(2,1)}, u32[]{:S(2)}, u32[]{:S(2)}) %collective-permute-start.1) | collective-permute-done | bytes 1441824 | tf_op jit(solution)/shard_map/ppermute | solution.py:242
  90.9 25.0 %collective-permute-done.3 = bf16[8,64,1088]{2,1,0:T(8,128)(2,1)S(1)} collective-permute-done((bf16[8,64,1088]{2,1,0:T(8,128)(2,1)S(1)}, bf16[8,64,1088]{2,1,0:T(8,128)(2,1)S(1)}, u32[]{:S(2)}, u32[]{:S(2)}) %collective-permute-start.3) | collective-permute-done | bytes 1114144 | tf_op jit(solution)/shard_map/ppermute | solution.py:242
  131.4 5.7 constant_dynamic-update-slice_fusion.9
  139.3 5.6 constant_dynamic-update-slice_fusion.8
  144.9 5.4 all-to-all-start.2
  157.4 6.1 fusion.25
  173.4 13.8 %shard_map.212 = (bf16[1024,256]{1,0:T(8,128)(2,1)S(1)}, f32[2,1024,512]{2,1,0:T(8,128)}, f32[2,1024,1]{2,1,0:T(8,128)S(1)}) custom-call(bf16[1024,256]{1,0:T(8,128)(2,1)S(1)} %slice.318.nope_ref, bf16[2,1024,64]{2,1,0:T(8,128)(2,1)S(1)} %pad_maximum_fusion.18.rot_ref, bf16[1024,512]{1,0:T(8,128)(2,1)} %multiply_convert_fusion.1.lat_ref, ...), custom_call_target="tpu_custom_call" | custom-call | tf_op jit(solution)/shard_map/pallas_call | solution.py:406
  190.8 4.2 all-to-all-start.1
  203.7 20.8 %all-to-all-done.1 = bf16[8,128,256]{1,2,0:T(8,128)(2,1)} async-done(((bf16[8,128,256]{1,2,0:T(8,128)(2,1)}), bf16[8,128,256]{1,2,0:T(8,128)(2,1)}, u32[]{:S(2)}, u32[]{:S(2)}) %all-to-all-start.1) | async-done | bytes 524320 | tf_op jit(solution)/shard_map/all_to_all | solution.py:300
  237.3 7.0 multiply_reduce_fusion.5
  246.3 49.8 %collective-permute-done.9 = bf16[2,1408,512]{2,1,0:T(8,128)(2,1)} collective-permute-done((bf16[2,1408,512]{2,1,0:T(8,128)(2,1)S(1)}, bf16[2,1408,512]{2,1,0:T(8,128)(2,1)}, u32[]{:S(2)}, u32[]{:S(2)}) %collective-permute-start.9) | collective-permute-done | bytes 2883616 | tf_op jit(solution)/shard_map/ppermute | solution.py:242
  296.1 23.0 %collective-permute-done.6 = bf16[8,64,1152]{2,1,0:T(8,128)(2,1)} collective-permute-done((bf16[8,64,1152]{2,1,0:T(8,128)(2,1)}, bf16[8,64,1152]{2,1,0:T(8,128)(2,1)}, u32[]{:S(2)}, u32[]{:S(2)}) %collective-permute-start.6) | collective-permute-done | bytes 1179680 | tf_op jit(solution)/shard_map/ppermute | solution.py:242
  322.8 5.0 copy.493
  330.0 4.4 convert_bitcast_fusion
  334.3 5.4 multiply_convert_fusion
  345.4 7.0 pad_maximum_fusion.5.gate_up_ref
  357.4 8.0 pad_maximum_fusion.dn_ref
  365.4 28.5 %all-gather.12.cloned.1.call-done = bf16[1024,2048]{1,0:T(8,128)(2,1)} async-done(((bf16[128,2048]{1,0:T(8,128)(2,1)}), bf16[1024,2048]{1,0:T(8,128)(2,1)}) %all-gather.12.cloned.1.call-update) | async-done | bytes 4194320 | tf_op jit(solution)/shard_map/all_gather | solution.py:292
  393.9 6.4 fusion.130
  405.3 5.5 convolution_convert_fusion.1
  410.7 48.8 %shard_map.213 = (bf16[2,432,1408]{2,1,0:T(8,128)(2,1)}, bf16[2,432,2816]{2,1,0:T(8,128)(2,1)}, bf16[2,432,2048]{2,1,0:T(8,128)(2,1)}, bf16[2,432,2048]{2,1,0:T(8,128)(2,1)}) custom-call(bf16[2,432,2048]{2,1,0:T(8,128)(2,1)} %bitcast.213, bf16[2,432,2048]{2,1,0:T(8,128)(2,1)} %bitcast.227, f32[2,432,1]{2,1,0:T(8,128)} %copy.502.gate_ref, ...), custom_call_target="tpu_custom_call" | custom-call | tf_op jit(solution)/shard_map/pallas_call | solution.py:518
  459.5 19.0 %shard_map.214 = bf16[1024,4096]{1,0:T(8,128)(2,1)} custom-call(bf16[1024,864]{1,0:T(8,128)(2,1)} %get-tuple-element.133.pick_ref, bf16[1024,768]{1,0:T(8,128)(2,1)S(1)} %pad_maximum_fusion.9.both_ref, bf16[1024,384]{1,0:T(8,128)(2,1)S(1)} %get-tuple-element.159.act_ref, bf16[864,2048]{1,0:T(8,128)(2,1)} %bitcast.244, bf16[864,2048]{1,0:T(8,128)(2,1)} %bitcast.243, ...), custom_call_target="tpu_custom_call" | custom-call | tf_op jit(solution)/shard_map/pallas_call | solution.py:629
  480.3 4.6 shard_map.215
  484.9 7.6 shard_map.216
  493.0 12.8 %collective-permute-done.19.refs_2_ = bf16[2,1408,512]{2,1,0:T(8,128)(2,1)} collective-permute-done((bf16[2,1408,512]{2,1,0:T(8,128)(2,1)S(1)}, bf16[2,1408,512]{2,1,0:T(8,128)(2,1)}, u32[]{:S(2)}, u32[]{:S(2)}) %collective-permute-start.19) | collective-permute-done | bytes 2883616 | tf_op jit(solution)/shard_map/ppermute | solution.py:242
  505.8 4.6 shard_map.217
  520.4 5.2 shard_map.218
  526.4 49.6 %collective-permute-done.21.refs_3_ = bf16[2,1408,512]{2,1,0:T(8,128)(2,1)} collective-permute-done((bf16[2,1408,512]{2,1,0:T(8,128)(2,1)}, bf16[2,1408,512]{2,1,0:T(8,128)(2,1)}, u32[]{:S(2)}, u32[]{:S(2)}) %collective-permute-start.21) | collective-permute-done | bytes 2883616 | tf_op jit(solution)/shard_map/ppermute | solution.py:242
  585.0 6.8 copy.503
  600.5 36.6 %collective-permute-done.20.refs_3_ = bf16[1,512,2816]{2,1,0:T(8,128)(2,1)S(1)} collective-permute-done((bf16[1,512,2816]{2,1,0:T(8,128)(2,1)}, bf16[1,512,2816]{2,1,0:T(8,128)(2,1)S(1)}, u32[]{:S(2)}, u32[]{:S(2)}) %collective-permute-start.20) | collective-permute-done | bytes 2883616 | tf_op jit(solution)/shard_map/ppermute | solution.py:242
  646.6 4.6 convolution_convert_fusion.2
  651.3 31.0 %all_to_all.54 = bf16[8,128,256]{2,1,0:T(8,128)(2,1)S(1)} all-to-all(bf16[8,128,256]{2,1,0:T(8,128)(2,1)S(1)} %bitcast.250), channel_id=1, replica_groups=mesh['ctx'=8,'fsdp'=4] {'ctx'}, dimensions={0} | all-to-all | bytes 1048576 | tf_op jit(solution)/shard_map/all_to_all | solution.py:300
  682.3 24.8 %shard_map.220 = (bf16[1024,256]{1,0:T(8,128)(2,1)S(1)}, f32[2,1024,64]{2,1,0:T(8,128)}, f32[2,512,256]{2,1,0:T(8,128)}, f32[1024,512]{1,0:T(8,128)}, f32[1024,64]{1,0:T(8,128)S(1)}) custom-call(bf16[1024,256]{1,0:T(8,128)(2,1)S(1)} %bitcast.226, bf16[1024,256]{1,0:T(8,128)(2,1)S(1)} %copy-done.20, bf16[2,1024,64]{2,1,0:T(8,128)(2,1)S(1)} %copy-done.18, ...), custom_call_target="tpu_custom_call" | custom-call | tf_op jit(solution)/shard_map/pallas_call | solution.py:441
  714.5 6.9 fusion.3
  730.5 4.3 all-to-all-start.5
  734.8 7.4 shard_map.229
  742.2 46.5 %all-to-all-done.5 = bf16[8,128,576]{1,2,0:T(8,128)(2,1)} async-done(((bf16[8,128,576]{1,2,0:T(8,128)(2,1)}), bf16[8,128,576]{1,2,0:T(8,128)(2,1)}, u32[]{:S(2)}, u32[]{:S(2)}) %all-to-all-start.5) | async-done | bytes 1179680 | tf_op jit(solution)/shard_map/all_to_all | solution.py:300
  802.4 4.3 shard_map.231
  815.3 7.0 all-to-all-start.9
  832.4 4.2 multiply_reduce_fusion.3
  907.6 6.3 all-to-all-start.8
  916.4 5.7 shard_map.232
  922.1 11.9 %shard_map.230 = f32[2,512,2816]{2,1,0:T(8,128)} custom-call(bf16[2,432,2048]{2,1,0:T(8,128)(2,1)} %bitcast.216, bf16[2,432,2816]{2,1,0:T(8,128)(2,1)} %get-tuple-element.90.refs_1_, bf16[2,512,2816]{2,1,0:T(8,128)(2,1)} %collective-permute-done.38.refs_2_, bf16[1,512,2816]{2,1,0:T(8,128)(2,1)S(1)} %copy-done.22, ...), custom_call_target="tpu_custom_call" | custom-call | tf_op jit(solution)/shard_map/pallas_call | solution.py:555
  940.4 6.0 all-to-all-start.7
  952.3 11.4 %all-to-all-done.7 = bf16[8,64,640]{2,1,0:T(8,128)(2,1)} async-done(((bf16[8,64,640]{2,1,0:T(8,128)(2,1)}), bf16[8,64,640]{2,1,0:T(8,128)(2,1)}, u32[]{:S(2)}, u32[]{:S(2)}) %all-to-all-start.7) | async-done | bytes 655392 | tf_op jit(solution)/shard_map/all_to_all | solution.py:300
  (519 shorter events, 273.3 us)
Async XLA Ops:
  7.2 115.5 %all-gather.6.cloned.1.call-start = ((), (), s32[]{:S(2)}) async-start(), calls=%async_computation.12 | async-start | bytes 4718592 | tf_op jit(solution)/shard_map/all_gather | solution.py:292
  12.8 76.4 %all-to-all-start = ((bf16[8,64,960]{2,1,0:T(8,128)(2,1)}), bf16[8,64,960]{2,1,0:T(8,128)(2,1)S(1)}, u32[]{:S(2)}, u32[]{:S(2)}) async-start(bf16[8,64,960]{2,1,0:T(8,128)(2,1)} %pad_maximum_fusion.13), calls=%async_computation | async-start | bytes 2097152 | tf_op jit(solution)/shard_map/all_to_all | solution.py:300
  20.1 217.2 %all-gather.8.cloned.1.call-start = ((), (), s32[]{:S(2)}) async-start(), calls=%async_computation.13 | async-start | bytes 8650752 | tf_op jit(solution)/shard_map/all_gather | solution.py:895
  25.2 34.5 %collective-permute-start = (bf16[2,128,2816]{2,1,0:T(8,128)(2,1)S(1)}, bf16[2,128,2816]{2,1,0:T(8,128)(2,1)S(1)}, u32[]{:S(2)}, u32[]{:S(2)}) collective-permute-start(bf16[2,128,2816]{2,1,0:T(8,128)(2,1)S(1)} %get-tuple-element.140), channel_id=1, source_target_pairs={{0,2},{1,3},{2,0},{3,1},{4,6},{5,7},{6,4},{7,5},{8,10},{9,11},{10,... | collective-permute-start | bytes 4325384 | tf_op jit(solution)/shard_map/ppermute | solution.py:242
  26.6 62.6 %collective-permute-start.1 = (bf16[2,128,2816]{2,1,0:T(8,128)(2,1)S(1)}, bf16[2,128,2816]{2,1,0:T(8,128)(2,1)}, u32[]{:S(2)}, u32[]{:S(2)}) collective-permute-start(bf16[2,128,2816]{2,1,0:T(8,128)(2,1)S(1)} %get-tuple-element.139), channel_id=1, source_target_pairs={{0,2},{1,3},{2,0},{3,1},{4,6},{5,7},{6,4},{7,5},{8,10},{9,11},{10,... | collective-permute-start | bytes 4325384 | tf_op jit(solution)/shard_map/ppermute | solution.py:242
  89.4 26.5 %collective-permute-start.3 = (bf16[8,64,1088]{2,1,0:T(8,128)(2,1)S(1)}, bf16[8,64,1088]{2,1,0:T(8,128)(2,1)S(1)}, u32[]{:S(2)}, u32[]{:S(2)}) collective-permute-start(bf16[8,64,1088]{2,1,0:T(8,128)(2,1)S(1)} %pad_maximum_fusion.11), channel_id=1, source_target_pairs={{0,2},{1,3},{2,0},{3,1},{4,6},{5,7},{6,4},{7,5},{8,10},{9,11},{10,... | collective-permute-start | bytes 3342344 | tf_op jit(solution)/shard_map/ppermute | solution.py:242
  90.9 25.0 %collective-permute-start.2 = (bf16[8,64,1088]{2,1,0:T(8,128)(2,1)S(1)}, bf16[8,64,1088]{2,1,0:T(8,128)(2,1)S(1)}, u32[]{:S(2)}, u32[]{:S(2)}) collective-permute-start(bf16[8,64,1088]{2,1,0:T(8,128)(2,1)S(1)} %pad_maximum_fusion.11), channel_id=1, source_target_pairs={{0,1},{1,0},{2,3},{3,2},{4,5},{5,4},{6,7},{7,6},{8,9},{9,8},{10,11... | collective-permute-start | bytes 3342344 | tf_op jit(solution)/shard_map/ppermute | solution.py:242
  122.8 16.5 %collective-permute-start.10 = (bf16[2,512,2816]{2,1,0:T(8,128)(2,1)}, bf16[2,512,2816]{2,1,0:T(8,128)(2,1)}, u32[]{:S(2)}, u32[]{:S(2)}) collective-permute-start(bf16[2,512,2816]{2,1,0:T(8,128)(2,1)} %param.22), channel_id=1, source_target_pairs={{0,1},{1,0},{2,3},{3,2},{4,5},{5,4},{6,7},{7,6},{8,9},{9,8},{10,11... | collective-permute-start | bytes 17301512 | tf_op jit(solution)/shard_map/ppermute | solution.py:242
  123.0 77.4 %collective-permute-start.8 = (bf16[2,128,2816]{2,1,0:T(8,128)(2,1)}, bf16[2,128,2816]{2,1,0:T(8,128)(2,1)}, u32[]{:S(2)}, u32[]{:S(2)}) collective-permute-start(bf16[2,128,2816]{2,1,0:T(8,128)(2,1)} %get-tuple-element.138), channel_id=1, source_target_pairs={{0,2},{1,3},{2,0},{3,1},{4,6},{5,7},{6,4},{7,5},{8,10},{9,11},{10,... | collective-permute-start | bytes 4325384 | tf_op jit(solution)/shard_map/ppermute | solution.py:242
  124.5 103.5 %collective-permute-start.11 = (bf16[2,128,2816]{2,1,0:T(8,128)(2,1)}, bf16[2,128,2816]{2,1,0:T(8,128)(2,1)}, u32[]{:S(2)}, u32[]{:S(2)}) collective-permute-start(bf16[2,128,2816]{2,1,0:T(8,128)(2,1)} %get-tuple-element.137), channel_id=1, source_target_pairs={{0,2},{1,3},{2,0},{3,1},{4,6},{5,7},{6,4},{7,5},{8,10},{9,11},{10,... | collective-permute-start | bytes 4325384 | tf_op jit(solution)/shard_map/ppermute | solution.py:242
  125.0 232.4 %collective-permute-start.16 = (bf16[2,1408,512]{2,1,0:T(8,128)(2,1)}, bf16[2,1408,512]{2,1,0:T(8,128)(2,1)}, u32[]{:S(2)}, u32[]{:S(2)}) collective-permute-start(bf16[2,1408,512]{2,1,0:T(8,128)(2,1)} %param.23), channel_id=1, source_target_pairs={{0,1},{1,0},{2,3},{3,2},{4,5},{5,4},{6,7},{7,6},{8,9},{9,8},{10,11... | collective-permute-start | bytes 8650760 | tf_op jit(solution)/shard_map/ppermute | solution.py:242
  144.9 45.9 %all-to-all-start.2 = ((bf16[8,64,1152]{2,1,0:T(8,128)(2,1)}), bf16[8,64,1152]{2,1,0:T(8,128)(2,1)}, u32[]{:S(2)}, u32[]{:S(2)}) async-start(bf16[8,64,1152]{2,1,0:T(8,128)(2,1)} %fusion.32), calls=%async_computation.2 | async-start | bytes 2359296 | tf_op jit(solution)/shard_map/all_to_all | solution.py:300
  150.3 168.8 %all-gather.10.cloned.1.call-start = ((), (), s32[]{:S(2)}) async-start(), calls=%async_computation.14 | async-start | bytes 4718592 | tf_op jit(solution)/shard_map/all_gather | solution.py:292
  190.8 33.7 %all-to-all-start.1 = ((bf16[8,128,256]{1,2,0:T(8,128)(2,1)}), bf16[8,128,256]{1,2,0:T(8,128)(2,1)}, u32[]{:S(2)}, u32[]{:S(2)}) async-start(bf16[8,128,256]{1,2,0:T(8,128)(2,1)} %copy.486), calls=%async_computation.1 | async-start | bytes 1048576 | tf_op jit(solution)/shard_map/all_to_all | solution.py:300
  227.9 166.0 %all-gather.12.cloned.1.call-start = ((), (), s32[]{:S(2)}) async-start(), calls=%async_computation.15 | async-start | bytes 4718592 | tf_op jit(solution)/shard_map/all_gather | solution.py:292
  230.6 65.5 %collective-permute-start.9 = (bf16[2,1408,512]{2,1,0:T(8,128)(2,1)S(1)}, bf16[2,1408,512]{2,1,0:T(8,128)(2,1)}, u32[]{:S(2)}, u32[]{:S(2)}) collective-permute-start(bf16[2,1408,512]{2,1,0:T(8,128)(2,1)S(1)} %copy-done.48), channel_id=1, source_target_pairs={{0,2},{1,3},{2,0},{3,1},{4,6},{5,7},{6,4},{7,5},{8,10},{9,11},{10,... | collective-permute-start | bytes 8650760 | tf_op jit(solution)/shard_map/ppermute | solution.py:242
  232.0 87.0 %collective-permute-start.6 = (bf16[8,64,1152]{2,1,0:T(8,128)(2,1)}, bf16[8,64,1152]{2,1,0:T(8,128)(2,1)}, u32[]{:S(2)}, u32[]{:S(2)}) collective-permute-start(bf16[8,64,1152]{2,1,0:T(8,128)(2,1)} %all-to-all-done.2), channel_id=1, source_target_pairs={{0,2},{1,3},{2,0},{3,1},{4,6},{5,7},{6,4},{7,5},{8,10},{9,11},{10,... | collective-permute-start | bytes 3538952 | tf_op jit(solution)/shard_map/ppermute | solution.py:242
  232.6 107.7 %collective-permute-start.5 = (bf16[8,64,1152]{2,1,0:T(8,128)(2,1)}, bf16[8,64,1152]{2,1,0:T(8,128)(2,1)}, u32[]{:S(2)}, u32[]{:S(2)}) collective-permute-start(bf16[8,64,1152]{2,1,0:T(8,128)(2,1)} %all-to-all-done.2), channel_id=1, source_target_pairs={{0,1},{1,0},{2,3},{3,2},{4,5},{5,4},{6,7},{7,6},{8,9},{9,8},{10,11... | collective-permute-start | bytes 3538952 | tf_op jit(solution)/shard_map/ppermute | solution.py:242
  319.1 318.0 %reduce-scatter.3.cloned.1.call-start = ((), (), s32[]{:S(2)}) async-start(), calls=%async_computation.16 | async-start | bytes 9437184 | tf_op jit(solution)/shard_map/reduce_scatter | solution.py:296
  340.1 13.5 %collective-permute-start.13 = (bf16[2,128,2816]{2,1,0:T(8,128)(2,1)}, bf16[2,128,2816]{2,1,0:T(8,128)(2,1)S(1)}, u32[]{:S(2)}, u32[]{:S(2)}) collective-permute-start(bf16[2,128,2816]{2,1,0:T(8,128)(2,1)} %collective-permute-done.1), channel_id=1, source_target_pairs={{0,1},{1,0},{2,3},{3,2},{4,5},{5,4},{6,7},{7,6},{8,9},{9,8},{10,11... | collective-permute-start | bytes 4325384 | tf_op jit(solution)/shard_map/ppermute | solution.py:242
  340.3 14.5 %collective-permute-start.14 = (bf16[2,128,2816]{2,1,0:T(8,128)(2,1)}, bf16[2,128,2816]{2,1,0:T(8,128)(2,1)S(1)}, u32[]{:S(2)}, u32[]{:S(2)}) collective-permute-start(bf16[2,128,2816]{2,1,0:T(8,128)(2,1)} %collective-permute-done.8), channel_id=1, source_target_pairs={{0,1},{1,0},{2,3},{3,2},{4,5},{5,4},{6,7},{7,6},{8,9},{9,8},{10,11... | collective-permute-start | bytes 4325384 | tf_op jit(solution)/shard_map/ppermute | solution.py:242
  340.6 16.7 %collective-permute-start.17 = (bf16[2,1408,512]{2,1,0:T(8,128)(2,1)}, bf16[2,1408,512]{2,1,0:T(8,128)(2,1)S(1)}, u32[]{:S(2)}, u32[]{:S(2)}) collective-permute-start(bf16[2,1408,512]{2,1,0:T(8,128)(2,1)} %collective-permute-done.9), channel_id=1, source_target_pairs={{0,1},{1,0},{2,3},{3,2},{4,5},{5,4},{6,7},{7,6},{8,9},{9,8},{10,11... | collective-permute-start | bytes 8650760 | tf_op jit(solution)/shard_map/ppermute | solution.py:242
  344.8 11.3 %collective-permute-start.15 = (bf16[2,128,2816]{2,1,0:T(8,128)(2,1)}, bf16[2,128,2816]{2,1,0:T(8,128)(2,1)S(1)}, u32[]{:S(2)}, u32[]{:S(2)}) collective-permute-start(bf16[2,128,2816]{2,1,0:T(8,128)(2,1)} %collective-permute-done.11), channel_id=1, source_target_pairs={{0,1},{1,0},{2,3},{3,2},{4,5},{5,4},{6,7},{7,6},{8,9},{9,8},{10,11... | collective-permute-start | bytes 4325384 | tf_op jit(solution)/shard_map/ppermute | solution.py:242
  478.5 343.8 %all-gather.14.cloned.1.call-start = ((), (), s32[]{:S(2)}) async-start(), calls=%async_computation.18 | async-start | bytes 4718592 | tf_op jit(solution)/shard_map/all_gather | solution.py:292
  492.5 19.3 %collective-permute-start.18 = (bf16[2,512,2816]{2,1,0:T(8,128)(2,1)}, bf16[2,512,2816]{2,1,0:T(8,128)(2,1)S(1)}, u32[]{:S(2)}, u32[]{:S(2)}) collective-permute-start(bf16[2,512,2816]{2,1,0:T(8,128)(2,1)} %shard_map.216), channel_id=1, source_target_pairs={{0,1},{1,0},{2,3},{3,2},{4,5},{5,4},{6,7},{7,6},{8,9},{9,8},{10,11... | collective-permute-start | bytes 17301512 | tf_op jit(solution)/shard_map/ppermute | solution.py:242
  492.5 13.3 %collective-permute-start.19 = (bf16[2,1408,512]{2,1,0:T(8,128)(2,1)S(1)}, bf16[2,1408,512]{2,1,0:T(8,128)(2,1)}, u32[]{:S(2)}, u32[]{:S(2)}) collective-permute-start(bf16[2,1408,512]{2,1,0:T(8,128)(2,1)S(1)} %copy-done.47), channel_id=1, source_target_pairs={{0,1},{1,0},{2,3},{3,2},{4,5},{5,4},{6,7},{7,6},{8,9},{9,8},{10,11... | collective-permute-start | bytes 8650760 | tf_op jit(solution)/shard_map/ppermute | solution.py:242
  510.3 65.6 %collective-permute-start.21 = (bf16[2,1408,512]{2,1,0:T(8,128)(2,1)}, bf16[2,1408,512]{2,1,0:T(8,128)(2,1)}, u32[]{:S(2)}, u32[]{:S(2)}) collective-permute-start(bf16[2,1408,512]{2,1,0:T(8,128)(2,1)} %shard_map.217), channel_id=1, source_target_pairs={{0,2},{1,3},{2,0},{3,1},{4,6},{5,7},{6,4},{7,5},{8,10},{9,11},{10,... | collective-permute-start | bytes 8650760 | tf_op jit(solution)/shard_map/ppermute | solution.py:242
  525.6 111.5 %collective-permute-start.20 = (bf16[1,512,2816]{2,1,0:T(8,128)(2,1)}, bf16[1,512,2816]{2,1,0:T(8,128)(2,1)S(1)}, u32[]{:S(2)}, u32[]{:S(2)}) collective-permute-start(bf16[1,512,2816]{2,1,0:T(8,128)(2,1)} %shard_map.218), channel_id=1, source_target_pairs={{0,2},{1,3},{2,0},{3,1},{4,6},{5,7},{6,4},{7,5},{8,10},{9,11},{10,... | collective-permute-start | bytes 8650760 | tf_op jit(solution)/shard_map/ppermute | solution.py:242
  644.8 293.7 %reduce-scatter.5.cloned.1.call-start = ((), (), s32[]{:S(2)}) async-start(), calls=%async_computation.17 | async-start | bytes 4718592 | tf_op jit(solution)/shard_map/reduce_scatter | solution.py:296
  645.0 85.5 %collective-permute-start.24 = (bf16[1,512,2816]{2,1,0:T(8,128)(2,1)}, bf16[1,512,2816]{2,1,0:T(8,128)(2,1)}, u32[]{:S(2)}, u32[]{:S(2)}) collective-permute-start(bf16[1,512,2816]{2,1,0:T(8,128)(2,1)} %copy-done.23), channel_id=1, source_target_pairs={{0,2},{1,3},{2,0},{3,1},{4,6},{5,7},{6,4},{7,5},{8,10},{9,11},{10,... | collective-permute-start | bytes 8650760 | tf_op jit(solution)/shard_map/ppermute | solution.py:242
  730.5 58.2 %all-to-all-start.5 = ((bf16[8,128,576]{1,2,0:T(8,128)(2,1)}), bf16[8,128,576]{1,2,0:T(8,128)(2,1)}, u32[]{:S(2)}, u32[]{:S(2)}) async-start(bf16[8,128,576]{1,2,0:T(8,128)(2,1)} %pad_maximum_fusion.12), calls=%async_computation.7 | async-start | bytes 2359296 | tf_op jit(solution)/shard_map/all_to_all | solution.py:300
  742.2 179.9 %collective-permute-start.38 = (bf16[2,512,2816]{2,1,0:T(8,128)(2,1)}, bf16[2,512,2816]{2,1,0:T(8,128)(2,1)}, u32[]{:S(2)}, u32[]{:S(2)}) collective-permute-start(bf16[2,512,2816]{2,1,0:T(8,128)(2,1)} %shard_map.229), channel_id=1, source_target_pairs={{0,1},{1,0},{2,3},{3,2},{4,5},{5,4},{6,7},{7,6},{8,9},{9,8},{10,11... | collective-permute-start | bytes 17301512 | tf_op jit(solution)/shard_map/ppermute | solution.py:242
  788.7 23.7 %collective-permute-start.37 = (bf16[8,64,1152]{2,1,0:T(8,128)(2,1)}, bf16[8,64,1152]{2,1,0:T(8,128)(2,1)}, u32[]{:S(2)}, u32[]{:S(2)}) collective-permute-start(bf16[8,64,1152]{2,1,0:T(8,128)(2,1)} %get-tuple-element.116), channel_id=1, source_target_pairs={{0,2},{1,3},{2,0},{3,1},{4,6},{5,7},{6,4},{7,5},{8,10},{9,11},{10,... | collective-permute-start | bytes 3538952 | tf_op jit(solution)/shard_map/ppermute | solution.py:242
  806.6 109.8 %collective-permute-start.39 = (bf16[2,1408,512]{2,1,0:T(8,128)(2,1)}, bf16[2,1408,512]{2,1,0:T(8,128)(2,1)}, u32[]{:S(2)}, u32[]{:S(2)}) collective-permute-start(bf16[2,1408,512]{2,1,0:T(8,128)(2,1)} %shard_map.231), channel_id=1, source_target_pairs={{0,1},{1,0},{2,3},{3,2},{4,5},{5,4},{6,7},{7,6},{8,9},{9,8},{10,11... | collective-permute-start | bytes 8650760 | tf_op jit(solution)/shard_map/ppermute | solution.py:242
  811.9 26.4 %collective-permute-start.35 = (bf16[512,128]{1,0:T(8,128)(2,1)}, bf16[512,128]{1,0:T(8,128)(2,1)}, u32[]{:S(2)}, u32[]{:S(2)}) collective-permute-start(bf16[512,128]{1,0:T(8,128)(2,1)} %bitcast.90), channel_id=1, source_target_pairs={{0,1},{1,0},{2,3},{3,2},{4,5},{5,4},{6,7},{7,6},{8,9},{9,8},{10,11... | collective-permute-start | bytes 393224 | tf_op jit(solution)/shard_map/ppermute | solution.py:242
  812.4 28.3 %collective-permute-start.34 = (bf16[512,128]{1,0:T(8,128)(2,1)}, bf16[512,128]{1,0:T(8,128)(2,1)}, u32[]{:S(2)}, u32[]{:S(2)}) collective-permute-start(bf16[512,128]{1,0:T(8,128)(2,1)} %bitcast.88), channel_id=1, source_target_pairs={{0,1},{1,0},{2,3},{3,2},{4,5},{5,4},{6,7},{7,6},{8,9},{9,8},{10,11... | collective-permute-start | bytes 393224 | tf_op jit(solution)/shard_map/ppermute | solution.py:242
  815.3 49.9 %all-to-all-start.9 = ((bf16[8,64,1152]{2,1,0:T(8,128)(2,1)}), bf16[8,64,1152]{2,1,0:T(8,128)(2,1)}, u32[]{:S(2)}, u32[]{:S(2)}) async-start(bf16[8,64,1152]{2,1,0:T(8,128)(2,1)} %add_convert_fusion), calls=%async_computation.11 | async-start | bytes 2359296 | tf_op jit(solution)/shard_map/all_to_all | solution.py:300
  840.4 18.6 %collective-permute-start.36 = (bf16[512,128]{1,0:T(8,128)(2,1)}, bf16[512,128]{1,0:T(8,128)(2,1)}, u32[]{:S(2)}, u32[]{:S(2)}) collective-permute-start(bf16[512,128]{1,0:T(8,128)(2,1)} %add_convert_fusion.2), channel_id=1, source_target_pairs={{0,2},{1,3},{2,0},{3,1},{4,6},{5,7},{6,4},{7,5},{8,10},{9,11},{10,... | collective-permute-start | bytes 393224 | tf_op jit(solution)/shard_map/ppermute | solution.py:242
  840.7 18.5 %collective-permute-start.25 = (f32[8,144]{1,0:T(8,128)S(1)}, f32[8,144]{1,0:T(8,128)S(1)}, u32[]{:S(2)}, u32[]{:S(2)}) collective-permute-start(f32[8,144]{1,0:T(8,128)S(1)} %bitcast.286), channel_id=1, source_target_pairs={{0,1},{1,0},{2,3},{3,2},{4,5},{5,4},{6,7},{7,6},{8,9},{9,8},{10,11... | collective-permute-start | bytes 13832 | tf_op jit(solution)/shard_map/ppermute | solution.py:242
  840.7 18.8 %collective-permute-start.27 = (f32[8,144]{1,0:T(8,128)S(1)}, f32[8,144]{1,0:T(8,128)S(1)}, u32[]{:S(2)}, u32[]{:S(2)}) collective-permute-start(f32[8,144]{1,0:T(8,128)S(1)} %add.537), channel_id=1, source_target_pairs={{0,2},{1,3},{2,0},{3,1},{4,6},{5,7},{6,4},{7,5},{8,10},{9,11},{10,... | collective-permute-start | bytes 13832 | tf_op jit(solution)/shard_map/ppermute | solution.py:242
  859.0 33.6 %collective-permute-start.31 = (bf16[1,512,576]{1,2,0:T(8,128)(2,1)}, bf16[1,512,576]{1,2,0:T(8,128)(2,1)}, u32[]{:S(2)}, u32[]{:S(2)}) collective-permute-start(bf16[1,512,576]{1,2,0:T(8,128)(2,1)} %copy.526), channel_id=1, source_target_pairs={{0,1},{1,0},{2,3},{3,2},{4,5},{5,4},{6,7},{7,6},{8,9},{9,8},{10,11... | collective-permute-start | bytes 1769480 | tf_op jit(solution)/shard_map/ppermute | solution.py:242
  859.2 35.6 %collective-permute-start.29 = (bf16[512,640]{1,0:T(8,128)(2,1)}, bf16[512,640]{1,0:T(8,128)(2,1)}, u32[]{:S(2)}, u32[]{:S(2)}) collective-permute-start(bf16[512,640]{1,0:T(8,128)(2,1)} %copy-done.37), channel_id=1, source_target_pairs={{0,1},{1,0},{2,3},{3,2},{4,5},{5,4},{6,7},{7,6},{8,9},{9,8},{10,11... | collective-permute-start | bytes 1966088 | tf_op jit(solution)/shard_map/ppermute | solution.py:242
  859.5 41.4 %collective-permute-start.33 = (bf16[1,512,576]{1,2,0:T(8,128)(2,1)}, bf16[1,512,576]{1,2,0:T(8,128)(2,1)}, u32[]{:S(2)}, u32[]{:S(2)}) collective-permute-start(bf16[1,512,576]{1,2,0:T(8,128)(2,1)} %copy.529), channel_id=1, source_target_pairs={{0,2},{1,3},{2,0},{3,1},{4,6},{5,7},{6,4},{7,5},{8,10},{9,11},{10,... | collective-permute-start | bytes 1769480 | tf_op jit(solution)/shard_map/ppermute | solution.py:242
  868.7 38.9 %all-to-all-start.6 = ((f32[8,1,144]{2,1,0:T(1,128)}), f32[8,1,144]{2,1,0:T(1,128)S(1)}, u32[]{:S(2)}, u32[]{:S(2)}) async-start(f32[8,1,144]{2,1,0:T(1,128)} %all_to_all.39), calls=%async_computation.8 | async-start | bytes 16384 | tf_op jit(solution)/shard_map/all_to_all | solution.py:300
  892.7 41.9 %collective-permute-start.28 = (bf16[512,640]{1,0:T(8,128)(2,1)}, bf16[512,640]{1,0:T(8,128)(2,1)}, u32[]{:S(2)}, u32[]{:S(2)}) collective-permute-start(bf16[512,640]{1,0:T(8,128)(2,1)} %shard_map.221), channel_id=1, source_target_pairs={{0,1},{1,0},{2,3},{3,2},{4,5},{5,4},{6,7},{7,6},{8,9},{9,8},{10,11... | collective-permute-start | bytes 1966088 | tf_op jit(solution)/shard_map/ppermute | solution.py:242
  899.4 35.1 %collective-permute-start.30 = (bf16[512,640]{1,0:T(8,128)(2,1)}, bf16[512,640]{1,0:T(8,128)(2,1)}, u32[]{:S(2)}, u32[]{:S(2)}) collective-permute-start(bf16[512,640]{1,0:T(8,128)(2,1)} %shard_map.223), channel_id=1, source_target_pairs={{0,2},{1,3},{2,0},{3,1},{4,6},{5,7},{6,4},{7,5},{8,10},{9,11},{10,... | collective-permute-start | bytes 1966088 | tf_op jit(solution)/shard_map/ppermute | solution.py:242
  907.6 32.8 %all-to-all-start.8 = ((bf16[8,64,576]{2,1,0:T(8,128)(2,1)}), bf16[8,64,576]{2,1,0:T(8,128)(2,1)}, u32[]{:S(2)}, u32[]{:S(2)}) async-start(bf16[8,64,576]{2,1,0:T(8,128)(2,1)} %bitcast.221), calls=%async_computation.10 | async-start | bytes 1310720 | tf_op jit(solution)/shard_map/all_to_all | solution.py:300
  940.4 23.2 %all-to-all-start.7 = ((bf16[8,64,640]{2,1,0:T(8,128)(2,1)}), bf16[8,64,640]{2,1,0:T(8,128)(2,1)}, u32[]{:S(2)}, u32[]{:S(2)}) async-start(bf16[8,64,640]{2,1,0:T(8,128)(2,1)} %bitcast.220), calls=%async_computation.9 | async-start | bytes 1310720 | tf_op jit(solution)/shard_map/all_to_all | solution.py:300
  (105 other events, 1250.6 us)
Sparse Core Ops, SparseCore 0:
  10.7 93.7 all-gather.5
  122.9 106.0 all-gather.7
  231.7 72.3 all-gather.9
  319.2 74.6 all-gather.11
  478.6 147.2 reduce-scatter.2
  644.9 83.0 all-gather.13
  732.0 129.1 reduce-scatter.4

commit v7 on v6

--- a/solution.py
+++ b/solution.py
@@ -601,6 +601,29 @@
         out_shape=jax.ShapeDtypeStruct((columns, width), jnp.bfloat16),
         compiler_params=pltpu.CompilerParams(vmem_limit_bytes=VMEM_BYTES),
     )(normed, query_grad, resid, heads_out, *more)
+
+
+def shared_unpack_body(got_ref, gate_up_ref, down_ref, *, width, padded):
+    half = gate_up_ref.shape[1] // 2
+    for r in range(got_ref.shape[0]):
+        at = r * width
+        for part in range(2):
+            piece = got_ref[r, :, part * padded : part * padded + width]
+            gate_up_ref[:, part * half + at : part * half + at + width] = piece.astype(jnp.float32)
+        piece = got_ref[r, :, 2 * padded : 2 * padded + width].astype(jnp.float32)
+        down_ref[at : at + width, :] = piece.T
+
+
+def shared_unpack_call(got, width, padded):
+    count, rows = got.shape[:2]
+    return pl.pallas_call(
+        functools.partial(shared_unpack_body, width=width, padded=padded),
+        out_shape=[
+            jax.ShapeDtypeStruct((rows, 2 * count * width), jnp.float32),
+            jax.ShapeDtypeStruct((count * width, rows), jnp.float32),
+        ],
+        compiler_params=pltpu.CompilerParams(vmem_limit_bytes=VMEM_BYTES),
+    )(got)
 
 
 def combine_body(
@@ -704,7 +727,7 @@
     normed_mid, inv_mid = norm_forward(resid_mid, gain_mid)
     mid_send = swap_chunks(normed_mid.astype(jnp.bfloat16), rank, 1)
     grads_all = ctx_gather(after(swap_chunks(out_grad[0], rank, 1), first_done))
-    mid_send = after(mid_send, grads_all, gu_far[2], dn_far, shared_far)
+    mid_send = after(mid_send, grads_all, gu_far[2], shared_far)
     mid_all = ctx_gather(mid_send)
     shared_full = whole_rows(
         [shared_got, fsdp_swap(shared_got, 1), shared_far, fsdp_swap(after(shared_far, resid_mid), 1)], rank
@@ -789,6 +812,9 @@
     gu_got = after(gu_got, dn_other)
     gu_other = [gu_term(2, jnp.bfloat16, gu_got[e : e + 1], only=e) for e in range(exp_local)]
     gu_back = [fsdp_swap(v, 2) for v in gu_other]
+    x_late, y_late, act_late = after((x_late, y_late, act_late), gu_other)
+    dn_near = fsdp_swap(dn_term(1, jnp.bfloat16), 1)
+    gu_near = fsdp_swap(gu_term(1, jnp.bfloat16), 1)
     mid_late, grads_late = after((mid_all, grads_all), gu_other, dn_back)
     shared_grad = jnp.concatenate(
         [
@@ -798,9 +824,10 @@
         -1,
     )
     shared_grad = swap_chunks(shared_grad, rank, 0).astype(jnp.bfloat16)
+    dn_grad = dn_term(0, jnp.float32, dn_near, dn_back)
     shared_own, shared_other = shard_rows(shared_grad, n_ctx, rank)
     sums = after(
-        ctx_scatter(sums_part), gu_back[0], shared_own, shared_other
+        ctx_scatter(sums_part), gu_back[0], dn_near, gu_near, dn_grad, shared_own, shared_other
     ).astype(jnp.float32)
     mid_grad = swap_chunks(sums[:, :D], rank, 1)
     ffn_out = swap_chunks(sums[:, D:], rank, 1)
@@ -816,22 +843,14 @@
     token_grad, stage, gains_grad, query_w, latent_w, expand_w, output_w = attn_backward(
         resid_grad.astype(jnp.bfloat16), gu_back[1:], reduce_gains
     )
-    scored, keys_there, sums_there = stage
-    x_late, y_late, act_late = after((x_late, y_late, act_late), scored)
-    dn_near = fsdp_swap(dn_term(1, jnp.bfloat16), 1)
-    gu_near = fsdp_swap(gu_term(1, jnp.bfloat16), 1)
-    shared_far = fsdp_swap(after(shared_other, keys_there), 2)
+    part_there, keys_there, sums_there = stage
+    shared_far = fsdp_swap(after(shared_other, part_there), 2)
     shared_term = shared_own.astype(jnp.float32) + shared_far.astype(jnp.float32)
-    shared_grad = ctx_exchange(shared_term.astype(jnp.bfloat16)).astype(jnp.float32)
-    gate_grad = shared_grad[:, :, :sff_dev].transpose(1, 0, 2).reshape(-1, SFF)
-    up_grad = shared_grad[:, :, sff_pad : sff_pad + sff_dev].transpose(1, 0, 2).reshape(-1, SFF)
-    shared_gu_grad = jnp.concatenate([gate_grad, up_grad], -1)
-    down_grad = shared_grad[:, :, 2 * sff_pad : 2 * sff_pad + sff_dev]
-    shared_dn_grad = down_grad.transpose(0, 2, 1).reshape(SFF, -1)
-
+    shared_gu_grad, shared_dn_grad = shared_unpack_call(
+        ctx_exchange(after(shared_term.astype(jnp.bfloat16), keys_there)), sff_dev, sff_pad
+    )
     hidden_in_grad = (resid_grad + token_grad).astype(jnp.bfloat16)
     hidden_out = (resid_mid + ffn_out).astype(jnp.bfloat16)
-    dn_grad = dn_term(0, jnp.float32, dn_near, after(dn_back, sums_there))
     gu_grad = gu_term(0, jnp.float32, gu_near, each=after(gu_back, sums_there))
     return (
         hidden_out[None],
@@ -941,25 +960,25 @@
         rot_grads = [
             rope_back(rot_grad[j], cos_table, sin_table).astype(jnp.bfloat16) for j in range(heads)
         ]
-        query_grad = jnp.concatenate([nope_grad, *rot_grads], -1)
+        query_grad = after(jnp.concatenate([nope_grad, *rot_grads], -1), stages)
         in_part = dot_f32(query_grad, query_full, ((1,), (1,))).astype(jnp.bfloat16)
         in_grad = ctx_scatter(in_part)
         key_terms = jnp.concatenate([lat_total, rot_total], -1).astype(jnp.bfloat16)
-        key_terms = after(key_terms.reshape(n_ctx, tok_dev, KVL + DR), in_part, stages)
+        key_terms = after(key_terms.reshape(n_ctx, tok_dev, KVL + DR), in_part)
         key_sent = ctx_exchange(key_terms)
-        key_got = after(key_sent, resid_all)
         gain_in_grad = jnp.sum(
             in_part.astype(jnp.float32)
             * (saved["hidden_all"].astype(jnp.float32) * saved["inv_all"]),
             0,
         )
-        query_late = after(query_grad, key_got)
+        query_late = after(query_grad, in_part)
 
         def head_terms(k, *more):
             return head_terms_call(k, normed_bf, query_late, resid_all, saved["heads_out"], *more)
 
         head_sums = fsdp_reduce_terms(head_terms)[1]
-        head_sums = ctx_exchange(head_sums.reshape(n_ctx, rows, -1))
+        key_got = after(key_sent, head_sums)
+        head_sums = ctx_exchange(after(head_sums, key_sent).reshape(n_ctx, rows, -1))
         query_terms = head_sums[:, :, :q_wide].astype(jnp.float32)
         output_w = head_sums[:, :, q_wide:].astype(jnp.float32)
         output_w = output_w.transpose(0, 2, 1).reshape(H * DV, rows)
@@ -972,15 +991,17 @@
             [lat_in_grad, rope_back(key_sum[:, KVL:], own_cos, own_sin)], -1
         ).astype(jnp.bfloat16)
         own_normed = own_rows(normed_bf)[None]
+        lat_wide = -(-(KVL + DR) // 128) * 128
+        sent_grad = pad_last(compressed_grad, lat_wide)[None]
 
         def latent_terms(k, *more):
             return expert_grad_call(
-                own_normed, compressed_grad[None], (D // 4, k), (KVL + DR, 0), jnp.bfloat16, *more
+                own_normed, sent_grad, (D // 4, k), (lat_wide, 0), jnp.bfloat16, *more
             )
 
         latent_sent, latent_w = fsdp_reduce_terms(latent_terms)
-        latent_w = ctx_exchange(latent_w.reshape(n_ctx, rows, KVL + DR))
-        latent_w = jnp.sum(after(latent_w, in_grad).astype(jnp.float32), 0)
+        latent_w = ctx_exchange(latent_w.reshape(n_ctx, rows, lat_wide))
+        latent_w = jnp.sum(after(latent_w, in_grad).astype(jnp.float32), 0)[:, : KVL + DR]
         inv_in = own_rows(saved["inv_all"])
         in_own = dot_f32(compressed_grad, latent_full, ((1,), (1,)))
         token_cols = columns_by_distance(tokens, n_ctx, rank)
@@ -996,7 +1017,7 @@
         in_grad = after(in_grad, gains_grad).astype(jnp.float32) + in_own
         token_grad = norm_backward(token_cols, inv_in, saved["gain_cols"], in_grad)[0]
         token_grad = columns_in_order(token_grad, n_ctx, rank)
-        stage = (lat_total, key_sent, latent_sent)
+        stage = (in_part, key_sent, latent_sent)
         return token_grad, stage, gains_grad, query_w, latent_w, expand_w, output_w
 
     return first, middle, backward

time: 988 us -> 911 us (0.922)
  local copies, waits for them, and re-layouts: 153 us -> 114 us
  waiting for transfers between devices: 380 us -> 344 us
    all_to_all x9, waiting for transfers between devices: 86.8 us -> 61.2 us  [ctx_exchange(): lax.all_to_all(values, 'ctx', split_axis=0, concat_axis=0, tiled=True)]
    ppermute x40, waiting for transfers between devices: 264 us -> 253 us  [fsdp_swap(): lax.ppermute(values, 'fsdp', [(at, at ^ distance) for at in range(count)])]
    unnamed x216 -> x205, local copies, waits for them, and re-layouts: 54 us -> 44.3 us
  transfers between devices with their start and end apart: 56 -> 56, of which waited for: 18 -> 19; matrix products, arithmetic and copies ran while one was open for 25% -> 24% of each run, Pallas kernels for 11% -> 13%
where the time goes in v7:
time: 911 us; the launch traced here: 901 us
  waiting for transfers between devices  344 us (38%)
  Pallas kernels  183 us (20%)
  local copies, waits for them, and re-layouts  114 us (13%)
  other arithmetic  85.2 us (9%)
  starting transfers between devices  69 us (8%)
  matrix products  57.7 us (6%)
  blocking collectives  31.2 us (3%)
  between operations  16.2 us (2%)
    ppermute x40, waiting for transfers between devices, fsdp_swap(): lax.ppermute(values, 'fsdp', [(at, at ^ distance) for at in range(count)])  253 us
    all_to_all x9, waiting for transfers between devices, ctx_exchange(): lax.all_to_all(values, 'ctx', split_axis=0, concat_axis=0, tiled=True)  61.2 us
    pallas_call x13, Pallas kernels, expert_grad_call(): pl.pallas_call(functools.partial(expert_grad_body, each=len(each)), grid=...  60.7 us
    dot_general x12, matrix products, dot_f32(): lax.dot_general(left, right, (dims, ((), ())), preferred_element_type=jnp...  57.7 us
    pallas_call x1, Pallas kernels, experts_call(): pl.pallas_call(experts_body, grid=(count,), in_specs=[pl.BlockSpec((1, sl...  48.7 us
    all_to_all x9, starting transfers between devices, ctx_exchange(): lax.all_to_all(values, 'ctx', split_axis=0, concat_axis=0, tiled=True)  47.1 us
    unnamed x205, local copies, waits for them, and re-layouts  44.3 us
    all_to_all x1, blocking collectives, ctx_exchange(): lax.all_to_all(values, 'ctx', split_axis=0, concat_axis=0, tiled=True)  31.2 us
  transfers between devices with their start and end apart: 56, of which 19 were waited for; matrix products, arithmetic and copies ran while one was open for 24% of the time, Pallas kernels for 13%

profile of v7, /device:TPU:0, one launch (start us, length us, event | category | flops | bytes accessed | tf_op | source)
XLA Modules:
  0.0 900.8 jit_solution(10186323966210619974)
XLA Ops:
  12.8 7.3 all-to-all-start
  20.1 5.0 fusion.117
  27.2 32.5 %collective-permute-done = bf16[2,128,2816]{2,1,0:T(8,128)(2,1)S(1)} collective-permute-done((bf16[2,128,2816]{2,1,0:T(8,128)(2,1)S(1)}, bf16[2,128,2816]{2,1,0:T(8,128)(2,1)S(1)}, u32[]{:S(2)}, u32[]{:S(2)}) %collective-permute-start) | collective-permute-done | bytes 1441824 | tf_op jit(solution)/shard_map/ppermute | solution.py:242
  60.8 28.4 %collective-permute-done.1 = bf16[2,128,2816]{2,1,0:T(8,128)(2,1)} collective-permute-done((bf16[2,128,2816]{2,1,0:T(8,128)(2,1)S(1)}, bf16[2,128,2816]{2,1,0:T(8,128)(2,1)}, u32[]{:S(2)}, u32[]{:S(2)}) %collective-permute-start.1) | collective-permute-done | bytes 1441824 | tf_op jit(solution)/shard_map/ppermute | solution.py:242
  90.9 25.0 %collective-permute-done.3 = bf16[8,64,1088]{2,1,0:T(8,128)(2,1)S(1)} collective-permute-done((bf16[8,64,1088]{2,1,0:T(8,128)(2,1)S(1)}, bf16[8,64,1088]{2,1,0:T(8,128)(2,1)S(1)}, u32[]{:S(2)}, u32[]{:S(2)}) %collective-permute-start.3) | collective-permute-done | bytes 1114144 | tf_op jit(solution)/shard_map/ppermute | solution.py:242
  130.9 5.8 constant_dynamic-update-slice_fusion.9
  138.9 5.6 constant_dynamic-update-slice_fusion.8
  144.5 5.4 all-to-all-start.2
  156.8 6.1 fusion.25
  173.4 13.9 %shard_map.212 = (bf16[1024,256]{1,0:T(8,128)(2,1)S(1)}, f32[2,1024,512]{2,1,0:T(8,128)}, f32[2,1024,1]{2,1,0:T(8,128)S(1)}) custom-call(bf16[1024,256]{1,0:T(8,128)(2,1)S(1)} %slice.305.nope_ref, bf16[2,1024,64]{2,1,0:T(8,128)(2,1)S(1)} %pad_maximum_fusion.17.rot_ref, bf16[1024,512]{1,0:T(8,128)(2,1)} %multiply_convert_fusion.1.lat_ref, ...), custom_call_target="tpu_custom_call" | custom-call | tf_op jit(solution)/shard_map/pallas_call | solution.py:406
  190.5 4.8 all-to-all-start.1
  202.4 21.4 %all-to-all-done.1 = bf16[8,128,256]{1,2,0:T(8,128)(2,1)S(1)} async-done(((bf16[8,128,256]{1,2,0:T(8,128)(2,1)}), bf16[8,128,256]{1,2,0:T(8,128)(2,1)S(1)}, u32[]{:S(2)}, u32[]{:S(2)}) %all-to-all-start.1) | async-done | bytes 524320 | tf_op jit(solution)/shard_map/all_to_all | solution.py:300
  235.6 6.7 multiply_reduce_fusion.5
  244.4 75.4 %collective-permute-done.6 = bf16[8,64,1152]{2,1,0:T(8,128)(2,1)S(1)} collective-permute-done((bf16[8,64,1152]{2,1,0:T(8,128)(2,1)}, bf16[8,64,1152]{2,1,0:T(8,128)(2,1)S(1)}, u32[]{:S(2)}, u32[]{:S(2)}) %collective-permute-start.6) | collective-permute-done | bytes 1179680 | tf_op jit(solution)/shard_map/ppermute | solution.py:242
  328.4 4.7 convert_bitcast_fusion
  333.2 5.5 multiply_convert_fusion
  343.9 7.0 pad_maximum_fusion.5.gate_up_ref
  355.9 8.9 pad_maximum_fusion.dn_ref
  364.8 29.6 %all-gather.12.cloned.1.call-done = bf16[1024,2048]{1,0:T(8,128)(2,1)} async-done(((bf16[128,2048]{1,0:T(8,128)(2,1)}), bf16[1024,2048]{1,0:T(8,128)(2,1)}) %all-gather.12.cloned.1.call-update) | async-done | bytes 4194320 | tf_op jit(solution)/shard_map/all_gather | solution.py:292
  394.4 6.4 fusion.124
  405.1 5.4 convolution_convert_fusion.1
  410.5 48.7 %shard_map.213 = (bf16[2,432,1408]{2,1,0:T(8,128)(2,1)}, bf16[2,432,2816]{2,1,0:T(8,128)(2,1)}, bf16[2,432,2048]{2,1,0:T(8,128)(2,1)}, bf16[2,432,2048]{2,1,0:T(8,128)(2,1)}) custom-call(bf16[2,432,2048]{2,1,0:T(8,128)(2,1)} %bitcast.208, bf16[2,432,2048]{2,1,0:T(8,128)(2,1)} %bitcast.220, f32[2,432,1]{2,1,0:T(8,128)} %copy.472.gate_ref, ...), custom_call_target="tpu_custom_call" | custom-call | tf_op jit(solution)/shard_map/pallas_call | solution.py:518
  459.3 19.0 %shard_map.214 = bf16[1024,4096]{1,0:T(8,128)(2,1)} custom-call(bf16[1024,864]{1,0:T(8,128)(2,1)} %get-tuple-element.229.pick_ref, bf16[1024,768]{1,0:T(8,128)(2,1)S(1)} %pad_maximum_fusion.9.both_ref, bf16[1024,384]{1,0:T(8,128)(2,1)S(1)} %get-tuple-element.255.act_ref, bf16[864,2048]{1,0:T(8,128)(2,1)} %bitcast.237, bf16[864,2048]{1,0:T(8,128)(2,1)} %bitcast.236, ...), custom_call_target="tpu_custom_call" | custom-call | tf_op jit(solution)/shard_map/pallas_call | solution.py:652
  480.1 4.7 shard_map.215
  484.7 7.6 shard_map.216
  492.8 12.6 %collective-permute-done.19.refs_2_ = bf16[2,1408,512]{2,1,0:T(8,128)(2,1)S(1)} collective-permute-done((bf16[2,1408,512]{2,1,0:T(8,128)(2,1)S(1)}, bf16[2,1408,512]{2,1,0:T(8,128)(2,1)S(1)}, u32[]{:S(2)}, u32[]{:S(2)}) %collective-permute-start.19) | collective-permute-done | bytes 2883616 | tf_op jit(solution)/shard_map/ppermute | solution.py:242
  507.1 4.6 shard_map.217
  516.1 4.3 shard_map.219
  521.9 5.3 shard_map.218
  527.3 7.7 shard_map.221
  535.7 4.6 shard_map.220
  540.4 36.9 %collective-permute-done.23.refs_3_ = bf16[2,1408,512]{2,1,0:T(8,128)(2,1)} collective-permute-done((bf16[2,1408,512]{2,1,0:T(8,128)(2,1)}, bf16[2,1408,512]{2,1,0:T(8,128)(2,1)}, u32[]{:S(2)}, u32[]{:S(2)}) %collective-permute-start.23) | collective-permute-done | bytes 2883616 | tf_op jit(solution)/shard_map/ppermute | solution.py:242
  586.4 6.7 copy.473
  601.8 5.7 shard_map.222
  607.5 30.9 %collective-permute-done.20.refs_3_ = bf16[1,512,2816]{2,1,0:T(8,128)(2,1)S(1)} collective-permute-done((bf16[1,512,2816]{2,1,0:T(8,128)(2,1)}, bf16[1,512,2816]{2,1,0:T(8,128)(2,1)S(1)}, u32[]{:S(2)}, u32[]{:S(2)}) %collective-permute-start.20) | collective-permute-done | bytes 2883616 | tf_op jit(solution)/shard_map/ppermute | solution.py:242
  647.2 4.6 convolution_convert_fusion.2
  651.9 31.2 %all_to_all.54 = bf16[8,128,256]{2,1,0:T(8,128)(2,1)S(1)} all-to-all(bf16[8,128,256]{2,1,0:T(8,128)(2,1)S(1)} %bitcast.243), channel_id=1, replica_groups=mesh['ctx'=8,'fsdp'=4] {'ctx'}, dimensions={0} | all-to-all | bytes 1048576 | tf_op jit(solution)/shard_map/all_to_all | solution.py:300
  683.1 24.8 %shard_map.223 = (bf16[1024,256]{1,0:T(8,128)(2,1)S(1)}, f32[2,1024,64]{2,1,0:T(8,128)}, f32[2,512,256]{2,1,0:T(8,128)}, f32[1024,512]{1,0:T(8,128)}, f32[1024,64]{1,0:T(8,128)S(1)}) custom-call(bf16[1024,256]{1,0:T(8,128)(2,1)S(1)} %bitcast.219, bf16[1024,256]{1,0:T(8,128)(2,1)S(1)} %copy-done.12, bf16[2,1024,64]{2,1,0:T(8,128)(2,1)S(1)} %copy-done.10, ...), custom_call_target="tpu_custom_call" | custom-call | tf_op jit(solution)/shard_map/pallas_call | solution.py:441
  715.1 6.6 fusion.3
  727.3 4.5 all-to-all-start.5
  764.1 16.9 %all-to-all-done.5 = bf16[8,128,576]{1,2,0:T(8,128)(2,1)} async-done(((bf16[8,128,576]{1,2,0:T(8,128)(2,1)}), bf16[8,128,576]{1,2,0:T(8,128)(2,1)}, u32[]{:S(2)}, u32[]{:S(2)}) %all-to-all-start.5) | async-done | bytes 1179680 | tf_op jit(solution)/shard_map/all_to_all | solution.py:300
  781.0 5.4 all-to-all-start.9
  807.4 11.6 %all-to-all-done.9.got_ref = bf16[8,64,1152]{2,1,0:T(8,128)(2,1)S(1)} async-done(((bf16[8,64,1152]{2,1,0:T(8,128)(2,1)}), bf16[8,64,1152]{2,1,0:T(8,128)(2,1)S(1)}, u32[]{:S(2)}, u32[]{:S(2)}) %all-to-all-start.9) | async-done | bytes 1179680 | tf_op jit(solution)/shard_map/all_to_all | solution.py:300
  818.9 4.1 all-to-all-start.6
  832.2 11.9 %shard_map.233 = f32[2,512,2816]{2,1,0:T(8,128)} custom-call(bf16[2,432,2048]{2,1,0:T(8,128)(2,1)} %bitcast.211, bf16[2,432,2816]{2,1,0:T(8,128)(2,1)} %get-tuple-element.94.refs_1_, bf16[2,512,2816]{2,1,0:T(8,128)(2,1)} %collective-permute-done.22.refs_2_, bf16[1,512,2816]{2,1,0:T(8,128)(2,1)S(1)} %copy-done.14, ...), custom_call_target="tpu_custom_call" | custom-call | tf_op jit(solution)/shard_map/pallas_call | solution.py:555
  844.1 6.3 all-to-all-start.7
  870.7 5.7 all-to-all-start.8
  884.9 8.0 all-to-all-done.8
  (495 shorter events, 232.6 us)
Async XLA Ops:
  7.2 115.6 %all-gather.6.cloned.1.call-start = ((), (), s32[]{:S(2)}) async-start(), calls=%async_computation.12 | async-start | bytes 4718592 | tf_op jit(solution)/shard_map/all_gather | solution.py:292
  12.8 76.4 %all-to-all-start = ((bf16[8,64,960]{2,1,0:T(8,128)(2,1)}), bf16[8,64,960]{2,1,0:T(8,128)(2,1)S(1)}, u32[]{:S(2)}, u32[]{:S(2)}) async-start(bf16[8,64,960]{2,1,0:T(8,128)(2,1)} %pad_maximum_fusion.12), calls=%async_computation | async-start | bytes 2097152 | tf_op jit(solution)/shard_map/all_to_all | solution.py:300
  20.1 215.5 %all-gather.8.cloned.1.call-start = ((), (), s32[]{:S(2)}) async-start(), calls=%async_computation.13 | async-start | bytes 8650752 | tf_op jit(solution)/shard_map/all_gather | solution.py:914
  25.2 34.5 %collective-permute-start = (bf16[2,128,2816]{2,1,0:T(8,128)(2,1)S(1)}, bf16[2,128,2816]{2,1,0:T(8,128)(2,1)S(1)}, u32[]{:S(2)}, u32[]{:S(2)}) collective-permute-start(bf16[2,128,2816]{2,1,0:T(8,128)(2,1)S(1)} %get-tuple-element.236), channel_id=1, source_target_pairs={{0,2},{1,3},{2,0},{3,1},{4,6},{5,7},{6,4},{7,5},{8,10},{9,11},{10,... | collective-permute-start | bytes 4325384 | tf_op jit(solution)/shard_map/ppermute | solution.py:242
  26.6 62.6 %collective-permute-start.1 = (bf16[2,128,2816]{2,1,0:T(8,128)(2,1)S(1)}, bf16[2,128,2816]{2,1,0:T(8,128)(2,1)}, u32[]{:S(2)}, u32[]{:S(2)}) collective-permute-start(bf16[2,128,2816]{2,1,0:T(8,128)(2,1)S(1)} %get-tuple-element.235), channel_id=1, source_target_pairs={{0,2},{1,3},{2,0},{3,1},{4,6},{5,7},{6,4},{7,5},{8,10},{9,11},{10,... | collective-permute-start | bytes 4325384 | tf_op jit(solution)/shard_map/ppermute | solution.py:242
  89.4 26.5 %collective-permute-start.3 = (bf16[8,64,1088]{2,1,0:T(8,128)(2,1)S(1)}, bf16[8,64,1088]{2,1,0:T(8,128)(2,1)S(1)}, u32[]{:S(2)}, u32[]{:S(2)}) collective-permute-start(bf16[8,64,1088]{2,1,0:T(8,128)(2,1)S(1)} %pad_maximum_fusion.10), channel_id=1, source_target_pairs={{0,2},{1,3},{2,0},{3,1},{4,6},{5,7},{6,4},{7,5},{8,10},{9,11},{10,... | collective-permute-start | bytes 3342344 | tf_op jit(solution)/shard_map/ppermute | solution.py:242
  90.9 25.0 %collective-permute-start.2 = (bf16[8,64,1088]{2,1,0:T(8,128)(2,1)S(1)}, bf16[8,64,1088]{2,1,0:T(8,128)(2,1)S(1)}, u32[]{:S(2)}, u32[]{:S(2)}) collective-permute-start(bf16[8,64,1088]{2,1,0:T(8,128)(2,1)S(1)} %pad_maximum_fusion.10), channel_id=1, source_target_pairs={{0,1},{1,0},{2,3},{3,2},{4,5},{5,4},{6,7},{7,6},{8,9},{9,8},{10,11... | collective-permute-start | bytes 3342344 | tf_op jit(solution)/shard_map/ppermute | solution.py:242
  122.8 16.1 %collective-permute-start.9 = (bf16[2,512,2816]{2,1,0:T(8,128)(2,1)}, bf16[2,512,2816]{2,1,0:T(8,128)(2,1)}, u32[]{:S(2)}, u32[]{:S(2)}) collective-permute-start(bf16[2,512,2816]{2,1,0:T(8,128)(2,1)} %param.22), channel_id=1, source_target_pairs={{0,1},{1,0},{2,3},{3,2},{4,5},{5,4},{6,7},{7,6},{8,9},{9,8},{10,11... | collective-permute-start | bytes 17301512 | tf_op jit(solution)/shard_map/ppermute | solution.py:242
  123.0 76.2 %collective-permute-start.8 = (bf16[2,128,2816]{2,1,0:T(8,128)(2,1)}, bf16[2,128,2816]{2,1,0:T(8,128)(2,1)}, u32[]{:S(2)}, u32[]{:S(2)}) collective-permute-start(bf16[2,128,2816]{2,1,0:T(8,128)(2,1)} %get-tuple-element.234), channel_id=1, source_target_pairs={{0,2},{1,3},{2,0},{3,1},{4,6},{5,7},{6,4},{7,5},{8,10},{9,11},{10,... | collective-permute-start | bytes 4325384 | tf_op jit(solution)/shard_map/ppermute | solution.py:242
  124.5 103.0 %collective-permute-start.10 = (bf16[2,128,2816]{2,1,0:T(8,128)(2,1)}, bf16[2,128,2816]{2,1,0:T(8,128)(2,1)}, u32[]{:S(2)}, u32[]{:S(2)}) collective-permute-start(bf16[2,128,2816]{2,1,0:T(8,128)(2,1)} %get-tuple-element.233), channel_id=1, source_target_pairs={{0,2},{1,3},{2,0},{3,1},{4,6},{5,7},{6,4},{7,5},{8,10},{9,11},{10,... | collective-permute-start | bytes 4325384 | tf_op jit(solution)/shard_map/ppermute | solution.py:242
  125.0 230.8 %collective-permute-start.15 = (bf16[2,1408,512]{2,1,0:T(8,128)(2,1)}, bf16[2,1408,512]{2,1,0:T(8,128)(2,1)}, u32[]{:S(2)}, u32[]{:S(2)}) collective-permute-start(bf16[2,1408,512]{2,1,0:T(8,128)(2,1)} %param.23), channel_id=1, source_target_pairs={{0,1},{1,0},{2,3},{3,2},{4,5},{5,4},{6,7},{7,6},{8,9},{9,8},{10,11... | collective-permute-start | bytes 8650760 | tf_op jit(solution)/shard_map/ppermute | solution.py:242
  144.5 46.0 %all-to-all-start.2 = ((bf16[8,64,1152]{2,1,0:T(8,128)(2,1)}), bf16[8,64,1152]{2,1,0:T(8,128)(2,1)}, u32[]{:S(2)}, u32[]{:S(2)}) async-start(bf16[8,64,1152]{2,1,0:T(8,128)(2,1)} %fusion.32), calls=%async_computation.2 | async-start | bytes 2359296 | tf_op jit(solution)/shard_map/all_to_all | solution.py:300
  149.9 169.9 %all-gather.10.cloned.1.call-start = ((), (), s32[]{:S(2)}) async-start(), calls=%async_computation.14 | async-start | bytes 4718592 | tf_op jit(solution)/shard_map/all_gather | solution.py:292
  190.5 33.4 %all-to-all-start.1 = ((bf16[8,128,256]{1,2,0:T(8,128)(2,1)}), bf16[8,128,256]{1,2,0:T(8,128)(2,1)S(1)}, u32[]{:S(2)}, u32[]{:S(2)}) async-start(bf16[8,128,256]{1,2,0:T(8,128)(2,1)} %copy.456), calls=%async_computation.1 | async-start | bytes 1048576 | tf_op jit(solution)/shard_map/all_to_all | solution.py:300
  227.5 166.9 %all-gather.12.cloned.1.call-start = ((), (), s32[]{:S(2)}) async-start(), calls=%async_computation.15 | async-start | bytes 4718592 | tf_op jit(solution)/shard_map/all_gather | solution.py:292
  230.1 108.9 %collective-permute-start.16 = (bf16[2,1408,512]{2,1,0:T(8,128)(2,1)}, bf16[2,1408,512]{2,1,0:T(8,128)(2,1)}, u32[]{:S(2)}, u32[]{:S(2)}) collective-permute-start(bf16[2,1408,512]{2,1,0:T(8,128)(2,1)} %param.23), channel_id=1, source_target_pairs={{0,2},{1,3},{2,0},{3,1},{4,6},{5,7},{6,4},{7,5},{8,10},{9,11},{10,... | collective-permute-start | bytes 8650760 | tf_op jit(solution)/shard_map/ppermute | solution.py:242
  231.6 88.2 %collective-permute-start.6 = (bf16[8,64,1152]{2,1,0:T(8,128)(2,1)}, bf16[8,64,1152]{2,1,0:T(8,128)(2,1)S(1)}, u32[]{:S(2)}, u32[]{:S(2)}) collective-permute-start(bf16[8,64,1152]{2,1,0:T(8,128)(2,1)} %all-to-all-done.2), channel_id=1, source_target_pairs={{0,2},{1,3},{2,0},{3,1},{4,6},{5,7},{6,4},{7,5},{8,10},{9,11},{10,... | collective-permute-start | bytes 3538952 | tf_op jit(solution)/shard_map/ppermute | solution.py:242
  232.1 107.1 %collective-permute-start.5 = (bf16[8,64,1152]{2,1,0:T(8,128)(2,1)}, bf16[8,64,1152]{2,1,0:T(8,128)(2,1)}, u32[]{:S(2)}, u32[]{:S(2)}) collective-permute-start(bf16[8,64,1152]{2,1,0:T(8,128)(2,1)} %all-to-all-done.2), channel_id=1, source_target_pairs={{0,1},{1,0},{2,3},{3,2},{4,5},{5,4},{6,7},{7,6},{8,9},{9,8},{10,11... | collective-permute-start | bytes 3538952 | tf_op jit(solution)/shard_map/ppermute | solution.py:242
  319.8 318.6 %reduce-scatter.3.cloned.1.call-start = ((), (), s32[]{:S(2)}) async-start(), calls=%async_computation.16 | async-start | bytes 9437184 | tf_op jit(solution)/shard_map/reduce_scatter | solution.py:296
  328.4 11.1 %collective-permute-start.7 = (bf16[8,64,1152]{2,1,0:T(8,128)(2,1)S(1)}, bf16[8,64,1152]{2,1,0:T(8,128)(2,1)S(1)}, u32[]{:S(2)}, u32[]{:S(2)}) collective-permute-start(bf16[8,64,1152]{2,1,0:T(8,128)(2,1)S(1)} %copy-done.51), channel_id=1, source_target_pairs={{0,1},{1,0},{2,3},{3,2},{4,5},{5,4},{6,7},{7,6},{8,9},{9,8},{10,11... | collective-permute-start | bytes 3538952 | tf_op jit(solution)/shard_map/ppermute | solution.py:242
  339.0 13.1 %collective-permute-start.12 = (bf16[2,128,2816]{2,1,0:T(8,128)(2,1)}, bf16[2,128,2816]{2,1,0:T(8,128)(2,1)S(1)}, u32[]{:S(2)}, u32[]{:S(2)}) collective-permute-start(bf16[2,128,2816]{2,1,0:T(8,128)(2,1)} %collective-permute-done.1), channel_id=1, source_target_pairs={{0,1},{1,0},{2,3},{3,2},{4,5},{5,4},{6,7},{7,6},{8,9},{9,8},{10,11... | collective-permute-start | bytes 4325384 | tf_op jit(solution)/shard_map/ppermute | solution.py:242
  339.2 14.2 %collective-permute-start.13 = (bf16[2,128,2816]{2,1,0:T(8,128)(2,1)}, bf16[2,128,2816]{2,1,0:T(8,128)(2,1)S(1)}, u32[]{:S(2)}, u32[]{:S(2)}) collective-permute-start(bf16[2,128,2816]{2,1,0:T(8,128)(2,1)} %collective-permute-done.8), channel_id=1, source_target_pairs={{0,1},{1,0},{2,3},{3,2},{4,5},{5,4},{6,7},{7,6},{8,9},{9,8},{10,11... | collective-permute-start | bytes 4325384 | tf_op jit(solution)/shard_map/ppermute | solution.py:242
  339.6 16.3 %collective-permute-start.17 = (bf16[2,1408,512]{2,1,0:T(8,128)(2,1)}, bf16[2,1408,512]{2,1,0:T(8,128)(2,1)S(1)}, u32[]{:S(2)}, u32[]{:S(2)}) collective-permute-start(bf16[2,1408,512]{2,1,0:T(8,128)(2,1)} %collective-permute-done.16), channel_id=1, source_target_pairs={{0,1},{1,0},{2,3},{3,2},{4,5},{5,4},{6,7},{7,6},{8,9},{9,8},{10,11... | collective-permute-start | bytes 8650760 | tf_op jit(solution)/shard_map/ppermute | solution.py:242
  343.3 11.3 %collective-permute-start.14 = (bf16[2,128,2816]{2,1,0:T(8,128)(2,1)}, bf16[2,128,2816]{2,1,0:T(8,128)(2,1)S(1)}, u32[]{:S(2)}, u32[]{:S(2)}) collective-permute-start(bf16[2,128,2816]{2,1,0:T(8,128)(2,1)} %collective-permute-done.10), channel_id=1, source_target_pairs={{0,1},{1,0},{2,3},{3,2},{4,5},{5,4},{6,7},{7,6},{8,9},{9,8},{10,11... | collective-permute-start | bytes 4325384 | tf_op jit(solution)/shard_map/ppermute | solution.py:242
  478.3 254.3 %all-gather.14.cloned.1.call-start = ((), (), s32[]{:S(2)}) async-start(), calls=%async_computation.18 | async-start | bytes 4718592 | tf_op jit(solution)/shard_map/all_gather | solution.py:292
  492.3 20.9 %collective-permute-start.18 = (bf16[2,512,2816]{2,1,0:T(8,128)(2,1)}, bf16[2,512,2816]{2,1,0:T(8,128)(2,1)S(1)}, u32[]{:S(2)}, u32[]{:S(2)}) collective-permute-start(bf16[2,512,2816]{2,1,0:T(8,128)(2,1)} %shard_map.216), channel_id=1, source_target_pairs={{0,1},{1,0},{2,3},{3,2},{4,5},{5,4},{6,7},{7,6},{8,9},{9,8},{10,11... | collective-permute-start | bytes 17301512 | tf_op jit(solution)/shard_map/ppermute | solution.py:242
  492.3 13.2 %collective-permute-start.19 = (bf16[2,1408,512]{2,1,0:T(8,128)(2,1)S(1)}, bf16[2,1408,512]{2,1,0:T(8,128)(2,1)S(1)}, u32[]{:S(2)}, u32[]{:S(2)}) collective-permute-start(bf16[2,1408,512]{2,1,0:T(8,128)(2,1)S(1)} %copy-done.37), channel_id=1, source_target_pairs={{0,1},{1,0},{2,3},{3,2},{4,5},{5,4},{6,7},{7,6},{8,9},{9,8},{10,11... | collective-permute-start | bytes 8650760 | tf_op jit(solution)/shard_map/ppermute | solution.py:242
  511.7 65.6 %collective-permute-start.23 = (bf16[2,1408,512]{2,1,0:T(8,128)(2,1)}, bf16[2,1408,512]{2,1,0:T(8,128)(2,1)}, u32[]{:S(2)}, u32[]{:S(2)}) collective-permute-start(bf16[2,1408,512]{2,1,0:T(8,128)(2,1)} %shard_map.217), channel_id=1, source_target_pairs={{0,2},{1,3},{2,0},{3,1},{4,6},{5,7},{6,4},{7,5},{8,10},{9,11},{10,... | collective-permute-start | bytes 8650760 | tf_op jit(solution)/shard_map/ppermute | solution.py:242
  535.0 103.5 %collective-permute-start.22 = (bf16[2,512,2816]{2,1,0:T(8,128)(2,1)}, bf16[2,512,2816]{2,1,0:T(8,128)(2,1)}, u32[]{:S(2)}, u32[]{:S(2)}) collective-permute-start(bf16[2,512,2816]{2,1,0:T(8,128)(2,1)} %shard_map.221), channel_id=1, source_target_pairs={{0,1},{1,0},{2,3},{3,2},{4,5},{5,4},{6,7},{7,6},{8,9},{9,8},{10,11... | collective-permute-start | bytes 17301512 | tf_op jit(solution)/shard_map/ppermute | solution.py:242
  535.0 103.4 %collective-permute-start.20 = (bf16[1,512,2816]{2,1,0:T(8,128)(2,1)}, bf16[1,512,2816]{2,1,0:T(8,128)(2,1)S(1)}, u32[]{:S(2)}, u32[]{:S(2)}) collective-permute-start(bf16[1,512,2816]{2,1,0:T(8,128)(2,1)} %shard_map.218), channel_id=1, source_target_pairs={{0,2},{1,3},{2,0},{3,1},{4,6},{5,7},{6,4},{7,5},{8,10},{9,11},{10,... | collective-permute-start | bytes 8650760 | tf_op jit(solution)/shard_map/ppermute | solution.py:242
  540.3 61.5 %collective-permute-start.21 = (bf16[2,1408,512]{2,1,0:T(8,128)(2,1)}, bf16[2,1408,512]{2,1,0:T(8,128)(2,1)}, u32[]{:S(2)}, u32[]{:S(2)}) collective-permute-start(bf16[2,1408,512]{2,1,0:T(8,128)(2,1)} %shard_map.220), channel_id=1, source_target_pairs={{0,1},{1,0},{2,3},{3,2},{4,5},{5,4},{6,7},{7,6},{8,9},{9,8},{10,11... | collective-permute-start | bytes 8650760 | tf_op jit(solution)/shard_map/ppermute | solution.py:242
  645.6 206.8 %reduce-scatter.5.cloned.1.call-start = ((), (), s32[]{:S(2)}) async-start(), calls=%async_computation.17 | async-start | bytes 4718592 | tf_op jit(solution)/shard_map/reduce_scatter | solution.py:296
  645.7 69.5 %collective-permute-start.26 = (bf16[1,512,2816]{2,1,0:T(8,128)(2,1)}, bf16[1,512,2816]{2,1,0:T(8,128)(2,1)}, u32[]{:S(2)}, u32[]{:S(2)}) collective-permute-start(bf16[1,512,2816]{2,1,0:T(8,128)(2,1)} %copy-done.15), channel_id=1, source_target_pairs={{0,2},{1,3},{2,0},{3,1},{4,6},{5,7},{6,4},{7,5},{8,10},{9,11},{10,... | collective-permute-start | bytes 8650760 | tf_op jit(solution)/shard_map/ppermute | solution.py:242
  727.3 53.7 %all-to-all-start.5 = ((bf16[8,128,576]{1,2,0:T(8,128)(2,1)}), bf16[8,128,576]{1,2,0:T(8,128)(2,1)}, u32[]{:S(2)}, u32[]{:S(2)}) async-start(bf16[8,128,576]{1,2,0:T(8,128)(2,1)} %pad_maximum_fusion.11), calls=%async_computation.7 | async-start | bytes 2359296 | tf_op jit(solution)/shard_map/all_to_all | solution.py:300
  731.8 29.7 %collective-permute-start.39 = (bf16[8,64,1152]{2,1,0:T(8,128)(2,1)}, bf16[8,64,1152]{2,1,0:T(8,128)(2,1)}, u32[]{:S(2)}, u32[]{:S(2)}) collective-permute-start(bf16[8,64,1152]{2,1,0:T(8,128)(2,1)} %get-tuple-element.125), channel_id=1, source_target_pairs={{0,2},{1,3},{2,0},{3,1},{4,6},{5,7},{6,4},{7,5},{8,10},{9,11},{10,... | collective-permute-start | bytes 3538952 | tf_op jit(solution)/shard_map/ppermute | solution.py:242
  736.0 14.2 %collective-permute-start.28 = (bf16[512,640]{1,0:T(8,128)(2,1)}, bf16[512,640]{1,0:T(8,128)(2,1)}, u32[]{:S(2)}, u32[]{:S(2)}) collective-permute-start(bf16[512,640]{1,0:T(8,128)(2,1)} %shard_map.225), channel_id=1, source_target_pairs={{0,1},{1,0},{2,3},{3,2},{4,5},{5,4},{6,7},{7,6},{8,9},{9,8},{10,11... | collective-permute-start | bytes 1966088 | tf_op jit(solution)/shard_map/ppermute | solution.py:242
  749.6 36.7 %collective-permute-start.27 = (bf16[512,640]{1,0:T(8,128)(2,1)}, bf16[512,640]{1,0:T(8,128)(2,1)}, u32[]{:S(2)}, u32[]{:S(2)}) collective-permute-start(bf16[512,640]{1,0:T(8,128)(2,1)} %shard_map.224), channel_id=1, source_target_pairs={{0,1},{1,0},{2,3},{3,2},{4,5},{5,4},{6,7},{7,6},{8,9},{9,8},{10,11... | collective-permute-start | bytes 1966088 | tf_op jit(solution)/shard_map/ppermute | solution.py:242
  753.8 32.6 %collective-permute-start.29 = (bf16[512,640]{1,0:T(8,128)(2,1)}, bf16[512,640]{1,0:T(8,128)(2,1)}, u32[]{:S(2)}, u32[]{:S(2)}) collective-permute-start(bf16[512,640]{1,0:T(8,128)(2,1)} %shard_map.226), channel_id=1, source_target_pairs={{0,2},{1,3},{2,0},{3,1},{4,6},{5,7},{6,4},{7,5},{8,10},{9,11},{10,... | collective-permute-start | bytes 1966088 | tf_op jit(solution)/shard_map/ppermute | solution.py:242
  761.0 42.1 %collective-permute-start.37 = (bf16[512,128]{1,0:T(8,128)(2,1)}, bf16[512,128]{1,0:T(8,128)(2,1)}, u32[]{:S(2)}, u32[]{:S(2)}) collective-permute-start(bf16[512,128]{1,0:T(8,128)(2,1)} %bitcast.273), channel_id=1, source_target_pairs={{0,1},{1,0},{2,3},{3,2},{4,5},{5,4},{6,7},{7,6},{8,9},{9,8},{10,11... | collective-permute-start | bytes 393224 | tf_op jit(solution)/shard_map/ppermute | solution.py:242
  761.0 62.0 %collective-permute-start.36 = (bf16[512,128]{1,0:T(8,128)(2,1)}, bf16[512,128]{1,0:T(8,128)(2,1)}, u32[]{:S(2)}, u32[]{:S(2)}) collective-permute-start(bf16[512,128]{1,0:T(8,128)(2,1)} %bitcast.272), channel_id=1, source_target_pairs={{0,1},{1,0},{2,3},{3,2},{4,5},{5,4},{6,7},{7,6},{8,9},{9,8},{10,11... | collective-permute-start | bytes 393224 | tf_op jit(solution)/shard_map/ppermute | solution.py:242
  781.0 38.0 %all-to-all-start.9 = ((bf16[8,64,1152]{2,1,0:T(8,128)(2,1)}), bf16[8,64,1152]{2,1,0:T(8,128)(2,1)S(1)}, u32[]{:S(2)}, u32[]{:S(2)}) async-start(bf16[8,64,1152]{2,1,0:T(8,128)(2,1)} %add_convert_fusion), calls=%async_computation.11 | async-start | bytes 2359296 | tf_op jit(solution)/shard_map/all_to_all | solution.py:300
  802.5 48.5 %collective-permute-start.34 = (bf16[1,512,640]{2,1,0:T(8,128)(2,1)}, bf16[1,512,640]{2,1,0:T(8,128)(2,1)S(1)}, u32[]{:S(2)}, u32[]{:S(2)}) collective-permute-start(bf16[1,512,640]{2,1,0:T(8,128)(2,1)} %shard_map.229), channel_id=1, source_target_pairs={{0,1},{1,0},{2,3},{3,2},{4,5},{5,4},{6,7},{7,6},{8,9},{9,8},{10,11... | collective-permute-start | bytes 1966088 | tf_op jit(solution)/shard_map/ppermute | solution.py:242
  804.1 18.9 %collective-permute-start.38 = (bf16[512,128]{1,0:T(8,128)(2,1)S(1)}, bf16[512,128]{1,0:T(8,128)(2,1)S(1)}, u32[]{:S(2)}, u32[]{:S(2)}) collective-permute-start(bf16[512,128]{1,0:T(8,128)(2,1)S(1)} %add_convert_fusion.2), channel_id=1, source_target_pairs={{0,2},{1,3},{2,0},{3,1},{4,6},{5,7},{6,4},{7,5},{8,10},{9,11},{10,... | collective-permute-start | bytes 393224 | tf_op jit(solution)/shard_map/ppermute | solution.py:242
  818.9 25.2 %all-to-all-start.6 = ((f32[8,1,144]{2,1,0:T(1,128)}), f32[8,1,144]{2,1,0:T(1,128)S(1)}, u32[]{:S(2)}, u32[]{:S(2)}) async-start(f32[8,1,144]{2,1,0:T(1,128)} %all_to_all.39), calls=%async_computation.8 | async-start | bytes 16384 | tf_op jit(solution)/shard_map/all_to_all | solution.py:300
  830.3 34.2 %collective-permute-start.33 = (bf16[1,512,640]{2,1,0:T(8,128)(2,1)S(1)}, bf16[1,512,640]{2,1,0:T(8,128)(2,1)}, u32[]{:S(2)}, u32[]{:S(2)}) collective-permute-start(bf16[1,512,640]{2,1,0:T(8,128)(2,1)S(1)} %shard_map.228), channel_id=1, source_target_pairs={{0,1},{1,0},{2,3},{3,2},{4,5},{5,4},{6,7},{7,6},{8,9},{9,8},{10,11... | collective-permute-start | bytes 1966088 | tf_op jit(solution)/shard_map/ppermute | solution.py:242
  844.1 26.5 %all-to-all-start.7 = ((bf16[8,64,640]{2,1,0:T(8,128)(2,1)}), bf16[8,64,640]{2,1,0:T(8,128)(2,1)}, u32[]{:S(2)}, u32[]{:S(2)}) async-start(bf16[8,64,640]{2,1,0:T(8,128)(2,1)} %bitcast.78), calls=%async_computation.9 | async-start | bytes 1310720 | tf_op jit(solution)/shard_map/all_to_all | solution.py:300
  851.4 16.9 %collective-permute-start.35 = (bf16[1,512,640]{2,1,0:T(8,128)(2,1)S(1)}, bf16[1,512,640]{2,1,0:T(8,128)(2,1)S(1)}, u32[]{:S(2)}, u32[]{:S(2)}) collective-permute-start(bf16[1,512,640]{2,1,0:T(8,128)(2,1)S(1)} %shard_map.230), channel_id=1, source_target_pairs={{0,2},{1,3},{2,0},{3,1},{4,6},{5,7},{6,4},{7,5},{8,10},{9,11},{10,... | collective-permute-start | bytes 1966088 | tf_op jit(solution)/shard_map/ppermute | solution.py:242
  870.7 22.3 %all-to-all-start.8 = ((bf16[8,64,640]{2,1,0:T(8,128)(2,1)}), bf16[8,64,640]{2,1,0:T(8,128)(2,1)S(1)}, u32[]{:S(2)}, u32[]{:S(2)}) async-start(bf16[8,64,640]{2,1,0:T(8,128)(2,1)} %bitcast.82), calls=%async_computation.10 | async-start | bytes 1310720 | tf_op jit(solution)/shard_map/all_to_all | solution.py:300
  (99 other events, 1507.3 us)
Sparse Core Ops, SparseCore 0:
  10.7 93.7 all-gather.5
  122.9 105.7 all-gather.7
  231.4 72.3 all-gather.9
  320.0 74.3 all-gather.11
  478.4 147.1 reduce-scatter.2
  645.7 83.0 all-gather.13
  732.8 117.8 reduce-scatter.4

commit v8 on v7

--- a/solution.py
+++ b/solution.py
@@ -702,6 +702,7 @@
         return lax.dynamic_slice_in_dim(values, first_row, tok_dev, 0)
 
     exp_local = expert_gate_up.shape[0]
+    order = rank ^ 2
     steps = 4
     step_rows = D // 4 // steps
     gu_far = [
@@ -721,28 +722,30 @@
     shared_send = jnp.concatenate([gate_send, up_send, down_send], -1)
     shared_got = ctx_exchange(after(shared_send, first_done))
     shared_far = fsdp_swap(shared_got, 2)
-    dn_far = fsdp_swap(after(expert_down, first_done), 2)
+    dn_far = fsdp_swap(after(expert_down, shared_far), 2)
 
     resid_mid = attn_mid((shared_got,))
     normed_mid, inv_mid = norm_forward(resid_mid, gain_mid)
-    mid_send = swap_chunks(normed_mid.astype(jnp.bfloat16), rank, 1)
-    grads_all = ctx_gather(after(swap_chunks(out_grad[0], rank, 1), first_done))
+    mid_send = swap_chunks(normed_mid.astype(jnp.bfloat16), order, 1)
+    grads_all = ctx_gather(after(swap_chunks(out_grad[0], order, 1), first_done))
     mid_send = after(mid_send, grads_all, gu_far[2], shared_far)
     mid_all = ctx_gather(mid_send)
     shared_full = whole_rows(
         [shared_got, fsdp_swap(shared_got, 1), shared_far, fsdp_swap(after(shared_far, resid_mid), 1)], rank
     )
-    shared_rel = swap_chunks(shared_full, rank, 0)
+    shared_rel = swap_chunks(shared_full, order, 0)
     shared_gu = shared_rel[:, : 2 * sff_pad]
     shared_dn = shared_rel[:, 2 * sff_pad :]
     gu_rel = jnp.concatenate(
-        [expert_gate_up, fsdp_swap(expert_gate_up, 1), *gu_far]
-        + [fsdp_swap(after(v, resid_mid), 1) for v in gu_far],
+        gu_far
+        + [fsdp_swap(after(v, resid_mid), 1) for v in gu_far]
+        + [expert_gate_up, fsdp_swap(expert_gate_up, 1)],
         1,
     )
     dn_rel = jnp.concatenate(
-        [expert_down, fsdp_swap(expert_down, 1), dn_far, fsdp_swap(after(dn_far, mid_send), 1)], 2
-    )
+        [dn_far, fsdp_swap(after(dn_far, mid_send), 1), expert_down, fsdp_swap(expert_down, 1)], 2
+    )
+
     n_exp = exp_local * n_ctx
     capacity = max(2, 9 * tok_dev * TOP // (8 * n_exp))
     slots = capacity * n_ctx
@@ -797,10 +800,10 @@
     quarter = D // 4
 
     def dn_term(k, kind, *more):
-        return expert_grad_call(act_late, y_late, (FF, 0), (quarter, k), kind, *more)
+        return expert_grad_call(act_late, y_late, (FF, 0), (quarter, k ^ 2), kind, *more)
 
     def gu_term(k, kind, *more, **which):
-        return expert_grad_call(x_late, both_grad, (quarter, k), (2 * FF, 0), kind, *more, **which)
+        return expert_grad_call(x_late, both_grad, (quarter, k ^ 2), (2 * FF, 0), kind, *more, **which)
 
     dn_send = dn_term(3, jnp.bfloat16)
     dn_got = fsdp_swap(dn_send, 1)
@@ -823,21 +826,21 @@
         ],
         -1,
     )
-    shared_grad = swap_chunks(shared_grad, rank, 0).astype(jnp.bfloat16)
+    shared_grad = swap_chunks(shared_grad, order, 0).astype(jnp.bfloat16)
     dn_grad = dn_term(0, jnp.float32, dn_near, dn_back)
     shared_own, shared_other = shard_rows(shared_grad, n_ctx, rank)
     sums = after(
         ctx_scatter(sums_part), gu_back[0], dn_near, gu_near, dn_grad, shared_own, shared_other
     ).astype(jnp.float32)
-    mid_grad = swap_chunks(sums[:, :D], rank, 1)
-    ffn_out = swap_chunks(sums[:, D:], rank, 1)
+    mid_grad = swap_chunks(sums[:, :D], order, 1)
+    ffn_out = swap_chunks(sums[:, D:], order, 1)
 
     resid_norm_grad, gain_mid_grad = norm_backward(resid_mid, inv_mid, gain_mid, mid_grad)
     resid_grad = out_grad[0].astype(jnp.float32) + resid_norm_grad
 
-    def reduce_gains(gain_in_grad, gain_lat_grad):
+    def reduce_gains(gain_in_grad, gain_lat_grad, *first):
         gains = jnp.concatenate([gain_in_grad, gain_mid_grad, gain_lat_grad], 0)
-        gains = fsdp_reduce(gains.reshape(n_ctx, 4, -1).transpose(1, 0, 2), rank)
+        gains = fsdp_reduce(gains.reshape(n_ctx, 4, -1).transpose(1, 0, 2), rank, *first)
         return jnp.sum(ctx_exchange(gains), 0)
 
     token_grad, stage, gains_grad, query_w, latent_w, expand_w, output_w = attn_backward(
@@ -846,8 +849,9 @@
     part_there, keys_there, sums_there = stage
     shared_far = fsdp_swap(after(shared_other, part_there), 2)
     shared_term = shared_own.astype(jnp.float32) + shared_far.astype(jnp.float32)
+    shared_sums = ctx_exchange(after(shared_term.astype(jnp.bfloat16), keys_there))
     shared_gu_grad, shared_dn_grad = shared_unpack_call(
-        ctx_exchange(after(shared_term.astype(jnp.bfloat16), keys_there)), sff_dev, sff_pad
+        after(shared_sums, sums_there), sff_dev, sff_pad
     )
     hidden_in_grad = (resid_grad + token_grad).astype(jnp.bfloat16)
     hidden_out = (resid_mid + ffn_out).astype(jnp.bfloat16)
@@ -899,7 +903,7 @@
         ).transpose(1, 0, 2)
         latent_send = jnp.broadcast_to(w_latent[None], (n_ctx,) + w_latent.shape)
         got = ctx_exchange(jnp.concatenate([query_send, latent_send], -1))
-        got = after(got, early[:2])
+        got = after(got, early[0])
         pieces = fsdp_pieces(jnp.concatenate([got, w_expand.reshape(n_ctx, rows, -1)], -1))
         full = jnp.concatenate([p.reshape(n_ctx * rows, -1) for p in pieces], 0)
         query_full = full[:, :q_wide]
@@ -1000,6 +1004,7 @@
             )
 
         latent_sent, latent_w = fsdp_reduce_terms(latent_terms)
+        latent_own = latent_w
         latent_w = ctx_exchange(latent_w.reshape(n_ctx, rows, lat_wide))
         latent_w = jnp.sum(after(latent_w, in_grad).astype(jnp.float32), 0)[:, : KVL + DR]
         inv_in = own_rows(saved["inv_all"])
@@ -1007,7 +1012,7 @@
         token_cols = columns_by_distance(tokens, n_ctx, rank)
         gain_in_grad = gain_in_grad + jnp.sum(in_own * (token_cols * inv_in), 0)
         gain_in_grad = columns_in_order(gain_in_grad[None], n_ctx, rank)[0]
-        gains_grad = reduce_gains(gain_in_grad, gain_lat_grad)
+        gains_grad = reduce_gains(gain_in_grad, gain_lat_grad, latent_own)
         expand_g = expand_g.transpose(1, 0, 2)
         expand_blocks = expand_g.reshape(KVL, 4, -1).transpose(1, 0, 2).astype(jnp.bfloat16)
         expand_w = fsdp_reduce(expand_blocks, rank)
@@ -1017,7 +1022,7 @@
         in_grad = after(in_grad, gains_grad).astype(jnp.float32) + in_own
         token_grad = norm_backward(token_cols, inv_in, saved["gain_cols"], in_grad)[0]
         token_grad = columns_in_order(token_grad, n_ctx, rank)
-        stage = (in_part, key_sent, latent_sent)
+        stage = (in_part, key_sent, latent_own)
         return token_grad, stage, gains_grad, query_w, latent_w, expand_w, output_w
 
     return first, middle, backward

time: 911 us -> 886 us (0.973)
  waiting for transfers between devices: 344 us -> 328 us
    all_to_all x9, waiting for transfers between devices: 61.2 us -> 48.4 us  [ctx_exchange(): lax.all_to_all(values, 'ctx', split_axis=0, concat_axis=0, tiled=True)]
    unnamed x205 -> x201, local copies, waits for them, and re-layouts: 44.3 us -> 34.9 us
  transfers between devices with their start and end apart: 56 -> 56, of which waited for: 19 -> 23; matrix products, arithmetic and copies ran while one was open for 24% -> 24% of each run, Pallas kernels for 13% -> 13%
where the time goes in v8:
time: 886 us; the launch traced here: 877 us
  waiting for transfers between devices  328 us (37%)
  Pallas kernels  181 us (20%)
  local copies, waits for them, and re-layouts  107 us (12%)
  other arithmetic  82.8 us (9%)
  starting transfers between devices  70.9 us (8%)
  matrix products  59.4 us (7%)
  blocking collectives  31.2 us (4%)
  between operations  16.2 us (2%)
    ppermute x40, waiting for transfers between devices, fsdp_swap(): lax.ppermute(values, 'fsdp', [(at, at ^ distance) for at in range(count)])  245 us
    pallas_call x13, Pallas kernels, expert_grad_call(): pl.pallas_call(functools.partial(expert_grad_body, each=len(each)), grid=...  60.5 us
    dot_general x12, matrix products, dot_f32(): lax.dot_general(left, right, (dims, ((), ())), preferred_element_type=jnp...  59.4 us
    pallas_call x1, Pallas kernels, experts_call(): pl.pallas_call(experts_body, grid=(count,), in_specs=[pl.BlockSpec((1, sl...  48.7 us
    all_to_all x9, waiting for transfers between devices, ctx_exchange(): lax.all_to_all(values, 'ctx', split_axis=0, concat_axis=0, tiled=True)  48.4 us
    all_to_all x9, starting transfers between devices, ctx_exchange(): lax.all_to_all(values, 'ctx', split_axis=0, concat_axis=0, tiled=True)  46.6 us
    unnamed x201, local copies, waits for them, and re-layouts  34.9 us
    all_gather x4, waiting for transfers between devices, ctx_gather(): return lax.all_gather(values, 'ctx', axis=0, tiled=True)  34.6 us
  transfers between devices with their start and end apart: 56, of which 23 were waited for; matrix products, arithmetic and copies ran while one was open for 24% of the time, Pallas kernels for 13%

profile of v8, /device:TPU:0, one launch (start us, length us, event | category | flops | bytes accessed | tf_op | source)
XLA Modules:
  0.0 876.6 jit_solution(4890401608979657623)
XLA Ops:
  12.8 7.3 all-to-all-start
  20.1 5.2 fusion.117
  26.8 31.7 %collective-permute-done = bf16[2,128,2816]{2,1,0:T(8,128)(2,1)} collective-permute-done((bf16[2,128,2816]{2,1,0:T(8,128)(2,1)S(1)}, bf16[2,128,2816]{2,1,0:T(8,128)(2,1)}, u32[]{:S(2)}, u32[]{:S(2)}) %collective-permute-start) | collective-permute-done | bytes 1441824 | tf_op jit(solution)/shard_map/ppermute | solution.py:242
  64.5 24.4 %collective-permute-done.2 = bf16[8,64,1088]{2,1,0:T(8,128)(2,1)S(1)} collective-permute-done((bf16[8,64,1088]{2,1,0:T(8,128)(2,1)S(1)}, bf16[8,64,1088]{2,1,0:T(8,128)(2,1)S(1)}, u32[]{:S(2)}, u32[]{:S(2)}) %collective-permute-start.2) | collective-permute-done | bytes 1114144 | tf_op jit(solution)/shard_map/ppermute | solution.py:242
  95.7 8.9 %all-gather.6.cloned.1.call-done = bf16[1024,2048]{1,0:T(8,128)(2,1)} async-done(((bf16[128,2048]{1,0:T(8,128)(2,1)}), bf16[1024,2048]{1,0:T(8,128)(2,1)}) %all-gather.6.cloned.1.call-update) | async-done | bytes 4194320 | tf_op jit(solution)/shard_map/all_gather | solution.py:292
  127.7 6.1 fusion.25
  143.8 13.8 %shard_map.212 = (bf16[1024,256]{1,0:T(8,128)(2,1)S(1)}, f32[2,1024,512]{2,1,0:T(8,128)}, f32[2,1024,1]{2,1,0:T(8,128)S(1)}) custom-call(bf16[1024,256]{1,0:T(8,128)(2,1)S(1)} %slice.305.nope_ref, bf16[2,1024,64]{2,1,0:T(8,128)(2,1)S(1)} %pad_maximum_fusion.17.rot_ref, bf16[1024,512]{1,0:T(8,128)(2,1)} %multiply_convert_fusion.1.lat_ref, ...), custom_call_target="tpu_custom_call" | custom-call | tf_op jit(solution)/shard_map/pallas_call | solution.py:406
  160.1 5.4 all-to-all-start.1
  170.9 18.7 %collective-permute-done.7 = bf16[2,128,2816]{2,1,0:T(8,128)(2,1)} collective-permute-done((bf16[2,128,2816]{2,1,0:T(8,128)(2,1)}, bf16[2,128,2816]{2,1,0:T(8,128)(2,1)}, u32[]{:S(2)}, u32[]{:S(2)}) %collective-permute-start.7) | collective-permute-done | bytes 1441824 | tf_op jit(solution)/shard_map/ppermute | solution.py:242
  196.5 28.6 %collective-permute-done.9 = bf16[2,128,2816]{2,1,0:T(8,128)(2,1)} collective-permute-done((bf16[2,128,2816]{2,1,0:T(8,128)(2,1)}, bf16[2,128,2816]{2,1,0:T(8,128)(2,1)}, u32[]{:S(2)}, u32[]{:S(2)}) %collective-permute-start.9) | collective-permute-done | bytes 1441824 | tf_op jit(solution)/shard_map/ppermute | solution.py:242
  238.7 16.9 %collective-permute-done.5 = bf16[8,64,1152]{2,1,0:T(8,128)(2,1)} collective-permute-done((bf16[8,64,1152]{2,1,0:T(8,128)(2,1)}, bf16[8,64,1152]{2,1,0:T(8,128)(2,1)}, u32[]{:S(2)}, u32[]{:S(2)}) %collective-permute-start.5) | collective-permute-done | bytes 1179680 | tf_op jit(solution)/shard_map/ppermute | solution.py:242
  261.4 6.4 multiply_reduce_fusion.5
  269.8 17.6 %all-gather.10.cloned.1.call-done = bf16[1024,2048]{1,0:T(8,128)(2,1)} async-done(((bf16[128,2048]{1,0:T(8,128)(2,1)}), bf16[1024,2048]{1,0:T(8,128)(2,1)}) %all-gather.10.cloned.1.call-update) | async-done | bytes 4194320 | tf_op jit(solution)/shard_map/all_gather | solution.py:292
  287.4 7.9 multiply_convert_fusion
  295.3 23.7 %collective-permute-done.15 = bf16[2,1408,512]{2,1,0:T(8,128)(2,1)} collective-permute-done((bf16[2,1408,512]{2,1,0:T(8,128)(2,1)}, bf16[2,1408,512]{2,1,0:T(8,128)(2,1)}, u32[]{:S(2)}, u32[]{:S(2)}) %collective-permute-start.15) | collective-permute-done | bytes 2883616 | tf_op jit(solution)/shard_map/ppermute | solution.py:242
  324.8 7.0 pad_maximum_fusion.5.gate_up_ref
  339.8 5.7 constant_dynamic-update-slice_fusion.gu_ref
  345.5 8.0 pad_maximum_fusion.dn_ref
  353.5 8.1 all-gather.12.cloned.1.call-done
  361.6 6.3 fusion.124
  372.1 5.8 convolution_convert_fusion.1
  378.0 48.7 %shard_map.213 = (bf16[2,432,1408]{2,1,0:T(8,128)(2,1)}, bf16[2,432,2816]{2,1,0:T(8,128)(2,1)}, bf16[2,432,2048]{2,1,0:T(8,128)(2,1)}, bf16[2,432,2048]{2,1,0:T(8,128)(2,1)}) custom-call(bf16[2,432,2048]{2,1,0:T(8,128)(2,1)} %bitcast.208, bf16[2,432,2048]{2,1,0:T(8,128)(2,1)} %bitcast.220, f32[2,432,1]{2,1,0:T(8,128)} %copy.472.gate_ref, ...), custom_call_target="tpu_custom_call" | custom-call | tf_op jit(solution)/shard_map/pallas_call | solution.py:518
  426.7 19.0 %shard_map.214 = bf16[1024,4096]{1,0:T(8,128)(2,1)} custom-call(bf16[1024,864]{1,0:T(8,128)(2,1)} %get-tuple-element.231.pick_ref, bf16[1024,768]{1,0:T(8,128)(2,1)S(1)} %pad_maximum_fusion.9.both_ref, bf16[1024,384]{1,0:T(8,128)(2,1)S(1)} %get-tuple-element.257.act_ref, bf16[864,2048]{1,0:T(8,128)(2,1)} %bitcast.239, bf16[864,2048]{1,0:T(8,128)(2,1)} %bitcast.238, ...), custom_call_target="tpu_custom_call" | custom-call | tf_op jit(solution)/shard_map/pallas_call | solution.py:652
  447.5 4.4 shard_map.215
  451.9 7.6 shard_map.216
  460.0 12.6 %collective-permute-done.19.refs_2_ = bf16[2,1408,512]{2,1,0:T(8,128)(2,1)S(1)} collective-permute-done((bf16[2,1408,512]{2,1,0:T(8,128)(2,1)S(1)}, bf16[2,1408,512]{2,1,0:T(8,128)(2,1)S(1)}, u32[]{:S(2)}, u32[]{:S(2)}) %collective-permute-start.19) | collective-permute-done | bytes 2883616 | tf_op jit(solution)/shard_map/ppermute | solution.py:242
  474.2 4.6 shard_map.217
  489.1 5.4 shard_map.218
  494.6 7.7 shard_map.221
  502.9 4.5 shard_map.220
  507.5 37.0 %collective-permute-done.23.refs_3_ = bf16[2,1408,512]{2,1,0:T(8,128)(2,1)} collective-permute-done((bf16[2,1408,512]{2,1,0:T(8,128)(2,1)}, bf16[2,1408,512]{2,1,0:T(8,128)(2,1)}, u32[]{:S(2)}, u32[]{:S(2)}) %collective-permute-start.23) | collective-permute-done | bytes 2883616 | tf_op jit(solution)/shard_map/ppermute | solution.py:242
  553.5 6.7 copy.473
  569.0 5.8 shard_map.222
  574.7 30.9 %collective-permute-done.20.refs_3_ = bf16[1,512,2816]{2,1,0:T(8,128)(2,1)S(1)} collective-permute-done((bf16[1,512,2816]{2,1,0:T(8,128)(2,1)}, bf16[1,512,2816]{2,1,0:T(8,128)(2,1)S(1)}, u32[]{:S(2)}, u32[]{:S(2)}) %collective-permute-start.20) | collective-permute-done | bytes 2883616 | tf_op jit(solution)/shard_map/ppermute | solution.py:242
  614.5 4.6 convolution_convert_fusion.2
  619.2 31.2 %all_to_all.54 = bf16[8,128,256]{2,1,0:T(8,128)(2,1)S(1)} all-to-all(bf16[8,128,256]{2,1,0:T(8,128)(2,1)S(1)} %bitcast.245), channel_id=1, replica_groups=mesh['ctx'=8,'fsdp'=4] {'ctx'}, dimensions={0} | all-to-all | bytes 1048576 | tf_op jit(solution)/shard_map/all_to_all | solution.py:300
  650.4 24.8 %shard_map.223 = (bf16[1024,256]{1,0:T(8,128)(2,1)S(1)}, f32[2,1024,64]{2,1,0:T(8,128)}, f32[2,512,256]{2,1,0:T(8,128)}, f32[1024,512]{1,0:T(8,128)}, f32[1024,64]{1,0:T(8,128)S(1)}) custom-call(bf16[1024,256]{1,0:T(8,128)(2,1)S(1)} %bitcast.219, bf16[1024,256]{1,0:T(8,128)(2,1)S(1)} %copy-done.12, bf16[2,1024,64]{2,1,0:T(8,128)(2,1)S(1)} %copy-done.10, ...), custom_call_target="tpu_custom_call" | custom-call | tf_op jit(solution)/shard_map/pallas_call | solution.py:441
  682.4 6.0 fusion.3
  692.2 4.7 all-to-all-start.5
  727.6 17.0 %all-to-all-done.5 = bf16[8,128,576]{1,2,0:T(8,128)(2,1)} async-done(((bf16[8,128,576]{1,2,0:T(8,128)(2,1)}), bf16[8,128,576]{1,2,0:T(8,128)(2,1)}, u32[]{:S(2)}, u32[]{:S(2)}) %all-to-all-start.5) | async-done | bytes 1179680 | tf_op jit(solution)/shard_map/all_to_all | solution.py:300
  746.5 4.7 all-to-all-start.7
  758.1 14.7 %all-to-all-done.7 = bf16[8,64,640]{2,1,0:T(8,128)(2,1)} async-done(((bf16[8,64,640]{2,1,0:T(8,128)(2,1)}), bf16[8,64,640]{2,1,0:T(8,128)(2,1)}, u32[]{:S(2)}, u32[]{:S(2)}) %all-to-all-start.7) | async-done | bytes 655392 | tf_op jit(solution)/shard_map/all_to_all | solution.py:300
  772.8 4.7 all-to-all-start.9
  796.6 11.3 %collective-permute-done.32.refs_3_ = bf16[1,512,640]{2,1,0:T(8,128)(2,1)S(1)} collective-permute-done((bf16[1,512,640]{2,1,0:T(8,128)(2,1)S(1)}, bf16[1,512,640]{2,1,0:T(8,128)(2,1)S(1)}, u32[]{:S(2)}, u32[]{:S(2)}) %collective-permute-start.32) | collective-permute-done | bytes 655392 | tf_op jit(solution)/shard_map/ppermute | solution.py:242
  817.4 6.2 all-to-all-start.6
  832.9 11.9 %shard_map.233 = f32[2,512,2816]{2,1,0:T(8,128)} custom-call(bf16[2,432,2048]{2,1,0:T(8,128)(2,1)} %bitcast.211, bf16[2,432,2816]{2,1,0:T(8,128)(2,1)} %get-tuple-element.95.refs_1_, bf16[2,512,2816]{2,1,0:T(8,128)(2,1)} %collective-permute-done.22.refs_2_, bf16[1,512,2816]{2,1,0:T(8,128)(2,1)S(1)} %copy-done.14, ...), custom_call_target="tpu_custom_call" | custom-call | tf_op jit(solution)/shard_map/pallas_call | solution.py:555
  844.8 6.0 all-to-all-start.8
  855.7 11.9 %all-to-all-done.8 = bf16[8,64,640]{2,1,0:T(8,128)(2,1)} async-done(((bf16[8,64,640]{2,1,0:T(8,128)(2,1)}), bf16[8,64,640]{2,1,0:T(8,128)(2,1)}, u32[]{:S(2)}, u32[]{:S(2)}) %all-to-all-start.8) | async-done | bytes 655392 | tf_op jit(solution)/shard_map/all_to_all | solution.py:300
  (492 shorter events, 242.2 us)
Async XLA Ops:
  7.2 97.4 %all-gather.6.cloned.1.call-start = ((), (), s32[]{:S(2)}) async-start(), calls=%async_computation.12 | async-start | bytes 4718592 | tf_op jit(solution)/shard_map/all_gather | solution.py:292
  12.8 49.9 %all-to-all-start = ((bf16[8,64,960]{2,1,0:T(8,128)(2,1)}), bf16[8,64,960]{2,1,0:T(8,128)(2,1)S(1)}, u32[]{:S(2)}, u32[]{:S(2)}) async-start(bf16[8,64,960]{2,1,0:T(8,128)(2,1)} %pad_maximum_fusion.12), calls=%async_computation | async-start | bytes 2097152 | tf_op jit(solution)/shard_map/all_to_all | solution.py:300
  20.1 241.3 %all-gather.8.cloned.1.call-start = ((), (), s32[]{:S(2)}) async-start(), calls=%async_computation.13 | async-start | bytes 8650752 | tf_op jit(solution)/shard_map/all_gather | solution.py:918
  25.4 33.1 %collective-permute-start = (bf16[2,128,2816]{2,1,0:T(8,128)(2,1)S(1)}, bf16[2,128,2816]{2,1,0:T(8,128)(2,1)}, u32[]{:S(2)}, u32[]{:S(2)}) collective-permute-start(bf16[2,128,2816]{2,1,0:T(8,128)(2,1)S(1)} %get-tuple-element.238), channel_id=1, source_target_pairs={{0,2},{1,3},{2,0},{3,1},{4,6},{5,7},{6,4},{7,5},{8,10},{9,11},{10,... | collective-permute-start | bytes 4325384 | tf_op jit(solution)/shard_map/ppermute | solution.py:242
  62.9 26.0 %collective-permute-start.2 = (bf16[8,64,1088]{2,1,0:T(8,128)(2,1)S(1)}, bf16[8,64,1088]{2,1,0:T(8,128)(2,1)S(1)}, u32[]{:S(2)}, u32[]{:S(2)}) collective-permute-start(bf16[8,64,1088]{2,1,0:T(8,128)(2,1)S(1)} %pad_maximum_fusion.10), channel_id=1, source_target_pairs={{0,2},{1,3},{2,0},{3,1},{4,6},{5,7},{6,4},{7,5},{8,10},{9,11},{10,... | collective-permute-start | bytes 3342344 | tf_op jit(solution)/shard_map/ppermute | solution.py:242
  64.5 24.4 %collective-permute-start.1 = (bf16[8,64,1088]{2,1,0:T(8,128)(2,1)S(1)}, bf16[8,64,1088]{2,1,0:T(8,128)(2,1)S(1)}, u32[]{:S(2)}, u32[]{:S(2)}) collective-permute-start(bf16[8,64,1088]{2,1,0:T(8,128)(2,1)S(1)} %pad_maximum_fusion.10), channel_id=1, source_target_pairs={{0,1},{1,0},{2,3},{3,2},{4,5},{5,4},{6,7},{7,6},{8,9},{9,8},{10,11... | collective-permute-start | bytes 3342344 | tf_op jit(solution)/shard_map/ppermute | solution.py:242
  104.6 235.2 %collective-permute-start.14 = (bf16[2,512,2816]{2,1,0:T(8,128)(2,1)}, bf16[2,512,2816]{2,1,0:T(8,128)(2,1)}, u32[]{:S(2)}, u32[]{:S(2)}) collective-permute-start(bf16[2,512,2816]{2,1,0:T(8,128)(2,1)} %param.22), channel_id=1, source_target_pairs={{0,1},{1,0},{2,3},{3,2},{4,5},{5,4},{6,7},{7,6},{8,9},{9,8},{10,11... | collective-permute-start | bytes 17301512 | tf_op jit(solution)/shard_map/ppermute | solution.py:242
  104.7 63.4 %collective-permute-start.8 = (bf16[2,128,2816]{2,1,0:T(8,128)(2,1)}, bf16[2,128,2816]{2,1,0:T(8,128)(2,1)}, u32[]{:S(2)}, u32[]{:S(2)}) collective-permute-start(bf16[2,128,2816]{2,1,0:T(8,128)(2,1)} %get-tuple-element.236), channel_id=1, source_target_pairs={{0,2},{1,3},{2,0},{3,1},{4,6},{5,7},{6,4},{7,5},{8,10},{9,11},{10,... | collective-permute-start | bytes 4325384 | tf_op jit(solution)/shard_map/ppermute | solution.py:242
  106.2 83.5 %collective-permute-start.7 = (bf16[2,128,2816]{2,1,0:T(8,128)(2,1)}, bf16[2,128,2816]{2,1,0:T(8,128)(2,1)}, u32[]{:S(2)}, u32[]{:S(2)}) collective-permute-start(bf16[2,128,2816]{2,1,0:T(8,128)(2,1)} %get-tuple-element.237), channel_id=1, source_target_pairs={{0,2},{1,3},{2,0},{3,1},{4,6},{5,7},{6,4},{7,5},{8,10},{9,11},{10,... | collective-permute-start | bytes 4325384 | tf_op jit(solution)/shard_map/ppermute | solution.py:242
  106.8 118.3 %collective-permute-start.9 = (bf16[2,128,2816]{2,1,0:T(8,128)(2,1)}, bf16[2,128,2816]{2,1,0:T(8,128)(2,1)}, u32[]{:S(2)}, u32[]{:S(2)}) collective-permute-start(bf16[2,128,2816]{2,1,0:T(8,128)(2,1)} %get-tuple-element.235), channel_id=1, source_target_pairs={{0,2},{1,3},{2,0},{3,1},{4,6},{5,7},{6,4},{7,5},{8,10},{9,11},{10,... | collective-permute-start | bytes 4325384 | tf_op jit(solution)/shard_map/ppermute | solution.py:242
  108.2 237.2 %collective-permute-start.17 = (bf16[2,1408,512]{2,1,0:T(8,128)(2,1)}, bf16[2,1408,512]{2,1,0:T(8,128)(2,1)}, u32[]{:S(2)}, u32[]{:S(2)}) collective-permute-start(bf16[2,1408,512]{2,1,0:T(8,128)(2,1)} %param.23), channel_id=1, source_target_pairs={{0,1},{1,0},{2,3},{3,2},{4,5},{5,4},{6,7},{7,6},{8,9},{9,8},{10,11... | collective-permute-start | bytes 8650760 | tf_op jit(solution)/shard_map/ppermute | solution.py:242
  116.4 43.8 %all-to-all-start.2 = ((bf16[8,64,1152]{2,1,0:T(8,128)(2,1)}), bf16[8,64,1152]{2,1,0:T(8,128)(2,1)}, u32[]{:S(2)}, u32[]{:S(2)}) async-start(bf16[8,64,1152]{2,1,0:T(8,128)(2,1)} %fusion.32), calls=%async_computation.2 | async-start | bytes 2359296 | tf_op jit(solution)/shard_map/all_to_all | solution.py:300
  120.7 166.7 %all-gather.10.cloned.1.call-start = ((), (), s32[]{:S(2)}) async-start(), calls=%async_computation.14 | async-start | bytes 4718592 | tf_op jit(solution)/shard_map/all_gather | solution.py:292
  160.1 32.7 %all-to-all-start.1 = ((bf16[8,128,256]{1,2,0:T(8,128)(2,1)}), bf16[8,128,256]{1,2,0:T(8,128)(2,1)S(1)}, u32[]{:S(2)}, u32[]{:S(2)}) async-start(bf16[8,128,256]{1,2,0:T(8,128)(2,1)} %copy.456), calls=%async_computation.1 | async-start | bytes 1048576 | tf_op jit(solution)/shard_map/all_to_all | solution.py:300
  192.8 36.3 %all-to-all-start.3 = ((bf16[8,128,24]{1,2,0:T(8,128)(2,1)}), bf16[8,128,24]{1,2,0:T(8,128)(2,1)S(1)}, u32[]{:S(2)}, u32[]{:S(2)}) async-start(bf16[8,128,24]{1,2,0:T(8,128)(2,1)} %broadcast_in_dim.45), calls=%async_computation.3 | async-start | bytes 98304 | tf_op jit(solution)/shard_map/all_to_all | solution.py:300
  196.3 165.3 %all-gather.12.cloned.1.call-start = ((), (), s32[]{:S(2)}) async-start(), calls=%async_computation.15 | async-start | bytes 4718592 | tf_op jit(solution)/shard_map/all_gather | solution.py:292
  227.7 27.8 %collective-permute-start.5 = (bf16[8,64,1152]{2,1,0:T(8,128)(2,1)}, bf16[8,64,1152]{2,1,0:T(8,128)(2,1)}, u32[]{:S(2)}, u32[]{:S(2)}) collective-permute-start(bf16[8,64,1152]{2,1,0:T(8,128)(2,1)} %all-to-all-done.2), channel_id=1, source_target_pairs={{0,2},{1,3},{2,0},{3,1},{4,6},{5,7},{6,4},{7,5},{8,10},{9,11},{10,... | collective-permute-start | bytes 3538952 | tf_op jit(solution)/shard_map/ppermute | solution.py:242
  229.2 89.8 %collective-permute-start.4 = (bf16[8,64,1152]{2,1,0:T(8,128)(2,1)}, bf16[8,64,1152]{2,1,0:T(8,128)(2,1)}, u32[]{:S(2)}, u32[]{:S(2)}) collective-permute-start(bf16[8,64,1152]{2,1,0:T(8,128)(2,1)} %all-to-all-done.2), channel_id=1, source_target_pairs={{0,1},{1,0},{2,3},{3,2},{4,5},{5,4},{6,7},{7,6},{8,9},{9,8},{10,11... | collective-permute-start | bytes 3538952 | tf_op jit(solution)/shard_map/ppermute | solution.py:242
  255.5 63.5 %collective-permute-start.15 = (bf16[2,1408,512]{2,1,0:T(8,128)(2,1)}, bf16[2,1408,512]{2,1,0:T(8,128)(2,1)}, u32[]{:S(2)}, u32[]{:S(2)}) collective-permute-start(bf16[2,1408,512]{2,1,0:T(8,128)(2,1)} %param.23), channel_id=1, source_target_pairs={{0,2},{1,3},{2,0},{3,1},{4,6},{5,7},{6,4},{7,5},{8,10},{9,11},{10,... | collective-permute-start | bytes 8650760 | tf_op jit(solution)/shard_map/ppermute | solution.py:242
  267.8 51.7 %collective-permute-start.6 = (bf16[8,64,1152]{2,1,0:T(8,128)(2,1)}, bf16[8,64,1152]{2,1,0:T(8,128)(2,1)S(1)}, u32[]{:S(2)}, u32[]{:S(2)}) collective-permute-start(bf16[8,64,1152]{2,1,0:T(8,128)(2,1)} %collective-permute-done.5), channel_id=1, source_target_pairs={{0,1},{1,0},{2,3},{3,2},{4,5},{5,4},{6,7},{7,6},{8,9},{9,8},{10,11... | collective-permute-start | bytes 3538952 | tf_op jit(solution)/shard_map/ppermute | solution.py:242
  287.4 318.3 %reduce-scatter.3.cloned.1.call-start = ((), (), s32[]{:S(2)}) async-start(), calls=%async_computation.16 | async-start | bytes 9437184 | tf_op jit(solution)/shard_map/reduce_scatter | solution.py:296
  319.0 5.5 collective-permute-start.11
  319.5 14.7 %collective-permute-start.12 = (bf16[2,128,2816]{2,1,0:T(8,128)(2,1)}, bf16[2,128,2816]{2,1,0:T(8,128)(2,1)S(1)}, u32[]{:S(2)}, u32[]{:S(2)}) collective-permute-start(bf16[2,128,2816]{2,1,0:T(8,128)(2,1)} %collective-permute-done.7), channel_id=1, source_target_pairs={{0,1},{1,0},{2,3},{3,2},{4,5},{5,4},{6,7},{7,6},{8,9},{9,8},{10,11... | collective-permute-start | bytes 4325384 | tf_op jit(solution)/shard_map/ppermute | solution.py:242
  323.7 11.8 %collective-permute-start.13 = (bf16[2,128,2816]{2,1,0:T(8,128)(2,1)}, bf16[2,128,2816]{2,1,0:T(8,128)(2,1)S(1)}, u32[]{:S(2)}, u32[]{:S(2)}) collective-permute-start(bf16[2,128,2816]{2,1,0:T(8,128)(2,1)} %collective-permute-done.9), channel_id=1, source_target_pairs={{0,1},{1,0},{2,3},{3,2},{4,5},{5,4},{6,7},{7,6},{8,9},{9,8},{10,11... | collective-permute-start | bytes 4325384 | tf_op jit(solution)/shard_map/ppermute | solution.py:242
  324.5 21.0 %collective-permute-start.16 = (bf16[2,1408,512]{2,1,0:T(8,128)(2,1)}, bf16[2,1408,512]{2,1,0:T(8,128)(2,1)S(1)}, u32[]{:S(2)}, u32[]{:S(2)}) collective-permute-start(bf16[2,1408,512]{2,1,0:T(8,128)(2,1)} %collective-permute-done.15), channel_id=1, source_target_pairs={{0,1},{1,0},{2,3},{3,2},{4,5},{5,4},{6,7},{7,6},{8,9},{9,8},{10,11... | collective-permute-start | bytes 8650760 | tf_op jit(solution)/shard_map/ppermute | solution.py:242
  445.8 251.1 %all-gather.14.cloned.1.call-start = ((), (), s32[]{:S(2)}) async-start(), calls=%async_computation.18 | async-start | bytes 4718592 | tf_op jit(solution)/shard_map/all_gather | solution.py:292
  459.5 20.9 %collective-permute-start.18 = (bf16[2,512,2816]{2,1,0:T(8,128)(2,1)}, bf16[2,512,2816]{2,1,0:T(8,128)(2,1)S(1)}, u32[]{:S(2)}, u32[]{:S(2)}) collective-permute-start(bf16[2,512,2816]{2,1,0:T(8,128)(2,1)} %shard_map.216), channel_id=1, source_target_pairs={{0,1},{1,0},{2,3},{3,2},{4,5},{5,4},{6,7},{7,6},{8,9},{9,8},{10,11... | collective-permute-start | bytes 17301512 | tf_op jit(solution)/shard_map/ppermute | solution.py:242
  459.5 13.2 %collective-permute-start.19 = (bf16[2,1408,512]{2,1,0:T(8,128)(2,1)S(1)}, bf16[2,1408,512]{2,1,0:T(8,128)(2,1)S(1)}, u32[]{:S(2)}, u32[]{:S(2)}) collective-permute-start(bf16[2,1408,512]{2,1,0:T(8,128)(2,1)S(1)} %copy-done.37), channel_id=1, source_target_pairs={{0,1},{1,0},{2,3},{3,2},{4,5},{5,4},{6,7},{7,6},{8,9},{9,8},{10,11... | collective-permute-start | bytes 8650760 | tf_op jit(solution)/shard_map/ppermute | solution.py:242
  478.8 65.6 %collective-permute-start.23 = (bf16[2,1408,512]{2,1,0:T(8,128)(2,1)}, bf16[2,1408,512]{2,1,0:T(8,128)(2,1)}, u32[]{:S(2)}, u32[]{:S(2)}) collective-permute-start(bf16[2,1408,512]{2,1,0:T(8,128)(2,1)} %shard_map.217), channel_id=1, source_target_pairs={{0,2},{1,3},{2,0},{3,1},{4,6},{5,7},{6,4},{7,5},{8,10},{9,11},{10,... | collective-permute-start | bytes 8650760 | tf_op jit(solution)/shard_map/ppermute | solution.py:242
  502.3 103.4 %collective-permute-start.22 = (bf16[2,512,2816]{2,1,0:T(8,128)(2,1)}, bf16[2,512,2816]{2,1,0:T(8,128)(2,1)}, u32[]{:S(2)}, u32[]{:S(2)}) collective-permute-start(bf16[2,512,2816]{2,1,0:T(8,128)(2,1)} %shard_map.221), channel_id=1, source_target_pairs={{0,1},{1,0},{2,3},{3,2},{4,5},{5,4},{6,7},{7,6},{8,9},{9,8},{10,11... | collective-permute-start | bytes 17301512 | tf_op jit(solution)/shard_map/ppermute | solution.py:242
  502.3 103.4 %collective-permute-start.20 = (bf16[1,512,2816]{2,1,0:T(8,128)(2,1)}, bf16[1,512,2816]{2,1,0:T(8,128)(2,1)S(1)}, u32[]{:S(2)}, u32[]{:S(2)}) collective-permute-start(bf16[1,512,2816]{2,1,0:T(8,128)(2,1)} %shard_map.218), channel_id=1, source_target_pairs={{0,2},{1,3},{2,0},{3,1},{4,6},{5,7},{6,4},{7,5},{8,10},{9,11},{10,... | collective-permute-start | bytes 8650760 | tf_op jit(solution)/shard_map/ppermute | solution.py:242
  507.4 61.5 %collective-permute-start.21 = (bf16[2,1408,512]{2,1,0:T(8,128)(2,1)}, bf16[2,1408,512]{2,1,0:T(8,128)(2,1)}, u32[]{:S(2)}, u32[]{:S(2)}) collective-permute-start(bf16[2,1408,512]{2,1,0:T(8,128)(2,1)} %shard_map.220), channel_id=1, source_target_pairs={{0,1},{1,0},{2,3},{3,2},{4,5},{5,4},{6,7},{7,6},{8,9},{9,8},{10,11... | collective-permute-start | bytes 8650760 | tf_op jit(solution)/shard_map/ppermute | solution.py:242
  612.8 238.6 %reduce-scatter.5.cloned.1.call-start = ((), (), s32[]{:S(2)}) async-start(), calls=%async_computation.17 | async-start | bytes 4718592 | tf_op jit(solution)/shard_map/reduce_scatter | solution.py:296
  612.9 69.5 %collective-permute-start.26 = (bf16[1,512,2816]{2,1,0:T(8,128)(2,1)}, bf16[1,512,2816]{2,1,0:T(8,128)(2,1)}, u32[]{:S(2)}, u32[]{:S(2)}) collective-permute-start(bf16[1,512,2816]{2,1,0:T(8,128)(2,1)} %copy-done.15), channel_id=1, source_target_pairs={{0,2},{1,3},{2,0},{3,1},{4,6},{5,7},{6,4},{7,5},{8,10},{9,11},{10,... | collective-permute-start | bytes 8650760 | tf_op jit(solution)/shard_map/ppermute | solution.py:242
  692.2 52.4 %all-to-all-start.5 = ((bf16[8,128,576]{1,2,0:T(8,128)(2,1)}), bf16[8,128,576]{1,2,0:T(8,128)(2,1)}, u32[]{:S(2)}, u32[]{:S(2)}) async-start(bf16[8,128,576]{1,2,0:T(8,128)(2,1)} %pad_maximum_fusion.11), calls=%async_computation.7 | async-start | bytes 2359296 | tf_op jit(solution)/shard_map/all_to_all | solution.py:300
  702.1 19.7 %collective-permute-start.27 = (bf16[512,640]{1,0:T(8,128)(2,1)S(1)}, bf16[512,640]{1,0:T(8,128)(2,1)S(1)}, u32[]{:S(2)}, u32[]{:S(2)}) collective-permute-start(bf16[512,640]{1,0:T(8,128)(2,1)S(1)} %shard_map.224), channel_id=1, source_target_pairs={{0,1},{1,0},{2,3},{3,2},{4,5},{5,4},{6,7},{7,6},{8,9},{9,8},{10,11... | collective-permute-start | bytes 1966088 | tf_op jit(solution)/shard_map/ppermute | solution.py:242
  706.1 17.9 %collective-permute-start.29 = (bf16[512,640]{1,0:T(8,128)(2,1)}, bf16[512,640]{1,0:T(8,128)(2,1)}, u32[]{:S(2)}, u32[]{:S(2)}) collective-permute-start(bf16[512,640]{1,0:T(8,128)(2,1)} %shard_map.226), channel_id=1, source_target_pairs={{0,2},{1,3},{2,0},{3,1},{4,6},{5,7},{6,4},{7,5},{8,10},{9,11},{10,... | collective-permute-start | bytes 1966088 | tf_op jit(solution)/shard_map/ppermute | solution.py:242
  709.7 45.8 %collective-permute-start.39 = (bf16[8,64,1152]{2,1,0:T(8,128)(2,1)}, bf16[8,64,1152]{2,1,0:T(8,128)(2,1)}, u32[]{:S(2)}, u32[]{:S(2)}) collective-permute-start(bf16[8,64,1152]{2,1,0:T(8,128)(2,1)} %get-tuple-element.126), channel_id=1, source_target_pairs={{0,2},{1,3},{2,0},{3,1},{4,6},{5,7},{6,4},{7,5},{8,10},{9,11},{10,... | collective-permute-start | bytes 3538952 | tf_op jit(solution)/shard_map/ppermute | solution.py:242
  721.2 56.3 %collective-permute-start.37 = (bf16[512,128]{1,0:T(8,128)(2,1)}, bf16[512,128]{1,0:T(8,128)(2,1)S(1)}, u32[]{:S(2)}, u32[]{:S(2)}) collective-permute-start(bf16[512,128]{1,0:T(8,128)(2,1)} %bitcast.274), channel_id=1, source_target_pairs={{0,1},{1,0},{2,3},{3,2},{4,5},{5,4},{6,7},{7,6},{8,9},{9,8},{10,11... | collective-permute-start | bytes 393224 | tf_op jit(solution)/shard_map/ppermute | solution.py:242
  721.2 66.1 %collective-permute-start.36 = (bf16[512,128]{1,0:T(8,128)(2,1)}, bf16[512,128]{1,0:T(8,128)(2,1)}, u32[]{:S(2)}, u32[]{:S(2)}) collective-permute-start(bf16[512,128]{1,0:T(8,128)(2,1)} %bitcast.273), channel_id=1, source_target_pairs={{0,1},{1,0},{2,3},{3,2},{4,5},{5,4},{6,7},{7,6},{8,9},{9,8},{10,11... | collective-permute-start | bytes 393224 | tf_op jit(solution)/shard_map/ppermute | solution.py:242
  746.5 26.3 %all-to-all-start.7 = ((bf16[8,64,640]{2,1,0:T(8,128)(2,1)}), bf16[8,64,640]{2,1,0:T(8,128)(2,1)}, u32[]{:S(2)}, u32[]{:S(2)}) async-start(bf16[8,64,640]{2,1,0:T(8,128)(2,1)} %bitcast.80), calls=%async_computation.9 | async-start | bytes 1310720 | tf_op jit(solution)/shard_map/all_to_all | solution.py:300
  755.4 34.9 %collective-permute-start.31 = (bf16[1,512,640]{2,1,0:T(8,128)(2,1)S(1)}, bf16[1,512,640]{2,1,0:T(8,128)(2,1)S(1)}, u32[]{:S(2)}, u32[]{:S(2)}) collective-permute-start(bf16[1,512,640]{2,1,0:T(8,128)(2,1)S(1)} %shard_map.229), channel_id=1, source_target_pairs={{0,1},{1,0},{2,3},{3,2},{4,5},{5,4},{6,7},{7,6},{8,9},{9,8},{10,11... | collective-permute-start | bytes 1966088 | tf_op jit(solution)/shard_map/ppermute | solution.py:242
  772.8 44.6 %all-to-all-start.9 = ((bf16[8,64,1152]{2,1,0:T(8,128)(2,1)}), bf16[8,64,1152]{2,1,0:T(8,128)(2,1)S(1)}, u32[]{:S(2)}, u32[]{:S(2)}) async-start(bf16[8,64,1152]{2,1,0:T(8,128)(2,1)} %add_convert_fusion), calls=%async_computation.11 | async-start | bytes 2359296 | tf_op jit(solution)/shard_map/all_to_all | solution.py:300
  778.2 9.1 %collective-permute-start.38 = (bf16[512,128]{1,0:T(8,128)(2,1)}, bf16[512,128]{1,0:T(8,128)(2,1)}, u32[]{:S(2)}, u32[]{:S(2)}) collective-permute-start(bf16[512,128]{1,0:T(8,128)(2,1)} %add_convert_fusion.2), channel_id=1, source_target_pairs={{0,2},{1,3},{2,0},{3,1},{4,6},{5,7},{6,4},{7,5},{8,10},{9,11},{10,... | collective-permute-start | bytes 393224 | tf_op jit(solution)/shard_map/ppermute | solution.py:242
  790.3 6.2 collective-permute-start.30
  790.7 17.2 %collective-permute-start.32 = (bf16[1,512,640]{2,1,0:T(8,128)(2,1)S(1)}, bf16[1,512,640]{2,1,0:T(8,128)(2,1)S(1)}, u32[]{:S(2)}, u32[]{:S(2)}) collective-permute-start(bf16[1,512,640]{2,1,0:T(8,128)(2,1)S(1)} %shard_map.230), channel_id=1, source_target_pairs={{0,2},{1,3},{2,0},{3,1},{4,6},{5,7},{6,4},{7,5},{8,10},{9,11},{10,... | collective-permute-start | bytes 1966088 | tf_op jit(solution)/shard_map/ppermute | solution.py:242
  817.4 27.4 %all-to-all-start.6 = ((f32[8,1,144]{2,1,0:T(1,128)}), f32[8,1,144]{2,1,0:T(1,128)S(1)}, u32[]{:S(2)}, u32[]{:S(2)}) async-start(f32[8,1,144]{2,1,0:T(1,128)} %all_to_all.39), calls=%async_computation.8 | async-start | bytes 16384 | tf_op jit(solution)/shard_map/all_to_all | solution.py:300
  844.8 22.9 %all-to-all-start.8 = ((bf16[8,64,640]{2,1,0:T(8,128)(2,1)}), bf16[8,64,640]{2,1,0:T(8,128)(2,1)}, u32[]{:S(2)}, u32[]{:S(2)}) async-start(bf16[8,64,640]{2,1,0:T(8,128)(2,1)} %bitcast.82), calls=%async_computation.10 | async-start | bytes 1310720 | tf_op jit(solution)/shard_map/all_to_all | solution.py:300
  (97 other events, 1441.1 us)
Sparse Core Ops, SparseCore 0:
  10.7 93.7 all-gather.5
  107.4 105.2 all-gather.7
  215.5 71.8 all-gather.9
  289.9 71.6 all-gather.11
  445.9 147.2 reduce-scatter.2
  612.9 83.1 all-gather.13
  700.1 123.8 reduce-scatter.4

commit v9 on v8

--- a/solution.py
+++ b/solution.py
@@ -807,12 +807,11 @@
 
     dn_send = dn_term(3, jnp.bfloat16)
     dn_got = fsdp_swap(dn_send, 1)
-    x_late = after(x_late, dn_send)
+    dn_other = dn_term(2, jnp.bfloat16, dn_got)
+    dn_back = fsdp_swap(dn_other, 2)
+    x_late = after(x_late, dn_other)
     gu_send = gu_term(3, jnp.bfloat16)
     gu_got = fsdp_swap(gu_send, 1)
-    dn_other = dn_term(2, jnp.bfloat16, after(dn_got, gu_send))
-    dn_back = fsdp_swap(dn_other, 2)
-    gu_got = after(gu_got, dn_other)
     gu_other = [gu_term(2, jnp.bfloat16, gu_got[e : e + 1], only=e) for e in range(exp_local)]
     gu_back = [fsdp_swap(v, 2) for v in gu_other]
     x_late, y_late, act_late = after((x_late, y_late, act_late), gu_other)
@@ -838,18 +837,20 @@
     resid_norm_grad, gain_mid_grad = norm_backward(resid_mid, inv_mid, gain_mid, mid_grad)
     resid_grad = out_grad[0].astype(jnp.float32) + resid_norm_grad
 
-    def reduce_gains(gain_in_grad, gain_lat_grad, *first):
+    def reduce_gains(gain_in_grad, gain_lat_grad, first=(), second=()):
         gains = jnp.concatenate([gain_in_grad, gain_mid_grad, gain_lat_grad], 0)
-        gains = fsdp_reduce(gains.reshape(n_ctx, 4, -1).transpose(1, 0, 2), rank, *first)
-        return jnp.sum(ctx_exchange(gains), 0)
+        gains = fsdp_reduce(gains.reshape(n_ctx, 4, -1).transpose(1, 0, 2), rank, first)
+        return jnp.sum(ctx_exchange(after(gains, second)), 0)
+
+    def exchange_shared(early, late):
+        far = fsdp_swap(after(shared_other, early), 2)
+        total = shared_own.astype(jnp.float32) + far.astype(jnp.float32)
+        return ctx_exchange(after(total.astype(jnp.bfloat16), late))
 
     token_grad, stage, gains_grad, query_w, latent_w, expand_w, output_w = attn_backward(
-        resid_grad.astype(jnp.bfloat16), gu_back[1:], reduce_gains
-    )
-    part_there, keys_there, sums_there = stage
-    shared_far = fsdp_swap(after(shared_other, part_there), 2)
-    shared_term = shared_own.astype(jnp.float32) + shared_far.astype(jnp.float32)
-    shared_sums = ctx_exchange(after(shared_term.astype(jnp.bfloat16), keys_there))
+        resid_grad.astype(jnp.bfloat16), gu_back[1:], reduce_gains, exchange_shared
+    )
+    shared_sums, sums_there = stage
     shared_gu_grad, shared_dn_grad = shared_unpack_call(
         after(shared_sums, sums_there), sff_dev, sff_pad
     )
@@ -949,7 +950,7 @@
         own_heads = ctx_exchange(heads_out).transpose(1, 0, 2).reshape(tok_dev, H * DV)
         return tokens + dot_f32(after(own_heads, early), saved["output_full"])
 
-    def backward(resid_bf, stages, reduce_gains):
+    def backward(resid_bf, stages, reduce_gains, exchange_shared):
         query_full, latent_full = saved["query_full"], saved["latent_full"]
         cos_table, sin_table = saved["cos_table"], saved["sin_table"]
         normed_bf = saved["normed_bf"]
@@ -1005,24 +1006,25 @@
 
         latent_sent, latent_w = fsdp_reduce_terms(latent_terms)
         latent_own = latent_w
-        latent_w = ctx_exchange(latent_w.reshape(n_ctx, rows, lat_wide))
-        latent_w = jnp.sum(after(latent_w, in_grad).astype(jnp.float32), 0)[:, : KVL + DR]
+        latent_got = ctx_exchange(latent_w.reshape(n_ctx, rows, lat_wide))
+        latent_w = jnp.sum(latent_got.astype(jnp.float32), 0)[:, : KVL + DR]
         inv_in = own_rows(saved["inv_all"])
         in_own = dot_f32(compressed_grad, latent_full, ((1,), (1,)))
         token_cols = columns_by_distance(tokens, n_ctx, rank)
         gain_in_grad = gain_in_grad + jnp.sum(in_own * (token_cols * inv_in), 0)
         gain_in_grad = columns_in_order(gain_in_grad[None], n_ctx, rank)[0]
-        gains_grad = reduce_gains(gain_in_grad, gain_lat_grad, latent_own)
+        gains_grad = reduce_gains(gain_in_grad, gain_lat_grad, latent_own, latent_got)
         expand_g = expand_g.transpose(1, 0, 2)
         expand_blocks = expand_g.reshape(KVL, 4, -1).transpose(1, 0, 2).astype(jnp.bfloat16)
         expand_w = fsdp_reduce(expand_blocks, rank)
         nope_w = query_terms[:, :, :n_wide].reshape(n_ctx, rows, heads, DN)
         rot_w = query_terms[:, :, n_wide:].reshape(n_ctx, rows, heads, DR)
         query_w = jnp.concatenate([nope_w, rot_w], -1).transpose(1, 0, 2, 3).reshape(rows, -1)
-        in_grad = after(in_grad, gains_grad).astype(jnp.float32) + in_own
+        shared_sums = exchange_shared(in_part, latent_sent)
+        in_grad = after(in_grad, shared_sums).astype(jnp.float32) + in_own
         token_grad = norm_backward(token_cols, inv_in, saved["gain_cols"], in_grad)[0]
         token_grad = columns_in_order(token_grad, n_ctx, rank)
-        stage = (in_part, key_sent, latent_own)
+        stage = (shared_sums, latent_own)
         return token_grad, stage, gains_grad, query_w, latent_w, expand_w, output_w
 
     return first, middle, backward
@@ -1082,7 +1084,7 @@
     )
     resid_mid = tokens + dot_f32(heads_out, output_full)
 
-    def backward(resid_bf, stages, reduce_gains):
+    def backward(resid_bf, stages, reduce_gains, exchange_shared):
         output_g = dot_f32(heads_out, resid_bf, ((0,), (0,)))
         heads_grad = (
             dot_f32(resid_bf, output_full, ((1,), (1,)))
@@ -1146,7 +1148,7 @@
             for g, at in ((query_g, 0), (latent_g, 0), (expand_g, 1), (output_g, 1))
         ]
         gains_grad = reduce_gains(gain_in_grad, gain_lat_grad)
-        return (token_grad, (resid_bf, lat_buffer, latent_grad), gains_grad, *scattered)
+        return (token_grad, (exchange_shared(resid_bf, lat_buffer), latent_grad), gains_grad, *scattered)
 
     return (lambda early: latent_full), (lambda early: resid_mid), backward
 

time: 886 us -> 878 us (level)
  waiting for transfers between devices: 328 us -> 315 us
    all_to_all x9, waiting for transfers between devices: 48.4 us -> 28.9 us  [ctx_exchange(): lax.all_to_all(values, 'ctx', split_axis=0, concat_axis=0, tiled=True)]
    unnamed x201 -> x203, local copies, waits for them, and re-layouts: 34.9 us -> 35.1 us
  transfers between devices with their start and end apart: 56 -> 56, of which waited for: 23 -> 24; matrix products, arithmetic and copies ran while one was open for 24% -> 25% of each run, Pallas kernels for 13% -> 13%
where the time goes in v9:
time: 878 us; the launch traced here: 869 us
  waiting for transfers between devices  315 us (36%)
  Pallas kernels  179 us (20%)
  local copies, waits for them, and re-layouts  112 us (13%)
  other arithmetic  84.9 us (10%)
  starting transfers between devices  71.4 us (8%)
  matrix products  59.1 us (7%)
  blocking collectives  30.9 us (4%)
  between operations  16.2 us (2%)
    ppermute x40, waiting for transfers between devices, fsdp_swap(): lax.ppermute(values, 'fsdp', [(at, at ^ distance) for at in range(count)])  251 us
    pallas_call x13, Pallas kernels, expert_grad_call(): pl.pallas_call(functools.partial(expert_grad_body, each=len(each)), grid=...  59.9 us
    dot_general x12, matrix products, dot_f32(): lax.dot_general(left, right, (dims, ((), ())), preferred_element_type=jnp...  59.1 us
    pallas_call x1, Pallas kernels, experts_call(): pl.pallas_call(experts_body, grid=(count,), in_specs=[pl.BlockSpec((1, sl...  48.7 us
    all_to_all x9, starting transfers between devices, ctx_exchange(): lax.all_to_all(values, 'ctx', split_axis=0, concat_axis=0, tiled=True)  46.8 us
    unnamed x203, local copies, waits for them, and re-layouts  35.1 us
    all_gather x4, waiting for transfers between devices, ctx_gather(): return lax.all_gather(values, 'ctx', axis=0, tiled=True)  34.6 us
    all_to_all x1, blocking collectives, ctx_exchange(): lax.all_to_all(values, 'ctx', split_axis=0, concat_axis=0, tiled=True)  30.9 us
  transfers between devices with their start and end apart: 56, of which 24 were waited for; matrix products, arithmetic and copies ran while one was open for 25% of the time, Pallas kernels for 13%

profile of v9, /device:TPU:0, one launch (start us, length us, event | category | flops | bytes accessed | tf_op | source)
XLA Modules:
  0.0 868.7 jit_solution(8806102773317347607)
XLA Ops:
  12.8 7.3 all-to-all-start
  20.1 5.2 fusion.117
  26.8 31.7 %collective-permute-done = bf16[2,128,2816]{2,1,0:T(8,128)(2,1)} collective-permute-done((bf16[2,128,2816]{2,1,0:T(8,128)(2,1)S(1)}, bf16[2,128,2816]{2,1,0:T(8,128)(2,1)}, u32[]{:S(2)}, u32[]{:S(2)}) %collective-permute-start) | collective-permute-done | bytes 1441824 | tf_op jit(solution)/shard_map/ppermute | solution.py:242
  64.5 24.4 %collective-permute-done.2 = bf16[8,64,1088]{2,1,0:T(8,128)(2,1)S(1)} collective-permute-done((bf16[8,64,1088]{2,1,0:T(8,128)(2,1)S(1)}, bf16[8,64,1088]{2,1,0:T(8,128)(2,1)S(1)}, u32[]{:S(2)}, u32[]{:S(2)}) %collective-permute-start.2) | collective-permute-done | bytes 1114144 | tf_op jit(solution)/shard_map/ppermute | solution.py:242
  95.7 8.8 %all-gather.6.cloned.1.call-done = bf16[1024,2048]{1,0:T(8,128)(2,1)} async-done(((bf16[128,2048]{1,0:T(8,128)(2,1)}), bf16[1024,2048]{1,0:T(8,128)(2,1)}) %all-gather.6.cloned.1.call-update) | async-done | bytes 4194320 | tf_op jit(solution)/shard_map/all_gather | solution.py:292
  127.3 6.1 fusion.25
  143.4 13.8 %shard_map.212 = (bf16[1024,256]{1,0:T(8,128)(2,1)S(1)}, f32[2,1024,512]{2,1,0:T(8,128)}, f32[2,1024,1]{2,1,0:T(8,128)S(1)}) custom-call(bf16[1024,256]{1,0:T(8,128)(2,1)S(1)} %slice.307.nope_ref, bf16[2,1024,64]{2,1,0:T(8,128)(2,1)S(1)} %pad_maximum_fusion.17.rot_ref, bf16[1024,512]{1,0:T(8,128)(2,1)} %multiply_convert_fusion.1.lat_ref, ...), custom_call_target="tpu_custom_call" | custom-call | tf_op jit(solution)/shard_map/pallas_call | solution.py:406
  160.1 5.0 all-to-all-start.1
  170.7 18.9 %collective-permute-done.7 = bf16[2,128,2816]{2,1,0:T(8,128)(2,1)} collective-permute-done((bf16[2,128,2816]{2,1,0:T(8,128)(2,1)}, bf16[2,128,2816]{2,1,0:T(8,128)(2,1)}, u32[]{:S(2)}, u32[]{:S(2)}) %collective-permute-start.7) | collective-permute-done | bytes 1441824 | tf_op jit(solution)/shard_map/ppermute | solution.py:242
  196.5 28.6 %collective-permute-done.9 = bf16[2,128,2816]{2,1,0:T(8,128)(2,1)} collective-permute-done((bf16[2,128,2816]{2,1,0:T(8,128)(2,1)}, bf16[2,128,2816]{2,1,0:T(8,128)(2,1)}, u32[]{:S(2)}, u32[]{:S(2)}) %collective-permute-start.9) | collective-permute-done | bytes 1441824 | tf_op jit(solution)/shard_map/ppermute | solution.py:242
  238.6 16.9 %collective-permute-done.5 = bf16[8,64,1152]{2,1,0:T(8,128)(2,1)} collective-permute-done((bf16[8,64,1152]{2,1,0:T(8,128)(2,1)}, bf16[8,64,1152]{2,1,0:T(8,128)(2,1)}, u32[]{:S(2)}, u32[]{:S(2)}) %collective-permute-start.5) | collective-permute-done | bytes 1179680 | tf_op jit(solution)/shard_map/ppermute | solution.py:242
  257.0 4.3 convert_bitcast_fusion
  261.3 6.4 multiply_reduce_fusion.5
  269.8 17.6 %all-gather.10.cloned.1.call-done = bf16[1024,2048]{1,0:T(8,128)(2,1)} async-done(((bf16[128,2048]{1,0:T(8,128)(2,1)}), bf16[1024,2048]{1,0:T(8,128)(2,1)}) %all-gather.10.cloned.1.call-update) | async-done | bytes 4194320 | tf_op jit(solution)/shard_map/all_gather | solution.py:292
  287.4 7.9 multiply_convert_fusion
  295.3 23.6 %collective-permute-done.15 = bf16[2,1408,512]{2,1,0:T(8,128)(2,1)} collective-permute-done((bf16[2,1408,512]{2,1,0:T(8,128)(2,1)}, bf16[2,1408,512]{2,1,0:T(8,128)(2,1)}, u32[]{:S(2)}, u32[]{:S(2)}) %collective-permute-start.15) | collective-permute-done | bytes 2883616 | tf_op jit(solution)/shard_map/ppermute | solution.py:242
  324.8 7.0 pad_maximum_fusion.5.gate_up_ref
  339.7 5.7 constant_dynamic-update-slice_fusion.gu_ref
  345.4 8.0 pad_maximum_fusion.dn_ref
  353.4 8.2 all-gather.12.cloned.1.call-done
  361.6 6.3 fusion.124
  372.1 5.6 convolution_convert_fusion.1
  377.8 48.7 %shard_map.213 = (bf16[2,432,1408]{2,1,0:T(8,128)(2,1)}, bf16[2,432,2816]{2,1,0:T(8,128)(2,1)}, bf16[2,432,2048]{2,1,0:T(8,128)(2,1)}, bf16[2,432,2048]{2,1,0:T(8,128)(2,1)}) custom-call(bf16[2,432,2048]{2,1,0:T(8,128)(2,1)} %bitcast.208, bf16[2,432,2048]{2,1,0:T(8,128)(2,1)} %bitcast.220, f32[2,432,1]{2,1,0:T(8,128)} %copy.472.gate_ref, ...), custom_call_target="tpu_custom_call" | custom-call | tf_op jit(solution)/shard_map/pallas_call | solution.py:518
  426.5 19.0 %shard_map.214 = bf16[1024,4096]{1,0:T(8,128)(2,1)} custom-call(bf16[1024,864]{1,0:T(8,128)(2,1)} %get-tuple-element.229.pick_ref, bf16[1024,768]{1,0:T(8,128)(2,1)S(1)} %pad_maximum_fusion.9.both_ref, bf16[1024,384]{1,0:T(8,128)(2,1)S(1)} %get-tuple-element.255.act_ref, bf16[864,2048]{1,0:T(8,128)(2,1)} %bitcast.239, bf16[864,2048]{1,0:T(8,128)(2,1)} %bitcast.238, ...), custom_call_target="tpu_custom_call" | custom-call | tf_op jit(solution)/shard_map/pallas_call | solution.py:652
  447.2 4.6 shard_map.215
  451.9 5.5 collective-permute-done.18.refs_2_
  458.9 4.6 shard_map.216
  463.5 7.4 shard_map.217
  472.6 8.0 collective-permute-done.19
  489.3 5.3 shard_map.218
  494.7 7.5 shard_map.221
  503.7 33.0 %collective-permute-done.23.refs_3_ = bf16[2,1408,512]{2,1,0:T(8,128)(2,1)} collective-permute-done((bf16[2,1408,512]{2,1,0:T(8,128)(2,1)}, bf16[2,1408,512]{2,1,0:T(8,128)(2,1)}, u32[]{:S(2)}, u32[]{:S(2)}) %collective-permute-start.23) | collective-permute-done | bytes 2883616 | tf_op jit(solution)/shard_map/ppermute | solution.py:242
  550.8 6.8 copy.473
  566.3 5.7 shard_map.222
  572.0 25.8 %collective-permute-done.20.refs_3_ = bf16[1,512,2816]{2,1,0:T(8,128)(2,1)S(1)} collective-permute-done((bf16[1,512,2816]{2,1,0:T(8,128)(2,1)}, bf16[1,512,2816]{2,1,0:T(8,128)(2,1)S(1)}, u32[]{:S(2)}, u32[]{:S(2)}) %collective-permute-start.20) | collective-permute-done | bytes 2883616 | tf_op jit(solution)/shard_map/ppermute | solution.py:242
  606.6 4.6 convolution_convert_fusion.2
  611.3 30.9 %all_to_all.54 = bf16[8,128,256]{2,1,0:T(8,128)(2,1)S(1)} all-to-all(bf16[8,128,256]{2,1,0:T(8,128)(2,1)S(1)} %bitcast.245), channel_id=1, replica_groups=mesh['ctx'=8,'fsdp'=4] {'ctx'}, dimensions={0} | all-to-all | bytes 1048576 | tf_op jit(solution)/shard_map/all_to_all | solution.py:300
  642.3 24.8 %shard_map.223 = (bf16[1024,256]{1,0:T(8,128)(2,1)S(1)}, f32[2,1024,64]{2,1,0:T(8,128)}, f32[2,512,256]{2,1,0:T(8,128)}, f32[1024,512]{1,0:T(8,128)}, f32[1024,64]{1,0:T(8,128)S(1)}) custom-call(bf16[1024,256]{1,0:T(8,128)(2,1)S(1)} %bitcast.219, bf16[1024,256]{1,0:T(8,128)(2,1)S(1)} %copy-done.12, bf16[2,1024,64]{2,1,0:T(8,128)(2,1)S(1)} %copy-done.10, ...), custom_call_target="tpu_custom_call" | custom-call | tf_op jit(solution)/shard_map/pallas_call | solution.py:441
  674.8 6.6 fusion.3
  701.7 16.9 %collective-permute-done.27 = bf16[8,64,1152]{2,1,0:T(8,128)(2,1)} collective-permute-done((bf16[8,64,1152]{2,1,0:T(8,128)(2,1)}, bf16[8,64,1152]{2,1,0:T(8,128)(2,1)}, u32[]{:S(2)}, u32[]{:S(2)}) %collective-permute-start.27) | collective-permute-done | bytes 1179680 | tf_op jit(solution)/shard_map/ppermute | solution.py:242
  721.2 9.3 %collective-permute-done.30.refs_5_ = bf16[512,640]{1,0:T(8,128)(2,1)S(1)} collective-permute-done((bf16[512,640]{1,0:T(8,128)(2,1)S(1)}, bf16[512,640]{1,0:T(8,128)(2,1)S(1)}, u32[]{:S(2)}, u32[]{:S(2)}) %collective-permute-start.30) | collective-permute-done | bytes 655392 | tf_op jit(solution)/shard_map/ppermute | solution.py:242
  736.6 6.0 all-to-all-start.9
  748.6 16.6 %all-to-all-done.9 = bf16[8,64,640]{2,1,0:T(8,128)(2,1)S(1)} async-done(((bf16[8,64,640]{2,1,0:T(8,128)(2,1)}), bf16[8,64,640]{2,1,0:T(8,128)(2,1)S(1)}, u32[]{:S(2)}, u32[]{:S(2)}) %all-to-all-start.9) | async-done | bytes 655392 | tf_op jit(solution)/shard_map/all_to_all | solution.py:300
  766.0 4.6 all-to-all-start.6
  812.9 11.9 %shard_map.233 = f32[2,512,2816]{2,1,0:T(8,128)} custom-call(bf16[2,432,2048]{2,1,0:T(8,128)(2,1)} %bitcast.211, bf16[2,432,2816]{2,1,0:T(8,128)(2,1)} %get-tuple-element.93.refs_1_, bf16[2,512,2816]{2,1,0:T(8,128)(2,1)} %collective-permute-done.22.refs_2_, bf16[1,512,2816]{2,1,0:T(8,128)(2,1)S(1)} %copy-done.14, ...), custom_call_target="tpu_custom_call" | custom-call | tf_op jit(solution)/shard_map/pallas_call | solution.py:555
  824.8 6.0 all-to-all-start.7
  848.5 6.0 all-to-all-start.8
  856.4 4.7 all-to-all-done.8
  (493 shorter events, 253.9 us)
Async XLA Ops:
  7.2 97.4 %all-gather.6.cloned.1.call-start = ((), (), s32[]{:S(2)}) async-start(), calls=%async_computation.12 | async-start | bytes 4718592 | tf_op jit(solution)/shard_map/all_gather | solution.py:292
  12.8 49.9 %all-to-all-start = ((bf16[8,64,960]{2,1,0:T(8,128)(2,1)}), bf16[8,64,960]{2,1,0:T(8,128)(2,1)S(1)}, u32[]{:S(2)}, u32[]{:S(2)}) async-start(bf16[8,64,960]{2,1,0:T(8,128)(2,1)} %pad_maximum_fusion.12), calls=%async_computation | async-start | bytes 2097152 | tf_op jit(solution)/shard_map/all_to_all | solution.py:300
  20.1 241.3 %all-gather.8.cloned.1.call-start = ((), (), s32[]{:S(2)}) async-start(), calls=%async_computation.13 | async-start | bytes 8650752 | tf_op jit(solution)/shard_map/all_gather | solution.py:919
  25.4 33.1 %collective-permute-start = (bf16[2,128,2816]{2,1,0:T(8,128)(2,1)S(1)}, bf16[2,128,2816]{2,1,0:T(8,128)(2,1)}, u32[]{:S(2)}, u32[]{:S(2)}) collective-permute-start(bf16[2,128,2816]{2,1,0:T(8,128)(2,1)S(1)} %get-tuple-element.236), channel_id=1, source_target_pairs={{0,2},{1,3},{2,0},{3,1},{4,6},{5,7},{6,4},{7,5},{8,10},{9,11},{10,... | collective-permute-start | bytes 4325384 | tf_op jit(solution)/shard_map/ppermute | solution.py:242
  62.9 26.0 %collective-permute-start.2 = (bf16[8,64,1088]{2,1,0:T(8,128)(2,1)S(1)}, bf16[8,64,1088]{2,1,0:T(8,128)(2,1)S(1)}, u32[]{:S(2)}, u32[]{:S(2)}) collective-permute-start(bf16[8,64,1088]{2,1,0:T(8,128)(2,1)S(1)} %pad_maximum_fusion.10), channel_id=1, source_target_pairs={{0,2},{1,3},{2,0},{3,1},{4,6},{5,7},{6,4},{7,5},{8,10},{9,11},{10,... | collective-permute-start | bytes 3342344 | tf_op jit(solution)/shard_map/ppermute | solution.py:242
  64.5 24.4 %collective-permute-start.1 = (bf16[8,64,1088]{2,1,0:T(8,128)(2,1)S(1)}, bf16[8,64,1088]{2,1,0:T(8,128)(2,1)S(1)}, u32[]{:S(2)}, u32[]{:S(2)}) collective-permute-start(bf16[8,64,1088]{2,1,0:T(8,128)(2,1)S(1)} %pad_maximum_fusion.10), channel_id=1, source_target_pairs={{0,1},{1,0},{2,3},{3,2},{4,5},{5,4},{6,7},{7,6},{8,9},{9,8},{10,11... | collective-permute-start | bytes 3342344 | tf_op jit(solution)/shard_map/ppermute | solution.py:242
  104.6 235.2 %collective-permute-start.14 = (bf16[2,512,2816]{2,1,0:T(8,128)(2,1)}, bf16[2,512,2816]{2,1,0:T(8,128)(2,1)}, u32[]{:S(2)}, u32[]{:S(2)}) collective-permute-start(bf16[2,512,2816]{2,1,0:T(8,128)(2,1)} %param.22), channel_id=1, source_target_pairs={{0,1},{1,0},{2,3},{3,2},{4,5},{5,4},{6,7},{7,6},{8,9},{9,8},{10,11... | collective-permute-start | bytes 17301512 | tf_op jit(solution)/shard_map/ppermute | solution.py:242
  104.6 63.1 %collective-permute-start.8 = (bf16[2,128,2816]{2,1,0:T(8,128)(2,1)}, bf16[2,128,2816]{2,1,0:T(8,128)(2,1)}, u32[]{:S(2)}, u32[]{:S(2)}) collective-permute-start(bf16[2,128,2816]{2,1,0:T(8,128)(2,1)} %get-tuple-element.234), channel_id=1, source_target_pairs={{0,2},{1,3},{2,0},{3,1},{4,6},{5,7},{6,4},{7,5},{8,10},{9,11},{10,... | collective-permute-start | bytes 4325384 | tf_op jit(solution)/shard_map/ppermute | solution.py:242
  106.2 83.5 %collective-permute-start.7 = (bf16[2,128,2816]{2,1,0:T(8,128)(2,1)}, bf16[2,128,2816]{2,1,0:T(8,128)(2,1)}, u32[]{:S(2)}, u32[]{:S(2)}) collective-permute-start(bf16[2,128,2816]{2,1,0:T(8,128)(2,1)} %get-tuple-element.235), channel_id=1, source_target_pairs={{0,2},{1,3},{2,0},{3,1},{4,6},{5,7},{6,4},{7,5},{8,10},{9,11},{10,... | collective-permute-start | bytes 4325384 | tf_op jit(solution)/shard_map/ppermute | solution.py:242
  106.7 118.3 %collective-permute-start.9 = (bf16[2,128,2816]{2,1,0:T(8,128)(2,1)}, bf16[2,128,2816]{2,1,0:T(8,128)(2,1)}, u32[]{:S(2)}, u32[]{:S(2)}) collective-permute-start(bf16[2,128,2816]{2,1,0:T(8,128)(2,1)} %get-tuple-element.233), channel_id=1, source_target_pairs={{0,2},{1,3},{2,0},{3,1},{4,6},{5,7},{6,4},{7,5},{8,10},{9,11},{10,... | collective-permute-start | bytes 4325384 | tf_op jit(solution)/shard_map/ppermute | solution.py:242
  108.2 237.2 %collective-permute-start.17 = (bf16[2,1408,512]{2,1,0:T(8,128)(2,1)}, bf16[2,1408,512]{2,1,0:T(8,128)(2,1)}, u32[]{:S(2)}, u32[]{:S(2)}) collective-permute-start(bf16[2,1408,512]{2,1,0:T(8,128)(2,1)} %param.23), channel_id=1, source_target_pairs={{0,1},{1,0},{2,3},{3,2},{4,5},{5,4},{6,7},{7,6},{8,9},{9,8},{10,11... | collective-permute-start | bytes 8650760 | tf_op jit(solution)/shard_map/ppermute | solution.py:242
  116.4 43.8 %all-to-all-start.2 = ((bf16[8,64,1152]{2,1,0:T(8,128)(2,1)}), bf16[8,64,1152]{2,1,0:T(8,128)(2,1)}, u32[]{:S(2)}, u32[]{:S(2)}) async-start(bf16[8,64,1152]{2,1,0:T(8,128)(2,1)} %fusion.32), calls=%async_computation.2 | async-start | bytes 2359296 | tf_op jit(solution)/shard_map/all_to_all | solution.py:300
  120.7 166.7 %all-gather.10.cloned.1.call-start = ((), (), s32[]{:S(2)}) async-start(), calls=%async_computation.14 | async-start | bytes 4718592 | tf_op jit(solution)/shard_map/all_gather | solution.py:292
  160.1 32.7 %all-to-all-start.1 = ((bf16[8,128,256]{1,2,0:T(8,128)(2,1)}), bf16[8,128,256]{1,2,0:T(8,128)(2,1)S(1)}, u32[]{:S(2)}, u32[]{:S(2)}) async-start(bf16[8,128,256]{1,2,0:T(8,128)(2,1)} %copy.456), calls=%async_computation.1 | async-start | bytes 1048576 | tf_op jit(solution)/shard_map/all_to_all | solution.py:300
  192.8 36.3 %all-to-all-start.3 = ((bf16[8,128,24]{1,2,0:T(8,128)(2,1)}), bf16[8,128,24]{1,2,0:T(8,128)(2,1)S(1)}, u32[]{:S(2)}, u32[]{:S(2)}) async-start(bf16[8,128,24]{1,2,0:T(8,128)(2,1)} %broadcast_in_dim.45), calls=%async_computation.3 | async-start | bytes 98304 | tf_op jit(solution)/shard_map/all_to_all | solution.py:300
  196.2 165.4 %all-gather.12.cloned.1.call-start = ((), (), s32[]{:S(2)}) async-start(), calls=%async_computation.15 | async-start | bytes 4718592 | tf_op jit(solution)/shard_map/all_gather | solution.py:292
  227.7 27.8 %collective-permute-start.5 = (bf16[8,64,1152]{2,1,0:T(8,128)(2,1)}, bf16[8,64,1152]{2,1,0:T(8,128)(2,1)}, u32[]{:S(2)}, u32[]{:S(2)}) collective-permute-start(bf16[8,64,1152]{2,1,0:T(8,128)(2,1)} %all-to-all-done.2), channel_id=1, source_target_pairs={{0,2},{1,3},{2,0},{3,1},{4,6},{5,7},{6,4},{7,5},{8,10},{9,11},{10,... | collective-permute-start | bytes 3538952 | tf_op jit(solution)/shard_map/ppermute | solution.py:242
  229.1 89.8 %collective-permute-start.4 = (bf16[8,64,1152]{2,1,0:T(8,128)(2,1)}, bf16[8,64,1152]{2,1,0:T(8,128)(2,1)}, u32[]{:S(2)}, u32[]{:S(2)}) collective-permute-start(bf16[8,64,1152]{2,1,0:T(8,128)(2,1)} %all-to-all-done.2), channel_id=1, source_target_pairs={{0,1},{1,0},{2,3},{3,2},{4,5},{5,4},{6,7},{7,6},{8,9},{9,8},{10,11... | collective-permute-start | bytes 3538952 | tf_op jit(solution)/shard_map/ppermute | solution.py:242
  255.5 63.5 %collective-permute-start.15 = (bf16[2,1408,512]{2,1,0:T(8,128)(2,1)}, bf16[2,1408,512]{2,1,0:T(8,128)(2,1)}, u32[]{:S(2)}, u32[]{:S(2)}) collective-permute-start(bf16[2,1408,512]{2,1,0:T(8,128)(2,1)} %param.23), channel_id=1, source_target_pairs={{0,2},{1,3},{2,0},{3,1},{4,6},{5,7},{6,4},{7,5},{8,10},{9,11},{10,... | collective-permute-start | bytes 8650760 | tf_op jit(solution)/shard_map/ppermute | solution.py:242
  267.8 51.7 %collective-permute-start.6 = (bf16[8,64,1152]{2,1,0:T(8,128)(2,1)}, bf16[8,64,1152]{2,1,0:T(8,128)(2,1)S(1)}, u32[]{:S(2)}, u32[]{:S(2)}) collective-permute-start(bf16[8,64,1152]{2,1,0:T(8,128)(2,1)} %collective-permute-done.5), channel_id=1, source_target_pairs={{0,1},{1,0},{2,3},{3,2},{4,5},{5,4},{6,7},{7,6},{8,9},{9,8},{10,11... | collective-permute-start | bytes 3538952 | tf_op jit(solution)/shard_map/ppermute | solution.py:242
  287.4 310.5 %reduce-scatter.3.cloned.1.call-start = ((), (), s32[]{:S(2)}) async-start(), calls=%async_computation.16 | async-start | bytes 9437184 | tf_op jit(solution)/shard_map/reduce_scatter | solution.py:296
  319.0 5.5 collective-permute-start.11
  319.5 14.8 %collective-permute-start.12 = (bf16[2,128,2816]{2,1,0:T(8,128)(2,1)}, bf16[2,128,2816]{2,1,0:T(8,128)(2,1)S(1)}, u32[]{:S(2)}, u32[]{:S(2)}) collective-permute-start(bf16[2,128,2816]{2,1,0:T(8,128)(2,1)} %collective-permute-done.7), channel_id=1, source_target_pairs={{0,1},{1,0},{2,3},{3,2},{4,5},{5,4},{6,7},{7,6},{8,9},{9,8},{10,11... | collective-permute-start | bytes 4325384 | tf_op jit(solution)/shard_map/ppermute | solution.py:242
  323.9 11.6 %collective-permute-start.13 = (bf16[2,128,2816]{2,1,0:T(8,128)(2,1)}, bf16[2,128,2816]{2,1,0:T(8,128)(2,1)S(1)}, u32[]{:S(2)}, u32[]{:S(2)}) collective-permute-start(bf16[2,128,2816]{2,1,0:T(8,128)(2,1)} %collective-permute-done.9), channel_id=1, source_target_pairs={{0,1},{1,0},{2,3},{3,2},{4,5},{5,4},{6,7},{7,6},{8,9},{9,8},{10,11... | collective-permute-start | bytes 4325384 | tf_op jit(solution)/shard_map/ppermute | solution.py:242
  324.5 21.0 %collective-permute-start.16 = (bf16[2,1408,512]{2,1,0:T(8,128)(2,1)}, bf16[2,1408,512]{2,1,0:T(8,128)(2,1)S(1)}, u32[]{:S(2)}, u32[]{:S(2)}) collective-permute-start(bf16[2,1408,512]{2,1,0:T(8,128)(2,1)} %collective-permute-done.15), channel_id=1, source_target_pairs={{0,1},{1,0},{2,3},{3,2},{4,5},{5,4},{6,7},{7,6},{8,9},{9,8},{10,11... | collective-permute-start | bytes 8650760 | tf_op jit(solution)/shard_map/ppermute | solution.py:242
  445.6 244.5 %all-gather.14.cloned.1.call-start = ((), (), s32[]{:S(2)}) async-start(), calls=%async_computation.18 | async-start | bytes 4718592 | tf_op jit(solution)/shard_map/all_gather | solution.py:292
  451.9 5.5 collective-permute-start.18
  471.0 9.6 %collective-permute-start.19 = (bf16[2,512,2816]{2,1,0:T(8,128)(2,1)}, bf16[2,512,2816]{2,1,0:T(8,128)(2,1)S(1)}, u32[]{:S(2)}, u32[]{:S(2)}) collective-permute-start(bf16[2,512,2816]{2,1,0:T(8,128)(2,1)} %shard_map.217), channel_id=1, source_target_pairs={{0,1},{1,0},{2,3},{3,2},{4,5},{5,4},{6,7},{7,6},{8,9},{9,8},{10,11... | collective-permute-start | bytes 17301512 | tf_op jit(solution)/shard_map/ppermute | solution.py:242
  471.1 65.6 %collective-permute-start.23 = (bf16[2,1408,512]{2,1,0:T(8,128)(2,1)}, bf16[2,1408,512]{2,1,0:T(8,128)(2,1)}, u32[]{:S(2)}, u32[]{:S(2)}) collective-permute-start(bf16[2,1408,512]{2,1,0:T(8,128)(2,1)} %shard_map.216), channel_id=1, source_target_pairs={{0,2},{1,3},{2,0},{3,1},{4,6},{5,7},{6,4},{7,5},{8,10},{9,11},{10,... | collective-permute-start | bytes 8650760 | tf_op jit(solution)/shard_map/ppermute | solution.py:242
  502.2 95.7 %collective-permute-start.22 = (bf16[2,512,2816]{2,1,0:T(8,128)(2,1)}, bf16[2,512,2816]{2,1,0:T(8,128)(2,1)}, u32[]{:S(2)}, u32[]{:S(2)}) collective-permute-start(bf16[2,512,2816]{2,1,0:T(8,128)(2,1)} %shard_map.221), channel_id=1, source_target_pairs={{0,1},{1,0},{2,3},{3,2},{4,5},{5,4},{6,7},{7,6},{8,9},{9,8},{10,11... | collective-permute-start | bytes 17301512 | tf_op jit(solution)/shard_map/ppermute | solution.py:242
  502.2 95.7 %collective-permute-start.20 = (bf16[1,512,2816]{2,1,0:T(8,128)(2,1)}, bf16[1,512,2816]{2,1,0:T(8,128)(2,1)S(1)}, u32[]{:S(2)}, u32[]{:S(2)}) collective-permute-start(bf16[1,512,2816]{2,1,0:T(8,128)(2,1)} %shard_map.218), channel_id=1, source_target_pairs={{0,2},{1,3},{2,0},{3,1},{4,6},{5,7},{6,4},{7,5},{8,10},{9,11},{10,... | collective-permute-start | bytes 8650760 | tf_op jit(solution)/shard_map/ppermute | solution.py:242
  540.9 25.3 %collective-permute-start.21 = (bf16[2,1408,512]{2,1,0:T(8,128)(2,1)}, bf16[2,1408,512]{2,1,0:T(8,128)(2,1)}, u32[]{:S(2)}, u32[]{:S(2)}) collective-permute-start(bf16[2,1408,512]{2,1,0:T(8,128)(2,1)} %shard_map.220), channel_id=1, source_target_pairs={{0,1},{1,0},{2,3},{3,2},{4,5},{5,4},{6,7},{7,6},{8,9},{9,8},{10,11... | collective-permute-start | bytes 8650760 | tf_op jit(solution)/shard_map/ppermute | solution.py:242
  605.0 225.8 %reduce-scatter.5.cloned.1.call-start = ((), (), s32[]{:S(2)}) async-start(), calls=%async_computation.17 | async-start | bytes 4718592 | tf_op jit(solution)/shard_map/reduce_scatter | solution.py:296
  605.1 69.7 %collective-permute-start.26 = (bf16[1,512,2816]{2,1,0:T(8,128)(2,1)}, bf16[1,512,2816]{2,1,0:T(8,128)(2,1)}, u32[]{:S(2)}, u32[]{:S(2)}) collective-permute-start(bf16[1,512,2816]{2,1,0:T(8,128)(2,1)} %copy-done.15), channel_id=1, source_target_pairs={{0,2},{1,3},{2,0},{3,1},{4,6},{5,7},{6,4},{7,5},{8,10},{9,11},{10,... | collective-permute-start | bytes 8650760 | tf_op jit(solution)/shard_map/ppermute | solution.py:242
  685.0 51.5 %all-to-all-start.5 = ((bf16[8,128,576]{1,2,0:T(8,128)(2,1)}), bf16[8,128,576]{1,2,0:T(8,128)(2,1)}, u32[]{:S(2)}, u32[]{:S(2)}) async-start(bf16[8,128,576]{1,2,0:T(8,128)(2,1)} %pad_maximum_fusion.11), calls=%async_computation.7 | async-start | bytes 2359296 | tf_op jit(solution)/shard_map/all_to_all | solution.py:300
  689.3 29.3 %collective-permute-start.27 = (bf16[8,64,1152]{2,1,0:T(8,128)(2,1)}, bf16[8,64,1152]{2,1,0:T(8,128)(2,1)}, u32[]{:S(2)}, u32[]{:S(2)}) collective-permute-start(bf16[8,64,1152]{2,1,0:T(8,128)(2,1)} %get-tuple-element.105), channel_id=1, source_target_pairs={{0,2},{1,3},{2,0},{3,1},{4,6},{5,7},{6,4},{7,5},{8,10},{9,11},{10,... | collective-permute-start | bytes 3538952 | tf_op jit(solution)/shard_map/ppermute | solution.py:242
  695.3 25.9 %collective-permute-start.28 = (bf16[512,640]{1,0:T(8,128)(2,1)S(1)}, bf16[512,640]{1,0:T(8,128)(2,1)S(1)}, u32[]{:S(2)}, u32[]{:S(2)}) collective-permute-start(bf16[512,640]{1,0:T(8,128)(2,1)S(1)} %shard_map.224), channel_id=1, source_target_pairs={{0,1},{1,0},{2,3},{3,2},{4,5},{5,4},{6,7},{7,6},{8,9},{9,8},{10,11... | collective-permute-start | bytes 1966088 | tf_op jit(solution)/shard_map/ppermute | solution.py:242
  698.4 32.1 %collective-permute-start.30 = (bf16[512,640]{1,0:T(8,128)(2,1)S(1)}, bf16[512,640]{1,0:T(8,128)(2,1)S(1)}, u32[]{:S(2)}, u32[]{:S(2)}) collective-permute-start(bf16[512,640]{1,0:T(8,128)(2,1)S(1)} %shard_map.226), channel_id=1, source_target_pairs={{0,2},{1,3},{2,0},{3,1},{4,6},{5,7},{6,4},{7,5},{8,10},{9,11},{10,... | collective-permute-start | bytes 1966088 | tf_op jit(solution)/shard_map/ppermute | solution.py:242
  736.6 28.6 %all-to-all-start.9 = ((bf16[8,64,640]{2,1,0:T(8,128)(2,1)}), bf16[8,64,640]{2,1,0:T(8,128)(2,1)S(1)}, u32[]{:S(2)}, u32[]{:S(2)}) async-start(bf16[8,64,640]{2,1,0:T(8,128)(2,1)} %bitcast.81), calls=%async_computation.11 | async-start | bytes 1310720 | tf_op jit(solution)/shard_map/all_to_all | solution.py:300
  766.0 58.8 %all-to-all-start.6 = ((bf16[8,64,1152]{2,1,0:T(8,128)(2,1)}), bf16[8,64,1152]{2,1,0:T(8,128)(2,1)S(1)}, u32[]{:S(2)}, u32[]{:S(2)}) async-start(bf16[8,64,1152]{2,1,0:T(8,128)(2,1)} %add_convert_fusion), calls=%async_computation.8 | async-start | bytes 2359296 | tf_op jit(solution)/shard_map/all_to_all | solution.py:300
  770.7 22.4 %collective-permute-start.32 = (bf16[1,512,640]{2,1,0:T(8,128)(2,1)S(1)}, bf16[1,512,640]{2,1,0:T(8,128)(2,1)S(1)}, u32[]{:S(2)}, u32[]{:S(2)}) collective-permute-start(bf16[1,512,640]{2,1,0:T(8,128)(2,1)S(1)} %shard_map.228), channel_id=1, source_target_pairs={{0,1},{1,0},{2,3},{3,2},{4,5},{5,4},{6,7},{7,6},{8,9},{9,8},{10,11... | collective-permute-start | bytes 1966088 | tf_op jit(solution)/shard_map/ppermute | solution.py:242
  782.6 12.3 %collective-permute-start.37 = (bf16[512,128]{1,0:T(8,128)(2,1)}, bf16[512,128]{1,0:T(8,128)(2,1)}, u32[]{:S(2)}, u32[]{:S(2)}) collective-permute-start(bf16[512,128]{1,0:T(8,128)(2,1)} %bitcast.270), channel_id=1, source_target_pairs={{0,1},{1,0},{2,3},{3,2},{4,5},{5,4},{6,7},{7,6},{8,9},{9,8},{10,11... | collective-permute-start | bytes 393224 | tf_op jit(solution)/shard_map/ppermute | solution.py:242
  783.4 11.5 %collective-permute-start.39 = (bf16[512,128]{1,0:T(8,128)(2,1)}, bf16[512,128]{1,0:T(8,128)(2,1)}, u32[]{:S(2)}, u32[]{:S(2)}) collective-permute-start(bf16[512,128]{1,0:T(8,128)(2,1)} %add_convert_fusion.2), channel_id=1, source_target_pairs={{0,2},{1,3},{2,0},{3,1},{4,6},{5,7},{6,4},{7,5},{8,10},{9,11},{10,... | collective-permute-start | bytes 393224 | tf_op jit(solution)/shard_map/ppermute | solution.py:242
  792.9 15.8 %collective-permute-start.31 = (bf16[1,512,640]{2,1,0:T(8,128)(2,1)}, bf16[1,512,640]{2,1,0:T(8,128)(2,1)}, u32[]{:S(2)}, u32[]{:S(2)}) collective-permute-start(bf16[1,512,640]{2,1,0:T(8,128)(2,1)} %shard_map.229), channel_id=1, source_target_pairs={{0,1},{1,0},{2,3},{3,2},{4,5},{5,4},{6,7},{7,6},{8,9},{9,8},{10,11... | collective-permute-start | bytes 1966088 | tf_op jit(solution)/shard_map/ppermute | solution.py:242
  793.5 17.0 %collective-permute-start.33 = (bf16[1,512,640]{2,1,0:T(8,128)(2,1)S(1)}, bf16[1,512,640]{2,1,0:T(8,128)(2,1)S(1)}, u32[]{:S(2)}, u32[]{:S(2)}) collective-permute-start(bf16[1,512,640]{2,1,0:T(8,128)(2,1)S(1)} %shard_map.230), channel_id=1, source_target_pairs={{0,2},{1,3},{2,0},{3,1},{4,6},{5,7},{6,4},{7,5},{8,10},{9,11},{10,... | collective-permute-start | bytes 1966088 | tf_op jit(solution)/shard_map/ppermute | solution.py:242
  824.8 23.1 %all-to-all-start.7 = ((bf16[8,64,640]{2,1,0:T(8,128)(2,1)}), bf16[8,64,640]{2,1,0:T(8,128)(2,1)}, u32[]{:S(2)}, u32[]{:S(2)}) async-start(bf16[8,64,640]{2,1,0:T(8,128)(2,1)} %bitcast.80), calls=%async_computation.9 | async-start | bytes 1310720 | tf_op jit(solution)/shard_map/all_to_all | solution.py:300
  836.0 11.2 %collective-permute-start.34 = (f32[8,144]{1,0:T(8,128)}, f32[8,144]{1,0:T(8,128)}, u32[]{:S(2)}, u32[]{:S(2)}) collective-permute-start(f32[8,144]{1,0:T(8,128)} %bitcast.203), channel_id=1, source_target_pairs={{0,1},{1,0},{2,3},{3,2},{4,5},{5,4},{6,7},{7,6},{8,9},{9,8},{10,11... | collective-permute-start | bytes 13832 | tf_op jit(solution)/shard_map/ppermute | solution.py:242
  848.5 12.5 %all-to-all-start.8 = ((f32[8,1,144]{2,1,0:T(1,128)}), f32[8,1,144]{2,1,0:T(1,128)S(1)}, u32[]{:S(2)}, u32[]{:S(2)}) async-start(f32[8,1,144]{2,1,0:T(1,128)} %all_to_all.41), calls=%async_computation.10 | async-start | bytes 16384 | tf_op jit(solution)/shard_map/all_to_all | solution.py:300
  (98 other events, 1375.4 us)
Sparse Core Ops, SparseCore 0:
  10.7 93.7 all-gather.5
  107.4 105.2 all-gather.7
  215.4 71.8 all-gather.9
  289.9 71.6 all-gather.11
  445.7 147.2 reduce-scatter.2
  605.1 82.8 all-gather.13
  692.0 125.0 reduce-scatter.4

commit v10 on v9

--- a/solution.py
+++ b/solution.py
@@ -840,7 +840,7 @@
     def reduce_gains(gain_in_grad, gain_lat_grad, first=(), second=()):
         gains = jnp.concatenate([gain_in_grad, gain_mid_grad, gain_lat_grad], 0)
         gains = fsdp_reduce(gains.reshape(n_ctx, 4, -1).transpose(1, 0, 2), rank, first)
-        return jnp.sum(ctx_exchange(after(gains, second)), 0)
+        return gains, jnp.sum(ctx_exchange(after(gains, second)), 0)
 
     def exchange_shared(early, late):
         far = fsdp_swap(after(shared_other, early), 2)
@@ -1013,18 +1013,18 @@
         token_cols = columns_by_distance(tokens, n_ctx, rank)
         gain_in_grad = gain_in_grad + jnp.sum(in_own * (token_cols * inv_in), 0)
         gain_in_grad = columns_in_order(gain_in_grad[None], n_ctx, rank)[0]
-        gains_grad = reduce_gains(gain_in_grad, gain_lat_grad, latent_own, latent_got)
+        gains_there, gains_grad = reduce_gains(gain_in_grad, gain_lat_grad, latent_own, latent_got)
         expand_g = expand_g.transpose(1, 0, 2)
         expand_blocks = expand_g.reshape(KVL, 4, -1).transpose(1, 0, 2).astype(jnp.bfloat16)
         expand_w = fsdp_reduce(expand_blocks, rank)
         nope_w = query_terms[:, :, :n_wide].reshape(n_ctx, rows, heads, DN)
         rot_w = query_terms[:, :, n_wide:].reshape(n_ctx, rows, heads, DR)
         query_w = jnp.concatenate([nope_w, rot_w], -1).transpose(1, 0, 2, 3).reshape(rows, -1)
-        shared_sums = exchange_shared(in_part, latent_sent)
-        in_grad = after(in_grad, shared_sums).astype(jnp.float32) + in_own
+        shared_sums = exchange_shared(in_part, latent_got)
+        in_grad = after(in_grad, gains_there).astype(jnp.float32) + in_own
         token_grad = norm_backward(token_cols, inv_in, saved["gain_cols"], in_grad)[0]
         token_grad = columns_in_order(token_grad, n_ctx, rank)
-        stage = (shared_sums, latent_own)
+        stage = (shared_sums, latent_got)
         return token_grad, stage, gains_grad, query_w, latent_w, expand_w, output_w
 
     return first, middle, backward
@@ -1147,7 +1147,7 @@
             )
             for g, at in ((query_g, 0), (latent_g, 0), (expand_g, 1), (output_g, 1))
         ]
-        gains_grad = reduce_gains(gain_in_grad, gain_lat_grad)
+        gains_grad = reduce_gains(gain_in_grad, gain_lat_grad)[1]
         return (token_grad, (exchange_shared(resid_bf, lat_buffer), latent_grad), gains_grad, *scattered)
 
     return (lambda early: latent_full), (lambda early: resid_mid), backward

time: 878 us -> 878 us (level)
  waiting for transfers between devices: 315 us -> 334 us
    all_to_all x9, waiting for transfers between devices: 28.9 us -> 39.6 us  [ctx_exchange(): lax.all_to_all(values, 'ctx', split_axis=0, concat_axis=0, tiled=True)]
    unnamed x203 -> x209, local copies, waits for them, and re-layouts: 35.1 us -> 34.3 us
  transfers between devices with their start and end apart: 56 -> 56, of which waited for: 24 -> 27; matrix products, arithmetic and copies ran while one was open for 25% -> 24% of each run, Pallas kernels for 13% -> 12%
where the time goes in v10:
time: 878 us; the launch traced here: 869 us
  waiting for transfers between devices  334 us (38%)
  Pallas kernels  178 us (20%)
  local copies, waits for them, and re-layouts  104 us (12%)
  other arithmetic  82.7 us (9%)
  starting transfers between devices  63.4 us (7%)
  matrix products  60.1 us (7%)
  blocking collectives  30.9 us (4%)
  between operations  16.3 us (2%)
    ppermute x40, waiting for transfers between devices, fsdp_swap(): lax.ppermute(values, 'fsdp', [(at, at ^ distance) for at in range(count)])  260 us
    dot_general x12, matrix products, dot_f32(): lax.dot_general(left, right, (dims, ((), ())), preferred_element_type=jnp...  60.1 us
    pallas_call x13, Pallas kernels, expert_grad_call(): pl.pallas_call(functools.partial(expert_grad_body, each=len(each)), grid=...  57.8 us
    pallas_call x1, Pallas kernels, experts_call(): pl.pallas_call(experts_body, grid=(count,), in_specs=[pl.BlockSpec((1, sl...  48.7 us
    all_to_all x9, starting transfers between devices, ctx_exchange(): lax.all_to_all(values, 'ctx', split_axis=0, concat_axis=0, tiled=True)  41.3 us
    all_to_all x9, waiting for transfers between devices, ctx_exchange(): lax.all_to_all(values, 'ctx', split_axis=0, concat_axis=0, tiled=True)  39.6 us
    all_gather x4, waiting for transfers between devices, ctx_gather(): return lax.all_gather(values, 'ctx', axis=0, tiled=True)  34.7 us
    unnamed x209, local copies, waits for them, and re-layouts  34.3 us
  transfers between devices with their start and end apart: 56, of which 27 were waited for; matrix products, arithmetic and copies ran while one was open for 24% of the time, Pallas kernels for 12%

profile of v10, /device:TPU:0, one launch (start us, length us, event | category | flops | bytes accessed | tf_op | source)
XLA Modules:
  0.0 869.3 jit_solution(7948431829159191409)
XLA Ops:
  12.8 7.3 all-to-all-start
  20.1 5.2 fusion.117
  26.8 31.7 %collective-permute-done = bf16[2,128,2816]{2,1,0:T(8,128)(2,1)} collective-permute-done((bf16[2,128,2816]{2,1,0:T(8,128)(2,1)S(1)}, bf16[2,128,2816]{2,1,0:T(8,128)(2,1)}, u32[]{:S(2)}, u32[]{:S(2)}) %collective-permute-start) | collective-permute-done | bytes 1441824 | tf_op jit(solution)/shard_map/ppermute | solution.py:242
  64.5 24.4 %collective-permute-done.2 = bf16[8,64,1088]{2,1,0:T(8,128)(2,1)S(1)} collective-permute-done((bf16[8,64,1088]{2,1,0:T(8,128)(2,1)S(1)}, bf16[8,64,1088]{2,1,0:T(8,128)(2,1)S(1)}, u32[]{:S(2)}, u32[]{:S(2)}) %collective-permute-start.2) | collective-permute-done | bytes 1114144 | tf_op jit(solution)/shard_map/ppermute | solution.py:242
  95.6 8.9 %all-gather.6.cloned.1.call-done = bf16[1024,2048]{1,0:T(8,128)(2,1)} async-done(((bf16[128,2048]{1,0:T(8,128)(2,1)}), bf16[1024,2048]{1,0:T(8,128)(2,1)}) %all-gather.6.cloned.1.call-update) | async-done | bytes 4194320 | tf_op jit(solution)/shard_map/all_gather | solution.py:292
  127.7 6.1 fusion.25
  143.8 13.8 %shard_map.212 = (bf16[1024,256]{1,0:T(8,128)(2,1)S(1)}, f32[2,1024,512]{2,1,0:T(8,128)}, f32[2,1024,1]{2,1,0:T(8,128)S(1)}) custom-call(bf16[1024,256]{1,0:T(8,128)(2,1)S(1)} %slice.307.nope_ref, bf16[2,1024,64]{2,1,0:T(8,128)(2,1)S(1)} %pad_maximum_fusion.17.rot_ref, bf16[1024,512]{1,0:T(8,128)(2,1)} %multiply_convert_fusion.1.lat_ref, ...), custom_call_target="tpu_custom_call" | custom-call | tf_op jit(solution)/shard_map/pallas_call | solution.py:406
  160.1 5.4 all-to-all-start.1
  170.9 18.8 %collective-permute-done.7 = bf16[2,128,2816]{2,1,0:T(8,128)(2,1)} collective-permute-done((bf16[2,128,2816]{2,1,0:T(8,128)(2,1)}, bf16[2,128,2816]{2,1,0:T(8,128)(2,1)}, u32[]{:S(2)}, u32[]{:S(2)}) %collective-permute-start.7) | collective-permute-done | bytes 1441824 | tf_op jit(solution)/shard_map/ppermute | solution.py:242
  196.5 28.6 %collective-permute-done.9 = bf16[2,128,2816]{2,1,0:T(8,128)(2,1)} collective-permute-done((bf16[2,128,2816]{2,1,0:T(8,128)(2,1)}, bf16[2,128,2816]{2,1,0:T(8,128)(2,1)}, u32[]{:S(2)}, u32[]{:S(2)}) %collective-permute-start.9) | collective-permute-done | bytes 1441824 | tf_op jit(solution)/shard_map/ppermute | solution.py:242
  238.6 16.9 %collective-permute-done.5 = bf16[8,64,1152]{2,1,0:T(8,128)(2,1)} collective-permute-done((bf16[8,64,1152]{2,1,0:T(8,128)(2,1)}, bf16[8,64,1152]{2,1,0:T(8,128)(2,1)}, u32[]{:S(2)}, u32[]{:S(2)}) %collective-permute-start.5) | collective-permute-done | bytes 1179680 | tf_op jit(solution)/shard_map/ppermute | solution.py:242
  257.0 4.4 convert_bitcast_fusion
  261.3 6.4 multiply_reduce_fusion.5
  269.8 17.6 %all-gather.10.cloned.1.call-done = bf16[1024,2048]{1,0:T(8,128)(2,1)} async-done(((bf16[128,2048]{1,0:T(8,128)(2,1)}), bf16[1024,2048]{1,0:T(8,128)(2,1)}) %all-gather.10.cloned.1.call-update) | async-done | bytes 4194320 | tf_op jit(solution)/shard_map/all_gather | solution.py:292
  287.4 7.9 multiply_convert_fusion
  295.3 23.6 %collective-permute-done.15 = bf16[2,1408,512]{2,1,0:T(8,128)(2,1)} collective-permute-done((bf16[2,1408,512]{2,1,0:T(8,128)(2,1)}, bf16[2,1408,512]{2,1,0:T(8,128)(2,1)}, u32[]{:S(2)}, u32[]{:S(2)}) %collective-permute-start.15) | collective-permute-done | bytes 2883616 | tf_op jit(solution)/shard_map/ppermute | solution.py:242
  324.7 7.0 pad_maximum_fusion.5.gate_up_ref
  339.7 5.7 constant_dynamic-update-slice_fusion.gu_ref
  345.4 8.0 pad_maximum_fusion.dn_ref
  353.4 8.2 all-gather.12.cloned.1.call-done
  361.6 6.3 fusion.124
  372.1 5.8 convolution_convert_fusion.1
  377.9 48.7 %shard_map.213 = (bf16[2,432,1408]{2,1,0:T(8,128)(2,1)}, bf16[2,432,2816]{2,1,0:T(8,128)(2,1)}, bf16[2,432,2048]{2,1,0:T(8,128)(2,1)}, bf16[2,432,2048]{2,1,0:T(8,128)(2,1)}) custom-call(bf16[2,432,2048]{2,1,0:T(8,128)(2,1)} %bitcast.208, bf16[2,432,2048]{2,1,0:T(8,128)(2,1)} %bitcast.220, f32[2,432,1]{2,1,0:T(8,128)} %copy.472.gate_ref, ...), custom_call_target="tpu_custom_call" | custom-call | tf_op jit(solution)/shard_map/pallas_call | solution.py:518
  426.7 19.0 %shard_map.214 = bf16[1024,4096]{1,0:T(8,128)(2,1)} custom-call(bf16[1024,864]{1,0:T(8,128)(2,1)} %get-tuple-element.227.pick_ref, bf16[1024,768]{1,0:T(8,128)(2,1)S(1)} %pad_maximum_fusion.9.both_ref, bf16[1024,384]{1,0:T(8,128)(2,1)S(1)} %get-tuple-element.253.act_ref, bf16[864,2048]{1,0:T(8,128)(2,1)} %bitcast.239, bf16[864,2048]{1,0:T(8,128)(2,1)} %bitcast.238, ...), custom_call_target="tpu_custom_call" | custom-call | tf_op jit(solution)/shard_map/pallas_call | solution.py:652
  447.4 4.3 shard_map.215
  451.7 5.5 collective-permute-done.18.refs_2_
  458.8 4.6 shard_map.216
  463.4 7.4 shard_map.217
  472.5 8.0 collective-permute-done.19
  483.4 4.3 shard_map.219
  489.2 5.4 shard_map.218
  494.7 7.5 shard_map.221
  503.8 32.8 %collective-permute-done.23.refs_3_ = bf16[2,1408,512]{2,1,0:T(8,128)(2,1)} collective-permute-done((bf16[2,1408,512]{2,1,0:T(8,128)(2,1)}, bf16[2,1408,512]{2,1,0:T(8,128)(2,1)}, u32[]{:S(2)}, u32[]{:S(2)}) %collective-permute-start.23) | collective-permute-done | bytes 2883616 | tf_op jit(solution)/shard_map/ppermute | solution.py:242
  550.6 6.9 copy.473
  566.3 5.8 shard_map.222
  572.1 25.7 %collective-permute-done.20.refs_3_ = bf16[1,512,2816]{2,1,0:T(8,128)(2,1)S(1)} collective-permute-done((bf16[1,512,2816]{2,1,0:T(8,128)(2,1)}, bf16[1,512,2816]{2,1,0:T(8,128)(2,1)S(1)}, u32[]{:S(2)}, u32[]{:S(2)}) %collective-permute-start.20) | collective-permute-done | bytes 2883616 | tf_op jit(solution)/shard_map/ppermute | solution.py:242
  606.5 4.6 convolution_convert_fusion.2
  611.2 30.9 %all_to_all.54 = bf16[8,128,256]{2,1,0:T(8,128)(2,1)S(1)} all-to-all(bf16[8,128,256]{2,1,0:T(8,128)(2,1)S(1)} %bitcast.245), channel_id=1, replica_groups=mesh['ctx'=8,'fsdp'=4] {'ctx'}, dimensions={0} | all-to-all | bytes 1048576 | tf_op jit(solution)/shard_map/all_to_all | solution.py:300
  642.2 24.9 %shard_map.223 = (bf16[1024,256]{1,0:T(8,128)(2,1)S(1)}, f32[2,1024,64]{2,1,0:T(8,128)}, f32[2,512,256]{2,1,0:T(8,128)}, f32[1024,512]{1,0:T(8,128)}, f32[1024,64]{1,0:T(8,128)S(1)}) custom-call(bf16[1024,256]{1,0:T(8,128)(2,1)S(1)} %bitcast.219, bf16[1024,256]{1,0:T(8,128)(2,1)S(1)} %copy-done.12, bf16[2,1024,64]{2,1,0:T(8,128)(2,1)S(1)} %copy-done.10, ...), custom_call_target="tpu_custom_call" | custom-call | tf_op jit(solution)/shard_map/pallas_call | solution.py:441
  674.2 6.6 fusion.3
  684.5 4.7 all-to-all-start.5
  719.0 18.1 %all-to-all-done.5 = bf16[8,128,576]{1,2,0:T(8,128)(2,1)} async-done(((bf16[8,128,576]{1,2,0:T(8,128)(2,1)}), bf16[8,128,576]{1,2,0:T(8,128)(2,1)}, u32[]{:S(2)}, u32[]{:S(2)}) %all-to-all-start.5) | async-done | bytes 1179680 | tf_op jit(solution)/shard_map/all_to_all | solution.py:300
  744.4 4.5 all-to-all-start.8
  757.0 18.3 %collective-permute-done.38 = bf16[512,128]{1,0:T(8,128)(2,1)} collective-permute-done((bf16[512,128]{1,0:T(8,128)(2,1)}, bf16[512,128]{1,0:T(8,128)(2,1)}, u32[]{:S(2)}, u32[]{:S(2)}) %collective-permute-start.38) | collective-permute-done | bytes 131104 | tf_op jit(solution)/shard_map/ppermute | solution.py:242
  782.3 12.8 %collective-permute-done.32.refs_3_ = bf16[1,512,640]{2,1,0:T(8,128)(2,1)S(1)} collective-permute-done((bf16[1,512,640]{2,1,0:T(8,128)(2,1)S(1)}, bf16[1,512,640]{2,1,0:T(8,128)(2,1)S(1)}, u32[]{:S(2)}, u32[]{:S(2)}) %collective-permute-start.32) | collective-permute-done | bytes 655392 | tf_op jit(solution)/shard_map/ppermute | solution.py:242
  796.3 4.5 all-to-all-start.6
  808.1 10.0 %all-to-all-done.6 = bf16[8,64,640]{2,1,0:T(8,128)(2,1)S(1)} async-done(((bf16[8,64,640]{2,1,0:T(8,128)(2,1)}), bf16[8,64,640]{2,1,0:T(8,128)(2,1)S(1)}, u32[]{:S(2)}, u32[]{:S(2)}) %all-to-all-start.6) | async-done | bytes 655392 | tf_op jit(solution)/shard_map/all_to_all | solution.py:300
  843.5 11.9 %shard_map.233 = f32[2,512,2816]{2,1,0:T(8,128)} custom-call(bf16[2,432,2048]{2,1,0:T(8,128)(2,1)} %bitcast.211, bf16[2,432,2816]{2,1,0:T(8,128)(2,1)} %get-tuple-element.93.refs_1_, bf16[2,512,2816]{2,1,0:T(8,128)(2,1)} %collective-permute-done.22.refs_2_, bf16[1,512,2816]{2,1,0:T(8,128)(2,1)S(1)} %copy-done.14, ...), custom_call_target="tpu_custom_call" | custom-call | tf_op jit(solution)/shard_map/pallas_call | solution.py:555
  (500 shorter events, 247.3 us)
Async XLA Ops:
  7.2 97.4 %all-gather.6.cloned.1.call-start = ((), (), s32[]{:S(2)}) async-start(), calls=%async_computation.12 | async-start | bytes 4718592 | tf_op jit(solution)/shard_map/all_gather | solution.py:292
  12.8 49.9 %all-to-all-start = ((bf16[8,64,960]{2,1,0:T(8,128)(2,1)}), bf16[8,64,960]{2,1,0:T(8,128)(2,1)S(1)}, u32[]{:S(2)}, u32[]{:S(2)}) async-start(bf16[8,64,960]{2,1,0:T(8,128)(2,1)} %pad_maximum_fusion.12), calls=%async_computation | async-start | bytes 2097152 | tf_op jit(solution)/shard_map/all_to_all | solution.py:300
  20.1 241.2 %all-gather.8.cloned.1.call-start = ((), (), s32[]{:S(2)}) async-start(), calls=%async_computation.13 | async-start | bytes 8650752 | tf_op jit(solution)/shard_map/all_gather | solution.py:919
  25.4 33.1 %collective-permute-start = (bf16[2,128,2816]{2,1,0:T(8,128)(2,1)S(1)}, bf16[2,128,2816]{2,1,0:T(8,128)(2,1)}, u32[]{:S(2)}, u32[]{:S(2)}) collective-permute-start(bf16[2,128,2816]{2,1,0:T(8,128)(2,1)S(1)} %get-tuple-element.234), channel_id=1, source_target_pairs={{0,2},{1,3},{2,0},{3,1},{4,6},{5,7},{6,4},{7,5},{8,10},{9,11},{10,... | collective-permute-start | bytes 4325384 | tf_op jit(solution)/shard_map/ppermute | solution.py:242
  62.9 26.0 %collective-permute-start.2 = (bf16[8,64,1088]{2,1,0:T(8,128)(2,1)S(1)}, bf16[8,64,1088]{2,1,0:T(8,128)(2,1)S(1)}, u32[]{:S(2)}, u32[]{:S(2)}) collective-permute-start(bf16[8,64,1088]{2,1,0:T(8,128)(2,1)S(1)} %pad_maximum_fusion.10), channel_id=1, source_target_pairs={{0,2},{1,3},{2,0},{3,1},{4,6},{5,7},{6,4},{7,5},{8,10},{9,11},{10,... | collective-permute-start | bytes 3342344 | tf_op jit(solution)/shard_map/ppermute | solution.py:242
  64.5 24.4 %collective-permute-start.1 = (bf16[8,64,1088]{2,1,0:T(8,128)(2,1)S(1)}, bf16[8,64,1088]{2,1,0:T(8,128)(2,1)S(1)}, u32[]{:S(2)}, u32[]{:S(2)}) collective-permute-start(bf16[8,64,1088]{2,1,0:T(8,128)(2,1)S(1)} %pad_maximum_fusion.10), channel_id=1, source_target_pairs={{0,1},{1,0},{2,3},{3,2},{4,5},{5,4},{6,7},{7,6},{8,9},{9,8},{10,11... | collective-permute-start | bytes 3342344 | tf_op jit(solution)/shard_map/ppermute | solution.py:242
  104.6 235.1 %collective-permute-start.14 = (bf16[2,512,2816]{2,1,0:T(8,128)(2,1)}, bf16[2,512,2816]{2,1,0:T(8,128)(2,1)}, u32[]{:S(2)}, u32[]{:S(2)}) collective-permute-start(bf16[2,512,2816]{2,1,0:T(8,128)(2,1)} %param.22), channel_id=1, source_target_pairs={{0,1},{1,0},{2,3},{3,2},{4,5},{5,4},{6,7},{7,6},{8,9},{9,8},{10,11... | collective-permute-start | bytes 17301512 | tf_op jit(solution)/shard_map/ppermute | solution.py:242
  104.7 63.4 %collective-permute-start.8 = (bf16[2,128,2816]{2,1,0:T(8,128)(2,1)}, bf16[2,128,2816]{2,1,0:T(8,128)(2,1)}, u32[]{:S(2)}, u32[]{:S(2)}) collective-permute-start(bf16[2,128,2816]{2,1,0:T(8,128)(2,1)} %get-tuple-element.232), channel_id=1, source_target_pairs={{0,2},{1,3},{2,0},{3,1},{4,6},{5,7},{6,4},{7,5},{8,10},{9,11},{10,... | collective-permute-start | bytes 4325384 | tf_op jit(solution)/shard_map/ppermute | solution.py:242
  106.2 83.5 %collective-permute-start.7 = (bf16[2,128,2816]{2,1,0:T(8,128)(2,1)}, bf16[2,128,2816]{2,1,0:T(8,128)(2,1)}, u32[]{:S(2)}, u32[]{:S(2)}) collective-permute-start(bf16[2,128,2816]{2,1,0:T(8,128)(2,1)} %get-tuple-element.233), channel_id=1, source_target_pairs={{0,2},{1,3},{2,0},{3,1},{4,6},{5,7},{6,4},{7,5},{8,10},{9,11},{10,... | collective-permute-start | bytes 4325384 | tf_op jit(solution)/shard_map/ppermute | solution.py:242
  106.7 118.3 %collective-permute-start.9 = (bf16[2,128,2816]{2,1,0:T(8,128)(2,1)}, bf16[2,128,2816]{2,1,0:T(8,128)(2,1)}, u32[]{:S(2)}, u32[]{:S(2)}) collective-permute-start(bf16[2,128,2816]{2,1,0:T(8,128)(2,1)} %get-tuple-element.231), channel_id=1, source_target_pairs={{0,2},{1,3},{2,0},{3,1},{4,6},{5,7},{6,4},{7,5},{8,10},{9,11},{10,... | collective-permute-start | bytes 4325384 | tf_op jit(solution)/shard_map/ppermute | solution.py:242
  108.2 237.2 %collective-permute-start.17 = (bf16[2,1408,512]{2,1,0:T(8,128)(2,1)}, bf16[2,1408,512]{2,1,0:T(8,128)(2,1)}, u32[]{:S(2)}, u32[]{:S(2)}) collective-permute-start(bf16[2,1408,512]{2,1,0:T(8,128)(2,1)} %param.23), channel_id=1, source_target_pairs={{0,1},{1,0},{2,3},{3,2},{4,5},{5,4},{6,7},{7,6},{8,9},{9,8},{10,11... | collective-permute-start | bytes 8650760 | tf_op jit(solution)/shard_map/ppermute | solution.py:242
  116.4 43.8 %all-to-all-start.2 = ((bf16[8,64,1152]{2,1,0:T(8,128)(2,1)}), bf16[8,64,1152]{2,1,0:T(8,128)(2,1)}, u32[]{:S(2)}, u32[]{:S(2)}) async-start(bf16[8,64,1152]{2,1,0:T(8,128)(2,1)} %fusion.32), calls=%async_computation.2 | async-start | bytes 2359296 | tf_op jit(solution)/shard_map/all_to_all | solution.py:300
  120.7 166.7 %all-gather.10.cloned.1.call-start = ((), (), s32[]{:S(2)}) async-start(), calls=%async_computation.14 | async-start | bytes 4718592 | tf_op jit(solution)/shard_map/all_gather | solution.py:292
  160.1 32.7 %all-to-all-start.1 = ((bf16[8,128,256]{1,2,0:T(8,128)(2,1)}), bf16[8,128,256]{1,2,0:T(8,128)(2,1)S(1)}, u32[]{:S(2)}, u32[]{:S(2)}) async-start(bf16[8,128,256]{1,2,0:T(8,128)(2,1)} %copy.456), calls=%async_computation.1 | async-start | bytes 1048576 | tf_op jit(solution)/shard_map/all_to_all | solution.py:300
  192.8 36.3 %all-to-all-start.3 = ((bf16[8,128,24]{1,2,0:T(8,128)(2,1)}), bf16[8,128,24]{1,2,0:T(8,128)(2,1)S(1)}, u32[]{:S(2)}, u32[]{:S(2)}) async-start(bf16[8,128,24]{1,2,0:T(8,128)(2,1)} %broadcast_in_dim.45), calls=%async_computation.3 | async-start | bytes 98304 | tf_op jit(solution)/shard_map/all_to_all | solution.py:300
  196.2 165.3 %all-gather.12.cloned.1.call-start = ((), (), s32[]{:S(2)}) async-start(), calls=%async_computation.15 | async-start | bytes 4718592 | tf_op jit(solution)/shard_map/all_gather | solution.py:292
  227.6 27.8 %collective-permute-start.5 = (bf16[8,64,1152]{2,1,0:T(8,128)(2,1)}, bf16[8,64,1152]{2,1,0:T(8,128)(2,1)}, u32[]{:S(2)}, u32[]{:S(2)}) collective-permute-start(bf16[8,64,1152]{2,1,0:T(8,128)(2,1)} %all-to-all-done.2), channel_id=1, source_target_pairs={{0,2},{1,3},{2,0},{3,1},{4,6},{5,7},{6,4},{7,5},{8,10},{9,11},{10,... | collective-permute-start | bytes 3538952 | tf_op jit(solution)/shard_map/ppermute | solution.py:242
  229.1 89.8 %collective-permute-start.4 = (bf16[8,64,1152]{2,1,0:T(8,128)(2,1)}, bf16[8,64,1152]{2,1,0:T(8,128)(2,1)}, u32[]{:S(2)}, u32[]{:S(2)}) collective-permute-start(bf16[8,64,1152]{2,1,0:T(8,128)(2,1)} %all-to-all-done.2), channel_id=1, source_target_pairs={{0,1},{1,0},{2,3},{3,2},{4,5},{5,4},{6,7},{7,6},{8,9},{9,8},{10,11... | collective-permute-start | bytes 3538952 | tf_op jit(solution)/shard_map/ppermute | solution.py:242
  255.5 63.5 %collective-permute-start.15 = (bf16[2,1408,512]{2,1,0:T(8,128)(2,1)}, bf16[2,1408,512]{2,1,0:T(8,128)(2,1)}, u32[]{:S(2)}, u32[]{:S(2)}) collective-permute-start(bf16[2,1408,512]{2,1,0:T(8,128)(2,1)} %param.23), channel_id=1, source_target_pairs={{0,2},{1,3},{2,0},{3,1},{4,6},{5,7},{6,4},{7,5},{8,10},{9,11},{10,... | collective-permute-start | bytes 8650760 | tf_op jit(solution)/shard_map/ppermute | solution.py:242
  267.8 51.7 %collective-permute-start.6 = (bf16[8,64,1152]{2,1,0:T(8,128)(2,1)}, bf16[8,64,1152]{2,1,0:T(8,128)(2,1)S(1)}, u32[]{:S(2)}, u32[]{:S(2)}) collective-permute-start(bf16[8,64,1152]{2,1,0:T(8,128)(2,1)} %collective-permute-done.5), channel_id=1, source_target_pairs={{0,1},{1,0},{2,3},{3,2},{4,5},{5,4},{6,7},{7,6},{8,9},{9,8},{10,11... | collective-permute-start | bytes 3538952 | tf_op jit(solution)/shard_map/ppermute | solution.py:242
  287.4 310.4 %reduce-scatter.3.cloned.1.call-start = ((), (), s32[]{:S(2)}) async-start(), calls=%async_computation.16 | async-start | bytes 9437184 | tf_op jit(solution)/shard_map/reduce_scatter | solution.py:296
  318.9 5.5 collective-permute-start.11
  319.5 14.8 %collective-permute-start.12 = (bf16[2,128,2816]{2,1,0:T(8,128)(2,1)}, bf16[2,128,2816]{2,1,0:T(8,128)(2,1)S(1)}, u32[]{:S(2)}, u32[]{:S(2)}) collective-permute-start(bf16[2,128,2816]{2,1,0:T(8,128)(2,1)} %collective-permute-done.7), channel_id=1, source_target_pairs={{0,1},{1,0},{2,3},{3,2},{4,5},{5,4},{6,7},{7,6},{8,9},{9,8},{10,11... | collective-permute-start | bytes 4325384 | tf_op jit(solution)/shard_map/ppermute | solution.py:242
  323.7 11.7 %collective-permute-start.13 = (bf16[2,128,2816]{2,1,0:T(8,128)(2,1)}, bf16[2,128,2816]{2,1,0:T(8,128)(2,1)S(1)}, u32[]{:S(2)}, u32[]{:S(2)}) collective-permute-start(bf16[2,128,2816]{2,1,0:T(8,128)(2,1)} %collective-permute-done.9), channel_id=1, source_target_pairs={{0,1},{1,0},{2,3},{3,2},{4,5},{5,4},{6,7},{7,6},{8,9},{9,8},{10,11... | collective-permute-start | bytes 4325384 | tf_op jit(solution)/shard_map/ppermute | solution.py:242
  324.4 20.9 %collective-permute-start.16 = (bf16[2,1408,512]{2,1,0:T(8,128)(2,1)}, bf16[2,1408,512]{2,1,0:T(8,128)(2,1)S(1)}, u32[]{:S(2)}, u32[]{:S(2)}) collective-permute-start(bf16[2,1408,512]{2,1,0:T(8,128)(2,1)} %collective-permute-done.15), channel_id=1, source_target_pairs={{0,1},{1,0},{2,3},{3,2},{4,5},{5,4},{6,7},{7,6},{8,9},{9,8},{10,11... | collective-permute-start | bytes 8650760 | tf_op jit(solution)/shard_map/ppermute | solution.py:242
  445.7 243.5 %all-gather.14.cloned.1.call-start = ((), (), s32[]{:S(2)}) async-start(), calls=%async_computation.18 | async-start | bytes 4718592 | tf_op jit(solution)/shard_map/all_gather | solution.py:292
  451.7 5.5 collective-permute-start.18
  470.8 9.6 %collective-permute-start.19 = (bf16[2,512,2816]{2,1,0:T(8,128)(2,1)}, bf16[2,512,2816]{2,1,0:T(8,128)(2,1)S(1)}, u32[]{:S(2)}, u32[]{:S(2)}) collective-permute-start(bf16[2,512,2816]{2,1,0:T(8,128)(2,1)} %shard_map.217), channel_id=1, source_target_pairs={{0,1},{1,0},{2,3},{3,2},{4,5},{5,4},{6,7},{7,6},{8,9},{9,8},{10,11... | collective-permute-start | bytes 17301512 | tf_op jit(solution)/shard_map/ppermute | solution.py:242
  471.0 65.6 %collective-permute-start.23 = (bf16[2,1408,512]{2,1,0:T(8,128)(2,1)}, bf16[2,1408,512]{2,1,0:T(8,128)(2,1)}, u32[]{:S(2)}, u32[]{:S(2)}) collective-permute-start(bf16[2,1408,512]{2,1,0:T(8,128)(2,1)} %shard_map.216), channel_id=1, source_target_pairs={{0,2},{1,3},{2,0},{3,1},{4,6},{5,7},{6,4},{7,5},{8,10},{9,11},{10,... | collective-permute-start | bytes 8650760 | tf_op jit(solution)/shard_map/ppermute | solution.py:242
  502.2 95.5 %collective-permute-start.22 = (bf16[2,512,2816]{2,1,0:T(8,128)(2,1)}, bf16[2,512,2816]{2,1,0:T(8,128)(2,1)}, u32[]{:S(2)}, u32[]{:S(2)}) collective-permute-start(bf16[2,512,2816]{2,1,0:T(8,128)(2,1)} %shard_map.221), channel_id=1, source_target_pairs={{0,1},{1,0},{2,3},{3,2},{4,5},{5,4},{6,7},{7,6},{8,9},{9,8},{10,11... | collective-permute-start | bytes 17301512 | tf_op jit(solution)/shard_map/ppermute | solution.py:242
  502.2 95.5 %collective-permute-start.20 = (bf16[1,512,2816]{2,1,0:T(8,128)(2,1)}, bf16[1,512,2816]{2,1,0:T(8,128)(2,1)S(1)}, u32[]{:S(2)}, u32[]{:S(2)}) collective-permute-start(bf16[1,512,2816]{2,1,0:T(8,128)(2,1)} %shard_map.218), channel_id=1, source_target_pairs={{0,2},{1,3},{2,0},{3,1},{4,6},{5,7},{6,4},{7,5},{8,10},{9,11},{10,... | collective-permute-start | bytes 8650760 | tf_op jit(solution)/shard_map/ppermute | solution.py:242
  540.8 25.5 %collective-permute-start.21 = (bf16[2,1408,512]{2,1,0:T(8,128)(2,1)}, bf16[2,1408,512]{2,1,0:T(8,128)(2,1)}, u32[]{:S(2)}, u32[]{:S(2)}) collective-permute-start(bf16[2,1408,512]{2,1,0:T(8,128)(2,1)} %shard_map.220), channel_id=1, source_target_pairs={{0,1},{1,0},{2,3},{3,2},{4,5},{5,4},{6,7},{7,6},{8,9},{9,8},{10,11... | collective-permute-start | bytes 8650760 | tf_op jit(solution)/shard_map/ppermute | solution.py:242
  604.9 229.8 %reduce-scatter.5.cloned.1.call-start = ((), (), s32[]{:S(2)}) async-start(), calls=%async_computation.17 | async-start | bytes 4718592 | tf_op jit(solution)/shard_map/reduce_scatter | solution.py:296
  604.9 69.3 %collective-permute-start.26 = (bf16[1,512,2816]{2,1,0:T(8,128)(2,1)}, bf16[1,512,2816]{2,1,0:T(8,128)(2,1)}, u32[]{:S(2)}, u32[]{:S(2)}) collective-permute-start(bf16[1,512,2816]{2,1,0:T(8,128)(2,1)} %copy-done.15), channel_id=1, source_target_pairs={{0,2},{1,3},{2,0},{3,1},{4,6},{5,7},{6,4},{7,5},{8,10},{9,11},{10,... | collective-permute-start | bytes 8650760 | tf_op jit(solution)/shard_map/ppermute | solution.py:242
  684.5 52.6 %all-to-all-start.5 = ((bf16[8,128,576]{1,2,0:T(8,128)(2,1)}), bf16[8,128,576]{1,2,0:T(8,128)(2,1)}, u32[]{:S(2)}, u32[]{:S(2)}) async-start(bf16[8,128,576]{1,2,0:T(8,128)(2,1)} %pad_maximum_fusion.11), calls=%async_computation.7 | async-start | bytes 2359296 | tf_op jit(solution)/shard_map/all_to_all | solution.py:300
  694.5 17.2 %collective-permute-start.27 = (bf16[512,640]{1,0:T(8,128)(2,1)S(1)}, bf16[512,640]{1,0:T(8,128)(2,1)S(1)}, u32[]{:S(2)}, u32[]{:S(2)}) collective-permute-start(bf16[512,640]{1,0:T(8,128)(2,1)S(1)} %shard_map.224), channel_id=1, source_target_pairs={{0,1},{1,0},{2,3},{3,2},{4,5},{5,4},{6,7},{7,6},{8,9},{9,8},{10,11... | collective-permute-start | bytes 1966088 | tf_op jit(solution)/shard_map/ppermute | solution.py:242
  698.4 17.0 %collective-permute-start.29 = (bf16[512,640]{1,0:T(8,128)(2,1)}, bf16[512,640]{1,0:T(8,128)(2,1)}, u32[]{:S(2)}, u32[]{:S(2)}) collective-permute-start(bf16[512,640]{1,0:T(8,128)(2,1)} %shard_map.226), channel_id=1, source_target_pairs={{0,2},{1,3},{2,0},{3,1},{4,6},{5,7},{6,4},{7,5},{8,10},{9,11},{10,... | collective-permute-start | bytes 1966088 | tf_op jit(solution)/shard_map/ppermute | solution.py:242
  711.6 37.2 %collective-permute-start.37 = (bf16[512,128]{1,0:T(8,128)(2,1)}, bf16[512,128]{1,0:T(8,128)(2,1)}, u32[]{:S(2)}, u32[]{:S(2)}) collective-permute-start(bf16[512,128]{1,0:T(8,128)(2,1)} %bitcast.88), channel_id=1, source_target_pairs={{0,1},{1,0},{2,3},{3,2},{4,5},{5,4},{6,7},{7,6},{8,9},{9,8},{10,11... | collective-permute-start | bytes 393224 | tf_op jit(solution)/shard_map/ppermute | solution.py:242
  742.7 34.8 %collective-permute-start.31 = (bf16[1,512,640]{2,1,0:T(8,128)(2,1)S(1)}, bf16[1,512,640]{2,1,0:T(8,128)(2,1)S(1)}, u32[]{:S(2)}, u32[]{:S(2)}) collective-permute-start(bf16[1,512,640]{2,1,0:T(8,128)(2,1)S(1)} %shard_map.229), channel_id=1, source_target_pairs={{0,1},{1,0},{2,3},{3,2},{4,5},{5,4},{6,7},{7,6},{8,9},{9,8},{10,11... | collective-permute-start | bytes 1966088 | tf_op jit(solution)/shard_map/ppermute | solution.py:242
  743.8 57.1 %collective-permute-start.39 = (bf16[8,64,1152]{2,1,0:T(8,128)(2,1)}, bf16[8,64,1152]{2,1,0:T(8,128)(2,1)}, u32[]{:S(2)}, u32[]{:S(2)}) collective-permute-start(bf16[8,64,1152]{2,1,0:T(8,128)(2,1)} %get-tuple-element.122), channel_id=1, source_target_pairs={{0,2},{1,3},{2,0},{3,1},{4,6},{5,7},{6,4},{7,5},{8,10},{9,11},{10,... | collective-permute-start | bytes 3538952 | tf_op jit(solution)/shard_map/ppermute | solution.py:242
  744.2 12.8 %collective-permute-start.36 = (bf16[512,128]{1,0:T(8,128)(2,1)}, bf16[512,128]{1,0:T(8,128)(2,1)}, u32[]{:S(2)}, u32[]{:S(2)}) collective-permute-start(bf16[512,128]{1,0:T(8,128)(2,1)} %bitcast.86), channel_id=1, source_target_pairs={{0,1},{1,0},{2,3},{3,2},{4,5},{5,4},{6,7},{7,6},{8,9},{9,8},{10,11... | collective-permute-start | bytes 393224 | tf_op jit(solution)/shard_map/ppermute | solution.py:242
  744.4 51.9 %all-to-all-start.8 = ((bf16[8,64,640]{2,1,0:T(8,128)(2,1)}), bf16[8,64,640]{2,1,0:T(8,128)(2,1)}, u32[]{:S(2)}, u32[]{:S(2)}) async-start(bf16[8,64,640]{2,1,0:T(8,128)(2,1)} %bitcast.81), calls=%async_computation.10 | async-start | bytes 1310720 | tf_op jit(solution)/shard_map/all_to_all | solution.py:300
  750.5 24.9 %collective-permute-start.38 = (bf16[512,128]{1,0:T(8,128)(2,1)}, bf16[512,128]{1,0:T(8,128)(2,1)}, u32[]{:S(2)}, u32[]{:S(2)}) collective-permute-start(bf16[512,128]{1,0:T(8,128)(2,1)} %add_convert_fusion.2), channel_id=1, source_target_pairs={{0,2},{1,3},{2,0},{3,1},{4,6},{5,7},{6,4},{7,5},{8,10},{9,11},{10,... | collective-permute-start | bytes 393224 | tf_op jit(solution)/shard_map/ppermute | solution.py:242
  777.4 4.9 collective-permute-start.30
  777.9 17.2 %collective-permute-start.32 = (bf16[1,512,640]{2,1,0:T(8,128)(2,1)S(1)}, bf16[1,512,640]{2,1,0:T(8,128)(2,1)S(1)}, u32[]{:S(2)}, u32[]{:S(2)}) collective-permute-start(bf16[1,512,640]{2,1,0:T(8,128)(2,1)S(1)} %shard_map.230), channel_id=1, source_target_pairs={{0,2},{1,3},{2,0},{3,1},{4,6},{5,7},{6,4},{7,5},{8,10},{9,11},{10,... | collective-permute-start | bytes 1966088 | tf_op jit(solution)/shard_map/ppermute | solution.py:242
  796.3 21.8 %all-to-all-start.6 = ((bf16[8,64,640]{2,1,0:T(8,128)(2,1)}), bf16[8,64,640]{2,1,0:T(8,128)(2,1)S(1)}, u32[]{:S(2)}, u32[]{:S(2)}) async-start(bf16[8,64,640]{2,1,0:T(8,128)(2,1)} %bitcast.80), calls=%async_computation.8 | async-start | bytes 1310720 | tf_op jit(solution)/shard_map/all_to_all | solution.py:300
  818.9 10.2 %all-to-all-start.7 = ((f32[8,1,144]{2,1,0:T(1,128)}), f32[8,1,144]{2,1,0:T(1,128)S(1)}, u32[]{:S(2)}, u32[]{:S(2)}) async-start(f32[8,1,144]{2,1,0:T(1,128)} %all_to_all.40), calls=%async_computation.9 | async-start | bytes 16384 | tf_op jit(solution)/shard_map/all_to_all | solution.py:300
  829.1 30.4 %all-to-all-start.9 = ((bf16[8,64,1152]{2,1,0:T(8,128)(2,1)}), bf16[8,64,1152]{2,1,0:T(8,128)(2,1)S(1)}, u32[]{:S(2)}, u32[]{:S(2)}) async-start(bf16[8,64,1152]{2,1,0:T(8,128)(2,1)} %add_convert_fusion), calls=%async_computation.11 | async-start | bytes 2359296 | tf_op jit(solution)/shard_map/all_to_all | solution.py:300
  (101 other events, 1455.6 us)
Sparse Core Ops, SparseCore 0:
  10.7 93.7 all-gather.5
  107.4 105.2 all-gather.7
  215.4 71.8 all-gather.9
  289.9 71.6 all-gather.11
  445.9 147.2 reduce-scatter.2
  604.9 82.8 all-gather.13
  692.5 108.3 reduce-scatter.4

commit v11 on v10

--- a/solution.py
+++ b/solution.py
@@ -842,13 +842,13 @@
         gains = fsdp_reduce(gains.reshape(n_ctx, 4, -1).transpose(1, 0, 2), rank, first)
         return gains, jnp.sum(ctx_exchange(after(gains, second)), 0)
 
-    def exchange_shared(early, late):
+    def sum_shared(early):
         far = fsdp_swap(after(shared_other, early), 2)
         total = shared_own.astype(jnp.float32) + far.astype(jnp.float32)
-        return ctx_exchange(after(total.astype(jnp.bfloat16), late))
+        return total.astype(jnp.bfloat16)
 
     token_grad, stage, gains_grad, query_w, latent_w, expand_w, output_w = attn_backward(
-        resid_grad.astype(jnp.bfloat16), gu_back[1:], reduce_gains, exchange_shared
+        resid_grad.astype(jnp.bfloat16), gu_back[1:], reduce_gains, sum_shared
     )
     shared_sums, sums_there = stage
     shared_gu_grad, shared_dn_grad = shared_unpack_call(
@@ -950,7 +950,7 @@
         own_heads = ctx_exchange(heads_out).transpose(1, 0, 2).reshape(tok_dev, H * DV)
         return tokens + dot_f32(after(own_heads, early), saved["output_full"])
 
-    def backward(resid_bf, stages, reduce_gains, exchange_shared):
+    def backward(resid_bf, stages, reduce_gains, sum_shared):
         query_full, latent_full = saved["query_full"], saved["latent_full"]
         cos_table, sin_table = saved["cos_table"], saved["sin_table"]
         normed_bf = saved["normed_bf"]
@@ -982,7 +982,11 @@
             return head_terms_call(k, normed_bf, query_late, resid_all, saved["heads_out"], *more)
 
         head_sums = fsdp_reduce_terms(head_terms)[1]
-        key_got = after(key_sent, head_sums)
+        expand_g = expand_g.transpose(1, 0, 2)
+        expand_blocks = expand_g.reshape(KVL, 4, -1).transpose(1, 0, 2).astype(jnp.bfloat16)
+        expand_w = fsdp_reduce(expand_blocks, rank, in_part)
+        shared_terms = sum_shared(in_part)
+        key_got = after(key_sent, head_sums, shared_terms, expand_w)
         head_sums = ctx_exchange(after(head_sums, key_sent).reshape(n_ctx, rows, -1))
         query_terms = head_sums[:, :, :q_wide].astype(jnp.float32)
         output_w = head_sums[:, :, q_wide:].astype(jnp.float32)
@@ -1014,13 +1018,10 @@
         gain_in_grad = gain_in_grad + jnp.sum(in_own * (token_cols * inv_in), 0)
         gain_in_grad = columns_in_order(gain_in_grad[None], n_ctx, rank)[0]
         gains_there, gains_grad = reduce_gains(gain_in_grad, gain_lat_grad, latent_own, latent_got)
-        expand_g = expand_g.transpose(1, 0, 2)
-        expand_blocks = expand_g.reshape(KVL, 4, -1).transpose(1, 0, 2).astype(jnp.bfloat16)
-        expand_w = fsdp_reduce(expand_blocks, rank)
         nope_w = query_terms[:, :, :n_wide].reshape(n_ctx, rows, heads, DN)
         rot_w = query_terms[:, :, n_wide:].reshape(n_ctx, rows, heads, DR)
         query_w = jnp.concatenate([nope_w, rot_w], -1).transpose(1, 0, 2, 3).reshape(rows, -1)
-        shared_sums = exchange_shared(in_part, latent_got)
+        shared_sums = ctx_exchange(after(shared_terms, latent_got))
         in_grad = after(in_grad, gains_there).astype(jnp.float32) + in_own
         token_grad = norm_backward(token_cols, inv_in, saved["gain_cols"], in_grad)[0]
         token_grad = columns_in_order(token_grad, n_ctx, rank)
@@ -1084,7 +1085,7 @@
     )
     resid_mid = tokens + dot_f32(heads_out, output_full)
 
-    def backward(resid_bf, stages, reduce_gains, exchange_shared):
+    def backward(resid_bf, stages, reduce_gains, sum_shared):
         output_g = dot_f32(heads_out, resid_bf, ((0,), (0,)))
         heads_grad = (
             dot_f32(resid_bf, output_full, ((1,), (1,)))
@@ -1148,7 +1149,7 @@
             for g, at in ((query_g, 0), (latent_g, 0), (expand_g, 1), (output_g, 1))
         ]
         gains_grad = reduce_gains(gain_in_grad, gain_lat_grad)[1]
-        return (token_grad, (exchange_shared(resid_bf, lat_buffer), latent_grad), gains_grad, *scattered)
+        return (token_grad, (ctx_exchange(sum_shared(resid_bf)), latent_grad), gains_grad, *scattered)
 
     return (lambda early: latent_full), (lambda early: resid_mid), backward
 

time: 878 us -> 865 us (0.985)
  waiting for transfers between devices: 334 us -> 322 us
    unnamed x209 -> x199, local copies, waits for them, and re-layouts: 34.3 us -> 35.6 us
  transfers between devices with their start and end apart: 56 -> 56, of which waited for: 27 -> 27; matrix products, arithmetic and copies ran while one was open for 24% -> 24% of each run, Pallas kernels for 12% -> 13%
where the time goes in v11:
time: 865 us; the launch traced here: 856 us
  waiting for transfers between devices  322 us (37%)
  Pallas kernels  178 us (21%)
  local copies, waits for them, and re-layouts  104 us (12%)
  other arithmetic  78.7 us (9%)
  starting transfers between devices  66.6 us (8%)
  matrix products  59.4 us (7%)
  blocking collectives  30.9 us (4%)
  between operations  16.2 us (2%)
    ppermute x40, waiting for transfers between devices, fsdp_swap(): lax.ppermute(values, 'fsdp', [(at, at ^ distance) for at in range(count)])  256 us
    dot_general x12, matrix products, dot_f32(): lax.dot_general(left, right, (dims, ((), ())), preferred_element_type=jnp...  59.4 us
    pallas_call x13, Pallas kernels, expert_grad_call(): pl.pallas_call(functools.partial(expert_grad_body, each=len(each)), grid=...  58.9 us
    pallas_call x1, Pallas kernels, experts_call(): pl.pallas_call(experts_body, grid=(count,), in_specs=[pl.BlockSpec((1, sl...  48.7 us
    all_to_all x9, starting transfers between devices, ctx_exchange(): lax.all_to_all(values, 'ctx', split_axis=0, concat_axis=0, tiled=True)  44 us
    unnamed x199, local copies, waits for them, and re-layouts  35.6 us
    all_gather x4, waiting for transfers between devices, ctx_gather(): return lax.all_gather(values, 'ctx', axis=0, tiled=True)  34.7 us
    all_to_all x9, waiting for transfers between devices, ctx_exchange(): lax.all_to_all(values, 'ctx', split_axis=0, concat_axis=0, tiled=True)  31.4 us
  transfers between devices with their start and end apart: 56, of which 27 were waited for; matrix products, arithmetic and copies ran while one was open for 24% of the time, Pallas kernels for 13%

profile of v11, /device:TPU:0, one launch (start us, length us, event | category | flops | bytes accessed | tf_op | source)
XLA Modules:
  0.0 856.3 jit_solution(13266730408175923431)
XLA Ops:
  12.8 7.3 all-to-all-start
  20.1 5.2 fusion.117
  26.8 31.7 %collective-permute-done = bf16[2,128,2816]{2,1,0:T(8,128)(2,1)} collective-permute-done((bf16[2,128,2816]{2,1,0:T(8,128)(2,1)S(1)}, bf16[2,128,2816]{2,1,0:T(8,128)(2,1)}, u32[]{:S(2)}, u32[]{:S(2)}) %collective-permute-start) | collective-permute-done | bytes 1441824 | tf_op jit(solution)/shard_map/ppermute | solution.py:242
  64.5 24.4 %collective-permute-done.2 = bf16[8,64,1088]{2,1,0:T(8,128)(2,1)S(1)} collective-permute-done((bf16[8,64,1088]{2,1,0:T(8,128)(2,1)S(1)}, bf16[8,64,1088]{2,1,0:T(8,128)(2,1)S(1)}, u32[]{:S(2)}, u32[]{:S(2)}) %collective-permute-start.2) | collective-permute-done | bytes 1114144 | tf_op jit(solution)/shard_map/ppermute | solution.py:242
  95.6 8.9 %all-gather.6.cloned.1.call-done = bf16[1024,2048]{1,0:T(8,128)(2,1)} async-done(((bf16[128,2048]{1,0:T(8,128)(2,1)}), bf16[1024,2048]{1,0:T(8,128)(2,1)}) %all-gather.6.cloned.1.call-update) | async-done | bytes 4194320 | tf_op jit(solution)/shard_map/all_gather | solution.py:292
  127.7 6.1 fusion.25
  143.8 13.8 %shard_map.212 = (bf16[1024,256]{1,0:T(8,128)(2,1)S(1)}, f32[2,1024,512]{2,1,0:T(8,128)}, f32[2,1024,1]{2,1,0:T(8,128)S(1)}) custom-call(bf16[1024,256]{1,0:T(8,128)(2,1)S(1)} %slice.307.nope_ref, bf16[2,1024,64]{2,1,0:T(8,128)(2,1)S(1)} %pad_maximum_fusion.17.rot_ref, bf16[1024,512]{1,0:T(8,128)(2,1)} %multiply_convert_fusion.1.lat_ref, ...), custom_call_target="tpu_custom_call" | custom-call | tf_op jit(solution)/shard_map/pallas_call | solution.py:406
  160.1 5.3 all-to-all-start.1
  170.9 18.8 %collective-permute-done.7 = bf16[2,128,2816]{2,1,0:T(8,128)(2,1)} collective-permute-done((bf16[2,128,2816]{2,1,0:T(8,128)(2,1)}, bf16[2,128,2816]{2,1,0:T(8,128)(2,1)}, u32[]{:S(2)}, u32[]{:S(2)}) %collective-permute-start.7) | collective-permute-done | bytes 1441824 | tf_op jit(solution)/shard_map/ppermute | solution.py:242
  196.4 28.6 %collective-permute-done.9 = bf16[2,128,2816]{2,1,0:T(8,128)(2,1)} collective-permute-done((bf16[2,128,2816]{2,1,0:T(8,128)(2,1)}, bf16[2,128,2816]{2,1,0:T(8,128)(2,1)}, u32[]{:S(2)}, u32[]{:S(2)}) %collective-permute-start.9) | collective-permute-done | bytes 1441824 | tf_op jit(solution)/shard_map/ppermute | solution.py:242
  238.6 16.9 %collective-permute-done.5 = bf16[8,64,1152]{2,1,0:T(8,128)(2,1)} collective-permute-done((bf16[8,64,1152]{2,1,0:T(8,128)(2,1)}, bf16[8,64,1152]{2,1,0:T(8,128)(2,1)}, u32[]{:S(2)}, u32[]{:S(2)}) %collective-permute-start.5) | collective-permute-done | bytes 1179680 | tf_op jit(solution)/shard_map/ppermute | solution.py:242
  257.0 4.4 convert_bitcast_fusion
  261.3 6.4 multiply_reduce_fusion.5
  269.8 17.6 %all-gather.10.cloned.1.call-done = bf16[1024,2048]{1,0:T(8,128)(2,1)} async-done(((bf16[128,2048]{1,0:T(8,128)(2,1)}), bf16[1024,2048]{1,0:T(8,128)(2,1)}) %all-gather.10.cloned.1.call-update) | async-done | bytes 4194320 | tf_op jit(solution)/shard_map/all_gather | solution.py:292
  287.4 7.9 multiply_convert_fusion
  295.3 23.6 %collective-permute-done.15 = bf16[2,1408,512]{2,1,0:T(8,128)(2,1)} collective-permute-done((bf16[2,1408,512]{2,1,0:T(8,128)(2,1)}, bf16[2,1408,512]{2,1,0:T(8,128)(2,1)}, u32[]{:S(2)}, u32[]{:S(2)}) %collective-permute-start.15) | collective-permute-done | bytes 2883616 | tf_op jit(solution)/shard_map/ppermute | solution.py:242
  324.8 7.0 pad_maximum_fusion.5.gate_up_ref
  339.7 5.7 constant_dynamic-update-slice_fusion.gu_ref
  345.4 8.0 pad_maximum_fusion.dn_ref
  353.4 8.2 all-gather.12.cloned.1.call-done
  361.6 6.3 fusion.124
  372.1 5.9 convolution_convert_fusion.1
  378.0 48.7 %shard_map.213 = (bf16[2,432,1408]{2,1,0:T(8,128)(2,1)}, bf16[2,432,2816]{2,1,0:T(8,128)(2,1)}, bf16[2,432,2048]{2,1,0:T(8,128)(2,1)}, bf16[2,432,2048]{2,1,0:T(8,128)(2,1)}) custom-call(bf16[2,432,2048]{2,1,0:T(8,128)(2,1)} %bitcast.208, bf16[2,432,2048]{2,1,0:T(8,128)(2,1)} %bitcast.220, f32[2,432,1]{2,1,0:T(8,128)} %copy.472.gate_ref, ...), custom_call_target="tpu_custom_call" | custom-call | tf_op jit(solution)/shard_map/pallas_call | solution.py:518
  426.7 19.0 %shard_map.214 = bf16[1024,4096]{1,0:T(8,128)(2,1)} custom-call(bf16[1024,864]{1,0:T(8,128)(2,1)} %get-tuple-element.227.pick_ref, bf16[1024,768]{1,0:T(8,128)(2,1)S(1)} %pad_maximum_fusion.9.both_ref, bf16[1024,384]{1,0:T(8,128)(2,1)S(1)} %get-tuple-element.253.act_ref, bf16[864,2048]{1,0:T(8,128)(2,1)} %bitcast.239, bf16[864,2048]{1,0:T(8,128)(2,1)} %bitcast.238, ...), custom_call_target="tpu_custom_call" | custom-call | tf_op jit(solution)/shard_map/pallas_call | solution.py:652
  447.5 4.3 shard_map.215
  451.8 5.5 collective-permute-done.18.refs_2_
  458.9 4.6 shard_map.216
  463.5 7.4 shard_map.217
  472.5 8.0 collective-permute-done.19
  483.4 4.3 shard_map.219
  489.3 5.4 shard_map.218
  494.7 7.6 shard_map.221
  503.8 32.9 %collective-permute-done.23.refs_3_ = bf16[2,1408,512]{2,1,0:T(8,128)(2,1)} collective-permute-done((bf16[2,1408,512]{2,1,0:T(8,128)(2,1)}, bf16[2,1408,512]{2,1,0:T(8,128)(2,1)}, u32[]{:S(2)}, u32[]{:S(2)}) %collective-permute-start.23) | collective-permute-done | bytes 2883616 | tf_op jit(solution)/shard_map/ppermute | solution.py:242
  550.7 6.9 copy.473
  566.4 5.8 shard_map.222
  572.2 25.7 %collective-permute-done.20.refs_3_ = bf16[1,512,2816]{2,1,0:T(8,128)(2,1)S(1)} collective-permute-done((bf16[1,512,2816]{2,1,0:T(8,128)(2,1)}, bf16[1,512,2816]{2,1,0:T(8,128)(2,1)S(1)}, u32[]{:S(2)}, u32[]{:S(2)}) %collective-permute-start.20) | collective-permute-done | bytes 2883616 | tf_op jit(solution)/shard_map/ppermute | solution.py:242
  606.5 4.6 convolution_convert_fusion.2
  611.2 30.9 %all_to_all.54 = bf16[8,128,256]{2,1,0:T(8,128)(2,1)S(1)} all-to-all(bf16[8,128,256]{2,1,0:T(8,128)(2,1)S(1)} %bitcast.245), channel_id=1, replica_groups=mesh['ctx'=8,'fsdp'=4] {'ctx'}, dimensions={0} | all-to-all | bytes 1048576 | tf_op jit(solution)/shard_map/all_to_all | solution.py:300
  642.2 24.9 %shard_map.223 = (bf16[1024,256]{1,0:T(8,128)(2,1)S(1)}, f32[2,1024,64]{2,1,0:T(8,128)}, f32[2,512,256]{2,1,0:T(8,128)}, f32[1024,512]{1,0:T(8,128)}, f32[1024,64]{1,0:T(8,128)S(1)}) custom-call(bf16[1024,256]{1,0:T(8,128)(2,1)S(1)} %bitcast.219, bf16[1024,256]{1,0:T(8,128)(2,1)S(1)} %copy-done.12, bf16[2,1024,64]{2,1,0:T(8,128)(2,1)S(1)} %copy-done.10, ...), custom_call_target="tpu_custom_call" | custom-call | tf_op jit(solution)/shard_map/pallas_call | solution.py:441
  674.7 6.6 fusion.3
  685.0 4.8 all-to-all-start.5
  709.5 12.3 %collective-permute-done.33 = bf16[512,128]{1,0:T(8,128)(2,1)S(1)} collective-permute-done((bf16[512,128]{1,0:T(8,128)(2,1)S(1)}, bf16[512,128]{1,0:T(8,128)(2,1)S(1)}, u32[]{:S(2)}, u32[]{:S(2)}) %collective-permute-start.33) | collective-permute-done | bytes 131104 | tf_op jit(solution)/shard_map/ppermute | solution.py:242
  725.1 8.7 %collective-permute-done.29.refs_5_ = bf16[512,640]{1,0:T(8,128)(2,1)S(1)} collective-permute-done((bf16[512,640]{1,0:T(8,128)(2,1)S(1)}, bf16[512,640]{1,0:T(8,128)(2,1)S(1)}, u32[]{:S(2)}, u32[]{:S(2)}) %collective-permute-start.29) | collective-permute-done | bytes 655392 | tf_op jit(solution)/shard_map/ppermute | solution.py:242
  743.5 5.7 all-to-all-start.8
  756.3 10.9 %collective-permute-done.36.refs_3_ = bf16[1,512,640]{2,1,0:T(8,128)(2,1)S(1)} collective-permute-done((bf16[1,512,640]{2,1,0:T(8,128)(2,1)S(1)}, bf16[1,512,640]{2,1,0:T(8,128)(2,1)S(1)}, u32[]{:S(2)}, u32[]{:S(2)}) %collective-permute-start.36) | collective-permute-done | bytes 655392 | tf_op jit(solution)/shard_map/ppermute | solution.py:242
  769.6 6.0 all-to-all-start.6
  785.3 19.0 %all-to-all-done.6 = bf16[8,64,640]{2,1,0:T(8,128)(2,1)S(1)} async-done(((bf16[8,64,640]{2,1,0:T(8,128)(2,1)}), bf16[8,64,640]{2,1,0:T(8,128)(2,1)S(1)}, u32[]{:S(2)}, u32[]{:S(2)}) %all-to-all-start.6) | async-done | bytes 655392 | tf_op jit(solution)/shard_map/all_to_all | solution.py:300
  829.6 11.9 %shard_map.233 = f32[2,512,2816]{2,1,0:T(8,128)} custom-call(bf16[2,432,2048]{2,1,0:T(8,128)(2,1)} %bitcast.211, bf16[2,432,2816]{2,1,0:T(8,128)(2,1)} %get-tuple-element.93.refs_1_, bf16[2,512,2816]{2,1,0:T(8,128)(2,1)} %collective-permute-done.22.refs_2_, bf16[1,512,2816]{2,1,0:T(8,128)(2,1)S(1)} %copy-done.14, ...), custom_call_target="tpu_custom_call" | custom-call | tf_op jit(solution)/shard_map/pallas_call | solution.py:555
  (490 shorter events, 239.9 us)
Async XLA Ops:
  7.2 97.4 %all-gather.6.cloned.1.call-start = ((), (), s32[]{:S(2)}) async-start(), calls=%async_computation.12 | async-start | bytes 4718592 | tf_op jit(solution)/shard_map/all_gather | solution.py:292
  12.8 49.9 %all-to-all-start = ((bf16[8,64,960]{2,1,0:T(8,128)(2,1)}), bf16[8,64,960]{2,1,0:T(8,128)(2,1)S(1)}, u32[]{:S(2)}, u32[]{:S(2)}) async-start(bf16[8,64,960]{2,1,0:T(8,128)(2,1)} %pad_maximum_fusion.12), calls=%async_computation | async-start | bytes 2097152 | tf_op jit(solution)/shard_map/all_to_all | solution.py:300
  20.1 241.2 %all-gather.8.cloned.1.call-start = ((), (), s32[]{:S(2)}) async-start(), calls=%async_computation.13 | async-start | bytes 8650752 | tf_op jit(solution)/shard_map/all_gather | solution.py:919
  25.4 33.1 %collective-permute-start = (bf16[2,128,2816]{2,1,0:T(8,128)(2,1)S(1)}, bf16[2,128,2816]{2,1,0:T(8,128)(2,1)}, u32[]{:S(2)}, u32[]{:S(2)}) collective-permute-start(bf16[2,128,2816]{2,1,0:T(8,128)(2,1)S(1)} %get-tuple-element.234), channel_id=1, source_target_pairs={{0,2},{1,3},{2,0},{3,1},{4,6},{5,7},{6,4},{7,5},{8,10},{9,11},{10,... | collective-permute-start | bytes 4325384 | tf_op jit(solution)/shard_map/ppermute | solution.py:242
  62.9 26.0 %collective-permute-start.2 = (bf16[8,64,1088]{2,1,0:T(8,128)(2,1)S(1)}, bf16[8,64,1088]{2,1,0:T(8,128)(2,1)S(1)}, u32[]{:S(2)}, u32[]{:S(2)}) collective-permute-start(bf16[8,64,1088]{2,1,0:T(8,128)(2,1)S(1)} %pad_maximum_fusion.10), channel_id=1, source_target_pairs={{0,2},{1,3},{2,0},{3,1},{4,6},{5,7},{6,4},{7,5},{8,10},{9,11},{10,... | collective-permute-start | bytes 3342344 | tf_op jit(solution)/shard_map/ppermute | solution.py:242
  64.5 24.4 %collective-permute-start.1 = (bf16[8,64,1088]{2,1,0:T(8,128)(2,1)S(1)}, bf16[8,64,1088]{2,1,0:T(8,128)(2,1)S(1)}, u32[]{:S(2)}, u32[]{:S(2)}) collective-permute-start(bf16[8,64,1088]{2,1,0:T(8,128)(2,1)S(1)} %pad_maximum_fusion.10), channel_id=1, source_target_pairs={{0,1},{1,0},{2,3},{3,2},{4,5},{5,4},{6,7},{7,6},{8,9},{9,8},{10,11... | collective-permute-start | bytes 3342344 | tf_op jit(solution)/shard_map/ppermute | solution.py:242
  104.6 235.1 %collective-permute-start.14 = (bf16[2,512,2816]{2,1,0:T(8,128)(2,1)}, bf16[2,512,2816]{2,1,0:T(8,128)(2,1)}, u32[]{:S(2)}, u32[]{:S(2)}) collective-permute-start(bf16[2,512,2816]{2,1,0:T(8,128)(2,1)} %param.22), channel_id=1, source_target_pairs={{0,1},{1,0},{2,3},{3,2},{4,5},{5,4},{6,7},{7,6},{8,9},{9,8},{10,11... | collective-permute-start | bytes 17301512 | tf_op jit(solution)/shard_map/ppermute | solution.py:242
  104.7 63.4 %collective-permute-start.8 = (bf16[2,128,2816]{2,1,0:T(8,128)(2,1)}, bf16[2,128,2816]{2,1,0:T(8,128)(2,1)}, u32[]{:S(2)}, u32[]{:S(2)}) collective-permute-start(bf16[2,128,2816]{2,1,0:T(8,128)(2,1)} %get-tuple-element.232), channel_id=1, source_target_pairs={{0,2},{1,3},{2,0},{3,1},{4,6},{5,7},{6,4},{7,5},{8,10},{9,11},{10,... | collective-permute-start | bytes 4325384 | tf_op jit(solution)/shard_map/ppermute | solution.py:242
  106.2 83.5 %collective-permute-start.7 = (bf16[2,128,2816]{2,1,0:T(8,128)(2,1)}, bf16[2,128,2816]{2,1,0:T(8,128)(2,1)}, u32[]{:S(2)}, u32[]{:S(2)}) collective-permute-start(bf16[2,128,2816]{2,1,0:T(8,128)(2,1)} %get-tuple-element.233), channel_id=1, source_target_pairs={{0,2},{1,3},{2,0},{3,1},{4,6},{5,7},{6,4},{7,5},{8,10},{9,11},{10,... | collective-permute-start | bytes 4325384 | tf_op jit(solution)/shard_map/ppermute | solution.py:242
  106.8 118.3 %collective-permute-start.9 = (bf16[2,128,2816]{2,1,0:T(8,128)(2,1)}, bf16[2,128,2816]{2,1,0:T(8,128)(2,1)}, u32[]{:S(2)}, u32[]{:S(2)}) collective-permute-start(bf16[2,128,2816]{2,1,0:T(8,128)(2,1)} %get-tuple-element.231), channel_id=1, source_target_pairs={{0,2},{1,3},{2,0},{3,1},{4,6},{5,7},{6,4},{7,5},{8,10},{9,11},{10,... | collective-permute-start | bytes 4325384 | tf_op jit(solution)/shard_map/ppermute | solution.py:242
  108.2 237.2 %collective-permute-start.17 = (bf16[2,1408,512]{2,1,0:T(8,128)(2,1)}, bf16[2,1408,512]{2,1,0:T(8,128)(2,1)}, u32[]{:S(2)}, u32[]{:S(2)}) collective-permute-start(bf16[2,1408,512]{2,1,0:T(8,128)(2,1)} %param.23), channel_id=1, source_target_pairs={{0,1},{1,0},{2,3},{3,2},{4,5},{5,4},{6,7},{7,6},{8,9},{9,8},{10,11... | collective-permute-start | bytes 8650760 | tf_op jit(solution)/shard_map/ppermute | solution.py:242
  116.4 43.8 %all-to-all-start.2 = ((bf16[8,64,1152]{2,1,0:T(8,128)(2,1)}), bf16[8,64,1152]{2,1,0:T(8,128)(2,1)}, u32[]{:S(2)}, u32[]{:S(2)}) async-start(bf16[8,64,1152]{2,1,0:T(8,128)(2,1)} %fusion.32), calls=%async_computation.2 | async-start | bytes 2359296 | tf_op jit(solution)/shard_map/all_to_all | solution.py:300
  120.6 166.7 %all-gather.10.cloned.1.call-start = ((), (), s32[]{:S(2)}) async-start(), calls=%async_computation.14 | async-start | bytes 4718592 | tf_op jit(solution)/shard_map/all_gather | solution.py:292
  160.1 32.7 %all-to-all-start.1 = ((bf16[8,128,256]{1,2,0:T(8,128)(2,1)}), bf16[8,128,256]{1,2,0:T(8,128)(2,1)S(1)}, u32[]{:S(2)}, u32[]{:S(2)}) async-start(bf16[8,128,256]{1,2,0:T(8,128)(2,1)} %copy.456), calls=%async_computation.1 | async-start | bytes 1048576 | tf_op jit(solution)/shard_map/all_to_all | solution.py:300
  192.8 36.3 %all-to-all-start.3 = ((bf16[8,128,24]{1,2,0:T(8,128)(2,1)}), bf16[8,128,24]{1,2,0:T(8,128)(2,1)S(1)}, u32[]{:S(2)}, u32[]{:S(2)}) async-start(bf16[8,128,24]{1,2,0:T(8,128)(2,1)} %broadcast_in_dim.45), calls=%async_computation.3 | async-start | bytes 98304 | tf_op jit(solution)/shard_map/all_to_all | solution.py:300
  196.2 165.4 %all-gather.12.cloned.1.call-start = ((), (), s32[]{:S(2)}) async-start(), calls=%async_computation.15 | async-start | bytes 4718592 | tf_op jit(solution)/shard_map/all_gather | solution.py:292
  227.7 27.8 %collective-permute-start.5 = (bf16[8,64,1152]{2,1,0:T(8,128)(2,1)}, bf16[8,64,1152]{2,1,0:T(8,128)(2,1)}, u32[]{:S(2)}, u32[]{:S(2)}) collective-permute-start(bf16[8,64,1152]{2,1,0:T(8,128)(2,1)} %all-to-all-done.2), channel_id=1, source_target_pairs={{0,2},{1,3},{2,0},{3,1},{4,6},{5,7},{6,4},{7,5},{8,10},{9,11},{10,... | collective-permute-start | bytes 3538952 | tf_op jit(solution)/shard_map/ppermute | solution.py:242
  229.1 89.8 %collective-permute-start.4 = (bf16[8,64,1152]{2,1,0:T(8,128)(2,1)}, bf16[8,64,1152]{2,1,0:T(8,128)(2,1)}, u32[]{:S(2)}, u32[]{:S(2)}) collective-permute-start(bf16[8,64,1152]{2,1,0:T(8,128)(2,1)} %all-to-all-done.2), channel_id=1, source_target_pairs={{0,1},{1,0},{2,3},{3,2},{4,5},{5,4},{6,7},{7,6},{8,9},{9,8},{10,11... | collective-permute-start | bytes 3538952 | tf_op jit(solution)/shard_map/ppermute | solution.py:242
  255.5 63.5 %collective-permute-start.15 = (bf16[2,1408,512]{2,1,0:T(8,128)(2,1)}, bf16[2,1408,512]{2,1,0:T(8,128)(2,1)}, u32[]{:S(2)}, u32[]{:S(2)}) collective-permute-start(bf16[2,1408,512]{2,1,0:T(8,128)(2,1)} %param.23), channel_id=1, source_target_pairs={{0,2},{1,3},{2,0},{3,1},{4,6},{5,7},{6,4},{7,5},{8,10},{9,11},{10,... | collective-permute-start | bytes 8650760 | tf_op jit(solution)/shard_map/ppermute | solution.py:242
  267.8 51.7 %collective-permute-start.6 = (bf16[8,64,1152]{2,1,0:T(8,128)(2,1)}, bf16[8,64,1152]{2,1,0:T(8,128)(2,1)S(1)}, u32[]{:S(2)}, u32[]{:S(2)}) collective-permute-start(bf16[8,64,1152]{2,1,0:T(8,128)(2,1)} %collective-permute-done.5), channel_id=1, source_target_pairs={{0,1},{1,0},{2,3},{3,2},{4,5},{5,4},{6,7},{7,6},{8,9},{9,8},{10,11... | collective-permute-start | bytes 3538952 | tf_op jit(solution)/shard_map/ppermute | solution.py:242
  287.4 310.4 %reduce-scatter.3.cloned.1.call-start = ((), (), s32[]{:S(2)}) async-start(), calls=%async_computation.16 | async-start | bytes 9437184 | tf_op jit(solution)/shard_map/reduce_scatter | solution.py:296
  319.0 5.5 collective-permute-start.11
  319.5 14.7 %collective-permute-start.12 = (bf16[2,128,2816]{2,1,0:T(8,128)(2,1)}, bf16[2,128,2816]{2,1,0:T(8,128)(2,1)S(1)}, u32[]{:S(2)}, u32[]{:S(2)}) collective-permute-start(bf16[2,128,2816]{2,1,0:T(8,128)(2,1)} %collective-permute-done.7), channel_id=1, source_target_pairs={{0,1},{1,0},{2,3},{3,2},{4,5},{5,4},{6,7},{7,6},{8,9},{9,8},{10,11... | collective-permute-start | bytes 4325384 | tf_op jit(solution)/shard_map/ppermute | solution.py:242
  323.7 11.7 %collective-permute-start.13 = (bf16[2,128,2816]{2,1,0:T(8,128)(2,1)}, bf16[2,128,2816]{2,1,0:T(8,128)(2,1)S(1)}, u32[]{:S(2)}, u32[]{:S(2)}) collective-permute-start(bf16[2,128,2816]{2,1,0:T(8,128)(2,1)} %collective-permute-done.9), channel_id=1, source_target_pairs={{0,1},{1,0},{2,3},{3,2},{4,5},{5,4},{6,7},{7,6},{8,9},{9,8},{10,11... | collective-permute-start | bytes 4325384 | tf_op jit(solution)/shard_map/ppermute | solution.py:242
  324.4 20.9 %collective-permute-start.16 = (bf16[2,1408,512]{2,1,0:T(8,128)(2,1)}, bf16[2,1408,512]{2,1,0:T(8,128)(2,1)S(1)}, u32[]{:S(2)}, u32[]{:S(2)}) collective-permute-start(bf16[2,1408,512]{2,1,0:T(8,128)(2,1)} %collective-permute-done.15), channel_id=1, source_target_pairs={{0,1},{1,0},{2,3},{3,2},{4,5},{5,4},{6,7},{7,6},{8,9},{9,8},{10,11... | collective-permute-start | bytes 8650760 | tf_op jit(solution)/shard_map/ppermute | solution.py:242
  445.8 246.9 %all-gather.14.cloned.1.call-start = ((), (), s32[]{:S(2)}) async-start(), calls=%async_computation.18 | async-start | bytes 4718592 | tf_op jit(solution)/shard_map/all_gather | solution.py:292
  451.8 5.5 collective-permute-start.18
  470.9 9.6 %collective-permute-start.19 = (bf16[2,512,2816]{2,1,0:T(8,128)(2,1)}, bf16[2,512,2816]{2,1,0:T(8,128)(2,1)S(1)}, u32[]{:S(2)}, u32[]{:S(2)}) collective-permute-start(bf16[2,512,2816]{2,1,0:T(8,128)(2,1)} %shard_map.217), channel_id=1, source_target_pairs={{0,1},{1,0},{2,3},{3,2},{4,5},{5,4},{6,7},{7,6},{8,9},{9,8},{10,11... | collective-permute-start | bytes 17301512 | tf_op jit(solution)/shard_map/ppermute | solution.py:242
  471.0 65.6 %collective-permute-start.23 = (bf16[2,1408,512]{2,1,0:T(8,128)(2,1)}, bf16[2,1408,512]{2,1,0:T(8,128)(2,1)}, u32[]{:S(2)}, u32[]{:S(2)}) collective-permute-start(bf16[2,1408,512]{2,1,0:T(8,128)(2,1)} %shard_map.216), channel_id=1, source_target_pairs={{0,2},{1,3},{2,0},{3,1},{4,6},{5,7},{6,4},{7,5},{8,10},{9,11},{10,... | collective-permute-start | bytes 8650760 | tf_op jit(solution)/shard_map/ppermute | solution.py:242
  502.2 95.6 %collective-permute-start.22 = (bf16[2,512,2816]{2,1,0:T(8,128)(2,1)}, bf16[2,512,2816]{2,1,0:T(8,128)(2,1)}, u32[]{:S(2)}, u32[]{:S(2)}) collective-permute-start(bf16[2,512,2816]{2,1,0:T(8,128)(2,1)} %shard_map.221), channel_id=1, source_target_pairs={{0,1},{1,0},{2,3},{3,2},{4,5},{5,4},{6,7},{7,6},{8,9},{9,8},{10,11... | collective-permute-start | bytes 17301512 | tf_op jit(solution)/shard_map/ppermute | solution.py:242
  502.2 95.6 %collective-permute-start.20 = (bf16[1,512,2816]{2,1,0:T(8,128)(2,1)}, bf16[1,512,2816]{2,1,0:T(8,128)(2,1)S(1)}, u32[]{:S(2)}, u32[]{:S(2)}) collective-permute-start(bf16[1,512,2816]{2,1,0:T(8,128)(2,1)} %shard_map.218), channel_id=1, source_target_pairs={{0,2},{1,3},{2,0},{3,1},{4,6},{5,7},{6,4},{7,5},{8,10},{9,11},{10,... | collective-permute-start | bytes 8650760 | tf_op jit(solution)/shard_map/ppermute | solution.py:242
  540.9 25.5 %collective-permute-start.21 = (bf16[2,1408,512]{2,1,0:T(8,128)(2,1)}, bf16[2,1408,512]{2,1,0:T(8,128)(2,1)}, u32[]{:S(2)}, u32[]{:S(2)}) collective-permute-start(bf16[2,1408,512]{2,1,0:T(8,128)(2,1)} %shard_map.220), channel_id=1, source_target_pairs={{0,1},{1,0},{2,3},{3,2},{4,5},{5,4},{6,7},{7,6},{8,9},{9,8},{10,11... | collective-permute-start | bytes 8650760 | tf_op jit(solution)/shard_map/ppermute | solution.py:242
  604.9 215.8 %reduce-scatter.5.cloned.1.call-start = ((), (), s32[]{:S(2)}) async-start(), calls=%async_computation.17 | async-start | bytes 4718592 | tf_op jit(solution)/shard_map/reduce_scatter | solution.py:296
  605.0 69.7 %collective-permute-start.26 = (bf16[1,512,2816]{2,1,0:T(8,128)(2,1)}, bf16[1,512,2816]{2,1,0:T(8,128)(2,1)}, u32[]{:S(2)}, u32[]{:S(2)}) collective-permute-start(bf16[1,512,2816]{2,1,0:T(8,128)(2,1)} %copy-done.15), channel_id=1, source_target_pairs={{0,2},{1,3},{2,0},{3,1},{4,6},{5,7},{6,4},{7,5},{8,10},{9,11},{10,... | collective-permute-start | bytes 8650760 | tf_op jit(solution)/shard_map/ppermute | solution.py:242
  685.0 52.4 %all-to-all-start.5 = ((bf16[8,128,576]{1,2,0:T(8,128)(2,1)}), bf16[8,128,576]{1,2,0:T(8,128)(2,1)}, u32[]{:S(2)}, u32[]{:S(2)}) async-start(bf16[8,128,576]{1,2,0:T(8,128)(2,1)} %pad_maximum_fusion.11), calls=%async_computation.7 | async-start | bytes 2359296 | tf_op jit(solution)/shard_map/all_to_all | solution.py:300
  689.7 32.7 %collective-permute-start.30 = (bf16[8,64,1152]{2,1,0:T(8,128)(2,1)}, bf16[8,64,1152]{2,1,0:T(8,128)(2,1)}, u32[]{:S(2)}, u32[]{:S(2)}) collective-permute-start(bf16[8,64,1152]{2,1,0:T(8,128)(2,1)} %get-tuple-element.109), channel_id=1, source_target_pairs={{0,2},{1,3},{2,0},{3,1},{4,6},{5,7},{6,4},{7,5},{8,10},{9,11},{10,... | collective-permute-start | bytes 3538952 | tf_op jit(solution)/shard_map/ppermute | solution.py:242
  695.4 10.7 %collective-permute-start.28 = (bf16[512,640]{1,0:T(8,128)(2,1)S(1)}, bf16[512,640]{1,0:T(8,128)(2,1)S(1)}, u32[]{:S(2)}, u32[]{:S(2)}) collective-permute-start(bf16[512,640]{1,0:T(8,128)(2,1)S(1)} %shard_map.225), channel_id=1, source_target_pairs={{0,1},{1,0},{2,3},{3,2},{4,5},{5,4},{6,7},{7,6},{8,9},{9,8},{10,11... | collective-permute-start | bytes 1966088 | tf_op jit(solution)/shard_map/ppermute | solution.py:242
  700.5 8.9 %collective-permute-start.31 = (bf16[512,128]{1,0:T(8,128)(2,1)}, bf16[512,128]{1,0:T(8,128)(2,1)S(1)}, u32[]{:S(2)}, u32[]{:S(2)}) collective-permute-start(bf16[512,128]{1,0:T(8,128)(2,1)} %bitcast.72), channel_id=1, source_target_pairs={{0,1},{1,0},{2,3},{3,2},{4,5},{5,4},{6,7},{7,6},{8,9},{9,8},{10,11... | collective-permute-start | bytes 393224 | tf_op jit(solution)/shard_map/ppermute | solution.py:242
  700.8 20.9 %collective-permute-start.33 = (bf16[512,128]{1,0:T(8,128)(2,1)S(1)}, bf16[512,128]{1,0:T(8,128)(2,1)S(1)}, u32[]{:S(2)}, u32[]{:S(2)}) collective-permute-start(bf16[512,128]{1,0:T(8,128)(2,1)S(1)} %add_convert_fusion.2), channel_id=1, source_target_pairs={{0,2},{1,3},{2,0},{3,1},{4,6},{5,7},{6,4},{7,5},{8,10},{9,11},{10,... | collective-permute-start | bytes 393224 | tf_op jit(solution)/shard_map/ppermute | solution.py:242
  705.9 19.2 %collective-permute-start.27 = (bf16[512,640]{1,0:T(8,128)(2,1)S(1)}, bf16[512,640]{1,0:T(8,128)(2,1)S(1)}, u32[]{:S(2)}, u32[]{:S(2)}) collective-permute-start(bf16[512,640]{1,0:T(8,128)(2,1)S(1)} %shard_map.224), channel_id=1, source_target_pairs={{0,1},{1,0},{2,3},{3,2},{4,5},{5,4},{6,7},{7,6},{8,9},{9,8},{10,11... | collective-permute-start | bytes 1966088 | tf_op jit(solution)/shard_map/ppermute | solution.py:242
  708.7 25.1 %collective-permute-start.29 = (bf16[512,640]{1,0:T(8,128)(2,1)S(1)}, bf16[512,640]{1,0:T(8,128)(2,1)S(1)}, u32[]{:S(2)}, u32[]{:S(2)}) collective-permute-start(bf16[512,640]{1,0:T(8,128)(2,1)S(1)} %shard_map.226), channel_id=1, source_target_pairs={{0,2},{1,3},{2,0},{3,1},{4,6},{5,7},{6,4},{7,5},{8,10},{9,11},{10,... | collective-permute-start | bytes 1966088 | tf_op jit(solution)/shard_map/ppermute | solution.py:242
  743.5 6.4 collective-permute-start.35
  743.5 26.0 %all-to-all-start.8 = ((bf16[8,64,640]{2,1,0:T(8,128)(2,1)}), bf16[8,64,640]{2,1,0:T(8,128)(2,1)}, u32[]{:S(2)}, u32[]{:S(2)}) async-start(bf16[8,64,640]{2,1,0:T(8,128)(2,1)} %bitcast.87), calls=%async_computation.10 | async-start | bytes 1310720 | tf_op jit(solution)/shard_map/all_to_all | solution.py:300
  749.6 6.8 collective-permute-start.34
  750.2 17.0 %collective-permute-start.36 = (bf16[1,512,640]{2,1,0:T(8,128)(2,1)S(1)}, bf16[1,512,640]{2,1,0:T(8,128)(2,1)S(1)}, u32[]{:S(2)}, u32[]{:S(2)}) collective-permute-start(bf16[1,512,640]{2,1,0:T(8,128)(2,1)S(1)} %shard_map.230), channel_id=1, source_target_pairs={{0,2},{1,3},{2,0},{3,1},{4,6},{5,7},{6,4},{7,5},{8,10},{9,11},{10,... | collective-permute-start | bytes 1966088 | tf_op jit(solution)/shard_map/ppermute | solution.py:242
  769.6 34.8 %all-to-all-start.6 = ((bf16[8,64,640]{2,1,0:T(8,128)(2,1)}), bf16[8,64,640]{2,1,0:T(8,128)(2,1)S(1)}, u32[]{:S(2)}, u32[]{:S(2)}) async-start(bf16[8,64,640]{2,1,0:T(8,128)(2,1)} %bitcast.86), calls=%async_computation.8 | async-start | bytes 1310720 | tf_op jit(solution)/shard_map/all_to_all | solution.py:300
  805.2 10.0 %all-to-all-start.7 = ((f32[8,1,144]{2,1,0:T(1,128)}), f32[8,1,144]{2,1,0:T(1,128)S(1)}, u32[]{:S(2)}, u32[]{:S(2)}) async-start(f32[8,1,144]{2,1,0:T(1,128)} %all_to_all.40), calls=%async_computation.9 | async-start | bytes 16384 | tf_op jit(solution)/shard_map/all_to_all | solution.py:300
  815.2 31.3 %all-to-all-start.9 = ((bf16[8,64,1152]{2,1,0:T(8,128)(2,1)}), bf16[8,64,1152]{2,1,0:T(8,128)(2,1)S(1)}, u32[]{:S(2)}, u32[]{:S(2)}) async-start(bf16[8,64,1152]{2,1,0:T(8,128)(2,1)} %add_convert_fusion), calls=%async_computation.11 | async-start | bytes 2359296 | tf_op jit(solution)/shard_map/all_to_all | solution.py:300
  (96 other events, 1298.9 us)
Sparse Core Ops, SparseCore 0:
  10.7 93.7 all-gather.5
  107.4 105.2 all-gather.7
  215.5 71.8 all-gather.9
  289.9 71.6 all-gather.11
  445.9 147.2 reduce-scatter.2
  605.0 82.8 all-gather.13
  692.5 118.0 reduce-scatter.4

commit v12 on v11

--- a/solution.py
+++ b/solution.py
@@ -705,9 +705,8 @@
     order = rank ^ 2
     steps = 4
     step_rows = D // 4 // steps
-    gu_far = [
-        fsdp_swap(expert_gate_up[:, i * step_rows : (i + 1) * step_rows], 2) for i in range(steps)
-    ]
+    gu_send = [expert_gate_up[:, i * step_rows : (i + 1) * step_rows] for i in range(steps)]
+    gu_far = [fsdp_swap(v, 2) for v in gu_send[:2]]
     sff_dev = SFF // n_ctx
     sff_pad = -(-sff_dev // 128) * 128
     attn = attention_split if H % n_ctx == 0 else attention_whole
@@ -721,6 +720,7 @@
     down_send = pad_last(rows_by_dest(shared_down, n_ctx), sff_pad)
     shared_send = jnp.concatenate([gate_send, up_send, down_send], -1)
     shared_got = ctx_exchange(after(shared_send, first_done))
+    gu_far += [fsdp_swap(after(v, shared_got), 2) for v in gu_send[2:]]
     shared_far = fsdp_swap(shared_got, 2)
     dn_far = fsdp_swap(after(expert_down, shared_far), 2)
 
@@ -1017,11 +1017,11 @@
         token_cols = columns_by_distance(tokens, n_ctx, rank)
         gain_in_grad = gain_in_grad + jnp.sum(in_own * (token_cols * inv_in), 0)
         gain_in_grad = columns_in_order(gain_in_grad[None], n_ctx, rank)[0]
-        gains_there, gains_grad = reduce_gains(gain_in_grad, gain_lat_grad, latent_own, latent_got)
         nope_w = query_terms[:, :, :n_wide].reshape(n_ctx, rows, heads, DN)
         rot_w = query_terms[:, :, n_wide:].reshape(n_ctx, rows, heads, DR)
         query_w = jnp.concatenate([nope_w, rot_w], -1).transpose(1, 0, 2, 3).reshape(rows, -1)
         shared_sums = ctx_exchange(after(shared_terms, latent_got))
+        gains_there, gains_grad = reduce_gains(gain_in_grad, gain_lat_grad, latent_own, shared_sums)
         in_grad = after(in_grad, gains_there).astype(jnp.float32) + in_own
         token_grad = norm_backward(token_cols, inv_in, saved["gain_cols"], in_grad)[0]
         token_grad = columns_in_order(token_grad, n_ctx, rank)

time: 865 us -> 907 us (1.049)
  waiting for transfers between devices: 322 us -> 358 us
    all_to_all x9, waiting for transfers between devices: 31.4 us -> 67.6 us  [ctx_exchange(): lax.all_to_all(values, 'ctx', split_axis=0, concat_axis=0, tiled=True)]
    all_gather x4, waiting for transfers between devices: 34.7 us -> 8.86 us  [ctx_gather(): return lax.all_gather(values, 'ctx', axis=0, tiled=True)]
    ppermute x40, waiting for transfers between devices: 256 us -> 281 us  [fsdp_swap(): lax.ppermute(values, 'fsdp', [(at, at ^ distance) for at in range(count)])]
    unnamed x199 -> x203, local copies, waits for them, and re-layouts: 35.6 us -> 36.8 us
  transfers between devices with their start and end apart: 56 -> 56, of which waited for: 27 -> 24; matrix products, arithmetic and copies ran while one was open for 24% -> 24% of each run, Pallas kernels for 13% -> 12%
where the time goes in v12:
time: 907 us; the launch traced here: 898 us
  waiting for transfers between devices  358 us (39%)
  Pallas kernels  178 us (20%)
  local copies, waits for them, and re-layouts  107 us (12%)
  other arithmetic  82.4 us (9%)
  starting transfers between devices  61.9 us (7%)
  matrix products  60.8 us (7%)
  blocking collectives  33.7 us (4%)
  between operations  16.2 us (2%)
    ppermute x40, waiting for transfers between devices, fsdp_swap(): lax.ppermute(values, 'fsdp', [(at, at ^ distance) for at in range(count)])  281 us
    all_to_all x9, waiting for transfers between devices, ctx_exchange(): lax.all_to_all(values, 'ctx', split_axis=0, concat_axis=0, tiled=True)  67.6 us
    dot_general x12, matrix products, dot_f32(): lax.dot_general(left, right, (dims, ((), ())), preferred_element_type=jnp...  60.8 us
    pallas_call x13, Pallas kernels, expert_grad_call(): pl.pallas_call(functools.partial(expert_grad_body, each=len(each)), grid=...  58.6 us
    pallas_call x1, Pallas kernels, experts_call(): pl.pallas_call(experts_body, grid=(count,), in_specs=[pl.BlockSpec((1, sl...  48.7 us
    all_to_all x9, starting transfers between devices, ctx_exchange(): lax.all_to_all(values, 'ctx', split_axis=0, concat_axis=0, tiled=True)  40.7 us
    unnamed x203, local copies, waits for them, and re-layouts  36.8 us
    all_to_all x1, blocking collectives, ctx_exchange(): lax.all_to_all(values, 'ctx', split_axis=0, concat_axis=0, tiled=True)  33.7 us
  transfers between devices with their start and end apart: 56, of which 24 were waited for; matrix products, arithmetic and copies ran while one was open for 24% of the time, Pallas kernels for 12%

profile of v12, /device:TPU:0, one launch (start us, length us, event | category | flops | bytes accessed | tf_op | source)
XLA Modules:
  0.0 898.2 jit_solution(9344088722494121610)
XLA Ops:
  12.8 7.3 all-to-all-start
  20.1 5.2 fusion.117
  26.8 31.7 %collective-permute-done = bf16[2,128,2816]{2,1,0:T(8,128)(2,1)} collective-permute-done((bf16[2,128,2816]{2,1,0:T(8,128)(2,1)S(1)}, bf16[2,128,2816]{2,1,0:T(8,128)(2,1)}, u32[]{:S(2)}, u32[]{:S(2)}) %collective-permute-start) | collective-permute-done | bytes 1441824 | tf_op jit(solution)/shard_map/ppermute | solution.py:242
  58.5 4.2 all-to-all-done
  64.5 24.4 %collective-permute-done.2 = bf16[8,64,1088]{2,1,0:T(8,128)(2,1)S(1)} collective-permute-done((bf16[8,64,1088]{2,1,0:T(8,128)(2,1)S(1)}, bf16[8,64,1088]{2,1,0:T(8,128)(2,1)S(1)}, u32[]{:S(2)}, u32[]{:S(2)}) %collective-permute-start.2) | collective-permute-done | bytes 1114144 | tf_op jit(solution)/shard_map/ppermute | solution.py:242
  95.7 8.9 all-gather.6.cloned.1.call-done
  114.4 4.3 all-to-all-start.2
  123.8 4.9 fusion.29
  128.9 6.2 fusion.25
  141.2 13.8 %shard_map.212 = (bf16[1024,256]{1,0:T(8,128)(2,1)S(1)}, f32[2,1024,512]{2,1,0:T(8,128)}, f32[2,1024,1]{2,1,0:T(8,128)S(1)}) custom-call(bf16[1024,256]{1,0:T(8,128)(2,1)S(1)} %slice.307.nope_ref, bf16[2,1024,64]{2,1,0:T(8,128)(2,1)S(1)} %pad_maximum_fusion.17.rot_ref, bf16[1024,512]{1,0:T(8,128)(2,1)} %multiply_convert_fusion.1.lat_ref, ...), custom_call_target="tpu_custom_call" | custom-call | tf_op jit(solution)/shard_map/pallas_call | solution.py:406
  157.0 5.7 all-to-all-done.2
  169.9 25.2 %all-to-all-done.1 = bf16[8,128,256]{1,2,0:T(8,128)(2,1)S(1)} async-done(((bf16[8,128,256]{1,2,0:T(8,128)(2,1)}), bf16[8,128,256]{1,2,0:T(8,128)(2,1)S(1)}, u32[]{:S(2)}, u32[]{:S(2)}) %all-to-all-start.1) | async-done | bytes 524320 | tf_op jit(solution)/shard_map/all_to_all | solution.py:300
  214.7 4.8 convert_bitcast_fusion
  219.5 71.4 %collective-permute-done.5 = bf16[8,64,1152]{2,1,0:T(8,128)(2,1)} collective-permute-done((bf16[8,64,1152]{2,1,0:T(8,128)(2,1)}, bf16[8,64,1152]{2,1,0:T(8,128)(2,1)}, u32[]{:S(2)}, u32[]{:S(2)}) %collective-permute-start.5) | collective-permute-done | bytes 1179680 | tf_op jit(solution)/shard_map/ppermute | solution.py:242
  296.4 6.4 multiply_reduce_fusion.5
  304.9 7.9 multiply_convert_fusion
  312.8 43.3 %collective-permute-done.15 = bf16[2,1408,512]{2,1,0:T(8,128)(2,1)} collective-permute-done((bf16[2,1408,512]{2,1,0:T(8,128)(2,1)}, bf16[2,1408,512]{2,1,0:T(8,128)(2,1)}, u32[]{:S(2)}, u32[]{:S(2)}) %collective-permute-start.15) | collective-permute-done | bytes 2883616 | tf_op jit(solution)/shard_map/ppermute | solution.py:242
  361.9 7.0 pad_maximum_fusion.5.gate_up_ref
  376.9 5.5 constant_dynamic-update-slice_fusion.gu_ref
  382.4 9.0 %pad_maximum_fusion.dn_ref = bf16[2,1408,2048]{2,1,0:T(8,128)(2,1)} fusion(bf16[2,1408,512]{2,1,0:T(8,128)(2,1)} %collective-permute-done.17, bf16[2,1408,512]{2,1,0:T(8,128)(2,1)} %param.23, bf16[2,1408,512]{2,1,0:T(8,128)(2,1)S(1)} %collective-permute-done.16, bf16[2,1408,512]{2,1,0:T(8,128)(2,1)} %collective-permute-done.15), kind=kLoop, calls=%fused_computation.8 | loop fusion | flops 46137344 | bytes 23068672 | tf_op jit(solution)/shard_map/concatenate | solution.py:745
  391.4 6.3 fusion.124
  402.6 5.9 convolution_convert_fusion.1
  408.4 48.7 %shard_map.213 = (bf16[2,432,1408]{2,1,0:T(8,128)(2,1)}, bf16[2,432,2816]{2,1,0:T(8,128)(2,1)}, bf16[2,432,2048]{2,1,0:T(8,128)(2,1)}, bf16[2,432,2048]{2,1,0:T(8,128)(2,1)}) custom-call(bf16[2,432,2048]{2,1,0:T(8,128)(2,1)} %bitcast.208, bf16[2,432,2048]{2,1,0:T(8,128)(2,1)} %bitcast.220, f32[2,432,1]{2,1,0:T(8,128)} %copy.472.gate_ref, ...), custom_call_target="tpu_custom_call" | custom-call | tf_op jit(solution)/shard_map/pallas_call | solution.py:518
  457.2 19.0 %shard_map.214 = bf16[1024,4096]{1,0:T(8,128)(2,1)} custom-call(bf16[1024,864]{1,0:T(8,128)(2,1)} %get-tuple-element.231.pick_ref, bf16[1024,768]{1,0:T(8,128)(2,1)S(1)} %pad_maximum_fusion.9.both_ref, bf16[1024,384]{1,0:T(8,128)(2,1)S(1)} %get-tuple-element.257.act_ref, bf16[864,2048]{1,0:T(8,128)(2,1)} %bitcast.239, bf16[864,2048]{1,0:T(8,128)(2,1)} %bitcast.238, ...), custom_call_target="tpu_custom_call" | custom-call | tf_op jit(solution)/shard_map/pallas_call | solution.py:652
  477.9 4.3 shard_map.215
  482.6 5.1 collective-permute-done.18.refs_2_
  489.3 4.6 shard_map.216
  493.9 7.4 shard_map.217
  502.0 9.0 collective-permute-done.19
  513.9 4.2 shard_map.219
  519.7 5.2 shard_map.218
  524.9 7.5 shard_map.221
  533.1 34.2 %collective-permute-done.23.refs_3_ = bf16[2,1408,512]{2,1,0:T(8,128)(2,1)} collective-permute-done((bf16[2,1408,512]{2,1,0:T(8,128)(2,1)}, bf16[2,1408,512]{2,1,0:T(8,128)(2,1)}, u32[]{:S(2)}, u32[]{:S(2)}) %collective-permute-start.23) | collective-permute-done | bytes 2883616 | tf_op jit(solution)/shard_map/ppermute | solution.py:242
  581.4 6.7 copy.473
  596.9 5.8 shard_map.222
  602.6 25.6 %collective-permute-done.20.refs_3_ = bf16[1,512,2816]{2,1,0:T(8,128)(2,1)S(1)} collective-permute-done((bf16[1,512,2816]{2,1,0:T(8,128)(2,1)}, bf16[1,512,2816]{2,1,0:T(8,128)(2,1)S(1)}, u32[]{:S(2)}, u32[]{:S(2)}) %collective-permute-start.20) | collective-permute-done | bytes 2883616 | tf_op jit(solution)/shard_map/ppermute | solution.py:242
  635.8 4.9 convolution_convert_fusion.2
  640.7 33.7 %all_to_all.54 = bf16[8,128,256]{2,1,0:T(8,128)(2,1)S(1)} all-to-all(bf16[8,128,256]{2,1,0:T(8,128)(2,1)S(1)} %bitcast.245), channel_id=1, replica_groups=mesh['ctx'=8,'fsdp'=4] {'ctx'}, dimensions={0} | all-to-all | bytes 1048576 | tf_op jit(solution)/shard_map/all_to_all | solution.py:300
  674.5 24.9 %shard_map.223 = (bf16[1024,256]{1,0:T(8,128)(2,1)S(1)}, f32[2,1024,64]{2,1,0:T(8,128)}, f32[2,512,256]{2,1,0:T(8,128)}, f32[1024,512]{1,0:T(8,128)}, f32[1024,64]{1,0:T(8,128)S(1)}) custom-call(bf16[1024,256]{1,0:T(8,128)(2,1)S(1)} %bitcast.219, bf16[1024,256]{1,0:T(8,128)(2,1)S(1)} %copy-done.10, bf16[2,1024,64]{2,1,0:T(8,128)(2,1)S(1)} %copy-done.12, ...), custom_call_target="tpu_custom_call" | custom-call | tf_op jit(solution)/shard_map/pallas_call | solution.py:441
  706.9 6.6 fusion.3
  717.2 4.8 all-to-all-start.5
  742.6 11.4 %collective-permute-done.33 = bf16[512,128]{1,0:T(8,128)(2,1)S(1)} collective-permute-done((bf16[512,128]{1,0:T(8,128)(2,1)S(1)}, bf16[512,128]{1,0:T(8,128)(2,1)S(1)}, u32[]{:S(2)}, u32[]{:S(2)}) %collective-permute-start.33) | collective-permute-done | bytes 131104 | tf_op jit(solution)/shard_map/ppermute | solution.py:242
  757.4 7.9 collective-permute-done.29.refs_5_
  789.7 9.5 %collective-permute-done.36.refs_3_ = bf16[1,512,640]{2,1,0:T(8,128)(2,1)S(1)} collective-permute-done((bf16[1,512,640]{2,1,0:T(8,128)(2,1)S(1)}, bf16[1,512,640]{2,1,0:T(8,128)(2,1)S(1)}, u32[]{:S(2)}, u32[]{:S(2)}) %collective-permute-start.36) | collective-permute-done | bytes 655392 | tf_op jit(solution)/shard_map/ppermute | solution.py:242
  801.5 5.9 all-to-all-start.6
  819.3 17.1 %all-to-all-done.6 = bf16[8,64,640]{2,1,0:T(8,128)(2,1)S(1)} async-done(((bf16[8,64,640]{2,1,0:T(8,128)(2,1)}), bf16[8,64,640]{2,1,0:T(8,128)(2,1)S(1)}, u32[]{:S(2)}, u32[]{:S(2)}) %all-to-all-start.6) | async-done | bytes 655392 | tf_op jit(solution)/shard_map/all_to_all | solution.py:300
  856.4 11.6 %all-to-all-done.7.got_ref = bf16[8,64,1152]{2,1,0:T(8,128)(2,1)S(1)} async-done(((bf16[8,64,1152]{2,1,0:T(8,128)(2,1)}), bf16[8,64,1152]{2,1,0:T(8,128)(2,1)S(1)}, u32[]{:S(2)}, u32[]{:S(2)}) %all-to-all-start.7) | async-done | bytes 1179680 | tf_op jit(solution)/shard_map/all_to_all | solution.py:300
  875.9 11.8 %shard_map.233 = f32[2,512,2816]{2,1,0:T(8,128)} custom-call(bf16[2,432,2048]{2,1,0:T(8,128)(2,1)} %bitcast.211, bf16[2,432,2816]{2,1,0:T(8,128)(2,1)} %get-tuple-element.97.refs_1_, bf16[2,512,2816]{2,1,0:T(8,128)(2,1)} %collective-permute-done.22.refs_2_, bf16[1,512,2816]{2,1,0:T(8,128)(2,1)S(1)} %copy-done.14, ...), custom_call_target="tpu_custom_call" | custom-call | tf_op jit(solution)/shard_map/pallas_call | solution.py:555
  (494 shorter events, 235.2 us)
Async XLA Ops:
  7.2 97.4 %all-gather.6.cloned.1.call-start = ((), (), s32[]{:S(2)}) async-start(), calls=%async_computation.12 | async-start | bytes 4718592 | tf_op jit(solution)/shard_map/all_gather | solution.py:292
  12.8 49.9 %all-to-all-start = ((bf16[8,64,960]{2,1,0:T(8,128)(2,1)}), bf16[8,64,960]{2,1,0:T(8,128)(2,1)S(1)}, u32[]{:S(2)}, u32[]{:S(2)}) async-start(bf16[8,64,960]{2,1,0:T(8,128)(2,1)} %pad_maximum_fusion.12), calls=%async_computation | async-start | bytes 2097152 | tf_op jit(solution)/shard_map/all_to_all | solution.py:300
  20.1 276.3 %all-gather.8.cloned.1.call-start = ((), (), s32[]{:S(2)}) async-start(), calls=%async_computation.13 | async-start | bytes 8650752 | tf_op jit(solution)/shard_map/all_gather | solution.py:919
  25.4 33.1 %collective-permute-start = (bf16[2,128,2816]{2,1,0:T(8,128)(2,1)S(1)}, bf16[2,128,2816]{2,1,0:T(8,128)(2,1)}, u32[]{:S(2)}, u32[]{:S(2)}) collective-permute-start(bf16[2,128,2816]{2,1,0:T(8,128)(2,1)S(1)} %get-tuple-element.238), channel_id=1, source_target_pairs={{0,2},{1,3},{2,0},{3,1},{4,6},{5,7},{6,4},{7,5},{8,10},{9,11},{10,... | collective-permute-start | bytes 4325384 | tf_op jit(solution)/shard_map/ppermute | solution.py:242
  62.9 26.0 %collective-permute-start.2 = (bf16[8,64,1088]{2,1,0:T(8,128)(2,1)S(1)}, bf16[8,64,1088]{2,1,0:T(8,128)(2,1)S(1)}, u32[]{:S(2)}, u32[]{:S(2)}) collective-permute-start(bf16[8,64,1088]{2,1,0:T(8,128)(2,1)S(1)} %pad_maximum_fusion.10), channel_id=1, source_target_pairs={{0,2},{1,3},{2,0},{3,1},{4,6},{5,7},{6,4},{7,5},{8,10},{9,11},{10,... | collective-permute-start | bytes 3342344 | tf_op jit(solution)/shard_map/ppermute | solution.py:242
  64.5 24.4 %collective-permute-start.1 = (bf16[8,64,1088]{2,1,0:T(8,128)(2,1)S(1)}, bf16[8,64,1088]{2,1,0:T(8,128)(2,1)S(1)}, u32[]{:S(2)}, u32[]{:S(2)}) collective-permute-start(bf16[8,64,1088]{2,1,0:T(8,128)(2,1)S(1)} %pad_maximum_fusion.10), channel_id=1, source_target_pairs={{0,1},{1,0},{2,3},{3,2},{4,5},{5,4},{6,7},{7,6},{8,9},{9,8},{10,11... | collective-permute-start | bytes 3342344 | tf_op jit(solution)/shard_map/ppermute | solution.py:242
  104.6 272.3 %collective-permute-start.14 = (bf16[2,512,2816]{2,1,0:T(8,128)(2,1)}, bf16[2,512,2816]{2,1,0:T(8,128)(2,1)}, u32[]{:S(2)}, u32[]{:S(2)}) collective-permute-start(bf16[2,512,2816]{2,1,0:T(8,128)(2,1)} %param.22), channel_id=1, source_target_pairs={{0,1},{1,0},{2,3},{3,2},{4,5},{5,4},{6,7},{7,6},{8,9},{9,8},{10,11... | collective-permute-start | bytes 17301512 | tf_op jit(solution)/shard_map/ppermute | solution.py:242
  104.6 94.0 %collective-permute-start.8 = (bf16[2,128,2816]{2,1,0:T(8,128)(2,1)}, bf16[2,128,2816]{2,1,0:T(8,128)(2,1)}, u32[]{:S(2)}, u32[]{:S(2)}) collective-permute-start(bf16[2,128,2816]{2,1,0:T(8,128)(2,1)} %get-tuple-element.236), channel_id=1, source_target_pairs={{0,2},{1,3},{2,0},{3,1},{4,6},{5,7},{6,4},{7,5},{8,10},{9,11},{10,... | collective-permute-start | bytes 4325384 | tf_op jit(solution)/shard_map/ppermute | solution.py:242
  106.2 276.2 %collective-permute-start.17 = (bf16[2,1408,512]{2,1,0:T(8,128)(2,1)}, bf16[2,1408,512]{2,1,0:T(8,128)(2,1)}, u32[]{:S(2)}, u32[]{:S(2)}) collective-permute-start(bf16[2,1408,512]{2,1,0:T(8,128)(2,1)} %param.23), channel_id=1, source_target_pairs={{0,1},{1,0},{2,3},{3,2},{4,5},{5,4},{6,7},{7,6},{8,9},{9,8},{10,11... | collective-permute-start | bytes 8650760 | tf_op jit(solution)/shard_map/ppermute | solution.py:242
  114.4 48.3 %all-to-all-start.2 = ((bf16[8,64,1152]{2,1,0:T(8,128)(2,1)}), bf16[8,64,1152]{2,1,0:T(8,128)(2,1)}, u32[]{:S(2)}, u32[]{:S(2)}) async-start(bf16[8,64,1152]{2,1,0:T(8,128)(2,1)} %fusion.32), calls=%async_computation.2 | async-start | bytes 2359296 | tf_op jit(solution)/shard_map/all_to_all | solution.py:300
  118.7 186.1 %all-gather.10.cloned.1.call-start = ((), (), s32[]{:S(2)}) async-start(), calls=%async_computation.14 | async-start | bytes 4718592 | tf_op jit(solution)/shard_map/all_gather | solution.py:292
  162.7 32.3 %all-to-all-start.1 = ((bf16[8,128,256]{1,2,0:T(8,128)(2,1)}), bf16[8,128,256]{1,2,0:T(8,128)(2,1)S(1)}, u32[]{:S(2)}, u32[]{:S(2)}) async-start(bf16[8,128,256]{1,2,0:T(8,128)(2,1)} %copy.456), calls=%async_computation.1 | async-start | bytes 1048576 | tf_op jit(solution)/shard_map/all_to_all | solution.py:300
  195.1 10.1 %all-to-all-start.3 = ((bf16[8,128,24]{1,2,0:T(8,128)(2,1)}), bf16[8,128,24]{1,2,0:T(8,128)(2,1)S(1)}, u32[]{:S(2)}, u32[]{:S(2)}) async-start(bf16[8,128,24]{1,2,0:T(8,128)(2,1)} %broadcast_in_dim.45), calls=%async_computation.3 | async-start | bytes 98304 | tf_op jit(solution)/shard_map/all_to_all | solution.py:300
  198.4 193.0 %all-gather.12.cloned.1.call-start = ((), (), s32[]{:S(2)}) async-start(), calls=%async_computation.15 | async-start | bytes 4718592 | tf_op jit(solution)/shard_map/all_gather | solution.py:292
  201.2 89.7 %collective-permute-start.7 = (bf16[2,128,2816]{2,1,0:T(8,128)(2,1)}, bf16[2,128,2816]{2,1,0:T(8,128)(2,1)}, u32[]{:S(2)}, u32[]{:S(2)}) collective-permute-start(bf16[2,128,2816]{2,1,0:T(8,128)(2,1)} %get-tuple-element.81), channel_id=1, source_target_pairs={{0,2},{1,3},{2,0},{3,1},{4,6},{5,7},{6,4},{7,5},{8,10},{9,11},{10,... | collective-permute-start | bytes 4325384 | tf_op jit(solution)/shard_map/ppermute | solution.py:242
  201.2 92.5 %collective-permute-start.9 = (bf16[2,128,2816]{2,1,0:T(8,128)(2,1)}, bf16[2,128,2816]{2,1,0:T(8,128)(2,1)}, u32[]{:S(2)}, u32[]{:S(2)}) collective-permute-start(bf16[2,128,2816]{2,1,0:T(8,128)(2,1)} %get-tuple-element.83), channel_id=1, source_target_pairs={{0,2},{1,3},{2,0},{3,1},{4,6},{5,7},{6,4},{7,5},{8,10},{9,11},{10,... | collective-permute-start | bytes 4325384 | tf_op jit(solution)/shard_map/ppermute | solution.py:242
  203.3 87.6 %collective-permute-start.5 = (bf16[8,64,1152]{2,1,0:T(8,128)(2,1)}, bf16[8,64,1152]{2,1,0:T(8,128)(2,1)}, u32[]{:S(2)}, u32[]{:S(2)}) collective-permute-start(bf16[8,64,1152]{2,1,0:T(8,128)(2,1)} %all-to-all-done.2), channel_id=1, source_target_pairs={{0,2},{1,3},{2,0},{3,1},{4,6},{5,7},{6,4},{7,5},{8,10},{9,11},{10,... | collective-permute-start | bytes 3538952 | tf_op jit(solution)/shard_map/ppermute | solution.py:242
  290.9 65.2 %collective-permute-start.4 = (bf16[8,64,1152]{2,1,0:T(8,128)(2,1)}, bf16[8,64,1152]{2,1,0:T(8,128)(2,1)S(1)}, u32[]{:S(2)}, u32[]{:S(2)}) collective-permute-start(bf16[8,64,1152]{2,1,0:T(8,128)(2,1)} %all-to-all-done.2), channel_id=1, source_target_pairs={{0,1},{1,0},{2,3},{3,2},{4,5},{5,4},{6,7},{7,6},{8,9},{9,8},{10,11... | collective-permute-start | bytes 3538952 | tf_op jit(solution)/shard_map/ppermute | solution.py:242
  290.9 65.2 %collective-permute-start.15 = (bf16[2,1408,512]{2,1,0:T(8,128)(2,1)}, bf16[2,1408,512]{2,1,0:T(8,128)(2,1)}, u32[]{:S(2)}, u32[]{:S(2)}) collective-permute-start(bf16[2,1408,512]{2,1,0:T(8,128)(2,1)} %param.23), channel_id=1, source_target_pairs={{0,2},{1,3},{2,0},{3,1},{4,6},{5,7},{6,4},{7,5},{8,10},{9,11},{10,... | collective-permute-start | bytes 8650760 | tf_op jit(solution)/shard_map/ppermute | solution.py:242
  302.8 53.8 %collective-permute-start.6 = (bf16[8,64,1152]{2,1,0:T(8,128)(2,1)}, bf16[8,64,1152]{2,1,0:T(8,128)(2,1)S(1)}, u32[]{:S(2)}, u32[]{:S(2)}) collective-permute-start(bf16[8,64,1152]{2,1,0:T(8,128)(2,1)} %collective-permute-done.5), channel_id=1, source_target_pairs={{0,1},{1,0},{2,3},{3,2},{4,5},{5,4},{6,7},{7,6},{8,9},{9,8},{10,11... | collective-permute-start | bytes 3538952 | tf_op jit(solution)/shard_map/ppermute | solution.py:242
  304.8 323.4 %reduce-scatter.3.cloned.1.call-start = ((), (), s32[]{:S(2)}) async-start(), calls=%async_computation.16 | async-start | bytes 9437184 | tf_op jit(solution)/shard_map/reduce_scatter | solution.py:296
  356.6 14.8 %collective-permute-start.12 = (bf16[2,128,2816]{2,1,0:T(8,128)(2,1)}, bf16[2,128,2816]{2,1,0:T(8,128)(2,1)S(1)}, u32[]{:S(2)}, u32[]{:S(2)}) collective-permute-start(bf16[2,128,2816]{2,1,0:T(8,128)(2,1)} %collective-permute-done.7), channel_id=1, source_target_pairs={{0,1},{1,0},{2,3},{3,2},{4,5},{5,4},{6,7},{7,6},{8,9},{9,8},{10,11... | collective-permute-start | bytes 4325384 | tf_op jit(solution)/shard_map/ppermute | solution.py:242
  360.5 12.1 %collective-permute-start.13 = (bf16[2,128,2816]{2,1,0:T(8,128)(2,1)}, bf16[2,128,2816]{2,1,0:T(8,128)(2,1)S(1)}, u32[]{:S(2)}, u32[]{:S(2)}) collective-permute-start(bf16[2,128,2816]{2,1,0:T(8,128)(2,1)} %collective-permute-done.9), channel_id=1, source_target_pairs={{0,1},{1,0},{2,3},{3,2},{4,5},{5,4},{6,7},{7,6},{8,9},{9,8},{10,11... | collective-permute-start | bytes 4325384 | tf_op jit(solution)/shard_map/ppermute | solution.py:242
  361.6 20.8 %collective-permute-start.16 = (bf16[2,1408,512]{2,1,0:T(8,128)(2,1)}, bf16[2,1408,512]{2,1,0:T(8,128)(2,1)S(1)}, u32[]{:S(2)}, u32[]{:S(2)}) collective-permute-start(bf16[2,1408,512]{2,1,0:T(8,128)(2,1)} %collective-permute-done.15), channel_id=1, source_target_pairs={{0,1},{1,0},{2,3},{3,2},{4,5},{5,4},{6,7},{7,6},{8,9},{9,8},{10,11... | collective-permute-start | bytes 8650760 | tf_op jit(solution)/shard_map/ppermute | solution.py:242
  476.2 249.7 %all-gather.14.cloned.1.call-start = ((), (), s32[]{:S(2)}) async-start(), calls=%async_computation.18 | async-start | bytes 4718592 | tf_op jit(solution)/shard_map/all_gather | solution.py:292
  482.2 5.5 collective-permute-start.18
  501.4 9.6 %collective-permute-start.19 = (bf16[2,512,2816]{2,1,0:T(8,128)(2,1)}, bf16[2,512,2816]{2,1,0:T(8,128)(2,1)S(1)}, u32[]{:S(2)}, u32[]{:S(2)}) collective-permute-start(bf16[2,512,2816]{2,1,0:T(8,128)(2,1)} %shard_map.217), channel_id=1, source_target_pairs={{0,1},{1,0},{2,3},{3,2},{4,5},{5,4},{6,7},{7,6},{8,9},{9,8},{10,11... | collective-permute-start | bytes 17301512 | tf_op jit(solution)/shard_map/ppermute | solution.py:242
  501.7 65.6 %collective-permute-start.23 = (bf16[2,1408,512]{2,1,0:T(8,128)(2,1)}, bf16[2,1408,512]{2,1,0:T(8,128)(2,1)}, u32[]{:S(2)}, u32[]{:S(2)}) collective-permute-start(bf16[2,1408,512]{2,1,0:T(8,128)(2,1)} %shard_map.216), channel_id=1, source_target_pairs={{0,2},{1,3},{2,0},{3,1},{4,6},{5,7},{6,4},{7,5},{8,10},{9,11},{10,... | collective-permute-start | bytes 8650760 | tf_op jit(solution)/shard_map/ppermute | solution.py:242
  532.4 95.8 %collective-permute-start.22 = (bf16[2,512,2816]{2,1,0:T(8,128)(2,1)}, bf16[2,512,2816]{2,1,0:T(8,128)(2,1)}, u32[]{:S(2)}, u32[]{:S(2)}) collective-permute-start(bf16[2,512,2816]{2,1,0:T(8,128)(2,1)} %shard_map.221), channel_id=1, source_target_pairs={{0,1},{1,0},{2,3},{3,2},{4,5},{5,4},{6,7},{7,6},{8,9},{9,8},{10,11... | collective-permute-start | bytes 17301512 | tf_op jit(solution)/shard_map/ppermute | solution.py:242
  532.9 95.4 %collective-permute-start.20 = (bf16[1,512,2816]{2,1,0:T(8,128)(2,1)}, bf16[1,512,2816]{2,1,0:T(8,128)(2,1)S(1)}, u32[]{:S(2)}, u32[]{:S(2)}) collective-permute-start(bf16[1,512,2816]{2,1,0:T(8,128)(2,1)} %shard_map.218), channel_id=1, source_target_pairs={{0,2},{1,3},{2,0},{3,1},{4,6},{5,7},{6,4},{7,5},{8,10},{9,11},{10,... | collective-permute-start | bytes 8650760 | tf_op jit(solution)/shard_map/ppermute | solution.py:242
  571.6 25.3 %collective-permute-start.21 = (bf16[2,1408,512]{2,1,0:T(8,128)(2,1)}, bf16[2,1408,512]{2,1,0:T(8,128)(2,1)}, u32[]{:S(2)}, u32[]{:S(2)}) collective-permute-start(bf16[2,1408,512]{2,1,0:T(8,128)(2,1)} %shard_map.220), channel_id=1, source_target_pairs={{0,1},{1,0},{2,3},{3,2},{4,5},{5,4},{6,7},{7,6},{8,9},{9,8},{10,11... | collective-permute-start | bytes 8650760 | tf_op jit(solution)/shard_map/ppermute | solution.py:242
  635.4 212.7 %reduce-scatter.5.cloned.1.call-start = ((), (), s32[]{:S(2)}) async-start(), calls=%async_computation.17 | async-start | bytes 4718592 | tf_op jit(solution)/shard_map/reduce_scatter | solution.py:296
  635.4 71.5 %collective-permute-start.26 = (bf16[1,512,2816]{2,1,0:T(8,128)(2,1)}, bf16[1,512,2816]{2,1,0:T(8,128)(2,1)}, u32[]{:S(2)}, u32[]{:S(2)}) collective-permute-start(bf16[1,512,2816]{2,1,0:T(8,128)(2,1)} %copy-done.15), channel_id=1, source_target_pairs={{0,2},{1,3},{2,0},{3,1},{4,6},{5,7},{6,4},{7,5},{8,10},{9,11},{10,... | collective-permute-start | bytes 8650760 | tf_op jit(solution)/shard_map/ppermute | solution.py:242
  717.2 53.6 %all-to-all-start.5 = ((bf16[8,128,576]{1,2,0:T(8,128)(2,1)}), bf16[8,128,576]{1,2,0:T(8,128)(2,1)}, u32[]{:S(2)}, u32[]{:S(2)}) async-start(bf16[8,128,576]{1,2,0:T(8,128)(2,1)} %pad_maximum_fusion.11), calls=%async_computation.7 | async-start | bytes 2359296 | tf_op jit(solution)/shard_map/all_to_all | solution.py:300
  722.0 32.7 %collective-permute-start.30 = (bf16[8,64,1152]{2,1,0:T(8,128)(2,1)}, bf16[8,64,1152]{2,1,0:T(8,128)(2,1)}, u32[]{:S(2)}, u32[]{:S(2)}) collective-permute-start(bf16[8,64,1152]{2,1,0:T(8,128)(2,1)} %get-tuple-element.113), channel_id=1, source_target_pairs={{0,2},{1,3},{2,0},{3,1},{4,6},{5,7},{6,4},{7,5},{8,10},{9,11},{10,... | collective-permute-start | bytes 3538952 | tf_op jit(solution)/shard_map/ppermute | solution.py:242
  728.5 9.8 %collective-permute-start.28 = (bf16[512,640]{1,0:T(8,128)(2,1)S(1)}, bf16[512,640]{1,0:T(8,128)(2,1)S(1)}, u32[]{:S(2)}, u32[]{:S(2)}) collective-permute-start(bf16[512,640]{1,0:T(8,128)(2,1)S(1)} %shard_map.225), channel_id=1, source_target_pairs={{0,1},{1,0},{2,3},{3,2},{4,5},{5,4},{6,7},{7,6},{8,9},{9,8},{10,11... | collective-permute-start | bytes 1966088 | tf_op jit(solution)/shard_map/ppermute | solution.py:242
  733.7 8.9 collective-permute-start.31
  734.0 20.1 %collective-permute-start.33 = (bf16[512,128]{1,0:T(8,128)(2,1)S(1)}, bf16[512,128]{1,0:T(8,128)(2,1)S(1)}, u32[]{:S(2)}, u32[]{:S(2)}) collective-permute-start(bf16[512,128]{1,0:T(8,128)(2,1)S(1)} %add_convert_fusion.2), channel_id=1, source_target_pairs={{0,2},{1,3},{2,0},{3,1},{4,6},{5,7},{6,4},{7,5},{8,10},{9,11},{10,... | collective-permute-start | bytes 393224 | tf_op jit(solution)/shard_map/ppermute | solution.py:242
  738.2 19.2 %collective-permute-start.27 = (bf16[512,640]{1,0:T(8,128)(2,1)S(1)}, bf16[512,640]{1,0:T(8,128)(2,1)S(1)}, u32[]{:S(2)}, u32[]{:S(2)}) collective-permute-start(bf16[512,640]{1,0:T(8,128)(2,1)S(1)} %shard_map.224), channel_id=1, source_target_pairs={{0,1},{1,0},{2,3},{3,2},{4,5},{5,4},{6,7},{7,6},{8,9},{9,8},{10,11... | collective-permute-start | bytes 1966088 | tf_op jit(solution)/shard_map/ppermute | solution.py:242
  741.0 24.3 %collective-permute-start.29 = (bf16[512,640]{1,0:T(8,128)(2,1)S(1)}, bf16[512,640]{1,0:T(8,128)(2,1)S(1)}, u32[]{:S(2)}, u32[]{:S(2)}) collective-permute-start(bf16[512,640]{1,0:T(8,128)(2,1)S(1)} %shard_map.226), channel_id=1, source_target_pairs={{0,2},{1,3},{2,0},{3,1},{4,6},{5,7},{6,4},{7,5},{8,10},{9,11},{10,... | collective-permute-start | bytes 1966088 | tf_op jit(solution)/shard_map/ppermute | solution.py:242
  777.0 24.6 %all-to-all-start.9 = ((bf16[8,64,640]{2,1,0:T(8,128)(2,1)}), bf16[8,64,640]{2,1,0:T(8,128)(2,1)}, u32[]{:S(2)}, u32[]{:S(2)}) async-start(bf16[8,64,640]{2,1,0:T(8,128)(2,1)} %bitcast.87), calls=%async_computation.11 | async-start | bytes 1310720 | tf_op jit(solution)/shard_map/all_to_all | solution.py:300
  781.5 8.2 collective-permute-start.34
  782.5 16.7 %collective-permute-start.36 = (bf16[1,512,640]{2,1,0:T(8,128)(2,1)S(1)}, bf16[1,512,640]{2,1,0:T(8,128)(2,1)S(1)}, u32[]{:S(2)}, u32[]{:S(2)}) collective-permute-start(bf16[1,512,640]{2,1,0:T(8,128)(2,1)S(1)} %shard_map.230), channel_id=1, source_target_pairs={{0,2},{1,3},{2,0},{3,1},{4,6},{5,7},{6,4},{7,5},{8,10},{9,11},{10,... | collective-permute-start | bytes 1966088 | tf_op jit(solution)/shard_map/ppermute | solution.py:242
  801.5 34.9 %all-to-all-start.6 = ((bf16[8,64,640]{2,1,0:T(8,128)(2,1)}), bf16[8,64,640]{2,1,0:T(8,128)(2,1)S(1)}, u32[]{:S(2)}, u32[]{:S(2)}) async-start(bf16[8,64,640]{2,1,0:T(8,128)(2,1)} %bitcast.86), calls=%async_computation.8 | async-start | bytes 1310720 | tf_op jit(solution)/shard_map/all_to_all | solution.py:300
  816.7 30.0 %collective-permute-start.37 = (f32[8,144]{1,0:T(8,128)}, f32[8,144]{1,0:T(8,128)}, u32[]{:S(2)}, u32[]{:S(2)}) collective-permute-start(f32[8,144]{1,0:T(8,128)} %bitcast.203), channel_id=1, source_target_pairs={{0,1},{1,0},{2,3},{3,2},{4,5},{5,4},{6,7},{7,6},{8,9},{9,8},{10,11... | collective-permute-start | bytes 13832 | tf_op jit(solution)/shard_map/ppermute | solution.py:242
  817.9 28.9 %collective-permute-start.39 = (f32[8,144]{1,0:T(8,128)}, f32[8,144]{1,0:T(8,128)}, u32[]{:S(2)}, u32[]{:S(2)}) collective-permute-start(f32[8,144]{1,0:T(8,128)} %add.543), channel_id=1, source_target_pairs={{0,2},{1,3},{2,0},{3,1},{4,6},{5,7},{6,4},{7,5},{8,10},{9,11},{10,... | collective-permute-start | bytes 13832 | tf_op jit(solution)/shard_map/ppermute | solution.py:242
  837.3 30.7 %all-to-all-start.7 = ((bf16[8,64,1152]{2,1,0:T(8,128)(2,1)}), bf16[8,64,1152]{2,1,0:T(8,128)(2,1)S(1)}, u32[]{:S(2)}, u32[]{:S(2)}) async-start(bf16[8,64,1152]{2,1,0:T(8,128)(2,1)} %add_convert_fusion), calls=%async_computation.9 | async-start | bytes 2359296 | tf_op jit(solution)/shard_map/all_to_all | solution.py:300
  868.6 22.0 %all-to-all-start.8 = ((f32[8,1,144]{2,1,0:T(1,128)}), f32[8,1,144]{2,1,0:T(1,128)S(1)}, u32[]{:S(2)}, u32[]{:S(2)}) async-start(f32[8,1,144]{2,1,0:T(1,128)} %all_to_all.41), calls=%async_computation.10 | async-start | bytes 16384 | tf_op jit(solution)/shard_map/all_to_all | solution.py:300
  (98 other events, 1338.5 us)
Sparse Core Ops, SparseCore 0:
  10.7 93.7 all-gather.5
  107.4 98.6 all-gather.7
  208.8 71.8 all-gather.9
  304.9 74.7 all-gather.11
  476.3 149.1 reduce-scatter.2
  635.4 84.7 all-gather.13
  724.9 117.4 reduce-scatter.4

commit v13 on v11

--- a/solution.py
+++ b/solution.py
@@ -298,6 +298,19 @@
 
 def ctx_exchange(values):
     return lax.all_to_all(values, "ctx", split_axis=0, concat_axis=0, tiled=True)
+
+
+def ctx_reduce(values):
+    count = lax.axis_size("ctx")
+    at = lax.axis_index("ctx")
+    half = count // 2
+    while half:
+        bit = at // half % 2
+        keep = lax.dynamic_slice_in_dim(values, bit * half, half, 0)
+        send = lax.dynamic_slice_in_dim(values, (1 - bit) * half, half, 0)
+        values = keep + lax.ppermute(send, "ctx", [(i, i ^ half) for i in range(count)])
+        half //= 2
+    return values[0]
 
 
 def dot_f32(left, right, dims=((1,), (0,))):
@@ -840,7 +853,7 @@
     def reduce_gains(gain_in_grad, gain_lat_grad, first=(), second=()):
         gains = jnp.concatenate([gain_in_grad, gain_mid_grad, gain_lat_grad], 0)
         gains = fsdp_reduce(gains.reshape(n_ctx, 4, -1).transpose(1, 0, 2), rank, first)
-        return gains, jnp.sum(ctx_exchange(after(gains, second)), 0)
+        return gains, ctx_reduce(after(gains, second))
 
     def sum_shared(early):
         far = fsdp_swap(after(shared_other, early), 2)

time: 865 us -> 888 us (1.027)
  waiting for transfers between devices: 322 us -> 342 us
    all_to_all x9 -> x8, waiting for transfers between devices: 31.4 us -> 4.94 us  [ctx_exchange(): lax.all_to_all(values, 'ctx', split_axis=0, concat_axis=0, tiled=True)]
    ppermute x0 -> x3, waiting for transfers between devices: none -> 24.1 us  [ctx_reduce(): lax.ppermute(send, 'ctx', [(i, i ^ half) for i in range(count)])]
    reduce_scatter x2, waiting for transfers between devices: 0.01 us -> 23.4 us  [ctx_scatter(): return lax.psum_scatter(values, 'ctx', scatter_dimension=0, tiled=True)]
    all_to_all x9 -> x8, starting transfers between devices: 44 us -> 40.3 us  [ctx_exchange(): lax.all_to_all(values, 'ctx', split_axis=0, concat_axis=0, tiled=True)]
    unnamed x199 -> x205, local copies, waits for them, and re-layouts: 35.6 us -> 35 us
  transfers between devices with their start and end apart: 56 -> 58, of which waited for: 27 -> 27; matrix products, arithmetic and copies ran while one was open for 24% -> 24% of each run, Pallas kernels for 13% -> 12%
where the time goes in v13:
time: 888 us; the launch traced here: 879 us
  waiting for transfers between devices  342 us (39%)
  Pallas kernels  177 us (20%)
  local copies, waits for them, and re-layouts  103 us (12%)
  other arithmetic  82.9 us (9%)
  starting transfers between devices  67.3 us (8%)
  matrix products  60 us (7%)
  blocking collectives  30.9 us (3%)
  between operations  16.2 us (2%)
    ppermute x40, waiting for transfers between devices, fsdp_swap(): lax.ppermute(values, 'fsdp', [(at, at ^ distance) for at in range(count)])  255 us
    dot_general x12, matrix products, dot_f32(): lax.dot_general(left, right, (dims, ((), ())), preferred_element_type=jnp...  60 us
    pallas_call x13, Pallas kernels, expert_grad_call(): pl.pallas_call(functools.partial(expert_grad_body, each=len(each)), grid=...  57.7 us
    pallas_call x1, Pallas kernels, experts_call(): pl.pallas_call(experts_body, grid=(count,), in_specs=[pl.BlockSpec((1, sl...  48.8 us
    all_to_all x8, starting transfers between devices, ctx_exchange(): lax.all_to_all(values, 'ctx', split_axis=0, concat_axis=0, tiled=True)  40.3 us
    unnamed x205, local copies, waits for them, and re-layouts  35 us
    all_gather x4, waiting for transfers between devices, ctx_gather(): return lax.all_gather(values, 'ctx', axis=0, tiled=True)  34.7 us
    all_to_all x1, blocking collectives, ctx_exchange(): lax.all_to_all(values, 'ctx', split_axis=0, concat_axis=0, tiled=True)  30.9 us
  transfers between devices with their start and end apart: 58, of which 27 were waited for; matrix products, arithmetic and copies ran while one was open for 24% of the time, Pallas kernels for 12%

profile of v13, /device:TPU:0, one launch (start us, length us, event | category | flops | bytes accessed | tf_op | source)
XLA Modules:
  0.0 879.4 jit_solution(9435041431583895282)
XLA Ops:
  12.8 7.3 all-to-all-start
  20.1 5.2 fusion.120
  26.8 31.7 %collective-permute-done = bf16[2,128,2816]{2,1,0:T(8,128)(2,1)} collective-permute-done((bf16[2,128,2816]{2,1,0:T(8,128)(2,1)S(1)}, bf16[2,128,2816]{2,1,0:T(8,128)(2,1)}, u32[]{:S(2)}, u32[]{:S(2)}) %collective-permute-start) | collective-permute-done | bytes 1441824 | tf_op jit(solution)/shard_map/ppermute | solution.py:242
  64.5 24.4 %collective-permute-done.2 = bf16[8,64,1088]{2,1,0:T(8,128)(2,1)S(1)} collective-permute-done((bf16[8,64,1088]{2,1,0:T(8,128)(2,1)S(1)}, bf16[8,64,1088]{2,1,0:T(8,128)(2,1)S(1)}, u32[]{:S(2)}, u32[]{:S(2)}) %collective-permute-start.2) | collective-permute-done | bytes 1114144 | tf_op jit(solution)/shard_map/ppermute | solution.py:242
  95.7 8.9 %all-gather.6.cloned.1.call-done = bf16[1024,2048]{1,0:T(8,128)(2,1)} async-done(((bf16[128,2048]{1,0:T(8,128)(2,1)}), bf16[1024,2048]{1,0:T(8,128)(2,1)}) %all-gather.6.cloned.1.call-update) | async-done | bytes 4194320 | tf_op jit(solution)/shard_map/all_gather | solution.py:292
  127.7 6.1 fusion.25
  143.7 13.8 %shard_map.212 = (bf16[1024,256]{1,0:T(8,128)(2,1)S(1)}, f32[2,1024,512]{2,1,0:T(8,128)}, f32[2,1024,1]{2,1,0:T(8,128)S(1)}) custom-call(bf16[1024,256]{1,0:T(8,128)(2,1)S(1)} %slice.307.nope_ref, bf16[2,1024,64]{2,1,0:T(8,128)(2,1)S(1)} %pad_maximum_fusion.17.rot_ref, bf16[1024,512]{1,0:T(8,128)(2,1)} %multiply_convert_fusion.1.lat_ref, ...), custom_call_target="tpu_custom_call" | custom-call | tf_op jit(solution)/shard_map/pallas_call | solution.py:419
  160.1 5.4 all-to-all-start.1
  170.9 18.8 %collective-permute-done.7 = bf16[2,128,2816]{2,1,0:T(8,128)(2,1)} collective-permute-done((bf16[2,128,2816]{2,1,0:T(8,128)(2,1)}, bf16[2,128,2816]{2,1,0:T(8,128)(2,1)}, u32[]{:S(2)}, u32[]{:S(2)}) %collective-permute-start.7) | collective-permute-done | bytes 1441824 | tf_op jit(solution)/shard_map/ppermute | solution.py:242
  196.4 28.6 %collective-permute-done.9 = bf16[2,128,2816]{2,1,0:T(8,128)(2,1)} collective-permute-done((bf16[2,128,2816]{2,1,0:T(8,128)(2,1)}, bf16[2,128,2816]{2,1,0:T(8,128)(2,1)}, u32[]{:S(2)}, u32[]{:S(2)}) %collective-permute-start.9) | collective-permute-done | bytes 1441824 | tf_op jit(solution)/shard_map/ppermute | solution.py:242
  238.6 16.9 %collective-permute-done.5 = bf16[8,64,1152]{2,1,0:T(8,128)(2,1)} collective-permute-done((bf16[8,64,1152]{2,1,0:T(8,128)(2,1)}, bf16[8,64,1152]{2,1,0:T(8,128)(2,1)}, u32[]{:S(2)}, u32[]{:S(2)}) %collective-permute-start.5) | collective-permute-done | bytes 1179680 | tf_op jit(solution)/shard_map/ppermute | solution.py:242
  256.9 4.4 convert_bitcast_fusion
  261.3 6.4 multiply_reduce_fusion.5
  269.7 17.6 %all-gather.10.cloned.1.call-done = bf16[1024,2048]{1,0:T(8,128)(2,1)} async-done(((bf16[128,2048]{1,0:T(8,128)(2,1)}), bf16[1024,2048]{1,0:T(8,128)(2,1)}) %all-gather.10.cloned.1.call-update) | async-done | bytes 4194320 | tf_op jit(solution)/shard_map/all_gather | solution.py:292
  287.4 7.9 multiply_convert_fusion
  295.3 23.6 %collective-permute-done.15 = bf16[2,1408,512]{2,1,0:T(8,128)(2,1)} collective-permute-done((bf16[2,1408,512]{2,1,0:T(8,128)(2,1)}, bf16[2,1408,512]{2,1,0:T(8,128)(2,1)}, u32[]{:S(2)}, u32[]{:S(2)}) %collective-permute-start.15) | collective-permute-done | bytes 2883616 | tf_op jit(solution)/shard_map/ppermute | solution.py:242
  324.7 7.0 pad_maximum_fusion.5.gate_up_ref
  339.7 5.7 constant_dynamic-update-slice_fusion.gu_ref
  345.4 8.0 pad_maximum_fusion.dn_ref
  353.4 8.2 all-gather.12.cloned.1.call-done
  361.6 6.3 fusion.127
  372.1 5.8 convolution_convert_fusion.1
  378.0 48.8 %shard_map.213 = (bf16[2,432,1408]{2,1,0:T(8,128)(2,1)}, bf16[2,432,2816]{2,1,0:T(8,128)(2,1)}, bf16[2,432,2048]{2,1,0:T(8,128)(2,1)}, bf16[2,432,2048]{2,1,0:T(8,128)(2,1)}) custom-call(bf16[2,432,2048]{2,1,0:T(8,128)(2,1)} %bitcast.209, bf16[2,432,2048]{2,1,0:T(8,128)(2,1)} %bitcast.221, f32[2,432,1]{2,1,0:T(8,128)} %copy.472.gate_ref, ...), custom_call_target="tpu_custom_call" | custom-call | tf_op jit(solution)/shard_map/pallas_call | solution.py:531
  426.7 19.0 %shard_map.214 = bf16[1024,4096]{1,0:T(8,128)(2,1)} custom-call(bf16[1024,864]{1,0:T(8,128)(2,1)} %get-tuple-element.227.pick_ref, bf16[1024,768]{1,0:T(8,128)(2,1)S(1)} %pad_maximum_fusion.9.both_ref, bf16[1024,384]{1,0:T(8,128)(2,1)S(1)} %get-tuple-element.253.act_ref, bf16[864,2048]{1,0:T(8,128)(2,1)} %bitcast.240, bf16[864,2048]{1,0:T(8,128)(2,1)} %bitcast.239, ...), custom_call_target="tpu_custom_call" | custom-call | tf_op jit(solution)/shard_map/pallas_call | solution.py:665
  447.4 4.3 shard_map.215
  451.8 5.5 collective-permute-done.18.refs_2_
  458.9 4.6 shard_map.216
  463.4 7.4 shard_map.217
  472.5 8.0 collective-permute-done.19
  489.3 5.4 shard_map.218
  494.7 7.6 shard_map.221
  503.8 32.8 %collective-permute-done.23.refs_3_ = bf16[2,1408,512]{2,1,0:T(8,128)(2,1)} collective-permute-done((bf16[2,1408,512]{2,1,0:T(8,128)(2,1)}, bf16[2,1408,512]{2,1,0:T(8,128)(2,1)}, u32[]{:S(2)}, u32[]{:S(2)}) %collective-permute-start.23) | collective-permute-done | bytes 2883616 | tf_op jit(solution)/shard_map/ppermute | solution.py:242
  550.6 6.9 copy.473
  566.2 5.8 shard_map.222
  572.0 25.8 %collective-permute-done.20.refs_3_ = bf16[1,512,2816]{2,1,0:T(8,128)(2,1)S(1)} collective-permute-done((bf16[1,512,2816]{2,1,0:T(8,128)(2,1)}, bf16[1,512,2816]{2,1,0:T(8,128)(2,1)S(1)}, u32[]{:S(2)}, u32[]{:S(2)}) %collective-permute-start.20) | collective-permute-done | bytes 2883616 | tf_op jit(solution)/shard_map/ppermute | solution.py:242
  606.5 4.6 convolution_convert_fusion.2
  611.2 30.9 %all_to_all.45 = bf16[8,128,256]{2,1,0:T(8,128)(2,1)S(1)} all-to-all(bf16[8,128,256]{2,1,0:T(8,128)(2,1)S(1)} %bitcast.246), channel_id=1, replica_groups=mesh['ctx'=8,'fsdp'=4] {'ctx'}, dimensions={0} | all-to-all | bytes 1048576 | tf_op jit(solution)/shard_map/all_to_all | solution.py:300
  642.1 24.9 %shard_map.223 = (bf16[1024,256]{1,0:T(8,128)(2,1)S(1)}, f32[2,1024,64]{2,1,0:T(8,128)}, f32[2,512,256]{2,1,0:T(8,128)}, f32[1024,512]{1,0:T(8,128)}, f32[1024,64]{1,0:T(8,128)S(1)}) custom-call(bf16[1024,256]{1,0:T(8,128)(2,1)S(1)} %bitcast.220, bf16[1024,256]{1,0:T(8,128)(2,1)S(1)} %copy-done.12, bf16[2,1024,64]{2,1,0:T(8,128)(2,1)S(1)} %copy-done.10, ...), custom_call_target="tpu_custom_call" | custom-call | tf_op jit(solution)/shard_map/pallas_call | solution.py:454
  674.2 6.6 fusion.3
  684.5 4.8 all-to-all-start.5
  709.0 12.3 %collective-permute-done.33 = bf16[512,128]{1,0:T(8,128)(2,1)S(1)} collective-permute-done((bf16[512,128]{1,0:T(8,128)(2,1)S(1)}, bf16[512,128]{1,0:T(8,128)(2,1)S(1)}, u32[]{:S(2)}, u32[]{:S(2)}) %collective-permute-start.33) | collective-permute-done | bytes 131104 | tf_op jit(solution)/shard_map/ppermute | solution.py:242
  724.7 8.8 collective-permute-done.29.refs_5_
  742.6 5.4 all-to-all-start.7
  761.2 10.7 %collective-permute-done.36.refs_3_ = bf16[1,512,640]{2,1,0:T(8,128)(2,1)S(1)} collective-permute-done((bf16[1,512,640]{2,1,0:T(8,128)(2,1)S(1)}, bf16[1,512,640]{2,1,0:T(8,128)(2,1)S(1)}, u32[]{:S(2)}, u32[]{:S(2)}) %collective-permute-start.36) | collective-permute-done | bytes 655392 | tf_op jit(solution)/shard_map/ppermute | solution.py:242
  773.2 6.2 all-to-all-start.6
  791.1 23.4 %reduce-scatter.5.cloned.1.call-done = bf16[128,2048]{1,0:T(8,128)(2,1)} async-done(((bf16[1024,2048]{1,0:T(8,128)(2,1)}), bf16[128,2048]{1,0:T(8,128)(2,1)}) %reduce-scatter.5.cloned.1.call-update) | async-done | bytes 524304 | tf_op jit(solution)/shard_map/reduce_scatter | solution.py:296
  828.6 21.5 %collective-permute-done.40 = f32[4,144]{1,0:T(4,128)S(1)} collective-permute-done((f32[4,144]{1,0:T(4,128)S(1)}, f32[4,144]{1,0:T(4,128)S(1)}, u32[]{:S(2)}, u32[]{:S(2)}) %collective-permute-start.40) | collective-permute-done | bytes 2336 | tf_op jit(solution)/shard_map/ppermute | solution.py:311
  857.1 11.8 %shard_map.233 = f32[2,512,2816]{2,1,0:T(8,128)} custom-call(bf16[2,432,2048]{2,1,0:T(8,128)(2,1)} %bitcast.212, bf16[2,432,2816]{2,1,0:T(8,128)(2,1)} %get-tuple-element.93.refs_1_, bf16[2,512,2816]{2,1,0:T(8,128)(2,1)} %collective-permute-done.22.refs_2_, bf16[1,512,2816]{2,1,0:T(8,128)(2,1)S(1)} %copy-done.14, ...), custom_call_target="tpu_custom_call" | custom-call | tf_op jit(solution)/shard_map/pallas_call | solution.py:568
  (504 shorter events, 241.7 us)
Async XLA Ops:
  7.2 97.4 %all-gather.6.cloned.1.call-start = ((), (), s32[]{:S(2)}) async-start(), calls=%async_computation.11 | async-start | bytes 4718592 | tf_op jit(solution)/shard_map/all_gather | solution.py:292
  12.8 49.9 %all-to-all-start = ((bf16[8,64,960]{2,1,0:T(8,128)(2,1)}), bf16[8,64,960]{2,1,0:T(8,128)(2,1)S(1)}, u32[]{:S(2)}, u32[]{:S(2)}) async-start(bf16[8,64,960]{2,1,0:T(8,128)(2,1)} %pad_maximum_fusion.12), calls=%async_computation | async-start | bytes 2097152 | tf_op jit(solution)/shard_map/all_to_all | solution.py:300
  20.1 241.2 %all-gather.8.cloned.1.call-start = ((), (), s32[]{:S(2)}) async-start(), calls=%async_computation.12 | async-start | bytes 8650752 | tf_op jit(solution)/shard_map/all_gather | solution.py:932
  25.4 33.1 %collective-permute-start = (bf16[2,128,2816]{2,1,0:T(8,128)(2,1)S(1)}, bf16[2,128,2816]{2,1,0:T(8,128)(2,1)}, u32[]{:S(2)}, u32[]{:S(2)}) collective-permute-start(bf16[2,128,2816]{2,1,0:T(8,128)(2,1)S(1)} %get-tuple-element.234), channel_id=1, source_target_pairs={{0,2},{1,3},{2,0},{3,1},{4,6},{5,7},{6,4},{7,5},{8,10},{9,11},{10,... | collective-permute-start | bytes 4325384 | tf_op jit(solution)/shard_map/ppermute | solution.py:242
  62.9 26.0 %collective-permute-start.2 = (bf16[8,64,1088]{2,1,0:T(8,128)(2,1)S(1)}, bf16[8,64,1088]{2,1,0:T(8,128)(2,1)S(1)}, u32[]{:S(2)}, u32[]{:S(2)}) collective-permute-start(bf16[8,64,1088]{2,1,0:T(8,128)(2,1)S(1)} %pad_maximum_fusion.10), channel_id=1, source_target_pairs={{0,2},{1,3},{2,0},{3,1},{4,6},{5,7},{6,4},{7,5},{8,10},{9,11},{10,... | collective-permute-start | bytes 3342344 | tf_op jit(solution)/shard_map/ppermute | solution.py:242
  64.5 24.4 %collective-permute-start.1 = (bf16[8,64,1088]{2,1,0:T(8,128)(2,1)S(1)}, bf16[8,64,1088]{2,1,0:T(8,128)(2,1)S(1)}, u32[]{:S(2)}, u32[]{:S(2)}) collective-permute-start(bf16[8,64,1088]{2,1,0:T(8,128)(2,1)S(1)} %pad_maximum_fusion.10), channel_id=1, source_target_pairs={{0,1},{1,0},{2,3},{3,2},{4,5},{5,4},{6,7},{7,6},{8,9},{9,8},{10,11... | collective-permute-start | bytes 3342344 | tf_op jit(solution)/shard_map/ppermute | solution.py:242
  104.6 235.1 %collective-permute-start.14 = (bf16[2,512,2816]{2,1,0:T(8,128)(2,1)}, bf16[2,512,2816]{2,1,0:T(8,128)(2,1)}, u32[]{:S(2)}, u32[]{:S(2)}) collective-permute-start(bf16[2,512,2816]{2,1,0:T(8,128)(2,1)} %param.22), channel_id=1, source_target_pairs={{0,1},{1,0},{2,3},{3,2},{4,5},{5,4},{6,7},{7,6},{8,9},{9,8},{10,11... | collective-permute-start | bytes 17301512 | tf_op jit(solution)/shard_map/ppermute | solution.py:242
  104.6 63.4 %collective-permute-start.8 = (bf16[2,128,2816]{2,1,0:T(8,128)(2,1)}, bf16[2,128,2816]{2,1,0:T(8,128)(2,1)}, u32[]{:S(2)}, u32[]{:S(2)}) collective-permute-start(bf16[2,128,2816]{2,1,0:T(8,128)(2,1)} %get-tuple-element.232), channel_id=1, source_target_pairs={{0,2},{1,3},{2,0},{3,1},{4,6},{5,7},{6,4},{7,5},{8,10},{9,11},{10,... | collective-permute-start | bytes 4325384 | tf_op jit(solution)/shard_map/ppermute | solution.py:242
  106.2 83.5 %collective-permute-start.7 = (bf16[2,128,2816]{2,1,0:T(8,128)(2,1)}, bf16[2,128,2816]{2,1,0:T(8,128)(2,1)}, u32[]{:S(2)}, u32[]{:S(2)}) collective-permute-start(bf16[2,128,2816]{2,1,0:T(8,128)(2,1)} %get-tuple-element.233), channel_id=1, source_target_pairs={{0,2},{1,3},{2,0},{3,1},{4,6},{5,7},{6,4},{7,5},{8,10},{9,11},{10,... | collective-permute-start | bytes 4325384 | tf_op jit(solution)/shard_map/ppermute | solution.py:242
  106.7 118.3 %collective-permute-start.9 = (bf16[2,128,2816]{2,1,0:T(8,128)(2,1)}, bf16[2,128,2816]{2,1,0:T(8,128)(2,1)}, u32[]{:S(2)}, u32[]{:S(2)}) collective-permute-start(bf16[2,128,2816]{2,1,0:T(8,128)(2,1)} %get-tuple-element.231), channel_id=1, source_target_pairs={{0,2},{1,3},{2,0},{3,1},{4,6},{5,7},{6,4},{7,5},{8,10},{9,11},{10,... | collective-permute-start | bytes 4325384 | tf_op jit(solution)/shard_map/ppermute | solution.py:242
  108.2 237.2 %collective-permute-start.17 = (bf16[2,1408,512]{2,1,0:T(8,128)(2,1)}, bf16[2,1408,512]{2,1,0:T(8,128)(2,1)}, u32[]{:S(2)}, u32[]{:S(2)}) collective-permute-start(bf16[2,1408,512]{2,1,0:T(8,128)(2,1)} %param.23), channel_id=1, source_target_pairs={{0,1},{1,0},{2,3},{3,2},{4,5},{5,4},{6,7},{7,6},{8,9},{9,8},{10,11... | collective-permute-start | bytes 8650760 | tf_op jit(solution)/shard_map/ppermute | solution.py:242
  116.4 43.8 %all-to-all-start.2 = ((bf16[8,64,1152]{2,1,0:T(8,128)(2,1)}), bf16[8,64,1152]{2,1,0:T(8,128)(2,1)}, u32[]{:S(2)}, u32[]{:S(2)}) async-start(bf16[8,64,1152]{2,1,0:T(8,128)(2,1)} %fusion.32), calls=%async_computation.2 | async-start | bytes 2359296 | tf_op jit(solution)/shard_map/all_to_all | solution.py:300
  120.6 166.7 %all-gather.10.cloned.1.call-start = ((), (), s32[]{:S(2)}) async-start(), calls=%async_computation.13 | async-start | bytes 4718592 | tf_op jit(solution)/shard_map/all_gather | solution.py:292
  160.1 32.7 %all-to-all-start.1 = ((bf16[8,128,256]{1,2,0:T(8,128)(2,1)}), bf16[8,128,256]{1,2,0:T(8,128)(2,1)S(1)}, u32[]{:S(2)}, u32[]{:S(2)}) async-start(bf16[8,128,256]{1,2,0:T(8,128)(2,1)} %copy.456), calls=%async_computation.1 | async-start | bytes 1048576 | tf_op jit(solution)/shard_map/all_to_all | solution.py:300
  192.9 36.2 %all-to-all-start.3 = ((bf16[8,128,24]{1,2,0:T(8,128)(2,1)}), bf16[8,128,24]{1,2,0:T(8,128)(2,1)S(1)}, u32[]{:S(2)}, u32[]{:S(2)}) async-start(bf16[8,128,24]{1,2,0:T(8,128)(2,1)} %broadcast_in_dim.45), calls=%async_computation.3 | async-start | bytes 98304 | tf_op jit(solution)/shard_map/all_to_all | solution.py:300
  196.2 165.4 %all-gather.12.cloned.1.call-start = ((), (), s32[]{:S(2)}) async-start(), calls=%async_computation.14 | async-start | bytes 4718592 | tf_op jit(solution)/shard_map/all_gather | solution.py:292
  227.6 27.8 %collective-permute-start.5 = (bf16[8,64,1152]{2,1,0:T(8,128)(2,1)}, bf16[8,64,1152]{2,1,0:T(8,128)(2,1)}, u32[]{:S(2)}, u32[]{:S(2)}) collective-permute-start(bf16[8,64,1152]{2,1,0:T(8,128)(2,1)} %all-to-all-done.2), channel_id=1, source_target_pairs={{0,2},{1,3},{2,0},{3,1},{4,6},{5,7},{6,4},{7,5},{8,10},{9,11},{10,... | collective-permute-start | bytes 3538952 | tf_op jit(solution)/shard_map/ppermute | solution.py:242
  229.1 89.8 %collective-permute-start.4 = (bf16[8,64,1152]{2,1,0:T(8,128)(2,1)}, bf16[8,64,1152]{2,1,0:T(8,128)(2,1)}, u32[]{:S(2)}, u32[]{:S(2)}) collective-permute-start(bf16[8,64,1152]{2,1,0:T(8,128)(2,1)} %all-to-all-done.2), channel_id=1, source_target_pairs={{0,1},{1,0},{2,3},{3,2},{4,5},{5,4},{6,7},{7,6},{8,9},{9,8},{10,11... | collective-permute-start | bytes 3538952 | tf_op jit(solution)/shard_map/ppermute | solution.py:242
  255.4 63.5 %collective-permute-start.15 = (bf16[2,1408,512]{2,1,0:T(8,128)(2,1)}, bf16[2,1408,512]{2,1,0:T(8,128)(2,1)}, u32[]{:S(2)}, u32[]{:S(2)}) collective-permute-start(bf16[2,1408,512]{2,1,0:T(8,128)(2,1)} %param.23), channel_id=1, source_target_pairs={{0,2},{1,3},{2,0},{3,1},{4,6},{5,7},{6,4},{7,5},{8,10},{9,11},{10,... | collective-permute-start | bytes 8650760 | tf_op jit(solution)/shard_map/ppermute | solution.py:242
  267.7 51.7 %collective-permute-start.6 = (bf16[8,64,1152]{2,1,0:T(8,128)(2,1)}, bf16[8,64,1152]{2,1,0:T(8,128)(2,1)S(1)}, u32[]{:S(2)}, u32[]{:S(2)}) collective-permute-start(bf16[8,64,1152]{2,1,0:T(8,128)(2,1)} %collective-permute-done.5), channel_id=1, source_target_pairs={{0,1},{1,0},{2,3},{3,2},{4,5},{5,4},{6,7},{7,6},{8,9},{9,8},{10,11... | collective-permute-start | bytes 3538952 | tf_op jit(solution)/shard_map/ppermute | solution.py:242
  287.4 310.4 %reduce-scatter.3.cloned.1.call-start = ((), (), s32[]{:S(2)}) async-start(), calls=%async_computation.15 | async-start | bytes 9437184 | tf_op jit(solution)/shard_map/reduce_scatter | solution.py:296
  319.4 14.8 %collective-permute-start.12 = (bf16[2,128,2816]{2,1,0:T(8,128)(2,1)}, bf16[2,128,2816]{2,1,0:T(8,128)(2,1)S(1)}, u32[]{:S(2)}, u32[]{:S(2)}) collective-permute-start(bf16[2,128,2816]{2,1,0:T(8,128)(2,1)} %collective-permute-done.7), channel_id=1, source_target_pairs={{0,1},{1,0},{2,3},{3,2},{4,5},{5,4},{6,7},{7,6},{8,9},{9,8},{10,11... | collective-permute-start | bytes 4325384 | tf_op jit(solution)/shard_map/ppermute | solution.py:242
  323.7 11.8 %collective-permute-start.13 = (bf16[2,128,2816]{2,1,0:T(8,128)(2,1)}, bf16[2,128,2816]{2,1,0:T(8,128)(2,1)S(1)}, u32[]{:S(2)}, u32[]{:S(2)}) collective-permute-start(bf16[2,128,2816]{2,1,0:T(8,128)(2,1)} %collective-permute-done.9), channel_id=1, source_target_pairs={{0,1},{1,0},{2,3},{3,2},{4,5},{5,4},{6,7},{7,6},{8,9},{9,8},{10,11... | collective-permute-start | bytes 4325384 | tf_op jit(solution)/shard_map/ppermute | solution.py:242
  324.4 21.0 %collective-permute-start.16 = (bf16[2,1408,512]{2,1,0:T(8,128)(2,1)}, bf16[2,1408,512]{2,1,0:T(8,128)(2,1)S(1)}, u32[]{:S(2)}, u32[]{:S(2)}) collective-permute-start(bf16[2,1408,512]{2,1,0:T(8,128)(2,1)} %collective-permute-done.15), channel_id=1, source_target_pairs={{0,1},{1,0},{2,3},{3,2},{4,5},{5,4},{6,7},{7,6},{8,9},{9,8},{10,11... | collective-permute-start | bytes 8650760 | tf_op jit(solution)/shard_map/ppermute | solution.py:242
  445.8 246.6 %all-gather.14.cloned.1.call-start = ((), (), s32[]{:S(2)}) async-start(), calls=%async_computation.17 | async-start | bytes 4718592 | tf_op jit(solution)/shard_map/all_gather | solution.py:292
  470.9 9.6 %collective-permute-start.19 = (bf16[2,512,2816]{2,1,0:T(8,128)(2,1)}, bf16[2,512,2816]{2,1,0:T(8,128)(2,1)S(1)}, u32[]{:S(2)}, u32[]{:S(2)}) collective-permute-start(bf16[2,512,2816]{2,1,0:T(8,128)(2,1)} %shard_map.217), channel_id=1, source_target_pairs={{0,1},{1,0},{2,3},{3,2},{4,5},{5,4},{6,7},{7,6},{8,9},{9,8},{10,11... | collective-permute-start | bytes 17301512 | tf_op jit(solution)/shard_map/ppermute | solution.py:242
  471.0 65.6 %collective-permute-start.23 = (bf16[2,1408,512]{2,1,0:T(8,128)(2,1)}, bf16[2,1408,512]{2,1,0:T(8,128)(2,1)}, u32[]{:S(2)}, u32[]{:S(2)}) collective-permute-start(bf16[2,1408,512]{2,1,0:T(8,128)(2,1)} %shard_map.216), channel_id=1, source_target_pairs={{0,2},{1,3},{2,0},{3,1},{4,6},{5,7},{6,4},{7,5},{8,10},{9,11},{10,... | collective-permute-start | bytes 8650760 | tf_op jit(solution)/shard_map/ppermute | solution.py:242
  502.3 95.5 %collective-permute-start.22 = (bf16[2,512,2816]{2,1,0:T(8,128)(2,1)}, bf16[2,512,2816]{2,1,0:T(8,128)(2,1)}, u32[]{:S(2)}, u32[]{:S(2)}) collective-permute-start(bf16[2,512,2816]{2,1,0:T(8,128)(2,1)} %shard_map.221), channel_id=1, source_target_pairs={{0,1},{1,0},{2,3},{3,2},{4,5},{5,4},{6,7},{7,6},{8,9},{9,8},{10,11... | collective-permute-start | bytes 17301512 | tf_op jit(solution)/shard_map/ppermute | solution.py:242
  502.3 95.5 %collective-permute-start.20 = (bf16[1,512,2816]{2,1,0:T(8,128)(2,1)}, bf16[1,512,2816]{2,1,0:T(8,128)(2,1)S(1)}, u32[]{:S(2)}, u32[]{:S(2)}) collective-permute-start(bf16[1,512,2816]{2,1,0:T(8,128)(2,1)} %shard_map.218), channel_id=1, source_target_pairs={{0,2},{1,3},{2,0},{3,1},{4,6},{5,7},{6,4},{7,5},{8,10},{9,11},{10,... | collective-permute-start | bytes 8650760 | tf_op jit(solution)/shard_map/ppermute | solution.py:242
  540.8 25.4 %collective-permute-start.21 = (bf16[2,1408,512]{2,1,0:T(8,128)(2,1)}, bf16[2,1408,512]{2,1,0:T(8,128)(2,1)}, u32[]{:S(2)}, u32[]{:S(2)}) collective-permute-start(bf16[2,1408,512]{2,1,0:T(8,128)(2,1)} %shard_map.220), channel_id=1, source_target_pairs={{0,1},{1,0},{2,3},{3,2},{4,5},{5,4},{6,7},{7,6},{8,9},{9,8},{10,11... | collective-permute-start | bytes 8650760 | tf_op jit(solution)/shard_map/ppermute | solution.py:242
  604.9 209.6 %reduce-scatter.5.cloned.1.call-start = ((), (), s32[]{:S(2)}) async-start(), calls=%async_computation.16 | async-start | bytes 4718592 | tf_op jit(solution)/shard_map/reduce_scatter | solution.py:296
  605.0 69.3 %collective-permute-start.26 = (bf16[1,512,2816]{2,1,0:T(8,128)(2,1)}, bf16[1,512,2816]{2,1,0:T(8,128)(2,1)}, u32[]{:S(2)}, u32[]{:S(2)}) collective-permute-start(bf16[1,512,2816]{2,1,0:T(8,128)(2,1)} %copy-done.15), channel_id=1, source_target_pairs={{0,2},{1,3},{2,0},{3,1},{4,6},{5,7},{6,4},{7,5},{8,10},{9,11},{10,... | collective-permute-start | bytes 8650760 | tf_op jit(solution)/shard_map/ppermute | solution.py:242
  684.5 52.5 %all-to-all-start.5 = ((bf16[8,128,576]{1,2,0:T(8,128)(2,1)}), bf16[8,128,576]{1,2,0:T(8,128)(2,1)}, u32[]{:S(2)}, u32[]{:S(2)}) async-start(bf16[8,128,576]{1,2,0:T(8,128)(2,1)} %pad_maximum_fusion.11), calls=%async_computation.7 | async-start | bytes 2359296 | tf_op jit(solution)/shard_map/all_to_all | solution.py:300
  689.3 32.7 %collective-permute-start.30 = (bf16[8,64,1152]{2,1,0:T(8,128)(2,1)}, bf16[8,64,1152]{2,1,0:T(8,128)(2,1)}, u32[]{:S(2)}, u32[]{:S(2)}) collective-permute-start(bf16[8,64,1152]{2,1,0:T(8,128)(2,1)} %get-tuple-element.109), channel_id=1, source_target_pairs={{0,2},{1,3},{2,0},{3,1},{4,6},{5,7},{6,4},{7,5},{8,10},{9,11},{10,... | collective-permute-start | bytes 3538952 | tf_op jit(solution)/shard_map/ppermute | solution.py:242
  695.0 10.6 %collective-permute-start.28 = (bf16[512,640]{1,0:T(8,128)(2,1)S(1)}, bf16[512,640]{1,0:T(8,128)(2,1)S(1)}, u32[]{:S(2)}, u32[]{:S(2)}) collective-permute-start(bf16[512,640]{1,0:T(8,128)(2,1)S(1)} %shard_map.225), channel_id=1, source_target_pairs={{0,1},{1,0},{2,3},{3,2},{4,5},{5,4},{6,7},{7,6},{8,9},{9,8},{10,11... | collective-permute-start | bytes 1966088 | tf_op jit(solution)/shard_map/ppermute | solution.py:242
  700.1 8.9 %collective-permute-start.31 = (bf16[512,128]{1,0:T(8,128)(2,1)}, bf16[512,128]{1,0:T(8,128)(2,1)S(1)}, u32[]{:S(2)}, u32[]{:S(2)}) collective-permute-start(bf16[512,128]{1,0:T(8,128)(2,1)} %bitcast.72), channel_id=1, source_target_pairs={{0,1},{1,0},{2,3},{3,2},{4,5},{5,4},{6,7},{7,6},{8,9},{9,8},{10,11... | collective-permute-start | bytes 393224 | tf_op jit(solution)/shard_map/ppermute | solution.py:242
  700.4 20.9 %collective-permute-start.33 = (bf16[512,128]{1,0:T(8,128)(2,1)S(1)}, bf16[512,128]{1,0:T(8,128)(2,1)S(1)}, u32[]{:S(2)}, u32[]{:S(2)}) collective-permute-start(bf16[512,128]{1,0:T(8,128)(2,1)S(1)} %add_convert_fusion.2), channel_id=1, source_target_pairs={{0,2},{1,3},{2,0},{3,1},{4,6},{5,7},{6,4},{7,5},{8,10},{9,11},{10,... | collective-permute-start | bytes 393224 | tf_op jit(solution)/shard_map/ppermute | solution.py:242
  705.4 19.2 %collective-permute-start.27 = (bf16[512,640]{1,0:T(8,128)(2,1)S(1)}, bf16[512,640]{1,0:T(8,128)(2,1)S(1)}, u32[]{:S(2)}, u32[]{:S(2)}) collective-permute-start(bf16[512,640]{1,0:T(8,128)(2,1)S(1)} %shard_map.224), channel_id=1, source_target_pairs={{0,1},{1,0},{2,3},{3,2},{4,5},{5,4},{6,7},{7,6},{8,9},{9,8},{10,11... | collective-permute-start | bytes 1966088 | tf_op jit(solution)/shard_map/ppermute | solution.py:242
  708.2 25.2 %collective-permute-start.29 = (bf16[512,640]{1,0:T(8,128)(2,1)S(1)}, bf16[512,640]{1,0:T(8,128)(2,1)S(1)}, u32[]{:S(2)}, u32[]{:S(2)}) collective-permute-start(bf16[512,640]{1,0:T(8,128)(2,1)S(1)} %shard_map.226), channel_id=1, source_target_pairs={{0,2},{1,3},{2,0},{3,1},{4,6},{5,7},{6,4},{7,5},{8,10},{9,11},{10,... | collective-permute-start | bytes 1966088 | tf_op jit(solution)/shard_map/ppermute | solution.py:242
  742.6 12.0 %collective-permute-start.35 = (bf16[1,512,640]{2,1,0:T(8,128)(2,1)S(1)}, bf16[1,512,640]{2,1,0:T(8,128)(2,1)S(1)}, u32[]{:S(2)}, u32[]{:S(2)}) collective-permute-start(bf16[1,512,640]{2,1,0:T(8,128)(2,1)S(1)} %shard_map.229), channel_id=1, source_target_pairs={{0,1},{1,0},{2,3},{3,2},{4,5},{5,4},{6,7},{7,6},{8,9},{9,8},{10,11... | collective-permute-start | bytes 1966088 | tf_op jit(solution)/shard_map/ppermute | solution.py:242
  742.6 30.5 %all-to-all-start.7 = ((bf16[8,64,640]{2,1,0:T(8,128)(2,1)}), bf16[8,64,640]{2,1,0:T(8,128)(2,1)}, u32[]{:S(2)}, u32[]{:S(2)}) async-start(bf16[8,64,640]{2,1,0:T(8,128)(2,1)} %bitcast.88), calls=%async_computation.9 | async-start | bytes 1310720 | tf_op jit(solution)/shard_map/all_to_all | solution.py:300
  754.3 6.9 collective-permute-start.34
  754.9 17.0 %collective-permute-start.36 = (bf16[1,512,640]{2,1,0:T(8,128)(2,1)S(1)}, bf16[1,512,640]{2,1,0:T(8,128)(2,1)S(1)}, u32[]{:S(2)}, u32[]{:S(2)}) collective-permute-start(bf16[1,512,640]{2,1,0:T(8,128)(2,1)S(1)} %shard_map.230), channel_id=1, source_target_pairs={{0,2},{1,3},{2,0},{3,1},{4,6},{5,7},{6,4},{7,5},{8,10},{9,11},{10,... | collective-permute-start | bytes 1966088 | tf_op jit(solution)/shard_map/ppermute | solution.py:242
  773.2 43.3 %all-to-all-start.6 = ((bf16[8,64,640]{2,1,0:T(8,128)(2,1)}), bf16[8,64,640]{2,1,0:T(8,128)(2,1)S(1)}, u32[]{:S(2)}, u32[]{:S(2)}) async-start(bf16[8,64,640]{2,1,0:T(8,128)(2,1)} %bitcast.86), calls=%async_computation.8 | async-start | bytes 1310720 | tf_op jit(solution)/shard_map/all_to_all | solution.py:300
  784.6 6.4 collective-permute-start.37
  817.3 52.2 %all-to-all-start.8 = ((bf16[8,64,1152]{2,1,0:T(8,128)(2,1)}), bf16[8,64,1152]{2,1,0:T(8,128)(2,1)S(1)}, u32[]{:S(2)}, u32[]{:S(2)}) async-start(bf16[8,64,1152]{2,1,0:T(8,128)(2,1)} %add_convert_fusion), calls=%async_computation.10 | async-start | bytes 2359296 | tf_op jit(solution)/shard_map/all_to_all | solution.py:300
  822.9 27.1 %collective-permute-start.40 = (f32[4,144]{1,0:T(4,128)S(1)}, f32[4,144]{1,0:T(4,128)S(1)}, u32[]{:S(2)}, u32[]{:S(2)}) collective-permute-start(f32[4,144]{1,0:T(4,128)S(1)} %constant_dynamic-slice_fusion.4), channel_id=1, source_target_pairs={{0,16},{4,20},{8,24},{12,28},{16,0},{20,4},{24,8},{28,12},{1,17},{... | collective-permute-start | bytes 6920 | tf_op jit(solution)/shard_map/ppermute | solution.py:311
  853.8 15.2 %collective-permute-start.42 = (f32[1,144]{1,0:T(1,128)S(1)}, f32[1,144]{1,0:T(1,128)S(1)}, u32[]{:S(2)}, u32[]{:S(2)}) collective-permute-start(f32[1,144]{1,0:T(1,128)S(1)} %constant_dynamic-slice_fusion), channel_id=1, source_target_pairs={{0,4},{4,0},{8,12},{12,8},{16,20},{20,16},{24,28},{28,24},{1,5},{5... | collective-permute-start | bytes 1736 | tf_op jit(solution)/shard_map/ppermute | solution.py:311
  (101 other events, 1430.3 us)
Sparse Core Ops, SparseCore 0:
  10.7 93.7 all-gather.5
  107.4 105.2 all-gather.7
  215.4 71.8 all-gather.9
  289.9 71.6 all-gather.11
  445.9 147.2 reduce-scatter.2
  605.0 82.8 all-gather.13
  692.5 121.9 reduce-scatter.4

commit v14 on v11

--- a/solution.py
+++ b/solution.py
@@ -610,20 +610,21 @@
         for part in range(2):
             piece = got_ref[r, :, part * padded : part * padded + width]
             gate_up_ref[:, part * half + at : part * half + at + width] = piece.astype(jnp.float32)
-        piece = got_ref[r, :, 2 * padded : 2 * padded + width].astype(jnp.float32)
-        down_ref[at : at + width, :] = piece.T
+        piece = got_ref[r, :, 2 * padded : 2 * padded + width]
+        down_ref[:, at : at + width] = piece.astype(jnp.float32)
 
 
 def shared_unpack_call(got, width, padded):
     count, rows = got.shape[:2]
-    return pl.pallas_call(
+    gate_up, down = pl.pallas_call(
         functools.partial(shared_unpack_body, width=width, padded=padded),
         out_shape=[
             jax.ShapeDtypeStruct((rows, 2 * count * width), jnp.float32),
-            jax.ShapeDtypeStruct((count * width, rows), jnp.float32),
+            jax.ShapeDtypeStruct((rows, count * width), jnp.float32),
         ],
         compiler_params=pltpu.CompilerParams(vmem_limit_bytes=VMEM_BYTES),
     )(got)
+    return gate_up, down.T
 
 
 def combine_body(

time: 865 us -> 864 us (level)
    unnamed x199 -> x198, local copies, waits for them, and re-layouts: 35.6 us -> 34.3 us
where the time goes in v14:
time: 864 us; the launch traced here: 855 us
  waiting for transfers between devices  322 us (37%)
  Pallas kernels  178 us (21%)
  local copies, waits for them, and re-layouts  103 us (12%)
  other arithmetic  78.7 us (9%)
  starting transfers between devices  66.6 us (8%)
  matrix products  59.4 us (7%)
  blocking collectives  30.9 us (4%)
  between operations  16.2 us (2%)
    ppermute x40, waiting for transfers between devices, fsdp_swap(): lax.ppermute(values, 'fsdp', [(at, at ^ distance) for at in range(count)])  256 us
    dot_general x12, matrix products, dot_f32(): lax.dot_general(left, right, (dims, ((), ())), preferred_element_type=jnp...  59.4 us
    pallas_call x13, Pallas kernels, expert_grad_call(): pl.pallas_call(functools.partial(expert_grad_body, each=len(each)), grid=...  58.9 us
    pallas_call x1, Pallas kernels, experts_call(): pl.pallas_call(experts_body, grid=(count,), in_specs=[pl.BlockSpec((1, sl...  48.7 us
    all_to_all x9, starting transfers between devices, ctx_exchange(): lax.all_to_all(values, 'ctx', split_axis=0, concat_axis=0, tiled=True)  44 us
    all_gather x4, waiting for transfers between devices, ctx_gather(): return lax.all_gather(values, 'ctx', axis=0, tiled=True)  34.7 us
    unnamed x198, local copies, waits for them, and re-layouts  34.3 us
    all_to_all x9, waiting for transfers between devices, ctx_exchange(): lax.all_to_all(values, 'ctx', split_axis=0, concat_axis=0, tiled=True)  31.4 us
  transfers between devices with their start and end apart: 56, of which 27 were waited for; matrix products, arithmetic and copies ran while one was open for 24% of the time, Pallas kernels for 13%

profile of v14, /device:TPU:0, one launch (start us, length us, event | category | flops | bytes accessed | tf_op | source)
XLA Modules:
  0.0 855.1 jit_solution(13284975980017676660)
XLA Ops:
  12.8 7.3 all-to-all-start
  20.1 5.2 fusion.117
  26.8 31.7 %collective-permute-done = bf16[2,128,2816]{2,1,0:T(8,128)(2,1)} collective-permute-done((bf16[2,128,2816]{2,1,0:T(8,128)(2,1)S(1)}, bf16[2,128,2816]{2,1,0:T(8,128)(2,1)}, u32[]{:S(2)}, u32[]{:S(2)}) %collective-permute-start) | collective-permute-done | bytes 1441824 | tf_op jit(solution)/shard_map/ppermute | solution.py:242
  64.5 24.4 %collective-permute-done.2 = bf16[8,64,1088]{2,1,0:T(8,128)(2,1)S(1)} collective-permute-done((bf16[8,64,1088]{2,1,0:T(8,128)(2,1)S(1)}, bf16[8,64,1088]{2,1,0:T(8,128)(2,1)S(1)}, u32[]{:S(2)}, u32[]{:S(2)}) %collective-permute-start.2) | collective-permute-done | bytes 1114144 | tf_op jit(solution)/shard_map/ppermute | solution.py:242
  95.6 8.9 %all-gather.6.cloned.1.call-done = bf16[1024,2048]{1,0:T(8,128)(2,1)} async-done(((bf16[128,2048]{1,0:T(8,128)(2,1)}), bf16[1024,2048]{1,0:T(8,128)(2,1)}) %all-gather.6.cloned.1.call-update) | async-done | bytes 4194320 | tf_op jit(solution)/shard_map/all_gather | solution.py:292
  127.7 6.1 fusion.25
  143.8 13.8 %shard_map.212 = (bf16[1024,256]{1,0:T(8,128)(2,1)S(1)}, f32[2,1024,512]{2,1,0:T(8,128)}, f32[2,1024,1]{2,1,0:T(8,128)S(1)}) custom-call(bf16[1024,256]{1,0:T(8,128)(2,1)S(1)} %slice.307.nope_ref, bf16[2,1024,64]{2,1,0:T(8,128)(2,1)S(1)} %pad_maximum_fusion.17.rot_ref, bf16[1024,512]{1,0:T(8,128)(2,1)} %multiply_convert_fusion.1.lat_ref, ...), custom_call_target="tpu_custom_call" | custom-call | tf_op jit(solution)/shard_map/pallas_call | solution.py:406
  160.1 5.3 all-to-all-start.1
  170.9 18.8 %collective-permute-done.7 = bf16[2,128,2816]{2,1,0:T(8,128)(2,1)} collective-permute-done((bf16[2,128,2816]{2,1,0:T(8,128)(2,1)}, bf16[2,128,2816]{2,1,0:T(8,128)(2,1)}, u32[]{:S(2)}, u32[]{:S(2)}) %collective-permute-start.7) | collective-permute-done | bytes 1441824 | tf_op jit(solution)/shard_map/ppermute | solution.py:242
  196.4 28.6 %collective-permute-done.9 = bf16[2,128,2816]{2,1,0:T(8,128)(2,1)} collective-permute-done((bf16[2,128,2816]{2,1,0:T(8,128)(2,1)}, bf16[2,128,2816]{2,1,0:T(8,128)(2,1)}, u32[]{:S(2)}, u32[]{:S(2)}) %collective-permute-start.9) | collective-permute-done | bytes 1441824 | tf_op jit(solution)/shard_map/ppermute | solution.py:242
  238.6 16.9 %collective-permute-done.5 = bf16[8,64,1152]{2,1,0:T(8,128)(2,1)} collective-permute-done((bf16[8,64,1152]{2,1,0:T(8,128)(2,1)}, bf16[8,64,1152]{2,1,0:T(8,128)(2,1)}, u32[]{:S(2)}, u32[]{:S(2)}) %collective-permute-start.5) | collective-permute-done | bytes 1179680 | tf_op jit(solution)/shard_map/ppermute | solution.py:242
  257.0 4.4 convert_bitcast_fusion
  261.3 6.4 multiply_reduce_fusion.5
  269.8 17.6 %all-gather.10.cloned.1.call-done = bf16[1024,2048]{1,0:T(8,128)(2,1)} async-done(((bf16[128,2048]{1,0:T(8,128)(2,1)}), bf16[1024,2048]{1,0:T(8,128)(2,1)}) %all-gather.10.cloned.1.call-update) | async-done | bytes 4194320 | tf_op jit(solution)/shard_map/all_gather | solution.py:292
  287.4 7.9 multiply_convert_fusion
  295.3 23.6 %collective-permute-done.15 = bf16[2,1408,512]{2,1,0:T(8,128)(2,1)} collective-permute-done((bf16[2,1408,512]{2,1,0:T(8,128)(2,1)}, bf16[2,1408,512]{2,1,0:T(8,128)(2,1)}, u32[]{:S(2)}, u32[]{:S(2)}) %collective-permute-start.15) | collective-permute-done | bytes 2883616 | tf_op jit(solution)/shard_map/ppermute | solution.py:242
  324.8 7.0 pad_maximum_fusion.5.gate_up_ref
  339.7 5.7 constant_dynamic-update-slice_fusion.gu_ref
  345.4 8.0 pad_maximum_fusion.dn_ref
  353.4 8.2 all-gather.12.cloned.1.call-done
  361.6 6.3 fusion.124
  372.1 5.9 convolution_convert_fusion.1
  378.0 48.7 %shard_map.213 = (bf16[2,432,1408]{2,1,0:T(8,128)(2,1)}, bf16[2,432,2816]{2,1,0:T(8,128)(2,1)}, bf16[2,432,2048]{2,1,0:T(8,128)(2,1)}, bf16[2,432,2048]{2,1,0:T(8,128)(2,1)}) custom-call(bf16[2,432,2048]{2,1,0:T(8,128)(2,1)} %bitcast.209, bf16[2,432,2048]{2,1,0:T(8,128)(2,1)} %bitcast.221, f32[2,432,1]{2,1,0:T(8,128)} %copy.465.gate_ref, ...), custom_call_target="tpu_custom_call" | custom-call | tf_op jit(solution)/shard_map/pallas_call | solution.py:518
  426.7 19.0 %shard_map.214 = bf16[1024,4096]{1,0:T(8,128)(2,1)} custom-call(bf16[1024,864]{1,0:T(8,128)(2,1)} %get-tuple-element.139.pick_ref, bf16[1024,768]{1,0:T(8,128)(2,1)S(1)} %pad_maximum_fusion.9.both_ref, bf16[1024,384]{1,0:T(8,128)(2,1)S(1)} %get-tuple-element.165.act_ref, bf16[864,2048]{1,0:T(8,128)(2,1)} %bitcast.240, bf16[864,2048]{1,0:T(8,128)(2,1)} %bitcast.239, ...), custom_call_target="tpu_custom_call" | custom-call | tf_op jit(solution)/shard_map/pallas_call | solution.py:653
  447.5 4.3 shard_map.215
  451.8 5.5 collective-permute-done.18.refs_2_
  458.9 4.6 shard_map.216
  463.5 7.4 shard_map.217
  472.5 8.0 collective-permute-done.19
  483.4 4.3 shard_map.219
  489.3 5.4 shard_map.218
  494.7 7.6 shard_map.221
  503.8 32.9 %collective-permute-done.23.refs_3_ = bf16[2,1408,512]{2,1,0:T(8,128)(2,1)} collective-permute-done((bf16[2,1408,512]{2,1,0:T(8,128)(2,1)}, bf16[2,1408,512]{2,1,0:T(8,128)(2,1)}, u32[]{:S(2)}, u32[]{:S(2)}) %collective-permute-start.23) | collective-permute-done | bytes 2883616 | tf_op jit(solution)/shard_map/ppermute | solution.py:242
  550.7 6.9 copy.466
  566.4 5.8 shard_map.222
  572.2 25.7 %collective-permute-done.20.refs_3_ = bf16[1,512,2816]{2,1,0:T(8,128)(2,1)S(1)} collective-permute-done((bf16[1,512,2816]{2,1,0:T(8,128)(2,1)}, bf16[1,512,2816]{2,1,0:T(8,128)(2,1)S(1)}, u32[]{:S(2)}, u32[]{:S(2)}) %collective-permute-start.20) | collective-permute-done | bytes 2883616 | tf_op jit(solution)/shard_map/ppermute | solution.py:242
  606.5 4.6 convolution_convert_fusion.2
  611.2 30.9 %all_to_all.54 = bf16[8,128,256]{2,1,0:T(8,128)(2,1)S(1)} all-to-all(bf16[8,128,256]{2,1,0:T(8,128)(2,1)S(1)} %bitcast.246), channel_id=1, replica_groups=mesh['ctx'=8,'fsdp'=4] {'ctx'}, dimensions={0} | all-to-all | bytes 1048576 | tf_op jit(solution)/shard_map/all_to_all | solution.py:300
  642.2 24.9 %shard_map.223 = (bf16[1024,256]{1,0:T(8,128)(2,1)S(1)}, f32[2,1024,64]{2,1,0:T(8,128)}, f32[2,512,256]{2,1,0:T(8,128)}, f32[1024,512]{1,0:T(8,128)}, f32[1024,64]{1,0:T(8,128)S(1)}) custom-call(bf16[1024,256]{1,0:T(8,128)(2,1)S(1)} %bitcast.220, bf16[1024,256]{1,0:T(8,128)(2,1)S(1)} %copy-done.12, bf16[2,1024,64]{2,1,0:T(8,128)(2,1)S(1)} %copy-done.10, ...), custom_call_target="tpu_custom_call" | custom-call | tf_op jit(solution)/shard_map/pallas_call | solution.py:441
  674.7 6.6 fusion.3
  685.0 4.8 all-to-all-start.5
  709.5 12.3 %collective-permute-done.33 = bf16[512,128]{1,0:T(8,128)(2,1)S(1)} collective-permute-done((bf16[512,128]{1,0:T(8,128)(2,1)S(1)}, bf16[512,128]{1,0:T(8,128)(2,1)S(1)}, u32[]{:S(2)}, u32[]{:S(2)}) %collective-permute-start.33) | collective-permute-done | bytes 131104 | tf_op jit(solution)/shard_map/ppermute | solution.py:242
  725.1 8.7 %collective-permute-done.29.refs_5_ = bf16[512,640]{1,0:T(8,128)(2,1)S(1)} collective-permute-done((bf16[512,640]{1,0:T(8,128)(2,1)S(1)}, bf16[512,640]{1,0:T(8,128)(2,1)S(1)}, u32[]{:S(2)}, u32[]{:S(2)}) %collective-permute-start.29) | collective-permute-done | bytes 655392 | tf_op jit(solution)/shard_map/ppermute | solution.py:242
  743.5 5.7 all-to-all-start.8
  756.3 10.9 %collective-permute-done.36.refs_3_ = bf16[1,512,640]{2,1,0:T(8,128)(2,1)S(1)} collective-permute-done((bf16[1,512,640]{2,1,0:T(8,128)(2,1)S(1)}, bf16[1,512,640]{2,1,0:T(8,128)(2,1)S(1)}, u32[]{:S(2)}, u32[]{:S(2)}) %collective-permute-start.36) | collective-permute-done | bytes 655392 | tf_op jit(solution)/shard_map/ppermute | solution.py:242
  769.6 6.0 all-to-all-start.6
  785.3 19.0 %all-to-all-done.6 = bf16[8,64,640]{2,1,0:T(8,128)(2,1)S(1)} async-done(((bf16[8,64,640]{2,1,0:T(8,128)(2,1)}), bf16[8,64,640]{2,1,0:T(8,128)(2,1)S(1)}, u32[]{:S(2)}, u32[]{:S(2)}) %all-to-all-start.6) | async-done | bytes 655392 | tf_op jit(solution)/shard_map/all_to_all | solution.py:300
  829.6 11.9 %shard_map.233 = f32[2,512,2816]{2,1,0:T(8,128)} custom-call(bf16[2,432,2048]{2,1,0:T(8,128)(2,1)} %bitcast.212, bf16[2,432,2816]{2,1,0:T(8,128)(2,1)} %get-tuple-element.93.refs_1_, bf16[2,512,2816]{2,1,0:T(8,128)(2,1)} %collective-permute-done.22.refs_2_, bf16[1,512,2816]{2,1,0:T(8,128)(2,1)S(1)} %copy-done.14, ...), custom_call_target="tpu_custom_call" | custom-call | tf_op jit(solution)/shard_map/pallas_call | solution.py:555
  (489 shorter events, 238.7 us)
Async XLA Ops:
  7.2 97.4 %all-gather.6.cloned.1.call-start = ((), (), s32[]{:S(2)}) async-start(), calls=%async_computation.12 | async-start | bytes 4718592 | tf_op jit(solution)/shard_map/all_gather | solution.py:292
  12.8 49.9 %all-to-all-start = ((bf16[8,64,960]{2,1,0:T(8,128)(2,1)}), bf16[8,64,960]{2,1,0:T(8,128)(2,1)S(1)}, u32[]{:S(2)}, u32[]{:S(2)}) async-start(bf16[8,64,960]{2,1,0:T(8,128)(2,1)} %pad_maximum_fusion.12), calls=%async_computation | async-start | bytes 2097152 | tf_op jit(solution)/shard_map/all_to_all | solution.py:300
  20.1 241.2 %all-gather.8.cloned.1.call-start = ((), (), s32[]{:S(2)}) async-start(), calls=%async_computation.13 | async-start | bytes 8650752 | tf_op jit(solution)/shard_map/all_gather | solution.py:920
  25.4 33.1 %collective-permute-start = (bf16[2,128,2816]{2,1,0:T(8,128)(2,1)S(1)}, bf16[2,128,2816]{2,1,0:T(8,128)(2,1)}, u32[]{:S(2)}, u32[]{:S(2)}) collective-permute-start(bf16[2,128,2816]{2,1,0:T(8,128)(2,1)S(1)} %get-tuple-element.146), channel_id=1, source_target_pairs={{0,2},{1,3},{2,0},{3,1},{4,6},{5,7},{6,4},{7,5},{8,10},{9,11},{10,... | collective-permute-start | bytes 4325384 | tf_op jit(solution)/shard_map/ppermute | solution.py:242
  62.9 26.0 %collective-permute-start.2 = (bf16[8,64,1088]{2,1,0:T(8,128)(2,1)S(1)}, bf16[8,64,1088]{2,1,0:T(8,128)(2,1)S(1)}, u32[]{:S(2)}, u32[]{:S(2)}) collective-permute-start(bf16[8,64,1088]{2,1,0:T(8,128)(2,1)S(1)} %pad_maximum_fusion.10), channel_id=1, source_target_pairs={{0,2},{1,3},{2,0},{3,1},{4,6},{5,7},{6,4},{7,5},{8,10},{9,11},{10,... | collective-permute-start | bytes 3342344 | tf_op jit(solution)/shard_map/ppermute | solution.py:242
  64.5 24.4 %collective-permute-start.1 = (bf16[8,64,1088]{2,1,0:T(8,128)(2,1)S(1)}, bf16[8,64,1088]{2,1,0:T(8,128)(2,1)S(1)}, u32[]{:S(2)}, u32[]{:S(2)}) collective-permute-start(bf16[8,64,1088]{2,1,0:T(8,128)(2,1)S(1)} %pad_maximum_fusion.10), channel_id=1, source_target_pairs={{0,1},{1,0},{2,3},{3,2},{4,5},{5,4},{6,7},{7,6},{8,9},{9,8},{10,11... | collective-permute-start | bytes 3342344 | tf_op jit(solution)/shard_map/ppermute | solution.py:242
  104.6 235.1 %collective-permute-start.14 = (bf16[2,512,2816]{2,1,0:T(8,128)(2,1)}, bf16[2,512,2816]{2,1,0:T(8,128)(2,1)}, u32[]{:S(2)}, u32[]{:S(2)}) collective-permute-start(bf16[2,512,2816]{2,1,0:T(8,128)(2,1)} %param.22), channel_id=1, source_target_pairs={{0,1},{1,0},{2,3},{3,2},{4,5},{5,4},{6,7},{7,6},{8,9},{9,8},{10,11... | collective-permute-start | bytes 17301512 | tf_op jit(solution)/shard_map/ppermute | solution.py:242
  104.7 63.4 %collective-permute-start.8 = (bf16[2,128,2816]{2,1,0:T(8,128)(2,1)}, bf16[2,128,2816]{2,1,0:T(8,128)(2,1)}, u32[]{:S(2)}, u32[]{:S(2)}) collective-permute-start(bf16[2,128,2816]{2,1,0:T(8,128)(2,1)} %get-tuple-element.144), channel_id=1, source_target_pairs={{0,2},{1,3},{2,0},{3,1},{4,6},{5,7},{6,4},{7,5},{8,10},{9,11},{10,... | collective-permute-start | bytes 4325384 | tf_op jit(solution)/shard_map/ppermute | solution.py:242
  106.2 83.5 %collective-permute-start.7 = (bf16[2,128,2816]{2,1,0:T(8,128)(2,1)}, bf16[2,128,2816]{2,1,0:T(8,128)(2,1)}, u32[]{:S(2)}, u32[]{:S(2)}) collective-permute-start(bf16[2,128,2816]{2,1,0:T(8,128)(2,1)} %get-tuple-element.145), channel_id=1, source_target_pairs={{0,2},{1,3},{2,0},{3,1},{4,6},{5,7},{6,4},{7,5},{8,10},{9,11},{10,... | collective-permute-start | bytes 4325384 | tf_op jit(solution)/shard_map/ppermute | solution.py:242
  106.8 118.3 %collective-permute-start.9 = (bf16[2,128,2816]{2,1,0:T(8,128)(2,1)}, bf16[2,128,2816]{2,1,0:T(8,128)(2,1)}, u32[]{:S(2)}, u32[]{:S(2)}) collective-permute-start(bf16[2,128,2816]{2,1,0:T(8,128)(2,1)} %get-tuple-element.143), channel_id=1, source_target_pairs={{0,2},{1,3},{2,0},{3,1},{4,6},{5,7},{6,4},{7,5},{8,10},{9,11},{10,... | collective-permute-start | bytes 4325384 | tf_op jit(solution)/shard_map/ppermute | solution.py:242
  108.2 237.2 %collective-permute-start.17 = (bf16[2,1408,512]{2,1,0:T(8,128)(2,1)}, bf16[2,1408,512]{2,1,0:T(8,128)(2,1)}, u32[]{:S(2)}, u32[]{:S(2)}) collective-permute-start(bf16[2,1408,512]{2,1,0:T(8,128)(2,1)} %param.23), channel_id=1, source_target_pairs={{0,1},{1,0},{2,3},{3,2},{4,5},{5,4},{6,7},{7,6},{8,9},{9,8},{10,11... | collective-permute-start | bytes 8650760 | tf_op jit(solution)/shard_map/ppermute | solution.py:242
  116.4 43.8 %all-to-all-start.2 = ((bf16[8,64,1152]{2,1,0:T(8,128)(2,1)}), bf16[8,64,1152]{2,1,0:T(8,128)(2,1)}, u32[]{:S(2)}, u32[]{:S(2)}) async-start(bf16[8,64,1152]{2,1,0:T(8,128)(2,1)} %fusion.32), calls=%async_computation.2 | async-start | bytes 2359296 | tf_op jit(solution)/shard_map/all_to_all | solution.py:300
  120.6 166.7 %all-gather.10.cloned.1.call-start = ((), (), s32[]{:S(2)}) async-start(), calls=%async_computation.14 | async-start | bytes 4718592 | tf_op jit(solution)/shard_map/all_gather | solution.py:292
  160.1 32.7 %all-to-all-start.1 = ((bf16[8,128,256]{1,2,0:T(8,128)(2,1)}), bf16[8,128,256]{1,2,0:T(8,128)(2,1)S(1)}, u32[]{:S(2)}, u32[]{:S(2)}) async-start(bf16[8,128,256]{1,2,0:T(8,128)(2,1)} %copy.449), calls=%async_computation.1 | async-start | bytes 1048576 | tf_op jit(solution)/shard_map/all_to_all | solution.py:300
  192.8 36.3 %all-to-all-start.3 = ((bf16[8,128,24]{1,2,0:T(8,128)(2,1)}), bf16[8,128,24]{1,2,0:T(8,128)(2,1)S(1)}, u32[]{:S(2)}, u32[]{:S(2)}) async-start(bf16[8,128,24]{1,2,0:T(8,128)(2,1)} %broadcast_in_dim.45), calls=%async_computation.3 | async-start | bytes 98304 | tf_op jit(solution)/shard_map/all_to_all | solution.py:300
  196.2 165.4 %all-gather.12.cloned.1.call-start = ((), (), s32[]{:S(2)}) async-start(), calls=%async_computation.15 | async-start | bytes 4718592 | tf_op jit(solution)/shard_map/all_gather | solution.py:292
  227.7 27.8 %collective-permute-start.5 = (bf16[8,64,1152]{2,1,0:T(8,128)(2,1)}, bf16[8,64,1152]{2,1,0:T(8,128)(2,1)}, u32[]{:S(2)}, u32[]{:S(2)}) collective-permute-start(bf16[8,64,1152]{2,1,0:T(8,128)(2,1)} %all-to-all-done.2), channel_id=1, source_target_pairs={{0,2},{1,3},{2,0},{3,1},{4,6},{5,7},{6,4},{7,5},{8,10},{9,11},{10,... | collective-permute-start | bytes 3538952 | tf_op jit(solution)/shard_map/ppermute | solution.py:242
  229.1 89.8 %collective-permute-start.4 = (bf16[8,64,1152]{2,1,0:T(8,128)(2,1)}, bf16[8,64,1152]{2,1,0:T(8,128)(2,1)}, u32[]{:S(2)}, u32[]{:S(2)}) collective-permute-start(bf16[8,64,1152]{2,1,0:T(8,128)(2,1)} %all-to-all-done.2), channel_id=1, source_target_pairs={{0,1},{1,0},{2,3},{3,2},{4,5},{5,4},{6,7},{7,6},{8,9},{9,8},{10,11... | collective-permute-start | bytes 3538952 | tf_op jit(solution)/shard_map/ppermute | solution.py:242
  255.5 63.5 %collective-permute-start.15 = (bf16[2,1408,512]{2,1,0:T(8,128)(2,1)}, bf16[2,1408,512]{2,1,0:T(8,128)(2,1)}, u32[]{:S(2)}, u32[]{:S(2)}) collective-permute-start(bf16[2,1408,512]{2,1,0:T(8,128)(2,1)} %param.23), channel_id=1, source_target_pairs={{0,2},{1,3},{2,0},{3,1},{4,6},{5,7},{6,4},{7,5},{8,10},{9,11},{10,... | collective-permute-start | bytes 8650760 | tf_op jit(solution)/shard_map/ppermute | solution.py:242
  267.8 51.7 %collective-permute-start.6 = (bf16[8,64,1152]{2,1,0:T(8,128)(2,1)}, bf16[8,64,1152]{2,1,0:T(8,128)(2,1)S(1)}, u32[]{:S(2)}, u32[]{:S(2)}) collective-permute-start(bf16[8,64,1152]{2,1,0:T(8,128)(2,1)} %collective-permute-done.5), channel_id=1, source_target_pairs={{0,1},{1,0},{2,3},{3,2},{4,5},{5,4},{6,7},{7,6},{8,9},{9,8},{10,11... | collective-permute-start | bytes 3538952 | tf_op jit(solution)/shard_map/ppermute | solution.py:242
  287.4 310.4 %reduce-scatter.3.cloned.1.call-start = ((), (), s32[]{:S(2)}) async-start(), calls=%async_computation.16 | async-start | bytes 9437184 | tf_op jit(solution)/shard_map/reduce_scatter | solution.py:296
  319.0 5.5 collective-permute-start.11
  319.5 14.7 %collective-permute-start.12 = (bf16[2,128,2816]{2,1,0:T(8,128)(2,1)}, bf16[2,128,2816]{2,1,0:T(8,128)(2,1)S(1)}, u32[]{:S(2)}, u32[]{:S(2)}) collective-permute-start(bf16[2,128,2816]{2,1,0:T(8,128)(2,1)} %collective-permute-done.7), channel_id=1, source_target_pairs={{0,1},{1,0},{2,3},{3,2},{4,5},{5,4},{6,7},{7,6},{8,9},{9,8},{10,11... | collective-permute-start | bytes 4325384 | tf_op jit(solution)/shard_map/ppermute | solution.py:242
  323.7 11.7 %collective-permute-start.13 = (bf16[2,128,2816]{2,1,0:T(8,128)(2,1)}, bf16[2,128,2816]{2,1,0:T(8,128)(2,1)S(1)}, u32[]{:S(2)}, u32[]{:S(2)}) collective-permute-start(bf16[2,128,2816]{2,1,0:T(8,128)(2,1)} %collective-permute-done.9), channel_id=1, source_target_pairs={{0,1},{1,0},{2,3},{3,2},{4,5},{5,4},{6,7},{7,6},{8,9},{9,8},{10,11... | collective-permute-start | bytes 4325384 | tf_op jit(solution)/shard_map/ppermute | solution.py:242
  324.4 20.9 %collective-permute-start.16 = (bf16[2,1408,512]{2,1,0:T(8,128)(2,1)}, bf16[2,1408,512]{2,1,0:T(8,128)(2,1)S(1)}, u32[]{:S(2)}, u32[]{:S(2)}) collective-permute-start(bf16[2,1408,512]{2,1,0:T(8,128)(2,1)} %collective-permute-done.15), channel_id=1, source_target_pairs={{0,1},{1,0},{2,3},{3,2},{4,5},{5,4},{6,7},{7,6},{8,9},{9,8},{10,11... | collective-permute-start | bytes 8650760 | tf_op jit(solution)/shard_map/ppermute | solution.py:242
  445.8 246.9 %all-gather.14.cloned.1.call-start = ((), (), s32[]{:S(2)}) async-start(), calls=%async_computation.18 | async-start | bytes 4718592 | tf_op jit(solution)/shard_map/all_gather | solution.py:292
  451.8 5.5 collective-permute-start.18
  470.9 9.6 %collective-permute-start.19 = (bf16[2,512,2816]{2,1,0:T(8,128)(2,1)}, bf16[2,512,2816]{2,1,0:T(8,128)(2,1)S(1)}, u32[]{:S(2)}, u32[]{:S(2)}) collective-permute-start(bf16[2,512,2816]{2,1,0:T(8,128)(2,1)} %shard_map.217), channel_id=1, source_target_pairs={{0,1},{1,0},{2,3},{3,2},{4,5},{5,4},{6,7},{7,6},{8,9},{9,8},{10,11... | collective-permute-start | bytes 17301512 | tf_op jit(solution)/shard_map/ppermute | solution.py:242
  471.0 65.6 %collective-permute-start.23 = (bf16[2,1408,512]{2,1,0:T(8,128)(2,1)}, bf16[2,1408,512]{2,1,0:T(8,128)(2,1)}, u32[]{:S(2)}, u32[]{:S(2)}) collective-permute-start(bf16[2,1408,512]{2,1,0:T(8,128)(2,1)} %shard_map.216), channel_id=1, source_target_pairs={{0,2},{1,3},{2,0},{3,1},{4,6},{5,7},{6,4},{7,5},{8,10},{9,11},{10,... | collective-permute-start | bytes 8650760 | tf_op jit(solution)/shard_map/ppermute | solution.py:242
  502.2 95.6 %collective-permute-start.22 = (bf16[2,512,2816]{2,1,0:T(8,128)(2,1)}, bf16[2,512,2816]{2,1,0:T(8,128)(2,1)}, u32[]{:S(2)}, u32[]{:S(2)}) collective-permute-start(bf16[2,512,2816]{2,1,0:T(8,128)(2,1)} %shard_map.221), channel_id=1, source_target_pairs={{0,1},{1,0},{2,3},{3,2},{4,5},{5,4},{6,7},{7,6},{8,9},{9,8},{10,11... | collective-permute-start | bytes 17301512 | tf_op jit(solution)/shard_map/ppermute | solution.py:242
  502.2 95.6 %collective-permute-start.20 = (bf16[1,512,2816]{2,1,0:T(8,128)(2,1)}, bf16[1,512,2816]{2,1,0:T(8,128)(2,1)S(1)}, u32[]{:S(2)}, u32[]{:S(2)}) collective-permute-start(bf16[1,512,2816]{2,1,0:T(8,128)(2,1)} %shard_map.218), channel_id=1, source_target_pairs={{0,2},{1,3},{2,0},{3,1},{4,6},{5,7},{6,4},{7,5},{8,10},{9,11},{10,... | collective-permute-start | bytes 8650760 | tf_op jit(solution)/shard_map/ppermute | solution.py:242
  540.9 25.5 %collective-permute-start.21 = (bf16[2,1408,512]{2,1,0:T(8,128)(2,1)}, bf16[2,1408,512]{2,1,0:T(8,128)(2,1)}, u32[]{:S(2)}, u32[]{:S(2)}) collective-permute-start(bf16[2,1408,512]{2,1,0:T(8,128)(2,1)} %shard_map.220), channel_id=1, source_target_pairs={{0,1},{1,0},{2,3},{3,2},{4,5},{5,4},{6,7},{7,6},{8,9},{9,8},{10,11... | collective-permute-start | bytes 8650760 | tf_op jit(solution)/shard_map/ppermute | solution.py:242
  604.9 215.8 %reduce-scatter.5.cloned.1.call-start = ((), (), s32[]{:S(2)}) async-start(), calls=%async_computation.17 | async-start | bytes 4718592 | tf_op jit(solution)/shard_map/reduce_scatter | solution.py:296
  605.0 69.7 %collective-permute-start.26 = (bf16[1,512,2816]{2,1,0:T(8,128)(2,1)}, bf16[1,512,2816]{2,1,0:T(8,128)(2,1)}, u32[]{:S(2)}, u32[]{:S(2)}) collective-permute-start(bf16[1,512,2816]{2,1,0:T(8,128)(2,1)} %copy-done.15), channel_id=1, source_target_pairs={{0,2},{1,3},{2,0},{3,1},{4,6},{5,7},{6,4},{7,5},{8,10},{9,11},{10,... | collective-permute-start | bytes 8650760 | tf_op jit(solution)/shard_map/ppermute | solution.py:242
  685.0 52.4 %all-to-all-start.5 = ((bf16[8,128,576]{1,2,0:T(8,128)(2,1)}), bf16[8,128,576]{1,2,0:T(8,128)(2,1)}, u32[]{:S(2)}, u32[]{:S(2)}) async-start(bf16[8,128,576]{1,2,0:T(8,128)(2,1)} %pad_maximum_fusion.11), calls=%async_computation.7 | async-start | bytes 2359296 | tf_op jit(solution)/shard_map/all_to_all | solution.py:300
  689.7 32.7 %collective-permute-start.30 = (bf16[8,64,1152]{2,1,0:T(8,128)(2,1)}, bf16[8,64,1152]{2,1,0:T(8,128)(2,1)}, u32[]{:S(2)}, u32[]{:S(2)}) collective-permute-start(bf16[8,64,1152]{2,1,0:T(8,128)(2,1)} %get-tuple-element.109), channel_id=1, source_target_pairs={{0,2},{1,3},{2,0},{3,1},{4,6},{5,7},{6,4},{7,5},{8,10},{9,11},{10,... | collective-permute-start | bytes 3538952 | tf_op jit(solution)/shard_map/ppermute | solution.py:242
  695.4 10.7 %collective-permute-start.28 = (bf16[512,640]{1,0:T(8,128)(2,1)S(1)}, bf16[512,640]{1,0:T(8,128)(2,1)S(1)}, u32[]{:S(2)}, u32[]{:S(2)}) collective-permute-start(bf16[512,640]{1,0:T(8,128)(2,1)S(1)} %shard_map.225), channel_id=1, source_target_pairs={{0,1},{1,0},{2,3},{3,2},{4,5},{5,4},{6,7},{7,6},{8,9},{9,8},{10,11... | collective-permute-start | bytes 1966088 | tf_op jit(solution)/shard_map/ppermute | solution.py:242
  700.5 8.9 %collective-permute-start.31 = (bf16[512,128]{1,0:T(8,128)(2,1)}, bf16[512,128]{1,0:T(8,128)(2,1)S(1)}, u32[]{:S(2)}, u32[]{:S(2)}) collective-permute-start(bf16[512,128]{1,0:T(8,128)(2,1)} %bitcast.72), channel_id=1, source_target_pairs={{0,1},{1,0},{2,3},{3,2},{4,5},{5,4},{6,7},{7,6},{8,9},{9,8},{10,11... | collective-permute-start | bytes 393224 | tf_op jit(solution)/shard_map/ppermute | solution.py:242
  700.8 20.9 %collective-permute-start.33 = (bf16[512,128]{1,0:T(8,128)(2,1)S(1)}, bf16[512,128]{1,0:T(8,128)(2,1)S(1)}, u32[]{:S(2)}, u32[]{:S(2)}) collective-permute-start(bf16[512,128]{1,0:T(8,128)(2,1)S(1)} %add_convert_fusion.2), channel_id=1, source_target_pairs={{0,2},{1,3},{2,0},{3,1},{4,6},{5,7},{6,4},{7,5},{8,10},{9,11},{10,... | collective-permute-start | bytes 393224 | tf_op jit(solution)/shard_map/ppermute | solution.py:242
  705.9 19.2 %collective-permute-start.27 = (bf16[512,640]{1,0:T(8,128)(2,1)S(1)}, bf16[512,640]{1,0:T(8,128)(2,1)S(1)}, u32[]{:S(2)}, u32[]{:S(2)}) collective-permute-start(bf16[512,640]{1,0:T(8,128)(2,1)S(1)} %shard_map.224), channel_id=1, source_target_pairs={{0,1},{1,0},{2,3},{3,2},{4,5},{5,4},{6,7},{7,6},{8,9},{9,8},{10,11... | collective-permute-start | bytes 1966088 | tf_op jit(solution)/shard_map/ppermute | solution.py:242
  708.7 25.1 %collective-permute-start.29 = (bf16[512,640]{1,0:T(8,128)(2,1)S(1)}, bf16[512,640]{1,0:T(8,128)(2,1)S(1)}, u32[]{:S(2)}, u32[]{:S(2)}) collective-permute-start(bf16[512,640]{1,0:T(8,128)(2,1)S(1)} %shard_map.226), channel_id=1, source_target_pairs={{0,2},{1,3},{2,0},{3,1},{4,6},{5,7},{6,4},{7,5},{8,10},{9,11},{10,... | collective-permute-start | bytes 1966088 | tf_op jit(solution)/shard_map/ppermute | solution.py:242
  743.5 6.4 collective-permute-start.35
  743.5 26.0 %all-to-all-start.8 = ((bf16[8,64,640]{2,1,0:T(8,128)(2,1)}), bf16[8,64,640]{2,1,0:T(8,128)(2,1)}, u32[]{:S(2)}, u32[]{:S(2)}) async-start(bf16[8,64,640]{2,1,0:T(8,128)(2,1)} %bitcast.87), calls=%async_computation.10 | async-start | bytes 1310720 | tf_op jit(solution)/shard_map/all_to_all | solution.py:300
  749.6 6.8 collective-permute-start.34
  750.2 17.0 %collective-permute-start.36 = (bf16[1,512,640]{2,1,0:T(8,128)(2,1)S(1)}, bf16[1,512,640]{2,1,0:T(8,128)(2,1)S(1)}, u32[]{:S(2)}, u32[]{:S(2)}) collective-permute-start(bf16[1,512,640]{2,1,0:T(8,128)(2,1)S(1)} %shard_map.230), channel_id=1, source_target_pairs={{0,2},{1,3},{2,0},{3,1},{4,6},{5,7},{6,4},{7,5},{8,10},{9,11},{10,... | collective-permute-start | bytes 1966088 | tf_op jit(solution)/shard_map/ppermute | solution.py:242
  769.6 34.8 %all-to-all-start.6 = ((bf16[8,64,640]{2,1,0:T(8,128)(2,1)}), bf16[8,64,640]{2,1,0:T(8,128)(2,1)S(1)}, u32[]{:S(2)}, u32[]{:S(2)}) async-start(bf16[8,64,640]{2,1,0:T(8,128)(2,1)} %bitcast.86), calls=%async_computation.8 | async-start | bytes 1310720 | tf_op jit(solution)/shard_map/all_to_all | solution.py:300
  805.2 10.0 %all-to-all-start.7 = ((f32[8,1,144]{2,1,0:T(1,128)}), f32[8,1,144]{2,1,0:T(1,128)S(1)}, u32[]{:S(2)}, u32[]{:S(2)}) async-start(f32[8,1,144]{2,1,0:T(1,128)} %all_to_all.40), calls=%async_computation.9 | async-start | bytes 16384 | tf_op jit(solution)/shard_map/all_to_all | solution.py:300
  815.2 31.3 %all-to-all-start.9 = ((bf16[8,64,1152]{2,1,0:T(8,128)(2,1)}), bf16[8,64,1152]{2,1,0:T(8,128)(2,1)S(1)}, u32[]{:S(2)}, u32[]{:S(2)}) async-start(bf16[8,64,1152]{2,1,0:T(8,128)(2,1)} %add_convert_fusion), calls=%async_computation.11 | async-start | bytes 2359296 | tf_op jit(solution)/shard_map/all_to_all | solution.py:300
  (96 other events, 1298.9 us)
Sparse Core Ops, SparseCore 0:
  10.7 93.7 all-gather.5
  107.4 105.2 all-gather.7
  215.5 71.8 all-gather.9
  289.9 71.6 all-gather.11
  445.9 147.2 reduce-scatter.2
  605.0 82.8 all-gather.13
  692.5 118.0 reduce-scatter.4
